TPU v7x, 32 devices: a whole 2x2x4 slice. The times are simulated.
32 devices in a mesh: ep: 8 (over z, x), tp: 4 (over y, core).
Axes of the slice: x: 2, y: 2, z: 4, core: 2. Of those that a mesh axis runs over, the one named last changes fastest.
Arguments:
- cache_pages: bfloat16 [512, 256, 576], P(('ep', 'tp')), may hold values from -6 to 6
- queries: bfloat16 [512, 128, 576], P(('ep', 'tp')), may hold values from -400 to 400
- lengths: int32 [512], replicated, may hold values from 2 to 256, as said below
- swap_slot: int32 [32], replicated, may hold values from 0 to 15
- swap_mask: int32 [1], replicated, may hold values from 1 to 7
- hidden: bfloat16 [512, 3584], P('ep'), may hold values from -6 to 6
- expert_ids: int32 [512, 8], P('ep'), may hold values from 0 to 23, all different within a row; in each aligned block of 64 rows (0 to 63, 64 to 127, ...) at most 42 rows name the same one
- gate_weights: float32 [512, 8], P('ep'), may hold values from 0.1 to 0.6
- w_gate: bfloat16 [24, 3584, 1024], P('ep', None, 'tp'), may hold values from -0.09375 to 0.09375
- w_up: bfloat16 [24, 3584, 1024], P('ep', None, 'tp'), may hold values from -0.09375 to 0.09375
- w_down: bfloat16 [24, 1024, 3584], P('ep', 'tp'), may hold values from -0.1875 to 0.1875
Outputs:
- attention_out: bfloat16 [512, 128, 512], P(('ep', 'tp'))
- moe_out: bfloat16 [512, 3584], P('ep', 'tp')
Inputs may be any that keep to these rules, and one draw needn't show every extreme that they name: `lengths`: each request's cache holds at least 2 tokens; some request holds exactly 256. `expert_ids`: A row's 8 experts are distinct. Among the 64 rows of one ep rank no expert is named by more than 42 rows, a bound that some block reaches.
All inputs are finite; a program needn't handle non-finite values.
Results may differ from a plain program's by a relative error of at most 0.012.
Values may be sent and summed in bfloat16 or wider, within the bound.
No kernel may reach another device: no remote copies, remote signals or barrier semaphores. Data moves between devices by JAX's collectives and lax.ppermute only.
A program may use at most 128 MiB of HBM per device.

v0:
```python
import jax
import jax.numpy as jnp
from jax import lax
from jax.sharding import PartitionSpec as P

LAT = 512


SCORE_SCALE = 192.0 ** (-0.5)
MASK_FLOOR = -1e30


def from_partner(block, axis, apart):
    count = lax.axis_size(axis)
    route = []
    for low in range(count):
        high = low | 1 << apart
        if high != low and high < count:
            route += [(low, high), (high, low)]
    return lax.ppermute(block, axis, route)


def bit_chosen(mask_value, bit_level):
    return jnp.bitwise_and(jnp.right_shift(mask_value, bit_level), 1) == 1


def apply_sections(payload, mask_value, sections, section_move):
    for bit_level in range(sections):
        chosen_bit = bit_chosen(mask_value, bit_level)
        swapped = section_move(payload, bit_level)
        payload = jnp.where(chosen_bit, swapped, payload)
    return payload


def page_section(payload, bit_level):
    return from_partner(payload, "ep", bit_level)


def attend_local(asked_rows, keys_vals, live_lengths):
    scores = (
        jnp.einsum("rhk,rpk->rhp", asked_rows, keys_vals, preferred_element_type=jnp.float32)
        * SCORE_SCALE
    )
    live_mask = (
        jnp.arange(keys_vals.shape[1], dtype=jnp.int32)[None, None, :] < live_lengths[:, None, None]
    )
    scores = jnp.where(live_mask, scores, MASK_FLOOR)
    highest = jnp.max(scores, axis=2, keepdims=True)
    weight = jnp.where(live_mask, jnp.exp(scores - highest), 0.0)
    totals = jnp.sum(weight, axis=2, keepdims=True)
    weight_low = weight.astype(jnp.bfloat16)
    blended = jnp.einsum(
        "rhp,rpd->rhd", weight_low, keys_vals[:, :, :LAT], preferred_element_type=jnp.float32
    )
    return (blended / totals).astype(jnp.bfloat16)


def local(
    cache_pages,
    queries,
    lengths,
    swap_slot,
    swap_mask,
    hidden,
    expert_ids,
    gate_weights,
    w_gate,
    w_up,
    w_down,
):
    local_count = cache_pages.shape[0]
    groups = lax.axis_size("tp")
    ep_rank = lax.axis_index("ep")
    tp_rank = lax.axis_index("tp")
    device = ep_rank * groups + tp_rank
    mask_value = swap_mask[0]
    partner = jnp.bitwise_xor(ep_rank, mask_value) * groups + tp_rank
    my_slot = swap_slot[device]
    far_slot = swap_slot[partner]
    sections = lax.axis_size("ep").bit_length() - 1
    own_lengths = lax.dynamic_slice_in_dim(lengths, device * local_count, local_count)
    slot_range = jnp.arange(local_count, dtype=jnp.int32)
    own_page = lax.dynamic_index_in_dim(cache_pages, my_slot, 0, keepdims=False)
    arrived = apply_sections(own_page, mask_value, sections, page_section)
    keys_vals = lax.dynamic_update_index_in_dim(cache_pages, arrived, my_slot, 0)
    live_lengths = jnp.where(
        slot_range == my_slot, lengths[partner * local_count + far_slot], own_lengths
    )
    attended = attend_local(queries, keys_vals, live_lengths)
    rows_count = hidden.shape[0]
    top_count = expert_ids.shape[1]
    expert_local = w_gate.shape[0]
    ep_size = lax.axis_size("ep")
    experts_all = ep_size * expert_local
    capacity = max(2, 2 * rows_count * top_count // experts_all)
    model_width = hidden.shape[1]
    flat_ids = expert_ids.reshape(-1)
    onehot = (flat_ids[:, None] == jnp.arange(experts_all, dtype=jnp.int32)[None, :]).astype(
        jnp.int32
    )
    pair_rank = jnp.sum(jnp.cumsum(onehot, axis=0) * onehot, axis=1) - 1
    slot_ids = flat_ids * capacity + pair_rank
    select = (
        slot_ids[None, :] == jnp.arange(experts_all * capacity, dtype=jnp.int32)[:, None]
    ).reshape(experts_all * capacity, rows_count, top_count)
    picker = jnp.any(select, axis=2).astype(jnp.bfloat16)
    pick_table = select.astype(jnp.bfloat16)
    column_count = model_width // groups
    hidden_part = lax.dynamic_slice_in_dim(hidden, tp_rank * column_count, column_count, 1)
    outgoing = jnp.dot(picker, hidden_part, preferred_element_type=jnp.float32).astype(jnp.bfloat16)
    outgoing = outgoing.reshape(ep_size, expert_local, capacity, column_count)
    arrived_cols = lax.all_to_all(outgoing, "ep", split_axis=0, concat_axis=0, tiled=True)
    piece_cols = lax.all_gather(arrived_cols, "tp", axis=3, tiled=True)
    gate_add = jnp.einsum("sejd,edf->sejf", piece_cols, w_gate, preferred_element_type=jnp.float32)
    up_add = jnp.einsum("sejd,edf->sejf", piece_cols, w_up, preferred_element_type=jnp.float32)
    inner_act = (jax.nn.silu(gate_add) * up_add).astype(jnp.bfloat16)
    summed = lax.psum_scatter(
        jnp.einsum("sejf,efd->dsej", inner_act, w_down, preferred_element_type=jnp.float32).astype(
            jnp.bfloat16
        ),
        "tp",
        scatter_dimension=0,
        tiled=True,
    )
    returned = lax.all_to_all(summed, "ep", split_axis=1, concat_axis=1, tiled=True)
    flat_back = returned.reshape(column_count, experts_all * capacity)
    picked = jnp.einsum("srk,cs->rkc", pick_table, flat_back, preferred_element_type=jnp.float32)
    moe_rows = jnp.sum(picked * gate_weights[:, :, None], axis=1)
    return (attended, moe_rows.astype(jnp.bfloat16))


def solution(mesh):
    in_specs = (
        P(("ep", "tp"), None, None),
        P(("ep", "tp"), None, None),
        P(),
        P(),
        P(),
        P("ep", None),
        P("ep", None),
        P("ep", None),
        P("ep", None, "tp"),
        P("ep", None, "tp"),
        P("ep", "tp", None),
    )
    out_specs = (P(("ep", "tp"), None, None), P("ep", "tp"))
    return jax.shard_map(local, mesh=mesh, in_specs=in_specs, out_specs=out_specs, check_vma=False)
```

profile of v0, /device:TPU:0, one launch (start us, length us, event | category | flops | bytes accessed | tf_op | source)
XLA Modules:
  0.0 377.8 jit_solution(16641957382146697092)
XLA Ops:
  7.2 0.9 copy.61
  8.4 1.2 reduce-window.6
  10.0 0.7 multiply_add_fusion
  10.8 0.7 fusion.14
  11.6 2.8 convolution_convert_fusion
  14.4 3.7 reshape.88
  18.1 54.8 %all_to_all.10 = bf16[8,3,42,896]{3,2,1,0:T(8,128)(2,1)S(1)} all-to-all(bf16[8,3,42,896]{3,2,1,0:T(8,128)(2,1)} %reshape.88), channel_id=1, replica_groups=mesh['ep'=8,'tp'=4] {'ep'}, dimensions={0} | all-to-all | bytes 3612672 | tf_op jit(solution)/shard_map/all_to_all | solution.py:112
  72.9 1.5 copy.67
  74.5 56.6 %all-gather.2.cloned.1.call-done = bf16[8,3,42,3584]{3,2,0,1:T(8,128)(2,1)} async-done(((bf16[8,3,42,896]{3,2,0,1:T(8,128)(2,1)}), bf16[8,3,42,3584]{3,2,0,1:T(8,128)(2,1)}) %all-gather.2.cloned.1.call-update) | async-done | bytes 7225360 | tf_op jit(solution)/shard_map/all_gather | solution.py:113
  131.1 8.2 %fusion.21 = f32[8,3,42,256]{3,2,0,1:T(8,128)} fusion(bf16[8,3,42,3584]{3,2,0,1:T(8,128)(2,1)} %all-gather.2.cloned.1.call-done, bf16[3,3584,256]{2,1,0:T(8,128)(2,1)} %param.19), kind=kOutput, calls=%fused_computation.23 | convolution fusion | flops 1849688064 | bytes 13762560 | tf_op jit(solution)/shard_map/sejd,edf->sejf/dot_general | solution.py:114
  139.3 14.7 %convert_bitcast_fusion = bf16[3584,8,3,42]{0,3,1,2:T(8,128)(2,1)} fusion(bf16[3,256,3584]{2,1,0:T(8,128)(2,1)} %param.21, bf16[8,3,42,3584]{3,2,0,1:T(8,128)(2,1)} %all-gather.2.cloned.1.call-done, bf16[3,3584,256]{2,1,0:T(8,128)(2,1)} %param.20, f32[8,3,42,256]{3,2,0,1:T(8,128)} %fusion.21), kind=kOutput, calls=%fused_computation.1 | convolution fusion | flops 3704537088 | bytes 26492928 | tf_op jit(solution)/shard_map/sejf,efd->dsej/dot_general | solution.py:118
  154.0 23.3 %copy.75 = bf16[3584,8,3,42]{3,1,2,0:T(8,128)(2,1)} copy(bf16[3584,8,3,42]{0,3,1,2:T(8,128)(2,1)} %convert_bitcast_fusion) | data formatting | bytes 14450688
  177.3 27.4 %reshape.95 = bf16[3584,1008]{1,0:T(8,128)(2,1)} reshape(bf16[3584,3,8,42]{3,2,1,0:T(8,128)(2,1)} %bitcast.98) | data formatting | bytes 14450688
  205.4 0.7 fusion.54
  208.0 62.3 %reduce-scatter.4.cloned.1.call-done = bf16[896,1008]{1,0:T(8,128)(2,1)} async-done(((bf16[3584,1008]{1,0:T(8,128)(2,1)}), bf16[896,1008]{1,0:T(8,128)(2,1)}) %reduce-scatter.4.cloned.1.call-update) | async-done | bytes 1806352
  270.3 8.3 %reshape.96 = bf16[896,3,8,42]{3,2,1,0:T(8,128)(2,1)} reshape(bf16[896,1008]{1,0:T(8,128)(2,1)} %reduce-scatter.4.cloned.1.call-done) | data formatting | bytes 3612672
  278.6 7.8 %copy.68 = bf16[896,8,3,42]{0,3,2,1:T(8,128)(2,1)} copy(bf16[896,8,3,42]{3,1,2,0:T(8,128)(2,1)} %bitcast.99) | data formatting | bytes 3612672 | tf_op jit(solution)/shard_map/reduce_scatter | solution.py:117
  286.3 5.5 %all-to-all-start.1 = ((bf16[896,8,3,42]{0,3,2,1:T(8,128)(2,1)}), bf16[896,8,3,42]{0,3,2,1:T(8,128)(2,1)}, u32[]{:S(2)}, u32[]{:S(2)}) async-start(bf16[896,8,3,42]{0,3,2,1:T(8,128)(2,1)} %copy.68), calls=%async_computation.1 | async-start | bytes 4128768 | tf_op jit(solution)/shard_map/all_to_all | solution.py:125
  291.8 1.0 constant_dynamic-slice_fusion
  293.0 2.1 collective-permute-start
  295.1 22.8 %collective-permute-done = bf16[256,576]{1,0:T(8,128)(2,1)S(1)} collective-permute-done((bf16[256,576]{1,0:T(8,128)(2,1)S(1)}, bf16[256,576]{1,0:T(8,128)(2,1)S(1)}, u32[]{:S(2)}, u32[]{:S(2)}) %collective-permute-start) | collective-permute-done | bytes 294944 | tf_op jit(solution)/shard_map/ppermute | solution.py:20
  318.2 7.7 %copy.58 = bf16[16,256,576]{2,1,0:T(8,128)(2,1)} copy(bf16[16,256,576]{1,2,0:T(8,128)(2,1)} %param.11) | data formatting | bytes 9437184 | tf_op args[0]
  326.7 0.6 dynamic_slice.21
  327.3 6.0 %collective-permute-done.1 = bf16[256,576]{1,0:T(8,128)(2,1)S(1)} collective-permute-done((bf16[256,576]{1,0:T(8,128)(2,1)S(1)}, bf16[256,576]{1,0:T(8,128)(2,1)S(1)}, u32[]{:S(2)}, u32[]{:S(2)}) %collective-permute-start.1) | collective-permute-done | bytes 294944 | tf_op jit(solution)/shard_map/ppermute | solution.py:20
  333.4 8.3 %collective-permute-start.2 = (bf16[256,576]{1,0:T(8,128)(2,1)S(1)}, bf16[256,576]{1,0:T(8,128)(2,1)S(1)}, u32[]{:S(2)}, u32[]{:S(2)}) collective-permute-start(bf16[256,576]{1,0:T(8,128)(2,1)S(1)} %broadcast_select_fusion.1), channel_id=1, source_target_pairs={{0,16},{16,0},{4,20},{20,4},{8,24},{24,8},{12,28},{28,12},{1,17},{... | collective-permute-start | bytes 884744 | tf_op jit(solution)/shard_map/ppermute | solution.py:20
  341.7 1.4 compare_select_fusion
  343.1 10.3 %collective-permute-done.2 = bf16[256,576]{1,0:T(8,128)(2,1)S(1)} collective-permute-done((bf16[256,576]{1,0:T(8,128)(2,1)S(1)}, bf16[256,576]{1,0:T(8,128)(2,1)S(1)}, u32[]{:S(2)}, u32[]{:S(2)}) %collective-permute-start.2) | collective-permute-done | bytes 294944 | tf_op jit(solution)/shard_map/ppermute | solution.py:20
  353.4 0.8 bitcast_dynamic-update-slice_fusion
  354.2 4.5 %fusion.55 = (f32[16,128]{1,0:T(8,128)S(1)}, bf16[16,128,256]{1,2,0:T(8,128)(2,1)}) fusion(pred[16,256]{1,0:T(8,128)(4,1)S(1)} %iota_compare_fusion.4, bf16[16,256,576]{2,1,0:T(8,128)(2,1)} %bitcast_dynamic-update-slice_fusion, bf16[16,128,576]{1,2,0:T(8,128)(2,1)S(1)} %copy-done), kind=kOutput, calls=%fused_computation.60 | convolution fusion | flops 607125760 | bytes 8138752 | tf_op jit(solution)/shard_map/sub | solution.py:49
  358.7 4.7 %divide_convert_fusion = bf16[16,128,512]{2,1,0:T(8,128)(2,1)} fusion(f32[16,128]{1,0:T(8,128)S(1)} %get-tuple-element.4, bf16[16,256,576]{2,1,0:T(8,128)(2,1)} %bitcast_dynamic-update-slice_fusion, bf16[16,128,256]{1,2,0:T(8,128)(2,1)} %get-tuple-element.5), kind=kOutput, calls=%fused_computation.9 | convolution fusion | flops 538968064 | bytes 7348224 | tf_op jit(solution)/shard_map/rhp,rpd->rhd/dot_general | solution.py:52
  363.4 3.9 %reshape.93 = bf16[896,1008,1]{0,1,2:T(8,128)(2,1)} reshape(bf16[896,8,3,42]{0,3,2,1:T(8,128)(2,1)} %all-to-all-done.1) | data formatting | bytes 3612672 | tf_op jit(solution)/shard_map/reshape | solution.py:126
  367.3 3.6 multiply_reduce_fusion
  (30 shorter events, 1.7 us)
Async XLA Ops:
  7.2 347.1 %copy-start = (bf16[16,128,576]{1,2,0:T(8,128)(2,1)S(1)}, bf16[16,128,576]{1,2,0:T(8,128)(2,1)}, u32[]{:S(2)}) copy-start(bf16[16,128,576]{1,2,0:T(8,128)(2,1)} %param.12) | copy-start | bytes 7077892
  7.2 123.9 %all-gather.2.cloned.1.call-start = ((), (), s32[]{:S(2)}) async-start(), calls=%async_computation.3 | async-start | bytes 10321920 | tf_op jit(solution)/shard_map/all_gather | solution.py:113
  74.4 195.8 %reduce-scatter.4.cloned.1.call-start = ((), (), s32[]{:S(2)}) async-start(), calls=%async_computation.4 | async-start | bytes 9175040
  204.7 0.7 copy-start.2
  286.3 77.1 %all-to-all-start.1 = ((bf16[896,8,3,42]{0,3,2,1:T(8,128)(2,1)}), bf16[896,8,3,42]{0,3,2,1:T(8,128)(2,1)}, u32[]{:S(2)}, u32[]{:S(2)}) async-start(bf16[896,8,3,42]{0,3,2,1:T(8,128)(2,1)} %copy.68), calls=%async_computation.1 | async-start | bytes 4128768 | tf_op jit(solution)/shard_map/all_to_all | solution.py:125
  293.0 24.8 %collective-permute-start = (bf16[256,576]{1,0:T(8,128)(2,1)S(1)}, bf16[256,576]{1,0:T(8,128)(2,1)S(1)}, u32[]{:S(2)}, u32[]{:S(2)}) collective-permute-start(bf16[256,576]{1,0:T(8,128)(2,1)S(1)} %bitcast.100), channel_id=1, source_target_pairs={{0,4},{4,0},{8,12},{12,8},{16,20},{20,16},{24,28},{28,24},{1,5},{5... | collective-permute-start | bytes 884744 | tf_op jit(solution)/shard_map/ppermute | solution.py:20
  317.9 8.7 %copy-start.1 = (f32[64,8]{0,1:T(8,128)S(1)}, f32[64,8]{0,1:T(8,128)}, u32[]{:S(2)}) copy-start(f32[64,8]{0,1:T(8,128)} %param.18) | copy-start | bytes 6148
  317.9 8.8 %copy-start.3 = (s32[512]{0:T(512)S(1)}, s32[512]{0:T(512)}, u32[]{:S(2)}) copy-start(s32[512]{0:T(512)} %param.13) | copy-start | bytes 6148
  317.9 15.4 %collective-permute-start.1 = (bf16[256,576]{1,0:T(8,128)(2,1)S(1)}, bf16[256,576]{1,0:T(8,128)(2,1)S(1)}, u32[]{:S(2)}, u32[]{:S(2)}) collective-permute-start(bf16[256,576]{1,0:T(8,128)(2,1)S(1)} %broadcast_select_fusion), channel_id=1, source_target_pairs={{0,8},{8,0},{4,12},{12,4},{16,24},{24,16},{20,28},{28,20},{1,9},{9... | collective-permute-start | bytes 884744 | tf_op jit(solution)/shard_map/ppermute | solution.py:20
  333.4 20.1 %collective-permute-start.2 = (bf16[256,576]{1,0:T(8,128)(2,1)S(1)}, bf16[256,576]{1,0:T(8,128)(2,1)S(1)}, u32[]{:S(2)}, u32[]{:S(2)}) collective-permute-start(bf16[256,576]{1,0:T(8,128)(2,1)S(1)} %broadcast_select_fusion.1), channel_id=1, source_target_pairs={{0,16},{16,0},{4,20},{20,4},{8,24},{24,8},{12,28},{28,12},{1,17},{... | collective-permute-start | bytes 884744 | tf_op jit(solution)/shard_map/ppermute | solution.py:20
Sparse Core Ops, SparseCore 0:
  74.5 56.5 all-gather.1
  204.9 65.3 reduce-scatter.3
where the time goes:
time: 380 us; the launch traced here: 378 us
  waiting for transfers between devices  158 us (42%)
  local copies, waits for them, and re-layouts  87.6 us (23%)
  blocking collectives  54.8 us (14%)
  matrix products  38.6 us (10%)
  between operations  17.4 us (5%)
  starting transfers between devices  16.3 us (4%)
  other arithmetic  5.04 us (1%)
    unnamed x14, local copies, waits for them, and re-layouts  67.7 us
    unnamed x3, waiting for transfers between devices  62.3 us
    all_gather x1, waiting for transfers between devices, local(): piece_cols = lax.all_gather(arrived_cols, 'tp', axis=3, tiled=True)  56.6 us
    all_to_all x1, blocking collectives, local(): lax.all_to_all(outgoing, 'ep', split_axis=0, concat_axis=0, tiled=True)  54.8 us
    ppermute x3, waiting for transfers between devices, from_partner(): return lax.ppermute(block, axis, route)  39.1 us
    dot_general x1, matrix products, local(): jnp.einsum('sejf,efd->dsej', inner_act, w_down, preferred_element_type=jn...  14.7 us
    ppermute x3, starting transfers between devices, from_partner(): return lax.ppermute(block, axis, route)  10.7 us
    dot_general x1, matrix products, local(): jnp.einsum('sejd,edf->sejf', piece_cols, w_gate, preferred_element_type=j...  8.21 us
  transfers between devices with their start and end apart: 6, of which 5 were waited for; matrix products, arithmetic and copies ran while one was open for 6% of the time, Pallas kernels for 0%

commit v1 on v0

v1 whole, which is shorter than its diff:
```python
import functools

import jax
import jax.numpy as jnp
from jax import lax
from jax.experimental import pallas as pl
from jax.experimental.pallas import tpu as pltpu
from jax.sharding import PartitionSpec as P

LAT = 512
SCORE_SCALE = 192.0 ** (-0.5)
MASK_FLOOR = -1e30
ROWS = 256
MIB = 1 << 20


def flip(block, axis, apart):
    count = lax.axis_size(axis)
    return lax.ppermute(block, axis, [(i, i ^ apart) for i in range(count)])


def attend_body(query, page, length):
    scores = (
        lax.dot_general(query, page, (((1,), (1,)), ((), ())), preferred_element_type=jnp.float32)
        * SCORE_SCALE
    )
    live = lax.broadcasted_iota(jnp.int32, scores.shape, 1) < length
    scores = jnp.where(live, scores, MASK_FLOOR)
    top = jnp.max(scores, axis=1, keepdims=True)
    weight = jnp.where(live, jnp.exp(scores - top), 0.0)
    total = jnp.sum(weight, axis=1, keepdims=True)
    blended = jnp.dot(
        weight.astype(jnp.bfloat16), page[:, :LAT], preferred_element_type=jnp.float32
    )
    return (blended / total).astype(jnp.bfloat16)


def attend_kernel(lengths_ref, place_ref, query_ref, page_ref, out_ref):
    length = lengths_ref[place_ref[0] + pl.program_id(0)]
    out_ref[0] = attend_body(query_ref[0], page_ref[0], length)


def attend_all(lengths, place, queries, pages):
    count, heads, width = queries.shape
    slots = pages.shape[1]
    return pl.pallas_call(
        attend_kernel,
        out_shape=jax.ShapeDtypeStruct((count, heads, LAT), jnp.bfloat16),
        grid_spec=pltpu.PrefetchScalarGridSpec(
            num_scalar_prefetch=2,
            grid=(count,),
            in_specs=[
                pl.BlockSpec((1, heads, width), lambda i, *_: (i, 0, 0)),
                pl.BlockSpec((1, slots, width), lambda i, *_: (i, 0, 0)),
            ],
            out_specs=pl.BlockSpec((1, heads, LAT), lambda i, *_: (i, 0, 0)),
        ),
        compiler_params=pltpu.CompilerParams(vmem_limit_bytes=16 * MIB),
        cost_estimate=pl.CostEstimate(
            flops=2 * count * heads * slots * (width + LAT),
            bytes_accessed=2 * count * (heads * (width + LAT) + slots * width),
            transcendentals=count * heads * slots,
        ),
        name="attend_local",
    )(lengths, place, queries, pages)


def attend_traded_kernel(place_ref, query_ref, page_ref, old_ref, out_ref):
    out_ref[0] = attend_body(query_ref[0], page_ref[...], place_ref[1])


def attend_traded(place, queries, page, attended):
    _, heads, width = queries.shape
    slots = page.shape[0]
    return pl.pallas_call(
        attend_traded_kernel,
        out_shape=jax.ShapeDtypeStruct(attended.shape, attended.dtype),
        grid_spec=pltpu.PrefetchScalarGridSpec(
            num_scalar_prefetch=1,
            grid=(1,),
            in_specs=[
                pl.BlockSpec((1, heads, width), lambda i, s: (s[0], 0, 0)),
                pl.BlockSpec((slots, width), lambda i, s: (0, 0)),
                pl.BlockSpec(memory_space=pl.ANY),
            ],
            out_specs=pl.BlockSpec((1, heads, LAT), lambda i, s: (s[0], 0, 0)),
        ),
        input_output_aliases={3: 0},
        compiler_params=pltpu.CompilerParams(vmem_limit_bytes=16 * MIB),
        cost_estimate=pl.CostEstimate(
            flops=2 * heads * slots * (width + LAT),
            bytes_accessed=2 * (heads * (width + LAT) + slots * width),
            transcendentals=heads * slots,
        ),
        name="attend_traded",
    )(place, queries, page, attended)


def experts_kernel(
    ranks_ref,
    gates_ref,
    hidden_ref,
    pieces,
    w_gate_ref,
    w_up_ref,
    inner_ref,
    rows_ref,
    gate_buf,
    up_buf,
    row_sems,
    gate_sems,
    up_sems,
):
    blocks = len(pieces) + 1
    experts, _, units = w_gate_ref.shape
    block_rows = hidden_ref.shape[0]
    quarter = pieces[0][0].shape[1]
    ep_rank, tp_rank = ranks_ref[0], ranks_ref[1]
    copies = [pltpu.make_async_copy(hidden_ref, rows_ref.at[pl.ds(0, block_rows), :], row_sems.at[0, 0])]
    for block in range(1, blocks):
        for part, piece in enumerate(pieces[block - 1]):
            column = pl.multiple_of((tp_rank ^ part) * quarter, 128)
            copies.append(
                pltpu.make_async_copy(
                    piece,
                    rows_ref.at[pl.ds(block * block_rows, block_rows), pl.ds(column, quarter)],
                    row_sems.at[block, part],
                )
            )
    weight_copies = []
    for e in range(experts):
        weight_copies.append(
            (
                pltpu.make_async_copy(w_gate_ref.at[e], gate_buf.at[e], gate_sems.at[e]),
                pltpu.make_async_copy(w_up_ref.at[e], up_buf.at[e], up_sems.at[e]),
            )
        )
    for one in weight_copies[0]:
        one.start()
    for one in copies:
        one.start()
    for pair in weight_copies[1:]:
        for one in pair:
            one.start()
    for one in copies:
        one.wait()
    per = ROWS // block_rows
    for e in range(experts):
        for one in weight_copies[e]:
            one.wait()
        column = ep_rank * experts + e

        @pl.loop(0, blocks * block_rows // ROWS)
        def _(step):
            start = pl.multiple_of(step * ROWS, ROWS)
            rows = rows_ref[pl.ds(start, ROWS), :]
            gate = jnp.dot(rows, gate_buf[e], preferred_element_type=jnp.float32)
            up = jnp.dot(rows, up_buf[e], preferred_element_type=jnp.float32)
            table = jnp.concatenate(
                [gates_ref[ep_rank ^ (step * per + i)] for i in range(per)], axis=0
            )
            lane = lax.broadcasted_iota(jnp.int32, table.shape, 1)
            scale = jnp.sum(jnp.where(lane == column, table, 0.0), axis=1, keepdims=True)
            act = gate / (1.0 + jnp.exp(-gate)) * up * scale
            inner_ref[pl.ds(start, ROWS), e * units : (e + 1) * units] = act.astype(jnp.bfloat16)


def run_experts(ranks, gates, hidden, pieces, w_gate, w_up):
    blocks = len(pieces) + 1
    rows = blocks * hidden.shape[0]
    experts, width, units = w_gate.shape
    anywhere = pl.BlockSpec(memory_space=pl.ANY)
    return pl.pallas_call(
        experts_kernel,
        out_shape=jax.ShapeDtypeStruct((rows, experts * units), jnp.bfloat16),
        in_specs=[
            pl.BlockSpec(memory_space=pltpu.SMEM),
            pl.BlockSpec(memory_space=pltpu.VMEM),
            anywhere,
            jax.tree.map(lambda _: anywhere, pieces),
            anywhere,
            anywhere,
        ],
        out_specs=pl.BlockSpec(memory_space=pltpu.VMEM),
        scratch_shapes=[
            pltpu.VMEM((rows, width), jnp.bfloat16),
            pltpu.VMEM((experts, width, units), jnp.bfloat16),
            pltpu.VMEM((experts, width, units), jnp.bfloat16),
            pltpu.SemaphoreType.DMA((blocks, 4)),
            pltpu.SemaphoreType.DMA((experts,)),
            pltpu.SemaphoreType.DMA((experts,)),
        ],
        compiler_params=pltpu.CompilerParams(vmem_limit_bytes=48 * MIB),
        cost_estimate=pl.CostEstimate(
            flops=4 * rows * width * units * experts,
            bytes_accessed=4 * experts * width * units + 2 * rows * width,
            transcendentals=rows * units * experts,
        ),
        name="experts_inner",
    )(ranks, gates, hidden, pieces, w_gate, w_up)


def down_kernel(blocks, ranks_ref, inner_ref, w_ref, *refs):
    out_refs = refs[-blocks:] if blocks else refs[-1:]
    experts, units, _ = w_ref.shape
    total_rows = inner_ref.shape[0]
    count = len(out_refs)
    each = total_rows // count
    stride = ROWS if each < ROWS else each
    stride = min(stride, ROWS)
    for start in range(0, total_rows, stride):
        value = None
        for e in range(experts):
            term = jnp.dot(
                inner_ref[start : start + stride, e * units : (e + 1) * units],
                w_ref[e],
                preferred_element_type=jnp.float32,
            )
            value = term if value is None else value + term
        if len(refs) > count:
            value = value + refs[0][start : start + stride, :].astype(jnp.float32)
        value = value.astype(jnp.bfloat16)
        if count == 1:
            out_refs[0][start : start + stride, :] = value
        else:
            for i in range(stride // each):
                out_refs[start // each + i][...] = value[i * each : (i + 1) * each]


def run_down(ranks, inner, w_down, part, columns, add=None, blocks=0):
    rows, depth = inner.shape
    experts, units, _ = w_down.shape
    whole = lambda shape: pl.BlockSpec(shape, lambda i, s: (0, 0))
    extra = [] if add is None else [add]
    if blocks:
        out_shape = [jax.ShapeDtypeStruct((rows // blocks, columns), jnp.bfloat16)] * blocks
        out_specs = [whole((rows // blocks, columns))] * blocks
    else:
        out_shape = jax.ShapeDtypeStruct((rows, columns), jnp.bfloat16)
        out_specs = whole((rows, columns))
    return pl.pallas_call(
        functools.partial(down_kernel, blocks),
        out_shape=out_shape,
        grid_spec=pltpu.PrefetchScalarGridSpec(
            num_scalar_prefetch=1,
            grid=(1,),
            in_specs=[
                whole((rows, depth)),
                pl.BlockSpec((experts, units, columns), lambda i, s: (0, 0, s[1] ^ part)),
            ]
            + [whole((rows, columns)) for _ in extra],
            out_specs=out_specs,
        ),
        compiler_params=pltpu.CompilerParams(vmem_limit_bytes=48 * MIB),
        cost_estimate=pl.CostEstimate(
            flops=2 * rows * depth * columns,
            bytes_accessed=2 * (rows * depth + depth * columns + rows * columns * (1 + len(extra))),
            transcendentals=0,
        ),
        name="experts_down",
    )(ranks, inner, w_down, *extra)


def total_of(*terms):
    value = terms[0].astype(jnp.float32)
    for term in terms[1:]:
        value = value + term.astype(jnp.float32)
    return value.astype(jnp.bfloat16)


def local(
    cache_pages,
    queries,
    lengths,
    swap_slot,
    swap_mask,
    hidden,
    expert_ids,
    gate_weights,
    w_gate,
    w_up,
    w_down,
):
    local_count = cache_pages.shape[0]
    groups = lax.axis_size("tp")
    ep_size = lax.axis_size("ep")
    ep_rank = lax.axis_index("ep")
    tp_rank = lax.axis_index("tp")
    device = ep_rank * groups + tp_rank
    mask_value = swap_mask[0]
    partner = jnp.bitwise_xor(ep_rank, mask_value) * groups + tp_rank
    my_slot = swap_slot[device]
    far_length = lengths[partner * local_count + swap_slot[partner]]
    ranks = jnp.stack([ep_rank, tp_rank]).astype(jnp.int32)
    model_width = hidden.shape[1]
    columns = model_width // groups
    expert_local = w_gate.shape[0]
    experts_all = ep_size * expert_local

    chosen = expert_ids[:, :, None] == jnp.arange(experts_all, dtype=jnp.int32)[None, None, :]
    gates = jnp.sum(jnp.where(chosen, gate_weights[:, :, None], 0.0), axis=1)
    gates = lax.all_gather(gates, "ep", axis=0)

    def quarter(part):
        start = jnp.bitwise_xor(tp_rank, part) * columns
        return lax.dynamic_slice_in_dim(hidden, start, columns, 1)

    near = {0: quarter(0)}
    far = {0: quarter(2)}
    pairs = ep_size // 2
    for m in range(1, pairs):
        near[2 * m] = flip(near[0], "ep", 2 * m)
    near[1] = flip(near[0], "ep", 1)
    far[1] = flip(far[0], "ep", 1)
    for m in range(1, pairs):
        far[2 * m] = flip(near[2 * m], "tp", 2)
        near[2 * m + 1] = flip(near[2 * m], "ep", 1)
        if m < pairs - 1:
            far[2 * m + 1] = flip(near[2 * m + 1], "tp", 2)
        else:
            far[2 * m + 1] = flip(far[2 * m], "ep", 1)
    pieces = []
    for k in range(1, ep_size):
        pieces.append((near[k], flip(near[k], "tp", 1), far[k], flip(far[k], "tp", 1)))

    place = jnp.stack([device * local_count]).astype(jnp.int32)
    attended = attend_all(lengths, place, queries, cache_pages)
    page = lax.dynamic_index_in_dim(cache_pages, my_slot, 0, keepdims=False)
    page, _ = lax.optimization_barrier((page, near[2 * pairs - 2]))
    for level in reversed(range(ep_size.bit_length() - 1)):
        swapped = flip(page, "ep", 1 << level)
        bit = jnp.bitwise_and(jnp.right_shift(mask_value, level), 1) == 1
        page = jnp.where(bit, swapped, page)
    traded = jnp.stack([my_slot, far_length]).astype(jnp.int32)
    attended = attend_traded(traded, queries, page, attended)

    inner = run_experts(ranks, gates, hidden, pieces, w_gate, w_up)
    down = functools.partial(run_down, ranks, inner, w_down, columns=columns)
    cross = flip(down(part=3), "tp", 1)
    side = flip(down(part=1), "tp", 1)
    sent = down(part=2, add=cross, blocks=ep_size)
    kept = down(part=0, add=side, blocks=ep_size)

    whole = {}
    for m in [*range(1, pairs), 0]:
        even, odd = 2 * m, 2 * m + 1
        if m == 2:
            here = flip(kept[odd], "ep", 1)
            there = total_of(sent[even], flip(sent[odd], "ep", 1))
            whole[m] = total_of(kept[even], here, flip(there, "tp", 2))
        else:
            over = total_of(kept[odd], flip(sent[odd], "tp", 2))
            whole[m] = total_of(kept[even], flip(sent[even], "tp", 2), flip(over, "ep", 1))
    moe_out = total_of(whole[0], *[flip(whole[m], "ep", 2 * m) for m in range(1, pairs)])
    return attended, moe_out


def solution(mesh):
    in_specs = (
        P(("ep", "tp"), None, None),
        P(("ep", "tp"), None, None),
        P(),
        P(),
        P(),
        P("ep", None),
        P("ep", None),
        P("ep", None),
        P("ep", None, "tp"),
        P("ep", None, "tp"),
        P("ep", "tp", None),
    )
    out_specs = (P(("ep", "tp"), None, None), P("ep", "tp"))
    return jax.shard_map(local, mesh=mesh, in_specs=in_specs, out_specs=out_specs, check_vma=False)
```

time: 380 us -> 199 us (0.52)
  waiting for transfers between devices: 158 us -> 44.6 us
  local copies, waits for them, and re-layouts: 87.6 us -> 28.2 us
  matrix products: 38.6 us -> 0 us
  Pallas kernels: 0 us -> 35.8 us
  starting transfers between devices: 16.3 us -> 47.6 us
  blocking collectives: 54.8 us -> 33.3 us
  between operations: 17.4 us -> 3.85 us
    unnamed x3 -> x0, waiting for transfers between devices: 62.3 us -> none
    all_gather x1 -> x0, waiting for transfers between devices: 56.6 us -> none  [local(): piece_cols = lax.all_gather(arrived_cols, 'tp', axis=3, tiled=True)]
    all_to_all x1 -> x0, blocking collectives: 54.8 us -> none  [local(): lax.all_to_all(outgoing, 'ep', split_axis=0, concat_axis=0, tiled=True)]
    unnamed x14 -> x38, local copies, waits for them, and re-layouts: 67.7 us -> 23.8 us
    ppermute x3 -> x48, starting transfers between devices: 10.7 us -> 47.6 us  [flip(): return lax.ppermute(block, axis, [(i, i ^ apart) for i in range(count)])]
    pallas_call x0 -> x7, Pallas kernels: none -> 35.8 us  [the longest x4 14 us: run_down(): pl.pallas_call(functools.partial(down_kernel, blocks), out_shape=out_shap...]
    dot_general x5 -> x0, matrix products: 34.1 us -> none  [the longest x1 14.7 us: local(): jnp.einsum('sejf,efd->dsej', inner_act, w_down, preferred_element_type=jn...]
    all_gather x0 -> x1, blocking collectives: none -> 33.3 us  [local(): gates = lax.all_gather(gates, 'ep', axis=0)]
  transfers between devices with their start and end apart: 6 -> 48, of which waited for: 5 -> 16; matrix products, arithmetic and copies ran while one was open for 6% -> 9% of each run, Pallas kernels for 0% -> 11%
where the time goes in v1:
time: 199 us; the launch traced here: 198 us
  starting transfers between devices  47.6 us (24%)
  waiting for transfers between devices  44.6 us (22%)
  Pallas kernels  35.8 us (18%)
  blocking collectives  33.3 us (17%)
  local copies, waits for them, and re-layouts  28.2 us (14%)
  other arithmetic  4.88 us (2%)
  between operations  3.85 us (2%)
    ppermute x48, starting transfers between devices, flip(): return lax.ppermute(block, axis, [(i, i ^ apart) for i in range(count)])  47.6 us
    ppermute x48, waiting for transfers between devices, flip(): return lax.ppermute(block, axis, [(i, i ^ apart) for i in range(count)])  44.6 us
    all_gather x1, blocking collectives, local(): gates = lax.all_gather(gates, 'ep', axis=0)  33.3 us
    unnamed x38, local copies, waits for them, and re-layouts  23.8 us
    pallas_call x4, Pallas kernels, run_down(): pl.pallas_call(functools.partial(down_kernel, blocks), out_shape=out_shap...  14 us
    pallas_call x1, Pallas kernels, attend_all(): pl.pallas_call(attend_kernel, out_shape=jax.ShapeDtypeStruct((count, head...  10.3 us
    pallas_call x1, Pallas kernels, run_experts(): pl.pallas_call(experts_kernel, out_shape=jax.ShapeDtypeStruct((rows, expe...  9.79 us
  transfers between devices with their start and end apart: 48, of which 16 were waited for; matrix products, arithmetic and copies ran while one was open for 9% of the time, Pallas kernels for 11%

profile of v1, /device:TPU:0, one launch (start us, length us, event | category | flops | bytes accessed | tf_op | source)
XLA Modules:
  0.0 198.2 jit_solution(2600414749918018482)
XLA Ops:
  1.6 3.0 %collective-permute-start.6 = (bf16[64,896]{1,0:T(8,128)(2,1)S(1)}, bf16[64,896]{1,0:T(8,128)(2,1)S(1)}, u32[]{:S(2)}, u32[]{:S(2)}) collective-permute-start(bf16[64,896]{1,0:T(8,128)(2,1)S(1)} %get-tuple-element.36), channel_id=1, source_target_pairs={{0,4},{4,0},{8,12},{12,8},{16,20},{20,16},{24,28},{28,24},{1,5},{5... | collective-permute-start | bytes 344072 | tf_op jit(solution)/shard_map/ppermute | solution.py:19
  4.6 2.6 %collective-permute-start.16 = (bf16[64,896]{1,0:T(8,128)(2,1)S(1)}, bf16[64,896]{1,0:T(8,128)(2,1)S(1)}, u32[]{:S(2)}, u32[]{:S(2)}) collective-permute-start(bf16[64,896]{1,0:T(8,128)(2,1)S(1)} %get-tuple-element.37), channel_id=1, source_target_pairs={{0,16},{4,20},{8,24},{12,28},{16,0},{20,4},{24,8},{28,12},{1,17},{... | collective-permute-start | bytes 344072 | tf_op jit(solution)/shard_map/ppermute | solution.py:19
  9.3 5.4 %collective-permute-done.16.pieces_3__0_ = bf16[64,896]{1,0:T(8,128)(2,1)S(1)} collective-permute-done((bf16[64,896]{1,0:T(8,128)(2,1)S(1)}, bf16[64,896]{1,0:T(8,128)(2,1)S(1)}, u32[]{:S(2)}, u32[]{:S(2)}) %collective-permute-start.16) | collective-permute-done | bytes 114720 | tf_op jit(solution)/shard_map/ppermute | solution.py:19
  16.3 2.1 %collective-permute-start.12 = (bf16[64,896]{1,0:T(8,128)(2,1)S(1)}, bf16[64,896]{1,0:T(8,128)(2,1)S(1)}, u32[]{:S(2)}, u32[]{:S(2)}) collective-permute-start(bf16[64,896]{1,0:T(8,128)(2,1)S(1)} %collective-permute-done.8.pieces_1__0_), channel_id=1, source_target_pairs={{0,4},{4,0},{8,12},{12,8},{16,20},{20,16},{24,28},{28,24},{1,5},{5... | collective-permute-start | bytes 344072 | tf_op jit(solution)/shard_map/ppermute | solution.py:19
  22.1 2.1 %collective-permute-start.25 = (bf16[64,896]{1,0:T(8,128)(2,1)S(1)}, bf16[64,896]{1,0:T(8,128)(2,1)S(1)}, u32[]{:S(2)}, u32[]{:S(2)}) collective-permute-start(bf16[64,896]{1,0:T(8,128)(2,1)S(1)} %collective-permute-done.pieces_5__0_), channel_id=1, source_target_pairs={{0,2},{1,3},{2,0},{3,1},{4,6},{5,7},{6,4},{7,5},{8,10},{9,11},{10,... | collective-permute-start | bytes 344072 | tf_op jit(solution)/shard_map/ppermute | solution.py:19
  25.5 2.5 %collective-permute-start.14 = (bf16[64,896]{1,0:T(8,128)(2,1)S(1)}, bf16[64,896]{1,0:T(8,128)(2,1)S(1)}, u32[]{:S(2)}, u32[]{:S(2)}) collective-permute-start(bf16[64,896]{1,0:T(8,128)(2,1)S(1)} %collective-permute-done.12.pieces_2__0_), channel_id=1, source_target_pairs={{0,2},{1,3},{2,0},{3,1},{4,6},{5,7},{6,4},{7,5},{8,10},{9,11},{10,... | collective-permute-start | bytes 344072 | tf_op jit(solution)/shard_map/ppermute | solution.py:19
  28.6 1.9 collective-permute-done.22.pieces_4__2_
  33.7 2.5 %collective-permute-done.29.pieces_6__2_ = bf16[64,896]{1,0:T(8,128)(2,1)S(1)} collective-permute-done((bf16[64,896]{1,0:T(8,128)(2,1)S(1)}, bf16[64,896]{1,0:T(8,128)(2,1)S(1)}, u32[]{:S(2)}, u32[]{:S(2)}) %collective-permute-start.29) | collective-permute-done | bytes 114720 | tf_op jit(solution)/shard_map/ppermute | solution.py:19
  36.1 33.3 %all-gather.1 = f32[8,64,24]{1,2,0:T(8,128)} all-gather(f32[1,64,24]{1,2,0:T(8,128)S(1)} %bitcast.14), channel_id=2, replica_groups=mesh['ep'=8,'tp'=4] {'ep'}, dimensions={0}, use_global_device_ids=true | all-gather | bytes 55296 | tf_op jit(solution)/shard_map/all_gather | solution.py:302
  81.1 9.8 %experts_inner.1.inner_ref = bf16[512,768]{1,0:T(8,128)(2,1)S(1)} custom-call(s32[2]{0:T(128)S(1)} %pad_add_fusion.1.ranks_ref, f32[8,64,24]{2,1,0:T(8,128)S(1)} %copy.31.gates_ref, bf16[64,3584]{1,0:T(8,128)(2,1)S(1)} %copy-done.1, bf16[64,896]{1,0:T(8,128)(2,1)S(1)} %collective-permute-done.4.pieces_0__0_, ...), custom_call_target="tpu_custom_call" | custom-call | flops 5637144576 | bytes 14680064 | tf_op jit(solution)/shard_map/experts_inner/pallas_call | solution.py:173
  90.9 3.8 %experts_down.6 = bf16[512,896]{1,0:T(8,128)(2,1)} custom-call(s32[2]{0:T(128)S(1)} %pad_add_fusion.1.ranks_ref, bf16[512,768]{1,0:T(8,128)(2,1)S(1)} %experts_inner.1.inner_ref, bf16[3,256,3584]{2,1,0:T(8,128)(2,1)} %w_ref.7), custom_call_target="tpu_custom_call" | custom-call | flops 704643072 | bytes 3080192 | tf_op jit(solution)/shard_map/experts_down/pallas_call | solution.py:241
  98.9 3.9 %experts_down.4 = bf16[512,896]{1,0:T(8,128)(2,1)} custom-call(s32[2]{0:T(128)S(1)} %pad_add_fusion.1.ranks_ref, bf16[512,768]{1,0:T(8,128)(2,1)S(1)} %experts_inner.1.inner_ref, bf16[3,256,3584]{2,1,0:T(8,128)(2,1)} %w_ref.7), custom_call_target="tpu_custom_call" | custom-call | flops 704643072 | bytes 3080192 | tf_op jit(solution)/shard_map/experts_down/pallas_call | solution.py:241
  103.3 11.9 %collective-permute-done.1 = bf16[256,576]{1,0:T(8,128)(2,1)S(1)} collective-permute-done((bf16[256,576]{1,0:T(8,128)(2,1)S(1)}, bf16[256,576]{1,0:T(8,128)(2,1)S(1)}, u32[]{:S(2)}, u32[]{:S(2)}) %collective-permute-start.1) | collective-permute-done | bytes 294944 | tf_op jit(solution)/shard_map/ppermute | solution.py:19
  115.9 7.7 %copy.29.page_ref = bf16[16,256,576]{2,1,0:T(8,128)(2,1)} copy(bf16[16,256,576]{1,2,0:T(8,128)(2,1)} %param.11) | data formatting | bytes 9437184 | tf_op args[0]
  124.3 3.1 %copy.30.query_ref = bf16[16,128,576]{2,1,0:T(8,128)(2,1)S(1)} copy(bf16[16,128,576]{1,2,0:T(8,128)(2,1)} %param.12) | data formatting | bytes 4718592 | tf_op args[1]
  128.0 2.5 %copy-done = bf16[16,256,576]{2,1,0:T(8,128)(2,1)S(1)} copy-done((bf16[16,256,576]{2,1,0:T(8,128)(2,1)S(1)}, bf16[16,256,576]{2,1,0:T(8,128)(2,1)}, u32[]{:S(2)}) %copy-start) | copy-done | bytes 4718616
  130.4 10.3 %attend_local.1.old_ref = bf16[16,128,512]{2,1,0:T(8,128)(2,1)} custom-call(s32[512]{0:T(512)S(1)} %copy-done.2, s32[1]{0:T(128)} %bitcast.4.place_ref, bf16[16,128,576]{2,1,0:T(8,128)(2,1)S(1)} %copy.30.query_ref, bf16[16,256,576]{2,1,0:T(8,128)(2,1)S(1)} %copy-done), custom_call_target="tpu_custom_call" | custom-call | flops 1140850688 | bytes 9175040 | tf_op jit(solution)/shard_map/attend_local/pallas_call | solution.py:46
  142.0 3.1 %experts_down.7 = (bf16[64,896]{1,0:T(8,128)(2,1)S(1)}, bf16[64,896]{1,0:T(8,128)(2,1)S(1)}, bf16[64,896]{1,0:T(8,128)(2,1)S(1)}, bf16[64,896]{1,0:T(8,128)(2,1)...) custom-call(s32[2]{0:T(128)S(1)} %pad_add_fusion.1.ranks_ref, ...), custom_call_target="tpu_custom_call" | custom-call | flops 704643072 | bytes 3997696 | tf_op jit(solution)/shard_map/experts_down/pallas_call | solution.py:241
  145.2 2.1 %collective-permute-start.34 = (bf16[64,896]{1,0:T(8,128)(2,1)S(1)}, bf16[64,896]{1,0:T(8,128)(2,1)S(1)}, u32[]{:S(2)}, u32[]{:S(2)}) collective-permute-start(bf16[64,896]{1,0:T(8,128)(2,1)S(1)} %get-tuple-element.23), channel_id=1, source_target_pairs={{0,2},{1,3},{2,0},{3,1},{4,6},{5,7},{6,4},{7,5},{8,10},{9,11},{10,... | collective-permute-start | bytes 344072 | tf_op jit(solution)/shard_map/ppermute | solution.py:19
  148.3 2.1 %collective-permute-start.3 = (bf16[256,576]{1,0:T(8,128)(2,1)S(1)}, bf16[256,576]{1,0:T(8,128)(2,1)S(1)}, u32[]{:S(2)}, u32[]{:S(2)}) collective-permute-start(bf16[256,576]{1,0:T(8,128)(2,1)S(1)} %broadcast_select_fusion.1), channel_id=1, source_target_pairs={{0,4},{4,0},{8,12},{12,8},{16,20},{20,16},{24,28},{28,24},{1,5},{5... | collective-permute-start | bytes 884744 | tf_op jit(solution)/shard_map/ppermute | solution.py:19
  150.5 3.1 %experts_down.5 = (bf16[64,896]{1,0:T(8,128)(2,1)S(1)}, bf16[64,896]{1,0:T(8,128)(2,1)S(1)}, bf16[64,896]{1,0:T(8,128)(2,1)S(1)}, bf16[64,896]{1,0:T(8,128)(2,1)...) custom-call(s32[2]{0:T(128)S(1)} %pad_add_fusion.1.ranks_ref, ...), custom_call_target="tpu_custom_call" | custom-call | flops 704643072 | bytes 3997696 | tf_op jit(solution)/shard_map/experts_down/pallas_call | solution.py:241
  157.2 5.7 %collective-permute-done.37 = bf16[64,896]{1,0:T(8,128)(2,1)S(1)} collective-permute-done((bf16[64,896]{1,0:T(8,128)(2,1)S(1)}, bf16[64,896]{1,0:T(8,128)(2,1)S(1)}, u32[]{:S(2)}, u32[]{:S(2)}) %collective-permute-start.37) | collective-permute-done | bytes 114720 | tf_op jit(solution)/shard_map/ppermute | solution.py:19
  162.9 1.7 collective-permute-start.41
  164.6 3.1 %collective-permute-done.41 = bf16[64,896]{1,0:T(8,128)(2,1)S(1)} collective-permute-done((bf16[64,896]{1,0:T(8,128)(2,1)S(1)}, bf16[64,896]{1,0:T(8,128)(2,1)S(1)}, u32[]{:S(2)}, u32[]{:S(2)}) %collective-permute-start.41) | collective-permute-done | bytes 114720 | tf_op jit(solution)/shard_map/ppermute | solution.py:19
  169.1 3.7 %collective-permute-done.45 = bf16[64,896]{1,0:T(8,128)(2,1)S(1)} collective-permute-done((bf16[64,896]{1,0:T(8,128)(2,1)S(1)}, bf16[64,896]{1,0:T(8,128)(2,1)S(1)}, u32[]{:S(2)}, u32[]{:S(2)}) %collective-permute-start.45) | collective-permute-done | bytes 114720 | tf_op jit(solution)/shard_map/ppermute | solution.py:19
  172.8 2.6 %collective-permute-start.38 = (bf16[64,896]{1,0:T(8,128)(2,1)S(1)}, bf16[64,896]{1,0:T(8,128)(2,1)S(1)}, u32[]{:S(2)}, u32[]{:S(2)}) collective-permute-start(bf16[64,896]{1,0:T(8,128)(2,1)S(1)} %add_convert_fusion.6), channel_id=1, source_target_pairs={{0,4},{4,0},{8,12},{12,8},{16,20},{20,16},{24,28},{28,24},{1,5},{5... | collective-permute-start | bytes 344072 | tf_op jit(solution)/shard_map/ppermute | solution.py:19
  176.8 1.8 collective-permute-done.38
  179.5 2.2 %collective-permute-start.35 = (bf16[64,896]{1,0:T(8,128)(2,1)S(1)}, bf16[64,896]{1,0:T(8,128)(2,1)S(1)}, u32[]{:S(2)}, u32[]{:S(2)}) collective-permute-start(bf16[64,896]{1,0:T(8,128)(2,1)S(1)} %add_convert_fusion.8), channel_id=1, source_target_pairs={{0,4},{4,0},{8,12},{12,8},{16,20},{20,16},{24,28},{28,24},{1,5},{5... | collective-permute-start | bytes 344072 | tf_op jit(solution)/shard_map/ppermute | solution.py:19
  183.4 1.7 collective-permute-start.46
  188.2 2.4 %collective-permute-start.43 = (bf16[64,896]{1,0:T(8,128)(2,1)S(1)}, bf16[64,896]{1,0:T(8,128)(2,1)S(1)}, u32[]{:S(2)}, u32[]{:S(2)}) collective-permute-start(bf16[64,896]{1,0:T(8,128)(2,1)S(1)} %add_convert_fusion.3), channel_id=1, source_target_pairs={{0,16},{4,20},{8,24},{12,28},{16,0},{20,4},{24,8},{28,12},{1,17},{... | collective-permute-start | bytes 344072 | tf_op jit(solution)/shard_map/ppermute | solution.py:19
  192.2 1.7 attend_traded.1
  195.1 2.3 %collective-permute-done.47 = bf16[64,896]{1,0:T(8,128)(2,1)S(1)} collective-permute-done((bf16[64,896]{1,0:T(8,128)(2,1)S(1)}, bf16[64,896]{1,0:T(8,128)(2,1)S(1)}, u32[]{:S(2)}, u32[]{:S(2)}) %collective-permute-start.47) | collective-permute-done | bytes 114720 | tf_op jit(solution)/shard_map/ppermute | solution.py:19
  (130 shorter events, 46.6 us)
Async XLA Ops:
  1.6 7.7 %collective-permute-start.6 = (bf16[64,896]{1,0:T(8,128)(2,1)S(1)}, bf16[64,896]{1,0:T(8,128)(2,1)S(1)}, u32[]{:S(2)}, u32[]{:S(2)}) collective-permute-start(bf16[64,896]{1,0:T(8,128)(2,1)S(1)} %get-tuple-element.36), channel_id=1, source_target_pairs={{0,4},{4,0},{8,12},{12,8},{16,20},{20,16},{24,28},{28,24},{1,5},{5... | collective-permute-start | bytes 344072 | tf_op jit(solution)/shard_map/ppermute | solution.py:19
  4.6 10.1 %collective-permute-start.16 = (bf16[64,896]{1,0:T(8,128)(2,1)S(1)}, bf16[64,896]{1,0:T(8,128)(2,1)S(1)}, u32[]{:S(2)}, u32[]{:S(2)}) collective-permute-start(bf16[64,896]{1,0:T(8,128)(2,1)S(1)} %get-tuple-element.37), channel_id=1, source_target_pairs={{0,16},{4,20},{8,24},{12,28},{16,0},{20,4},{24,8},{28,12},{1,17},{... | collective-permute-start | bytes 344072 | tf_op jit(solution)/shard_map/ppermute | solution.py:19
  7.2 7.5 %collective-permute-start.8 = (bf16[64,896]{1,0:T(8,128)(2,1)S(1)}, bf16[64,896]{1,0:T(8,128)(2,1)S(1)}, u32[]{:S(2)}, u32[]{:S(2)}) collective-permute-start(bf16[64,896]{1,0:T(8,128)(2,1)S(1)} %get-tuple-element.37), channel_id=1, source_target_pairs={{0,8},{4,12},{8,0},{12,4},{16,24},{20,28},{24,16},{28,20},{1,9},{5... | collective-permute-start | bytes 344072 | tf_op jit(solution)/shard_map/ppermute | solution.py:19
  8.8 7.5 %collective-permute-start.4 = (bf16[64,896]{1,0:T(8,128)(2,1)S(1)}, bf16[64,896]{1,0:T(8,128)(2,1)S(1)}, u32[]{:S(2)}, u32[]{:S(2)}) collective-permute-start(bf16[64,896]{1,0:T(8,128)(2,1)S(1)} %get-tuple-element.37), channel_id=1, source_target_pairs={{0,4},{4,0},{8,12},{12,8},{16,20},{20,16},{24,28},{28,24},{1,5},{5... | collective-permute-start | bytes 344072 | tf_op jit(solution)/shard_map/ppermute | solution.py:19
  9.3 6.9 %collective-permute-start = (bf16[64,896]{1,0:T(8,128)(2,1)S(1)}, bf16[64,896]{1,0:T(8,128)(2,1)S(1)}, u32[]{:S(2)}, u32[]{:S(2)}) collective-permute-start(bf16[64,896]{1,0:T(8,128)(2,1)S(1)} %get-tuple-element.37), channel_id=1, source_target_pairs={{0,24},{4,28},{8,16},{12,20},{16,8},{20,12},{24,0},{28,4},{1,25},{... | collective-permute-start | bytes 344072 | tf_op jit(solution)/shard_map/ppermute | solution.py:19
  9.3 9.0 %collective-permute-start.7 = (bf16[64,896]{1,0:T(8,128)(2,1)S(1)}, bf16[64,896]{1,0:T(8,128)(2,1)S(1)}, u32[]{:S(2)}, u32[]{:S(2)}) collective-permute-start(bf16[64,896]{1,0:T(8,128)(2,1)S(1)} %collective-permute-done.6.pieces_0__2_), channel_id=1, source_target_pairs={{0,1},{1,0},{2,3},{3,2},{4,5},{5,4},{6,7},{7,6},{8,9},{9,8},{10,11... | collective-permute-start | bytes 344072 | tf_op jit(solution)/shard_map/ppermute | solution.py:19
  16.3 5.8 %collective-permute-start.12 = (bf16[64,896]{1,0:T(8,128)(2,1)S(1)}, bf16[64,896]{1,0:T(8,128)(2,1)S(1)}, u32[]{:S(2)}, u32[]{:S(2)}) collective-permute-start(bf16[64,896]{1,0:T(8,128)(2,1)S(1)} %collective-permute-done.8.pieces_1__0_), channel_id=1, source_target_pairs={{0,4},{4,0},{8,12},{12,8},{16,20},{20,16},{24,28},{28,24},{1,5},{5... | collective-permute-start | bytes 344072 | tf_op jit(solution)/shard_map/ppermute | solution.py:19
  22.1 6.0 %collective-permute-start.25 = (bf16[64,896]{1,0:T(8,128)(2,1)S(1)}, bf16[64,896]{1,0:T(8,128)(2,1)S(1)}, u32[]{:S(2)}, u32[]{:S(2)}) collective-permute-start(bf16[64,896]{1,0:T(8,128)(2,1)S(1)} %collective-permute-done.pieces_5__0_), channel_id=1, source_target_pairs={{0,2},{1,3},{2,0},{3,1},{4,6},{5,7},{6,4},{7,5},{8,10},{9,11},{10,... | collective-permute-start | bytes 344072 | tf_op jit(solution)/shard_map/ppermute | solution.py:19
  24.2 6.4 %collective-permute-start.22 = (bf16[64,896]{1,0:T(8,128)(2,1)S(1)}, bf16[64,896]{1,0:T(8,128)(2,1)S(1)}, u32[]{:S(2)}, u32[]{:S(2)}) collective-permute-start(bf16[64,896]{1,0:T(8,128)(2,1)S(1)} %collective-permute-done.20.pieces_4__0_), channel_id=1, source_target_pairs={{0,2},{1,3},{2,0},{3,1},{4,6},{5,7},{6,4},{7,5},{8,10},{9,11},{10,... | collective-permute-start | bytes 344072 | tf_op jit(solution)/shard_map/ppermute | solution.py:19
  24.5 6.1 %collective-permute-start.21 = (bf16[64,896]{1,0:T(8,128)(2,1)S(1)}, bf16[64,896]{1,0:T(8,128)(2,1)S(1)}, u32[]{:S(2)}, u32[]{:S(2)}) collective-permute-start(bf16[64,896]{1,0:T(8,128)(2,1)S(1)} %collective-permute-done.20.pieces_4__0_), channel_id=1, source_target_pairs={{0,1},{1,0},{2,3},{3,2},{4,5},{5,4},{6,7},{7,6},{8,9},{9,8},{10,11... | collective-permute-start | bytes 344072 | tf_op jit(solution)/shard_map/ppermute | solution.py:19
  25.5 7.4 %collective-permute-start.14 = (bf16[64,896]{1,0:T(8,128)(2,1)S(1)}, bf16[64,896]{1,0:T(8,128)(2,1)S(1)}, u32[]{:S(2)}, u32[]{:S(2)}) collective-permute-start(bf16[64,896]{1,0:T(8,128)(2,1)S(1)} %collective-permute-done.12.pieces_2__0_), channel_id=1, source_target_pairs={{0,2},{1,3},{2,0},{3,1},{4,6},{5,7},{6,4},{7,5},{8,10},{9,11},{10,... | collective-permute-start | bytes 344072 | tf_op jit(solution)/shard_map/ppermute | solution.py:19
  32.6 38.6 %collective-permute-start.26 = (bf16[64,896]{1,0:T(8,128)(2,1)S(1)}, bf16[64,896]{1,0:T(8,128)(2,1)S(1)}, u32[]{:S(2)}, u32[]{:S(2)}) collective-permute-start(bf16[64,896]{1,0:T(8,128)(2,1)S(1)} %collective-permute-done.25.pieces_5__2_), channel_id=1, source_target_pairs={{0,1},{1,0},{2,3},{3,2},{4,5},{5,4},{6,7},{7,6},{8,9},{9,8},{10,11... | collective-permute-start | bytes 344072 | tf_op jit(solution)/shard_map/ppermute | solution.py:19
  32.9 37.7 %collective-permute-start.28 = (bf16[64,896]{1,0:T(8,128)(2,1)S(1)}, bf16[64,896]{1,0:T(8,128)(2,1)S(1)}, u32[]{:S(2)}, u32[]{:S(2)}) collective-permute-start(bf16[64,896]{1,0:T(8,128)(2,1)S(1)} %collective-permute-done.27.pieces_6__0_), channel_id=1, source_target_pairs={{0,1},{1,0},{2,3},{3,2},{4,5},{5,4},{6,7},{7,6},{8,9},{9,8},{10,11... | collective-permute-start | bytes 344072 | tf_op jit(solution)/shard_map/ppermute | solution.py:19
  33.1 38.7 %collective-permute-start.23 = (bf16[64,896]{1,0:T(8,128)(2,1)S(1)}, bf16[64,896]{1,0:T(8,128)(2,1)S(1)}, u32[]{:S(2)}, u32[]{:S(2)}) collective-permute-start(bf16[64,896]{1,0:T(8,128)(2,1)S(1)} %collective-permute-done.22.pieces_4__2_), channel_id=1, source_target_pairs={{0,1},{1,0},{2,3},{3,2},{4,5},{5,4},{6,7},{7,6},{8,9},{9,8},{10,11... | collective-permute-start | bytes 344072 | tf_op jit(solution)/shard_map/ppermute | solution.py:19
  33.4 39.1 %collective-permute-start.15 = (bf16[64,896]{1,0:T(8,128)(2,1)S(1)}, bf16[64,896]{1,0:T(8,128)(2,1)S(1)}, u32[]{:S(2)}, u32[]{:S(2)}) collective-permute-start(bf16[64,896]{1,0:T(8,128)(2,1)S(1)} %collective-permute-done.14.pieces_2__2_), channel_id=1, source_target_pairs={{0,1},{1,0},{2,3},{3,2},{4,5},{5,4},{6,7},{7,6},{8,9},{9,8},{10,11... | collective-permute-start | bytes 344072 | tf_op jit(solution)/shard_map/ppermute | solution.py:19
  36.1 37.0 %collective-permute-start.30 = (bf16[64,896]{1,0:T(8,128)(2,1)S(1)}, bf16[64,896]{1,0:T(8,128)(2,1)S(1)}, u32[]{:S(2)}, u32[]{:S(2)}) collective-permute-start(bf16[64,896]{1,0:T(8,128)(2,1)S(1)} %collective-permute-done.29.pieces_6__2_), channel_id=1, source_target_pairs={{0,1},{1,0},{2,3},{3,2},{4,5},{5,4},{6,7},{7,6},{8,9},{9,8},{10,11... | collective-permute-start | bytes 344072 | tf_op jit(solution)/shard_map/ppermute | solution.py:19
  94.7 47.3 %collective-permute-start.32 = (bf16[512,896]{1,0:T(8,128)(2,1)}, bf16[512,896]{1,0:T(8,128)(2,1)}, u32[]{:S(2)}, u32[]{:S(2)}) collective-permute-start(bf16[512,896]{1,0:T(8,128)(2,1)} %experts_down.6), channel_id=1, source_target_pairs={{0,1},{1,0},{2,3},{3,2},{4,5},{5,4},{6,7},{7,6},{8,9},{9,8},{10,11... | collective-permute-start | bytes 2752520 | tf_op jit(solution)/shard_map/ppermute | solution.py:19
  98.8 16.3 %collective-permute-start.1 = (bf16[256,576]{1,0:T(8,128)(2,1)S(1)}, bf16[256,576]{1,0:T(8,128)(2,1)S(1)}, u32[]{:S(2)}, u32[]{:S(2)}) collective-permute-start(bf16[256,576]{1,0:T(8,128)(2,1)S(1)} %bitcast.12), channel_id=1, source_target_pairs={{0,16},{4,20},{8,24},{12,28},{16,0},{20,4},{24,8},{28,12},{1,17},{... | collective-permute-start | bytes 884744 | tf_op jit(solution)/shard_map/ppermute | solution.py:19
  102.8 47.7 %collective-permute-start.31 = (bf16[512,896]{1,0:T(8,128)(2,1)}, bf16[512,896]{1,0:T(8,128)(2,1)}, u32[]{:S(2)}, u32[]{:S(2)}) collective-permute-start(bf16[512,896]{1,0:T(8,128)(2,1)} %experts_down.4), channel_id=1, source_target_pairs={{0,1},{1,0},{2,3},{3,2},{4,5},{5,4},{6,7},{7,6},{8,9},{9,8},{10,11... | collective-permute-start | bytes 2752520 | tf_op jit(solution)/shard_map/ppermute | solution.py:19
  115.9 31.4 %collective-permute-start.2 = (bf16[256,576]{1,0:T(8,128)(2,1)}, bf16[256,576]{1,0:T(8,128)(2,1)}, u32[]{:S(2)}, u32[]{:S(2)}) collective-permute-start(bf16[256,576]{1,0:T(8,128)(2,1)} %broadcast_select_fusion), channel_id=1, source_target_pairs={{0,8},{4,12},{8,0},{12,4},{16,24},{20,28},{24,16},{28,20},{1,9},{5... | collective-permute-start | bytes 884744 | tf_op jit(solution)/shard_map/ppermute | solution.py:19
  145.2 10.6 %collective-permute-start.34 = (bf16[64,896]{1,0:T(8,128)(2,1)S(1)}, bf16[64,896]{1,0:T(8,128)(2,1)S(1)}, u32[]{:S(2)}, u32[]{:S(2)}) collective-permute-start(bf16[64,896]{1,0:T(8,128)(2,1)S(1)} %get-tuple-element.23), channel_id=1, source_target_pairs={{0,2},{1,3},{2,0},{3,1},{4,6},{5,7},{6,4},{7,5},{8,10},{9,11},{10,... | collective-permute-start | bytes 344072 | tf_op jit(solution)/shard_map/ppermute | solution.py:19
  148.3 42.3 %collective-permute-start.3 = (bf16[256,576]{1,0:T(8,128)(2,1)S(1)}, bf16[256,576]{1,0:T(8,128)(2,1)S(1)}, u32[]{:S(2)}, u32[]{:S(2)}) collective-permute-start(bf16[256,576]{1,0:T(8,128)(2,1)S(1)} %broadcast_select_fusion.1), channel_id=1, source_target_pairs={{0,4},{4,0},{8,12},{12,8},{16,20},{20,16},{24,28},{28,24},{1,5},{5... | collective-permute-start | bytes 884744 | tf_op jit(solution)/shard_map/ppermute | solution.py:19
  153.6 25.9 %collective-permute-start.40 = (bf16[64,896]{1,0:T(8,128)(2,1)S(1)}, bf16[64,896]{1,0:T(8,128)(2,1)S(1)}, u32[]{:S(2)}, u32[]{:S(2)}) collective-permute-start(bf16[64,896]{1,0:T(8,128)(2,1)S(1)} %get-tuple-element.29), channel_id=1, source_target_pairs={{0,4},{4,0},{8,12},{12,8},{16,20},{20,16},{24,28},{28,24},{1,5},{5... | collective-permute-start | bytes 344072 | tf_op jit(solution)/shard_map/ppermute | solution.py:19
  153.7 40.1 %collective-permute-start.33 = (bf16[64,896]{1,0:T(8,128)(2,1)S(1)}, bf16[64,896]{1,0:T(8,128)(2,1)S(1)}, u32[]{:S(2)}, u32[]{:S(2)}) collective-permute-start(bf16[64,896]{1,0:T(8,128)(2,1)S(1)} %get-tuple-element.21), channel_id=1, source_target_pairs={{0,2},{1,3},{2,0},{3,1},{4,6},{5,7},{6,4},{7,5},{8,10},{9,11},{10,... | collective-permute-start | bytes 344072 | tf_op jit(solution)/shard_map/ppermute | solution.py:19
  155.1 20.3 %collective-permute-start.36 = (bf16[64,896]{1,0:T(8,128)(2,1)S(1)}, bf16[64,896]{1,0:T(8,128)(2,1)S(1)}, u32[]{:S(2)}, u32[]{:S(2)}) collective-permute-start(bf16[64,896]{1,0:T(8,128)(2,1)S(1)} %get-tuple-element.25), channel_id=1, source_target_pairs={{0,2},{1,3},{2,0},{3,1},{4,6},{5,7},{6,4},{7,5},{8,10},{9,11},{10,... | collective-permute-start | bytes 344072 | tf_op jit(solution)/shard_map/ppermute | solution.py:19
  155.8 7.1 %collective-permute-start.37 = (bf16[64,896]{1,0:T(8,128)(2,1)S(1)}, bf16[64,896]{1,0:T(8,128)(2,1)S(1)}, u32[]{:S(2)}, u32[]{:S(2)}) collective-permute-start(bf16[64,896]{1,0:T(8,128)(2,1)S(1)} %get-tuple-element.27), channel_id=1, source_target_pairs={{0,2},{1,3},{2,0},{3,1},{4,6},{5,7},{6,4},{7,5},{8,10},{9,11},{10,... | collective-permute-start | bytes 344072 | tf_op jit(solution)/shard_map/ppermute | solution.py:19
  172.8 5.8 %collective-permute-start.38 = (bf16[64,896]{1,0:T(8,128)(2,1)S(1)}, bf16[64,896]{1,0:T(8,128)(2,1)S(1)}, u32[]{:S(2)}, u32[]{:S(2)}) collective-permute-start(bf16[64,896]{1,0:T(8,128)(2,1)S(1)} %add_convert_fusion.6), channel_id=1, source_target_pairs={{0,4},{4,0},{8,12},{12,8},{16,20},{20,16},{24,28},{28,24},{1,5},{5... | collective-permute-start | bytes 344072 | tf_op jit(solution)/shard_map/ppermute | solution.py:19
  175.4 9.7 %collective-permute-start.44 = (bf16[64,896]{1,0:T(8,128)(2,1)S(1)}, bf16[64,896]{1,0:T(8,128)(2,1)S(1)}, u32[]{:S(2)}, u32[]{:S(2)}) collective-permute-start(bf16[64,896]{1,0:T(8,128)(2,1)S(1)} %get-tuple-element.33), channel_id=1, source_target_pairs={{0,2},{1,3},{2,0},{3,1},{4,6},{5,7},{6,4},{7,5},{8,10},{9,11},{10,... | collective-permute-start | bytes 344072 | tf_op jit(solution)/shard_map/ppermute | solution.py:19
  179.5 14.4 %collective-permute-start.35 = (bf16[64,896]{1,0:T(8,128)(2,1)S(1)}, bf16[64,896]{1,0:T(8,128)(2,1)S(1)}, u32[]{:S(2)}, u32[]{:S(2)}) collective-permute-start(bf16[64,896]{1,0:T(8,128)(2,1)S(1)} %add_convert_fusion.8), channel_id=1, source_target_pairs={{0,4},{4,0},{8,12},{12,8},{16,20},{20,16},{24,28},{28,24},{1,5},{5... | collective-permute-start | bytes 344072 | tf_op jit(solution)/shard_map/ppermute | solution.py:19
  185.1 8.7 %collective-permute-start.39 = (bf16[64,896]{1,0:T(8,128)(2,1)S(1)}, bf16[64,896]{1,0:T(8,128)(2,1)S(1)}, u32[]{:S(2)}, u32[]{:S(2)}) collective-permute-start(bf16[64,896]{1,0:T(8,128)(2,1)S(1)} %add_convert_fusion.5), channel_id=1, source_target_pairs={{0,8},{4,12},{8,0},{12,4},{16,24},{20,28},{24,16},{28,20},{1,9},{5... | collective-permute-start | bytes 344072 | tf_op jit(solution)/shard_map/ppermute | solution.py:19
  188.2 6.9 %collective-permute-start.43 = (bf16[64,896]{1,0:T(8,128)(2,1)S(1)}, bf16[64,896]{1,0:T(8,128)(2,1)S(1)}, u32[]{:S(2)}, u32[]{:S(2)}) collective-permute-start(bf16[64,896]{1,0:T(8,128)(2,1)S(1)} %add_convert_fusion.3), channel_id=1, source_target_pairs={{0,16},{4,20},{8,24},{12,28},{16,0},{20,4},{24,8},{28,12},{1,17},{... | collective-permute-start | bytes 344072 | tf_op jit(solution)/shard_map/ppermute | solution.py:19
  190.7 6.8 %collective-permute-start.47 = (bf16[64,896]{1,0:T(8,128)(2,1)S(1)}, bf16[64,896]{1,0:T(8,128)(2,1)S(1)}, u32[]{:S(2)}, u32[]{:S(2)}) collective-permute-start(bf16[64,896]{1,0:T(8,128)(2,1)S(1)} %add_convert_fusion.1), channel_id=1, source_target_pairs={{0,24},{4,28},{8,16},{12,20},{16,8},{20,12},{24,0},{28,4},{1,25},{... | collective-permute-start | bytes 344072 | tf_op jit(solution)/shard_map/ppermute | solution.py:19
  (34 other events, 172.4 us)

commit v2 on v1

v2 whole, which is shorter than its diff:
```python
import functools
import math

import jax
import jax.numpy as jnp
from jax import lax
from jax.experimental import pallas as pl
from jax.experimental.pallas import tpu as pltpu
from jax.sharding import PartitionSpec as P

LAT = 512
SCORE_SCALE = 192.0 ** (-0.5)
MASK_FLOOR = -1e30
ROWS = 256
MIB = 1 << 20


def flip(block, axis, apart):
    count = lax.axis_size(axis)
    return lax.ppermute(block, axis, [(i, i ^ apart) for i in range(count)])


def attend_body(query, page, length):
    scores = (
        lax.dot_general(query, page, (((0,), (0,)), ((), ())), preferred_element_type=jnp.float32)
        * SCORE_SCALE
    )
    live = lax.broadcasted_iota(jnp.int32, scores.shape, 1) < length
    scores = jnp.where(live, scores, MASK_FLOOR)
    top = jnp.max(scores, axis=1, keepdims=True)
    weight = jnp.where(live, jnp.exp(scores - top), 0.0)
    total = jnp.sum(weight, axis=1, keepdims=True)
    blended = lax.dot_general(
        weight.astype(jnp.bfloat16),
        page[:LAT],
        (((1,), (1,)), ((), ())),
        preferred_element_type=jnp.float32,
    )
    return (blended / total).astype(jnp.bfloat16)


def attend_kernel(each, lengths_ref, place_ref, query_ref, page_ref, out_ref):
    first = place_ref[0] + pl.program_id(0) * each
    for i in range(each):
        out_ref[i] = attend_body(query_ref[i], page_ref[i], lengths_ref[first + i])


def attend_all(lengths, place, queries, pages):
    count, width, heads = queries.shape
    slots = pages.shape[2]
    each = math.gcd(count, 4)
    return pl.pallas_call(
        functools.partial(attend_kernel, each),
        out_shape=jax.ShapeDtypeStruct((count, heads, LAT), jnp.bfloat16),
        grid_spec=pltpu.PrefetchScalarGridSpec(
            num_scalar_prefetch=2,
            grid=(count // each,),
            in_specs=[
                pl.BlockSpec((each, width, heads), lambda i, *_: (i, 0, 0)),
                pl.BlockSpec((each, width, slots), lambda i, *_: (i, 0, 0)),
            ],
            out_specs=pl.BlockSpec((each, heads, LAT), lambda i, *_: (i, 0, 0)),
        ),
        compiler_params=pltpu.CompilerParams(vmem_limit_bytes=16 * MIB),
        cost_estimate=pl.CostEstimate(
            flops=2 * count * heads * slots * (width + LAT),
            bytes_accessed=2 * count * (heads * (width + LAT) + slots * width),
            transcendentals=count * heads * slots,
        ),
        name="attend_local",
    )(lengths, place, queries, pages)


def attend_traded_kernel(place_ref, query_ref, page_ref, old_ref, out_ref):
    out_ref[0] = attend_body(query_ref[0], page_ref[...], place_ref[1])


def attend_traded(place, queries, page, attended):
    _, width, heads = queries.shape
    slots = page.shape[1]
    return pl.pallas_call(
        attend_traded_kernel,
        out_shape=jax.ShapeDtypeStruct(attended.shape, attended.dtype),
        grid_spec=pltpu.PrefetchScalarGridSpec(
            num_scalar_prefetch=1,
            grid=(1,),
            in_specs=[
                pl.BlockSpec((1, width, heads), lambda i, s: (s[0], 0, 0)),
                pl.BlockSpec((width, slots), lambda i, s: (0, 0)),
                pl.BlockSpec(memory_space=pl.ANY),
            ],
            out_specs=pl.BlockSpec((1, heads, LAT), lambda i, s: (s[0], 0, 0)),
        ),
        input_output_aliases={3: 0},
        compiler_params=pltpu.CompilerParams(vmem_limit_bytes=16 * MIB),
        cost_estimate=pl.CostEstimate(
            flops=2 * heads * slots * (width + LAT),
            bytes_accessed=2 * (heads * (width + LAT) + slots * width),
            transcendentals=heads * slots,
        ),
        name="attend_traded",
    )(place, queries, page, attended)


def experts_kernel(
    ranks_ref,
    gates,
    hidden_ref,
    pieces,
    w_gate_ref,
    w_up_ref,
    w_down_ref,
    cross_ref,
    side_ref,
    sent,
    kept,
    rows_ref,
    gate_buf,
    up_buf,
    down_buf,
    inner_ref,
    table_ref,
    row_sems,
    weight_sems,
):
    blocks = len(pieces) + 1
    experts, _, units = w_gate_ref.shape
    block_rows = hidden_ref.shape[0]
    quarter = pieces[0][0].shape[1]
    total_rows = blocks * block_rows
    ep_rank, tp_rank = ranks_ref[0], ranks_ref[1]
    copies = [pltpu.make_async_copy(hidden_ref, rows_ref.at[pl.ds(0, block_rows), :], row_sems.at[0, 0])]
    for block in range(1, blocks):
        for part, piece in enumerate(pieces[block - 1]):
            column = pl.multiple_of((tp_rank ^ part) * quarter, 128)
            copies.append(
                pltpu.make_async_copy(
                    piece,
                    rows_ref.at[pl.ds(block * block_rows, block_rows), pl.ds(column, quarter)],
                    row_sems.at[block, part],
                )
            )
    ups, downs = [], []
    for e in range(experts):
        ups.append(
            (
                pltpu.make_async_copy(w_gate_ref.at[e], gate_buf.at[e], weight_sems.at[e, 0]),
                pltpu.make_async_copy(w_up_ref.at[e], up_buf.at[e], weight_sems.at[e, 1]),
            )
        )
        downs.append(
            pltpu.make_async_copy(
                w_down_ref.at[e], down_buf.at[pl.ds(e * units, units), :], weight_sems.at[e, 2]
            )
        )
    for one in ups[0]:
        one.start()
    for one in copies:
        one.start()
    for pair in ups[1:]:
        for one in pair:
            one.start()
    for one in downs:
        one.start()
    lane = lax.broadcasted_iota(jnp.int32, (block_rows, gates[0].shape[2]), 1)
    for pair, gate_ref in enumerate(gates):
        for i in range(2):
            start = (2 * pair + i) * block_rows
            for e in range(experts):
                mine = jnp.where(lane == ep_rank * experts + e, gate_ref[i], 0.0)
                table_ref[start : start + block_rows, e : e + 1] = jnp.sum(
                    mine, axis=1, keepdims=True
                )
    for one in copies:
        one.wait()
    for e in range(experts):
        for one in ups[e]:
            one.wait()

        @pl.loop(0, total_rows // ROWS)
        def _(step):
            start = pl.multiple_of(step * ROWS, ROWS)
            rows = rows_ref[pl.ds(start, ROWS), :]
            gate = jnp.dot(rows, gate_buf[e], preferred_element_type=jnp.float32)
            up = jnp.dot(rows, up_buf[e], preferred_element_type=jnp.float32)
            scale = table_ref[pl.ds(start, ROWS), e : e + 1]
            act = gate / (1.0 + jnp.exp(-gate)) * up * scale
            inner_ref[pl.ds(start, ROWS), e * units : (e + 1) * units] = act.astype(jnp.bfloat16)

    for one in downs:
        one.wait()
    for part, out in ((3, cross_ref), (1, side_ref), (2, sent), (0, kept)):
        column = pl.multiple_of((tp_rank ^ part) * quarter, 128)
        for start in range(0, total_rows, ROWS):
            value = jnp.dot(
                inner_ref[start : start + ROWS, :],
                down_buf[:, pl.ds(column, quarter)],
                preferred_element_type=jnp.float32,
            ).astype(jnp.bfloat16)
            if isinstance(out, (list, tuple)):
                for i in range(ROWS // block_rows):
                    out[start // block_rows + i][...] = value[i * block_rows : (i + 1) * block_rows]
            else:
                out[start : start + ROWS, :] = value


def run_experts(ranks, gates, hidden, pieces, w_gate, w_up, w_down):
    blocks = len(pieces) + 1
    block_rows, width = hidden.shape
    rows = blocks * block_rows
    experts, _, units = w_gate.shape
    quarter = pieces[0][0].shape[1]
    anywhere = pl.BlockSpec(memory_space=pl.ANY)
    vmem = pl.BlockSpec(memory_space=pltpu.VMEM)
    whole = jax.ShapeDtypeStruct((rows, quarter), jnp.bfloat16)
    block = [jax.ShapeDtypeStruct((block_rows, quarter), jnp.bfloat16)] * blocks
    need = 2 * (rows * width + 3 * experts * width * units + 5 * rows * quarter) + rows * 512
    return pl.pallas_call(
        experts_kernel,
        out_shape=(whole, whole, block, block),
        in_specs=[
            pl.BlockSpec(memory_space=pltpu.SMEM),
            jax.tree.map(lambda _: vmem, gates),
            anywhere,
            jax.tree.map(lambda _: anywhere, pieces),
            anywhere,
            anywhere,
            anywhere,
        ],
        out_specs=(vmem, vmem, [vmem] * blocks, [vmem] * blocks),
        scratch_shapes=[
            pltpu.VMEM((rows, width), jnp.bfloat16),
            pltpu.VMEM((experts, width, units), jnp.bfloat16),
            pltpu.VMEM((experts, width, units), jnp.bfloat16),
            pltpu.VMEM((experts * units, width), jnp.bfloat16),
            pltpu.VMEM((rows, experts * units), jnp.bfloat16),
            pltpu.VMEM((rows, 128), jnp.float32),
            pltpu.SemaphoreType.DMA((blocks, 4)),
            pltpu.SemaphoreType.DMA((experts, 3)),
        ],
        compiler_params=pltpu.CompilerParams(vmem_limit_bytes=need + 8 * MIB),
        cost_estimate=pl.CostEstimate(
            flops=6 * rows * width * units * experts,
            bytes_accessed=6 * experts * width * units + 4 * rows * width,
            transcendentals=rows * units * experts,
        ),
        name="experts",
    )(ranks, gates, hidden, pieces, w_gate, w_up, w_down)


def total_of(*terms):
    value = terms[0].astype(jnp.float32)
    for term in terms[1:]:
        value = value + term.astype(jnp.float32)
    return value.astype(jnp.bfloat16)


def local(
    cache_pages,
    queries,
    lengths,
    swap_slot,
    swap_mask,
    hidden,
    expert_ids,
    gate_weights,
    w_gate,
    w_up,
    w_down,
):
    local_count = cache_pages.shape[0]
    groups = lax.axis_size("tp")
    ep_size = lax.axis_size("ep")
    ep_rank = lax.axis_index("ep")
    tp_rank = lax.axis_index("tp")
    device = ep_rank * groups + tp_rank
    mask_value = swap_mask[0]
    partner = jnp.bitwise_xor(ep_rank, mask_value) * groups + tp_rank
    my_slot = swap_slot[device]
    far_length = lengths[partner * local_count + swap_slot[partner]]
    ranks = jnp.stack([ep_rank, tp_rank]).astype(jnp.int32)
    model_width = hidden.shape[1]
    columns = model_width // groups
    expert_local = w_gate.shape[0]
    experts_all = ep_size * expert_local

    chosen = expert_ids[:, :, None] == jnp.arange(experts_all, dtype=jnp.int32)[None, None, :]
    gates = jnp.sum(jnp.where(chosen, gate_weights[:, :, None], 0.0), axis=1)
    gates = jnp.stack([gates, flip(gates, "ep", 1)])
    gates = [gates] + [flip(gates, "ep", 2 * m) for m in range(1, ep_size // 2)]

    def quarter(part):
        start = jnp.bitwise_xor(tp_rank, part) * columns
        return lax.dynamic_slice_in_dim(hidden, start, columns, 1)

    near = {0: quarter(0)}
    far = {0: quarter(2)}
    pairs = ep_size // 2
    for m in range(1, pairs):
        near[2 * m] = flip(near[0], "ep", 2 * m)
    near[1] = flip(near[0], "ep", 1)
    far[1] = flip(far[0], "ep", 1)
    for m in range(1, pairs):
        far[2 * m] = flip(near[2 * m], "tp", 2)
        near[2 * m + 1] = flip(near[2 * m], "ep", 1)
        if m < pairs - 1:
            far[2 * m + 1] = flip(near[2 * m + 1], "tp", 2)
        else:
            far[2 * m + 1] = flip(far[2 * m], "ep", 1)
    pieces = []
    for k in range(1, ep_size):
        pieces.append((near[k], flip(near[k], "tp", 1), far[k], flip(far[k], "tp", 1)))

    cache_pages = jnp.swapaxes(cache_pages, 1, 2)
    queries = jnp.swapaxes(queries, 1, 2)
    place = jnp.stack([device * local_count]).astype(jnp.int32)
    attended = attend_all(lengths, place, queries, cache_pages)
    levels = ep_size.bit_length() - 1

    def page_hop(page, level):
        swapped = flip(page, "ep", 1 << level)
        bit = jnp.bitwise_and(jnp.right_shift(mask_value, level), 1) == 1
        return jnp.where(bit, swapped, page)

    page = lax.dynamic_index_in_dim(cache_pages, my_slot, 0, keepdims=False)
    page = page_hop(page, 0)
    page, near[ep_size - 2] = lax.optimization_barrier((page, near[ep_size - 2]))
    for level in range(levels - 1, 1, -1):
        page = page_hop(page, level)
    ranks, attended, page = lax.optimization_barrier((ranks, attended, page))
    if levels > 1:
        page = page_hop(page, 1)
    traded = jnp.stack([my_slot, far_length]).astype(jnp.int32)
    attended = attend_traded(traded, queries, page, attended)

    cross, side, sent, kept = run_experts(ranks, gates, hidden, pieces, w_gate, w_up, w_down)
    cross = flip(cross, "tp", 1)
    side = flip(side, "tp", 1)
    cross, attended = lax.optimization_barrier((cross, attended))
    rows = hidden.shape[0]

    def block_of(array, k):
        return lax.slice_in_dim(array, k * rows, (k + 1) * rows, axis=0)

    sent = [total_of(one, block_of(cross, k)) for k, one in enumerate(sent)]
    kept = [total_of(one, block_of(side, k)) for k, one in enumerate(kept)]

    whole = {}
    for m in [*range(1, pairs), 0]:
        even, odd = 2 * m, 2 * m + 1
        if m == 2:
            here = flip(kept[odd], "ep", 1)
            there = total_of(sent[even], flip(sent[odd], "ep", 1))
            whole[m] = total_of(kept[even], here, flip(there, "tp", 2))
        else:
            over = total_of(kept[odd], flip(sent[odd], "tp", 2))
            whole[m] = total_of(kept[even], flip(sent[even], "tp", 2), flip(over, "ep", 1))
    moe_out = total_of(whole[0], *[flip(whole[m], "ep", 2 * m) for m in range(1, pairs)])
    return attended, moe_out


def solution(mesh):
    in_specs = (
        P(("ep", "tp"), None, None),
        P(("ep", "tp"), None, None),
        P(),
        P(),
        P(),
        P("ep", None),
        P("ep", None),
        P("ep", None),
        P("ep", None, "tp"),
        P("ep", None, "tp"),
        P("ep", "tp", None),
    )
    out_specs = (P(("ep", "tp"), None, None), P("ep", "tp"))
    return jax.shard_map(local, mesh=mesh, in_specs=in_specs, out_specs=out_specs, check_vma=False)
```

time: 199 us -> 168 us (0.84)
  blocking collectives: 33.3 us -> 0 us
  local copies, waits for them, and re-layouts: 28.2 us -> 50.7 us
  waiting for transfers between devices: 44.6 us -> 28.2 us
  Pallas kernels: 35.8 us -> 21.5 us
  other arithmetic: 4.88 us -> 12.1 us
    all_gather x1 -> x0, blocking collectives: 33.3 us -> none  [local(): gates = lax.all_gather(gates, 'ep', axis=0)]
    unnamed x38 -> x164, local copies, waits for them, and re-layouts: 23.8 us -> 45.9 us
    ppermute x48 -> x52, waiting for transfers between devices: 44.6 us -> 28.2 us  [flip(): return lax.ppermute(block, axis, [(i, i ^ apart) for i in range(count)])]
    pallas_call x6 -> x2, Pallas kernels: 34.1 us -> 19.7 us  [the longest x1 13.2 us: run_experts(): pl.pallas_call(experts_kernel, out_shape=(whole, whole, block, block), in...]
    convert_element_type x8 -> x5, other arithmetic: 0.99 us -> 6.47 us  [total_of(): return value.astype(jnp.bfloat16)]
    dynamic_slice x1 -> x2, local copies, waits for them, and re-layouts: 0.59 us -> 2.73 us  [local(): far_length = lengths[partner * local_count + swap_slot[partner]]]
    ppermute x48 -> x52, starting transfers between devices: 47.6 us -> 49.5 us  [flip(): return lax.ppermute(block, axis, [(i, i ^ apart) for i in range(count)])]
  transfers between devices with their start and end apart: 48 -> 52, of which waited for: 16 -> 13; matrix products, arithmetic and copies ran while one was open for 9% -> 9% of each run, Pallas kernels for 11% -> 5%
where the time goes in v2:
time: 168 us; the launch traced here: 166 us
  local copies, waits for them, and re-layouts  50.7 us (30%)
  starting transfers between devices  49.5 us (29%)
  waiting for transfers between devices  28.2 us (17%)
  Pallas kernels  21.5 us (13%)
  other arithmetic  12.1 us (7%)
  between operations  4.36 us (3%)
    ppermute x52, starting transfers between devices, flip(): return lax.ppermute(block, axis, [(i, i ^ apart) for i in range(count)])  49.5 us
    unnamed x164, local copies, waits for them, and re-layouts  45.9 us
    ppermute x52, waiting for transfers between devices, flip(): return lax.ppermute(block, axis, [(i, i ^ apart) for i in range(count)])  28.2 us
    pallas_call x1, Pallas kernels, run_experts(): pl.pallas_call(experts_kernel, out_shape=(whole, whole, block, block), in...  13.2 us
    pallas_call x1, Pallas kernels, attend_all(): pl.pallas_call(functools.partial(attend_kernel, each), out_shape=jax.Shap...  6.55 us
    convert_element_type x5, other arithmetic, total_of(): return value.astype(jnp.bfloat16)  6.47 us
    select_n x3, other arithmetic, page_hop(): return jnp.where(bit, swapped, page)  3.46 us
  transfers between devices with their start and end apart: 52, of which 13 were waited for; matrix products, arithmetic and copies ran while one was open for 9% of the time, Pallas kernels for 5%

profile of v2, /device:TPU:0, one launch (start us, length us, event | category | flops | bytes accessed | tf_op | source)
XLA Modules:
  0.0 166.3 jit_solution(11952346549627751463)
XLA Ops:
  1.4 3.0 %collective-permute-start.3 = (f32[64,24]{0,1:T(8,128)S(1)}, f32[64,24]{0,1:T(8,128)S(1)}, u32[]{:S(2)}, u32[]{:S(2)}) collective-permute-start(f32[64,24]{0,1:T(8,128)S(1)} %select_reduce_fusion), channel_id=1, source_target_pairs={{0,4},{4,0},{8,12},{12,8},{16,20},{20,16},{24,28},{28,24},{1,5},{5... | collective-permute-start | bytes 18440 | tf_op jit(solution)/shard_map/ppermute | solution.py:20
  5.3 3.7 %collective-permute-start.1 = (bf16[64,896]{1,0:T(8,128)(2,1)S(1)}, bf16[64,896]{1,0:T(8,128)(2,1)S(1)}, u32[]{:S(2)}, u32[]{:S(2)}) collective-permute-start(bf16[64,896]{1,0:T(8,128)(2,1)S(1)} %get-tuple-element.65), channel_id=1, source_target_pairs={{0,24},{4,28},{8,16},{12,20},{16,8},{20,12},{24,0},{28,4},{1,25},{... | collective-permute-start | bytes 344072 | tf_op jit(solution)/shard_map/ppermute | solution.py:20
  9.2 1.7 %collective-permute-start.5 = (f32[2,64,24]{2,1,0:T(8,128)S(1)}, f32[2,64,24]{2,1,0:T(8,128)S(1)}, u32[]{:S(2)}, u32[]{:S(2)}) collective-permute-start(f32[2,64,24]{2,1,0:T(8,128)S(1)} %copy.25.gates_0_), channel_id=1, source_target_pairs={{0,16},{4,20},{8,24},{12,28},{16,0},{20,4},{24,8},{28,12},{1,17},{... | collective-permute-start | bytes 36872 | tf_op jit(solution)/shard_map/ppermute | solution.py:20
  10.9 2.7 %collective-permute-start.6 = (f32[2,64,24]{2,1,0:T(8,128)S(1)}, f32[2,64,24]{2,1,0:T(8,128)S(1)}, u32[]{:S(2)}, u32[]{:S(2)}) collective-permute-start(f32[2,64,24]{2,1,0:T(8,128)S(1)} %copy.25.gates_0_), channel_id=1, source_target_pairs={{0,24},{4,28},{8,16},{12,20},{16,8},{20,12},{24,0},{28,4},{1,25},{... | collective-permute-start | bytes 36872 | tf_op jit(solution)/shard_map/ppermute | solution.py:20
  18.1 1.7 %collective-permute-start.19 = (bf16[64,896]{1,0:T(8,128)(2,1)S(1)}, bf16[64,896]{1,0:T(8,128)(2,1)S(1)}, u32[]{:S(2)}, u32[]{:S(2)}) collective-permute-start(bf16[64,896]{1,0:T(8,128)(2,1)S(1)} %get-tuple-element.65), channel_id=1, source_target_pairs={{0,16},{4,20},{8,24},{12,28},{16,0},{20,4},{24,8},{28,12},{1,17},{... | collective-permute-start | bytes 344072 | tf_op jit(solution)/shard_map/ppermute | solution.py:20
  20.5 1.5 collective-permute-start.7
  23.1 1.5 collective-permute-start.28
  25.6 1.6 collective-permute-start
  27.7 1.5 collective-permute-start.23
  29.8 2.2 %collective-permute-start.13 = (bf16[64,896]{1,0:T(8,128)(2,1)S(1)}, bf16[64,896]{1,0:T(8,128)(2,1)S(1)}, u32[]{:S(2)}, u32[]{:S(2)}) collective-permute-start(bf16[64,896]{1,0:T(8,128)(2,1)S(1)} %collective-permute-done.11.pieces_1__0_), channel_id=1, source_target_pairs={{0,2},{1,3},{2,0},{3,1},{4,6},{5,7},{6,4},{7,5},{8,10},{9,11},{10,... | collective-permute-start | bytes 344072 | tf_op jit(solution)/shard_map/ppermute | solution.py:20
  32.0 5.8 %collective-permute-done.15.pieces_2__0_ = bf16[64,896]{1,0:T(8,128)(2,1)S(1)} collective-permute-done((bf16[64,896]{1,0:T(8,128)(2,1)S(1)}, bf16[64,896]{1,0:T(8,128)(2,1)S(1)}, u32[]{:S(2)}, u32[]{:S(2)}) %collective-permute-start.15) | collective-permute-done | bytes 114720 | tf_op jit(solution)/shard_map/ppermute | solution.py:20
  40.7 1.8 %collective-permute-done.21.pieces_3__2_ = bf16[64,896]{1,0:T(8,128)(2,1)S(1)} collective-permute-done((bf16[64,896]{1,0:T(8,128)(2,1)S(1)}, bf16[64,896]{1,0:T(8,128)(2,1)S(1)}, u32[]{:S(2)}, u32[]{:S(2)}) %collective-permute-start.21) | collective-permute-done | bytes 114720 | tf_op jit(solution)/shard_map/ppermute | solution.py:20
  43.0 1.5 collective-permute-start.32
  46.6 1.7 %broadcast_select_fusion.1 = bf16[576,256]{1,0:T(8,128)(2,1)} fusion(bf16[576,256]{1,0:T(8,128)(2,1)S(1)} %collective-permute-done, pred[]{:T(512)S(6)} %eq.23, bf16[16,256,576]{1,2,0:T(8,128)(2,1)} %param.11, s32[]{:T(128)S(6)} %select_n.46), kind=kLoop, calls=%fused_computation.2 | loop fusion | flops 147456 | bytes 884741 | tf_op jit(solution)/shard_map/jit(_where)/select_n | solution.py:323
  51.9 1.7 %copy-done = bf16[16,128,576]{1,2,0:T(8,128)(2,1)S(1)} copy-done((bf16[16,128,576]{1,2,0:T(8,128)(2,1)S(1)}, bf16[16,128,576]{1,2,0:T(8,128)(2,1)}, u32[]{:S(2)}) %copy-start) | copy-done | bytes 2359320
  53.6 2.3 %copy-done.2 = bf16[16,256,576]{1,2,0:T(8,128)(2,1)S(1)} copy-done((bf16[16,256,576]{1,2,0:T(8,128)(2,1)S(1)}, bf16[16,256,576]{1,2,0:T(8,128)(2,1)}, u32[]{:S(2)}) %copy-start.2) | copy-done | bytes 4718616
  56.6 6.6 %attend_local.1.old_ref = bf16[16,128,512]{2,1,0:T(8,128)(2,1)} custom-call(s32[512]{0:T(512)S(1)} %copy-done.26, s32[1]{0:T(128)} %bitcast.2.place_ref, bf16[16,576,128]{2,1,0:T(8,128)(2,1)S(1)} %bitcast.20, bf16[16,576,256]{2,1,0:T(8,128)(2,1)S(1)} %bitcast.22), custom_call_target="tpu_custom_call" | custom-call | flops 1140850688 | bytes 9175040 | tf_op jit(solution)/shard_map/attend_local/pallas_call | solution.py:52
  67.4 1.7 %broadcast_select_fusion.2 = bf16[576,256]{1,0:T(8,128)(2,1)} fusion(bf16[576,256]{1,0:T(8,128)(2,1)} %collective-permute-done.2, bf16[576,256]{1,0:T(8,128)(2,1)} %broadcast_select_fusion.1, pred[]{:T(512)S(6)} %eq.22), kind=kLoop, calls=%fused_computation.3 | loop fusion | flops 147456 | bytes 884737 | tf_op jit(solution)/shard_map/jit(_where)/select_n | solution.py:323
  70.2 2.6 %copy-done.27 = bf16[3,3584,256]{2,1,0:T(8,128)(2,1)S(1)} copy-done((bf16[3,3584,256]{2,1,0:T(8,128)(2,1)S(1)}, bf16[3,3584,256]{2,1,0:T(8,128)(2,1)}, u32[]{:S(2)}) %copy-start.27) | copy-done | bytes 5505048
  72.8 2.6 %copy-done.28 = bf16[3,3584,256]{2,1,0:T(8,128)(2,1)S(1)} copy-done((bf16[3,3584,256]{2,1,0:T(8,128)(2,1)S(1)}, bf16[3,3584,256]{2,1,0:T(8,128)(2,1)}, u32[]{:S(2)}) %copy-start.28) | copy-done | bytes 5505048
  98.5 13.2 %experts.1 = (bf16[512,896]{1,0:T(8,128)(2,1)}, bf16[512,896]{1,0:T(8,128)(2,1)S(1)}, bf16[64,896]{1,0:T(8,128)(2,1)S(1)}, bf16[64,896]{1,0:T(8,128)(2,1)S(1)}, ...) custom-call(s32[2]{0:T(128)S(1)} %pad_add_fusion.ranks_ref, ...), custom_call_target="tpu_custom_call" | custom-call | flops 8455716864 | bytes 23855104 | tf_op jit(solution)/shard_map/experts/pallas_call | solution.py:218
  123.0 5.7 %collective-permute-done.35 = bf16[576,256]{1,0:T(8,128)(2,1)S(1)} collective-permute-done((bf16[576,256]{1,0:T(8,128)(2,1)}, bf16[576,256]{1,0:T(8,128)(2,1)S(1)}, u32[]{:S(2)}, u32[]{:S(2)}) %collective-permute-start.35) | collective-permute-done | bytes 294944 | tf_op jit(solution)/shard_map/ppermute | solution.py:20
  128.8 1.8 %attend_traded.1 = bf16[16,128,512]{2,1,0:T(8,128)(2,1)} custom-call(s32[2]{0:T(128)S(1)} %pad_add_fusion.1.place_ref, bf16[16,576,128]{2,1,0:T(8,128)(2,1)S(1)} %bitcast.21, bf16[576,256]{1,0:T(8,128)(2,1)S(1)} %broadcast_select_fusion.page_ref, bf16[16,128,512]{2,1,0:T(8,128)(2,1)} %attend_local.1.old_ref), custom_call_target="tpu_custom_call", output_to_operand_aliasing={{}: (3, {})} | custom-call | flops 71303168 | bytes 573440 | tf_op jit(solution)/shard_map/attend_traded/pallas_call | solution.py:81
  141.2 2.5 %collective-permute-done.49 = bf16[64,896]{1,0:T(8,128)(2,1)S(1)} collective-permute-done((bf16[64,896]{1,0:T(8,128)(2,1)S(1)}, bf16[64,896]{1,0:T(8,128)(2,1)S(1)}, u32[]{:S(2)}, u32[]{:S(2)}) %collective-permute-start.49) | collective-permute-done | bytes 114720 | tf_op jit(solution)/shard_map/ppermute | solution.py:20
  144.9 1.6 collective-permute-start.42
  147.0 1.5 collective-permute-start.50
  150.6 1.5 collective-permute-start.39
  152.2 1.6 collective-permute-done.50
  155.4 2.6 %collective-permute-start.47 = (bf16[64,896]{1,0:T(8,128)(2,1)S(1)}, bf16[64,896]{1,0:T(8,128)(2,1)S(1)}, u32[]{:S(2)}, u32[]{:S(2)}) collective-permute-start(bf16[64,896]{1,0:T(8,128)(2,1)S(1)} %get-tuple-element.63), channel_id=1, source_target_pairs={{0,16},{4,20},{8,24},{12,28},{16,0},{20,4},{24,8},{28,12},{1,17},{... | collective-permute-start | bytes 344072 | tf_op jit(solution)/shard_map/ppermute | solution.py:20
  159.8 2.5 %collective-permute-done.47 = bf16[64,896]{1,0:T(8,128)(2,1)S(1)} collective-permute-done((bf16[64,896]{1,0:T(8,128)(2,1)S(1)}, bf16[64,896]{1,0:T(8,128)(2,1)S(1)}, u32[]{:S(2)}, u32[]{:S(2)}) %collective-permute-start.47) | collective-permute-done | bytes 114720 | tf_op jit(solution)/shard_map/ppermute | solution.py:20
  162.3 2.3 %collective-permute-done.51 = bf16[64,896]{1,0:T(8,128)(2,1)S(1)} collective-permute-done((bf16[64,896]{1,0:T(8,128)(2,1)S(1)}, bf16[64,896]{1,0:T(8,128)(2,1)S(1)}, u32[]{:S(2)}, u32[]{:S(2)}) %collective-permute-start.51) | collective-permute-done | bytes 114720 | tf_op jit(solution)/shard_map/ppermute | solution.py:20
  164.7 1.6 add_convert_fusion
  (256 shorter events, 74.5 us)
Async XLA Ops:
  1.4 7.7 %collective-permute-start.3 = (f32[64,24]{0,1:T(8,128)S(1)}, f32[64,24]{0,1:T(8,128)S(1)}, u32[]{:S(2)}, u32[]{:S(2)}) collective-permute-start(f32[64,24]{0,1:T(8,128)S(1)} %select_reduce_fusion), channel_id=1, source_target_pairs={{0,4},{4,0},{8,12},{12,8},{16,20},{20,16},{24,28},{28,24},{1,5},{5... | collective-permute-start | bytes 18440 | tf_op jit(solution)/shard_map/ppermute | solution.py:20
  5.3 17.8 %collective-permute-start.1 = (bf16[64,896]{1,0:T(8,128)(2,1)S(1)}, bf16[64,896]{1,0:T(8,128)(2,1)S(1)}, u32[]{:S(2)}, u32[]{:S(2)}) collective-permute-start(bf16[64,896]{1,0:T(8,128)(2,1)S(1)} %get-tuple-element.65), channel_id=1, source_target_pairs={{0,24},{4,28},{8,16},{12,20},{16,8},{20,12},{24,0},{28,4},{1,25},{... | collective-permute-start | bytes 344072 | tf_op jit(solution)/shard_map/ppermute | solution.py:20
  9.1 8.4 %collective-permute-start.4 = (f32[2,64,24]{2,1,0:T(8,128)S(1)}, f32[2,64,24]{2,1,0:T(8,128)S(1)}, u32[]{:S(2)}, u32[]{:S(2)}) collective-permute-start(f32[2,64,24]{2,1,0:T(8,128)S(1)} %copy.25.gates_0_), channel_id=1, source_target_pairs={{0,8},{4,12},{8,0},{12,4},{16,24},{20,28},{24,16},{28,20},{1,9},{5... | collective-permute-start | bytes 36872 | tf_op jit(solution)/shard_map/ppermute | solution.py:20
  9.2 10.7 %collective-permute-start.5 = (f32[2,64,24]{2,1,0:T(8,128)S(1)}, f32[2,64,24]{2,1,0:T(8,128)S(1)}, u32[]{:S(2)}, u32[]{:S(2)}) collective-permute-start(f32[2,64,24]{2,1,0:T(8,128)S(1)} %copy.25.gates_0_), channel_id=1, source_target_pairs={{0,16},{4,20},{8,24},{12,28},{16,0},{20,4},{24,8},{28,12},{1,17},{... | collective-permute-start | bytes 36872 | tf_op jit(solution)/shard_map/ppermute | solution.py:20
  10.9 11.1 %collective-permute-start.6 = (f32[2,64,24]{2,1,0:T(8,128)S(1)}, f32[2,64,24]{2,1,0:T(8,128)S(1)}, u32[]{:S(2)}, u32[]{:S(2)}) collective-permute-start(f32[2,64,24]{2,1,0:T(8,128)S(1)} %copy.25.gates_0_), channel_id=1, source_target_pairs={{0,24},{4,28},{8,16},{12,20},{16,8},{20,12},{24,0},{28,4},{1,25},{... | collective-permute-start | bytes 36872 | tf_op jit(solution)/shard_map/ppermute | solution.py:20
  13.6 12.1 %collective-permute-start.11 = (bf16[64,896]{1,0:T(8,128)(2,1)S(1)}, bf16[64,896]{1,0:T(8,128)(2,1)S(1)}, u32[]{:S(2)}, u32[]{:S(2)}) collective-permute-start(bf16[64,896]{1,0:T(8,128)(2,1)S(1)} %get-tuple-element.65), channel_id=1, source_target_pairs={{0,8},{4,12},{8,0},{12,4},{16,24},{20,28},{24,16},{28,20},{1,9},{5... | collective-permute-start | bytes 344072 | tf_op jit(solution)/shard_map/ppermute | solution.py:20
  18.1 9.1 %collective-permute-start.19 = (bf16[64,896]{1,0:T(8,128)(2,1)S(1)}, bf16[64,896]{1,0:T(8,128)(2,1)S(1)}, u32[]{:S(2)}, u32[]{:S(2)}) collective-permute-start(bf16[64,896]{1,0:T(8,128)(2,1)S(1)} %get-tuple-element.65), channel_id=1, source_target_pairs={{0,16},{4,20},{8,24},{12,28},{16,0},{20,4},{24,8},{28,12},{1,17},{... | collective-permute-start | bytes 344072 | tf_op jit(solution)/shard_map/ppermute | solution.py:20
  20.5 7.3 %collective-permute-start.7 = (bf16[64,896]{1,0:T(8,128)(2,1)S(1)}, bf16[64,896]{1,0:T(8,128)(2,1)S(1)}, u32[]{:S(2)}, u32[]{:S(2)}) collective-permute-start(bf16[64,896]{1,0:T(8,128)(2,1)S(1)} %get-tuple-element.65), channel_id=1, source_target_pairs={{0,4},{4,0},{8,12},{12,8},{16,20},{20,16},{24,28},{28,24},{1,5},{5... | collective-permute-start | bytes 344072 | tf_op jit(solution)/shard_map/ppermute | solution.py:20
  25.6 20.1 %collective-permute-start = (bf16[576,256]{1,0:T(8,128)(2,1)S(1)}, bf16[576,256]{1,0:T(8,128)(2,1)S(1)}, u32[]{:S(2)}, u32[]{:S(2)}) collective-permute-start(bf16[576,256]{1,0:T(8,128)(2,1)S(1)} %dynamic-slice_bitcast_fusion), channel_id=1, source_target_pairs={{0,4},{4,0},{8,12},{12,8},{16,20},{20,16},{24,28},{28,24},{1,5},{5... | collective-permute-start | bytes 884744 | tf_op jit(solution)/shard_map/ppermute | solution.py:20
  27.2 10.5 %collective-permute-start.15 = (bf16[64,896]{1,0:T(8,128)(2,1)S(1)}, bf16[64,896]{1,0:T(8,128)(2,1)S(1)}, u32[]{:S(2)}, u32[]{:S(2)}) collective-permute-start(bf16[64,896]{1,0:T(8,128)(2,1)S(1)} %collective-permute-done.11.pieces_1__0_), channel_id=1, source_target_pairs={{0,4},{4,0},{8,12},{12,8},{16,20},{20,16},{24,28},{28,24},{1,5},{5... | collective-permute-start | bytes 344072 | tf_op jit(solution)/shard_map/ppermute | solution.py:20
  27.7 11.2 %collective-permute-start.23 = (bf16[64,896]{1,0:T(8,128)(2,1)S(1)}, bf16[64,896]{1,0:T(8,128)(2,1)S(1)}, u32[]{:S(2)}, u32[]{:S(2)}) collective-permute-start(bf16[64,896]{1,0:T(8,128)(2,1)S(1)} %collective-permute-done.19.pieces_3__0_), channel_id=1, source_target_pairs={{0,4},{4,0},{8,12},{12,8},{16,20},{20,16},{24,28},{28,24},{1,5},{5... | collective-permute-start | bytes 344072 | tf_op jit(solution)/shard_map/ppermute | solution.py:20
  29.2 10.9 %collective-permute-start.30 = (bf16[64,896]{1,0:T(8,128)(2,1)S(1)}, bf16[64,896]{1,0:T(8,128)(2,1)S(1)}, u32[]{:S(2)}, u32[]{:S(2)}) collective-permute-start(bf16[64,896]{1,0:T(8,128)(2,1)S(1)} %collective-permute-done.1.pieces_5__0_), channel_id=1, source_target_pairs={{0,4},{4,0},{8,12},{12,8},{16,20},{20,16},{24,28},{28,24},{1,5},{5... | collective-permute-start | bytes 344072 | tf_op jit(solution)/shard_map/ppermute | solution.py:20
  29.8 10.4 %collective-permute-start.13 = (bf16[64,896]{1,0:T(8,128)(2,1)S(1)}, bf16[64,896]{1,0:T(8,128)(2,1)S(1)}, u32[]{:S(2)}, u32[]{:S(2)}) collective-permute-start(bf16[64,896]{1,0:T(8,128)(2,1)S(1)} %collective-permute-done.11.pieces_1__0_), channel_id=1, source_target_pairs={{0,2},{1,3},{2,0},{3,1},{4,6},{5,7},{6,4},{7,5},{8,10},{9,11},{10,... | collective-permute-start | bytes 344072 | tf_op jit(solution)/shard_map/ppermute | solution.py:20
  48.3 18.7 %collective-permute-start.2 = (bf16[576,256]{1,0:T(8,128)(2,1)}, bf16[576,256]{1,0:T(8,128)(2,1)}, u32[]{:S(2)}, u32[]{:S(2)}) collective-permute-start(bf16[576,256]{1,0:T(8,128)(2,1)} %broadcast_select_fusion.1), channel_id=1, source_target_pairs={{0,16},{4,20},{8,24},{12,28},{16,0},{20,4},{24,8},{28,12},{1,17},{... | collective-permute-start | bytes 884744 | tf_op jit(solution)/shard_map/ppermute | solution.py:20
  49.0 14.4 %collective-permute-start.29 = (bf16[64,896]{1,0:T(8,128)(2,1)S(1)}, bf16[64,896]{1,0:T(8,128)(2,1)S(1)}, u32[]{:S(2)}, u32[]{:S(2)}) collective-permute-start(bf16[64,896]{1,0:T(8,128)(2,1)S(1)} %collective-permute-done.28.pieces_5__2_), channel_id=1, source_target_pairs={{0,1},{1,0},{2,3},{3,2},{4,5},{5,4},{6,7},{7,6},{8,9},{9,8},{10,11... | collective-permute-start | bytes 344072 | tf_op jit(solution)/shard_map/ppermute | solution.py:20
  49.0 15.5 %collective-permute-start.16 = (bf16[64,896]{1,0:T(8,128)(2,1)S(1)}, bf16[64,896]{1,0:T(8,128)(2,1)S(1)}, u32[]{:S(2)}, u32[]{:S(2)}) collective-permute-start(bf16[64,896]{1,0:T(8,128)(2,1)S(1)} %collective-permute-done.15.pieces_2__0_), channel_id=1, source_target_pairs={{0,1},{1,0},{2,3},{3,2},{4,5},{5,4},{6,7},{7,6},{8,9},{9,8},{10,11... | collective-permute-start | bytes 344072 | tf_op jit(solution)/shard_map/ppermute | solution.py:20
  50.6 14.6 %collective-permute-start.24 = (bf16[64,896]{1,0:T(8,128)(2,1)S(1)}, bf16[64,896]{1,0:T(8,128)(2,1)S(1)}, u32[]{:S(2)}, u32[]{:S(2)}) collective-permute-start(bf16[64,896]{1,0:T(8,128)(2,1)S(1)} %collective-permute-done.23.pieces_4__0_), channel_id=1, source_target_pairs={{0,1},{1,0},{2,3},{3,2},{4,5},{5,4},{6,7},{7,6},{8,9},{9,8},{10,11... | collective-permute-start | bytes 344072 | tf_op jit(solution)/shard_map/ppermute | solution.py:20
  51.9 14.4 %collective-permute-start.31 = (bf16[64,896]{1,0:T(8,128)(2,1)S(1)}, bf16[64,896]{1,0:T(8,128)(2,1)S(1)}, u32[]{:S(2)}, u32[]{:S(2)}) collective-permute-start(bf16[64,896]{1,0:T(8,128)(2,1)S(1)} %collective-permute-done.30.pieces_6__0_), channel_id=1, source_target_pairs={{0,1},{1,0},{2,3},{3,2},{4,5},{5,4},{6,7},{7,6},{8,9},{9,8},{10,11... | collective-permute-start | bytes 344072 | tf_op jit(solution)/shard_map/ppermute | solution.py:20
  119.1 11.5 %collective-permute-start.34 = (bf16[512,896]{1,0:T(8,128)(2,1)}, bf16[512,896]{1,0:T(8,128)(2,1)}, u32[]{:S(2)}, u32[]{:S(2)}) collective-permute-start(bf16[512,896]{1,0:T(8,128)(2,1)} %get-tuple-element.28), channel_id=1, source_target_pairs={{0,1},{1,0},{2,3},{3,2},{4,5},{5,4},{6,7},{7,6},{8,9},{9,8},{10,11... | collective-permute-start | bytes 2752520 | tf_op jit(solution)/shard_map/ppermute | solution.py:20
  119.1 9.6 %collective-permute-start.35 = (bf16[576,256]{1,0:T(8,128)(2,1)}, bf16[576,256]{1,0:T(8,128)(2,1)S(1)}, u32[]{:S(2)}, u32[]{:S(2)}) collective-permute-start(bf16[576,256]{1,0:T(8,128)(2,1)} %broadcast_select_fusion.2), channel_id=1, source_target_pairs={{0,8},{4,12},{8,0},{12,4},{16,24},{20,28},{24,16},{28,20},{1,9},{5... | collective-permute-start | bytes 884744 | tf_op jit(solution)/shard_map/ppermute | solution.py:20
  121.2 17.9 %collective-permute-start.36 = (bf16[512,896]{1,0:T(8,128)(2,1)}, bf16[512,896]{1,0:T(8,128)(2,1)}, u32[]{:S(2)}, u32[]{:S(2)}) collective-permute-start(bf16[512,896]{1,0:T(8,128)(2,1)} %copy-done.29), channel_id=1, source_target_pairs={{0,1},{1,0},{2,3},{3,2},{4,5},{5,4},{6,7},{7,6},{8,9},{9,8},{10,11... | collective-permute-start | bytes 2752520 | tf_op jit(solution)/shard_map/ppermute | solution.py:20
  132.7 7.3 %collective-permute-start.38 = (bf16[64,896]{1,0:T(8,128)(2,1)S(1)}, bf16[64,896]{1,0:T(8,128)(2,1)S(1)}, u32[]{:S(2)}, u32[]{:S(2)}) collective-permute-start(bf16[64,896]{1,0:T(8,128)(2,1)S(1)} %get-tuple-element.56), channel_id=1, source_target_pairs={{0,2},{1,3},{2,0},{3,1},{4,6},{5,7},{6,4},{7,5},{8,10},{9,11},{10,... | collective-permute-start | bytes 344072 | tf_op jit(solution)/shard_map/ppermute | solution.py:20
  133.9 7.3 %collective-permute-start.41 = (bf16[64,896]{1,0:T(8,128)(2,1)S(1)}, bf16[64,896]{1,0:T(8,128)(2,1)S(1)}, u32[]{:S(2)}, u32[]{:S(2)}) collective-permute-start(bf16[64,896]{1,0:T(8,128)(2,1)S(1)} %get-tuple-element.54), channel_id=1, source_target_pairs={{0,2},{1,3},{2,0},{3,1},{4,6},{5,7},{6,4},{7,5},{8,10},{9,11},{10,... | collective-permute-start | bytes 344072 | tf_op jit(solution)/shard_map/ppermute | solution.py:20
  134.7 9.0 %collective-permute-start.49 = (bf16[64,896]{1,0:T(8,128)(2,1)S(1)}, bf16[64,896]{1,0:T(8,128)(2,1)S(1)}, u32[]{:S(2)}, u32[]{:S(2)}) collective-permute-start(bf16[64,896]{1,0:T(8,128)(2,1)S(1)} %get-tuple-element.51), channel_id=1, source_target_pairs={{0,2},{1,3},{2,0},{3,1},{4,6},{5,7},{6,4},{7,5},{8,10},{9,11},{10,... | collective-permute-start | bytes 344072 | tf_op jit(solution)/shard_map/ppermute | solution.py:20
  136.9 10.1 %collective-permute-start.40 = (bf16[64,896]{1,0:T(8,128)(2,1)S(1)}, bf16[64,896]{1,0:T(8,128)(2,1)S(1)}, u32[]{:S(2)}, u32[]{:S(2)}) collective-permute-start(bf16[64,896]{1,0:T(8,128)(2,1)S(1)} %get-tuple-element.55), channel_id=1, source_target_pairs={{0,2},{1,3},{2,0},{3,1},{4,6},{5,7},{6,4},{7,5},{8,10},{9,11},{10,... | collective-permute-start | bytes 344072 | tf_op jit(solution)/shard_map/ppermute | solution.py:20
  139.1 9.4 %collective-permute-start.48 = (bf16[64,896]{1,0:T(8,128)(2,1)S(1)}, bf16[64,896]{1,0:T(8,128)(2,1)S(1)}, u32[]{:S(2)}, u32[]{:S(2)}) collective-permute-start(bf16[64,896]{1,0:T(8,128)(2,1)S(1)} %get-tuple-element.52), channel_id=1, source_target_pairs={{0,2},{1,3},{2,0},{3,1},{4,6},{5,7},{6,4},{7,5},{8,10},{9,11},{10,... | collective-permute-start | bytes 344072 | tf_op jit(solution)/shard_map/ppermute | solution.py:20
  140.0 10.7 %collective-permute-start.46 = (bf16[64,896]{1,0:T(8,128)(2,1)S(1)}, bf16[64,896]{1,0:T(8,128)(2,1)S(1)}, u32[]{:S(2)}, u32[]{:S(2)}) collective-permute-start(bf16[64,896]{1,0:T(8,128)(2,1)S(1)} %add_convert_fusion.8), channel_id=1, source_target_pairs={{0,2},{1,3},{2,0},{3,1},{4,6},{5,7},{6,4},{7,5},{8,10},{9,11},{10,... | collective-permute-start | bytes 344072 | tf_op jit(solution)/shard_map/ppermute | solution.py:20
  144.9 7.2 %collective-permute-start.42 = (bf16[64,896]{1,0:T(8,128)(2,1)S(1)}, bf16[64,896]{1,0:T(8,128)(2,1)S(1)}, u32[]{:S(2)}, u32[]{:S(2)}) collective-permute-start(bf16[64,896]{1,0:T(8,128)(2,1)S(1)} %get-tuple-element.60), channel_id=1, source_target_pairs={{0,4},{4,0},{8,12},{12,8},{16,20},{20,16},{24,28},{28,24},{1,5},{5... | collective-permute-start | bytes 344072 | tf_op jit(solution)/shard_map/ppermute | solution.py:20
  147.0 6.7 %collective-permute-start.50 = (bf16[64,896]{1,0:T(8,128)(2,1)S(1)}, bf16[64,896]{1,0:T(8,128)(2,1)S(1)}, u32[]{:S(2)}, u32[]{:S(2)}) collective-permute-start(bf16[64,896]{1,0:T(8,128)(2,1)S(1)} %get-tuple-element.58), channel_id=1, source_target_pairs={{0,4},{4,0},{8,12},{12,8},{16,20},{20,16},{24,28},{28,24},{1,5},{5... | collective-permute-start | bytes 344072 | tf_op jit(solution)/shard_map/ppermute | solution.py:20
  148.5 10.9 %collective-permute-start.37 = (bf16[64,896]{1,0:T(8,128)(2,1)S(1)}, bf16[64,896]{1,0:T(8,128)(2,1)S(1)}, u32[]{:S(2)}, u32[]{:S(2)}) collective-permute-start(bf16[64,896]{1,0:T(8,128)(2,1)S(1)} %get-tuple-element.50), channel_id=1, source_target_pairs={{0,2},{1,3},{2,0},{3,1},{4,6},{5,7},{6,4},{7,5},{8,10},{9,11},{10,... | collective-permute-start | bytes 344072 | tf_op jit(solution)/shard_map/ppermute | solution.py:20
  150.6 8.7 %collective-permute-start.39 = (bf16[64,896]{1,0:T(8,128)(2,1)S(1)}, bf16[64,896]{1,0:T(8,128)(2,1)S(1)}, u32[]{:S(2)}, u32[]{:S(2)}) collective-permute-start(bf16[64,896]{1,0:T(8,128)(2,1)S(1)} %get-tuple-element.57), channel_id=1, source_target_pairs={{0,4},{4,0},{8,12},{12,8},{16,20},{20,16},{24,28},{28,24},{1,5},{5... | collective-permute-start | bytes 344072 | tf_op jit(solution)/shard_map/ppermute | solution.py:20
  155.4 6.9 %collective-permute-start.47 = (bf16[64,896]{1,0:T(8,128)(2,1)S(1)}, bf16[64,896]{1,0:T(8,128)(2,1)S(1)}, u32[]{:S(2)}, u32[]{:S(2)}) collective-permute-start(bf16[64,896]{1,0:T(8,128)(2,1)S(1)} %get-tuple-element.63), channel_id=1, source_target_pairs={{0,16},{4,20},{8,24},{12,28},{16,0},{20,4},{24,8},{28,12},{1,17},{... | collective-permute-start | bytes 344072 | tf_op jit(solution)/shard_map/ppermute | solution.py:20
  (102 other events, 859.7 us)

commit v3 on v2

v3 whole, which is shorter than its diff:
```python
import functools
import math

import jax
import jax.numpy as jnp
from jax import lax
from jax.experimental import pallas as pl
from jax.experimental.pallas import tpu as pltpu
from jax.sharding import PartitionSpec as P

LAT = 512
SCORE_SCALE = 192.0 ** (-0.5)
MASK_FLOOR = -1e30
ROWS = 256
MIB = 1 << 20


def flip(block, axis, apart):
    count = lax.axis_size(axis)
    return lax.ppermute(block, axis, [(i, i ^ apart) for i in range(count)])


def attend_body(query, page, length):
    scores = (
        lax.dot_general(query, page, (((0,), (0,)), ((), ())), preferred_element_type=jnp.float32)
        * SCORE_SCALE
    )
    live = lax.broadcasted_iota(jnp.int32, scores.shape, 1) < length
    scores = jnp.where(live, scores, MASK_FLOOR)
    top = jnp.max(scores, axis=1, keepdims=True)
    weight = jnp.where(live, jnp.exp(scores - top), 0.0)
    total = jnp.sum(weight, axis=1, keepdims=True)
    blended = lax.dot_general(
        weight.astype(jnp.bfloat16),
        page[:LAT],
        (((1,), (1,)), ((), ())),
        preferred_element_type=jnp.float32,
    )
    return (blended / total).astype(jnp.bfloat16)


def attend_kernel(each, lengths_ref, place_ref, query_ref, page_ref, out_ref):
    first = place_ref[0] + pl.program_id(0) * each
    for i in range(each):
        out_ref[i] = attend_body(query_ref[i], page_ref[i], lengths_ref[first + i])


def attend_all(lengths, place, queries, pages):
    count, width, heads = queries.shape
    slots = pages.shape[2]
    each = math.gcd(count, 4)
    return pl.pallas_call(
        functools.partial(attend_kernel, each),
        out_shape=jax.ShapeDtypeStruct((count, heads, LAT), jnp.bfloat16),
        grid_spec=pltpu.PrefetchScalarGridSpec(
            num_scalar_prefetch=2,
            grid=(count // each,),
            in_specs=[
                pl.BlockSpec((each, width, heads), lambda i, *_: (i, 0, 0)),
                pl.BlockSpec((each, width, slots), lambda i, *_: (i, 0, 0)),
            ],
            out_specs=pl.BlockSpec((each, heads, LAT), lambda i, *_: (i, 0, 0)),
        ),
        compiler_params=pltpu.CompilerParams(vmem_limit_bytes=16 * MIB),
        cost_estimate=pl.CostEstimate(
            flops=2 * count * heads * slots * (width + LAT),
            bytes_accessed=2 * count * (heads * (width + LAT) + slots * width),
            transcendentals=count * heads * slots,
        ),
        name="attend_local",
    )(lengths, place, queries, pages)


def attend_traded_kernel(place_ref, query_ref, page_ref, old_ref, out_ref):
    out_ref[0] = attend_body(query_ref[0], page_ref[...], place_ref[1])


def attend_traded(place, queries, page, attended):
    _, width, heads = queries.shape
    slots = page.shape[1]
    return pl.pallas_call(
        attend_traded_kernel,
        out_shape=jax.ShapeDtypeStruct(attended.shape, attended.dtype),
        grid_spec=pltpu.PrefetchScalarGridSpec(
            num_scalar_prefetch=1,
            grid=(1,),
            in_specs=[
                pl.BlockSpec((1, width, heads), lambda i, s: (s[0], 0, 0)),
                pl.BlockSpec((width, slots), lambda i, s: (0, 0)),
                pl.BlockSpec(memory_space=pl.ANY),
            ],
            out_specs=pl.BlockSpec((1, heads, LAT), lambda i, s: (s[0], 0, 0)),
        ),
        input_output_aliases={3: 0},
        compiler_params=pltpu.CompilerParams(vmem_limit_bytes=16 * MIB),
        cost_estimate=pl.CostEstimate(
            flops=2 * heads * slots * (width + LAT),
            bytes_accessed=2 * (heads * (width + LAT) + slots * width),
            transcendentals=heads * slots,
        ),
        name="attend_traded",
    )(place, queries, page, attended)


def experts_kernel(
    order,
    ranks_ref,
    gates,
    hidden_ref,
    pieces,
    w_gate_ref,
    w_up_ref,
    w_down_ref,
    cross_ref,
    side_ref,
    sent_ref,
    kept_ref,
    rows_ref,
    gate_buf,
    up_buf,
    down_buf,
    inner_ref,
    table_ref,
    row_sems,
    up_sems,
    down_sems,
):
    experts, _, units = w_gate_ref.shape
    block_rows, width = hidden_ref.shape
    total_rows = rows_ref.shape[0]
    quarter = kept_ref.shape[1]
    ep_rank, tp_rank = ranks_ref[0], ranks_ref[1]

    def columns_of(part):
        return pl.ds(pl.multiple_of((tp_rank ^ part) * quarter, 128), quarter)

    copies = [(hidden_ref, rows_ref.at[pl.ds(0, block_rows), :])]
    for start, parts, piece in pieces:
        rows = pl.ds(start * block_rows, piece.shape[0])
        for i, part in enumerate(parts):
            copies.append(
                (piece.at[:, pl.ds(i * quarter, quarter)], rows_ref.at[rows, columns_of(part)])
            )
    copies = [
        pltpu.make_async_copy(source, target, row_sems.at[i])
        for i, (source, target) in enumerate(copies)
    ]

    def up_copies(e):
        slot = e % 2
        return (
            pltpu.make_async_copy(w_gate_ref.at[e], gate_buf.at[slot], up_sems.at[slot, 0]),
            pltpu.make_async_copy(w_up_ref.at[e], up_buf.at[slot], up_sems.at[slot, 1]),
        )

    parts = (3, 1, 2, 0)
    downs = [
        pltpu.make_async_copy(
            w_down_ref.at[e, :, columns_of(part)],
            down_buf.at[i, pl.ds(e * units, units), :],
            down_sems.at[i, e],
        )
        for i, part in enumerate(parts)
        for e in range(experts)
    ]
    for one in up_copies(0):
        one.start()
    for one in copies:
        one.start()
    for e in range(1, min(2, experts)):
        for one in up_copies(e):
            one.start()
    for one in downs:
        one.start()
    lane = lax.broadcasted_iota(jnp.int32, (block_rows, gates[0].shape[2]), 1)
    for position, block in enumerate(order):
        start = position * block_rows
        for e in range(experts):
            mine = jnp.where(lane == ep_rank * experts + e, gates[block // 2][block % 2], 0.0)
            table_ref[start : start + block_rows, e : e + 1] = jnp.sum(mine, axis=1, keepdims=True)
    for one in copies:
        one.wait()
    for e in range(experts):
        slot = e % 2
        for one in up_copies(e):
            one.wait()

        @pl.loop(0, total_rows // ROWS)
        def _(step):
            start = pl.multiple_of(step * ROWS, ROWS)
            rows = rows_ref[pl.ds(start, ROWS), :]
            gate = jnp.dot(rows, gate_buf[slot], preferred_element_type=jnp.float32)
            up = jnp.dot(rows, up_buf[slot], preferred_element_type=jnp.float32)
            scale = table_ref[pl.ds(start, ROWS), e : e + 1]
            act = gate / (1.0 + jnp.exp(-gate)) * up * scale
            inner_ref[pl.ds(start, ROWS), e * units : (e + 1) * units] = act.astype(jnp.bfloat16)

        if e + 2 < experts:
            for one in up_copies(e + 2):
                one.start()

    for one in downs:
        one.wait()
    for i, out_ref in enumerate((cross_ref, side_ref, sent_ref, kept_ref)):

        @pl.loop(0, total_rows // ROWS)
        def _(step):
            rows = pl.ds(pl.multiple_of(step * ROWS, ROWS), ROWS)
            out_ref[rows, :] = jnp.dot(
                inner_ref[rows, :], down_buf[i], preferred_element_type=jnp.float32
            ).astype(jnp.bfloat16)


def run_experts(order, ranks, gates, hidden, pieces, w_gate, w_up, w_down, columns):
    block_rows, width = hidden.shape
    rows = len(order) * block_rows
    experts, _, units = w_gate.shape
    anywhere = pl.BlockSpec(memory_space=pl.ANY)
    vmem = pl.BlockSpec(memory_space=pltpu.VMEM)
    arrays = [piece for _, _, piece in pieces]
    count = 1 + sum(len(parts) for _, parts, _ in pieces)

    def kernel(ranks_ref, gates, hidden_ref, array_refs, *refs):
        named = [(start, parts, ref) for (start, parts, _), ref in zip(pieces, array_refs)]
        experts_kernel(order, ranks_ref, gates, hidden_ref, named, *refs)

    need = 2 * (rows * width + 4 * width * units + experts * units * (width + rows))
    need += 8 * rows * columns + 512 * rows
    return pl.pallas_call(
        kernel,
        out_shape=[jax.ShapeDtypeStruct((rows, columns), jnp.bfloat16)] * 4,
        in_specs=[
            pl.BlockSpec(memory_space=pltpu.SMEM),
            [vmem] * len(gates),
            anywhere,
            [anywhere] * len(arrays),
            anywhere,
            anywhere,
            anywhere,
        ],
        out_specs=[vmem] * 4,
        scratch_shapes=[
            pltpu.VMEM((rows, width), jnp.bfloat16),
            pltpu.VMEM((2, width, units), jnp.bfloat16),
            pltpu.VMEM((2, width, units), jnp.bfloat16),
            pltpu.VMEM((4, experts * units, columns), jnp.bfloat16),
            pltpu.VMEM((rows, experts * units), jnp.bfloat16),
            pltpu.VMEM((rows, 128), jnp.float32),
            pltpu.SemaphoreType.DMA((count,)),
            pltpu.SemaphoreType.DMA((2, 2)),
            pltpu.SemaphoreType.DMA((4, experts)),
        ],
        compiler_params=pltpu.CompilerParams(vmem_limit_bytes=need + 3 * MIB),
        cost_estimate=pl.CostEstimate(
            flops=6 * rows * width * units * experts,
            bytes_accessed=6 * experts * width * units + 4 * rows * width,
            transcendentals=rows * units * experts,
        ),
        name="experts",
    )(ranks, gates, hidden, arrays, w_gate, w_up, w_down)


def total_of(*terms):
    value = terms[0].astype(jnp.float32)
    for term in terms[1:]:
        value = value + term.astype(jnp.float32)
    return value.astype(jnp.bfloat16)


def local(
    cache_pages,
    queries,
    lengths,
    swap_slot,
    swap_mask,
    hidden,
    expert_ids,
    gate_weights,
    w_gate,
    w_up,
    w_down,
):
    local_count = cache_pages.shape[0]
    groups = lax.axis_size("tp")
    ep_size = lax.axis_size("ep")
    ep_rank = lax.axis_index("ep")
    tp_rank = lax.axis_index("tp")
    device = ep_rank * groups + tp_rank
    mask_value = swap_mask[0]
    partner = jnp.bitwise_xor(ep_rank, mask_value) * groups + tp_rank
    my_slot = swap_slot[device]
    far_length = lengths[partner * local_count + swap_slot[partner]]
    ranks = jnp.stack([ep_rank, tp_rank]).astype(jnp.int32)
    model_width = hidden.shape[1]
    columns = model_width // groups
    expert_local = w_gate.shape[0]
    experts_all = ep_size * expert_local

    rows = hidden.shape[0]
    pairs = ep_size // 2
    late = list(range(2, pairs))
    half = len(late) // 2
    order = [0, 1, 2, 3] + [2 * m for m in late] + [2 * m + 1 for m in late]
    evens, odds = 4, 4 + len(late)

    def quarter(part):
        start = jnp.bitwise_xor(tp_rank, part) * columns
        return lax.dynamic_slice_in_dim(hidden, start, columns, 1)

    def cut(array, start, count):
        return lax.slice_in_dim(array, start * rows, (start + count) * rows, axis=0)

    own = quarter(0)
    near_late = jnp.concatenate([flip(own, "ep", 2 * m) for m in late], axis=0)
    near_2 = flip(own, "ep", 2)
    both_1 = flip(jnp.concatenate([own, quarter(2)], axis=1), "ep", 1)

    expert_ids, gate_weights, both_1 = lax.optimization_barrier((expert_ids, gate_weights, both_1))
    chosen = expert_ids[:, :, None] == jnp.arange(experts_all, dtype=jnp.int32)[None, None, :]
    gates = jnp.sum(jnp.where(chosen, gate_weights[:, :, None], 0.0), axis=1)
    gates = jnp.stack([gates, flip(gates, "ep", 1)])
    gates = [gates] + [flip(gates, "ep", 2 * m) for m in range(1, pairs)]

    far_2 = flip(near_2, "tp", 2)
    near_3 = flip(near_2, "ep", 1)
    far_3 = flip(near_3, "tp", 2)

    cache_pages = jnp.swapaxes(cache_pages, 1, 2)
    queries = jnp.swapaxes(queries, 1, 2)
    place = jnp.stack([device * local_count]).astype(jnp.int32)
    attended = attend_all(lengths, place, queries, cache_pages)
    near_late, attended = lax.optimization_barrier((near_late, attended))

    far_late = flip(near_late, "tp", 2)
    near_odds = flip(near_late, "ep", 1)
    far_odds_y = flip(cut(near_odds, 0, half), "tp", 2)
    far_odds_x = flip(cut(far_late, half, len(late) - half), "ep", 1)
    pieces = [(1, (0, 2), both_1), (1, (1, 3), flip(both_1, "tp", 1))]
    for start, part, array in (
        (2, 0, near_2),
        (2, 2, far_2),
        (3, 0, near_3),
        (3, 2, far_3),
        (evens, 0, near_late),
        (evens, 2, far_late),
        (odds, 0, near_odds),
        (odds, 2, far_odds_y),
        (odds + half, 2, far_odds_x),
    ):
        pieces += [(start, (part,), array), (start, (part ^ 1,), flip(array, "tp", 1))]

    levels = ep_size.bit_length() - 1

    def page_hop(page, level):
        swapped = flip(page, "ep", 1 << level)
        bit = jnp.bitwise_and(jnp.right_shift(mask_value, level), 1) == 1
        return jnp.where(bit, swapped, page)

    page = lax.dynamic_index_in_dim(cache_pages, my_slot, 0, keepdims=False)
    page, _ = lax.optimization_barrier((page, near_late))
    for level in range(levels - 1, 1, -1):
        page = page_hop(page, level)
    ranks, page = lax.optimization_barrier((ranks, page))
    for level in range(min(levels, 2)):
        page = page_hop(page, level)
    traded = jnp.stack([my_slot, far_length]).astype(jnp.int32)
    attended = attend_traded(traded, queries, page, attended)

    cross, side, sent, kept = run_experts(
        order, ranks, gates, hidden, pieces, w_gate, w_up, w_down, columns
    )
    cross = flip(cross, "tp", 1)
    side = flip(side, "tp", 1)

    def sent_of(start, count):
        return total_of(cut(sent, start, count), cut(cross, start, count))

    def kept_of(start, count):
        return total_of(cut(kept, start, count), cut(side, start, count))

    rest = len(late) - half
    over_y = flip(sent_of(odds, half), "tp", 2)
    over_x = flip(sent_of(odds + half, rest), "ep", 1)
    over_3 = flip(sent_of(3, 1), "tp", 2)
    over_2 = flip(sent_of(2, 1), "tp", 2)
    over_1 = flip(jnp.concatenate([kept_of(1, 1), sent_of(1, 1)], axis=1), "ep", 1)
    odd = total_of(kept_of(odds, len(late)), jnp.pad(over_y, ((0, rest * rows), (0, 0))))
    odd = flip(odd, "ep", 1)
    even = total_of(sent_of(evens, len(late)), jnp.pad(over_x, ((half * rows, 0), (0, 0))))
    even = flip(even, "tp", 2)
    near_3 = flip(total_of(kept_of(3, 1), over_3), "ep", 1)
    zero = flip(total_of(sent_of(0, 1), over_1[:, columns:]), "tp", 2)
    even = total_of(kept_of(evens, len(late)), even, odd)
    back = [flip(cut(even, i, 1), "ep", 2 * m) for i, m in enumerate(late)]
    back.append(flip(total_of(kept_of(2, 1), over_2, near_3), "ep", 2))
    moe_out = total_of(kept_of(0, 1), over_1[:, :columns], zero, *back)
    return attended, moe_out


def solution(mesh):
    in_specs = (
        P(("ep", "tp"), None, None),
        P(("ep", "tp"), None, None),
        P(),
        P(),
        P(),
        P("ep", None),
        P("ep", None),
        P("ep", None),
        P("ep", None, "tp"),
        P("ep", None, "tp"),
        P("ep", "tp", None),
    )
    out_specs = (P(("ep", "tp"), None, None), P("ep", "tp"))
    return jax.shard_map(local, mesh=mesh, in_specs=in_specs, out_specs=out_specs, check_vma=False)
```

time: 168 us -> 154 us (0.917)
  local copies, waits for them, and re-layouts: 50.7 us -> 26.3 us
  waiting for transfers between devices: 28.2 us -> 44.7 us
  starting transfers between devices: 49.5 us -> 41.4 us
  other arithmetic: 12.1 us -> 13.9 us
    unnamed x164 -> x56, local copies, waits for them, and re-layouts: 45.9 us -> 22.5 us
    ppermute x52 -> x42, waiting for transfers between devices: 28.2 us -> 44.7 us  [flip(): return lax.ppermute(block, axis, [(i, i ^ apart) for i in range(count)])]
    ppermute x52 -> x42, starting transfers between devices: 49.5 us -> 41.4 us  [flip(): return lax.ppermute(block, axis, [(i, i ^ apart) for i in range(count)])]
    convert_element_type x5 -> x9, other arithmetic: 6.47 us -> 9.96 us  [total_of(): return value.astype(jnp.bfloat16)]
    select_n x3, other arithmetic: 3.46 us -> 1.78 us  [page_hop(): return jnp.where(bit, swapped, page)]
  transfers between devices with their start and end apart: 52 -> 42, of which waited for: 13 -> 18; matrix products, arithmetic and copies ran while one was open for 9% -> 9% of each run, Pallas kernels for 5% -> 5%
where the time goes in v3:
time: 154 us; the launch traced here: 153 us
  waiting for transfers between devices  44.7 us (29%)
  starting transfers between devices  41.4 us (27%)
  local copies, waits for them, and re-layouts  26.3 us (17%)
  Pallas kernels  22.8 us (15%)
  other arithmetic  13.9 us (9%)
  between operations  4.05 us (3%)
    ppermute x42, waiting for transfers between devices, flip(): return lax.ppermute(block, axis, [(i, i ^ apart) for i in range(count)])  44.7 us
    ppermute x42, starting transfers between devices, flip(): return lax.ppermute(block, axis, [(i, i ^ apart) for i in range(count)])  41.4 us
    unnamed x56, local copies, waits for them, and re-layouts  22.5 us
    pallas_call x1, Pallas kernels, run_experts(): pl.pallas_call(kernel, out_shape=[jax.ShapeDtypeStruct((rows, columns), j...  14.6 us
    convert_element_type x9, other arithmetic, total_of(): return value.astype(jnp.bfloat16)  9.96 us
    pallas_call x1, Pallas kernels, attend_all(): pl.pallas_call(functools.partial(attend_kernel, each), out_shape=jax.Shap...  6.37 us
  transfers between devices with their start and end apart: 42, of which 18 were waited for; matrix products, arithmetic and copies ran while one was open for 9% of the time, Pallas kernels for 5%

profile of v3, /device:TPU:0, one launch (start us, length us, event | category | flops | bytes accessed | tf_op | source)
XLA Modules:
  0.0 153.2 jit_solution(2975226497908859237)
XLA Ops:
  1.6 5.1 %collective-permute-start.1 = (bf16[64,896]{1,0:T(8,128)(2,1)S(1)}, bf16[64,896]{1,0:T(8,128)(2,1)S(1)}, u32[]{:S(2)}, u32[]{:S(2)}) collective-permute-start(bf16[64,896]{1,0:T(8,128)(2,1)S(1)} %get-tuple-element.32), channel_id=1, source_target_pairs={{0,24},{4,28},{8,16},{12,20},{16,8},{20,12},{24,0},{28,4},{1,25},{... | collective-permute-start | bytes 344072 | tf_op jit(solution)/shard_map/ppermute | solution.py:20
  6.8 1.6 %collective-permute-start.5 = (bf16[64,1792]{1,0:T(8,128)(2,1)S(1)}, bf16[64,1792]{1,0:T(8,128)(2,1)S(1)}, u32[]{:S(2)}, u32[]{:S(2)}) collective-permute-start(bf16[64,1792]{1,0:T(8,128)(2,1)S(1)} %pad_maximum_fusion.1), channel_id=1, source_target_pairs={{0,4},{4,0},{8,12},{12,8},{16,20},{20,16},{24,28},{28,24},{1,5},{5... | collective-permute-start | bytes 688136 | tf_op jit(solution)/shard_map/ppermute | solution.py:20
  13.0 1.7 %copy-done = bf16[16,128,576]{1,2,0:T(8,128)(2,1)S(1)} copy-done((bf16[16,128,576]{1,2,0:T(8,128)(2,1)S(1)}, bf16[16,128,576]{1,2,0:T(8,128)(2,1)}, u32[]{:S(2)}) %copy-start) | copy-done | bytes 2359320
  14.7 2.3 %copy-done.2 = bf16[16,256,576]{1,2,0:T(8,128)(2,1)S(1)} copy-done((bf16[16,256,576]{1,2,0:T(8,128)(2,1)S(1)}, bf16[16,256,576]{1,2,0:T(8,128)(2,1)}, u32[]{:S(2)}) %copy-start.2) | copy-done | bytes 4718616
  17.7 6.4 %attend_local.1.old_ref = bf16[16,128,512]{2,1,0:T(8,128)(2,1)} custom-call(s32[512]{0:T(512)S(1)} %copy-done.6, s32[1]{0:T(128)} %bitcast.8.place_ref, bf16[16,576,128]{2,1,0:T(8,128)(2,1)S(1)} %bitcast.18, bf16[16,576,256]{2,1,0:T(8,128)(2,1)S(1)} %bitcast.20), custom_call_target="tpu_custom_call" | custom-call | flops 1140850688 | bytes 9175040 | tf_op jit(solution)/shard_map/attend_local/pallas_call | solution.py:52
  24.1 1.6 %collective-permute-start.20 = (bf16[128,896]{1,0:T(8,128)(2,1)S(1)}, bf16[128,896]{1,0:T(8,128)(2,1)S(1)}, u32[]{:S(2)}, u32[]{:S(2)}) collective-permute-start(bf16[128,896]{1,0:T(8,128)(2,1)S(1)} %pad_maximum_fusion.array_refs_10_), channel_id=1, source_target_pairs={{0,2},{1,3},{2,0},{3,1},{4,6},{5,7},{6,4},{7,5},{8,10},{9,11},{10,... | collective-permute-start | bytes 688136 | tf_op jit(solution)/shard_map/ppermute | solution.py:20
  26.6 1.6 %collective-permute-start.15 = (bf16[64,896]{1,0:T(8,128)(2,1)S(1)}, bf16[64,896]{1,0:T(8,128)(2,1)S(1)}, u32[]{:S(2)}, u32[]{:S(2)}) collective-permute-start(bf16[64,896]{1,0:T(8,128)(2,1)S(1)} %collective-permute-done.11.array_refs_2_), channel_id=1, source_target_pairs={{0,4},{4,0},{8,12},{12,8},{16,20},{20,16},{24,28},{28,24},{1,5},{5... | collective-permute-start | bytes 344072 | tf_op jit(solution)/shard_map/ppermute | solution.py:20
  29.1 3.9 %collective-permute-done.13.array_refs_4_ = bf16[64,896]{1,0:T(8,128)(2,1)S(1)} collective-permute-done((bf16[64,896]{1,0:T(8,128)(2,1)S(1)}, bf16[64,896]{1,0:T(8,128)(2,1)S(1)}, u32[]{:S(2)}, u32[]{:S(2)}) %collective-permute-start.13) | collective-permute-done | bytes 114720 | tf_op jit(solution)/shard_map/ppermute | solution.py:20
  33.0 2.3 %collective-permute-start.2 = (bf16[576,256]{1,0:T(8,128)(2,1)S(1)}, bf16[576,256]{1,0:T(8,128)(2,1)S(1)}, u32[]{:S(2)}, u32[]{:S(2)}) collective-permute-start(bf16[576,256]{1,0:T(8,128)(2,1)S(1)} %dynamic-slice_bitcast_fusion), channel_id=1, source_target_pairs={{0,16},{4,20},{8,24},{12,28},{16,0},{20,4},{24,8},{28,12},{1,17},{... | collective-permute-start | bytes 884744 | tf_op jit(solution)/shard_map/ppermute | solution.py:20
  35.4 1.8 %collective-permute-start.7 = (f32[2,64,24]{2,1,0:T(8,128)S(1)}, f32[2,64,24]{2,1,0:T(8,128)S(1)}, u32[]{:S(2)}, u32[]{:S(2)}) collective-permute-start(f32[2,64,24]{2,1,0:T(8,128)S(1)} %copy.25.gates_0_), channel_id=1, source_target_pairs={{0,8},{4,12},{8,0},{12,4},{16,24},{20,28},{24,16},{28,20},{1,9},{5... | collective-permute-start | bytes 36872 | tf_op jit(solution)/shard_map/ppermute | solution.py:20
  37.2 4.8 %collective-permute-done.7.gates_1_ = f32[2,64,24]{2,1,0:T(8,128)S(1)} collective-permute-done((f32[2,64,24]{2,1,0:T(8,128)S(1)}, f32[2,64,24]{2,1,0:T(8,128)S(1)}, u32[]{:S(2)}, u32[]{:S(2)}) %collective-permute-start.7) | collective-permute-done | bytes 12320 | tf_op jit(solution)/shard_map/ppermute | solution.py:20
  42.6 2.8 %collective-permute-start.8 = (f32[2,64,24]{2,1,0:T(8,128)S(1)}, f32[2,64,24]{2,1,0:T(8,128)S(1)}, u32[]{:S(2)}, u32[]{:S(2)}) collective-permute-start(f32[2,64,24]{2,1,0:T(8,128)S(1)} %copy.25.gates_0_), channel_id=1, source_target_pairs={{0,16},{4,20},{8,24},{12,28},{16,0},{20,4},{24,8},{28,12},{1,17},{... | collective-permute-start | bytes 36872 | tf_op jit(solution)/shard_map/ppermute | solution.py:20
  45.4 5.5 %collective-permute-done.8.gates_2_ = f32[2,64,24]{2,1,0:T(8,128)S(1)} collective-permute-done((f32[2,64,24]{2,1,0:T(8,128)S(1)}, f32[2,64,24]{2,1,0:T(8,128)S(1)}, u32[]{:S(2)}, u32[]{:S(2)}) %collective-permute-start.8) | collective-permute-done | bytes 12320 | tf_op jit(solution)/shard_map/ppermute | solution.py:20
  51.6 3.0 %collective-permute-start.9 = (f32[2,64,24]{2,1,0:T(8,128)S(1)}, f32[2,64,24]{2,1,0:T(8,128)S(1)}, u32[]{:S(2)}, u32[]{:S(2)}) collective-permute-start(f32[2,64,24]{2,1,0:T(8,128)S(1)} %copy.25.gates_0_), channel_id=1, source_target_pairs={{0,24},{4,28},{8,16},{12,20},{16,8},{20,12},{24,0},{28,4},{1,25},{... | collective-permute-start | bytes 36872 | tf_op jit(solution)/shard_map/ppermute | solution.py:20
  54.6 3.0 %collective-permute-done.9.gates_3_ = f32[2,64,24]{2,1,0:T(8,128)S(1)} collective-permute-done((f32[2,64,24]{2,1,0:T(8,128)S(1)}, f32[2,64,24]{2,1,0:T(8,128)S(1)}, u32[]{:S(2)}, u32[]{:S(2)}) %collective-permute-start.9) | collective-permute-done | bytes 12320 | tf_op jit(solution)/shard_map/ppermute | solution.py:20
  62.2 3.2 %collective-permute-done.17.array_refs_8_ = bf16[64,896]{1,0:T(8,128)(2,1)S(1)} collective-permute-done((bf16[64,896]{1,0:T(8,128)(2,1)S(1)}, bf16[64,896]{1,0:T(8,128)(2,1)S(1)}, u32[]{:S(2)}, u32[]{:S(2)}) %collective-permute-start.17) | collective-permute-done | bytes 114720 | tf_op jit(solution)/shard_map/ppermute | solution.py:20
  68.0 2.2 %collective-permute-done.26.array_refs_18_ = bf16[64,896]{1,0:T(8,128)(2,1)S(1)} collective-permute-done((bf16[64,896]{1,0:T(8,128)(2,1)S(1)}, bf16[64,896]{1,0:T(8,128)(2,1)S(1)}, u32[]{:S(2)}, u32[]{:S(2)}) %collective-permute-start.26) | collective-permute-done | bytes 114720 | tf_op jit(solution)/shard_map/ppermute | solution.py:20
  71.6 2.6 %copy-done.7 = bf16[3,3584,256]{2,1,0:T(8,128)(2,1)S(1)} copy-done((bf16[3,3584,256]{2,1,0:T(8,128)(2,1)S(1)}, bf16[3,3584,256]{2,1,0:T(8,128)(2,1)}, u32[]{:S(2)}) %copy-start.7) | copy-done | bytes 5505048
  74.1 2.6 %copy-done.8 = bf16[3,3584,256]{2,1,0:T(8,128)(2,1)S(1)} copy-done((bf16[3,3584,256]{2,1,0:T(8,128)(2,1)S(1)}, bf16[3,3584,256]{2,1,0:T(8,128)(2,1)}, u32[]{:S(2)}) %copy-start.8) | copy-done | bytes 5505048
  76.7 2.6 %copy-done.9 = bf16[3,256,3584]{2,1,0:T(8,128)(2,1)S(1)} copy-done((bf16[3,256,3584]{2,1,0:T(8,128)(2,1)S(1)}, bf16[3,256,3584]{2,1,0:T(8,128)(2,1)}, u32[]{:S(2)}) %copy-start.9) | copy-done | bytes 5505048
  86.3 14.6 %experts.1 = (bf16[512,896]{1,0:T(8,128)(2,1)S(1)}, bf16[512,896]{1,0:T(8,128)(2,1)S(1)}, bf16[512,896]{1,0:T(8,128)(2,1)S(1)}, bf16[512,896]{1,0:T(8,128)(2,1)S(1)}) custom-call(s32[2]{0:T(128)S(1)} %pad_add_fusion.1.ranks_ref, f32[2,64,24]{2,1,0:T(8,128)S(1)} %copy.25.gates_0_, f32[2,64,24]{2,1,0:T(8,128)S(1)} %copy-done.21, f32[2,64,24]{2,1,0:T(8,128)S(1)} %copy-done.23, ...), custom_call_target="tpu_custom_call" | custom-call | flops 8455716864 | bytes 23855104 | tf_op jit(solution)/shard_map/experts/pallas_call | solution.py:229
  101.5 2.1 %collective-permute-done.29 = bf16[512,896]{1,0:T(8,128)(2,1)} collective-permute-done((bf16[512,896]{1,0:T(8,128)(2,1)S(1)}, bf16[512,896]{1,0:T(8,128)(2,1)}, u32[]{:S(2)}, u32[]{:S(2)}) %collective-permute-start.29) | collective-permute-done | bytes 917536 | tf_op jit(solution)/shard_map/ppermute | solution.py:20
  111.8 3.4 %collective-permute-done.30 = bf16[64,1792]{1,0:T(8,128)(2,1)S(1)} collective-permute-done((bf16[64,1792]{1,0:T(8,128)(2,1)}, bf16[64,1792]{1,0:T(8,128)(2,1)S(1)}, u32[]{:S(2)}, u32[]{:S(2)}) %collective-permute-start.30) | collective-permute-done | bytes 229408 | tf_op jit(solution)/shard_map/ppermute | solution.py:20
  117.1 3.8 %collective-permute-done.3 = bf16[576,256]{1,0:T(8,128)(2,1)} collective-permute-done((bf16[576,256]{1,0:T(8,128)(2,1)}, bf16[576,256]{1,0:T(8,128)(2,1)}, u32[]{:S(2)}, u32[]{:S(2)}) %collective-permute-start.3) | collective-permute-done | bytes 294944 | tf_op jit(solution)/shard_map/ppermute | solution.py:20
  122.5 1.6 %collective-permute-start.34 = (bf16[64,896]{1,0:T(8,128)(2,1)S(1)}, bf16[64,896]{1,0:T(8,128)(2,1)S(1)}, u32[]{:S(2)}, u32[]{:S(2)}) collective-permute-start(bf16[64,896]{1,0:T(8,128)(2,1)S(1)} %get-tuple-element.29), channel_id=1, source_target_pairs={{0,2},{1,3},{2,0},{3,1},{4,6},{5,7},{6,4},{7,5},{8,10},{9,11},{10,... | collective-permute-start | bytes 344072 | tf_op jit(solution)/shard_map/ppermute | solution.py:20
  127.0 3.0 %collective-permute-done.34 = bf16[64,896]{1,0:T(8,128)(2,1)S(1)} collective-permute-done((bf16[64,896]{1,0:T(8,128)(2,1)S(1)}, bf16[64,896]{1,0:T(8,128)(2,1)S(1)}, u32[]{:S(2)}, u32[]{:S(2)}) %collective-permute-start.34) | collective-permute-done | bytes 114720 | tf_op jit(solution)/shard_map/ppermute | solution.py:20
  138.7 1.7 %collective-permute-done.33 = bf16[128,896]{1,0:T(8,128)(2,1)S(1)} collective-permute-done((bf16[128,896]{1,0:T(8,128)(2,1)S(1)}, bf16[128,896]{1,0:T(8,128)(2,1)S(1)}, u32[]{:S(2)}, u32[]{:S(2)}) %collective-permute-start.33) | collective-permute-done | bytes 229408 | tf_op jit(solution)/shard_map/ppermute | solution.py:20
  141.5 3.1 %collective-permute-start.37 = (bf16[64,896]{1,0:T(8,128)(2,1)S(1)}, bf16[64,896]{1,0:T(8,128)(2,1)S(1)}, u32[]{:S(2)}, u32[]{:S(2)}) collective-permute-start(bf16[64,896]{1,0:T(8,128)(2,1)S(1)} %get-tuple-element.34), channel_id=1, source_target_pairs={{0,24},{4,28},{8,16},{12,20},{16,8},{20,12},{24,0},{28,4},{1,25},{... | collective-permute-start | bytes 344072 | tf_op jit(solution)/shard_map/ppermute | solution.py:20
  144.9 1.8 %attend_traded.1 = bf16[16,128,512]{2,1,0:T(8,128)(2,1)} custom-call(s32[2]{0:T(128)S(1)} %pad_add_fusion.place_ref, bf16[16,576,128]{2,1,0:T(8,128)(2,1)S(1)} %bitcast.19, bf16[576,256]{1,0:T(8,128)(2,1)S(1)} %broadcast_select_fusion.2.page_ref, bf16[16,128,512]{2,1,0:T(8,128)(2,1)} %attend_local.1.old_ref), custom_call_target="tpu_custom_call", output_to_operand_aliasing={{}: (3, {})} | custom-call | flops 71303168 | bytes 573440 | tf_op jit(solution)/shard_map/attend_traded/pallas_call | solution.py:81
  146.7 1.6 %collective-permute-done.37 = bf16[64,896]{1,0:T(8,128)(2,1)S(1)} collective-permute-done((bf16[64,896]{1,0:T(8,128)(2,1)S(1)}, bf16[64,896]{1,0:T(8,128)(2,1)S(1)}, u32[]{:S(2)}, u32[]{:S(2)}) %collective-permute-start.37) | collective-permute-done | bytes 114720 | tf_op jit(solution)/shard_map/ppermute | solution.py:20
  148.2 3.3 %collective-permute-done.36 = bf16[64,896]{1,0:T(8,128)(2,1)S(1)} collective-permute-done((bf16[64,896]{1,0:T(8,128)(2,1)S(1)}, bf16[64,896]{1,0:T(8,128)(2,1)S(1)}, u32[]{:S(2)}, u32[]{:S(2)}) %collective-permute-start.36) | collective-permute-done | bytes 114720 | tf_op jit(solution)/shard_map/ppermute | solution.py:20
  151.5 1.7 %add_convert_fusion.6 = bf16[64,896]{1,0:T(8,128)(2,1)} fusion(bf16[64,896]{1,0:T(8,128)(2,1)S(1)} %collective-permute-done.41, bf16[64,896]{1,0:T(8,128)(2,1)S(1)} %collective-permute-done.37, bf16[64,896]{1,0:T(8,128)(2,1)S(1)} %collective-permute-done.36, bf16[64,896]{1,0:T(8,128)(2,1)S(1)} %collective-permute-done.31, ...), kind=kLoop, calls=%fused_computation.13 | loop fusion | flops 917504 | bytes 917504 | tf_op jit(solution)/shard_map/convert_element_type | solution.py:267
  (138 shorter events, 47.0 us)
Async XLA Ops:
  1.6 22.5 %collective-permute-start.1 = (bf16[64,896]{1,0:T(8,128)(2,1)S(1)}, bf16[64,896]{1,0:T(8,128)(2,1)S(1)}, u32[]{:S(2)}, u32[]{:S(2)}) collective-permute-start(bf16[64,896]{1,0:T(8,128)(2,1)S(1)} %get-tuple-element.32), channel_id=1, source_target_pairs={{0,24},{4,28},{8,16},{12,20},{16,8},{20,12},{24,0},{28,4},{1,25},{... | collective-permute-start | bytes 344072 | tf_op jit(solution)/shard_map/ppermute | solution.py:20
  6.7 17.4 %collective-permute-start = (bf16[64,896]{1,0:T(8,128)(2,1)S(1)}, bf16[64,896]{1,0:T(8,128)(2,1)S(1)}, u32[]{:S(2)}, u32[]{:S(2)}) collective-permute-start(bf16[64,896]{1,0:T(8,128)(2,1)S(1)} %get-tuple-element.32), channel_id=1, source_target_pairs={{0,16},{4,20},{8,24},{12,28},{16,0},{20,4},{24,8},{28,12},{1,17},{... | collective-permute-start | bytes 344072 | tf_op jit(solution)/shard_map/ppermute | solution.py:20
  6.8 19.9 %collective-permute-start.5 = (bf16[64,1792]{1,0:T(8,128)(2,1)S(1)}, bf16[64,1792]{1,0:T(8,128)(2,1)S(1)}, u32[]{:S(2)}, u32[]{:S(2)}) collective-permute-start(bf16[64,1792]{1,0:T(8,128)(2,1)S(1)} %pad_maximum_fusion.1), channel_id=1, source_target_pairs={{0,4},{4,0},{8,12},{12,8},{16,20},{20,16},{24,28},{28,24},{1,5},{5... | collective-permute-start | bytes 688136 | tf_op jit(solution)/shard_map/ppermute | solution.py:20
  8.3 17.9 %collective-permute-start.11 = (bf16[64,896]{1,0:T(8,128)(2,1)S(1)}, bf16[64,896]{1,0:T(8,128)(2,1)S(1)}, u32[]{:S(2)}, u32[]{:S(2)}) collective-permute-start(bf16[64,896]{1,0:T(8,128)(2,1)S(1)} %get-tuple-element.32), channel_id=1, source_target_pairs={{0,8},{4,12},{8,0},{12,4},{16,24},{20,28},{24,16},{28,20},{1,9},{5... | collective-permute-start | bytes 344072 | tf_op jit(solution)/shard_map/ppermute | solution.py:20
  24.1 35.3 %collective-permute-start.20 = (bf16[128,896]{1,0:T(8,128)(2,1)S(1)}, bf16[128,896]{1,0:T(8,128)(2,1)S(1)}, u32[]{:S(2)}, u32[]{:S(2)}) collective-permute-start(bf16[128,896]{1,0:T(8,128)(2,1)S(1)} %pad_maximum_fusion.array_refs_10_), channel_id=1, source_target_pairs={{0,2},{1,3},{2,0},{3,1},{4,6},{5,7},{6,4},{7,5},{8,10},{9,11},{10,... | collective-permute-start | bytes 688136 | tf_op jit(solution)/shard_map/ppermute | solution.py:20
  25.7 33.7 %collective-permute-start.22 = (bf16[128,896]{1,0:T(8,128)(2,1)S(1)}, bf16[128,896]{1,0:T(8,128)(2,1)S(1)}, u32[]{:S(2)}, u32[]{:S(2)}) collective-permute-start(bf16[128,896]{1,0:T(8,128)(2,1)S(1)} %pad_maximum_fusion.array_refs_10_), channel_id=1, source_target_pairs={{0,4},{4,0},{8,12},{12,8},{16,20},{20,16},{24,28},{28,24},{1,5},{5... | collective-permute-start | bytes 688136 | tf_op jit(solution)/shard_map/ppermute | solution.py:20
  26.3 6.8 %collective-permute-start.13 = (bf16[64,896]{1,0:T(8,128)(2,1)S(1)}, bf16[64,896]{1,0:T(8,128)(2,1)S(1)}, u32[]{:S(2)}, u32[]{:S(2)}) collective-permute-start(bf16[64,896]{1,0:T(8,128)(2,1)S(1)} %collective-permute-done.11.array_refs_2_), channel_id=1, source_target_pairs={{0,2},{1,3},{2,0},{3,1},{4,6},{5,7},{6,4},{7,5},{8,10},{9,11},{10,... | collective-permute-start | bytes 344072 | tf_op jit(solution)/shard_map/ppermute | solution.py:20
  26.6 8.8 %collective-permute-start.15 = (bf16[64,896]{1,0:T(8,128)(2,1)S(1)}, bf16[64,896]{1,0:T(8,128)(2,1)S(1)}, u32[]{:S(2)}, u32[]{:S(2)}) collective-permute-start(bf16[64,896]{1,0:T(8,128)(2,1)S(1)} %collective-permute-done.11.array_refs_2_), channel_id=1, source_target_pairs={{0,4},{4,0},{8,12},{12,8},{16,20},{20,16},{24,28},{28,24},{1,5},{5... | collective-permute-start | bytes 344072 | tf_op jit(solution)/shard_map/ppermute | solution.py:20
  28.3 7.0 %collective-permute-start.6 = (f32[64,24]{0,1:T(8,128)S(1)}, f32[64,24]{0,1:T(8,128)S(1)}, u32[]{:S(2)}, u32[]{:S(2)}) collective-permute-start(f32[64,24]{0,1:T(8,128)S(1)} %select_reduce_fusion), channel_id=1, source_target_pairs={{0,4},{4,0},{8,12},{12,8},{16,20},{20,16},{24,28},{28,24},{1,5},{5... | collective-permute-start | bytes 18440 | tf_op jit(solution)/shard_map/ppermute | solution.py:20
  33.0 34.0 %collective-permute-start.2 = (bf16[576,256]{1,0:T(8,128)(2,1)S(1)}, bf16[576,256]{1,0:T(8,128)(2,1)S(1)}, u32[]{:S(2)}, u32[]{:S(2)}) collective-permute-start(bf16[576,256]{1,0:T(8,128)(2,1)S(1)} %dynamic-slice_bitcast_fusion), channel_id=1, source_target_pairs={{0,16},{4,20},{8,24},{12,28},{16,0},{20,4},{24,8},{28,12},{1,17},{... | collective-permute-start | bytes 884744 | tf_op jit(solution)/shard_map/ppermute | solution.py:20
  35.3 22.9 %collective-permute-start.14 = (bf16[64,896]{1,0:T(8,128)(2,1)S(1)}, bf16[64,896]{1,0:T(8,128)(2,1)S(1)}, u32[]{:S(2)}, u32[]{:S(2)}) collective-permute-start(bf16[64,896]{1,0:T(8,128)(2,1)S(1)} %collective-permute-done.13.array_refs_4_), channel_id=1, source_target_pairs={{0,1},{1,0},{2,3},{3,2},{4,5},{5,4},{6,7},{7,6},{8,9},{9,8},{10,11... | collective-permute-start | bytes 344072 | tf_op jit(solution)/shard_map/ppermute | solution.py:20
  35.4 6.6 %collective-permute-start.7 = (f32[2,64,24]{2,1,0:T(8,128)S(1)}, f32[2,64,24]{2,1,0:T(8,128)S(1)}, u32[]{:S(2)}, u32[]{:S(2)}) collective-permute-start(f32[2,64,24]{2,1,0:T(8,128)S(1)} %copy.25.gates_0_), channel_id=1, source_target_pairs={{0,8},{4,12},{8,0},{12,4},{16,24},{20,28},{24,16},{28,20},{1,9},{5... | collective-permute-start | bytes 36872 | tf_op jit(solution)/shard_map/ppermute | solution.py:20
  42.6 8.3 %collective-permute-start.8 = (f32[2,64,24]{2,1,0:T(8,128)S(1)}, f32[2,64,24]{2,1,0:T(8,128)S(1)}, u32[]{:S(2)}, u32[]{:S(2)}) collective-permute-start(f32[2,64,24]{2,1,0:T(8,128)S(1)} %copy.25.gates_0_), channel_id=1, source_target_pairs={{0,16},{4,20},{8,24},{12,28},{16,0},{20,4},{24,8},{28,12},{1,17},{... | collective-permute-start | bytes 36872 | tf_op jit(solution)/shard_map/ppermute | solution.py:20
  51.6 6.1 %collective-permute-start.9 = (f32[2,64,24]{2,1,0:T(8,128)S(1)}, f32[2,64,24]{2,1,0:T(8,128)S(1)}, u32[]{:S(2)}, u32[]{:S(2)}) collective-permute-start(f32[2,64,24]{2,1,0:T(8,128)S(1)} %copy.25.gates_0_), channel_id=1, source_target_pairs={{0,24},{4,28},{8,16},{12,20},{16,8},{20,12},{24,0},{28,4},{1,25},{... | collective-permute-start | bytes 36872 | tf_op jit(solution)/shard_map/ppermute | solution.py:20
  58.2 8.7 %collective-permute-start.19 = (bf16[128,896]{1,0:T(8,128)(2,1)S(1)}, bf16[128,896]{1,0:T(8,128)(2,1)S(1)}, u32[]{:S(2)}, u32[]{:S(2)}) collective-permute-start(bf16[128,896]{1,0:T(8,128)(2,1)S(1)} %pad_maximum_fusion.array_refs_10_), channel_id=1, source_target_pairs={{0,1},{1,0},{2,3},{3,2},{4,5},{5,4},{6,7},{7,6},{8,9},{9,8},{10,11... | collective-permute-start | bytes 688136 | tf_op jit(solution)/shard_map/ppermute | solution.py:20
  58.9 8.6 %collective-permute-start.10 = (bf16[64,1792]{1,0:T(8,128)(2,1)S(1)}, bf16[64,1792]{1,0:T(8,128)(2,1)S(1)}, u32[]{:S(2)}, u32[]{:S(2)}) collective-permute-start(bf16[64,1792]{1,0:T(8,128)(2,1)S(1)} %collective-permute-done.5.array_refs_0_), channel_id=1, source_target_pairs={{0,1},{1,0},{2,3},{3,2},{4,5},{5,4},{6,7},{7,6},{8,9},{9,8},{10,11... | collective-permute-start | bytes 688136 | tf_op jit(solution)/shard_map/ppermute | solution.py:20
  59.4 6.0 %collective-permute-start.17 = (bf16[64,896]{1,0:T(8,128)(2,1)S(1)}, bf16[64,896]{1,0:T(8,128)(2,1)S(1)}, u32[]{:S(2)}, u32[]{:S(2)}) collective-permute-start(bf16[64,896]{1,0:T(8,128)(2,1)S(1)} %collective-permute-done.15.array_refs_6_), channel_id=1, source_target_pairs={{0,2},{1,3},{2,0},{3,1},{4,6},{5,7},{6,4},{7,5},{8,10},{9,11},{10,... | collective-permute-start | bytes 344072 | tf_op jit(solution)/shard_map/ppermute | solution.py:20
  61.4 6.2 %collective-permute-start.24 = (bf16[64,896]{1,0:T(8,128)(2,1)S(1)}, bf16[64,896]{1,0:T(8,128)(2,1)S(1)}, u32[]{:S(2)}, u32[]{:S(2)}) collective-permute-start(bf16[64,896]{1,0:T(8,128)(2,1)S(1)} %slice.128), channel_id=1, source_target_pairs={{0,2},{1,3},{2,0},{3,1},{4,6},{5,7},{6,4},{7,5},{8,10},{9,11},{10,... | collective-permute-start | bytes 344072 | tf_op jit(solution)/shard_map/ppermute | solution.py:20
  106.6 8.7 %collective-permute-start.30 = (bf16[64,1792]{1,0:T(8,128)(2,1)}, bf16[64,1792]{1,0:T(8,128)(2,1)S(1)}, u32[]{:S(2)}, u32[]{:S(2)}) collective-permute-start(bf16[64,1792]{1,0:T(8,128)(2,1)} %pad_maximum_fusion.2), channel_id=1, source_target_pairs={{0,4},{4,0},{8,12},{12,8},{16,20},{20,16},{24,28},{28,24},{1,5},{5... | collective-permute-start | bytes 688136 | tf_op jit(solution)/shard_map/ppermute | solution.py:20
  109.8 11.0 %collective-permute-start.3 = (bf16[576,256]{1,0:T(8,128)(2,1)}, bf16[576,256]{1,0:T(8,128)(2,1)}, u32[]{:S(2)}, u32[]{:S(2)}) collective-permute-start(bf16[576,256]{1,0:T(8,128)(2,1)} %broadcast_select_fusion), channel_id=1, source_target_pairs={{0,4},{4,0},{8,12},{12,8},{16,20},{20,16},{24,28},{28,24},{1,5},{5... | collective-permute-start | bytes 884744 | tf_op jit(solution)/shard_map/ppermute | solution.py:20
  116.5 8.9 %collective-permute-start.39 = (bf16[64,896]{1,0:T(8,128)(2,1)S(1)}, bf16[64,896]{1,0:T(8,128)(2,1)S(1)}, u32[]{:S(2)}, u32[]{:S(2)}) collective-permute-start(bf16[64,896]{1,0:T(8,128)(2,1)S(1)} %get-tuple-element.27), channel_id=1, source_target_pairs={{0,2},{1,3},{2,0},{3,1},{4,6},{5,7},{6,4},{7,5},{8,10},{9,11},{10,... | collective-permute-start | bytes 344072 | tf_op jit(solution)/shard_map/ppermute | solution.py:20
  121.9 23.0 %collective-permute-start.4 = (bf16[576,256]{1,0:T(8,128)(2,1)S(1)}, bf16[576,256]{1,0:T(8,128)(2,1)S(1)}, u32[]{:S(2)}, u32[]{:S(2)}) collective-permute-start(bf16[576,256]{1,0:T(8,128)(2,1)S(1)} %broadcast_select_fusion.1), channel_id=1, source_target_pairs={{0,8},{4,12},{8,0},{12,4},{16,24},{20,28},{24,16},{28,20},{1,9},{5... | collective-permute-start | bytes 884744 | tf_op jit(solution)/shard_map/ppermute | solution.py:20
  121.9 12.4 %collective-permute-start.38 = (bf16[64,896]{1,0:T(8,128)(2,1)S(1)}, bf16[64,896]{1,0:T(8,128)(2,1)S(1)}, u32[]{:S(2)}, u32[]{:S(2)}) collective-permute-start(bf16[64,896]{1,0:T(8,128)(2,1)S(1)} %get-tuple-element.28), channel_id=1, source_target_pairs={{0,2},{1,3},{2,0},{3,1},{4,6},{5,7},{6,4},{7,5},{8,10},{9,11},{10,... | collective-permute-start | bytes 344072 | tf_op jit(solution)/shard_map/ppermute | solution.py:20
  122.5 7.6 %collective-permute-start.34 = (bf16[64,896]{1,0:T(8,128)(2,1)S(1)}, bf16[64,896]{1,0:T(8,128)(2,1)S(1)}, u32[]{:S(2)}, u32[]{:S(2)}) collective-permute-start(bf16[64,896]{1,0:T(8,128)(2,1)S(1)} %get-tuple-element.29), channel_id=1, source_target_pairs={{0,2},{1,3},{2,0},{3,1},{4,6},{5,7},{6,4},{7,5},{8,10},{9,11},{10,... | collective-permute-start | bytes 344072 | tf_op jit(solution)/shard_map/ppermute | solution.py:20
  124.0 8.6 %collective-permute-start.32 = (bf16[64,896]{1,0:T(8,128)(2,1)S(1)}, bf16[64,896]{1,0:T(8,128)(2,1)S(1)}, u32[]{:S(2)}, u32[]{:S(2)}) collective-permute-start(bf16[64,896]{1,0:T(8,128)(2,1)S(1)} %get-tuple-element.30), channel_id=1, source_target_pairs={{0,4},{4,0},{8,12},{12,8},{16,20},{20,16},{24,28},{28,24},{1,5},{5... | collective-permute-start | bytes 344072 | tf_op jit(solution)/shard_map/ppermute | solution.py:20
  125.5 21.2 %collective-permute-start.31 = (bf16[64,896]{1,0:T(8,128)(2,1)S(1)}, bf16[64,896]{1,0:T(8,128)(2,1)S(1)}, u32[]{:S(2)}, u32[]{:S(2)}) collective-permute-start(bf16[64,896]{1,0:T(8,128)(2,1)S(1)} %get-tuple-element.26), channel_id=1, source_target_pairs={{0,2},{1,3},{2,0},{3,1},{4,6},{5,7},{6,4},{7,5},{8,10},{9,11},{10,... | collective-permute-start | bytes 344072 | tf_op jit(solution)/shard_map/ppermute | solution.py:20
  130.1 5.8 %collective-permute-start.40 = (bf16[64,896]{1,0:T(8,128)(2,1)S(1)}, bf16[64,896]{1,0:T(8,128)(2,1)S(1)}, u32[]{:S(2)}, u32[]{:S(2)}) collective-permute-start(bf16[64,896]{1,0:T(8,128)(2,1)S(1)} %add_convert_fusion.8), channel_id=1, source_target_pairs={{0,4},{4,0},{8,12},{12,8},{16,20},{20,16},{24,28},{28,24},{1,5},{5... | collective-permute-start | bytes 344072 | tf_op jit(solution)/shard_map/ppermute | solution.py:20
  132.6 6.1 %collective-permute-start.35 = (bf16[128,896]{1,0:T(8,128)(2,1)S(1)}, bf16[128,896]{1,0:T(8,128)(2,1)S(1)}, u32[]{:S(2)}, u32[]{:S(2)}) collective-permute-start(bf16[128,896]{1,0:T(8,128)(2,1)S(1)} %add_convert_fusion.1), channel_id=1, source_target_pairs={{0,4},{4,0},{8,12},{12,8},{16,20},{20,16},{24,28},{28,24},{1,5},{5... | collective-permute-start | bytes 688136 | tf_op jit(solution)/shard_map/ppermute | solution.py:20
  134.3 6.1 %collective-permute-start.33 = (bf16[128,896]{1,0:T(8,128)(2,1)S(1)}, bf16[128,896]{1,0:T(8,128)(2,1)S(1)}, u32[]{:S(2)}, u32[]{:S(2)}) collective-permute-start(bf16[128,896]{1,0:T(8,128)(2,1)S(1)} %add_convert_fusion.3), channel_id=1, source_target_pairs={{0,2},{1,3},{2,0},{3,1},{4,6},{5,7},{6,4},{7,5},{8,10},{9,11},{10,... | collective-permute-start | bytes 688136 | tf_op jit(solution)/shard_map/ppermute | solution.py:20
  136.8 9.8 %collective-permute-start.41 = (bf16[64,896]{1,0:T(8,128)(2,1)S(1)}, bf16[64,896]{1,0:T(8,128)(2,1)S(1)}, u32[]{:S(2)}, u32[]{:S(2)}) collective-permute-start(bf16[64,896]{1,0:T(8,128)(2,1)S(1)} %add_convert_fusion.7), channel_id=1, source_target_pairs={{0,8},{4,12},{8,0},{12,4},{16,24},{20,28},{24,16},{28,20},{1,9},{5... | collective-permute-start | bytes 344072 | tf_op jit(solution)/shard_map/ppermute | solution.py:20
  141.5 6.8 %collective-permute-start.37 = (bf16[64,896]{1,0:T(8,128)(2,1)S(1)}, bf16[64,896]{1,0:T(8,128)(2,1)S(1)}, u32[]{:S(2)}, u32[]{:S(2)}) collective-permute-start(bf16[64,896]{1,0:T(8,128)(2,1)S(1)} %get-tuple-element.34), channel_id=1, source_target_pairs={{0,24},{4,28},{8,16},{12,20},{16,8},{20,12},{24,0},{28,4},{1,25},{... | collective-permute-start | bytes 344072 | tf_op jit(solution)/shard_map/ppermute | solution.py:20
  144.6 6.9 %collective-permute-start.36 = (bf16[64,896]{1,0:T(8,128)(2,1)S(1)}, bf16[64,896]{1,0:T(8,128)(2,1)S(1)}, u32[]{:S(2)}, u32[]{:S(2)}) collective-permute-start(bf16[64,896]{1,0:T(8,128)(2,1)S(1)} %get-tuple-element.33), channel_id=1, source_target_pairs={{0,16},{4,20},{8,24},{12,28},{16,0},{20,4},{24,8},{28,12},{1,17},{... | collective-permute-start | bytes 344072 | tf_op jit(solution)/shard_map/ppermute | solution.py:20
  (38 other events, 210.3 us)

commit v4 on v3

v4 whole, which is shorter than its diff:
```python
import functools
import math

import jax
import jax.numpy as jnp
from jax import lax
from jax.experimental import pallas as pl
from jax.experimental.pallas import tpu as pltpu
from jax.sharding import PartitionSpec as P

LAT = 512
SCORE_SCALE = 192.0 ** (-0.5)
MASK_FLOOR = -1e30
ROWS = 512
MIB = 1 << 20


def flip(block, axis, apart):
    count = lax.axis_size(axis)
    return lax.ppermute(block, axis, [(i, i ^ apart) for i in range(count)])


def attend_body(query, page, length):
    scores = (
        lax.dot_general(query, page, (((0,), (0,)), ((), ())), preferred_element_type=jnp.float32)
        * SCORE_SCALE
    )
    live = lax.broadcasted_iota(jnp.int32, scores.shape, 1) < length
    scores = jnp.where(live, scores, MASK_FLOOR)
    top = jnp.max(scores, axis=1, keepdims=True)
    weight = jnp.where(live, jnp.exp(scores - top), 0.0)
    total = jnp.sum(weight, axis=1, keepdims=True)
    blended = lax.dot_general(
        weight.astype(jnp.bfloat16),
        page[:LAT],
        (((1,), (1,)), ((), ())),
        preferred_element_type=jnp.float32,
    )
    return (blended / total).astype(jnp.bfloat16)


def in_hbm(array):
    return pltpu.with_memory_space_constraint(array, pltpu.HBM)


def in_vmem(array):
    return pltpu.with_memory_space_constraint(array, pltpu.VMEM)


ANYWHERE = pl.BlockSpec(memory_space=pl.ANY)
IN_VMEM = pl.BlockSpec(memory_space=pltpu.VMEM)
IN_SMEM = pl.BlockSpec(memory_space=pltpu.SMEM)


def device_of(ranks_ref, groups, mask=0):
    return (ranks_ref[0] ^ mask) * groups + ranks_ref[1]


def pick_kernel(groups, ranks_ref, slots_ref, ids_ref, gates_ref, hidden_ref, pages_ref, near_ref, both_ref, page_ref, sems):
    rows = hidden_ref.shape[0]
    columns = hidden_ref.shape[1] // groups

    def quarter(part):
        start = pl.multiple_of((ranks_ref[1] ^ part) * columns, 128)
        return hidden_ref.at[:, pl.ds(start, columns)]

    copies = [
        (quarter(0), near_ref.at[:, pl.ds(0, columns)]),
        (quarter(0), both_ref.at[:, pl.ds(0, columns)]),
        (quarter(2), both_ref.at[:, pl.ds(columns, columns)]),
        (pages_ref.at[slots_ref[device_of(ranks_ref, groups)]], page_ref),
    ]
    copies = [pltpu.make_async_copy(*pair, sems.at[i]) for i, pair in enumerate(copies)]
    for one in copies:
        one.start()
    gates = gates_ref[...]
    high = gates.astype(jnp.bfloat16).astype(jnp.float32)
    middle = (gates - high).astype(jnp.bfloat16).astype(jnp.float32)
    low = gates - high - middle
    top = gates.shape[0]
    table = jnp.concatenate(
        [ids_ref[...].astype(jnp.float32), high, middle, low, jnp.zeros((128 - 4 * top, rows), jnp.float32)],
        axis=0,
    )
    table = jnp.concatenate([table, jnp.zeros((128, 128 - rows), jnp.float32)], axis=1)
    table = table.T[:rows].astype(jnp.bfloat16)
    near_ref[:, columns:] = table
    both_ref[:, 2 * columns :] = table
    for one in copies:
        one.wait()


def pick(ranks, swap_slot, expert_ids, gate_weights, hidden, pages, groups):
    rows, width = hidden.shape
    columns = width // groups
    return pl.pallas_call(
        functools.partial(pick_kernel, groups),
        out_shape=(
            pltpu.VMEM((rows, columns + 128), jnp.bfloat16),
            pltpu.VMEM((rows, 2 * columns + 128), jnp.bfloat16),
            pltpu.VMEM(pages.shape[1:], jnp.bfloat16),
        ),
        in_specs=[IN_SMEM, IN_SMEM, IN_VMEM, IN_VMEM, ANYWHERE, ANYWHERE],
        out_specs=(IN_VMEM, IN_VMEM, IN_VMEM),
        scratch_shapes=[pltpu.SemaphoreType.DMA((4,))],
        compiler_params=pltpu.CompilerParams(vmem_limit_bytes=2 * MIB),
        name="pick",
    )(ranks, swap_slot, expert_ids.T, gate_weights.T, in_hbm(hidden), in_hbm(pages))


def attend_kernel(
    each,
    groups,
    ranks_ref,
    lengths_ref,
    query_ref,
    page_ref,
    w_gate_ref,
    w_up_ref,
    w_down_ref,
    out_ref,
    gate_ref,
    up_ref,
    down_ref,
    sems,
):
    step, steps = pl.program_id(0), pl.num_programs(0)
    copies = [
        pltpu.make_async_copy(source, target, sems.at[i])
        for i, (source, target) in enumerate(
            ((w_gate_ref, gate_ref), (w_up_ref, up_ref), (w_down_ref, down_ref))
        )
    ]

    @pl.when(step == 0)
    def _():
        for one in copies:
            one.start()

    first = device_of(ranks_ref, groups) * each * steps + step * each
    for i in range(each):
        out_ref[i] = attend_body(query_ref[i], page_ref[i], lengths_ref[first + i])

    @pl.when(step == steps - 1)
    def _():
        for one in copies:
            one.wait()


def attend_all(ranks, lengths, queries, pages, groups, *weights):
    count, width, heads = queries.shape
    slots = pages.shape[2]
    each = math.gcd(count, 4)
    moved = sum(2 * math.prod(w.shape) for w in weights)
    return pl.pallas_call(
        functools.partial(attend_kernel, each, groups),
        out_shape=[jax.ShapeDtypeStruct((count, heads, LAT), jnp.bfloat16)]
        + [pltpu.VMEM(w.shape, w.dtype) for w in weights],
        grid_spec=pltpu.PrefetchScalarGridSpec(
            num_scalar_prefetch=2,
            grid=(count // each,),
            in_specs=[
                pl.BlockSpec((each, width, heads), lambda i, *_: (i, 0, 0)),
                pl.BlockSpec((each, width, slots), lambda i, *_: (i, 0, 0)),
            ]
            + [ANYWHERE] * len(weights),
            out_specs=[pl.BlockSpec((each, heads, LAT), lambda i, *_: (i, 0, 0))]
            + [ANYWHERE] * len(weights),
            scratch_shapes=[pltpu.SemaphoreType.DMA((len(weights),))],
        ),
        compiler_params=pltpu.CompilerParams(vmem_limit_bytes=12 * MIB),
        cost_estimate=pl.CostEstimate(
            flops=2 * count * heads * slots * (width + LAT),
            bytes_accessed=2 * count * (heads * (width + LAT) + slots * width) + moved,
            transcendentals=count * heads * slots,
        ),
        name="attend_local",
    )(ranks, lengths, in_hbm(queries), in_hbm(pages), *[in_hbm(w) for w in weights])


def attend_traded_kernel(
    groups, ranks_ref, lengths_ref, slots_ref, mask_ref, query_ref, page_ref, old_ref, out_ref
):
    partner = device_of(ranks_ref, groups, mask_ref[0])
    length = lengths_ref[partner * old_ref.shape[0] + slots_ref[partner]]
    out_ref[0] = attend_body(query_ref[0], page_ref[...], length)


def attend_traded(ranks, lengths, swap_slot, swap_mask, queries, page, attended, groups):
    _, width, heads = queries.shape
    slots = page.shape[1]

    def mine(i, ranks_ref, lengths_ref, slots_ref, mask_ref):
        return slots_ref[device_of(ranks_ref, groups)], 0, 0

    return pl.pallas_call(
        functools.partial(attend_traded_kernel, groups),
        out_shape=jax.ShapeDtypeStruct(attended.shape, attended.dtype),
        grid_spec=pltpu.PrefetchScalarGridSpec(
            num_scalar_prefetch=4,
            grid=(1,),
            in_specs=[
                pl.BlockSpec((1, width, heads), mine),
                pl.BlockSpec((width, slots), lambda i, *_: (0, 0)),
                ANYWHERE,
            ],
            out_specs=pl.BlockSpec((1, heads, LAT), mine),
        ),
        input_output_aliases={6: 0},
        compiler_params=pltpu.CompilerParams(vmem_limit_bytes=4 * MIB),
        cost_estimate=pl.CostEstimate(
            flops=2 * heads * slots * (width + LAT),
            bytes_accessed=2 * (heads * (width + LAT) + slots * width),
            transcendentals=heads * slots,
        ),
        name="attend_traded",
    )(ranks, lengths, swap_slot, swap_mask, in_hbm(queries), page, attended)


def experts_kernel(
    top,
    ranks_ref,
    hidden_ref,
    pieces,
    gate_ref,
    up_ref,
    down_ref,
    cross_ref,
    side_ref,
    sent_ref,
    kept_ref,
    rows_ref,
    meta_ref,
    inner_ref,
    table_ref,
    sems,
):
    experts, _, units = gate_ref.shape
    block_rows = hidden_ref.shape[0]
    total_rows = rows_ref.shape[0]
    quarter = kept_ref.shape[1]
    ep_rank, tp_rank = ranks_ref[0], ranks_ref[1]

    def columns_of(part):
        return pl.ds(pl.multiple_of((tp_rank ^ part) * quarter, 128), quarter)

    copies = [(hidden_ref, rows_ref.at[pl.ds(0, block_rows), :])]
    for start, parts, has_meta, piece in pieces:
        rows = pl.ds(start * block_rows, piece.shape[0])
        for i, part in enumerate(parts):
            copies.append(
                (piece.at[:, pl.ds(i * quarter, quarter)], rows_ref.at[rows, columns_of(part)])
            )
        if has_meta:
            copies.append((piece.at[:, pl.ds(piece.shape[1] - 128, 128)], meta_ref.at[rows, :]))
    copies = [
        pltpu.make_async_copy(source, target, sems.at[i])
        for i, (source, target) in enumerate(copies)
    ]
    for one in copies:
        one.start()
    for one in copies:
        one.wait()
    meta = meta_ref[...].astype(jnp.float32)
    gates = sum(pltpu.roll(meta, 128 - i * top, 1) for i in range(1, 4))
    lane = lax.broadcasted_iota(jnp.int32, meta.shape, 1)
    for e in range(experts):
        name = (ep_rank * experts + e).astype(jnp.float32)
        mine = jnp.where((lane < top) & (meta == name), gates, 0.0)
        table_ref[:, e : e + 1] = jnp.sum(mine, axis=1, keepdims=True)
    stride = math.gcd(total_rows, ROWS)
    for e in range(experts):

        @pl.loop(0, total_rows // stride)
        def _(step):
            at = pl.ds(pl.multiple_of(step * stride, stride), stride)
            rows = rows_ref[at, :]
            gate = jnp.dot(rows, gate_ref[e], preferred_element_type=jnp.float32)
            up = jnp.dot(rows, up_ref[e], preferred_element_type=jnp.float32)
            act = gate / (1.0 + jnp.exp(-gate)) * up * table_ref[at, e : e + 1]
            inner_ref[at, e * units : (e + 1) * units] = act.astype(jnp.bfloat16)

    for part, out_ref in ((3, cross_ref), (1, side_ref), (2, sent_ref), (0, kept_ref)):

        @pl.loop(0, total_rows // stride)
        def _(step):
            at = pl.ds(pl.multiple_of(step * stride, stride), stride)
            weight = down_ref[:, :, columns_of(part)].reshape(experts * units, quarter)
            out_ref[at, :] = jnp.dot(
                inner_ref[at, :], weight, preferred_element_type=jnp.float32
            ).astype(jnp.bfloat16)


def run_experts(ranks, hidden, pieces, weights, rows, columns, top):
    width = hidden.shape[1]
    experts, _, units = weights[0].shape
    arrays = [piece for *_, piece in pieces]
    count = 1 + sum(len(parts) + has_meta for _, parts, has_meta, _ in pieces)

    def kernel(ranks_ref, hidden_ref, refs, *others):
        named = [(*about[:3], ref) for about, ref in zip(pieces, refs)]
        experts_kernel(top, ranks_ref, hidden_ref, named, *others)

    need = 2 * rows * (width + 128 + experts * units) + 512 * rows
    return pl.pallas_call(
        kernel,
        out_shape=[pltpu.VMEM((rows, columns), jnp.bfloat16)] * 4,
        in_specs=[IN_SMEM, ANYWHERE, [ANYWHERE] * len(arrays), IN_VMEM, IN_VMEM, IN_VMEM],
        out_specs=[IN_VMEM] * 4,
        scratch_shapes=[
            pltpu.VMEM((rows, width), jnp.bfloat16),
            pltpu.VMEM((rows, 128), jnp.bfloat16),
            pltpu.VMEM((rows, experts * units), jnp.bfloat16),
            pltpu.VMEM((rows, 128), jnp.float32),
            pltpu.SemaphoreType.DMA((count,)),
        ],
        compiler_params=pltpu.CompilerParams(vmem_limit_bytes=need + 6 * MIB),
        cost_estimate=pl.CostEstimate(
            flops=6 * rows * width * units * experts,
            bytes_accessed=4 * rows * width,
            transcendentals=rows * units * experts,
        ),
        name="experts",
    )(ranks, in_hbm(hidden), arrays, *[in_vmem(w) for w in weights])


def total_of(*terms):
    value = terms[0].astype(jnp.float32)
    for term in terms[1:]:
        value = value + term.astype(jnp.float32)
    return value.astype(jnp.bfloat16)


def local(
    cache_pages,
    queries,
    lengths,
    swap_slot,
    swap_mask,
    hidden,
    expert_ids,
    gate_weights,
    w_gate,
    w_up,
    w_down,
):
    groups = lax.axis_size("tp")
    ep_size = lax.axis_size("ep")
    ranks = jnp.stack([lax.axis_index("ep"), lax.axis_index("tp")]).astype(jnp.int32)
    mask_value = swap_mask[0]
    columns = hidden.shape[1] // groups
    top = expert_ids.shape[1]
    cache_pages = jnp.swapaxes(cache_pages, 1, 2)
    queries = jnp.swapaxes(queries, 1, 2)

    rows = hidden.shape[0]
    pairs = ep_size // 2
    late = list(range(2, pairs))
    half = len(late) // 2
    evens, odds = 4, 4 + len(late)

    def cut(array, start, count):
        return lax.slice_in_dim(array, start * rows, (start + count) * rows, axis=0)

    def bare(array):
        return array[:, :columns]

    own, both, page = pick(
        ranks, swap_slot, expert_ids, gate_weights, hidden, cache_pages, groups
    )
    late_pieces = [flip(own, "ep", 2 * m) for m in late]
    near_2 = flip(own, "ep", 2)
    both_1 = flip(both, "ep", 1)
    far_2 = flip(bare(near_2), "tp", 2)
    near_3 = flip(near_2, "ep", 1)
    far_3 = flip(bare(near_3), "tp", 2)

    levels = ep_size.bit_length() - 1

    def page_hop(page, level):
        swapped = flip(page, "ep", 1 << level)
        bit = jnp.bitwise_and(jnp.right_shift(mask_value, level), 1) == 1
        return jnp.where(bit, swapped, page)

    attended, *weights = attend_all(
        ranks, lengths, queries, cache_pages, groups, w_gate, w_up, w_down
    )
    page = page_hop(page, 0)
    near_late = jnp.concatenate(late_pieces, axis=0)
    near_late, attended, page = lax.optimization_barrier((near_late, attended, page))

    far_late = flip(bare(near_late), "tp", 2)
    near_odds = flip(near_late, "ep", 1)
    far_odds_y = flip(bare(cut(near_odds, 0, half)), "tp", 2)
    far_odds_x = flip(cut(far_late, half, len(late) - half), "ep", 1)
    pieces = [
        (0, (), True, own),
        (1, (0, 2), True, both_1),
        (1, (1, 3), False, flip(both_1, "tp", 1)),
    ]
    for start, part, array in (
        (2, 0, near_2),
        (2, 2, far_2),
        (3, 0, near_3),
        (3, 2, far_3),
        (evens, 0, near_late),
        (evens, 2, far_late),
        (odds, 0, near_odds),
        (odds, 2, far_odds_y),
        (odds + half, 2, far_odds_x),
    ):
        pieces += [
            (start, (part,), part == 0, array),
            (start, (part ^ 1,), False, flip(array, "tp", 1)),
        ]

    for level in range(levels - 1, 1, -1):
        page = page_hop(page, level)
    ranks, page = lax.optimization_barrier((ranks, page))
    if levels > 1:
        page = page_hop(page, 1)
    attended = attend_traded(
        ranks, lengths, swap_slot, swap_mask, queries, page, attended, groups
    )

    cross, side, sent, kept = run_experts(
        ranks, hidden, pieces, weights, ep_size * rows, columns, top
    )
    cross = flip(cross, "tp", 1)
    side = flip(side, "tp", 1)

    def sent_of(start, count):
        return total_of(cut(sent, start, count), cut(cross, start, count))

    def kept_of(start, count):
        return total_of(cut(kept, start, count), cut(side, start, count))

    rest = len(late) - half
    over_y = flip(sent_of(odds, half), "tp", 2)
    over_x = flip(sent_of(odds + half, rest), "ep", 1)
    over_3 = flip(sent_of(3, 1), "tp", 2)
    over_2 = flip(sent_of(2, 1), "tp", 2)
    over_1 = flip(jnp.concatenate([kept_of(1, 1), sent_of(1, 1)], axis=1), "ep", 1)
    odd = total_of(kept_of(odds, len(late)), jnp.pad(over_y, ((0, rest * rows), (0, 0))))
    odd = flip(odd, "ep", 1)
    even = total_of(sent_of(evens, len(late)), jnp.pad(over_x, ((half * rows, 0), (0, 0))))
    even = flip(even, "tp", 2)
    near_3 = flip(total_of(kept_of(3, 1), over_3), "ep", 1)
    zero = flip(total_of(sent_of(0, 1), over_1[:, columns:]), "tp", 2)
    even = total_of(kept_of(evens, len(late)), even, odd)
    back = [flip(cut(even, i, 1), "ep", 2 * m) for i, m in enumerate(late)]
    back.append(flip(total_of(kept_of(2, 1), over_2, near_3), "ep", 2))
    moe_out = total_of(kept_of(0, 1), over_1[:, :columns], zero, *back)
    return attended, moe_out


def solution(mesh):
    in_specs = (
        P(("ep", "tp"), None, None),
        P(("ep", "tp"), None, None),
        P(),
        P(),
        P(),
        P("ep", None),
        P("ep", None),
        P("ep", None),
        P("ep", None, "tp"),
        P("ep", None, "tp"),
        P("ep", "tp", None),
    )
    out_specs = (P(("ep", "tp"), None, None), P("ep", "tp"))
    return jax.shard_map(local, mesh=mesh, in_specs=in_specs, out_specs=out_specs, check_vma=False)
```

time: 154 us -> 104 us (0.68)
  local copies, waits for them, and re-layouts: 26.3 us -> 2.8 us
  other arithmetic: 13.9 us -> 1.6 us
  waiting for transfers between devices: 44.7 us -> 35 us
  starting transfers between devices: 41.4 us -> 34.7 us
  Pallas kernels: 22.8 us -> 27.5 us
  between operations: 4.05 us -> 1.53 us
    unnamed x56 -> x12, local copies, waits for them, and re-layouts: 22.5 us -> 2.72 us
    ppermute x42 -> x38, waiting for transfers between devices: 44.7 us -> 35 us  [flip(): return lax.ppermute(block, axis, [(i, i ^ apart) for i in range(count)])]
    convert_element_type x9, other arithmetic: 9.96 us -> 1.37 us  [total_of(): return value.astype(jnp.bfloat16)]
    ppermute x42 -> x38, starting transfers between devices: 41.4 us -> 34.7 us  [flip(): return lax.ppermute(block, axis, [(i, i ^ apart) for i in range(count)])]
    pallas_call x3 -> x4, Pallas kernels: 22.8 us -> 27.5 us  [the longest x1 12.1 us: attend_all(): pl.pallas_call(functools.partial(attend_kernel, each, groups), out_shape=...]
    dynamic_slice x3 -> x0, local copies, waits for them, and re-layouts: 3.62 us -> none  [the longest x1 1.37 us: local(): my_slot = swap_slot[device]]
    select_n x3, other arithmetic: 1.78 us -> 0.11 us  [page_hop(): return jnp.where(bit, swapped, page)]
  transfers between devices with their start and end apart: 42 -> 38, of which waited for: 18 -> 17; matrix products, arithmetic and copies ran while one was open for 9% -> 1% of each run, Pallas kernels for 5% -> 14%
where the time goes in v4:
time: 104 us; the launch traced here: 103 us
  waiting for transfers between devices  35 us (34%)
  starting transfers between devices  34.7 us (33%)
  Pallas kernels  27.5 us (26%)
  local copies, waits for them, and re-layouts  2.8 us (3%)
  other arithmetic  1.6 us (2%)
  between operations  1.53 us (1%)
    ppermute x38, waiting for transfers between devices, flip(): return lax.ppermute(block, axis, [(i, i ^ apart) for i in range(count)])  35 us
    ppermute x38, starting transfers between devices, flip(): return lax.ppermute(block, axis, [(i, i ^ apart) for i in range(count)])  34.7 us
    pallas_call x1, Pallas kernels, attend_all(): pl.pallas_call(functools.partial(attend_kernel, each, groups), out_shape=...  12.1 us
    pallas_call x1, Pallas kernels, run_experts(): pl.pallas_call(kernel, out_shape=[pltpu.VMEM((rows, columns), jnp.bfloat1...  11 us
    unnamed x12, local copies, waits for them, and re-layouts  2.72 us
    pallas_call x1, Pallas kernels, attend_traded(): pl.pallas_call(functools.partial(attend_traded_kernel, groups), out_shape...  2.71 us
  transfers between devices with their start and end apart: 38, of which 17 were waited for; matrix products, arithmetic and copies ran while one was open for 1% of the time, Pallas kernels for 14%

profile of v4, /device:TPU:0, one launch (start us, length us, event | category | flops | bytes accessed | tf_op | source)
XLA Modules:
  0.0 103.1 jit_solution(16037773714126027665)
XLA Ops:
  2.7 1.7 %pick.1 = (bf16[64,1024]{1,0:T(8,128)(2,1)S(1)}, bf16[64,1920]{1,0:T(8,128)(2,1)S(1)}, bf16[576,256]{1,0:T(8,128)(2,1)S(1)}) custom-call(s32[2]{0:T(128)S(1)} %pad_add_fusion.ranks_ref, s32[32]{0:T(128)S(1)} %copy-done.4, s32[8,64]{1,0:T(8,128)S(1)} %bitcast.9, f32[8,64]{1,0:T(8,128)S(1)} %bitcast.10, bf16[64,3584]{1,0:T(8,128)(2,1)} %hidden_ref.3, ...), custom_call_target="tpu_custom_call" | custom-call | tf_op jit(solution)/shard_map/pick/pallas_call | solution.py:96
  4.5 3.0 %collective-permute-start.2 = (bf16[576,256]{1,0:T(8,128)(2,1)S(1)}, bf16[576,256]{1,0:T(8,128)(2,1)S(1)}, u32[]{:S(2)}, u32[]{:S(2)}) collective-permute-start(bf16[576,256]{1,0:T(8,128)(2,1)S(1)} %get-tuple-element.20), channel_id=1, source_target_pairs={{0,4},{4,0},{8,12},{12,8},{16,20},{20,16},{24,28},{28,24},{1,5},{5... | collective-permute-start | bytes 884744 | tf_op jit(solution)/shard_map/ppermute | solution.py:20
  7.5 1.6 %collective-permute-start.7 = (bf16[64,1024]{1,0:T(8,128)(2,1)S(1)}, bf16[64,1024]{1,0:T(8,128)(2,1)S(1)}, u32[]{:S(2)}, u32[]{:S(2)}) collective-permute-start(bf16[64,1024]{1,0:T(8,128)(2,1)S(1)} %get-tuple-element.18.refs_0_), channel_id=1, source_target_pairs={{0,8},{4,12},{8,0},{12,4},{16,24},{20,28},{24,16},{28,20},{1,9},{5... | collective-permute-start | bytes 393224 | tf_op jit(solution)/shard_map/ppermute | solution.py:20
  9.0 2.5 %collective-permute-start.1 = (bf16[64,1024]{1,0:T(8,128)(2,1)S(1)}, bf16[64,1024]{1,0:T(8,128)(2,1)S(1)}, u32[]{:S(2)}, u32[]{:S(2)}) collective-permute-start(bf16[64,1024]{1,0:T(8,128)(2,1)S(1)} %get-tuple-element.18.refs_0_), channel_id=1, source_target_pairs={{0,24},{4,28},{8,16},{12,20},{16,8},{20,12},{24,0},{28,4},{1,25},{... | collective-permute-start | bytes 393224 | tf_op jit(solution)/shard_map/ppermute | solution.py:20
  13.5 12.1 %attend_local.1 = (bf16[16,128,512]{2,1,0:T(8,128)(2,1)}, bf16[3,3584,256]{2,1,0:T(8,128)(2,1)S(1)}, bf16[3,3584,256]{2,1,0:T(8,128)(2,1)S(1)}, bf16[3,256,3584]{2,1,0:T(8,128)(2,1)S(1)}) custom-call(s32[2]{0:T(128)S(1)} %pad_add_fusion.ranks_ref, s32[512]{0:T(512)S(1)} %copy-done, bf16[16,576,128]{2,1,0:T(8,128)(2,1)} %bitcast.13, ...), custom_call_target="tpu_custom_call" | custom-call | flops 1140850688 | bytes 25690112 | tf_op jit(solution)/shard_map/attend_local/pallas_call | solution.py:155
  25.6 1.6 %collective-permute-start.11 = (bf16[64,1024]{1,0:T(8,128)(2,1)S(1)}, bf16[64,1024]{1,0:T(8,128)(2,1)S(1)}, u32[]{:S(2)}, u32[]{:S(2)}) collective-permute-start(bf16[64,1024]{1,0:T(8,128)(2,1)S(1)} %collective-permute-done.7.refs_3_), channel_id=1, source_target_pairs={{0,4},{4,0},{8,12},{12,8},{16,20},{20,16},{24,28},{28,24},{1,5},{5... | collective-permute-start | bytes 393224 | tf_op jit(solution)/shard_map/ppermute | solution.py:20
  27.3 1.6 %collective-permute-start.16 = (bf16[128,896]{1,0:T(8,128)(2,1)S(1)}, bf16[128,896]{1,0:T(8,128)(2,1)S(1)}, u32[]{:S(2)}, u32[]{:S(2)}) collective-permute-start(bf16[128,896]{1,0:T(8,128)(2,1)S(1)} %slice.109), channel_id=1, source_target_pairs={{0,2},{1,3},{2,0},{3,1},{4,6},{5,7},{6,4},{7,5},{8,10},{9,11},{10,... | collective-permute-start | bytes 688136 | tf_op jit(solution)/shard_map/ppermute | solution.py:20
  29.5 1.2 %collective-permute-done.11.refs_7_ = bf16[64,1024]{1,0:T(8,128)(2,1)S(1)} collective-permute-done((bf16[64,1024]{1,0:T(8,128)(2,1)S(1)}, bf16[64,1024]{1,0:T(8,128)(2,1)S(1)}, u32[]{:S(2)}, u32[]{:S(2)}) %collective-permute-start.11) | collective-permute-done | bytes 131104 | tf_op jit(solution)/shard_map/ppermute | solution.py:20
  30.7 1.5 %collective-permute-start.18 = (bf16[128,1024]{1,0:T(8,128)(2,1)S(1)}, bf16[128,1024]{1,0:T(8,128)(2,1)S(1)}, u32[]{:S(2)}, u32[]{:S(2)}) collective-permute-start(bf16[128,1024]{1,0:T(8,128)(2,1)S(1)} %pad_maximum_fusion.refs_11_), channel_id=1, source_target_pairs={{0,4},{4,0},{8,12},{12,8},{16,20},{20,16},{24,28},{28,24},{1,5},{5... | collective-permute-start | bytes 786440 | tf_op jit(solution)/shard_map/ppermute | solution.py:20
  32.2 1.6 %collective-permute-start.13 = (bf16[64,896]{1,0:T(8,128)(2,1)S(1)}, bf16[64,896]{1,0:T(8,128)(2,1)S(1)}, u32[]{:S(2)}, u32[]{:S(2)}) collective-permute-start(bf16[64,896]{1,0:T(8,128)(2,1)S(1)} %slice.143), channel_id=1, source_target_pairs={{0,2},{1,3},{2,0},{3,1},{4,6},{5,7},{6,4},{7,5},{8,10},{9,11},{10,... | collective-permute-start | bytes 344072 | tf_op jit(solution)/shard_map/ppermute | solution.py:20
  33.8 3.2 %collective-permute-done.9.refs_5_ = bf16[64,896]{1,0:T(8,128)(2,1)S(1)} collective-permute-done((bf16[64,896]{1,0:T(8,128)(2,1)S(1)}, bf16[64,896]{1,0:T(8,128)(2,1)S(1)}, u32[]{:S(2)}, u32[]{:S(2)}) %collective-permute-start.9) | collective-permute-done | bytes 114720 | tf_op jit(solution)/shard_map/ppermute | solution.py:20
  37.0 2.6 %collective-permute-start.3 = (bf16[576,256]{1,0:T(8,128)(2,1)S(1)}, bf16[576,256]{1,0:T(8,128)(2,1)S(1)}, u32[]{:S(2)}, u32[]{:S(2)}) collective-permute-start(bf16[576,256]{1,0:T(8,128)(2,1)S(1)} %broadcast_select_fusion.1), channel_id=1, source_target_pairs={{0,16},{4,20},{8,24},{12,28},{16,0},{20,4},{24,8},{28,12},{1,17},{... | collective-permute-start | bytes 884744 | tf_op jit(solution)/shard_map/ppermute | solution.py:20
  42.0 1.5 %collective-permute-start.20 = (bf16[64,896]{1,0:T(8,128)(2,1)S(1)}, bf16[64,896]{1,0:T(8,128)(2,1)S(1)}, u32[]{:S(2)}, u32[]{:S(2)}) collective-permute-start(bf16[64,896]{1,0:T(8,128)(2,1)S(1)} %slice.144), channel_id=1, source_target_pairs={{0,2},{1,3},{2,0},{3,1},{4,6},{5,7},{6,4},{7,5},{8,10},{9,11},{10,... | collective-permute-start | bytes 344072 | tf_op jit(solution)/shard_map/ppermute | solution.py:20
  44.0 5.4 %collective-permute-done.3 = bf16[576,256]{1,0:T(8,128)(2,1)S(1)} collective-permute-done((bf16[576,256]{1,0:T(8,128)(2,1)S(1)}, bf16[576,256]{1,0:T(8,128)(2,1)S(1)}, u32[]{:S(2)}, u32[]{:S(2)}) %collective-permute-start.3) | collective-permute-done | bytes 294944 | tf_op jit(solution)/shard_map/ppermute | solution.py:20
  51.3 11.0 %experts.1 = (bf16[512,896]{1,0:T(8,128)(2,1)S(1)}, bf16[512,896]{1,0:T(8,128)(2,1)S(1)}, bf16[512,896]{1,0:T(8,128)(2,1)S(1)}, bf16[512,896]{1,0:T(8,128)(2,1)S(1)}) custom-call(s32[2]{0:T(128)S(1)} %pad_add_fusion.ranks_ref, bf16[64,3584]{1,0:T(8,128)(2,1)} %hidden_ref.3, bf16[64,1024]{1,0:T(8,128)(2,1)S(1)} %get-tuple-element.18.refs_0_, ...), custom_call_target="tpu_custom_call" | custom-call | flops 8455716864 | bytes 7340032 | tf_op jit(solution)/shard_map/experts/pallas_call | solution.py:305
  62.9 2.0 %collective-permute-done.25 = bf16[512,896]{1,0:T(8,128)(2,1)S(1)} collective-permute-done((bf16[512,896]{1,0:T(8,128)(2,1)S(1)}, bf16[512,896]{1,0:T(8,128)(2,1)S(1)}, u32[]{:S(2)}, u32[]{:S(2)}) %collective-permute-start.25) | collective-permute-done | bytes 917536 | tf_op jit(solution)/shard_map/ppermute | solution.py:20
  64.9 1.3 %collective-permute-done.24 = bf16[512,896]{1,0:T(8,128)(2,1)S(1)} collective-permute-done((bf16[512,896]{1,0:T(8,128)(2,1)S(1)}, bf16[512,896]{1,0:T(8,128)(2,1)S(1)}, u32[]{:S(2)}, u32[]{:S(2)}) %collective-permute-start.24) | collective-permute-done | bytes 917536 | tf_op jit(solution)/shard_map/ppermute | solution.py:20
  66.8 7.1 %collective-permute-done.26 = bf16[64,1792]{1,0:T(8,128)(2,1)S(1)} collective-permute-done((bf16[64,1792]{1,0:T(8,128)(2,1)S(1)}, bf16[64,1792]{1,0:T(8,128)(2,1)S(1)}, u32[]{:S(2)}, u32[]{:S(2)}) %collective-permute-start.26) | collective-permute-done | bytes 229408 | tf_op jit(solution)/shard_map/ppermute | solution.py:20
  74.2 1.6 %collective-permute-start.35 = (bf16[64,896]{1,0:T(8,128)(2,1)S(1)}, bf16[64,896]{1,0:T(8,128)(2,1)S(1)}, u32[]{:S(2)}, u32[]{:S(2)}) collective-permute-start(bf16[64,896]{1,0:T(8,128)(2,1)S(1)} %get-tuple-element.35), channel_id=1, source_target_pairs={{0,2},{1,3},{2,0},{3,1},{4,6},{5,7},{6,4},{7,5},{8,10},{9,11},{10,... | collective-permute-start | bytes 344072 | tf_op jit(solution)/shard_map/ppermute | solution.py:20
  76.3 1.5 %collective-permute-start.30 = (bf16[64,896]{1,0:T(8,128)(2,1)S(1)}, bf16[64,896]{1,0:T(8,128)(2,1)S(1)}, u32[]{:S(2)}, u32[]{:S(2)}) collective-permute-start(bf16[64,896]{1,0:T(8,128)(2,1)S(1)} %get-tuple-element.37), channel_id=1, source_target_pairs={{0,2},{1,3},{2,0},{3,1},{4,6},{5,7},{6,4},{7,5},{8,10},{9,11},{10,... | collective-permute-start | bytes 344072 | tf_op jit(solution)/shard_map/ppermute | solution.py:20
  78.3 2.0 %collective-permute-done.35 = bf16[64,896]{1,0:T(8,128)(2,1)S(1)} collective-permute-done((bf16[64,896]{1,0:T(8,128)(2,1)S(1)}, bf16[64,896]{1,0:T(8,128)(2,1)S(1)}, u32[]{:S(2)}, u32[]{:S(2)}) %collective-permute-start.35) | collective-permute-done | bytes 114720 | tf_op jit(solution)/shard_map/ppermute | solution.py:20
  80.3 1.5 %collective-permute-start.27 = (bf16[64,896]{1,0:T(8,128)(2,1)S(1)}, bf16[64,896]{1,0:T(8,128)(2,1)S(1)}, u32[]{:S(2)}, u32[]{:S(2)}) collective-permute-start(bf16[64,896]{1,0:T(8,128)(2,1)S(1)} %get-tuple-element.34), channel_id=1, source_target_pairs={{0,2},{1,3},{2,0},{3,1},{4,6},{5,7},{6,4},{7,5},{8,10},{9,11},{10,... | collective-permute-start | bytes 344072 | tf_op jit(solution)/shard_map/ppermute | solution.py:20
  81.9 2.9 %collective-permute-done.30 = bf16[64,896]{1,0:T(8,128)(2,1)S(1)} collective-permute-done((bf16[64,896]{1,0:T(8,128)(2,1)S(1)}, bf16[64,896]{1,0:T(8,128)(2,1)S(1)}, u32[]{:S(2)}, u32[]{:S(2)}) %collective-permute-start.30) | collective-permute-done | bytes 114720 | tf_op jit(solution)/shard_map/ppermute | solution.py:20
  85.4 1.5 %collective-permute-start.31 = (bf16[128,896]{1,0:T(8,128)(2,1)S(1)}, bf16[128,896]{1,0:T(8,128)(2,1)S(1)}, u32[]{:S(2)}, u32[]{:S(2)}) collective-permute-start(bf16[128,896]{1,0:T(8,128)(2,1)S(1)} %add_convert_fusion.1), channel_id=1, source_target_pairs={{0,4},{4,0},{8,12},{12,8},{16,20},{20,16},{24,28},{28,24},{1,5},{5... | collective-permute-start | bytes 688136 | tf_op jit(solution)/shard_map/ppermute | solution.py:20
  87.0 1.6 %collective-permute-start.29 = (bf16[128,896]{1,0:T(8,128)(2,1)S(1)}, bf16[128,896]{1,0:T(8,128)(2,1)S(1)}, u32[]{:S(2)}, u32[]{:S(2)}) collective-permute-start(bf16[128,896]{1,0:T(8,128)(2,1)S(1)} %add_convert_fusion.3), channel_id=1, source_target_pairs={{0,2},{1,3},{2,0},{3,1},{4,6},{5,7},{6,4},{7,5},{8,10},{9,11},{10,... | collective-permute-start | bytes 688136 | tf_op jit(solution)/shard_map/ppermute | solution.py:20
  88.6 1.0 collective-permute-done.36
  90.2 1.8 %collective-permute-done.31 = bf16[128,896]{1,0:T(8,128)(2,1)S(1)} collective-permute-done((bf16[128,896]{1,0:T(8,128)(2,1)S(1)}, bf16[128,896]{1,0:T(8,128)(2,1)S(1)}, u32[]{:S(2)}, u32[]{:S(2)}) %collective-permute-start.31) | collective-permute-done | bytes 229408 | tf_op jit(solution)/shard_map/ppermute | solution.py:20
  92.0 1.1 %collective-permute-done.29 = bf16[128,896]{1,0:T(8,128)(2,1)S(1)} collective-permute-done((bf16[128,896]{1,0:T(8,128)(2,1)S(1)}, bf16[128,896]{1,0:T(8,128)(2,1)S(1)}, u32[]{:S(2)}, u32[]{:S(2)}) %collective-permute-start.29) | collective-permute-done | bytes 229408 | tf_op jit(solution)/shard_map/ppermute | solution.py:20
  93.3 2.4 %collective-permute-start.33 = (bf16[64,896]{1,0:T(8,128)(2,1)S(1)}, bf16[64,896]{1,0:T(8,128)(2,1)S(1)}, u32[]{:S(2)}, u32[]{:S(2)}) collective-permute-start(bf16[64,896]{1,0:T(8,128)(2,1)S(1)} %get-tuple-element.40), channel_id=1, source_target_pairs={{0,24},{4,28},{8,16},{12,20},{16,8},{20,12},{24,0},{28,4},{1,25},{... | collective-permute-start | bytes 344072 | tf_op jit(solution)/shard_map/ppermute | solution.py:20
  95.7 2.7 %attend_traded.1 = bf16[16,128,512]{2,1,0:T(8,128)(2,1)} custom-call(s32[2]{0:T(128)S(1)} %pad_add_fusion.ranks_ref, s32[512]{0:T(512)S(1)} %copy-done.1, s32[32]{0:T(128)S(1)} %copy-done.5, s32[1]{0:T(128)S(6)} %copy.15.mask_ref, bf16[16,576,128]{2,1,0:T(8,128)(2,1)} %bitcast.14, ...), custom_call_target="tpu_custom_call", output_to_operand_aliasing={{}: (6, {})} | custom-call | flops 71303168 | bytes 573440 | tf_op jit(solution)/shard_map/attend_traded/pallas_call | solution.py:196
  98.5 1.5 %collective-permute-done.33 = bf16[64,896]{1,0:T(8,128)(2,1)S(1)} collective-permute-done((bf16[64,896]{1,0:T(8,128)(2,1)S(1)}, bf16[64,896]{1,0:T(8,128)(2,1)S(1)}, u32[]{:S(2)}, u32[]{:S(2)}) %collective-permute-start.33) | collective-permute-done | bytes 114720 | tf_op jit(solution)/shard_map/ppermute | solution.py:20
  99.9 2.5 %collective-permute-done.32 = bf16[64,896]{1,0:T(8,128)(2,1)S(1)} collective-permute-done((bf16[64,896]{1,0:T(8,128)(2,1)S(1)}, bf16[64,896]{1,0:T(8,128)(2,1)S(1)}, u32[]{:S(2)}, u32[]{:S(2)}) %collective-permute-start.32) | collective-permute-done | bytes 114720 | tf_op jit(solution)/shard_map/ppermute | solution.py:20
  (81 shorter events, 13.7 us)
Async XLA Ops:
  4.5 22.8 %collective-permute-start.2 = (bf16[576,256]{1,0:T(8,128)(2,1)S(1)}, bf16[576,256]{1,0:T(8,128)(2,1)S(1)}, u32[]{:S(2)}, u32[]{:S(2)}) collective-permute-start(bf16[576,256]{1,0:T(8,128)(2,1)S(1)} %get-tuple-element.20), channel_id=1, source_target_pairs={{0,4},{4,0},{8,12},{12,8},{16,20},{20,16},{24,28},{28,24},{1,5},{5... | collective-permute-start | bytes 884744 | tf_op jit(solution)/shard_map/ppermute | solution.py:20
  7.5 18.2 %collective-permute-start.7 = (bf16[64,1024]{1,0:T(8,128)(2,1)S(1)}, bf16[64,1024]{1,0:T(8,128)(2,1)S(1)}, u32[]{:S(2)}, u32[]{:S(2)}) collective-permute-start(bf16[64,1024]{1,0:T(8,128)(2,1)S(1)} %get-tuple-element.18.refs_0_), channel_id=1, source_target_pairs={{0,8},{4,12},{8,0},{12,4},{16,24},{20,28},{24,16},{28,20},{1,9},{5... | collective-permute-start | bytes 393224 | tf_op jit(solution)/shard_map/ppermute | solution.py:20
  9.0 18.1 %collective-permute-start.1 = (bf16[64,1024]{1,0:T(8,128)(2,1)S(1)}, bf16[64,1024]{1,0:T(8,128)(2,1)S(1)}, u32[]{:S(2)}, u32[]{:S(2)}) collective-permute-start(bf16[64,1024]{1,0:T(8,128)(2,1)S(1)} %get-tuple-element.18.refs_0_), channel_id=1, source_target_pairs={{0,24},{4,28},{8,16},{12,20},{16,8},{20,12},{24,0},{28,4},{1,25},{... | collective-permute-start | bytes 393224 | tf_op jit(solution)/shard_map/ppermute | solution.py:20
  11.5 15.7 %collective-permute-start = (bf16[64,1024]{1,0:T(8,128)(2,1)S(1)}, bf16[64,1024]{1,0:T(8,128)(2,1)S(1)}, u32[]{:S(2)}, u32[]{:S(2)}) collective-permute-start(bf16[64,1024]{1,0:T(8,128)(2,1)S(1)} %get-tuple-element.18.refs_0_), channel_id=1, source_target_pairs={{0,16},{4,20},{8,24},{12,28},{16,0},{20,4},{24,8},{28,12},{1,17},{... | collective-permute-start | bytes 393224 | tf_op jit(solution)/shard_map/ppermute | solution.py:20
  11.6 20.5 %collective-permute-start.5 = (bf16[64,1920]{1,0:T(8,128)(2,1)S(1)}, bf16[64,1920]{1,0:T(8,128)(2,1)S(1)}, u32[]{:S(2)}, u32[]{:S(2)}) collective-permute-start(bf16[64,1920]{1,0:T(8,128)(2,1)S(1)} %get-tuple-element.25), channel_id=1, source_target_pairs={{0,4},{4,0},{8,12},{12,8},{16,20},{20,16},{24,28},{28,24},{1,5},{5... | collective-permute-start | bytes 737288 | tf_op jit(solution)/shard_map/ppermute | solution.py:20
  25.6 5.0 %collective-permute-start.11 = (bf16[64,1024]{1,0:T(8,128)(2,1)S(1)}, bf16[64,1024]{1,0:T(8,128)(2,1)S(1)}, u32[]{:S(2)}, u32[]{:S(2)}) collective-permute-start(bf16[64,1024]{1,0:T(8,128)(2,1)S(1)} %collective-permute-done.7.refs_3_), channel_id=1, source_target_pairs={{0,4},{4,0},{8,12},{12,8},{16,20},{20,16},{24,28},{28,24},{1,5},{5... | collective-permute-start | bytes 393224 | tf_op jit(solution)/shard_map/ppermute | solution.py:20
  27.3 12.8 %collective-permute-start.16 = (bf16[128,896]{1,0:T(8,128)(2,1)S(1)}, bf16[128,896]{1,0:T(8,128)(2,1)S(1)}, u32[]{:S(2)}, u32[]{:S(2)}) collective-permute-start(bf16[128,896]{1,0:T(8,128)(2,1)S(1)} %slice.109), channel_id=1, source_target_pairs={{0,2},{1,3},{2,0},{3,1},{4,6},{5,7},{6,4},{7,5},{8,10},{9,11},{10,... | collective-permute-start | bytes 688136 | tf_op jit(solution)/shard_map/ppermute | solution.py:20
  28.9 8.1 %collective-permute-start.9 = (bf16[64,896]{1,0:T(8,128)(2,1)S(1)}, bf16[64,896]{1,0:T(8,128)(2,1)S(1)}, u32[]{:S(2)}, u32[]{:S(2)}) collective-permute-start(bf16[64,896]{1,0:T(8,128)(2,1)S(1)} %slice.142), channel_id=1, source_target_pairs={{0,2},{1,3},{2,0},{3,1},{4,6},{5,7},{6,4},{7,5},{8,10},{9,11},{10,... | collective-permute-start | bytes 344072 | tf_op jit(solution)/shard_map/ppermute | solution.py:20
  29.5 10.1 %collective-permute-start.8 = (bf16[64,1024]{1,0:T(8,128)(2,1)S(1)}, bf16[64,1024]{1,0:T(8,128)(2,1)S(1)}, u32[]{:S(2)}, u32[]{:S(2)}) collective-permute-start(bf16[64,1024]{1,0:T(8,128)(2,1)S(1)} %collective-permute-done.7.refs_3_), channel_id=1, source_target_pairs={{0,1},{1,0},{2,3},{3,2},{4,5},{5,4},{6,7},{7,6},{8,9},{9,8},{10,11... | collective-permute-start | bytes 393224 | tf_op jit(solution)/shard_map/ppermute | solution.py:20
  30.7 9.5 %collective-permute-start.18 = (bf16[128,1024]{1,0:T(8,128)(2,1)S(1)}, bf16[128,1024]{1,0:T(8,128)(2,1)S(1)}, u32[]{:S(2)}, u32[]{:S(2)}) collective-permute-start(bf16[128,1024]{1,0:T(8,128)(2,1)S(1)} %pad_maximum_fusion.refs_11_), channel_id=1, source_target_pairs={{0,4},{4,0},{8,12},{12,8},{16,20},{20,16},{24,28},{28,24},{1,5},{5... | collective-permute-start | bytes 786440 | tf_op jit(solution)/shard_map/ppermute | solution.py:20
  32.2 7.4 %collective-permute-start.13 = (bf16[64,896]{1,0:T(8,128)(2,1)S(1)}, bf16[64,896]{1,0:T(8,128)(2,1)S(1)}, u32[]{:S(2)}, u32[]{:S(2)}) collective-permute-start(bf16[64,896]{1,0:T(8,128)(2,1)S(1)} %slice.143), channel_id=1, source_target_pairs={{0,2},{1,3},{2,0},{3,1},{4,6},{5,7},{6,4},{7,5},{8,10},{9,11},{10,... | collective-permute-start | bytes 344072 | tf_op jit(solution)/shard_map/ppermute | solution.py:20
  37.0 12.4 %collective-permute-start.3 = (bf16[576,256]{1,0:T(8,128)(2,1)S(1)}, bf16[576,256]{1,0:T(8,128)(2,1)S(1)}, u32[]{:S(2)}, u32[]{:S(2)}) collective-permute-start(bf16[576,256]{1,0:T(8,128)(2,1)S(1)} %broadcast_select_fusion.1), channel_id=1, source_target_pairs={{0,16},{4,20},{8,24},{12,28},{16,0},{20,4},{24,8},{28,12},{1,17},{... | collective-permute-start | bytes 884744 | tf_op jit(solution)/shard_map/ppermute | solution.py:20
  39.6 3.9 %collective-permute-start.6 = (bf16[64,1920]{1,0:T(8,128)(2,1)S(1)}, bf16[64,1920]{1,0:T(8,128)(2,1)S(1)}, u32[]{:S(2)}, u32[]{:S(2)}) collective-permute-start(bf16[64,1920]{1,0:T(8,128)(2,1)S(1)} %collective-permute-done.5.refs_1_), channel_id=1, source_target_pairs={{0,1},{1,0},{2,3},{3,2},{4,5},{5,4},{6,7},{7,6},{8,9},{9,8},{10,11... | collective-permute-start | bytes 737288 | tf_op jit(solution)/shard_map/ppermute | solution.py:20
  40.2 3.3 %collective-permute-start.14 = (bf16[64,896]{1,0:T(8,128)(2,1)S(1)}, bf16[64,896]{1,0:T(8,128)(2,1)S(1)}, u32[]{:S(2)}, u32[]{:S(2)}) collective-permute-start(bf16[64,896]{1,0:T(8,128)(2,1)S(1)} %collective-permute-done.13.refs_9_), channel_id=1, source_target_pairs={{0,1},{1,0},{2,3},{3,2},{4,5},{5,4},{6,7},{7,6},{8,9},{9,8},{10,11... | collective-permute-start | bytes 344072 | tf_op jit(solution)/shard_map/ppermute | solution.py:20
  41.4 8.0 %collective-permute-start.22 = (bf16[64,896]{1,0:T(8,128)(2,1)S(1)}, bf16[64,896]{1,0:T(8,128)(2,1)S(1)}, u32[]{:S(2)}, u32[]{:S(2)}) collective-permute-start(bf16[64,896]{1,0:T(8,128)(2,1)S(1)} %slice.145), channel_id=1, source_target_pairs={{0,4},{4,0},{8,12},{12,8},{16,20},{20,16},{24,28},{28,24},{1,5},{5... | collective-permute-start | bytes 344072 | tf_op jit(solution)/shard_map/ppermute | solution.py:20
  42.0 8.0 %collective-permute-start.20 = (bf16[64,896]{1,0:T(8,128)(2,1)S(1)}, bf16[64,896]{1,0:T(8,128)(2,1)S(1)}, u32[]{:S(2)}, u32[]{:S(2)}) collective-permute-start(bf16[64,896]{1,0:T(8,128)(2,1)S(1)} %slice.144), channel_id=1, source_target_pairs={{0,2},{1,3},{2,0},{3,1},{4,6},{5,7},{6,4},{7,5},{8,10},{9,11},{10,... | collective-permute-start | bytes 344072 | tf_op jit(solution)/shard_map/ppermute | solution.py:20
  43.5 6.6 %collective-permute-start.15 = (bf16[128,1024]{1,0:T(8,128)(2,1)S(1)}, bf16[128,1024]{1,0:T(8,128)(2,1)S(1)}, u32[]{:S(2)}, u32[]{:S(2)}) collective-permute-start(bf16[128,1024]{1,0:T(8,128)(2,1)S(1)} %pad_maximum_fusion.refs_11_), channel_id=1, source_target_pairs={{0,1},{1,0},{2,3},{3,2},{4,5},{5,4},{6,7},{7,6},{8,9},{9,8},{10,11... | collective-permute-start | bytes 786440 | tf_op jit(solution)/shard_map/ppermute | solution.py:20
  43.5 7.8 %collective-permute-start.19 = (bf16[128,1024]{1,0:T(8,128)(2,1)S(1)}, bf16[128,1024]{1,0:T(8,128)(2,1)S(1)}, u32[]{:S(2)}, u32[]{:S(2)}) collective-permute-start(bf16[128,1024]{1,0:T(8,128)(2,1)S(1)} %collective-permute-done.18.refs_15_), channel_id=1, source_target_pairs={{0,1},{1,0},{2,3},{3,2},{4,5},{5,4},{6,7},{7,6},{8,9},{9,8},{10,11... | collective-permute-start | bytes 786440 | tf_op jit(solution)/shard_map/ppermute | solution.py:20
  62.5 3.6 %collective-permute-start.24 = (bf16[512,896]{1,0:T(8,128)(2,1)S(1)}, bf16[512,896]{1,0:T(8,128)(2,1)S(1)}, u32[]{:S(2)}, u32[]{:S(2)}) collective-permute-start(bf16[512,896]{1,0:T(8,128)(2,1)S(1)} %get-tuple-element.31), channel_id=1, source_target_pairs={{0,1},{1,0},{2,3},{3,2},{4,5},{5,4},{6,7},{7,6},{8,9},{9,8},{10,11... | collective-permute-start | bytes 2752520 | tf_op jit(solution)/shard_map/ppermute | solution.py:20
  66.2 7.7 %collective-permute-start.26 = (bf16[64,1792]{1,0:T(8,128)(2,1)S(1)}, bf16[64,1792]{1,0:T(8,128)(2,1)S(1)}, u32[]{:S(2)}, u32[]{:S(2)}) collective-permute-start(bf16[64,1792]{1,0:T(8,128)(2,1)S(1)} %pad_maximum_fusion.1), channel_id=1, source_target_pairs={{0,4},{4,0},{8,12},{12,8},{16,20},{20,16},{24,28},{28,24},{1,5},{5... | collective-permute-start | bytes 688136 | tf_op jit(solution)/shard_map/ppermute | solution.py:20
  74.2 6.1 %collective-permute-start.35 = (bf16[64,896]{1,0:T(8,128)(2,1)S(1)}, bf16[64,896]{1,0:T(8,128)(2,1)S(1)}, u32[]{:S(2)}, u32[]{:S(2)}) collective-permute-start(bf16[64,896]{1,0:T(8,128)(2,1)S(1)} %get-tuple-element.35), channel_id=1, source_target_pairs={{0,2},{1,3},{2,0},{3,1},{4,6},{5,7},{6,4},{7,5},{8,10},{9,11},{10,... | collective-permute-start | bytes 344072 | tf_op jit(solution)/shard_map/ppermute | solution.py:20
  75.7 20.0 %collective-permute-start.4 = (bf16[576,256]{1,0:T(8,128)(2,1)S(1)}, bf16[576,256]{1,0:T(8,128)(2,1)S(1)}, u32[]{:S(2)}, u32[]{:S(2)}) collective-permute-start(bf16[576,256]{1,0:T(8,128)(2,1)S(1)} %broadcast_select_fusion.2), channel_id=1, source_target_pairs={{0,8},{4,12},{8,0},{12,4},{16,24},{20,28},{24,16},{28,20},{1,9},{5... | collective-permute-start | bytes 884744 | tf_op jit(solution)/shard_map/ppermute | solution.py:20
  75.7 11.3 %collective-permute-start.34 = (bf16[64,896]{1,0:T(8,128)(2,1)S(1)}, bf16[64,896]{1,0:T(8,128)(2,1)S(1)}, u32[]{:S(2)}, u32[]{:S(2)}) collective-permute-start(bf16[64,896]{1,0:T(8,128)(2,1)S(1)} %get-tuple-element.36), channel_id=1, source_target_pairs={{0,2},{1,3},{2,0},{3,1},{4,6},{5,7},{6,4},{7,5},{8,10},{9,11},{10,... | collective-permute-start | bytes 344072 | tf_op jit(solution)/shard_map/ppermute | solution.py:20
  76.3 8.5 %collective-permute-start.30 = (bf16[64,896]{1,0:T(8,128)(2,1)S(1)}, bf16[64,896]{1,0:T(8,128)(2,1)S(1)}, u32[]{:S(2)}, u32[]{:S(2)}) collective-permute-start(bf16[64,896]{1,0:T(8,128)(2,1)S(1)} %get-tuple-element.37), channel_id=1, source_target_pairs={{0,2},{1,3},{2,0},{3,1},{4,6},{5,7},{6,4},{7,5},{8,10},{9,11},{10,... | collective-permute-start | bytes 344072 | tf_op jit(solution)/shard_map/ppermute | solution.py:20
  77.8 7.6 %collective-permute-start.28 = (bf16[64,896]{1,0:T(8,128)(2,1)S(1)}, bf16[64,896]{1,0:T(8,128)(2,1)S(1)}, u32[]{:S(2)}, u32[]{:S(2)}) collective-permute-start(bf16[64,896]{1,0:T(8,128)(2,1)S(1)} %get-tuple-element.38), channel_id=1, source_target_pairs={{0,4},{4,0},{8,12},{12,8},{16,20},{20,16},{24,28},{28,24},{1,5},{5... | collective-permute-start | bytes 344072 | tf_op jit(solution)/shard_map/ppermute | solution.py:20
  80.3 18.1 %collective-permute-start.27 = (bf16[64,896]{1,0:T(8,128)(2,1)S(1)}, bf16[64,896]{1,0:T(8,128)(2,1)S(1)}, u32[]{:S(2)}, u32[]{:S(2)}) collective-permute-start(bf16[64,896]{1,0:T(8,128)(2,1)S(1)} %get-tuple-element.34), channel_id=1, source_target_pairs={{0,2},{1,3},{2,0},{3,1},{4,6},{5,7},{6,4},{7,5},{8,10},{9,11},{10,... | collective-permute-start | bytes 344072 | tf_op jit(solution)/shard_map/ppermute | solution.py:20
  84.8 4.8 %collective-permute-start.36 = (bf16[64,896]{1,0:T(8,128)(2,1)S(1)}, bf16[64,896]{1,0:T(8,128)(2,1)S(1)}, u32[]{:S(2)}, u32[]{:S(2)}) collective-permute-start(bf16[64,896]{1,0:T(8,128)(2,1)S(1)} %add_convert_fusion.8), channel_id=1, source_target_pairs={{0,4},{4,0},{8,12},{12,8},{16,20},{20,16},{24,28},{28,24},{1,5},{5... | collective-permute-start | bytes 344072 | tf_op jit(solution)/shard_map/ppermute | solution.py:20
  85.4 6.6 %collective-permute-start.31 = (bf16[128,896]{1,0:T(8,128)(2,1)S(1)}, bf16[128,896]{1,0:T(8,128)(2,1)S(1)}, u32[]{:S(2)}, u32[]{:S(2)}) collective-permute-start(bf16[128,896]{1,0:T(8,128)(2,1)S(1)} %add_convert_fusion.1), channel_id=1, source_target_pairs={{0,4},{4,0},{8,12},{12,8},{16,20},{20,16},{24,28},{28,24},{1,5},{5... | collective-permute-start | bytes 688136 | tf_op jit(solution)/shard_map/ppermute | solution.py:20
  87.0 6.1 %collective-permute-start.29 = (bf16[128,896]{1,0:T(8,128)(2,1)S(1)}, bf16[128,896]{1,0:T(8,128)(2,1)S(1)}, u32[]{:S(2)}, u32[]{:S(2)}) collective-permute-start(bf16[128,896]{1,0:T(8,128)(2,1)S(1)} %add_convert_fusion.3), channel_id=1, source_target_pairs={{0,2},{1,3},{2,0},{3,1},{4,6},{5,7},{6,4},{7,5},{8,10},{9,11},{10,... | collective-permute-start | bytes 688136 | tf_op jit(solution)/shard_map/ppermute | solution.py:20
  89.6 8.8 %collective-permute-start.37 = (bf16[64,896]{1,0:T(8,128)(2,1)S(1)}, bf16[64,896]{1,0:T(8,128)(2,1)S(1)}, u32[]{:S(2)}, u32[]{:S(2)}) collective-permute-start(bf16[64,896]{1,0:T(8,128)(2,1)S(1)} %add_convert_fusion.7), channel_id=1, source_target_pairs={{0,8},{4,12},{8,0},{12,4},{16,24},{20,28},{24,16},{28,20},{1,9},{5... | collective-permute-start | bytes 344072 | tf_op jit(solution)/shard_map/ppermute | solution.py:20
  93.3 6.7 %collective-permute-start.33 = (bf16[64,896]{1,0:T(8,128)(2,1)S(1)}, bf16[64,896]{1,0:T(8,128)(2,1)S(1)}, u32[]{:S(2)}, u32[]{:S(2)}) collective-permute-start(bf16[64,896]{1,0:T(8,128)(2,1)S(1)} %get-tuple-element.40), channel_id=1, source_target_pairs={{0,24},{4,28},{8,16},{12,20},{16,8},{20,12},{24,0},{28,4},{1,25},{... | collective-permute-start | bytes 344072 | tf_op jit(solution)/shard_map/ppermute | solution.py:20
  95.7 6.7 %collective-permute-start.32 = (bf16[64,896]{1,0:T(8,128)(2,1)S(1)}, bf16[64,896]{1,0:T(8,128)(2,1)S(1)}, u32[]{:S(2)}, u32[]{:S(2)}) collective-permute-start(bf16[64,896]{1,0:T(8,128)(2,1)S(1)} %get-tuple-element.39), channel_id=1, source_target_pairs={{0,16},{4,20},{8,24},{12,28},{16,0},{20,4},{24,8},{28,12},{1,17},{... | collective-permute-start | bytes 344072 | tf_op jit(solution)/shard_map/ppermute | solution.py:20
  (12 other events, 80.3 us)

commit v5 on v4

--- a/solution.py
+++ b/solution.py
@@ -105,77 +105,73 @@
         scratch_shapes=[pltpu.SemaphoreType.DMA((4,))],
         compiler_params=pltpu.CompilerParams(vmem_limit_bytes=2 * MIB),
         name="pick",
-    )(ranks, swap_slot, expert_ids.T, gate_weights.T, in_hbm(hidden), in_hbm(pages))
-
-
-def attend_kernel(
-    each,
-    groups,
-    ranks_ref,
-    lengths_ref,
-    query_ref,
-    page_ref,
-    w_gate_ref,
-    w_up_ref,
-    w_down_ref,
-    out_ref,
-    gate_ref,
-    up_ref,
-    down_ref,
-    sems,
-):
+    )(
+        ranks,
+        in_hbm(swap_slot),
+        in_hbm(expert_ids.T),
+        in_hbm(gate_weights.T),
+        in_hbm(hidden),
+        in_hbm(pages),
+    )
+
+
+def attend_kernel(each, groups, ranks_ref, lengths_ref, query_ref, page_ref, out_ref):
     step, steps = pl.program_id(0), pl.num_programs(0)
-    copies = [
-        pltpu.make_async_copy(source, target, sems.at[i])
-        for i, (source, target) in enumerate(
-            ((w_gate_ref, gate_ref), (w_up_ref, up_ref), (w_down_ref, down_ref))
-        )
-    ]
-
-    @pl.when(step == 0)
-    def _():
-        for one in copies:
-            one.start()
-
     first = device_of(ranks_ref, groups) * each * steps + step * each
     for i in range(each):
         out_ref[i] = attend_body(query_ref[i], page_ref[i], lengths_ref[first + i])
 
-    @pl.when(step == steps - 1)
-    def _():
-        for one in copies:
-            one.wait()
-
-
-def attend_all(ranks, lengths, queries, pages, groups, *weights):
+
+def attend_all(ranks, lengths, queries, pages, groups):
     count, width, heads = queries.shape
     slots = pages.shape[2]
     each = math.gcd(count, 4)
-    moved = sum(2 * math.prod(w.shape) for w in weights)
     return pl.pallas_call(
         functools.partial(attend_kernel, each, groups),
-        out_shape=[jax.ShapeDtypeStruct((count, heads, LAT), jnp.bfloat16)]
-        + [pltpu.VMEM(w.shape, w.dtype) for w in weights],
+        out_shape=jax.ShapeDtypeStruct((count, heads, LAT), jnp.bfloat16),
         grid_spec=pltpu.PrefetchScalarGridSpec(
             num_scalar_prefetch=2,
             grid=(count // each,),
             in_specs=[
                 pl.BlockSpec((each, width, heads), lambda i, *_: (i, 0, 0)),
                 pl.BlockSpec((each, width, slots), lambda i, *_: (i, 0, 0)),
-            ]
-            + [ANYWHERE] * len(weights),
-            out_specs=[pl.BlockSpec((each, heads, LAT), lambda i, *_: (i, 0, 0))]
-            + [ANYWHERE] * len(weights),
-            scratch_shapes=[pltpu.SemaphoreType.DMA((len(weights),))],
+            ],
+            out_specs=pl.BlockSpec((each, heads, LAT), lambda i, *_: (i, 0, 0)),
         ),
         compiler_params=pltpu.CompilerParams(vmem_limit_bytes=12 * MIB),
         cost_estimate=pl.CostEstimate(
             flops=2 * count * heads * slots * (width + LAT),
-            bytes_accessed=2 * count * (heads * (width + LAT) + slots * width) + moved,
+            bytes_accessed=2 * count * (heads * (width + LAT) + slots * width),
             transcendentals=count * heads * slots,
         ),
         name="attend_local",
-    )(ranks, lengths, in_hbm(queries), in_hbm(pages), *[in_hbm(w) for w in weights])
+    )(ranks, lengths, in_hbm(queries), in_hbm(pages))
+
+
+def load_kernel(*refs):
+    count = len(refs) // 2
+    copies = [
+        pltpu.make_async_copy(refs[i], refs[count + i], refs[-1].at[i]) for i in range(count)
+    ]
+    for one in copies:
+        one.start()
+    for one in copies:
+        one.wait()
+
+
+def load(*arrays):
+    return pl.pallas_call(
+        load_kernel,
+        out_shape=[pltpu.VMEM(w.shape, w.dtype) for w in arrays],
+        in_specs=[ANYWHERE] * len(arrays),
+        out_specs=[ANYWHERE] * len(arrays),
+        scratch_shapes=[pltpu.SemaphoreType.DMA((len(arrays),))],
+        compiler_params=pltpu.CompilerParams(vmem_limit_bytes=MIB),
+        cost_estimate=pl.CostEstimate(
+            flops=0, bytes_accessed=sum(2 * math.prod(w.shape) for w in arrays), transcendentals=0
+        ),
+        name="load",
+    )(*[in_hbm(w) for w in arrays])
 
 
 def attend_traded_kernel(
@@ -219,24 +215,24 @@
 
 def experts_kernel(
     top,
+    fetch,
     ranks_ref,
-    hidden_ref,
     pieces,
     gate_ref,
     up_ref,
-    down_ref,
+    source_ref,
     cross_ref,
     side_ref,
     sent_ref,
     kept_ref,
-    rows_ref,
-    meta_ref,
-    inner_ref,
-    table_ref,
-    sems,
+    *refs,
 ):
+    if fetch:
+        down_ref, *refs = refs
+    else:
+        down_ref = source_ref
+    rows_ref, meta_ref, inner_ref, table_ref, sems, down_sem = refs
     experts, _, units = gate_ref.shape
-    block_rows = hidden_ref.shape[0]
     total_rows = rows_ref.shape[0]
     quarter = kept_ref.shape[1]
     ep_rank, tp_rank = ranks_ref[0], ranks_ref[1]
@@ -244,9 +240,12 @@
     def columns_of(part):
         return pl.ds(pl.multiple_of((tp_rank ^ part) * quarter, 128), quarter)
 
-    copies = [(hidden_ref, rows_ref.at[pl.ds(0, block_rows), :])]
+    copies = []
     for start, parts, has_meta, piece in pieces:
-        rows = pl.ds(start * block_rows, piece.shape[0])
+        rows = pl.ds(start, piece.shape[0])
+        if parts is None:
+            copies.append((piece, rows_ref.at[rows, :]))
+            continue
         for i, part in enumerate(parts):
             copies.append(
                 (piece.at[:, pl.ds(i * quarter, quarter)], rows_ref.at[rows, columns_of(part)])
@@ -259,6 +258,9 @@
     ]
     for one in copies:
         one.start()
+    if fetch:
+        down_copy = pltpu.make_async_copy(source_ref, down_ref, down_sem)
+        down_copy.start()
     for one in copies:
         one.wait()
     meta = meta_ref[...].astype(jnp.float32)
@@ -280,6 +282,8 @@
             act = gate / (1.0 + jnp.exp(-gate)) * up * table_ref[at, e : e + 1]
             inner_ref[at, e * units : (e + 1) * units] = act.astype(jnp.bfloat16)
 
+    if fetch:
+        down_copy.wait()
     for part, out_ref in ((3, cross_ref), (1, side_ref), (2, sent_ref), (0, kept_ref)):
 
         @pl.loop(0, total_rows // stride)
@@ -291,28 +295,35 @@
             ).astype(jnp.bfloat16)
 
 
-def run_experts(ranks, hidden, pieces, weights, rows, columns, top):
-    width = hidden.shape[1]
-    experts, _, units = weights[0].shape
+def run_experts(ranks, pieces, w_gate, w_up, w_down, rows, columns, top, fetch):
+    experts, width, units = w_gate.shape
     arrays = [piece for *_, piece in pieces]
-    count = 1 + sum(len(parts) + has_meta for _, parts, has_meta, _ in pieces)
-
-    def kernel(ranks_ref, hidden_ref, refs, *others):
+    count = sum(1 if parts is None else len(parts) + has_meta for _, parts, has_meta, _ in pieces)
+
+    def kernel(ranks_ref, refs, *others):
         named = [(*about[:3], ref) for about, ref in zip(pieces, refs)]
-        experts_kernel(top, ranks_ref, hidden_ref, named, *others)
+        experts_kernel(top, fetch, ranks_ref, named, *others)
 
     need = 2 * rows * (width + 128 + experts * units) + 512 * rows
+    down_shape = [pltpu.VMEM(w_down.shape, w_down.dtype)] if fetch else []
     return pl.pallas_call(
         kernel,
-        out_shape=[pltpu.VMEM((rows, columns), jnp.bfloat16)] * 4,
-        in_specs=[IN_SMEM, ANYWHERE, [ANYWHERE] * len(arrays), IN_VMEM, IN_VMEM, IN_VMEM],
-        out_specs=[IN_VMEM] * 4,
+        out_shape=[pltpu.VMEM((rows, columns), jnp.bfloat16)] * 4 + down_shape,
+        in_specs=[
+            IN_SMEM,
+            [ANYWHERE] * len(arrays),
+            IN_VMEM,
+            IN_VMEM,
+            ANYWHERE if fetch else IN_VMEM,
+        ],
+        out_specs=[IN_VMEM] * (4 + len(down_shape)),
         scratch_shapes=[
             pltpu.VMEM((rows, width), jnp.bfloat16),
             pltpu.VMEM((rows, 128), jnp.bfloat16),
             pltpu.VMEM((rows, experts * units), jnp.bfloat16),
             pltpu.VMEM((rows, 128), jnp.float32),
             pltpu.SemaphoreType.DMA((count,)),
+            pltpu.SemaphoreType.DMA,
         ],
         compiler_params=pltpu.CompilerParams(vmem_limit_bytes=need + 6 * MIB),
         cost_estimate=pl.CostEstimate(
@@ -321,7 +332,13 @@
             transcendentals=rows * units * experts,
         ),
         name="experts",
-    )(ranks, in_hbm(hidden), arrays, *[in_vmem(w) for w in weights])
+    )(
+        ranks,
+        arrays,
+        in_vmem(w_gate),
+        in_vmem(w_up),
+        in_hbm(w_down) if fetch else in_vmem(w_down),
+    )
 
 
 def total_of(*terms):
@@ -357,100 +374,107 @@
     pairs = ep_size // 2
     late = list(range(2, pairs))
     half = len(late) // 2
-    evens, odds = 4, 4 + len(late)
+    rest = len(late) - half
+    levels = ep_size.bit_length() - 1
+    tie = lax.optimization_barrier
 
     def cut(array, start, count):
         return lax.slice_in_dim(array, start * rows, (start + count) * rows, axis=0)
 
     def bare(array):
         return array[:, :columns]
-
-    own, both, page = pick(
-        ranks, swap_slot, expert_ids, gate_weights, hidden, cache_pages, groups
-    )
-    late_pieces = [flip(own, "ep", 2 * m) for m in late]
-    near_2 = flip(own, "ep", 2)
-    both_1 = flip(both, "ep", 1)
-    far_2 = flip(bare(near_2), "tp", 2)
-    near_3 = flip(near_2, "ep", 1)
-    far_3 = flip(bare(near_3), "tp", 2)
-
-    levels = ep_size.bit_length() - 1
 
     def page_hop(page, level):
         swapped = flip(page, "ep", 1 << level)
         bit = jnp.bitwise_and(jnp.right_shift(mask_value, level), 1) == 1
         return jnp.where(bit, swapped, page)
 
-    attended, *weights = attend_all(
-        ranks, lengths, queries, cache_pages, groups, w_gate, w_up, w_down
-    )
-    page = page_hop(page, 0)
+    own, both, page = pick(
+        ranks, swap_slot, expert_ids, gate_weights, hidden, cache_pages, groups
+    )
+    late_pieces = [flip(own, "ep", 2 * m) for m in late]
+    near_2 = flip(own, "ep", 2)
+    both_1 = flip(both, "ep", 1)
+
+    near_2, w_gate, w_up = tie((near_2, w_gate, w_up))
+    far_2 = flip(bare(near_2), "tp", 2)
+    near_3 = flip(near_2, "ep", 1)
+    w_gate, w_up = load(w_gate, w_up)
+    far_2, near_3, w_gate, w_up, page, both_1, *late_pieces = tie(
+        (far_2, near_3, w_gate, w_up, page, both_1, *late_pieces)
+    )
+    for level in range(levels - 1, 1, -1):
+        page = page_hop(page, level)
+    far_3 = flip(bare(near_3), "tp", 2)
+
     near_late = jnp.concatenate(late_pieces, axis=0)
-    near_late, attended, page = lax.optimization_barrier((near_late, attended, page))
-
+    far_2, queries = tie((far_2, queries))
     far_late = flip(bare(near_late), "tp", 2)
     near_odds = flip(near_late, "ep", 1)
+    attended = attend_all(ranks, lengths, queries, cache_pages, groups)
+    early = [flip(array, "tp", 1) for array in (both_1, near_2, far_2, near_3)]
+    far_late, near_odds, far_3, attended, page, early = tie(
+        (far_late, near_odds, far_3, attended, page, early)
+    )
+    page = page_hop(page, 0)
     far_odds_y = flip(bare(cut(near_odds, 0, half)), "tp", 2)
-    far_odds_x = flip(cut(far_late, half, len(late) - half), "ep", 1)
-    pieces = [
-        (0, (), True, own),
-        (1, (0, 2), True, both_1),
-        (1, (1, 3), False, flip(both_1, "tp", 1)),
-    ]
-    for start, part, array in (
-        (2, 0, near_2),
-        (2, 2, far_2),
-        (3, 0, near_3),
-        (3, 2, far_3),
-        (evens, 0, near_late),
-        (evens, 2, far_late),
-        (odds, 0, near_odds),
-        (odds, 2, far_odds_y),
-        (odds + half, 2, far_odds_x),
-    ):
-        pieces += [
-            (start, (part,), part == 0, array),
-            (start, (part ^ 1,), False, flip(array, "tp", 1)),
-        ]
-
-    for level in range(levels - 1, 1, -1):
-        page = page_hop(page, level)
-    ranks, page = lax.optimization_barrier((ranks, page))
+    far_odds_x = flip(cut(far_late, half, rest), "ep", 1)
+
+    def with_core(start, part, array, other):
+        start = start * rows
+        return [(start, (part,), part == 0, array), (start, (part ^ 1,), False, other)]
+
+    pieces = [(0, None, False, hidden), (0, (), True, own)]
+    pieces += [(rows, (0, 2), True, both_1), (rows, (1, 3), False, early[0])]
+    pieces += with_core(2, 0, near_2, early[1]) + with_core(2, 2, far_2, early[2])
+    pieces += with_core(3, 0, near_3, early[3])
+    pieces += with_core(3, 2, far_3, flip(far_3, "tp", 1))
+    *first, w_down = run_experts(
+        ranks, pieces, w_gate, w_up, w_down, 4 * rows, columns, top, True
+    )
+    early = [flip(array, "tp", 1) for array in (near_late, far_late, near_odds)]
+    first, far_odds_y, far_odds_x, early = tie((first, far_odds_y, far_odds_x, early))
+
+    def add_core(cross, side, sent, kept):
+        return total_of(sent, flip(cross, "tp", 1)), total_of(kept, flip(side, "tp", 1))
+
+    sent, kept = add_core(*first)
+    last = [flip(array, "tp", 1) for array in (far_odds_y, far_odds_x)]
+    sent, kept, last, page = tie((sent, kept, last, page))
+    over_23 = flip(cut(sent, 2, 2), "tp", 2)
+    over_1 = flip(jnp.concatenate([cut(kept, 1, 1), cut(sent, 1, 1)], axis=1), "ep", 1)
     if levels > 1:
         page = page_hop(page, 1)
+    pieces = with_core(0, 0, near_late, early[0]) + with_core(0, 2, far_late, early[1])
+    pieces += with_core(len(late), 0, near_odds, early[2])
+    pieces += with_core(len(late), 2, far_odds_y, last[0])
+    pieces += with_core(len(late) + half, 2, far_odds_x, last[1])
+    second = [
+        *run_experts(
+            ranks, pieces, w_gate, w_up, w_down, 2 * len(late) * rows, columns, top, False
+        )
+    ]
+    second, over_23, over_1 = tie((second, over_23, over_1))
+    late_sent, late_kept = add_core(*second)
+
+    over_y = flip(cut(late_sent, len(late), half), "tp", 2)
+    over_x = flip(cut(late_sent, len(late) + half, rest), "ep", 1)
+    over_3 = flip(total_of(cut(kept, 3, 1), cut(over_23, 1, 1)), "ep", 1)
+    zero = flip(total_of(cut(sent, 0, 1), over_1[:, columns:]), "tp", 2)
     attended = attend_traded(
         ranks, lengths, swap_slot, swap_mask, queries, page, attended, groups
     )
-
-    cross, side, sent, kept = run_experts(
-        ranks, hidden, pieces, weights, ep_size * rows, columns, top
-    )
-    cross = flip(cross, "tp", 1)
-    side = flip(side, "tp", 1)
-
-    def sent_of(start, count):
-        return total_of(cut(sent, start, count), cut(cross, start, count))
-
-    def kept_of(start, count):
-        return total_of(cut(kept, start, count), cut(side, start, count))
-
-    rest = len(late) - half
-    over_y = flip(sent_of(odds, half), "tp", 2)
-    over_x = flip(sent_of(odds + half, rest), "ep", 1)
-    over_3 = flip(sent_of(3, 1), "tp", 2)
-    over_2 = flip(sent_of(2, 1), "tp", 2)
-    over_1 = flip(jnp.concatenate([kept_of(1, 1), sent_of(1, 1)], axis=1), "ep", 1)
-    odd = total_of(kept_of(odds, len(late)), jnp.pad(over_y, ((0, rest * rows), (0, 0))))
+    over_y, over_x, over_3, zero, attended = tie((over_y, over_x, over_3, zero, attended))
+    odd = total_of(
+        cut(late_kept, len(late), len(late)), jnp.pad(over_y, ((0, rest * rows), (0, 0)))
+    )
     odd = flip(odd, "ep", 1)
-    even = total_of(sent_of(evens, len(late)), jnp.pad(over_x, ((half * rows, 0), (0, 0))))
+    even = total_of(cut(late_sent, 0, len(late)), jnp.pad(over_x, ((half * rows, 0), (0, 0))))
     even = flip(even, "tp", 2)
-    near_3 = flip(total_of(kept_of(3, 1), over_3), "ep", 1)
-    zero = flip(total_of(sent_of(0, 1), over_1[:, columns:]), "tp", 2)
-    even = total_of(kept_of(evens, len(late)), even, odd)
-    back = [flip(cut(even, i, 1), "ep", 2 * m) for i, m in enumerate(late)]
-    back.append(flip(total_of(kept_of(2, 1), over_2, near_3), "ep", 2))
-    moe_out = total_of(kept_of(0, 1), over_1[:, :columns], zero, *back)
+    back = [flip(total_of(cut(kept, 2, 1), cut(over_23, 0, 1), over_3), "ep", 2)]
+    even = total_of(cut(late_kept, 0, len(late)), even, odd)
+    back += [flip(cut(even, i, 1), "ep", 2 * m) for i, m in enumerate(late)]
+    moe_out = total_of(cut(kept, 0, 1), over_1[:, :columns], zero, *back)
     return attended, moe_out
 
 

time: 104 us -> 96.7 us (0.930)
  waiting for transfers between devices: 35 us -> 26.8 us
  local copies, waits for them, and re-layouts: 2.8 us -> 0.18 us
  starting transfers between devices: 34.7 us -> 36.9 us
  Pallas kernels: 27.5 us -> 29.2 us
    ppermute x38 -> x39, waiting for transfers between devices: 35 us -> 26.8 us  [flip(): return lax.ppermute(block, axis, [(i, i ^ apart) for i in range(count)])]
    pallas_call x0 -> x1, Pallas kernels: none -> 4.22 us  [load(): pl.pallas_call(load_kernel, out_shape=[pltpu.VMEM(w.shape, w.dtype) for w...]
    pallas_call x1, Pallas kernels: 12.1 us -> 8.29 us  [attend_all(): pl.pallas_call(functools.partial(attend_kernel, each, groups), out_shape=...]
    unnamed x12 -> x7, local copies, waits for them, and re-layouts: 2.72 us -> 0.03 us
    ppermute x38 -> x39, starting transfers between devices: 34.7 us -> 36.9 us  [flip(): return lax.ppermute(block, axis, [(i, i ^ apart) for i in range(count)])]
    pallas_call x1 -> x2, Pallas kernels: 11 us -> 12.1 us  [run_experts(): pl.pallas_call(kernel, out_shape=[pltpu.VMEM((rows, columns), jnp.bfloat1...]
  transfers between devices with their start and end apart: 38 -> 39, of which waited for: 17 -> 11; matrix products, arithmetic and copies ran while one was open for 1% -> 1% of each run, Pallas kernels for 14% -> 28%
where the time goes in v5:
time: 96.7 us; the launch traced here: 96.4 us
  starting transfers between devices  36.9 us (38%)
  Pallas kernels  29.2 us (30%)
  waiting for transfers between devices  26.8 us (28%)
  other arithmetic  1.69 us (2%)
  between operations  1.67 us (2%)
    ppermute x39, starting transfers between devices, flip(): return lax.ppermute(block, axis, [(i, i ^ apart) for i in range(count)])  36.9 us
    ppermute x39, waiting for transfers between devices, flip(): return lax.ppermute(block, axis, [(i, i ^ apart) for i in range(count)])  26.8 us
    pallas_call x2, Pallas kernels, run_experts(): pl.pallas_call(kernel, out_shape=[pltpu.VMEM((rows, columns), jnp.bfloat1...  12.1 us
    pallas_call x1, Pallas kernels, attend_all(): pl.pallas_call(functools.partial(attend_kernel, each, groups), out_shape=...  8.29 us
    pallas_call x1, Pallas kernels, load(): pl.pallas_call(load_kernel, out_shape=[pltpu.VMEM(w.shape, w.dtype) for w...  4.22 us
    pallas_call x1, Pallas kernels, attend_traded(): pl.pallas_call(functools.partial(attend_traded_kernel, groups), out_shape...  2.71 us
  transfers between devices with their start and end apart: 39, of which 11 were waited for; matrix products, arithmetic and copies ran while one was open for 1% of the time, Pallas kernels for 28%

profile of v5, /device:TPU:0, one launch (start us, length us, event | category | flops | bytes accessed | tf_op | source)
XLA Modules:
  0.0 96.4 jit_solution(9074884947921081379)
XLA Ops:
  0.7 1.9 %pick.1 = (bf16[64,1024]{1,0:T(8,128)(2,1)S(1)}, bf16[64,1920]{1,0:T(8,128)(2,1)S(1)}, bf16[576,256]{1,0:T(8,128)(2,1)S(1)}) custom-call(s32[2]{0:T(128)S(1)} %pad_add_fusion.ranks_ref, s32[32]{0:T(128)} %slots_ref.3, s32[8,64]{1,0:T(8,128)} %bitcast.13, f32[8,64]{1,0:T(8,128)} %bitcast.14, bf16[64,3584]{1,0:T(8,128)(2,1)} %refs_0_.2, ...), custom_call_target="tpu_custom_call" | custom-call | tf_op jit(solution)/shard_map/pick/pallas_call | solution.py:96
  2.6 3.1 %collective-permute-start = (bf16[64,1024]{1,0:T(8,128)(2,1)S(1)}, bf16[64,1024]{1,0:T(8,128)(2,1)S(1)}, u32[]{:S(2)}, u32[]{:S(2)}) collective-permute-start(bf16[64,1024]{1,0:T(8,128)(2,1)S(1)} %get-tuple-element.63.refs_1_), channel_id=1, source_target_pairs={{0,8},{4,12},{8,0},{12,4},{16,24},{20,28},{24,16},{28,20},{1,9},{5... | collective-permute-start | bytes 393224 | tf_op jit(solution)/shard_map/ppermute | solution.py:20
  5.7 1.5 %collective-permute-start.3 = (bf16[64,1920]{1,0:T(8,128)(2,1)S(1)}, bf16[64,1920]{1,0:T(8,128)(2,1)S(1)}, u32[]{:S(2)}, u32[]{:S(2)}) collective-permute-start(bf16[64,1920]{1,0:T(8,128)(2,1)S(1)} %get-tuple-element.70), channel_id=1, source_target_pairs={{0,4},{4,0},{8,12},{12,8},{16,20},{20,16},{24,28},{28,24},{1,5},{5... | collective-permute-start | bytes 737288 | tf_op jit(solution)/shard_map/ppermute | solution.py:20
  7.2 2.6 %collective-permute-start.4 = (bf16[64,1024]{1,0:T(8,128)(2,1)S(1)}, bf16[64,1024]{1,0:T(8,128)(2,1)S(1)}, u32[]{:S(2)}, u32[]{:S(2)}) collective-permute-start(bf16[64,1024]{1,0:T(8,128)(2,1)S(1)} %get-tuple-element.63.refs_1_), channel_id=1, source_target_pairs={{0,16},{4,20},{8,24},{12,28},{16,0},{20,4},{24,8},{28,12},{1,17},{... | collective-permute-start | bytes 393224 | tf_op jit(solution)/shard_map/ppermute | solution.py:20
  10.0 2.3 %collective-permute-start.2 = (bf16[64,1024]{1,0:T(8,128)(2,1)S(1)}, bf16[64,1024]{1,0:T(8,128)(2,1)S(1)}, u32[]{:S(2)}, u32[]{:S(2)}) collective-permute-start(bf16[64,1024]{1,0:T(8,128)(2,1)S(1)} %collective-permute-done.refs_4_), channel_id=1, source_target_pairs={{0,4},{4,0},{8,12},{12,8},{16,20},{20,16},{24,28},{28,24},{1,5},{5... | collective-permute-start | bytes 393224 | tf_op jit(solution)/shard_map/ppermute | solution.py:20
  12.3 1.6 %collective-permute-start.1 = (bf16[64,896]{1,0:T(8,128)(2,1)S(1)}, bf16[64,896]{1,0:T(8,128)(2,1)S(1)}, u32[]{:S(2)}, u32[]{:S(2)}) collective-permute-start(bf16[64,896]{1,0:T(8,128)(2,1)S(1)} %slice.71), channel_id=1, source_target_pairs={{0,2},{1,3},{2,0},{3,1},{4,6},{5,7},{6,4},{7,5},{8,10},{9,11},{10,... | collective-permute-start | bytes 344072 | tf_op jit(solution)/shard_map/ppermute | solution.py:20
  14.5 4.2 %load.1 = (bf16[3,3584,256]{2,1,0:T(8,128)(2,1)S(1)}, bf16[3,3584,256]{2,1,0:T(8,128)(2,1)S(1)}) custom-call(bf16[3,3584,256]{2,1,0:T(8,128)(2,1)} %refs_0_.1, bf16[3,3584,256]{2,1,0:T(8,128)(2,1)} %refs_1_), custom_call_target="tpu_custom_call" | custom-call | bytes 11010048 | tf_op jit(solution)/shard_map/load/pallas_call | solution.py:163
  19.6 1.5 %collective-permute-start.8 = (bf16[64,896]{1,0:T(8,128)(2,1)S(1)}, bf16[64,896]{1,0:T(8,128)(2,1)S(1)}, u32[]{:S(2)}, u32[]{:S(2)}) collective-permute-start(bf16[64,896]{1,0:T(8,128)(2,1)S(1)} %slice.73), channel_id=1, source_target_pairs={{0,2},{1,3},{2,0},{3,1},{4,6},{5,7},{6,4},{7,5},{8,10},{9,11},{10,... | collective-permute-start | bytes 344072 | tf_op jit(solution)/shard_map/ppermute | solution.py:20
  21.1 3.4 %collective-permute-start.9 = (bf16[576,256]{1,0:T(8,128)(2,1)S(1)}, bf16[576,256]{1,0:T(8,128)(2,1)S(1)}, u32[]{:S(2)}, u32[]{:S(2)}) collective-permute-start(bf16[576,256]{1,0:T(8,128)(2,1)S(1)} %get-tuple-element.77), channel_id=1, source_target_pairs={{0,16},{4,20},{8,24},{12,28},{16,0},{20,4},{24,8},{28,12},{1,17},{... | collective-permute-start | bytes 884744 | tf_op jit(solution)/shard_map/ppermute | solution.py:20
  25.1 8.3 %attend_local.1.old_ref = bf16[16,128,512]{2,1,0:T(8,128)(2,1)} custom-call(s32[2]{0:T(128)S(1)} %pad_add_fusion.ranks_ref, s32[512]{0:T(512)S(1)} %copy-done.1, bf16[16,576,128]{2,1,0:T(8,128)(2,1)} %bitcast.11, bf16[16,576,256]{2,1,0:T(8,128)(2,1)} %bitcast.10), custom_call_target="tpu_custom_call" | custom-call | flops 1140850688 | bytes 9175040 | tf_op jit(solution)/shard_map/attend_local/pallas_call | solution.py:129
  34.6 2.9 %collective-permute-done.9 = bf16[576,256]{1,0:T(8,128)(2,1)S(1)} collective-permute-done((bf16[576,256]{1,0:T(8,128)(2,1)S(1)}, bf16[576,256]{1,0:T(8,128)(2,1)S(1)}, u32[]{:S(2)}, u32[]{:S(2)}) %collective-permute-start.9) | collective-permute-done | bytes 294944 | tf_op jit(solution)/shard_map/ppermute | solution.py:20
  37.5 4.3 %collective-permute-done.6.refs_2_ = bf16[128,896]{1,0:T(8,128)(2,1)S(1)} collective-permute-done((bf16[128,896]{1,0:T(8,128)(2,1)S(1)}, bf16[128,896]{1,0:T(8,128)(2,1)S(1)}, u32[]{:S(2)}, u32[]{:S(2)}) %collective-permute-start.6) | collective-permute-done | bytes 229408 | tf_op jit(solution)/shard_map/ppermute | solution.py:20
  43.1 1.5 %collective-permute-start.16 = (bf16[64,896]{1,0:T(8,128)(2,1)S(1)}, bf16[64,896]{1,0:T(8,128)(2,1)S(1)}, u32[]{:S(2)}, u32[]{:S(2)}) collective-permute-start(bf16[64,896]{1,0:T(8,128)(2,1)S(1)} %slice.75), channel_id=1, source_target_pairs={{0,4},{4,0},{8,12},{12,8},{16,20},{20,16},{24,28},{28,24},{1,5},{5... | collective-permute-start | bytes 344072 | tf_op jit(solution)/shard_map/ppermute | solution.py:20
  45.1 6.3 %experts.2 = (bf16[256,896]{1,0:T(8,128)(2,1)S(1)}, bf16[256,896]{1,0:T(8,128)(2,1)S(1)}, bf16[256,896]{1,0:T(8,128)(2,1)S(1)}, bf16[256,896]{1,0:T(8,128)(2,1)S(1)}, bf16[3,256,3584]{2,1,0:T(8,128)(2,1)S(1)}) custom-call(s32[2]{0:T(128)S(1)} %pad_add_fusion.ranks_ref, bf16[64,3584]{1,0:T(8,128)(2,1)S(1)} %copy-done, ...), custom_call_target="tpu_custom_call" | custom-call | flops 4227858432 | bytes 3670016 | tf_op jit(solution)/shard_map/experts/pallas_call | solution.py:309
  52.5 2.1 %collective-permute-done.24 = bf16[576,256]{1,0:T(8,128)(2,1)S(1)} collective-permute-done((bf16[576,256]{1,0:T(8,128)(2,1)S(1)}, bf16[576,256]{1,0:T(8,128)(2,1)S(1)}, u32[]{:S(2)}, u32[]{:S(2)}) %collective-permute-start.24) | collective-permute-done | bytes 294944 | tf_op jit(solution)/shard_map/ppermute | solution.py:20
  55.0 1.5 %collective-permute-start.25 = (bf16[128,896]{1,0:T(8,128)(2,1)S(1)}, bf16[128,896]{1,0:T(8,128)(2,1)S(1)}, u32[]{:S(2)}, u32[]{:S(2)}) collective-permute-start(bf16[128,896]{1,0:T(8,128)(2,1)S(1)} %slice.76), channel_id=1, source_target_pairs={{0,2},{1,3},{2,0},{3,1},{4,6},{5,7},{6,4},{7,5},{8,10},{9,11},{10,... | collective-permute-start | bytes 688136 | tf_op jit(solution)/shard_map/ppermute | solution.py:20
  56.5 1.6 %collective-permute-start.26 = (bf16[64,1792]{1,0:T(8,128)(2,1)S(1)}, bf16[64,1792]{1,0:T(8,128)(2,1)S(1)}, u32[]{:S(2)}, u32[]{:S(2)}) collective-permute-start(bf16[64,1792]{1,0:T(8,128)(2,1)S(1)} %pad_maximum_fusion), channel_id=1, source_target_pairs={{0,4},{4,0},{8,12},{12,8},{16,20},{20,16},{24,28},{28,24},{1,5},{5... | collective-permute-start | bytes 688136 | tf_op jit(solution)/shard_map/ppermute | solution.py:20
  58.1 5.9 %experts.3 = (bf16[256,896]{1,0:T(8,128)(2,1)S(1)}, bf16[256,896]{1,0:T(8,128)(2,1)S(1)}, bf16[256,896]{1,0:T(8,128)(2,1)S(1)}, bf16[256,896]{1,0:T(8,128)(2,1)S(1)}) custom-call(s32[2]{0:T(128)S(1)} %pad_add_fusion.ranks_ref, bf16[128,1024]{1,0:T(8,128)(2,1)S(1)} %constant_dynamic-update-slice_fusion.refs_0_, ...), custom_call_target="tpu_custom_call" | custom-call | flops 4227858432 | bytes 3670016 | tf_op jit(solution)/shard_map/experts/pallas_call | solution.py:309
  64.1 0.8 collective-permute-start.30
  66.0 2.7 %attend_traded.1 = bf16[16,128,512]{2,1,0:T(8,128)(2,1)} custom-call(s32[2]{0:T(128)S(1)} %pad_add_fusion.ranks_ref, s32[512]{0:T(512)S(1)} %copy-done.1, s32[32]{0:T(128)S(1)} %copy-done.2, s32[1]{0:T(128)S(6)} %copy.16.mask_ref, bf16[16,576,128]{2,1,0:T(8,128)(2,1)} %bitcast.12, ...), custom_call_target="tpu_custom_call", output_to_operand_aliasing={{}: (6, {})} | custom-call | flops 71303168 | bytes 573440 | tf_op jit(solution)/shard_map/attend_traded/pallas_call | solution.py:192
  68.8 1.2 %collective-permute-start.28 = (bf16[64,896]{1,0:T(8,128)(2,1)S(1)}, bf16[64,896]{1,0:T(8,128)(2,1)S(1)}, u32[]{:S(2)}, u32[]{:S(2)}) collective-permute-start(bf16[64,896]{1,0:T(8,128)(2,1)S(1)} %get-tuple-element.125), channel_id=1, source_target_pairs={{0,2},{1,3},{2,0},{3,1},{4,6},{5,7},{6,4},{7,5},{8,10},{9,11},{10,... | collective-permute-start | bytes 344072 | tf_op jit(solution)/shard_map/ppermute | solution.py:20
  70.0 1.3 %collective-permute-start.29 = (bf16[64,896]{1,0:T(8,128)(2,1)S(1)}, bf16[64,896]{1,0:T(8,128)(2,1)S(1)}, u32[]{:S(2)}, u32[]{:S(2)}) collective-permute-start(bf16[64,896]{1,0:T(8,128)(2,1)S(1)} %get-tuple-element.124), channel_id=1, source_target_pairs={{0,4},{4,0},{8,12},{12,8},{16,20},{20,16},{24,28},{28,24},{1,5},{5... | collective-permute-start | bytes 344072 | tf_op jit(solution)/shard_map/ppermute | solution.py:20
  71.5 2.6 %collective-permute-done.28 = bf16[64,896]{1,0:T(8,128)(2,1)S(1)} collective-permute-done((bf16[64,896]{1,0:T(8,128)(2,1)S(1)}, bf16[64,896]{1,0:T(8,128)(2,1)S(1)}, u32[]{:S(2)}, u32[]{:S(2)}) %collective-permute-start.28) | collective-permute-done | bytes 114720 | tf_op jit(solution)/shard_map/ppermute | solution.py:20
  74.1 1.2 %collective-permute-done.29 = bf16[64,896]{1,0:T(8,128)(2,1)S(1)} collective-permute-done((bf16[64,896]{1,0:T(8,128)(2,1)S(1)}, bf16[64,896]{1,0:T(8,128)(2,1)S(1)}, u32[]{:S(2)}, u32[]{:S(2)}) %collective-permute-start.29) | collective-permute-done | bytes 114720 | tf_op jit(solution)/shard_map/ppermute | solution.py:20
  75.3 1.4 %collective-permute-start.36 = (bf16[128,896]{1,0:T(8,128)(2,1)S(1)}, bf16[128,896]{1,0:T(8,128)(2,1)S(1)}, u32[]{:S(2)}, u32[]{:S(2)}) collective-permute-start(bf16[128,896]{1,0:T(8,128)(2,1)S(1)} %add_convert_fusion.5), channel_id=1, source_target_pairs={{0,4},{4,0},{8,12},{12,8},{16,20},{20,16},{24,28},{28,24},{1,5},{5... | collective-permute-start | bytes 688136 | tf_op jit(solution)/shard_map/ppermute | solution.py:20
  77.5 2.0 %collective-permute-start.33 = (bf16[64,896]{1,0:T(8,128)(2,1)S(1)}, bf16[64,896]{1,0:T(8,128)(2,1)S(1)}, u32[]{:S(2)}, u32[]{:S(2)}) collective-permute-start(bf16[64,896]{1,0:T(8,128)(2,1)S(1)} %add_convert_fusion.8), channel_id=1, source_target_pairs={{0,8},{4,12},{8,0},{12,4},{16,24},{20,28},{24,16},{28,20},{1,9},{5... | collective-permute-start | bytes 344072 | tf_op jit(solution)/shard_map/ppermute | solution.py:20
  79.5 2.8 %collective-permute-done.36 = bf16[128,896]{1,0:T(8,128)(2,1)S(1)} collective-permute-done((bf16[128,896]{1,0:T(8,128)(2,1)S(1)}, bf16[128,896]{1,0:T(8,128)(2,1)S(1)}, u32[]{:S(2)}, u32[]{:S(2)}) %collective-permute-start.36) | collective-permute-done | bytes 229408 | tf_op jit(solution)/shard_map/ppermute | solution.py:20
  82.3 1.1 %collective-permute-done.35 = bf16[128,896]{1,0:T(8,128)(2,1)S(1)} collective-permute-done((bf16[128,896]{1,0:T(8,128)(2,1)S(1)}, bf16[128,896]{1,0:T(8,128)(2,1)S(1)}, u32[]{:S(2)}, u32[]{:S(2)}) %collective-permute-start.35) | collective-permute-done | bytes 229408 | tf_op jit(solution)/shard_map/ppermute | solution.py:20
  83.5 1.5 %collective-permute-start.38 = (bf16[64,896]{1,0:T(8,128)(2,1)S(1)}, bf16[64,896]{1,0:T(8,128)(2,1)S(1)}, u32[]{:S(2)}, u32[]{:S(2)}) collective-permute-start(bf16[64,896]{1,0:T(8,128)(2,1)S(1)} %get-tuple-element.127), channel_id=1, source_target_pairs={{0,24},{4,28},{8,16},{12,20},{16,8},{20,12},{24,0},{28,4},{1,25},{... | collective-permute-start | bytes 344072 | tf_op jit(solution)/shard_map/ppermute | solution.py:20
  85.1 2.0 %collective-permute-start.37 = (bf16[64,896]{1,0:T(8,128)(2,1)S(1)}, bf16[64,896]{1,0:T(8,128)(2,1)S(1)}, u32[]{:S(2)}, u32[]{:S(2)}) collective-permute-start(bf16[64,896]{1,0:T(8,128)(2,1)S(1)} %get-tuple-element.126), channel_id=1, source_target_pairs={{0,16},{4,20},{8,24},{12,28},{16,0},{20,4},{24,8},{28,12},{1,17},{... | collective-permute-start | bytes 344072 | tf_op jit(solution)/shard_map/ppermute | solution.py:20
  87.1 3.2 %collective-permute-done.38 = bf16[64,896]{1,0:T(8,128)(2,1)S(1)} collective-permute-done((bf16[64,896]{1,0:T(8,128)(2,1)S(1)}, bf16[64,896]{1,0:T(8,128)(2,1)S(1)}, u32[]{:S(2)}, u32[]{:S(2)}) %collective-permute-start.38) | collective-permute-done | bytes 114720 | tf_op jit(solution)/shard_map/ppermute | solution.py:20
  90.3 5.4 %collective-permute-done.37 = bf16[64,896]{1,0:T(8,128)(2,1)S(1)} collective-permute-done((bf16[64,896]{1,0:T(8,128)(2,1)S(1)}, bf16[64,896]{1,0:T(8,128)(2,1)S(1)}, u32[]{:S(2)}, u32[]{:S(2)}) %collective-permute-start.37) | collective-permute-done | bytes 114720 | tf_op jit(solution)/shard_map/ppermute | solution.py:20
  (86 shorter events, 9.4 us)
Async XLA Ops:
  2.6 7.4 %collective-permute-start = (bf16[64,1024]{1,0:T(8,128)(2,1)S(1)}, bf16[64,1024]{1,0:T(8,128)(2,1)S(1)}, u32[]{:S(2)}, u32[]{:S(2)}) collective-permute-start(bf16[64,1024]{1,0:T(8,128)(2,1)S(1)} %get-tuple-element.63.refs_1_), channel_id=1, source_target_pairs={{0,8},{4,12},{8,0},{12,4},{16,24},{20,28},{24,16},{28,20},{1,9},{5... | collective-permute-start | bytes 393224 | tf_op jit(solution)/shard_map/ppermute | solution.py:20
  5.7 13.8 %collective-permute-start.3 = (bf16[64,1920]{1,0:T(8,128)(2,1)S(1)}, bf16[64,1920]{1,0:T(8,128)(2,1)S(1)}, u32[]{:S(2)}, u32[]{:S(2)}) collective-permute-start(bf16[64,1920]{1,0:T(8,128)(2,1)S(1)} %get-tuple-element.70), channel_id=1, source_target_pairs={{0,4},{4,0},{8,12},{12,8},{16,20},{20,16},{24,28},{28,24},{1,5},{5... | collective-permute-start | bytes 737288 | tf_op jit(solution)/shard_map/ppermute | solution.py:20
  7.2 12.3 %collective-permute-start.4 = (bf16[64,1024]{1,0:T(8,128)(2,1)S(1)}, bf16[64,1024]{1,0:T(8,128)(2,1)S(1)}, u32[]{:S(2)}, u32[]{:S(2)}) collective-permute-start(bf16[64,1024]{1,0:T(8,128)(2,1)S(1)} %get-tuple-element.63.refs_1_), channel_id=1, source_target_pairs={{0,16},{4,20},{8,24},{12,28},{16,0},{20,4},{24,8},{28,12},{1,17},{... | collective-permute-start | bytes 393224 | tf_op jit(solution)/shard_map/ppermute | solution.py:20
  9.8 9.7 %collective-permute-start.5 = (bf16[64,1024]{1,0:T(8,128)(2,1)S(1)}, bf16[64,1024]{1,0:T(8,128)(2,1)S(1)}, u32[]{:S(2)}, u32[]{:S(2)}) collective-permute-start(bf16[64,1024]{1,0:T(8,128)(2,1)S(1)} %get-tuple-element.63.refs_1_), channel_id=1, source_target_pairs={{0,24},{4,28},{8,16},{12,20},{16,8},{20,12},{24,0},{28,4},{1,25},{... | collective-permute-start | bytes 393224 | tf_op jit(solution)/shard_map/ppermute | solution.py:20
  10.0 9.5 %collective-permute-start.2 = (bf16[64,1024]{1,0:T(8,128)(2,1)S(1)}, bf16[64,1024]{1,0:T(8,128)(2,1)S(1)}, u32[]{:S(2)}, u32[]{:S(2)}) collective-permute-start(bf16[64,1024]{1,0:T(8,128)(2,1)S(1)} %collective-permute-done.refs_4_), channel_id=1, source_target_pairs={{0,4},{4,0},{8,12},{12,8},{16,20},{20,16},{24,28},{28,24},{1,5},{5... | collective-permute-start | bytes 393224 | tf_op jit(solution)/shard_map/ppermute | solution.py:20
  12.3 7.3 %collective-permute-start.1 = (bf16[64,896]{1,0:T(8,128)(2,1)S(1)}, bf16[64,896]{1,0:T(8,128)(2,1)S(1)}, u32[]{:S(2)}, u32[]{:S(2)}) collective-permute-start(bf16[64,896]{1,0:T(8,128)(2,1)S(1)} %slice.71), channel_id=1, source_target_pairs={{0,2},{1,3},{2,0},{3,1},{4,6},{5,7},{6,4},{7,5},{8,10},{9,11},{10,... | collective-permute-start | bytes 344072 | tf_op jit(solution)/shard_map/ppermute | solution.py:20
  19.5 13.9 %collective-permute-start.11 = (bf16[64,1024]{1,0:T(8,128)(2,1)S(1)}, bf16[64,1024]{1,0:T(8,128)(2,1)S(1)}, u32[]{:S(2)}, u32[]{:S(2)}) collective-permute-start(bf16[64,1024]{1,0:T(8,128)(2,1)S(1)} %collective-permute-done.refs_4_), channel_id=1, source_target_pairs={{0,1},{1,0},{2,3},{3,2},{4,5},{5,4},{6,7},{7,6},{8,9},{9,8},{10,11... | collective-permute-start | bytes 393224 | tf_op jit(solution)/shard_map/ppermute | solution.py:20
  19.6 14.1 %collective-permute-start.8 = (bf16[64,896]{1,0:T(8,128)(2,1)S(1)}, bf16[64,896]{1,0:T(8,128)(2,1)S(1)}, u32[]{:S(2)}, u32[]{:S(2)}) collective-permute-start(bf16[64,896]{1,0:T(8,128)(2,1)S(1)} %slice.73), channel_id=1, source_target_pairs={{0,2},{1,3},{2,0},{3,1},{4,6},{5,7},{6,4},{7,5},{8,10},{9,11},{10,... | collective-permute-start | bytes 344072 | tf_op jit(solution)/shard_map/ppermute | solution.py:20
  21.1 16.4 %collective-permute-start.9 = (bf16[576,256]{1,0:T(8,128)(2,1)S(1)}, bf16[576,256]{1,0:T(8,128)(2,1)S(1)}, u32[]{:S(2)}, u32[]{:S(2)}) collective-permute-start(bf16[576,256]{1,0:T(8,128)(2,1)S(1)} %get-tuple-element.77), channel_id=1, source_target_pairs={{0,16},{4,20},{8,24},{12,28},{16,0},{20,4},{24,8},{28,12},{1,17},{... | collective-permute-start | bytes 884744 | tf_op jit(solution)/shard_map/ppermute | solution.py:20
  24.4 9.6 %collective-permute-start.12 = (bf16[64,896]{1,0:T(8,128)(2,1)S(1)}, bf16[64,896]{1,0:T(8,128)(2,1)S(1)}, u32[]{:S(2)}, u32[]{:S(2)}) collective-permute-start(bf16[64,896]{1,0:T(8,128)(2,1)S(1)} %collective-permute-done.1.refs_6_), channel_id=1, source_target_pairs={{0,1},{1,0},{2,3},{3,2},{4,5},{5,4},{6,7},{7,6},{8,9},{9,8},{10,11... | collective-permute-start | bytes 344072 | tf_op jit(solution)/shard_map/ppermute | solution.py:20
  24.5 17.3 %collective-permute-start.7 = (bf16[128,1024]{1,0:T(8,128)(2,1)S(1)}, bf16[128,1024]{1,0:T(8,128)(2,1)S(1)}, u32[]{:S(2)}, u32[]{:S(2)}) collective-permute-start(bf16[128,1024]{1,0:T(8,128)(2,1)S(1)} %constant_dynamic-update-slice_fusion.refs_0_), channel_id=1, source_target_pairs={{0,4},{4,0},{8,12},{12,8},{16,20},{20,16},{24,28},{28,24},{1,5},{5... | collective-permute-start | bytes 786440 | tf_op jit(solution)/shard_map/ppermute | solution.py:20
  33.7 9.4 %collective-permute-start.17 = (bf16[128,1024]{1,0:T(8,128)(2,1)S(1)}, bf16[128,1024]{1,0:T(8,128)(2,1)S(1)}, u32[]{:S(2)}, u32[]{:S(2)}) collective-permute-start(bf16[128,1024]{1,0:T(8,128)(2,1)S(1)} %constant_dynamic-update-slice_fusion.refs_0_), channel_id=1, source_target_pairs={{0,1},{1,0},{2,3},{3,2},{4,5},{5,4},{6,7},{7,6},{8,9},{9,8},{10,11... | collective-permute-start | bytes 786440 | tf_op jit(solution)/shard_map/ppermute | solution.py:20
  34.0 7.7 %collective-permute-start.6 = (bf16[128,896]{1,0:T(8,128)(2,1)S(1)}, bf16[128,896]{1,0:T(8,128)(2,1)S(1)}, u32[]{:S(2)}, u32[]{:S(2)}) collective-permute-start(bf16[128,896]{1,0:T(8,128)(2,1)S(1)} %slice.94), channel_id=1, source_target_pairs={{0,2},{1,3},{2,0},{3,1},{4,6},{5,7},{6,4},{7,5},{8,10},{9,11},{10,... | collective-permute-start | bytes 688136 | tf_op jit(solution)/shard_map/ppermute | solution.py:20
  41.8 9.6 %collective-permute-start.18 = (bf16[128,896]{1,0:T(8,128)(2,1)S(1)}, bf16[128,896]{1,0:T(8,128)(2,1)S(1)}, u32[]{:S(2)}, u32[]{:S(2)}) collective-permute-start(bf16[128,896]{1,0:T(8,128)(2,1)S(1)} %collective-permute-done.6.refs_2_), channel_id=1, source_target_pairs={{0,1},{1,0},{2,3},{3,2},{4,5},{5,4},{6,7},{7,6},{8,9},{9,8},{10,11... | collective-permute-start | bytes 688136 | tf_op jit(solution)/shard_map/ppermute | solution.py:20
  42.3 9.1 %collective-permute-start.19 = (bf16[128,1024]{1,0:T(8,128)(2,1)S(1)}, bf16[128,1024]{1,0:T(8,128)(2,1)S(1)}, u32[]{:S(2)}, u32[]{:S(2)}) collective-permute-start(bf16[128,1024]{1,0:T(8,128)(2,1)S(1)} %collective-permute-done.7.refs_4_), channel_id=1, source_target_pairs={{0,1},{1,0},{2,3},{3,2},{4,5},{5,4},{6,7},{7,6},{8,9},{9,8},{10,11... | collective-permute-start | bytes 786440 | tf_op jit(solution)/shard_map/ppermute | solution.py:20
  42.4 8.9 %collective-permute-start.15 = (bf16[64,896]{1,0:T(8,128)(2,1)S(1)}, bf16[64,896]{1,0:T(8,128)(2,1)S(1)}, u32[]{:S(2)}, u32[]{:S(2)}) collective-permute-start(bf16[64,896]{1,0:T(8,128)(2,1)S(1)} %slice.74), channel_id=1, source_target_pairs={{0,2},{1,3},{2,0},{3,1},{4,6},{5,7},{6,4},{7,5},{8,10},{9,11},{10,... | collective-permute-start | bytes 344072 | tf_op jit(solution)/shard_map/ppermute | solution.py:20
  43.1 8.3 %collective-permute-start.16 = (bf16[64,896]{1,0:T(8,128)(2,1)S(1)}, bf16[64,896]{1,0:T(8,128)(2,1)S(1)}, u32[]{:S(2)}, u32[]{:S(2)}) collective-permute-start(bf16[64,896]{1,0:T(8,128)(2,1)S(1)} %slice.75), channel_id=1, source_target_pairs={{0,4},{4,0},{8,12},{12,8},{16,20},{20,16},{24,28},{28,24},{1,5},{5... | collective-permute-start | bytes 344072 | tf_op jit(solution)/shard_map/ppermute | solution.py:20
  44.5 10.1 %collective-permute-start.24 = (bf16[576,256]{1,0:T(8,128)(2,1)S(1)}, bf16[576,256]{1,0:T(8,128)(2,1)S(1)}, u32[]{:S(2)}, u32[]{:S(2)}) collective-permute-start(bf16[576,256]{1,0:T(8,128)(2,1)S(1)} %broadcast_select_fusion.2), channel_id=1, source_target_pairs={{0,4},{4,0},{8,12},{12,8},{16,20},{20,16},{24,28},{28,24},{1,5},{5... | collective-permute-start | bytes 884744 | tf_op jit(solution)/shard_map/ppermute | solution.py:20
  55.0 9.0 %collective-permute-start.25 = (bf16[128,896]{1,0:T(8,128)(2,1)S(1)}, bf16[128,896]{1,0:T(8,128)(2,1)S(1)}, u32[]{:S(2)}, u32[]{:S(2)}) collective-permute-start(bf16[128,896]{1,0:T(8,128)(2,1)S(1)} %slice.76), channel_id=1, source_target_pairs={{0,2},{1,3},{2,0},{3,1},{4,6},{5,7},{6,4},{7,5},{8,10},{9,11},{10,... | collective-permute-start | bytes 688136 | tf_op jit(solution)/shard_map/ppermute | solution.py:20
  56.5 7.4 %collective-permute-start.26 = (bf16[64,1792]{1,0:T(8,128)(2,1)S(1)}, bf16[64,1792]{1,0:T(8,128)(2,1)S(1)}, u32[]{:S(2)}, u32[]{:S(2)}) collective-permute-start(bf16[64,1792]{1,0:T(8,128)(2,1)S(1)} %pad_maximum_fusion), channel_id=1, source_target_pairs={{0,4},{4,0},{8,12},{12,8},{16,20},{20,16},{24,28},{28,24},{1,5},{5... | collective-permute-start | bytes 688136 | tf_op jit(solution)/shard_map/ppermute | solution.py:20
  58.1 7.8 %collective-permute-start.32 = (bf16[576,256]{1,0:T(8,128)(2,1)S(1)}, bf16[576,256]{1,0:T(8,128)(2,1)S(1)}, u32[]{:S(2)}, u32[]{:S(2)}) collective-permute-start(bf16[576,256]{1,0:T(8,128)(2,1)S(1)} %broadcast_select_fusion.1), channel_id=1, source_target_pairs={{0,8},{4,12},{8,0},{12,4},{16,24},{20,28},{24,16},{28,20},{1,9},{5... | collective-permute-start | bytes 884744 | tf_op jit(solution)/shard_map/ppermute | solution.py:20
  64.0 4.7 %collective-permute-start.27 = (bf16[256,896]{1,0:T(8,128)(2,1)S(1)}, bf16[256,896]{1,0:T(8,128)(2,1)S(1)}, u32[]{:S(2)}, u32[]{:S(2)}) collective-permute-start(bf16[256,896]{1,0:T(8,128)(2,1)S(1)} %get-tuple-element.112), channel_id=1, source_target_pairs={{0,1},{1,0},{2,3},{3,2},{4,5},{5,4},{6,7},{7,6},{8,9},{9,8},{10,11... | collective-permute-start | bytes 1376264 | tf_op jit(solution)/shard_map/ppermute | solution.py:20
  64.1 7.3 %collective-permute-start.30 = (bf16[64,896]{1,0:T(8,128)(2,1)S(1)}, bf16[64,896]{1,0:T(8,128)(2,1)S(1)}, u32[]{:S(2)}, u32[]{:S(2)}) collective-permute-start(bf16[64,896]{1,0:T(8,128)(2,1)S(1)} %add_convert_fusion.10), channel_id=1, source_target_pairs={{0,4},{4,0},{8,12},{12,8},{16,20},{20,16},{24,28},{28,24},{1,5},{5... | collective-permute-start | bytes 344072 | tf_op jit(solution)/shard_map/ppermute | solution.py:20
  64.9 6.5 %collective-permute-start.31 = (bf16[64,896]{1,0:T(8,128)(2,1)S(1)}, bf16[64,896]{1,0:T(8,128)(2,1)S(1)}, u32[]{:S(2)}, u32[]{:S(2)}) collective-permute-start(bf16[64,896]{1,0:T(8,128)(2,1)S(1)} %add_convert_fusion.9), channel_id=1, source_target_pairs={{0,2},{1,3},{2,0},{3,1},{4,6},{5,7},{6,4},{7,5},{8,10},{9,11},{10,... | collective-permute-start | bytes 344072 | tf_op jit(solution)/shard_map/ppermute | solution.py:20
  65.5 5.8 %collective-permute-start.34 = (bf16[256,896]{1,0:T(8,128)(2,1)S(1)}, bf16[256,896]{1,0:T(8,128)(2,1)S(1)}, u32[]{:S(2)}, u32[]{:S(2)}) collective-permute-start(bf16[256,896]{1,0:T(8,128)(2,1)S(1)} %get-tuple-element.121), channel_id=1, source_target_pairs={{0,1},{1,0},{2,3},{3,2},{4,5},{5,4},{6,7},{7,6},{8,9},{9,8},{10,11... | collective-permute-start | bytes 1376264 | tf_op jit(solution)/shard_map/ppermute | solution.py:20
  68.8 5.2 %collective-permute-start.28 = (bf16[64,896]{1,0:T(8,128)(2,1)S(1)}, bf16[64,896]{1,0:T(8,128)(2,1)S(1)}, u32[]{:S(2)}, u32[]{:S(2)}) collective-permute-start(bf16[64,896]{1,0:T(8,128)(2,1)S(1)} %get-tuple-element.125), channel_id=1, source_target_pairs={{0,2},{1,3},{2,0},{3,1},{4,6},{5,7},{6,4},{7,5},{8,10},{9,11},{10,... | collective-permute-start | bytes 344072 | tf_op jit(solution)/shard_map/ppermute | solution.py:20
  70.0 5.3 %collective-permute-start.29 = (bf16[64,896]{1,0:T(8,128)(2,1)S(1)}, bf16[64,896]{1,0:T(8,128)(2,1)S(1)}, u32[]{:S(2)}, u32[]{:S(2)}) collective-permute-start(bf16[64,896]{1,0:T(8,128)(2,1)S(1)} %get-tuple-element.124), channel_id=1, source_target_pairs={{0,4},{4,0},{8,12},{12,8},{16,20},{20,16},{24,28},{28,24},{1,5},{5... | collective-permute-start | bytes 344072 | tf_op jit(solution)/shard_map/ppermute | solution.py:20
  75.3 7.0 %collective-permute-start.36 = (bf16[128,896]{1,0:T(8,128)(2,1)S(1)}, bf16[128,896]{1,0:T(8,128)(2,1)S(1)}, u32[]{:S(2)}, u32[]{:S(2)}) collective-permute-start(bf16[128,896]{1,0:T(8,128)(2,1)S(1)} %add_convert_fusion.5), channel_id=1, source_target_pairs={{0,4},{4,0},{8,12},{12,8},{16,20},{20,16},{24,28},{28,24},{1,5},{5... | collective-permute-start | bytes 688136 | tf_op jit(solution)/shard_map/ppermute | solution.py:20
  76.7 6.7 %collective-permute-start.35 = (bf16[128,896]{1,0:T(8,128)(2,1)S(1)}, bf16[128,896]{1,0:T(8,128)(2,1)S(1)}, u32[]{:S(2)}, u32[]{:S(2)}) collective-permute-start(bf16[128,896]{1,0:T(8,128)(2,1)S(1)} %add_convert_fusion.6), channel_id=1, source_target_pairs={{0,2},{1,3},{2,0},{3,1},{4,6},{5,7},{6,4},{7,5},{8,10},{9,11},{10,... | collective-permute-start | bytes 688136 | tf_op jit(solution)/shard_map/ppermute | solution.py:20
  77.5 9.6 %collective-permute-start.33 = (bf16[64,896]{1,0:T(8,128)(2,1)S(1)}, bf16[64,896]{1,0:T(8,128)(2,1)S(1)}, u32[]{:S(2)}, u32[]{:S(2)}) collective-permute-start(bf16[64,896]{1,0:T(8,128)(2,1)S(1)} %add_convert_fusion.8), channel_id=1, source_target_pairs={{0,8},{4,12},{8,0},{12,4},{16,24},{20,28},{24,16},{28,20},{1,9},{5... | collective-permute-start | bytes 344072 | tf_op jit(solution)/shard_map/ppermute | solution.py:20
  83.5 6.7 %collective-permute-start.38 = (bf16[64,896]{1,0:T(8,128)(2,1)S(1)}, bf16[64,896]{1,0:T(8,128)(2,1)S(1)}, u32[]{:S(2)}, u32[]{:S(2)}) collective-permute-start(bf16[64,896]{1,0:T(8,128)(2,1)S(1)} %get-tuple-element.127), channel_id=1, source_target_pairs={{0,24},{4,28},{8,16},{12,20},{16,8},{20,12},{24,0},{28,4},{1,25},{... | collective-permute-start | bytes 344072 | tf_op jit(solution)/shard_map/ppermute | solution.py:20
  85.1 10.6 %collective-permute-start.37 = (bf16[64,896]{1,0:T(8,128)(2,1)S(1)}, bf16[64,896]{1,0:T(8,128)(2,1)S(1)}, u32[]{:S(2)}, u32[]{:S(2)}) collective-permute-start(bf16[64,896]{1,0:T(8,128)(2,1)S(1)} %get-tuple-element.126), channel_id=1, source_target_pairs={{0,16},{4,20},{8,24},{12,28},{16,0},{20,4},{24,8},{28,12},{1,17},{... | collective-permute-start | bytes 344072 | tf_op jit(solution)/shard_map/ppermute | solution.py:20
  (10 other events, 62.6 us)

commit v6 on v5

--- a/solution.py
+++ b/solution.py
@@ -115,37 +115,40 @@
     )
 
 
-def attend_kernel(each, groups, ranks_ref, lengths_ref, query_ref, page_ref, out_ref):
-    step, steps = pl.program_id(0), pl.num_programs(0)
-    first = device_of(ranks_ref, groups) * each * steps + step * each
-    for i in range(each):
-        out_ref[i] = attend_body(query_ref[i], page_ref[i], lengths_ref[first + i])
-
-
-def attend_all(ranks, lengths, queries, pages, groups):
+def attend_part(ranks, lengths, queries, pages, groups, first, some, before=None):
     count, width, heads = queries.shape
     slots = pages.shape[2]
-    each = math.gcd(count, 4)
+    each = math.gcd(some, 2)
+    skip = first // each
+
+    def kernel(ranks_ref, lengths_ref, query_ref, page_ref, *refs):
+        start = device_of(ranks_ref, groups) * count + first + pl.program_id(0) * each
+        for i in range(each):
+            refs[-1][i] = attend_body(query_ref[i], page_ref[i], lengths_ref[start + i])
+
+    earlier = [] if before is None else [before]
     return pl.pallas_call(
-        functools.partial(attend_kernel, each, groups),
+        kernel,
         out_shape=jax.ShapeDtypeStruct((count, heads, LAT), jnp.bfloat16),
         grid_spec=pltpu.PrefetchScalarGridSpec(
             num_scalar_prefetch=2,
-            grid=(count // each,),
+            grid=(some // each,),
             in_specs=[
-                pl.BlockSpec((each, width, heads), lambda i, *_: (i, 0, 0)),
-                pl.BlockSpec((each, width, slots), lambda i, *_: (i, 0, 0)),
-            ],
-            out_specs=pl.BlockSpec((each, heads, LAT), lambda i, *_: (i, 0, 0)),
-        ),
-        compiler_params=pltpu.CompilerParams(vmem_limit_bytes=12 * MIB),
+                pl.BlockSpec((each, width, heads), lambda i, *_: (skip + i, 0, 0)),
+                pl.BlockSpec((each, width, slots), lambda i, *_: (skip + i, 0, 0)),
+            ]
+            + [ANYWHERE] * len(earlier),
+            out_specs=pl.BlockSpec((each, heads, LAT), lambda i, *_: (skip + i, 0, 0)),
+        ),
+        input_output_aliases={4: 0} if earlier else {},
+        compiler_params=pltpu.CompilerParams(vmem_limit_bytes=8 * MIB),
         cost_estimate=pl.CostEstimate(
-            flops=2 * count * heads * slots * (width + LAT),
-            bytes_accessed=2 * count * (heads * (width + LAT) + slots * width),
-            transcendentals=count * heads * slots,
+            flops=2 * some * heads * slots * (width + LAT),
+            bytes_accessed=2 * some * (heads * (width + LAT) + slots * width),
+            transcendentals=some * heads * slots,
         ),
         name="attend_local",
-    )(ranks, lengths, in_hbm(queries), in_hbm(pages))
+    )(ranks, lengths, in_hbm(queries), in_hbm(pages), *earlier)
 
 
 def load_kernel(*refs):
@@ -221,9 +224,7 @@
     gate_ref,
     up_ref,
     source_ref,
-    cross_ref,
-    side_ref,
-    sent_ref,
+    given_ref,
     kept_ref,
     *refs,
 ):
@@ -284,13 +285,14 @@
 
     if fetch:
         down_copy.wait()
-    for part, out_ref in ((3, cross_ref), (1, side_ref), (2, sent_ref), (0, kept_ref)):
+    for part, out_ref, half in ((3, given_ref, 0), (1, given_ref, 1), (2, kept_ref, 0), (0, kept_ref, 1)):
 
         @pl.loop(0, total_rows // stride)
         def _(step):
             at = pl.ds(pl.multiple_of(step * stride, stride), stride)
+            to = pl.ds(pl.multiple_of(half * total_rows + step * stride, stride), stride)
             weight = down_ref[:, :, columns_of(part)].reshape(experts * units, quarter)
-            out_ref[at, :] = jnp.dot(
+            out_ref[to, :] = jnp.dot(
                 inner_ref[at, :], weight, preferred_element_type=jnp.float32
             ).astype(jnp.bfloat16)
 
@@ -308,7 +310,7 @@
     down_shape = [pltpu.VMEM(w_down.shape, w_down.dtype)] if fetch else []
     return pl.pallas_call(
         kernel,
-        out_shape=[pltpu.VMEM((rows, columns), jnp.bfloat16)] * 4 + down_shape,
+        out_shape=[pltpu.VMEM((2 * rows, columns), jnp.bfloat16)] * 2 + down_shape,
         in_specs=[
             IN_SMEM,
             [ANYWHERE] * len(arrays),
@@ -316,7 +318,7 @@
             IN_VMEM,
             ANYWHERE if fetch else IN_VMEM,
         ],
-        out_specs=[IN_VMEM] * (4 + len(down_shape)),
+        out_specs=[IN_VMEM] * (2 + len(down_shape)),
         scratch_shapes=[
             pltpu.VMEM((rows, width), jnp.bfloat16),
             pltpu.VMEM((rows, 128), jnp.bfloat16),
@@ -384,10 +386,17 @@
     def bare(array):
         return array[:, :columns]
 
-    def page_hop(page, level):
-        swapped = flip(page, "ep", 1 << level)
+    def page_take(page, swapped, level):
         bit = jnp.bitwise_and(jnp.right_shift(mask_value, level), 1) == 1
         return jnp.where(bit, swapped, page)
+
+    def page_hop(page, level):
+        return page_take(page, flip(page, "ep", 1 << level), level)
+
+    def page_far(page):
+        for level in range(levels - 1, 2, -1):
+            page = page_hop(page, level)
+        return flip(page, "ep", 4) if levels > 2 else page, page
 
     own, both, page = pick(
         ranks, swap_slot, expert_ids, gate_weights, hidden, cache_pages, groups
@@ -403,22 +412,14 @@
     far_2, near_3, w_gate, w_up, page, both_1, *late_pieces = tie(
         (far_2, near_3, w_gate, w_up, page, both_1, *late_pieces)
     )
-    for level in range(levels - 1, 1, -1):
-        page = page_hop(page, level)
+    upper, lower = jnp.split(page, 2, axis=0)
+    upper_far, upper = page_far(upper)
     far_3 = flip(bare(near_3), "tp", 2)
 
     near_late = jnp.concatenate(late_pieces, axis=0)
-    far_2, queries = tie((far_2, queries))
     far_late = flip(bare(near_late), "tp", 2)
     near_odds = flip(near_late, "ep", 1)
-    attended = attend_all(ranks, lengths, queries, cache_pages, groups)
     early = [flip(array, "tp", 1) for array in (both_1, near_2, far_2, near_3)]
-    far_late, near_odds, far_3, attended, page, early = tie(
-        (far_late, near_odds, far_3, attended, page, early)
-    )
-    page = page_hop(page, 0)
-    far_odds_y = flip(bare(cut(near_odds, 0, half)), "tp", 2)
-    far_odds_x = flip(cut(far_late, half, rest), "ep", 1)
 
     def with_core(start, part, array, other):
         start = start * rows
@@ -432,19 +433,24 @@
     *first, w_down = run_experts(
         ranks, pieces, w_gate, w_up, w_down, 4 * rows, columns, top, True
     )
+    first, far_late, near_odds, upper_far = tie((first, far_late, near_odds, upper_far))
+
+    def add_core(given, own):
+        total = total_of(own, flip(given, "tp", 1))
+        return jnp.split(total, 2, axis=0)
+
+    far_odds_y = flip(bare(cut(near_odds, 0, half)), "tp", 2)
+    far_odds_x = flip(cut(far_late, half, rest), "ep", 1)
+    sent, kept = add_core(*first)
+    far_odds_y, far_odds_x, sent, kept, lower, near_late, far_late, near_odds = tie(
+        (far_odds_y, far_odds_x, sent, kept, lower, near_late, far_late, near_odds)
+    )
     early = [flip(array, "tp", 1) for array in (near_late, far_late, near_odds)]
-    first, far_odds_y, far_odds_x, early = tie((first, far_odds_y, far_odds_x, early))
-
-    def add_core(cross, side, sent, kept):
-        return total_of(sent, flip(cross, "tp", 1)), total_of(kept, flip(side, "tp", 1))
-
-    sent, kept = add_core(*first)
     last = [flip(array, "tp", 1) for array in (far_odds_y, far_odds_x)]
-    sent, kept, last, page = tie((sent, kept, last, page))
     over_23 = flip(cut(sent, 2, 2), "tp", 2)
     over_1 = flip(jnp.concatenate([cut(kept, 1, 1), cut(sent, 1, 1)], axis=1), "ep", 1)
-    if levels > 1:
-        page = page_hop(page, 1)
+    lower_far, lower = page_far(lower)
+
     pieces = with_core(0, 0, near_late, early[0]) + with_core(0, 2, far_late, early[1])
     pieces += with_core(len(late), 0, near_odds, early[2])
     pieces += with_core(len(late), 2, far_odds_y, last[0])
@@ -454,26 +460,39 @@
             ranks, pieces, w_gate, w_up, w_down, 2 * len(late) * rows, columns, top, False
         )
     ]
-    second, over_23, over_1 = tie((second, over_23, over_1))
+    second, over_23, over_1, lower_far = tie((second, over_23, over_1, lower_far))
+    page = jnp.concatenate([upper, lower], axis=0)
+    page = page_take(page, jnp.concatenate([upper_far, lower_far], axis=0), 2)
     late_sent, late_kept = add_core(*second)
+    over_3 = flip(total_of(cut(kept, 3, 1), cut(over_23, 1, 1)), "ep", 1)
+    zero = flip(total_of(cut(sent, 0, 1), over_1[:, columns:]), "tp", 2)
+    late_sent, late_kept, queries, page = tie((late_sent, late_kept, queries, page))
 
     over_y = flip(cut(late_sent, len(late), half), "tp", 2)
     over_x = flip(cut(late_sent, len(late) + half, rest), "ep", 1)
-    over_3 = flip(total_of(cut(kept, 3, 1), cut(over_23, 1, 1)), "ep", 1)
-    zero = flip(total_of(cut(sent, 0, 1), over_1[:, columns:]), "tp", 2)
-    attended = attend_traded(
-        ranks, lengths, swap_slot, swap_mask, queries, page, attended, groups
-    )
-    over_y, over_x, over_3, zero, attended = tie((over_y, over_x, over_3, zero, attended))
+    if levels > 1:
+        page = page_hop(page, 1)
+    some = queries.shape[0] // 2
+    attended = attend_part(ranks, lengths, queries, cache_pages, groups, 0, some)
+    over_y, over_x, attended = tie((over_y, over_x, attended))
     odd = total_of(
         cut(late_kept, len(late), len(late)), jnp.pad(over_y, ((0, rest * rows), (0, 0)))
     )
     odd = flip(odd, "ep", 1)
     even = total_of(cut(late_sent, 0, len(late)), jnp.pad(over_x, ((half * rows, 0), (0, 0))))
     even = flip(even, "tp", 2)
-    back = [flip(total_of(cut(kept, 2, 1), cut(over_23, 0, 1), over_3), "ep", 2)]
+    attended = attend_part(
+        ranks, lengths, queries, cache_pages, groups, some, queries.shape[0] - some, attended
+    )
+    odd, even, over_3, attended, page = tie((odd, even, over_3, attended, page))
     even = total_of(cut(late_kept, 0, len(late)), even, odd)
-    back += [flip(cut(even, i, 1), "ep", 2 * m) for i, m in enumerate(late)]
+    back = [flip(cut(even, i, 1), "ep", 2 * m) for i, m in enumerate(late)]
+    back.append(flip(total_of(cut(kept, 2, 1), cut(over_23, 0, 1), over_3), "ep", 2))
+    page = page_hop(page, 0)
+    attended = attend_traded(
+        ranks, lengths, swap_slot, swap_mask, queries, page, attended, groups
+    )
+    *back, attended = tie((*back, attended))
     moe_out = total_of(cut(kept, 0, 1), over_1[:, :columns], zero, *back)
     return attended, moe_out
 

time: 96.7 us -> 90.8 us (0.939)
  waiting for transfers between devices: 26.8 us -> 18.8 us
  Pallas kernels: 29.2 us -> 31.9 us
    ppermute x39 -> x38, waiting for transfers between devices: 26.8 us -> 18.8 us  [flip(): return lax.ppermute(block, axis, [(i, i ^ apart) for i in range(count)])]
    pallas_call x3 -> x4, Pallas kernels: 20.4 us -> 23.1 us  [the longest x2 11.9 us: run_experts(): pl.pallas_call(kernel, out_shape=[pltpu.VMEM((2 * rows, columns), jnp.bfl...]
    ppermute x39 -> x38, starting transfers between devices: 36.9 us -> 36.1 us  [flip(): return lax.ppermute(block, axis, [(i, i ^ apart) for i in range(count)])]
  transfers between devices with their start and end apart: 39 -> 38, of which waited for: 11 -> 13; matrix products, arithmetic and copies ran while one was open for 1% -> 1% of each run, Pallas kernels for 28% -> 33%
where the time goes in v6:
time: 90.8 us; the launch traced here: 90.5 us
  starting transfers between devices  36.1 us (40%)
  Pallas kernels  31.9 us (35%)
  waiting for transfers between devices  18.8 us (21%)
  other arithmetic  1.69 us (2%)
  between operations  1.6 us (2%)
    ppermute x38, starting transfers between devices, flip(): return lax.ppermute(block, axis, [(i, i ^ apart) for i in range(count)])  36.1 us
    ppermute x38, waiting for transfers between devices, flip(): return lax.ppermute(block, axis, [(i, i ^ apart) for i in range(count)])  18.8 us
    pallas_call x2, Pallas kernels, run_experts(): pl.pallas_call(kernel, out_shape=[pltpu.VMEM((2 * rows, columns), jnp.bfl...  11.9 us
    pallas_call x2, Pallas kernels, attend_part(): pl.pallas_call(kernel, out_shape=jax.ShapeDtypeStruct((count, heads, LAT)...  11.1 us
    pallas_call x1, Pallas kernels, load(): pl.pallas_call(load_kernel, out_shape=[pltpu.VMEM(w.shape, w.dtype) for w...  4.21 us
    pallas_call x1, Pallas kernels, attend_traded(): pl.pallas_call(functools.partial(attend_traded_kernel, groups), out_shape...  2.71 us
    pallas_call x1, Pallas kernels, pick(): pl.pallas_call(functools.partial(pick_kernel, groups), out_shape=(pltpu.V...  1.89 us
  transfers between devices with their start and end apart: 38, of which 13 were waited for; matrix products, arithmetic and copies ran while one was open for 1% of the time, Pallas kernels for 33%

profile of v6, /device:TPU:0, one launch (start us, length us, event | category | flops | bytes accessed | tf_op | source)
XLA Modules:
  0.0 90.5 jit_solution(8444273655213864807)
XLA Ops:
  0.7 1.9 %pick.1 = (bf16[64,1024]{1,0:T(8,128)(2,1)S(1)}, bf16[64,1920]{1,0:T(8,128)(2,1)S(1)}, bf16[576,256]{1,0:T(8,128)(2,1)S(1)}) custom-call(s32[2]{0:T(128)S(1)} %pad_add_fusion.ranks_ref, s32[32]{0:T(128)} %slots_ref.3, s32[8,64]{1,0:T(8,128)} %bitcast.15, f32[8,64]{1,0:T(8,128)} %bitcast.16, bf16[64,3584]{1,0:T(8,128)(2,1)} %refs_0_.2, ...), custom_call_target="tpu_custom_call" | custom-call | tf_op jit(solution)/shard_map/pick/pallas_call | solution.py:96
  2.6 3.1 %collective-permute-start = (bf16[64,1024]{1,0:T(8,128)(2,1)S(1)}, bf16[64,1024]{1,0:T(8,128)(2,1)S(1)}, u32[]{:S(2)}, u32[]{:S(2)}) collective-permute-start(bf16[64,1024]{1,0:T(8,128)(2,1)S(1)} %get-tuple-element.57.refs_1_), channel_id=1, source_target_pairs={{0,8},{4,12},{8,0},{12,4},{16,24},{20,28},{24,16},{28,20},{1,9},{5... | collective-permute-start | bytes 393224 | tf_op jit(solution)/shard_map/ppermute | solution.py:20
  5.7 1.5 %collective-permute-start.3 = (bf16[64,1920]{1,0:T(8,128)(2,1)S(1)}, bf16[64,1920]{1,0:T(8,128)(2,1)S(1)}, u32[]{:S(2)}, u32[]{:S(2)}) collective-permute-start(bf16[64,1920]{1,0:T(8,128)(2,1)S(1)} %get-tuple-element.64), channel_id=1, source_target_pairs={{0,4},{4,0},{8,12},{12,8},{16,20},{20,16},{24,28},{28,24},{1,5},{5... | collective-permute-start | bytes 737288 | tf_op jit(solution)/shard_map/ppermute | solution.py:20
  7.2 2.6 %collective-permute-start.4 = (bf16[64,1024]{1,0:T(8,128)(2,1)S(1)}, bf16[64,1024]{1,0:T(8,128)(2,1)S(1)}, u32[]{:S(2)}, u32[]{:S(2)}) collective-permute-start(bf16[64,1024]{1,0:T(8,128)(2,1)S(1)} %get-tuple-element.57.refs_1_), channel_id=1, source_target_pairs={{0,16},{4,20},{8,24},{12,28},{16,0},{20,4},{24,8},{28,12},{1,17},{... | collective-permute-start | bytes 393224 | tf_op jit(solution)/shard_map/ppermute | solution.py:20
  10.0 2.3 %collective-permute-start.2 = (bf16[64,1024]{1,0:T(8,128)(2,1)S(1)}, bf16[64,1024]{1,0:T(8,128)(2,1)S(1)}, u32[]{:S(2)}, u32[]{:S(2)}) collective-permute-start(bf16[64,1024]{1,0:T(8,128)(2,1)S(1)} %collective-permute-done.refs_4_), channel_id=1, source_target_pairs={{0,4},{4,0},{8,12},{12,8},{16,20},{20,16},{24,28},{28,24},{1,5},{5... | collective-permute-start | bytes 393224 | tf_op jit(solution)/shard_map/ppermute | solution.py:20
  12.3 1.5 %collective-permute-start.1 = (bf16[64,896]{1,0:T(8,128)(2,1)S(1)}, bf16[64,896]{1,0:T(8,128)(2,1)S(1)}, u32[]{:S(2)}, u32[]{:S(2)}) collective-permute-start(bf16[64,896]{1,0:T(8,128)(2,1)S(1)} %slice.71), channel_id=1, source_target_pairs={{0,2},{1,3},{2,0},{3,1},{4,6},{5,7},{6,4},{7,5},{8,10},{9,11},{10,... | collective-permute-start | bytes 344072 | tf_op jit(solution)/shard_map/ppermute | solution.py:20
  13.9 4.2 %load.1 = (bf16[3,3584,256]{2,1,0:T(8,128)(2,1)S(1)}, bf16[3,3584,256]{2,1,0:T(8,128)(2,1)S(1)}) custom-call(bf16[3,3584,256]{2,1,0:T(8,128)(2,1)} %refs_0_.1, bf16[3,3584,256]{2,1,0:T(8,128)(2,1)} %refs_1_), custom_call_target="tpu_custom_call" | custom-call | bytes 11010048 | tf_op jit(solution)/shard_map/load/pallas_call | solution.py:166
  18.1 1.4 %collective-permute-done.4 = bf16[64,1024]{1,0:T(8,128)(2,1)S(1)} collective-permute-done((bf16[64,1024]{1,0:T(8,128)(2,1)S(1)}, bf16[64,1024]{1,0:T(8,128)(2,1)S(1)}, u32[]{:S(2)}, u32[]{:S(2)}) %collective-permute-start.4) | collective-permute-done | bytes 131104 | tf_op jit(solution)/shard_map/ppermute | solution.py:20
  20.7 1.5 %collective-permute-start.10 = (bf16[64,896]{1,0:T(8,128)(2,1)S(1)}, bf16[64,896]{1,0:T(8,128)(2,1)S(1)}, u32[]{:S(2)}, u32[]{:S(2)}) collective-permute-start(bf16[64,896]{1,0:T(8,128)(2,1)S(1)} %slice.72), channel_id=1, source_target_pairs={{0,2},{1,3},{2,0},{3,1},{4,6},{5,7},{6,4},{7,5},{8,10},{9,11},{10,... | collective-permute-start | bytes 344072 | tf_op jit(solution)/shard_map/ppermute | solution.py:20
  22.2 3.6 %collective-permute-done.10.refs_10_ = bf16[64,896]{1,0:T(8,128)(2,1)S(1)} collective-permute-done((bf16[64,896]{1,0:T(8,128)(2,1)S(1)}, bf16[64,896]{1,0:T(8,128)(2,1)S(1)}, u32[]{:S(2)}, u32[]{:S(2)}) %collective-permute-start.10) | collective-permute-done | bytes 114720 | tf_op jit(solution)/shard_map/ppermute | solution.py:20
  25.8 1.0 %collective-permute-start.13 = (bf16[128,1024]{1,0:T(8,128)(2,1)S(1)}, bf16[128,1024]{1,0:T(8,128)(2,1)S(1)}, u32[]{:S(2)}, u32[]{:S(2)}) collective-permute-start(bf16[128,1024]{1,0:T(8,128)(2,1)S(1)} %constant_dynamic-update-slice_fusion.refs_0_), channel_id=1, source_target_pairs={{0,4},{4,0},{8,12},{12,8},{16,20},{20,16},{24,28},{28,24},{1,5},{5... | collective-permute-start | bytes 786440 | tf_op jit(solution)/shard_map/ppermute | solution.py:20
  26.9 1.4 %collective-permute-start.12 = (bf16[128,896]{1,0:T(8,128)(2,1)S(1)}, bf16[128,896]{1,0:T(8,128)(2,1)S(1)}, u32[]{:S(2)}, u32[]{:S(2)}) collective-permute-start(bf16[128,896]{1,0:T(8,128)(2,1)S(1)} %slice.94), channel_id=1, source_target_pairs={{0,2},{1,3},{2,0},{3,1},{4,6},{5,7},{6,4},{7,5},{8,10},{9,11},{10,... | collective-permute-start | bytes 688136 | tf_op jit(solution)/shard_map/ppermute | solution.py:20
  28.3 2.9 %collective-permute-start.14 = (bf16[288,256]{1,0:T(8,128)(2,1)S(1)}, bf16[288,256]{1,0:T(8,128)(2,1)S(1)}, u32[]{:S(2)}, u32[]{:S(2)}) collective-permute-start(bf16[288,256]{1,0:T(8,128)(2,1)S(1)} %get-tuple-element.119), channel_id=1, source_target_pairs={{0,16},{4,20},{8,24},{12,28},{16,0},{20,4},{24,8},{28,12},{1,17},{... | collective-permute-start | bytes 442376 | tf_op jit(solution)/shard_map/ppermute | solution.py:20
  31.3 6.2 %experts.2 = (bf16[512,896]{1,0:T(8,128)(2,1)S(1)}, bf16[512,896]{1,0:T(8,128)(2,1)S(1)}, bf16[3,256,3584]{2,1,0:T(8,128)(2,1)S(1)}) custom-call(s32[2]{0:T(128)S(1)} %pad_add_fusion.ranks_ref, bf16[64,3584]{1,0:T(8,128)(2,1)S(1)} %copy-done, bf16[64,1024]{1,0:T(8,128)(2,1)S(1)} %get-tuple-element.57.refs_1_, ...), custom_call_target="tpu_custom_call" | custom-call | flops 4227858432 | bytes 3670016 | tf_op jit(solution)/shard_map/experts/pallas_call | solution.py:311
  37.5 0.9 collective-permute-done.14
  39.0 1.5 %collective-permute-start.16 = (bf16[64,896]{1,0:T(8,128)(2,1)S(1)}, bf16[64,896]{1,0:T(8,128)(2,1)S(1)}, u32[]{:S(2)}, u32[]{:S(2)}) collective-permute-start(bf16[64,896]{1,0:T(8,128)(2,1)S(1)} %slice.75), channel_id=1, source_target_pairs={{0,4},{4,0},{8,12},{12,8},{16,20},{20,16},{24,28},{28,24},{1,5},{5... | collective-permute-start | bytes 344072 | tf_op jit(solution)/shard_map/ppermute | solution.py:20
  41.2 2.8 %collective-permute-done.15.refs_6_ = bf16[64,896]{1,0:T(8,128)(2,1)S(1)} collective-permute-done((bf16[64,896]{1,0:T(8,128)(2,1)S(1)}, bf16[64,896]{1,0:T(8,128)(2,1)S(1)}, u32[]{:S(2)}, u32[]{:S(2)}) %collective-permute-start.15) | collective-permute-done | bytes 114720 | tf_op jit(solution)/shard_map/ppermute | solution.py:20
  45.5 1.3 %collective-permute-done.21.refs_7_ = bf16[64,896]{1,0:T(8,128)(2,1)S(1)} collective-permute-done((bf16[64,896]{1,0:T(8,128)(2,1)S(1)}, bf16[64,896]{1,0:T(8,128)(2,1)S(1)}, u32[]{:S(2)}, u32[]{:S(2)}) %collective-permute-start.21) | collective-permute-done | bytes 114720 | tf_op jit(solution)/shard_map/ppermute | solution.py:20
  46.7 1.5 %collective-permute-start.23 = (bf16[128,896]{1,0:T(8,128)(2,1)S(1)}, bf16[128,896]{1,0:T(8,128)(2,1)S(1)}, u32[]{:S(2)}, u32[]{:S(2)}) collective-permute-start(bf16[128,896]{1,0:T(8,128)(2,1)S(1)} %slice.76), channel_id=1, source_target_pairs={{0,2},{1,3},{2,0},{3,1},{4,6},{5,7},{6,4},{7,5},{8,10},{9,11},{10,... | collective-permute-start | bytes 688136 | tf_op jit(solution)/shard_map/ppermute | solution.py:20
  48.2 1.5 %collective-permute-start.24 = (bf16[64,1792]{1,0:T(8,128)(2,1)S(1)}, bf16[64,1792]{1,0:T(8,128)(2,1)S(1)}, u32[]{:S(2)}, u32[]{:S(2)}) collective-permute-start(bf16[64,1792]{1,0:T(8,128)(2,1)S(1)} %pad_maximum_fusion), channel_id=1, source_target_pairs={{0,4},{4,0},{8,12},{12,8},{16,20},{20,16},{24,28},{28,24},{1,5},{5... | collective-permute-start | bytes 688136 | tf_op jit(solution)/shard_map/ppermute | solution.py:20
  49.7 5.7 %experts.3 = (bf16[512,896]{1,0:T(8,128)(2,1)S(1)}, bf16[512,896]{1,0:T(8,128)(2,1)S(1)}) custom-call(s32[2]{0:T(128)S(1)} %pad_add_fusion.ranks_ref, bf16[128,1024]{1,0:T(8,128)(2,1)S(1)} %constant_dynamic-update-slice_fusion.refs_0_, bf16[128,1024]{1,0:T(8,128)(2,1)S(1)} %collective-permute-done.18.refs_1_, ...), custom_call_target="tpu_custom_call" | custom-call | flops 4227858432 | bytes 3670016 | tf_op jit(solution)/shard_map/experts/pallas_call | solution.py:311
  55.4 3.0 %collective-permute-done.25 = bf16[288,256]{1,0:T(8,128)(2,1)S(1)} collective-permute-done((bf16[288,256]{1,0:T(8,128)(2,1)S(1)}, bf16[288,256]{1,0:T(8,128)(2,1)S(1)}, u32[]{:S(2)}, u32[]{:S(2)}) %collective-permute-start.25) | collective-permute-done | bytes 147488 | tf_op jit(solution)/shard_map/ppermute | solution.py:20
  59.1 0.8 collective-permute-start.31
  62.7 1.5 %collective-permute-start.37 = (bf16[64,896]{1,0:T(8,128)(2,1)S(1)}, bf16[64,896]{1,0:T(8,128)(2,1)S(1)}, u32[]{:S(2)}, u32[]{:S(2)}) collective-permute-start(bf16[64,896]{1,0:T(8,128)(2,1)S(1)} %add_convert_fusion.6), channel_id=1, source_target_pairs={{0,2},{1,3},{2,0},{3,1},{4,6},{5,7},{6,4},{7,5},{8,10},{9,11},{10,... | collective-permute-start | bytes 344072 | tf_op jit(solution)/shard_map/ppermute | solution.py:20
  64.2 5.6 %attend_local.2.refs_0_ = bf16[16,128,512]{2,1,0:T(8,128)(2,1)} custom-call(s32[2]{0:T(128)S(1)} %pad_add_fusion.ranks_ref, s32[512]{0:T(512)S(1)} %copy-done.1, bf16[16,576,128]{2,1,0:T(8,128)(2,1)} %bitcast.12, bf16[16,576,256]{2,1,0:T(8,128)(2,1)} %bitcast.10), custom_call_target="tpu_custom_call" | custom-call | flops 570425344 | bytes 4587520 | tf_op jit(solution)/shard_map/attend_local/pallas_call | solution.py:130
  69.8 1.3 %collective-permute-start.29 = (bf16[128,896]{1,0:T(8,128)(2,1)S(1)}, bf16[128,896]{1,0:T(8,128)(2,1)S(1)}, u32[]{:S(2)}, u32[]{:S(2)}) collective-permute-start(bf16[128,896]{1,0:T(8,128)(2,1)S(1)} %add_convert_fusion.4), channel_id=1, source_target_pairs={{0,4},{4,0},{8,12},{12,8},{16,20},{20,16},{24,28},{28,24},{1,5},{5... | collective-permute-start | bytes 688136 | tf_op jit(solution)/shard_map/ppermute | solution.py:20
  71.8 5.6 %attend_local.3.old_ref = bf16[16,128,512]{2,1,0:T(8,128)(2,1)} custom-call(s32[2]{0:T(128)S(1)} %pad_add_fusion.ranks_ref, s32[512]{0:T(512)S(1)} %copy-done.1, bf16[16,576,128]{2,1,0:T(8,128)(2,1)} %bitcast.13, bf16[16,576,256]{2,1,0:T(8,128)(2,1)} %bitcast.11, bf16[16,128,512]{2,1,0:T(8,128)(2,1)} %attend_local.2.refs_0_), custom_call_target="tpu_custom_call", output_to_operand_aliasing={{}: (4, {})} | custom-call | flops 570425344 | bytes 4587520 | tf_op jit(solution)/shard_map/attend_local/pallas_call | solution.py:130
  78.7 2.2 %collective-permute-start.33 = (bf16[64,896]{1,0:T(8,128)(2,1)S(1)}, bf16[64,896]{1,0:T(8,128)(2,1)S(1)}, u32[]{:S(2)}, u32[]{:S(2)}) collective-permute-start(bf16[64,896]{1,0:T(8,128)(2,1)S(1)} %get-tuple-element.121), channel_id=1, source_target_pairs={{0,16},{4,20},{8,24},{12,28},{16,0},{20,4},{24,8},{28,12},{1,17},{... | collective-permute-start | bytes 344072 | tf_op jit(solution)/shard_map/ppermute | solution.py:20
  80.9 2.0 %collective-permute-start.34 = (bf16[64,896]{1,0:T(8,128)(2,1)S(1)}, bf16[64,896]{1,0:T(8,128)(2,1)S(1)}, u32[]{:S(2)}, u32[]{:S(2)}) collective-permute-start(bf16[64,896]{1,0:T(8,128)(2,1)S(1)} %get-tuple-element.120), channel_id=1, source_target_pairs={{0,24},{4,28},{8,16},{12,20},{16,8},{20,12},{24,0},{28,4},{1,25},{... | collective-permute-start | bytes 344072 | tf_op jit(solution)/shard_map/ppermute | solution.py:20
  83.0 2.1 %collective-permute-done.36 = bf16[576,256]{1,0:T(8,128)(2,1)S(1)} collective-permute-done((bf16[576,256]{1,0:T(8,128)(2,1)S(1)}, bf16[576,256]{1,0:T(8,128)(2,1)S(1)}, u32[]{:S(2)}, u32[]{:S(2)}) %collective-permute-start.36) | collective-permute-done | bytes 294944 | tf_op jit(solution)/shard_map/ppermute | solution.py:20
  85.2 2.7 %attend_traded.1 = bf16[16,128,512]{2,1,0:T(8,128)(2,1)} custom-call(s32[2]{0:T(128)S(1)} %pad_add_fusion.ranks_ref, s32[512]{0:T(512)S(1)} %copy-done.1, s32[32]{0:T(128)S(1)} %copy-done.2, s32[1]{0:T(128)S(6)} %copy.18.mask_ref, bf16[16,576,128]{2,1,0:T(8,128)(2,1)} %bitcast.14, ...), custom_call_target="tpu_custom_call", output_to_operand_aliasing={{}: (6, {})} | custom-call | flops 71303168 | bytes 573440 | tf_op jit(solution)/shard_map/attend_traded/pallas_call | solution.py:195
  87.9 1.2 %collective-permute-done.33 = bf16[64,896]{1,0:T(8,128)(2,1)S(1)} collective-permute-done((bf16[64,896]{1,0:T(8,128)(2,1)S(1)}, bf16[64,896]{1,0:T(8,128)(2,1)S(1)}, u32[]{:S(2)}, u32[]{:S(2)}) %collective-permute-start.33) | collective-permute-done | bytes 114720 | tf_op jit(solution)/shard_map/ppermute | solution.py:20
  (86 shorter events, 10.4 us)
Async XLA Ops:
  2.6 7.4 %collective-permute-start = (bf16[64,1024]{1,0:T(8,128)(2,1)S(1)}, bf16[64,1024]{1,0:T(8,128)(2,1)S(1)}, u32[]{:S(2)}, u32[]{:S(2)}) collective-permute-start(bf16[64,1024]{1,0:T(8,128)(2,1)S(1)} %get-tuple-element.57.refs_1_), channel_id=1, source_target_pairs={{0,8},{4,12},{8,0},{12,4},{16,24},{20,28},{24,16},{28,20},{1,9},{5... | collective-permute-start | bytes 393224 | tf_op jit(solution)/shard_map/ppermute | solution.py:20
  5.7 13.8 %collective-permute-start.3 = (bf16[64,1920]{1,0:T(8,128)(2,1)S(1)}, bf16[64,1920]{1,0:T(8,128)(2,1)S(1)}, u32[]{:S(2)}, u32[]{:S(2)}) collective-permute-start(bf16[64,1920]{1,0:T(8,128)(2,1)S(1)} %get-tuple-element.64), channel_id=1, source_target_pairs={{0,4},{4,0},{8,12},{12,8},{16,20},{20,16},{24,28},{28,24},{1,5},{5... | collective-permute-start | bytes 737288 | tf_op jit(solution)/shard_map/ppermute | solution.py:20
  7.2 12.3 %collective-permute-start.4 = (bf16[64,1024]{1,0:T(8,128)(2,1)S(1)}, bf16[64,1024]{1,0:T(8,128)(2,1)S(1)}, u32[]{:S(2)}, u32[]{:S(2)}) collective-permute-start(bf16[64,1024]{1,0:T(8,128)(2,1)S(1)} %get-tuple-element.57.refs_1_), channel_id=1, source_target_pairs={{0,16},{4,20},{8,24},{12,28},{16,0},{20,4},{24,8},{28,12},{1,17},{... | collective-permute-start | bytes 393224 | tf_op jit(solution)/shard_map/ppermute | solution.py:20
  9.8 9.7 %collective-permute-start.5 = (bf16[64,1024]{1,0:T(8,128)(2,1)S(1)}, bf16[64,1024]{1,0:T(8,128)(2,1)S(1)}, u32[]{:S(2)}, u32[]{:S(2)}) collective-permute-start(bf16[64,1024]{1,0:T(8,128)(2,1)S(1)} %get-tuple-element.57.refs_1_), channel_id=1, source_target_pairs={{0,24},{4,28},{8,16},{12,20},{16,8},{20,12},{24,0},{28,4},{1,25},{... | collective-permute-start | bytes 393224 | tf_op jit(solution)/shard_map/ppermute | solution.py:20
  10.0 9.5 %collective-permute-start.2 = (bf16[64,1024]{1,0:T(8,128)(2,1)S(1)}, bf16[64,1024]{1,0:T(8,128)(2,1)S(1)}, u32[]{:S(2)}, u32[]{:S(2)}) collective-permute-start(bf16[64,1024]{1,0:T(8,128)(2,1)S(1)} %collective-permute-done.refs_4_), channel_id=1, source_target_pairs={{0,4},{4,0},{8,12},{12,8},{16,20},{20,16},{24,28},{28,24},{1,5},{5... | collective-permute-start | bytes 393224 | tf_op jit(solution)/shard_map/ppermute | solution.py:20
  12.3 7.2 %collective-permute-start.1 = (bf16[64,896]{1,0:T(8,128)(2,1)S(1)}, bf16[64,896]{1,0:T(8,128)(2,1)S(1)}, u32[]{:S(2)}, u32[]{:S(2)}) collective-permute-start(bf16[64,896]{1,0:T(8,128)(2,1)S(1)} %slice.71), channel_id=1, source_target_pairs={{0,2},{1,3},{2,0},{3,1},{4,6},{5,7},{6,4},{7,5},{8,10},{9,11},{10,... | collective-permute-start | bytes 344072 | tf_op jit(solution)/shard_map/ppermute | solution.py:20
  19.5 6.4 %collective-permute-start.7 = (bf16[64,1024]{1,0:T(8,128)(2,1)S(1)}, bf16[64,1024]{1,0:T(8,128)(2,1)S(1)}, u32[]{:S(2)}, u32[]{:S(2)}) collective-permute-start(bf16[64,1024]{1,0:T(8,128)(2,1)S(1)} %collective-permute-done.refs_4_), channel_id=1, source_target_pairs={{0,1},{1,0},{2,3},{3,2},{4,5},{5,4},{6,7},{7,6},{8,9},{9,8},{10,11... | collective-permute-start | bytes 393224 | tf_op jit(solution)/shard_map/ppermute | solution.py:20
  19.5 8.8 %collective-permute-start.9 = (bf16[64,1024]{1,0:T(8,128)(2,1)S(1)}, bf16[64,1024]{1,0:T(8,128)(2,1)S(1)}, u32[]{:S(2)}, u32[]{:S(2)}) collective-permute-start(bf16[64,1024]{1,0:T(8,128)(2,1)S(1)} %collective-permute-done.2.refs_8_), channel_id=1, source_target_pairs={{0,1},{1,0},{2,3},{3,2},{4,5},{5,4},{6,7},{7,6},{8,9},{9,8},{10,11... | collective-permute-start | bytes 393224 | tf_op jit(solution)/shard_map/ppermute | solution.py:20
  20.1 11.2 %collective-permute-start.6 = (bf16[64,1920]{1,0:T(8,128)(2,1)S(1)}, bf16[64,1920]{1,0:T(8,128)(2,1)S(1)}, u32[]{:S(2)}, u32[]{:S(2)}) collective-permute-start(bf16[64,1920]{1,0:T(8,128)(2,1)S(1)} %collective-permute-done.3.refs_2_), channel_id=1, source_target_pairs={{0,1},{1,0},{2,3},{3,2},{4,5},{5,4},{6,7},{7,6},{8,9},{9,8},{10,11... | collective-permute-start | bytes 737288 | tf_op jit(solution)/shard_map/ppermute | solution.py:20
  20.2 6.7 %collective-permute-start.8 = (bf16[64,896]{1,0:T(8,128)(2,1)S(1)}, bf16[64,896]{1,0:T(8,128)(2,1)S(1)}, u32[]{:S(2)}, u32[]{:S(2)}) collective-permute-start(bf16[64,896]{1,0:T(8,128)(2,1)S(1)} %collective-permute-done.1.refs_6_), channel_id=1, source_target_pairs={{0,1},{1,0},{2,3},{3,2},{4,5},{5,4},{6,7},{7,6},{8,9},{9,8},{10,11... | collective-permute-start | bytes 344072 | tf_op jit(solution)/shard_map/ppermute | solution.py:20
  25.8 5.5 %collective-permute-start.11 = (bf16[64,896]{1,0:T(8,128)(2,1)S(1)}, bf16[64,896]{1,0:T(8,128)(2,1)S(1)}, u32[]{:S(2)}, u32[]{:S(2)}) collective-permute-start(bf16[64,896]{1,0:T(8,128)(2,1)S(1)} %collective-permute-done.10.refs_10_), channel_id=1, source_target_pairs={{0,1},{1,0},{2,3},{3,2},{4,5},{5,4},{6,7},{7,6},{8,9},{9,8},{10,11... | collective-permute-start | bytes 344072 | tf_op jit(solution)/shard_map/ppermute | solution.py:20
  25.8 12.5 %collective-permute-start.13 = (bf16[128,1024]{1,0:T(8,128)(2,1)S(1)}, bf16[128,1024]{1,0:T(8,128)(2,1)S(1)}, u32[]{:S(2)}, u32[]{:S(2)}) collective-permute-start(bf16[128,1024]{1,0:T(8,128)(2,1)S(1)} %constant_dynamic-update-slice_fusion.refs_0_), channel_id=1, source_target_pairs={{0,4},{4,0},{8,12},{12,8},{16,20},{20,16},{24,28},{28,24},{1,5},{5... | collective-permute-start | bytes 786440 | tf_op jit(solution)/shard_map/ppermute | solution.py:20
  26.9 11.5 %collective-permute-start.12 = (bf16[128,896]{1,0:T(8,128)(2,1)S(1)}, bf16[128,896]{1,0:T(8,128)(2,1)S(1)}, u32[]{:S(2)}, u32[]{:S(2)}) collective-permute-start(bf16[128,896]{1,0:T(8,128)(2,1)S(1)} %slice.94), channel_id=1, source_target_pairs={{0,2},{1,3},{2,0},{3,1},{4,6},{5,7},{6,4},{7,5},{8,10},{9,11},{10,... | collective-permute-start | bytes 688136 | tf_op jit(solution)/shard_map/ppermute | solution.py:20
  28.3 10.0 %collective-permute-start.14 = (bf16[288,256]{1,0:T(8,128)(2,1)S(1)}, bf16[288,256]{1,0:T(8,128)(2,1)S(1)}, u32[]{:S(2)}, u32[]{:S(2)}) collective-permute-start(bf16[288,256]{1,0:T(8,128)(2,1)S(1)} %get-tuple-element.119), channel_id=1, source_target_pairs={{0,16},{4,20},{8,24},{12,28},{16,0},{20,4},{24,8},{28,12},{1,17},{... | collective-permute-start | bytes 442376 | tf_op jit(solution)/shard_map/ppermute | solution.py:20
  38.4 5.6 %collective-permute-start.15 = (bf16[64,896]{1,0:T(8,128)(2,1)S(1)}, bf16[64,896]{1,0:T(8,128)(2,1)S(1)}, u32[]{:S(2)}, u32[]{:S(2)}) collective-permute-start(bf16[64,896]{1,0:T(8,128)(2,1)S(1)} %slice.74), channel_id=1, source_target_pairs={{0,2},{1,3},{2,0},{3,1},{4,6},{5,7},{6,4},{7,5},{8,10},{9,11},{10,... | collective-permute-start | bytes 344072 | tf_op jit(solution)/shard_map/ppermute | solution.py:20
  39.0 5.3 %collective-permute-start.16 = (bf16[64,896]{1,0:T(8,128)(2,1)S(1)}, bf16[64,896]{1,0:T(8,128)(2,1)S(1)}, u32[]{:S(2)}, u32[]{:S(2)}) collective-permute-start(bf16[64,896]{1,0:T(8,128)(2,1)S(1)} %slice.75), channel_id=1, source_target_pairs={{0,4},{4,0},{8,12},{12,8},{16,20},{20,16},{24,28},{28,24},{1,5},{5... | collective-permute-start | bytes 344072 | tf_op jit(solution)/shard_map/ppermute | solution.py:20
  44.3 5.4 %collective-permute-start.18 = (bf16[128,1024]{1,0:T(8,128)(2,1)S(1)}, bf16[128,1024]{1,0:T(8,128)(2,1)S(1)}, u32[]{:S(2)}, u32[]{:S(2)}) collective-permute-start(bf16[128,1024]{1,0:T(8,128)(2,1)S(1)} %constant_dynamic-update-slice_fusion.refs_0_), channel_id=1, source_target_pairs={{0,1},{1,0},{2,3},{3,2},{4,5},{5,4},{6,7},{7,6},{8,9},{9,8},{10,11... | collective-permute-start | bytes 786440 | tf_op jit(solution)/shard_map/ppermute | solution.py:20
  44.3 5.4 %collective-permute-start.20 = (bf16[128,1024]{1,0:T(8,128)(2,1)S(1)}, bf16[128,1024]{1,0:T(8,128)(2,1)S(1)}, u32[]{:S(2)}, u32[]{:S(2)}) collective-permute-start(bf16[128,1024]{1,0:T(8,128)(2,1)S(1)} %collective-permute-done.13.refs_4_), channel_id=1, source_target_pairs={{0,1},{1,0},{2,3},{3,2},{4,5},{5,4},{6,7},{7,6},{8,9},{9,8},{10,11... | collective-permute-start | bytes 786440 | tf_op jit(solution)/shard_map/ppermute | solution.py:20
  46.7 11.7 %collective-permute-start.23 = (bf16[128,896]{1,0:T(8,128)(2,1)S(1)}, bf16[128,896]{1,0:T(8,128)(2,1)S(1)}, u32[]{:S(2)}, u32[]{:S(2)}) collective-permute-start(bf16[128,896]{1,0:T(8,128)(2,1)S(1)} %slice.76), channel_id=1, source_target_pairs={{0,2},{1,3},{2,0},{3,1},{4,6},{5,7},{6,4},{7,5},{8,10},{9,11},{10,... | collective-permute-start | bytes 688136 | tf_op jit(solution)/shard_map/ppermute | solution.py:20
  48.2 10.2 %collective-permute-start.24 = (bf16[64,1792]{1,0:T(8,128)(2,1)S(1)}, bf16[64,1792]{1,0:T(8,128)(2,1)S(1)}, u32[]{:S(2)}, u32[]{:S(2)}) collective-permute-start(bf16[64,1792]{1,0:T(8,128)(2,1)S(1)} %pad_maximum_fusion), channel_id=1, source_target_pairs={{0,4},{4,0},{8,12},{12,8},{16,20},{20,16},{24,28},{28,24},{1,5},{5... | collective-permute-start | bytes 688136 | tf_op jit(solution)/shard_map/ppermute | solution.py:20
  49.7 8.7 %collective-permute-start.25 = (bf16[288,256]{1,0:T(8,128)(2,1)S(1)}, bf16[288,256]{1,0:T(8,128)(2,1)S(1)}, u32[]{:S(2)}, u32[]{:S(2)}) collective-permute-start(bf16[288,256]{1,0:T(8,128)(2,1)S(1)} %get-tuple-element.89), channel_id=1, source_target_pairs={{0,16},{4,20},{8,24},{12,28},{16,0},{20,4},{24,8},{28,12},{1,17},{... | collective-permute-start | bytes 442376 | tf_op jit(solution)/shard_map/ppermute | solution.py:20
  59.1 18.2 %collective-permute-start.31 = (bf16[64,896]{1,0:T(8,128)(2,1)S(1)}, bf16[64,896]{1,0:T(8,128)(2,1)S(1)}, u32[]{:S(2)}, u32[]{:S(2)}) collective-permute-start(bf16[64,896]{1,0:T(8,128)(2,1)S(1)} %add_convert_fusion.8), channel_id=1, source_target_pairs={{0,4},{4,0},{8,12},{12,8},{16,20},{20,16},{24,28},{28,24},{1,5},{5... | collective-permute-start | bytes 344072 | tf_op jit(solution)/shard_map/ppermute | solution.py:20
  61.2 8.6 %collective-permute-start.27 = (bf16[64,896]{1,0:T(8,128)(2,1)S(1)}, bf16[64,896]{1,0:T(8,128)(2,1)S(1)}, u32[]{:S(2)}, u32[]{:S(2)}) collective-permute-start(bf16[64,896]{1,0:T(8,128)(2,1)S(1)} %get-tuple-element.117), channel_id=1, source_target_pairs={{0,2},{1,3},{2,0},{3,1},{4,6},{5,7},{6,4},{7,5},{8,10},{9,11},{10,... | collective-permute-start | bytes 344072 | tf_op jit(solution)/shard_map/ppermute | solution.py:20
  61.8 8.0 %collective-permute-start.28 = (bf16[64,896]{1,0:T(8,128)(2,1)S(1)}, bf16[64,896]{1,0:T(8,128)(2,1)S(1)}, u32[]{:S(2)}, u32[]{:S(2)}) collective-permute-start(bf16[64,896]{1,0:T(8,128)(2,1)S(1)} %get-tuple-element.116), channel_id=1, source_target_pairs={{0,4},{4,0},{8,12},{12,8},{16,20},{20,16},{24,28},{28,24},{1,5},{5... | collective-permute-start | bytes 344072 | tf_op jit(solution)/shard_map/ppermute | solution.py:20
  62.7 27.1 %collective-permute-start.37 = (bf16[64,896]{1,0:T(8,128)(2,1)S(1)}, bf16[64,896]{1,0:T(8,128)(2,1)S(1)}, u32[]{:S(2)}, u32[]{:S(2)}) collective-permute-start(bf16[64,896]{1,0:T(8,128)(2,1)S(1)} %add_convert_fusion.6), channel_id=1, source_target_pairs={{0,2},{1,3},{2,0},{3,1},{4,6},{5,7},{6,4},{7,5},{8,10},{9,11},{10,... | collective-permute-start | bytes 344072 | tf_op jit(solution)/shard_map/ppermute | solution.py:20
  64.2 13.1 %collective-permute-start.32 = (bf16[576,256]{1,0:T(8,128)(2,1)S(1)}, bf16[576,256]{1,0:T(8,128)(2,1)S(1)}, u32[]{:S(2)}, u32[]{:S(2)}) collective-permute-start(bf16[576,256]{1,0:T(8,128)(2,1)S(1)} %maximum_select_fusion), channel_id=1, source_target_pairs={{0,8},{4,12},{8,0},{12,4},{16,24},{20,28},{24,16},{28,20},{1,9},{5... | collective-permute-start | bytes 884744 | tf_op jit(solution)/shard_map/ppermute | solution.py:20
  69.8 7.5 %collective-permute-start.29 = (bf16[128,896]{1,0:T(8,128)(2,1)S(1)}, bf16[128,896]{1,0:T(8,128)(2,1)S(1)}, u32[]{:S(2)}, u32[]{:S(2)}) collective-permute-start(bf16[128,896]{1,0:T(8,128)(2,1)S(1)} %add_convert_fusion.4), channel_id=1, source_target_pairs={{0,4},{4,0},{8,12},{12,8},{16,20},{20,16},{24,28},{28,24},{1,5},{5... | collective-permute-start | bytes 688136 | tf_op jit(solution)/shard_map/ppermute | solution.py:20
  71.2 6.6 %collective-permute-start.30 = (bf16[128,896]{1,0:T(8,128)(2,1)S(1)}, bf16[128,896]{1,0:T(8,128)(2,1)S(1)}, u32[]{:S(2)}, u32[]{:S(2)}) collective-permute-start(bf16[128,896]{1,0:T(8,128)(2,1)S(1)} %add_convert_fusion.3), channel_id=1, source_target_pairs={{0,2},{1,3},{2,0},{3,1},{4,6},{5,7},{6,4},{7,5},{8,10},{9,11},{10,... | collective-permute-start | bytes 688136 | tf_op jit(solution)/shard_map/ppermute | solution.py:20
  77.8 7.3 %collective-permute-start.36 = (bf16[576,256]{1,0:T(8,128)(2,1)S(1)}, bf16[576,256]{1,0:T(8,128)(2,1)S(1)}, u32[]{:S(2)}, u32[]{:S(2)}) collective-permute-start(bf16[576,256]{1,0:T(8,128)(2,1)S(1)} %broadcast_select_fusion.1), channel_id=1, source_target_pairs={{0,4},{4,0},{8,12},{12,8},{16,20},{20,16},{24,28},{28,24},{1,5},{5... | collective-permute-start | bytes 884744 | tf_op jit(solution)/shard_map/ppermute | solution.py:20
  78.7 10.4 %collective-permute-start.33 = (bf16[64,896]{1,0:T(8,128)(2,1)S(1)}, bf16[64,896]{1,0:T(8,128)(2,1)S(1)}, u32[]{:S(2)}, u32[]{:S(2)}) collective-permute-start(bf16[64,896]{1,0:T(8,128)(2,1)S(1)} %get-tuple-element.121), channel_id=1, source_target_pairs={{0,16},{4,20},{8,24},{12,28},{16,0},{20,4},{24,8},{28,12},{1,17},{... | collective-permute-start | bytes 344072 | tf_op jit(solution)/shard_map/ppermute | solution.py:20
  80.9 8.2 %collective-permute-start.34 = (bf16[64,896]{1,0:T(8,128)(2,1)S(1)}, bf16[64,896]{1,0:T(8,128)(2,1)S(1)}, u32[]{:S(2)}, u32[]{:S(2)}) collective-permute-start(bf16[64,896]{1,0:T(8,128)(2,1)S(1)} %get-tuple-element.120), channel_id=1, source_target_pairs={{0,24},{4,28},{8,16},{12,20},{16,8},{20,12},{24,0},{28,4},{1,25},{... | collective-permute-start | bytes 344072 | tf_op jit(solution)/shard_map/ppermute | solution.py:20
  82.9 6.8 %collective-permute-start.35 = (bf16[64,896]{1,0:T(8,128)(2,1)S(1)}, bf16[64,896]{1,0:T(8,128)(2,1)S(1)}, u32[]{:S(2)}, u32[]{:S(2)}) collective-permute-start(bf16[64,896]{1,0:T(8,128)(2,1)S(1)} %add_convert_fusion.7), channel_id=1, source_target_pairs={{0,8},{4,12},{8,0},{12,4},{16,24},{20,28},{24,16},{28,20},{1,9},{5... | collective-permute-start | bytes 344072 | tf_op jit(solution)/shard_map/ppermute | solution.py:20
  (9 other events, 44.9 us)

commit v7 on v6

--- a/solution.py
+++ b/solution.py
@@ -412,8 +412,6 @@
     far_2, near_3, w_gate, w_up, page, both_1, *late_pieces = tie(
         (far_2, near_3, w_gate, w_up, page, both_1, *late_pieces)
     )
-    upper, lower = jnp.split(page, 2, axis=0)
-    upper_far, upper = page_far(upper)
     far_3 = flip(bare(near_3), "tp", 2)
 
     near_late = jnp.concatenate(late_pieces, axis=0)
@@ -433,7 +431,7 @@
     *first, w_down = run_experts(
         ranks, pieces, w_gate, w_up, w_down, 4 * rows, columns, top, True
     )
-    first, far_late, near_odds, upper_far = tie((first, far_late, near_odds, upper_far))
+    first, far_late, near_odds, page = tie((first, far_late, near_odds, page))
 
     def add_core(given, own):
         total = total_of(own, flip(given, "tp", 1))
@@ -442,14 +440,14 @@
     far_odds_y = flip(bare(cut(near_odds, 0, half)), "tp", 2)
     far_odds_x = flip(cut(far_late, half, rest), "ep", 1)
     sent, kept = add_core(*first)
-    far_odds_y, far_odds_x, sent, kept, lower, near_late, far_late, near_odds = tie(
-        (far_odds_y, far_odds_x, sent, kept, lower, near_late, far_late, near_odds)
+    swapped = flip(page, "ep", 2)
+    far_odds_y, far_odds_x, sent, kept, swapped, near_late, far_late, near_odds = tie(
+        (far_odds_y, far_odds_x, sent, kept, swapped, near_late, far_late, near_odds)
     )
     early = [flip(array, "tp", 1) for array in (near_late, far_late, near_odds)]
     last = [flip(array, "tp", 1) for array in (far_odds_y, far_odds_x)]
     over_23 = flip(cut(sent, 2, 2), "tp", 2)
     over_1 = flip(jnp.concatenate([cut(kept, 1, 1), cut(sent, 1, 1)], axis=1), "ep", 1)
-    lower_far, lower = page_far(lower)
 
     pieces = with_core(0, 0, near_late, early[0]) + with_core(0, 2, far_late, early[1])
     pieces += with_core(len(late), 0, near_odds, early[2])
@@ -460,9 +458,8 @@
             ranks, pieces, w_gate, w_up, w_down, 2 * len(late) * rows, columns, top, False
         )
     ]
-    second, over_23, over_1, lower_far = tie((second, over_23, over_1, lower_far))
-    page = jnp.concatenate([upper, lower], axis=0)
-    page = page_take(page, jnp.concatenate([upper_far, lower_far], axis=0), 2)
+    second, over_23, over_1 = tie((second, over_23, over_1))
+    page = page_take(page, swapped, 1)
     late_sent, late_kept = add_core(*second)
     over_3 = flip(total_of(cut(kept, 3, 1), cut(over_23, 1, 1)), "ep", 1)
     zero = flip(total_of(cut(sent, 0, 1), over_1[:, columns:]), "tp", 2)
@@ -470,10 +467,11 @@
 
     over_y = flip(cut(late_sent, len(late), half), "tp", 2)
     over_x = flip(cut(late_sent, len(late) + half, rest), "ep", 1)
-    if levels > 1:
-        page = page_hop(page, 1)
-    some = queries.shape[0] // 2
-    attended = attend_part(ranks, lengths, queries, cache_pages, groups, 0, some)
+    swapped, page = page_far(page)
+    count = queries.shape[0]
+    starts = [0, count // 4, 3 * count // 4, count]
+    attend = functools.partial(attend_part, ranks, lengths, queries, cache_pages, groups)
+    attended = attend(starts[0], starts[1])
     over_y, over_x, attended = tie((over_y, over_x, attended))
     odd = total_of(
         cut(late_kept, len(late), len(late)), jnp.pad(over_y, ((0, rest * rows), (0, 0)))
@@ -481,14 +479,15 @@
     odd = flip(odd, "ep", 1)
     even = total_of(cut(late_sent, 0, len(late)), jnp.pad(over_x, ((half * rows, 0), (0, 0))))
     even = flip(even, "tp", 2)
-    attended = attend_part(
-        ranks, lengths, queries, cache_pages, groups, some, queries.shape[0] - some, attended
-    )
-    odd, even, over_3, attended, page = tie((odd, even, over_3, attended, page))
+    attended = attend(starts[1], starts[2] - starts[1], attended)
+    odd, even, over_3, zero, attended, swapped = tie(
+        (odd, even, over_3, zero, attended, swapped)
+    )
     even = total_of(cut(late_kept, 0, len(late)), even, odd)
     back = [flip(cut(even, i, 1), "ep", 2 * m) for i, m in enumerate(late)]
     back.append(flip(total_of(cut(kept, 2, 1), cut(over_23, 0, 1), over_3), "ep", 2))
-    page = page_hop(page, 0)
+    page = page_hop(page_take(page, swapped, 2) if levels > 2 else page, 0)
+    attended = attend(starts[2], starts[3] - starts[2], attended)
     attended = attend_traded(
         ranks, lengths, swap_slot, swap_mask, queries, page, attended, groups
     )

time: 90.8 us -> 91.6 us (level)
  waiting for transfers between devices: 18.8 us -> 14.2 us
  starting transfers between devices: 36.1 us -> 39.9 us
  Pallas kernels: 31.9 us -> 33.6 us
    ppermute x38 -> x37, waiting for transfers between devices: 18.8 us -> 14.2 us  [flip(): return lax.ppermute(block, axis, [(i, i ^ apart) for i in range(count)])]
    ppermute x38 -> x37, starting transfers between devices: 36.1 us -> 39.9 us  [flip(): return lax.ppermute(block, axis, [(i, i ^ apart) for i in range(count)])]
    pallas_call x2 -> x3, Pallas kernels: 11.1 us -> 12.9 us  [attend_part(): pl.pallas_call(kernel, out_shape=jax.ShapeDtypeStruct((count, heads, LAT)...]
  transfers between devices with their start and end apart: 38 -> 37, of which waited for: 13 -> 9; matrix products, arithmetic and copies ran while one was open for 1% -> 1% of each run, Pallas kernels for 33% -> 35%
where the time goes in v7:
time: 91.6 us; the launch traced here: 91.2 us
  starting transfers between devices  39.9 us (44%)
  Pallas kernels  33.6 us (37%)
  waiting for transfers between devices  14.2 us (16%)
  other arithmetic  1.65 us (2%)
  between operations  1.59 us (2%)
    ppermute x37, starting transfers between devices, flip(): return lax.ppermute(block, axis, [(i, i ^ apart) for i in range(count)])  39.9 us
    ppermute x37, waiting for transfers between devices, flip(): return lax.ppermute(block, axis, [(i, i ^ apart) for i in range(count)])  14.2 us
    pallas_call x3, Pallas kernels, attend_part(): pl.pallas_call(kernel, out_shape=jax.ShapeDtypeStruct((count, heads, LAT)...  12.9 us
    pallas_call x2, Pallas kernels, run_experts(): pl.pallas_call(kernel, out_shape=[pltpu.VMEM((2 * rows, columns), jnp.bfl...  11.9 us
    pallas_call x1, Pallas kernels, load(): pl.pallas_call(load_kernel, out_shape=[pltpu.VMEM(w.shape, w.dtype) for w...  4.21 us
    pallas_call x1, Pallas kernels, attend_traded(): pl.pallas_call(functools.partial(attend_traded_kernel, groups), out_shape...  2.71 us
    pallas_call x1, Pallas kernels, pick(): pl.pallas_call(functools.partial(pick_kernel, groups), out_shape=(pltpu.V...  1.89 us
  transfers between devices with their start and end apart: 37, of which 9 were waited for; matrix products, arithmetic and copies ran while one was open for 1% of the time, Pallas kernels for 35%

profile of v7, /device:TPU:0, one launch (start us, length us, event | category | flops | bytes accessed | tf_op | source)
XLA Modules:
  0.0 91.2 jit_solution(15900456591422585136)
XLA Ops:
  0.7 1.9 %pick.1 = (bf16[64,1024]{1,0:T(8,128)(2,1)S(1)}, bf16[64,1920]{1,0:T(8,128)(2,1)S(1)}, bf16[576,256]{1,0:T(8,128)(2,1)S(1)}) custom-call(s32[2]{0:T(128)S(1)} %pad_add_fusion.ranks_ref, s32[32]{0:T(128)} %slots_ref.3, s32[8,64]{1,0:T(8,128)} %bitcast.17, f32[8,64]{1,0:T(8,128)} %bitcast.18, bf16[64,3584]{1,0:T(8,128)(2,1)} %refs_0_.2, ...), custom_call_target="tpu_custom_call" | custom-call | tf_op jit(solution)/shard_map/pick/pallas_call | solution.py:96
  2.6 3.1 %collective-permute-start = (bf16[64,1024]{1,0:T(8,128)(2,1)S(1)}, bf16[64,1024]{1,0:T(8,128)(2,1)S(1)}, u32[]{:S(2)}, u32[]{:S(2)}) collective-permute-start(bf16[64,1024]{1,0:T(8,128)(2,1)S(1)} %get-tuple-element.57.refs_1_), channel_id=1, source_target_pairs={{0,8},{4,12},{8,0},{12,4},{16,24},{20,28},{24,16},{28,20},{1,9},{5... | collective-permute-start | bytes 393224 | tf_op jit(solution)/shard_map/ppermute | solution.py:20
  5.7 1.5 %collective-permute-start.3 = (bf16[64,1920]{1,0:T(8,128)(2,1)S(1)}, bf16[64,1920]{1,0:T(8,128)(2,1)S(1)}, u32[]{:S(2)}, u32[]{:S(2)}) collective-permute-start(bf16[64,1920]{1,0:T(8,128)(2,1)S(1)} %get-tuple-element.64), channel_id=1, source_target_pairs={{0,4},{4,0},{8,12},{12,8},{16,20},{20,16},{24,28},{28,24},{1,5},{5... | collective-permute-start | bytes 737288 | tf_op jit(solution)/shard_map/ppermute | solution.py:20
  7.2 2.6 %collective-permute-start.4 = (bf16[64,1024]{1,0:T(8,128)(2,1)S(1)}, bf16[64,1024]{1,0:T(8,128)(2,1)S(1)}, u32[]{:S(2)}, u32[]{:S(2)}) collective-permute-start(bf16[64,1024]{1,0:T(8,128)(2,1)S(1)} %get-tuple-element.57.refs_1_), channel_id=1, source_target_pairs={{0,16},{4,20},{8,24},{12,28},{16,0},{20,4},{24,8},{28,12},{1,17},{... | collective-permute-start | bytes 393224 | tf_op jit(solution)/shard_map/ppermute | solution.py:20
  10.0 2.3 %collective-permute-start.2 = (bf16[64,1024]{1,0:T(8,128)(2,1)S(1)}, bf16[64,1024]{1,0:T(8,128)(2,1)S(1)}, u32[]{:S(2)}, u32[]{:S(2)}) collective-permute-start(bf16[64,1024]{1,0:T(8,128)(2,1)S(1)} %collective-permute-done.refs_4_), channel_id=1, source_target_pairs={{0,4},{4,0},{8,12},{12,8},{16,20},{20,16},{24,28},{28,24},{1,5},{5... | collective-permute-start | bytes 393224 | tf_op jit(solution)/shard_map/ppermute | solution.py:20
  12.4 1.5 %collective-permute-start.1 = (bf16[64,896]{1,0:T(8,128)(2,1)S(1)}, bf16[64,896]{1,0:T(8,128)(2,1)S(1)}, u32[]{:S(2)}, u32[]{:S(2)}) collective-permute-start(bf16[64,896]{1,0:T(8,128)(2,1)S(1)} %slice.71), channel_id=1, source_target_pairs={{0,2},{1,3},{2,0},{3,1},{4,6},{5,7},{6,4},{7,5},{8,10},{9,11},{10,... | collective-permute-start | bytes 344072 | tf_op jit(solution)/shard_map/ppermute | solution.py:20
  13.9 4.2 %load.1 = (bf16[3,3584,256]{2,1,0:T(8,128)(2,1)S(1)}, bf16[3,3584,256]{2,1,0:T(8,128)(2,1)S(1)}) custom-call(bf16[3,3584,256]{2,1,0:T(8,128)(2,1)} %refs_0_.1, bf16[3,3584,256]{2,1,0:T(8,128)(2,1)} %refs_1_), custom_call_target="tpu_custom_call" | custom-call | bytes 11010048 | tf_op jit(solution)/shard_map/load/pallas_call | solution.py:166
  18.1 1.4 %collective-permute-done.4 = bf16[64,1024]{1,0:T(8,128)(2,1)S(1)} collective-permute-done((bf16[64,1024]{1,0:T(8,128)(2,1)S(1)}, bf16[64,1024]{1,0:T(8,128)(2,1)S(1)}, u32[]{:S(2)}, u32[]{:S(2)}) %collective-permute-start.4) | collective-permute-done | bytes 131104 | tf_op jit(solution)/shard_map/ppermute | solution.py:20
  20.2 1.4 %collective-permute-start.10 = (bf16[64,896]{1,0:T(8,128)(2,1)S(1)}, bf16[64,896]{1,0:T(8,128)(2,1)S(1)}, u32[]{:S(2)}, u32[]{:S(2)}) collective-permute-start(bf16[64,896]{1,0:T(8,128)(2,1)S(1)} %slice.72), channel_id=1, source_target_pairs={{0,2},{1,3},{2,0},{3,1},{4,6},{5,7},{6,4},{7,5},{8,10},{9,11},{10,... | collective-permute-start | bytes 344072 | tf_op jit(solution)/shard_map/ppermute | solution.py:20
  21.9 3.8 %collective-permute-done.10.refs_10_ = bf16[64,896]{1,0:T(8,128)(2,1)S(1)} collective-permute-done((bf16[64,896]{1,0:T(8,128)(2,1)S(1)}, bf16[64,896]{1,0:T(8,128)(2,1)S(1)}, u32[]{:S(2)}, u32[]{:S(2)}) %collective-permute-start.10) | collective-permute-done | bytes 114720 | tf_op jit(solution)/shard_map/ppermute | solution.py:20
  26.8 1.5 %collective-permute-start.12 = (bf16[128,896]{1,0:T(8,128)(2,1)S(1)}, bf16[128,896]{1,0:T(8,128)(2,1)S(1)}, u32[]{:S(2)}, u32[]{:S(2)}) collective-permute-start(bf16[128,896]{1,0:T(8,128)(2,1)S(1)} %slice.94), channel_id=1, source_target_pairs={{0,2},{1,3},{2,0},{3,1},{4,6},{5,7},{6,4},{7,5},{8,10},{9,11},{10,... | collective-permute-start | bytes 688136 | tf_op jit(solution)/shard_map/ppermute | solution.py:20
  28.3 6.2 %experts.2 = (bf16[512,896]{1,0:T(8,128)(2,1)S(1)}, bf16[512,896]{1,0:T(8,128)(2,1)S(1)}, bf16[3,256,3584]{2,1,0:T(8,128)(2,1)S(1)}) custom-call(s32[2]{0:T(128)S(1)} %pad_add_fusion.ranks_ref, bf16[64,3584]{1,0:T(8,128)(2,1)S(1)} %copy-done, bf16[64,1024]{1,0:T(8,128)(2,1)S(1)} %get-tuple-element.57.refs_1_, ...), custom_call_target="tpu_custom_call" | custom-call | flops 4227858432 | bytes 3670016 | tf_op jit(solution)/shard_map/experts/pallas_call | solution.py:311
  34.6 2.3 %collective-permute-start.17 = (bf16[576,256]{1,0:T(8,128)(2,1)S(1)}, bf16[576,256]{1,0:T(8,128)(2,1)S(1)}, u32[]{:S(2)}, u32[]{:S(2)}) collective-permute-start(bf16[576,256]{1,0:T(8,128)(2,1)S(1)} %get-tuple-element.79), channel_id=1, source_target_pairs={{0,8},{4,12},{8,0},{12,4},{16,24},{20,28},{24,16},{28,20},{1,9},{5... | collective-permute-start | bytes 884744 | tf_op jit(solution)/shard_map/ppermute | solution.py:20
  36.9 1.5 %collective-permute-start.14 = (bf16[64,896]{1,0:T(8,128)(2,1)S(1)}, bf16[64,896]{1,0:T(8,128)(2,1)S(1)}, u32[]{:S(2)}, u32[]{:S(2)}) collective-permute-start(bf16[64,896]{1,0:T(8,128)(2,1)S(1)} %slice.74), channel_id=1, source_target_pairs={{0,2},{1,3},{2,0},{3,1},{4,6},{5,7},{6,4},{7,5},{8,10},{9,11},{10,... | collective-permute-start | bytes 344072 | tf_op jit(solution)/shard_map/ppermute | solution.py:20
  38.5 1.1 %collective-permute-start.15 = (bf16[64,896]{1,0:T(8,128)(2,1)S(1)}, bf16[64,896]{1,0:T(8,128)(2,1)S(1)}, u32[]{:S(2)}, u32[]{:S(2)}) collective-permute-start(bf16[64,896]{1,0:T(8,128)(2,1)S(1)} %slice.75), channel_id=1, source_target_pairs={{0,4},{4,0},{8,12},{12,8},{16,20},{20,16},{24,28},{28,24},{1,5},{5... | collective-permute-start | bytes 344072 | tf_op jit(solution)/shard_map/ppermute | solution.py:20
  39.9 2.4 %collective-permute-done.14.refs_6_ = bf16[64,896]{1,0:T(8,128)(2,1)S(1)} collective-permute-done((bf16[64,896]{1,0:T(8,128)(2,1)S(1)}, bf16[64,896]{1,0:T(8,128)(2,1)S(1)}, u32[]{:S(2)}, u32[]{:S(2)}) %collective-permute-start.14) | collective-permute-done | bytes 114720 | tf_op jit(solution)/shard_map/ppermute | solution.py:20
  42.3 1.2 %collective-permute-done.15.refs_8_ = bf16[64,896]{1,0:T(8,128)(2,1)S(1)} collective-permute-done((bf16[64,896]{1,0:T(8,128)(2,1)S(1)}, bf16[64,896]{1,0:T(8,128)(2,1)S(1)}, u32[]{:S(2)}, u32[]{:S(2)}) %collective-permute-start.15) | collective-permute-done | bytes 114720 | tf_op jit(solution)/shard_map/ppermute | solution.py:20
  45.8 1.2 %collective-permute-done.21.refs_7_ = bf16[64,896]{1,0:T(8,128)(2,1)S(1)} collective-permute-done((bf16[64,896]{1,0:T(8,128)(2,1)S(1)}, bf16[64,896]{1,0:T(8,128)(2,1)S(1)}, u32[]{:S(2)}, u32[]{:S(2)}) %collective-permute-start.21) | collective-permute-done | bytes 114720 | tf_op jit(solution)/shard_map/ppermute | solution.py:20
  48.1 1.4 %collective-permute-start.23 = (bf16[128,896]{1,0:T(8,128)(2,1)S(1)}, bf16[128,896]{1,0:T(8,128)(2,1)S(1)}, u32[]{:S(2)}, u32[]{:S(2)}) collective-permute-start(bf16[128,896]{1,0:T(8,128)(2,1)S(1)} %slice.76), channel_id=1, source_target_pairs={{0,2},{1,3},{2,0},{3,1},{4,6},{5,7},{6,4},{7,5},{8,10},{9,11},{10,... | collective-permute-start | bytes 688136 | tf_op jit(solution)/shard_map/ppermute | solution.py:20
  49.5 5.7 %experts.3 = (bf16[512,896]{1,0:T(8,128)(2,1)S(1)}, bf16[512,896]{1,0:T(8,128)(2,1)S(1)}) custom-call(s32[2]{0:T(128)S(1)} %pad_add_fusion.ranks_ref, bf16[128,1024]{1,0:T(8,128)(2,1)S(1)} %constant_dynamic-update-slice_fusion.refs_0_, bf16[128,1024]{1,0:T(8,128)(2,1)S(1)} %collective-permute-done.18.refs_1_, ...), custom_call_target="tpu_custom_call" | custom-call | flops 4227858432 | bytes 3670016 | tf_op jit(solution)/shard_map/experts/pallas_call | solution.py:311
  56.2 1.8 %collective-permute-done.25 = bf16[512,896]{1,0:T(8,128)(2,1)S(1)} collective-permute-done((bf16[512,896]{1,0:T(8,128)(2,1)S(1)}, bf16[512,896]{1,0:T(8,128)(2,1)S(1)}, u32[]{:S(2)}, u32[]{:S(2)}) %collective-permute-start.25) | collective-permute-done | bytes 917536 | tf_op jit(solution)/shard_map/ppermute | solution.py:20
  58.3 1.4 %collective-permute-start.26 = (bf16[64,896]{1,0:T(8,128)(2,1)S(1)}, bf16[64,896]{1,0:T(8,128)(2,1)S(1)}, u32[]{:S(2)}, u32[]{:S(2)}) collective-permute-start(bf16[64,896]{1,0:T(8,128)(2,1)S(1)} %get-tuple-element.117), channel_id=1, source_target_pairs={{0,2},{1,3},{2,0},{3,1},{4,6},{5,7},{6,4},{7,5},{8,10},{9,11},{10,... | collective-permute-start | bytes 344072 | tf_op jit(solution)/shard_map/ppermute | solution.py:20
  61.4 2.8 %collective-permute-start.32 = (bf16[576,256]{1,0:T(8,128)(2,1)S(1)}, bf16[576,256]{1,0:T(8,128)(2,1)S(1)}, u32[]{:S(2)}, u32[]{:S(2)}) collective-permute-start(bf16[576,256]{1,0:T(8,128)(2,1)S(1)} %broadcast_select_fusion.2), channel_id=1, source_target_pairs={{0,16},{4,20},{8,24},{12,28},{16,0},{20,4},{24,8},{28,12},{1,17},{... | collective-permute-start | bytes 884744 | tf_op jit(solution)/shard_map/ppermute | solution.py:20
  64.2 3.6 %attend_local.3.refs_0_ = bf16[16,128,512]{2,1,0:T(8,128)(2,1)} custom-call(s32[2]{0:T(128)S(1)} %pad_add_fusion.ranks_ref, s32[512]{0:T(512)S(1)} %copy-done.1, bf16[16,576,128]{2,1,0:T(8,128)(2,1)} %bitcast.13, bf16[16,576,256]{2,1,0:T(8,128)(2,1)} %bitcast.10), custom_call_target="tpu_custom_call" | custom-call | flops 285212672 | bytes 2293760 | tf_op jit(solution)/shard_map/attend_local/pallas_call | solution.py:130
  67.9 1.6 %collective-permute-start.29 = (bf16[128,896]{1,0:T(8,128)(2,1)S(1)}, bf16[128,896]{1,0:T(8,128)(2,1)S(1)}, u32[]{:S(2)}, u32[]{:S(2)}) collective-permute-start(bf16[128,896]{1,0:T(8,128)(2,1)S(1)} %add_convert_fusion.3), channel_id=1, source_target_pairs={{0,2},{1,3},{2,0},{3,1},{4,6},{5,7},{6,4},{7,5},{8,10},{9,11},{10,... | collective-permute-start | bytes 688136 | tf_op jit(solution)/shard_map/ppermute | solution.py:20
  69.4 1.1 %collective-permute-start.28 = (bf16[128,896]{1,0:T(8,128)(2,1)S(1)}, bf16[128,896]{1,0:T(8,128)(2,1)S(1)}, u32[]{:S(2)}, u32[]{:S(2)}) collective-permute-start(bf16[128,896]{1,0:T(8,128)(2,1)S(1)} %add_convert_fusion.4), channel_id=1, source_target_pairs={{0,4},{4,0},{8,12},{12,8},{16,20},{20,16},{24,28},{28,24},{1,5},{5... | collective-permute-start | bytes 688136 | tf_op jit(solution)/shard_map/ppermute | solution.py:20
  71.6 5.6 %attend_local.4.refs_0_ = bf16[16,128,512]{2,1,0:T(8,128)(2,1)} custom-call(s32[2]{0:T(128)S(1)} %pad_add_fusion.ranks_ref, s32[512]{0:T(512)S(1)} %copy-done.1, bf16[16,576,128]{2,1,0:T(8,128)(2,1)} %bitcast.14, bf16[16,576,256]{2,1,0:T(8,128)(2,1)} %bitcast.11, bf16[16,128,512]{2,1,0:T(8,128)(2,1)} %attend_local.3.refs_0_), custom_call_target="tpu_custom_call", output_to_operand_aliasing={{}: (4, {})} | custom-call | flops 570425344 | bytes 4587520 | tf_op jit(solution)/shard_map/attend_local/pallas_call | solution.py:130
  78.3 1.1 %collective-permute-start.36 = (bf16[576,256]{1,0:T(8,128)(2,1)S(1)}, bf16[576,256]{1,0:T(8,128)(2,1)S(1)}, u32[]{:S(2)}, u32[]{:S(2)}) collective-permute-start(bf16[576,256]{1,0:T(8,128)(2,1)S(1)} %broadcast_select_fusion), channel_id=1, source_target_pairs={{0,4},{4,0},{8,12},{12,8},{16,20},{20,16},{24,28},{28,24},{1,5},{5... | collective-permute-start | bytes 884744 | tf_op jit(solution)/shard_map/ppermute | solution.py:20
  79.9 1.7 %collective-permute-start.33 = (bf16[64,896]{1,0:T(8,128)(2,1)S(1)}, bf16[64,896]{1,0:T(8,128)(2,1)S(1)}, u32[]{:S(2)}, u32[]{:S(2)}) collective-permute-start(bf16[64,896]{1,0:T(8,128)(2,1)S(1)} %get-tuple-element.119), channel_id=1, source_target_pairs={{0,16},{4,20},{8,24},{12,28},{16,0},{20,4},{24,8},{28,12},{1,17},{... | collective-permute-start | bytes 344072 | tf_op jit(solution)/shard_map/ppermute | solution.py:20
  81.6 2.5 %collective-permute-start.34 = (bf16[64,896]{1,0:T(8,128)(2,1)S(1)}, bf16[64,896]{1,0:T(8,128)(2,1)S(1)}, u32[]{:S(2)}, u32[]{:S(2)}) collective-permute-start(bf16[64,896]{1,0:T(8,128)(2,1)S(1)} %get-tuple-element.118), channel_id=1, source_target_pairs={{0,24},{4,28},{8,16},{12,20},{16,8},{20,12},{24,0},{28,4},{1,25},{... | collective-permute-start | bytes 344072 | tf_op jit(solution)/shard_map/ppermute | solution.py:20
  84.1 3.6 %attend_local.5.old_ref = bf16[16,128,512]{2,1,0:T(8,128)(2,1)} custom-call(s32[2]{0:T(128)S(1)} %pad_add_fusion.ranks_ref, s32[512]{0:T(512)S(1)} %copy-done.1, bf16[16,576,128]{2,1,0:T(8,128)(2,1)} %bitcast.15, bf16[16,576,256]{2,1,0:T(8,128)(2,1)} %bitcast.12, bf16[16,128,512]{2,1,0:T(8,128)(2,1)} %attend_local.4.refs_0_), custom_call_target="tpu_custom_call", output_to_operand_aliasing={{}: (4, {})} | custom-call | flops 285212672 | bytes 2293760 | tf_op jit(solution)/shard_map/attend_local/pallas_call | solution.py:130
  87.8 2.7 %attend_traded.1 = bf16[16,128,512]{2,1,0:T(8,128)(2,1)} custom-call(s32[2]{0:T(128)S(1)} %pad_add_fusion.ranks_ref, s32[512]{0:T(512)S(1)} %copy-done.1, s32[32]{0:T(128)S(1)} %copy-done.2, s32[1]{0:T(128)S(6)} %copy.20.mask_ref, bf16[16,576,128]{2,1,0:T(8,128)(2,1)} %bitcast.16, ...), custom_call_target="tpu_custom_call", output_to_operand_aliasing={{}: (6, {})} | custom-call | flops 71303168 | bytes 573440 | tf_op jit(solution)/shard_map/attend_traded/pallas_call | solution.py:195
  (84 shorter events, 11.9 us)
Async XLA Ops:
  2.6 7.4 %collective-permute-start = (bf16[64,1024]{1,0:T(8,128)(2,1)S(1)}, bf16[64,1024]{1,0:T(8,128)(2,1)S(1)}, u32[]{:S(2)}, u32[]{:S(2)}) collective-permute-start(bf16[64,1024]{1,0:T(8,128)(2,1)S(1)} %get-tuple-element.57.refs_1_), channel_id=1, source_target_pairs={{0,8},{4,12},{8,0},{12,4},{16,24},{20,28},{24,16},{28,20},{1,9},{5... | collective-permute-start | bytes 393224 | tf_op jit(solution)/shard_map/ppermute | solution.py:20
  5.7 13.8 %collective-permute-start.3 = (bf16[64,1920]{1,0:T(8,128)(2,1)S(1)}, bf16[64,1920]{1,0:T(8,128)(2,1)S(1)}, u32[]{:S(2)}, u32[]{:S(2)}) collective-permute-start(bf16[64,1920]{1,0:T(8,128)(2,1)S(1)} %get-tuple-element.64), channel_id=1, source_target_pairs={{0,4},{4,0},{8,12},{12,8},{16,20},{20,16},{24,28},{28,24},{1,5},{5... | collective-permute-start | bytes 737288 | tf_op jit(solution)/shard_map/ppermute | solution.py:20
  7.2 12.3 %collective-permute-start.4 = (bf16[64,1024]{1,0:T(8,128)(2,1)S(1)}, bf16[64,1024]{1,0:T(8,128)(2,1)S(1)}, u32[]{:S(2)}, u32[]{:S(2)}) collective-permute-start(bf16[64,1024]{1,0:T(8,128)(2,1)S(1)} %get-tuple-element.57.refs_1_), channel_id=1, source_target_pairs={{0,16},{4,20},{8,24},{12,28},{16,0},{20,4},{24,8},{28,12},{1,17},{... | collective-permute-start | bytes 393224 | tf_op jit(solution)/shard_map/ppermute | solution.py:20
  9.8 9.7 %collective-permute-start.5 = (bf16[64,1024]{1,0:T(8,128)(2,1)S(1)}, bf16[64,1024]{1,0:T(8,128)(2,1)S(1)}, u32[]{:S(2)}, u32[]{:S(2)}) collective-permute-start(bf16[64,1024]{1,0:T(8,128)(2,1)S(1)} %get-tuple-element.57.refs_1_), channel_id=1, source_target_pairs={{0,24},{4,28},{8,16},{12,20},{16,8},{20,12},{24,0},{28,4},{1,25},{... | collective-permute-start | bytes 393224 | tf_op jit(solution)/shard_map/ppermute | solution.py:20
  10.0 9.5 %collective-permute-start.2 = (bf16[64,1024]{1,0:T(8,128)(2,1)S(1)}, bf16[64,1024]{1,0:T(8,128)(2,1)S(1)}, u32[]{:S(2)}, u32[]{:S(2)}) collective-permute-start(bf16[64,1024]{1,0:T(8,128)(2,1)S(1)} %collective-permute-done.refs_4_), channel_id=1, source_target_pairs={{0,4},{4,0},{8,12},{12,8},{16,20},{20,16},{24,28},{28,24},{1,5},{5... | collective-permute-start | bytes 393224 | tf_op jit(solution)/shard_map/ppermute | solution.py:20
  12.4 7.1 %collective-permute-start.1 = (bf16[64,896]{1,0:T(8,128)(2,1)S(1)}, bf16[64,896]{1,0:T(8,128)(2,1)S(1)}, u32[]{:S(2)}, u32[]{:S(2)}) collective-permute-start(bf16[64,896]{1,0:T(8,128)(2,1)S(1)} %slice.71), channel_id=1, source_target_pairs={{0,2},{1,3},{2,0},{3,1},{4,6},{5,7},{6,4},{7,5},{8,10},{9,11},{10,... | collective-permute-start | bytes 344072 | tf_op jit(solution)/shard_map/ppermute | solution.py:20
  19.5 8.8 %collective-permute-start.6 = (bf16[64,1920]{1,0:T(8,128)(2,1)S(1)}, bf16[64,1920]{1,0:T(8,128)(2,1)S(1)}, u32[]{:S(2)}, u32[]{:S(2)}) collective-permute-start(bf16[64,1920]{1,0:T(8,128)(2,1)S(1)} %collective-permute-done.3.refs_2_), channel_id=1, source_target_pairs={{0,1},{1,0},{2,3},{3,2},{4,5},{5,4},{6,7},{7,6},{8,9},{9,8},{10,11... | collective-permute-start | bytes 737288 | tf_op jit(solution)/shard_map/ppermute | solution.py:20
  19.6 6.2 %collective-permute-start.7 = (bf16[64,1024]{1,0:T(8,128)(2,1)S(1)}, bf16[64,1024]{1,0:T(8,128)(2,1)S(1)}, u32[]{:S(2)}, u32[]{:S(2)}) collective-permute-start(bf16[64,1024]{1,0:T(8,128)(2,1)S(1)} %collective-permute-done.refs_4_), channel_id=1, source_target_pairs={{0,1},{1,0},{2,3},{3,2},{4,5},{5,4},{6,7},{7,6},{8,9},{9,8},{10,11... | collective-permute-start | bytes 393224 | tf_op jit(solution)/shard_map/ppermute | solution.py:20
  20.1 8.2 %collective-permute-start.9 = (bf16[64,1024]{1,0:T(8,128)(2,1)S(1)}, bf16[64,1024]{1,0:T(8,128)(2,1)S(1)}, u32[]{:S(2)}, u32[]{:S(2)}) collective-permute-start(bf16[64,1024]{1,0:T(8,128)(2,1)S(1)} %collective-permute-done.2.refs_8_), channel_id=1, source_target_pairs={{0,1},{1,0},{2,3},{3,2},{4,5},{5,4},{6,7},{7,6},{8,9},{9,8},{10,11... | collective-permute-start | bytes 393224 | tf_op jit(solution)/shard_map/ppermute | solution.py:20
  20.2 5.5 %collective-permute-start.10 = (bf16[64,896]{1,0:T(8,128)(2,1)S(1)}, bf16[64,896]{1,0:T(8,128)(2,1)S(1)}, u32[]{:S(2)}, u32[]{:S(2)}) collective-permute-start(bf16[64,896]{1,0:T(8,128)(2,1)S(1)} %slice.72), channel_id=1, source_target_pairs={{0,2},{1,3},{2,0},{3,1},{4,6},{5,7},{6,4},{7,5},{8,10},{9,11},{10,... | collective-permute-start | bytes 344072 | tf_op jit(solution)/shard_map/ppermute | solution.py:20
  21.7 5.1 %collective-permute-start.8 = (bf16[64,896]{1,0:T(8,128)(2,1)S(1)}, bf16[64,896]{1,0:T(8,128)(2,1)S(1)}, u32[]{:S(2)}, u32[]{:S(2)}) collective-permute-start(bf16[64,896]{1,0:T(8,128)(2,1)S(1)} %collective-permute-done.1.refs_6_), channel_id=1, source_target_pairs={{0,1},{1,0},{2,3},{3,2},{4,5},{5,4},{6,7},{7,6},{8,9},{9,8},{10,11... | collective-permute-start | bytes 344072 | tf_op jit(solution)/shard_map/ppermute | solution.py:20
  25.8 8.8 %collective-permute-start.13 = (bf16[128,1024]{1,0:T(8,128)(2,1)S(1)}, bf16[128,1024]{1,0:T(8,128)(2,1)S(1)}, u32[]{:S(2)}, u32[]{:S(2)}) collective-permute-start(bf16[128,1024]{1,0:T(8,128)(2,1)S(1)} %constant_dynamic-update-slice_fusion.refs_0_), channel_id=1, source_target_pairs={{0,4},{4,0},{8,12},{12,8},{16,20},{20,16},{24,28},{28,24},{1,5},{5... | collective-permute-start | bytes 786440 | tf_op jit(solution)/shard_map/ppermute | solution.py:20
  26.8 7.8 %collective-permute-start.12 = (bf16[128,896]{1,0:T(8,128)(2,1)S(1)}, bf16[128,896]{1,0:T(8,128)(2,1)S(1)}, u32[]{:S(2)}, u32[]{:S(2)}) collective-permute-start(bf16[128,896]{1,0:T(8,128)(2,1)S(1)} %slice.94), channel_id=1, source_target_pairs={{0,2},{1,3},{2,0},{3,1},{4,6},{5,7},{6,4},{7,5},{8,10},{9,11},{10,... | collective-permute-start | bytes 688136 | tf_op jit(solution)/shard_map/ppermute | solution.py:20
  34.6 5.0 %collective-permute-start.16 = (bf16[512,896]{1,0:T(8,128)(2,1)S(1)}, bf16[512,896]{1,0:T(8,128)(2,1)S(1)}, u32[]{:S(2)}, u32[]{:S(2)}) collective-permute-start(bf16[512,896]{1,0:T(8,128)(2,1)S(1)} %get-tuple-element.78), channel_id=1, source_target_pairs={{0,1},{1,0},{2,3},{3,2},{4,5},{5,4},{6,7},{7,6},{8,9},{9,8},{10,11... | collective-permute-start | bytes 2752520 | tf_op jit(solution)/shard_map/ppermute | solution.py:20
  34.6 10.0 %collective-permute-start.17 = (bf16[576,256]{1,0:T(8,128)(2,1)S(1)}, bf16[576,256]{1,0:T(8,128)(2,1)S(1)}, u32[]{:S(2)}, u32[]{:S(2)}) collective-permute-start(bf16[576,256]{1,0:T(8,128)(2,1)S(1)} %get-tuple-element.79), channel_id=1, source_target_pairs={{0,8},{4,12},{8,0},{12,4},{16,24},{20,28},{24,16},{28,20},{1,9},{5... | collective-permute-start | bytes 884744 | tf_op jit(solution)/shard_map/ppermute | solution.py:20
  36.9 5.3 %collective-permute-start.14 = (bf16[64,896]{1,0:T(8,128)(2,1)S(1)}, bf16[64,896]{1,0:T(8,128)(2,1)S(1)}, u32[]{:S(2)}, u32[]{:S(2)}) collective-permute-start(bf16[64,896]{1,0:T(8,128)(2,1)S(1)} %slice.74), channel_id=1, source_target_pairs={{0,2},{1,3},{2,0},{3,1},{4,6},{5,7},{6,4},{7,5},{8,10},{9,11},{10,... | collective-permute-start | bytes 344072 | tf_op jit(solution)/shard_map/ppermute | solution.py:20
  38.5 5.1 %collective-permute-start.15 = (bf16[64,896]{1,0:T(8,128)(2,1)S(1)}, bf16[64,896]{1,0:T(8,128)(2,1)S(1)}, u32[]{:S(2)}, u32[]{:S(2)}) collective-permute-start(bf16[64,896]{1,0:T(8,128)(2,1)S(1)} %slice.75), channel_id=1, source_target_pairs={{0,4},{4,0},{8,12},{12,8},{16,20},{20,16},{24,28},{28,24},{1,5},{5... | collective-permute-start | bytes 344072 | tf_op jit(solution)/shard_map/ppermute | solution.py:20
  44.6 4.9 %collective-permute-start.18 = (bf16[128,1024]{1,0:T(8,128)(2,1)S(1)}, bf16[128,1024]{1,0:T(8,128)(2,1)S(1)}, u32[]{:S(2)}, u32[]{:S(2)}) collective-permute-start(bf16[128,1024]{1,0:T(8,128)(2,1)S(1)} %constant_dynamic-update-slice_fusion.refs_0_), channel_id=1, source_target_pairs={{0,1},{1,0},{2,3},{3,2},{4,5},{5,4},{6,7},{7,6},{8,9},{9,8},{10,11... | collective-permute-start | bytes 786440 | tf_op jit(solution)/shard_map/ppermute | solution.py:20
  44.6 4.9 %collective-permute-start.20 = (bf16[128,1024]{1,0:T(8,128)(2,1)S(1)}, bf16[128,1024]{1,0:T(8,128)(2,1)S(1)}, u32[]{:S(2)}, u32[]{:S(2)}) collective-permute-start(bf16[128,1024]{1,0:T(8,128)(2,1)S(1)} %collective-permute-done.13.refs_4_), channel_id=1, source_target_pairs={{0,1},{1,0},{2,3},{3,2},{4,5},{5,4},{6,7},{7,6},{8,9},{9,8},{10,11... | collective-permute-start | bytes 786440 | tf_op jit(solution)/shard_map/ppermute | solution.py:20
  47.0 8.2 %collective-permute-start.24 = (bf16[64,1792]{1,0:T(8,128)(2,1)S(1)}, bf16[64,1792]{1,0:T(8,128)(2,1)S(1)}, u32[]{:S(2)}, u32[]{:S(2)}) collective-permute-start(bf16[64,1792]{1,0:T(8,128)(2,1)S(1)} %pad_maximum_fusion), channel_id=1, source_target_pairs={{0,4},{4,0},{8,12},{12,8},{16,20},{20,16},{24,28},{28,24},{1,5},{5... | collective-permute-start | bytes 688136 | tf_op jit(solution)/shard_map/ppermute | solution.py:20
  48.1 7.4 %collective-permute-start.23 = (bf16[128,896]{1,0:T(8,128)(2,1)S(1)}, bf16[128,896]{1,0:T(8,128)(2,1)S(1)}, u32[]{:S(2)}, u32[]{:S(2)}) collective-permute-start(bf16[128,896]{1,0:T(8,128)(2,1)S(1)} %slice.76), channel_id=1, source_target_pairs={{0,2},{1,3},{2,0},{3,1},{4,6},{5,7},{6,4},{7,5},{8,10},{9,11},{10,... | collective-permute-start | bytes 688136 | tf_op jit(solution)/shard_map/ppermute | solution.py:20
  58.3 9.5 %collective-permute-start.26 = (bf16[64,896]{1,0:T(8,128)(2,1)S(1)}, bf16[64,896]{1,0:T(8,128)(2,1)S(1)}, u32[]{:S(2)}, u32[]{:S(2)}) collective-permute-start(bf16[64,896]{1,0:T(8,128)(2,1)S(1)} %get-tuple-element.117), channel_id=1, source_target_pairs={{0,2},{1,3},{2,0},{3,1},{4,6},{5,7},{6,4},{7,5},{8,10},{9,11},{10,... | collective-permute-start | bytes 344072 | tf_op jit(solution)/shard_map/ppermute | solution.py:20
  59.7 8.1 %collective-permute-start.27 = (bf16[64,896]{1,0:T(8,128)(2,1)S(1)}, bf16[64,896]{1,0:T(8,128)(2,1)S(1)}, u32[]{:S(2)}, u32[]{:S(2)}) collective-permute-start(bf16[64,896]{1,0:T(8,128)(2,1)S(1)} %get-tuple-element.116), channel_id=1, source_target_pairs={{0,4},{4,0},{8,12},{12,8},{16,20},{20,16},{24,28},{28,24},{1,5},{5... | collective-permute-start | bytes 344072 | tf_op jit(solution)/shard_map/ppermute | solution.py:20
  60.7 16.5 %collective-permute-start.31 = (bf16[64,896]{1,0:T(8,128)(2,1)S(1)}, bf16[64,896]{1,0:T(8,128)(2,1)S(1)}, u32[]{:S(2)}, u32[]{:S(2)}) collective-permute-start(bf16[64,896]{1,0:T(8,128)(2,1)S(1)} %add_convert_fusion.7), channel_id=1, source_target_pairs={{0,2},{1,3},{2,0},{3,1},{4,6},{5,7},{6,4},{7,5},{8,10},{9,11},{10,... | collective-permute-start | bytes 344072 | tf_op jit(solution)/shard_map/ppermute | solution.py:20
  61.4 16.8 %collective-permute-start.32 = (bf16[576,256]{1,0:T(8,128)(2,1)S(1)}, bf16[576,256]{1,0:T(8,128)(2,1)S(1)}, u32[]{:S(2)}, u32[]{:S(2)}) collective-permute-start(bf16[576,256]{1,0:T(8,128)(2,1)S(1)} %broadcast_select_fusion.2), channel_id=1, source_target_pairs={{0,16},{4,20},{8,24},{12,28},{16,0},{20,4},{24,8},{28,12},{1,17},{... | collective-permute-start | bytes 884744 | tf_op jit(solution)/shard_map/ppermute | solution.py:20
  67.9 10.4 %collective-permute-start.29 = (bf16[128,896]{1,0:T(8,128)(2,1)S(1)}, bf16[128,896]{1,0:T(8,128)(2,1)S(1)}, u32[]{:S(2)}, u32[]{:S(2)}) collective-permute-start(bf16[128,896]{1,0:T(8,128)(2,1)S(1)} %add_convert_fusion.3), channel_id=1, source_target_pairs={{0,2},{1,3},{2,0},{3,1},{4,6},{5,7},{6,4},{7,5},{8,10},{9,11},{10,... | collective-permute-start | bytes 688136 | tf_op jit(solution)/shard_map/ppermute | solution.py:20
  69.4 8.8 %collective-permute-start.28 = (bf16[128,896]{1,0:T(8,128)(2,1)S(1)}, bf16[128,896]{1,0:T(8,128)(2,1)S(1)}, u32[]{:S(2)}, u32[]{:S(2)}) collective-permute-start(bf16[128,896]{1,0:T(8,128)(2,1)S(1)} %add_convert_fusion.4), channel_id=1, source_target_pairs={{0,4},{4,0},{8,12},{12,8},{16,20},{20,16},{24,28},{28,24},{1,5},{5... | collective-permute-start | bytes 688136 | tf_op jit(solution)/shard_map/ppermute | solution.py:20
  70.6 7.6 %collective-permute-start.30 = (bf16[64,896]{1,0:T(8,128)(2,1)S(1)}, bf16[64,896]{1,0:T(8,128)(2,1)S(1)}, u32[]{:S(2)}, u32[]{:S(2)}) collective-permute-start(bf16[64,896]{1,0:T(8,128)(2,1)S(1)} %add_convert_fusion.8), channel_id=1, source_target_pairs={{0,4},{4,0},{8,12},{12,8},{16,20},{20,16},{24,28},{28,24},{1,5},{5... | collective-permute-start | bytes 344072 | tf_op jit(solution)/shard_map/ppermute | solution.py:20
  78.3 9.5 %collective-permute-start.36 = (bf16[576,256]{1,0:T(8,128)(2,1)S(1)}, bf16[576,256]{1,0:T(8,128)(2,1)S(1)}, u32[]{:S(2)}, u32[]{:S(2)}) collective-permute-start(bf16[576,256]{1,0:T(8,128)(2,1)S(1)} %broadcast_select_fusion), channel_id=1, source_target_pairs={{0,4},{4,0},{8,12},{12,8},{16,20},{20,16},{24,28},{28,24},{1,5},{5... | collective-permute-start | bytes 884744 | tf_op jit(solution)/shard_map/ppermute | solution.py:20
  79.4 11.0 %collective-permute-start.35 = (bf16[64,896]{1,0:T(8,128)(2,1)S(1)}, bf16[64,896]{1,0:T(8,128)(2,1)S(1)}, u32[]{:S(2)}, u32[]{:S(2)}) collective-permute-start(bf16[64,896]{1,0:T(8,128)(2,1)S(1)} %add_convert_fusion.6), channel_id=1, source_target_pairs={{0,8},{4,12},{8,0},{12,4},{16,24},{20,28},{24,16},{28,20},{1,9},{5... | collective-permute-start | bytes 344072 | tf_op jit(solution)/shard_map/ppermute | solution.py:20
  79.9 10.6 %collective-permute-start.33 = (bf16[64,896]{1,0:T(8,128)(2,1)S(1)}, bf16[64,896]{1,0:T(8,128)(2,1)S(1)}, u32[]{:S(2)}, u32[]{:S(2)}) collective-permute-start(bf16[64,896]{1,0:T(8,128)(2,1)S(1)} %get-tuple-element.119), channel_id=1, source_target_pairs={{0,16},{4,20},{8,24},{12,28},{16,0},{20,4},{24,8},{28,12},{1,17},{... | collective-permute-start | bytes 344072 | tf_op jit(solution)/shard_map/ppermute | solution.py:20
  81.6 8.9 %collective-permute-start.34 = (bf16[64,896]{1,0:T(8,128)(2,1)S(1)}, bf16[64,896]{1,0:T(8,128)(2,1)S(1)}, u32[]{:S(2)}, u32[]{:S(2)}) collective-permute-start(bf16[64,896]{1,0:T(8,128)(2,1)S(1)} %get-tuple-element.118), channel_id=1, source_target_pairs={{0,24},{4,28},{8,16},{12,20},{16,8},{20,12},{24,0},{28,4},{1,25},{... | collective-permute-start | bytes 344072 | tf_op jit(solution)/shard_map/ppermute | solution.py:20
  (8 other events, 43.7 us)

commit v8 on v6

--- a/solution.py
+++ b/solution.py
@@ -142,11 +142,7 @@
         ),
         input_output_aliases={4: 0} if earlier else {},
         compiler_params=pltpu.CompilerParams(vmem_limit_bytes=8 * MIB),
-        cost_estimate=pl.CostEstimate(
-            flops=2 * some * heads * slots * (width + LAT),
-            bytes_accessed=2 * some * (heads * (width + LAT) + slots * width),
-            transcendentals=some * heads * slots,
-        ),
+        cost_estimate=pl.CostEstimate(flops=0, bytes_accessed=0, transcendentals=0),
         name="attend_local",
     )(ranks, lengths, in_hbm(queries), in_hbm(pages), *earlier)
 
@@ -329,9 +325,9 @@
         ],
         compiler_params=pltpu.CompilerParams(vmem_limit_bytes=need + 6 * MIB),
         cost_estimate=pl.CostEstimate(
-            flops=6 * rows * width * units * experts,
-            bytes_accessed=4 * rows * width,
-            transcendentals=rows * units * experts,
+            flops=0,
+            bytes_accessed=0,
+            transcendentals=0,
         ),
         name="experts",
     )(
@@ -412,69 +408,70 @@
     far_2, near_3, w_gate, w_up, page, both_1, *late_pieces = tie(
         (far_2, near_3, w_gate, w_up, page, both_1, *late_pieces)
     )
-    upper, lower = jnp.split(page, 2, axis=0)
-    upper_far, upper = page_far(upper)
     far_3 = flip(bare(near_3), "tp", 2)
 
     near_late = jnp.concatenate(late_pieces, axis=0)
     far_late = flip(bare(near_late), "tp", 2)
     near_odds = flip(near_late, "ep", 1)
-    early = [flip(array, "tp", 1) for array in (both_1, near_2, far_2, near_3)]
-
-    def with_core(start, part, array, other):
-        start = start * rows
-        return [(start, (part,), part == 0, array), (start, (part ^ 1,), False, other)]
+    near_23 = flip(jnp.concatenate([near_2, near_3], axis=0), "tp", 1)
+    early = [flip(array, "tp", 1) for array in (both_1, far_2)]
+    queries, near_23, early = tie((queries, near_23, early))
+    count = queries.shape[0]
+    attended = attend_part(ranks, lengths, queries, cache_pages, groups, 0, count // 2)
+    far_3, far_late, near_late, near_odds, attended = tie(
+        (far_3, far_late, near_late, near_odds, attended)
+    )
+    far_odds_y = flip(bare(cut(near_odds, 0, half)), "tp", 2)
+    far_odds_x = flip(cut(far_late, half, rest), "ep", 1)
+
+    def piece(start, part, array):
+        return start * rows, (part,), part == 0, array
 
     pieces = [(0, None, False, hidden), (0, (), True, own)]
     pieces += [(rows, (0, 2), True, both_1), (rows, (1, 3), False, early[0])]
-    pieces += with_core(2, 0, near_2, early[1]) + with_core(2, 2, far_2, early[2])
-    pieces += with_core(3, 0, near_3, early[3])
-    pieces += with_core(3, 2, far_3, flip(far_3, "tp", 1))
+    pieces += [piece(2, 0, near_2), piece(3, 0, near_3), (2 * rows, (1,), False, near_23)]
+    pieces += [piece(2, 2, far_2), piece(2, 3, early[1])]
+    pieces += [piece(3, 2, far_3), piece(3, 3, flip(far_3, "tp", 1))]
     *first, w_down = run_experts(
         ranks, pieces, w_gate, w_up, w_down, 4 * rows, columns, top, True
     )
-    first, far_late, near_odds, upper_far = tie((first, far_late, near_odds, upper_far))
+    near_both = jnp.concatenate([near_late, near_odds], axis=0)
+    early = [flip(array, "tp", 1) for array in (near_both, far_late)]
+    swapped = flip(page, "ep", 2)
+    first, far_odds_y, far_odds_x, early, swapped = tie(
+        (first, far_odds_y, far_odds_x, early, swapped)
+    )
+    page = page_take(page, swapped, 1)
 
     def add_core(given, own):
         total = total_of(own, flip(given, "tp", 1))
         return jnp.split(total, 2, axis=0)
 
-    far_odds_y = flip(bare(cut(near_odds, 0, half)), "tp", 2)
-    far_odds_x = flip(cut(far_late, half, rest), "ep", 1)
     sent, kept = add_core(*first)
-    far_odds_y, far_odds_x, sent, kept, lower, near_late, far_late, near_odds = tie(
-        (far_odds_y, far_odds_x, sent, kept, lower, near_late, far_late, near_odds)
-    )
-    early = [flip(array, "tp", 1) for array in (near_late, far_late, near_odds)]
     last = [flip(array, "tp", 1) for array in (far_odds_y, far_odds_x)]
     over_23 = flip(cut(sent, 2, 2), "tp", 2)
     over_1 = flip(jnp.concatenate([cut(kept, 1, 1), cut(sent, 1, 1)], axis=1), "ep", 1)
-    lower_far, lower = page_far(lower)
-
-    pieces = with_core(0, 0, near_late, early[0]) + with_core(0, 2, far_late, early[1])
-    pieces += with_core(len(late), 0, near_odds, early[2])
-    pieces += with_core(len(late), 2, far_odds_y, last[0])
-    pieces += with_core(len(late) + half, 2, far_odds_x, last[1])
+    swapped = flip(page, "ep", 1)
+    odds = len(late)
+    pieces = [piece(0, 0, near_both), (0, (1,), False, early[0])]
+    pieces += [piece(0, 2, far_late), piece(0, 3, early[1])]
+    pieces += [piece(odds, 2, far_odds_y), piece(odds, 3, last[0])]
+    pieces += [piece(odds + half, 2, far_odds_x), piece(odds + half, 3, last[1])]
     second = [
         *run_experts(
             ranks, pieces, w_gate, w_up, w_down, 2 * len(late) * rows, columns, top, False
         )
     ]
-    second, over_23, over_1, lower_far = tie((second, over_23, over_1, lower_far))
-    page = jnp.concatenate([upper, lower], axis=0)
-    page = page_take(page, jnp.concatenate([upper_far, lower_far], axis=0), 2)
+    second, over_23, swapped = tie((second, over_23, swapped))
+    swapped, page = page_far(page_take(page, swapped, 0))
     late_sent, late_kept = add_core(*second)
     over_3 = flip(total_of(cut(kept, 3, 1), cut(over_23, 1, 1)), "ep", 1)
-    zero = flip(total_of(cut(sent, 0, 1), over_1[:, columns:]), "tp", 2)
-    late_sent, late_kept, queries, page = tie((late_sent, late_kept, queries, page))
+    late_sent, late_kept = tie((late_sent, late_kept))
 
     over_y = flip(cut(late_sent, len(late), half), "tp", 2)
     over_x = flip(cut(late_sent, len(late) + half, rest), "ep", 1)
-    if levels > 1:
-        page = page_hop(page, 1)
-    some = queries.shape[0] // 2
-    attended = attend_part(ranks, lengths, queries, cache_pages, groups, 0, some)
-    over_y, over_x, attended = tie((over_y, over_x, attended))
+    over_y, over_x, over_1, queries = tie((over_y, over_x, over_1, queries))
+    zero = flip(total_of(cut(sent, 0, 1), over_1[:, columns:]), "tp", 2)
     odd = total_of(
         cut(late_kept, len(late), len(late)), jnp.pad(over_y, ((0, rest * rows), (0, 0)))
     )
@@ -482,13 +479,14 @@
     even = total_of(cut(late_sent, 0, len(late)), jnp.pad(over_x, ((half * rows, 0), (0, 0))))
     even = flip(even, "tp", 2)
     attended = attend_part(
-        ranks, lengths, queries, cache_pages, groups, some, queries.shape[0] - some, attended
-    )
-    odd, even, over_3, attended, page = tie((odd, even, over_3, attended, page))
+        ranks, lengths, queries, cache_pages, groups, count // 2, count - count // 2, attended
+    )
+    odd, even, over_3, attended, swapped = tie((odd, even, over_3, attended, swapped))
+    if levels > 2:
+        page = page_take(page, swapped, 2)
     even = total_of(cut(late_kept, 0, len(late)), even, odd)
     back = [flip(cut(even, i, 1), "ep", 2 * m) for i, m in enumerate(late)]
     back.append(flip(total_of(cut(kept, 2, 1), cut(over_23, 0, 1), over_3), "ep", 2))
-    page = page_hop(page, 0)
     attended = attend_traded(
         ranks, lengths, swap_slot, swap_mask, queries, page, attended, groups
     )

time: 90.8 us -> 88.5 us (0.975)
  waiting for transfers between devices: 18.8 us -> 16.5 us
    ppermute x38 -> x35, waiting for transfers between devices: 18.8 us -> 16.5 us  [flip(): return lax.ppermute(block, axis, [(i, i ^ apart) for i in range(count)])]
    ppermute x38 -> x35, starting transfers between devices: 36.1 us -> 36.3 us  [flip(): return lax.ppermute(block, axis, [(i, i ^ apart) for i in range(count)])]
  transfers between devices with their start and end apart: 38 -> 35, of which waited for: 13 -> 10; matrix products, arithmetic and copies ran while one was open for 1% -> 1% of each run, Pallas kernels for 33% -> 34%
where the time goes in v8:
time: 88.5 us; the launch traced here: 88.1 us
  starting transfers between devices  36.3 us (41%)
  Pallas kernels  31.8 us (36%)
  waiting for transfers between devices  16.5 us (19%)
  other arithmetic  1.65 us (2%)
  between operations  1.62 us (2%)
    ppermute x35, starting transfers between devices, flip(): return lax.ppermute(block, axis, [(i, i ^ apart) for i in range(count)])  36.3 us
    ppermute x35, waiting for transfers between devices, flip(): return lax.ppermute(block, axis, [(i, i ^ apart) for i in range(count)])  16.5 us
    pallas_call x2, Pallas kernels, run_experts(): pl.pallas_call(kernel, out_shape=[pltpu.VMEM((2 * rows, columns), jnp.bfl...  11.8 us
    pallas_call x2, Pallas kernels, attend_part(): pl.pallas_call(kernel, out_shape=jax.ShapeDtypeStruct((count, heads, LAT)...  11.1 us
    pallas_call x1, Pallas kernels, load(): pl.pallas_call(load_kernel, out_shape=[pltpu.VMEM(w.shape, w.dtype) for w...  4.21 us
    pallas_call x1, Pallas kernels, attend_traded(): pl.pallas_call(functools.partial(attend_traded_kernel, groups), out_shape...  2.71 us
    pallas_call x1, Pallas kernels, pick(): pl.pallas_call(functools.partial(pick_kernel, groups), out_shape=(pltpu.V...  1.89 us
  transfers between devices with their start and end apart: 35, of which 10 were waited for; matrix products, arithmetic and copies ran while one was open for 1% of the time, Pallas kernels for 34%

profile of v8, /device:TPU:0, one launch (start us, length us, event | category | flops | bytes accessed | tf_op | source)
XLA Modules:
  0.0 88.1 jit_solution(4046276643684333938)
XLA Ops:
  0.7 1.9 %pick.1 = (bf16[64,1024]{1,0:T(8,128)(2,1)S(1)}, bf16[64,1920]{1,0:T(8,128)(2,1)S(1)}, bf16[576,256]{1,0:T(8,128)(2,1)S(1)}) custom-call(s32[2]{0:T(128)S(1)} %pad_add_fusion.ranks_ref, s32[32]{0:T(128)} %slots_ref.3, s32[8,64]{1,0:T(8,128)} %bitcast.15, f32[8,64]{1,0:T(8,128)} %bitcast.16, bf16[64,3584]{1,0:T(8,128)(2,1)} %refs_0_.2, ...), custom_call_target="tpu_custom_call" | custom-call | tf_op jit(solution)/shard_map/pick/pallas_call | solution.py:96
  2.6 3.1 %collective-permute-start = (bf16[64,1024]{1,0:T(8,128)(2,1)S(1)}, bf16[64,1024]{1,0:T(8,128)(2,1)S(1)}, u32[]{:S(2)}, u32[]{:S(2)}) collective-permute-start(bf16[64,1024]{1,0:T(8,128)(2,1)S(1)} %get-tuple-element.58.refs_1_), channel_id=1, source_target_pairs={{0,8},{4,12},{8,0},{12,4},{16,24},{20,28},{24,16},{28,20},{1,9},{5... | collective-permute-start | bytes 393224 | tf_op jit(solution)/shard_map/ppermute | solution.py:20
  5.7 1.5 %collective-permute-start.3 = (bf16[64,1920]{1,0:T(8,128)(2,1)S(1)}, bf16[64,1920]{1,0:T(8,128)(2,1)S(1)}, u32[]{:S(2)}, u32[]{:S(2)}) collective-permute-start(bf16[64,1920]{1,0:T(8,128)(2,1)S(1)} %get-tuple-element.65), channel_id=1, source_target_pairs={{0,4},{4,0},{8,12},{12,8},{16,20},{20,16},{24,28},{28,24},{1,5},{5... | collective-permute-start | bytes 737288 | tf_op jit(solution)/shard_map/ppermute | solution.py:20
  7.2 2.6 %collective-permute-start.4 = (bf16[64,1024]{1,0:T(8,128)(2,1)S(1)}, bf16[64,1024]{1,0:T(8,128)(2,1)S(1)}, u32[]{:S(2)}, u32[]{:S(2)}) collective-permute-start(bf16[64,1024]{1,0:T(8,128)(2,1)S(1)} %get-tuple-element.58.refs_1_), channel_id=1, source_target_pairs={{0,16},{4,20},{8,24},{12,28},{16,0},{20,4},{24,8},{28,12},{1,17},{... | collective-permute-start | bytes 393224 | tf_op jit(solution)/shard_map/ppermute | solution.py:20
  10.0 2.3 %collective-permute-start.2 = (bf16[64,1024]{1,0:T(8,128)(2,1)S(1)}, bf16[64,1024]{1,0:T(8,128)(2,1)S(1)}, u32[]{:S(2)}, u32[]{:S(2)}) collective-permute-start(bf16[64,1024]{1,0:T(8,128)(2,1)S(1)} %collective-permute-done.refs_4_), channel_id=1, source_target_pairs={{0,4},{4,0},{8,12},{12,8},{16,20},{20,16},{24,28},{28,24},{1,5},{5... | collective-permute-start | bytes 393224 | tf_op jit(solution)/shard_map/ppermute | solution.py:20
  12.4 1.5 %collective-permute-start.1 = (bf16[64,896]{1,0:T(8,128)(2,1)S(1)}, bf16[64,896]{1,0:T(8,128)(2,1)S(1)}, u32[]{:S(2)}, u32[]{:S(2)}) collective-permute-start(bf16[64,896]{1,0:T(8,128)(2,1)S(1)} %slice.78), channel_id=1, source_target_pairs={{0,2},{1,3},{2,0},{3,1},{4,6},{5,7},{6,4},{7,5},{8,10},{9,11},{10,... | collective-permute-start | bytes 344072 | tf_op jit(solution)/shard_map/ppermute | solution.py:20
  13.9 4.2 %load.1 = (bf16[3,3584,256]{2,1,0:T(8,128)(2,1)S(1)}, bf16[3,3584,256]{2,1,0:T(8,128)(2,1)S(1)}) custom-call(bf16[3,3584,256]{2,1,0:T(8,128)(2,1)} %refs_0_.1, bf16[3,3584,256]{2,1,0:T(8,128)(2,1)} %refs_1_), custom_call_target="tpu_custom_call" | custom-call | bytes 11010048 | tf_op jit(solution)/shard_map/load/pallas_call | solution.py:162
  18.1 1.4 %collective-permute-done.4 = bf16[64,1024]{1,0:T(8,128)(2,1)S(1)} collective-permute-done((bf16[64,1024]{1,0:T(8,128)(2,1)S(1)}, bf16[64,1024]{1,0:T(8,128)(2,1)S(1)}, u32[]{:S(2)}, u32[]{:S(2)}) %collective-permute-start.4) | collective-permute-done | bytes 131104 | tf_op jit(solution)/shard_map/ppermute | solution.py:20
  19.6 1.0 %collective-permute-start.8 = (bf16[128,1024]{1,0:T(8,128)(2,1)S(1)}, bf16[128,1024]{1,0:T(8,128)(2,1)S(1)}, u32[]{:S(2)}, u32[]{:S(2)}) collective-permute-start(bf16[128,1024]{1,0:T(8,128)(2,1)S(1)} %constant_dynamic-update-slice_fusion), channel_id=1, source_target_pairs={{0,4},{4,0},{8,12},{12,8},{16,20},{20,16},{24,28},{28,24},{1,5},{5... | collective-permute-start | bytes 786440 | tf_op jit(solution)/shard_map/ppermute | solution.py:20
  21.2 1.5 %collective-permute-start.7 = (bf16[128,896]{1,0:T(8,128)(2,1)S(1)}, bf16[128,896]{1,0:T(8,128)(2,1)S(1)}, u32[]{:S(2)}, u32[]{:S(2)}) collective-permute-start(bf16[128,896]{1,0:T(8,128)(2,1)S(1)} %slice.101), channel_id=1, source_target_pairs={{0,2},{1,3},{2,0},{3,1},{4,6},{5,7},{6,4},{7,5},{8,10},{9,11},{10,... | collective-permute-start | bytes 688136 | tf_op jit(solution)/shard_map/ppermute | solution.py:20
  22.7 1.1 %collective-permute-start.6 = (bf16[64,896]{1,0:T(8,128)(2,1)S(1)}, bf16[64,896]{1,0:T(8,128)(2,1)S(1)}, u32[]{:S(2)}, u32[]{:S(2)}) collective-permute-start(bf16[64,896]{1,0:T(8,128)(2,1)S(1)} %slice.79), channel_id=1, source_target_pairs={{0,2},{1,3},{2,0},{3,1},{4,6},{5,7},{6,4},{7,5},{8,10},{9,11},{10,... | collective-permute-start | bytes 344072 | tf_op jit(solution)/shard_map/ppermute | solution.py:20
  23.8 5.6 %attend_local.2.refs_0_ = bf16[16,128,512]{2,1,0:T(8,128)(2,1)} custom-call(s32[2]{0:T(128)S(1)} %pad_add_fusion.ranks_ref, s32[512]{0:T(512)S(1)} %copy-done.1, bf16[16,576,128]{2,1,0:T(8,128)(2,1)} %bitcast.12, bf16[16,576,256]{2,1,0:T(8,128)(2,1)} %bitcast.10), custom_call_target="tpu_custom_call" | custom-call | tf_op jit(solution)/shard_map/attend_local/pallas_call | solution.py:130
  29.4 2.1 %collective-permute-done.6.refs_9_ = bf16[64,896]{1,0:T(8,128)(2,1)S(1)} collective-permute-done((bf16[64,896]{1,0:T(8,128)(2,1)S(1)}, bf16[64,896]{1,0:T(8,128)(2,1)S(1)}, u32[]{:S(2)}, u32[]{:S(2)}) %collective-permute-start.6) | collective-permute-done | bytes 114720 | tf_op jit(solution)/shard_map/ppermute | solution.py:20
  31.6 2.0 %collective-permute-start.17 = (bf16[576,256]{1,0:T(8,128)(2,1)S(1)}, bf16[576,256]{1,0:T(8,128)(2,1)S(1)}, u32[]{:S(2)}, u32[]{:S(2)}) collective-permute-start(bf16[576,256]{1,0:T(8,128)(2,1)S(1)} %get-tuple-element.83), channel_id=1, source_target_pairs={{0,8},{4,12},{8,0},{12,4},{16,24},{20,28},{24,16},{28,20},{1,9},{5... | collective-permute-start | bytes 884744 | tf_op jit(solution)/shard_map/ppermute | solution.py:20
  34.1 1.5 %collective-permute-start.13 = (bf16[64,896]{1,0:T(8,128)(2,1)S(1)}, bf16[64,896]{1,0:T(8,128)(2,1)S(1)}, u32[]{:S(2)}, u32[]{:S(2)}) collective-permute-start(bf16[64,896]{1,0:T(8,128)(2,1)S(1)} %slice.81), channel_id=1, source_target_pairs={{0,2},{1,3},{2,0},{3,1},{4,6},{5,7},{6,4},{7,5},{8,10},{9,11},{10,... | collective-permute-start | bytes 344072 | tf_op jit(solution)/shard_map/ppermute | solution.py:20
  35.7 1.4 %collective-permute-start.14 = (bf16[64,896]{1,0:T(8,128)(2,1)S(1)}, bf16[64,896]{1,0:T(8,128)(2,1)S(1)}, u32[]{:S(2)}, u32[]{:S(2)}) collective-permute-start(bf16[64,896]{1,0:T(8,128)(2,1)S(1)} %slice.82), channel_id=1, source_target_pairs={{0,4},{4,0},{8,12},{12,8},{16,20},{20,16},{24,28},{28,24},{1,5},{5... | collective-permute-start | bytes 344072 | tf_op jit(solution)/shard_map/ppermute | solution.py:20
  37.1 6.2 %experts.2 = (bf16[512,896]{1,0:T(8,128)(2,1)S(1)}, bf16[512,896]{1,0:T(8,128)(2,1)S(1)}, bf16[3,256,3584]{2,1,0:T(8,128)(2,1)S(1)}) custom-call(s32[2]{0:T(128)S(1)} %pad_add_fusion.ranks_ref, bf16[64,3584]{1,0:T(8,128)(2,1)S(1)} %copy-done, bf16[64,1024]{1,0:T(8,128)(2,1)S(1)} %get-tuple-element.58.refs_1_, ...), custom_call_target="tpu_custom_call" | custom-call | tf_op jit(solution)/shard_map/experts/pallas_call | solution.py:307
  44.8 1.1 %collective-permute-done.20 = bf16[512,896]{1,0:T(8,128)(2,1)S(1)} collective-permute-done((bf16[512,896]{1,0:T(8,128)(2,1)S(1)}, bf16[512,896]{1,0:T(8,128)(2,1)S(1)}, u32[]{:S(2)}, u32[]{:S(2)}) %collective-permute-start.20) | collective-permute-done | bytes 917536 | tf_op jit(solution)/shard_map/ppermute | solution.py:20
  48.5 5.6 %experts.3 = (bf16[512,896]{1,0:T(8,128)(2,1)S(1)}, bf16[512,896]{1,0:T(8,128)(2,1)S(1)}) custom-call(s32[2]{0:T(128)S(1)} %pad_add_fusion.ranks_ref, bf16[256,1024]{1,0:T(8,128)(2,1)S(1)} %constant_dynamic-update-slice_fusion.2.refs_0_, bf16[256,1024]{1,0:T(8,128)(2,1)S(1)} %collective-permute-done.15.refs_1_, ...), custom_call_target="tpu_custom_call" | custom-call | tf_op jit(solution)/shard_map/experts/pallas_call | solution.py:307
  55.2 1.4 %collective-permute-done.23 = bf16[512,896]{1,0:T(8,128)(2,1)S(1)} collective-permute-done((bf16[512,896]{1,0:T(8,128)(2,1)S(1)}, bf16[512,896]{1,0:T(8,128)(2,1)S(1)}, u32[]{:S(2)}, u32[]{:S(2)}) %collective-permute-start.23) | collective-permute-done | bytes 917536 | tf_op jit(solution)/shard_map/ppermute | solution.py:20
  57.0 1.4 %collective-permute-start.24 = (bf16[64,896]{1,0:T(8,128)(2,1)S(1)}, bf16[64,896]{1,0:T(8,128)(2,1)S(1)}, u32[]{:S(2)}, u32[]{:S(2)}) collective-permute-start(bf16[64,896]{1,0:T(8,128)(2,1)S(1)} %get-tuple-element.121), channel_id=1, source_target_pairs={{0,2},{1,3},{2,0},{3,1},{4,6},{5,7},{6,4},{7,5},{8,10},{9,11},{10,... | collective-permute-start | bytes 344072 | tf_op jit(solution)/shard_map/ppermute | solution.py:20
  58.9 1.5 %collective-permute-start.30 = (bf16[576,256]{1,0:T(8,128)(2,1)S(1)}, bf16[576,256]{1,0:T(8,128)(2,1)S(1)}, u32[]{:S(2)}, u32[]{:S(2)}) collective-permute-start(bf16[576,256]{1,0:T(8,128)(2,1)S(1)} %broadcast_select_fusion.1), channel_id=1, source_target_pairs={{0,16},{4,20},{8,24},{12,28},{16,0},{20,4},{24,8},{28,12},{1,17},{... | collective-permute-start | bytes 884744 | tf_op jit(solution)/shard_map/ppermute | solution.py:20
  60.5 2.6 %collective-permute-done.26 = bf16[64,1792]{1,0:T(8,128)(2,1)S(1)} collective-permute-done((bf16[64,1792]{1,0:T(8,128)(2,1)S(1)}, bf16[64,1792]{1,0:T(8,128)(2,1)S(1)}, u32[]{:S(2)}, u32[]{:S(2)}) %collective-permute-start.26) | collective-permute-done | bytes 229408 | tf_op jit(solution)/shard_map/ppermute | solution.py:20
  63.1 1.7 %collective-permute-done.25 = bf16[64,896]{1,0:T(8,128)(2,1)S(1)} collective-permute-done((bf16[64,896]{1,0:T(8,128)(2,1)S(1)}, bf16[64,896]{1,0:T(8,128)(2,1)S(1)}, u32[]{:S(2)}, u32[]{:S(2)}) %collective-permute-start.25) | collective-permute-done | bytes 114720 | tf_op jit(solution)/shard_map/ppermute | solution.py:20
  64.8 1.4 %collective-permute-start.28 = (bf16[128,896]{1,0:T(8,128)(2,1)S(1)}, bf16[128,896]{1,0:T(8,128)(2,1)S(1)}, u32[]{:S(2)}, u32[]{:S(2)}) collective-permute-start(bf16[128,896]{1,0:T(8,128)(2,1)S(1)} %add_convert_fusion.3), channel_id=1, source_target_pairs={{0,2},{1,3},{2,0},{3,1},{4,6},{5,7},{6,4},{7,5},{8,10},{9,11},{10,... | collective-permute-start | bytes 688136 | tf_op jit(solution)/shard_map/ppermute | solution.py:20
  66.9 1.5 %collective-permute-start.29 = (bf16[64,896]{1,0:T(8,128)(2,1)S(1)}, bf16[64,896]{1,0:T(8,128)(2,1)S(1)}, u32[]{:S(2)}, u32[]{:S(2)}) collective-permute-start(bf16[64,896]{1,0:T(8,128)(2,1)S(1)} %add_convert_fusion.8), channel_id=1, source_target_pairs={{0,4},{4,0},{8,12},{12,8},{16,20},{20,16},{24,28},{28,24},{1,5},{5... | collective-permute-start | bytes 344072 | tf_op jit(solution)/shard_map/ppermute | solution.py:20
  68.4 5.6 %attend_local.3.old_ref = bf16[16,128,512]{2,1,0:T(8,128)(2,1)} custom-call(s32[2]{0:T(128)S(1)} %pad_add_fusion.ranks_ref, s32[512]{0:T(512)S(1)} %copy-done.1, bf16[16,576,128]{2,1,0:T(8,128)(2,1)} %bitcast.13, bf16[16,576,256]{2,1,0:T(8,128)(2,1)} %bitcast.11, bf16[16,128,512]{2,1,0:T(8,128)(2,1)} %attend_local.2.refs_0_), custom_call_target="tpu_custom_call", output_to_operand_aliasing={{}: (4, {})} | custom-call | tf_op jit(solution)/shard_map/attend_local/pallas_call | solution.py:130
  74.0 1.3 %collective-permute-done.29 = bf16[64,896]{1,0:T(8,128)(2,1)S(1)} collective-permute-done((bf16[64,896]{1,0:T(8,128)(2,1)S(1)}, bf16[64,896]{1,0:T(8,128)(2,1)S(1)}, u32[]{:S(2)}, u32[]{:S(2)}) %collective-permute-start.29) | collective-permute-done | bytes 114720 | tf_op jit(solution)/shard_map/ppermute | solution.py:20
  75.6 3.1 %collective-permute-start.31 = (bf16[64,896]{1,0:T(8,128)(2,1)S(1)}, bf16[64,896]{1,0:T(8,128)(2,1)S(1)}, u32[]{:S(2)}, u32[]{:S(2)}) collective-permute-start(bf16[64,896]{1,0:T(8,128)(2,1)S(1)} %get-tuple-element.123), channel_id=1, source_target_pairs={{0,16},{4,20},{8,24},{12,28},{16,0},{20,4},{24,8},{28,12},{1,17},{... | collective-permute-start | bytes 344072 | tf_op jit(solution)/shard_map/ppermute | solution.py:20
  78.7 1.3 %collective-permute-start.32 = (bf16[64,896]{1,0:T(8,128)(2,1)S(1)}, bf16[64,896]{1,0:T(8,128)(2,1)S(1)}, u32[]{:S(2)}, u32[]{:S(2)}) collective-permute-start(bf16[64,896]{1,0:T(8,128)(2,1)S(1)} %get-tuple-element.122), channel_id=1, source_target_pairs={{0,24},{4,28},{8,16},{12,20},{16,8},{20,12},{24,0},{28,4},{1,25},{... | collective-permute-start | bytes 344072 | tf_op jit(solution)/shard_map/ppermute | solution.py:20
  80.8 2.7 %attend_traded.1 = bf16[16,128,512]{2,1,0:T(8,128)(2,1)} custom-call(s32[2]{0:T(128)S(1)} %pad_add_fusion.ranks_ref, s32[512]{0:T(512)S(1)} %copy-done.1, s32[32]{0:T(128)S(1)} %copy-done.2, s32[1]{0:T(128)S(6)} %copy.19.mask_ref, bf16[16,576,128]{2,1,0:T(8,128)(2,1)} %bitcast.14, ...), custom_call_target="tpu_custom_call", output_to_operand_aliasing={{}: (6, {})} | custom-call | flops 71303168 | bytes 573440 | tf_op jit(solution)/shard_map/attend_traded/pallas_call | solution.py:191
  83.5 3.9 %collective-permute-done.31 = bf16[64,896]{1,0:T(8,128)(2,1)S(1)} collective-permute-done((bf16[64,896]{1,0:T(8,128)(2,1)S(1)}, bf16[64,896]{1,0:T(8,128)(2,1)S(1)}, u32[]{:S(2)}, u32[]{:S(2)}) %collective-permute-start.31) | collective-permute-done | bytes 114720 | tf_op jit(solution)/shard_map/ppermute | solution.py:20
  (79 shorter events, 9.5 us)
Async XLA Ops:
  2.6 7.4 %collective-permute-start = (bf16[64,1024]{1,0:T(8,128)(2,1)S(1)}, bf16[64,1024]{1,0:T(8,128)(2,1)S(1)}, u32[]{:S(2)}, u32[]{:S(2)}) collective-permute-start(bf16[64,1024]{1,0:T(8,128)(2,1)S(1)} %get-tuple-element.58.refs_1_), channel_id=1, source_target_pairs={{0,8},{4,12},{8,0},{12,4},{16,24},{20,28},{24,16},{28,20},{1,9},{5... | collective-permute-start | bytes 393224 | tf_op jit(solution)/shard_map/ppermute | solution.py:20
  5.7 13.8 %collective-permute-start.3 = (bf16[64,1920]{1,0:T(8,128)(2,1)S(1)}, bf16[64,1920]{1,0:T(8,128)(2,1)S(1)}, u32[]{:S(2)}, u32[]{:S(2)}) collective-permute-start(bf16[64,1920]{1,0:T(8,128)(2,1)S(1)} %get-tuple-element.65), channel_id=1, source_target_pairs={{0,4},{4,0},{8,12},{12,8},{16,20},{20,16},{24,28},{28,24},{1,5},{5... | collective-permute-start | bytes 737288 | tf_op jit(solution)/shard_map/ppermute | solution.py:20
  7.2 12.3 %collective-permute-start.4 = (bf16[64,1024]{1,0:T(8,128)(2,1)S(1)}, bf16[64,1024]{1,0:T(8,128)(2,1)S(1)}, u32[]{:S(2)}, u32[]{:S(2)}) collective-permute-start(bf16[64,1024]{1,0:T(8,128)(2,1)S(1)} %get-tuple-element.58.refs_1_), channel_id=1, source_target_pairs={{0,16},{4,20},{8,24},{12,28},{16,0},{20,4},{24,8},{28,12},{1,17},{... | collective-permute-start | bytes 393224 | tf_op jit(solution)/shard_map/ppermute | solution.py:20
  9.8 9.7 %collective-permute-start.5 = (bf16[64,1024]{1,0:T(8,128)(2,1)S(1)}, bf16[64,1024]{1,0:T(8,128)(2,1)S(1)}, u32[]{:S(2)}, u32[]{:S(2)}) collective-permute-start(bf16[64,1024]{1,0:T(8,128)(2,1)S(1)} %get-tuple-element.58.refs_1_), channel_id=1, source_target_pairs={{0,24},{4,28},{8,16},{12,20},{16,8},{20,12},{24,0},{28,4},{1,25},{... | collective-permute-start | bytes 393224 | tf_op jit(solution)/shard_map/ppermute | solution.py:20
  10.0 9.5 %collective-permute-start.2 = (bf16[64,1024]{1,0:T(8,128)(2,1)S(1)}, bf16[64,1024]{1,0:T(8,128)(2,1)S(1)}, u32[]{:S(2)}, u32[]{:S(2)}) collective-permute-start(bf16[64,1024]{1,0:T(8,128)(2,1)S(1)} %collective-permute-done.refs_4_), channel_id=1, source_target_pairs={{0,4},{4,0},{8,12},{12,8},{16,20},{20,16},{24,28},{28,24},{1,5},{5... | collective-permute-start | bytes 393224 | tf_op jit(solution)/shard_map/ppermute | solution.py:20
  12.4 7.1 %collective-permute-start.1 = (bf16[64,896]{1,0:T(8,128)(2,1)S(1)}, bf16[64,896]{1,0:T(8,128)(2,1)S(1)}, u32[]{:S(2)}, u32[]{:S(2)}) collective-permute-start(bf16[64,896]{1,0:T(8,128)(2,1)S(1)} %slice.78), channel_id=1, source_target_pairs={{0,2},{1,3},{2,0},{3,1},{4,6},{5,7},{6,4},{7,5},{8,10},{9,11},{10,... | collective-permute-start | bytes 344072 | tf_op jit(solution)/shard_map/ppermute | solution.py:20
  19.5 4.3 %collective-permute-start.9 = (bf16[128,1024]{1,0:T(8,128)(2,1)S(1)}, bf16[128,1024]{1,0:T(8,128)(2,1)S(1)}, u32[]{:S(2)}, u32[]{:S(2)}) collective-permute-start(bf16[128,1024]{1,0:T(8,128)(2,1)S(1)} %pad_maximum_fusion), channel_id=1, source_target_pairs={{0,1},{1,0},{2,3},{3,2},{4,5},{5,4},{6,7},{7,6},{8,9},{9,8},{10,11... | collective-permute-start | bytes 786440 | tf_op jit(solution)/shard_map/ppermute | solution.py:20
  19.6 11.8 %collective-permute-start.8 = (bf16[128,1024]{1,0:T(8,128)(2,1)S(1)}, bf16[128,1024]{1,0:T(8,128)(2,1)S(1)}, u32[]{:S(2)}, u32[]{:S(2)}) collective-permute-start(bf16[128,1024]{1,0:T(8,128)(2,1)S(1)} %constant_dynamic-update-slice_fusion), channel_id=1, source_target_pairs={{0,4},{4,0},{8,12},{12,8},{16,20},{20,16},{24,28},{28,24},{1,5},{5... | collective-permute-start | bytes 786440 | tf_op jit(solution)/shard_map/ppermute | solution.py:20
  20.7 3.1 %collective-permute-start.10 = (bf16[64,1920]{1,0:T(8,128)(2,1)S(1)}, bf16[64,1920]{1,0:T(8,128)(2,1)S(1)}, u32[]{:S(2)}, u32[]{:S(2)}) collective-permute-start(bf16[64,1920]{1,0:T(8,128)(2,1)S(1)} %collective-permute-done.3.refs_2_), channel_id=1, source_target_pairs={{0,1},{1,0},{2,3},{3,2},{4,5},{5,4},{6,7},{7,6},{8,9},{9,8},{10,11... | collective-permute-start | bytes 737288 | tf_op jit(solution)/shard_map/ppermute | solution.py:20
  21.2 10.2 %collective-permute-start.7 = (bf16[128,896]{1,0:T(8,128)(2,1)S(1)}, bf16[128,896]{1,0:T(8,128)(2,1)S(1)}, u32[]{:S(2)}, u32[]{:S(2)}) collective-permute-start(bf16[128,896]{1,0:T(8,128)(2,1)S(1)} %slice.101), channel_id=1, source_target_pairs={{0,2},{1,3},{2,0},{3,1},{4,6},{5,7},{6,4},{7,5},{8,10},{9,11},{10,... | collective-permute-start | bytes 688136 | tf_op jit(solution)/shard_map/ppermute | solution.py:20
  22.7 8.7 %collective-permute-start.6 = (bf16[64,896]{1,0:T(8,128)(2,1)S(1)}, bf16[64,896]{1,0:T(8,128)(2,1)S(1)}, u32[]{:S(2)}, u32[]{:S(2)}) collective-permute-start(bf16[64,896]{1,0:T(8,128)(2,1)S(1)} %slice.79), channel_id=1, source_target_pairs={{0,2},{1,3},{2,0},{3,1},{4,6},{5,7},{6,4},{7,5},{8,10},{9,11},{10,... | collective-permute-start | bytes 344072 | tf_op jit(solution)/shard_map/ppermute | solution.py:20
  31.5 11.9 %collective-permute-start.15 = (bf16[256,1024]{1,0:T(8,128)(2,1)S(1)}, bf16[256,1024]{1,0:T(8,128)(2,1)S(1)}, u32[]{:S(2)}, u32[]{:S(2)}) collective-permute-start(bf16[256,1024]{1,0:T(8,128)(2,1)S(1)} %constant_dynamic-update-slice_fusion.2.refs_0_), channel_id=1, source_target_pairs={{0,1},{1,0},{2,3},{3,2},{4,5},{5,4},{6,7},{7,6},{8,9},{9,8},{10,11... | collective-permute-start | bytes 1572872 | tf_op jit(solution)/shard_map/ppermute | solution.py:20
  31.6 11.7 %collective-permute-start.17 = (bf16[576,256]{1,0:T(8,128)(2,1)S(1)}, bf16[576,256]{1,0:T(8,128)(2,1)S(1)}, u32[]{:S(2)}, u32[]{:S(2)}) collective-permute-start(bf16[576,256]{1,0:T(8,128)(2,1)S(1)} %get-tuple-element.83), channel_id=1, source_target_pairs={{0,8},{4,12},{8,0},{12,4},{16,24},{20,28},{24,16},{28,20},{1,9},{5... | collective-permute-start | bytes 884744 | tf_op jit(solution)/shard_map/ppermute | solution.py:20
  33.6 2.1 %collective-permute-start.12 = (bf16[64,896]{1,0:T(8,128)(2,1)S(1)}, bf16[64,896]{1,0:T(8,128)(2,1)S(1)}, u32[]{:S(2)}, u32[]{:S(2)}) collective-permute-start(bf16[64,896]{1,0:T(8,128)(2,1)S(1)} %collective-permute-done.6.refs_9_), channel_id=1, source_target_pairs={{0,1},{1,0},{2,3},{3,2},{4,5},{5,4},{6,7},{7,6},{8,9},{9,8},{10,11... | collective-permute-start | bytes 344072 | tf_op jit(solution)/shard_map/ppermute | solution.py:20
  33.8 9.6 %collective-permute-start.16 = (bf16[128,896]{1,0:T(8,128)(2,1)S(1)}, bf16[128,896]{1,0:T(8,128)(2,1)S(1)}, u32[]{:S(2)}, u32[]{:S(2)}) collective-permute-start(bf16[128,896]{1,0:T(8,128)(2,1)S(1)} %collective-permute-done.7.refs_2_), channel_id=1, source_target_pairs={{0,1},{1,0},{2,3},{3,2},{4,5},{5,4},{6,7},{7,6},{8,9},{9,8},{10,11... | collective-permute-start | bytes 688136 | tf_op jit(solution)/shard_map/ppermute | solution.py:20
  34.1 9.2 %collective-permute-start.13 = (bf16[64,896]{1,0:T(8,128)(2,1)S(1)}, bf16[64,896]{1,0:T(8,128)(2,1)S(1)}, u32[]{:S(2)}, u32[]{:S(2)}) collective-permute-start(bf16[64,896]{1,0:T(8,128)(2,1)S(1)} %slice.81), channel_id=1, source_target_pairs={{0,2},{1,3},{2,0},{3,1},{4,6},{5,7},{6,4},{7,5},{8,10},{9,11},{10,... | collective-permute-start | bytes 344072 | tf_op jit(solution)/shard_map/ppermute | solution.py:20
  35.7 7.7 %collective-permute-start.14 = (bf16[64,896]{1,0:T(8,128)(2,1)S(1)}, bf16[64,896]{1,0:T(8,128)(2,1)S(1)}, u32[]{:S(2)}, u32[]{:S(2)}) collective-permute-start(bf16[64,896]{1,0:T(8,128)(2,1)S(1)} %slice.82), channel_id=1, source_target_pairs={{0,4},{4,0},{8,12},{12,8},{16,20},{20,16},{24,28},{28,24},{1,5},{5... | collective-permute-start | bytes 344072 | tf_op jit(solution)/shard_map/ppermute | solution.py:20
  43.4 2.5 %collective-permute-start.20 = (bf16[512,896]{1,0:T(8,128)(2,1)S(1)}, bf16[512,896]{1,0:T(8,128)(2,1)S(1)}, u32[]{:S(2)}, u32[]{:S(2)}) collective-permute-start(bf16[512,896]{1,0:T(8,128)(2,1)S(1)} %get-tuple-element.92), channel_id=1, source_target_pairs={{0,1},{1,0},{2,3},{3,2},{4,5},{5,4},{6,7},{7,6},{8,9},{9,8},{10,11... | collective-permute-start | bytes 2752520 | tf_op jit(solution)/shard_map/ppermute | solution.py:20
  44.2 9.9 %collective-permute-start.22 = (bf16[576,256]{1,0:T(8,128)(2,1)S(1)}, bf16[576,256]{1,0:T(8,128)(2,1)S(1)}, u32[]{:S(2)}, u32[]{:S(2)}) collective-permute-start(bf16[576,256]{1,0:T(8,128)(2,1)S(1)} %broadcast_select_fusion.2), channel_id=1, source_target_pairs={{0,4},{4,0},{8,12},{12,8},{16,20},{20,16},{24,28},{28,24},{1,5},{5... | collective-permute-start | bytes 884744 | tf_op jit(solution)/shard_map/ppermute | solution.py:20
  46.2 7.9 %collective-permute-start.21 = (bf16[128,896]{1,0:T(8,128)(2,1)S(1)}, bf16[128,896]{1,0:T(8,128)(2,1)S(1)}, u32[]{:S(2)}, u32[]{:S(2)}) collective-permute-start(bf16[128,896]{1,0:T(8,128)(2,1)S(1)} %slice.102), channel_id=1, source_target_pairs={{0,2},{1,3},{2,0},{3,1},{4,6},{5,7},{6,4},{7,5},{8,10},{9,11},{10,... | collective-permute-start | bytes 688136 | tf_op jit(solution)/shard_map/ppermute | solution.py:20
  54.1 2.5 %collective-permute-start.23 = (bf16[512,896]{1,0:T(8,128)(2,1)S(1)}, bf16[512,896]{1,0:T(8,128)(2,1)S(1)}, u32[]{:S(2)}, u32[]{:S(2)}) collective-permute-start(bf16[512,896]{1,0:T(8,128)(2,1)S(1)} %get-tuple-element.95), channel_id=1, source_target_pairs={{0,1},{1,0},{2,3},{3,2},{4,5},{5,4},{6,7},{7,6},{8,9},{9,8},{10,11... | collective-permute-start | bytes 2752520 | tf_op jit(solution)/shard_map/ppermute | solution.py:20
  54.5 8.5 %collective-permute-start.26 = (bf16[64,1792]{1,0:T(8,128)(2,1)S(1)}, bf16[64,1792]{1,0:T(8,128)(2,1)S(1)}, u32[]{:S(2)}, u32[]{:S(2)}) collective-permute-start(bf16[64,1792]{1,0:T(8,128)(2,1)S(1)} %pad_maximum_fusion.1), channel_id=1, source_target_pairs={{0,4},{4,0},{8,12},{12,8},{16,20},{20,16},{24,28},{28,24},{1,5},{5... | collective-permute-start | bytes 688136 | tf_op jit(solution)/shard_map/ppermute | solution.py:20
  57.0 6.1 %collective-permute-start.24 = (bf16[64,896]{1,0:T(8,128)(2,1)S(1)}, bf16[64,896]{1,0:T(8,128)(2,1)S(1)}, u32[]{:S(2)}, u32[]{:S(2)}) collective-permute-start(bf16[64,896]{1,0:T(8,128)(2,1)S(1)} %get-tuple-element.121), channel_id=1, source_target_pairs={{0,2},{1,3},{2,0},{3,1},{4,6},{5,7},{6,4},{7,5},{8,10},{9,11},{10,... | collective-permute-start | bytes 344072 | tf_op jit(solution)/shard_map/ppermute | solution.py:20
  58.3 6.4 %collective-permute-start.25 = (bf16[64,896]{1,0:T(8,128)(2,1)S(1)}, bf16[64,896]{1,0:T(8,128)(2,1)S(1)}, u32[]{:S(2)}, u32[]{:S(2)}) collective-permute-start(bf16[64,896]{1,0:T(8,128)(2,1)S(1)} %get-tuple-element.120), channel_id=1, source_target_pairs={{0,4},{4,0},{8,12},{12,8},{16,20},{20,16},{24,28},{28,24},{1,5},{5... | collective-permute-start | bytes 344072 | tf_op jit(solution)/shard_map/ppermute | solution.py:20
  58.9 16.3 %collective-permute-start.30 = (bf16[576,256]{1,0:T(8,128)(2,1)S(1)}, bf16[576,256]{1,0:T(8,128)(2,1)S(1)}, u32[]{:S(2)}, u32[]{:S(2)}) collective-permute-start(bf16[576,256]{1,0:T(8,128)(2,1)S(1)} %broadcast_select_fusion.1), channel_id=1, source_target_pairs={{0,16},{4,20},{8,24},{12,28},{16,0},{20,4},{24,8},{28,12},{1,17},{... | collective-permute-start | bytes 884744 | tf_op jit(solution)/shard_map/ppermute | solution.py:20
  64.8 10.5 %collective-permute-start.28 = (bf16[128,896]{1,0:T(8,128)(2,1)S(1)}, bf16[128,896]{1,0:T(8,128)(2,1)S(1)}, u32[]{:S(2)}, u32[]{:S(2)}) collective-permute-start(bf16[128,896]{1,0:T(8,128)(2,1)S(1)} %add_convert_fusion.3), channel_id=1, source_target_pairs={{0,2},{1,3},{2,0},{3,1},{4,6},{5,7},{6,4},{7,5},{8,10},{9,11},{10,... | collective-permute-start | bytes 688136 | tf_op jit(solution)/shard_map/ppermute | solution.py:20
  66.2 9.1 %collective-permute-start.27 = (bf16[128,896]{1,0:T(8,128)(2,1)S(1)}, bf16[128,896]{1,0:T(8,128)(2,1)S(1)}, u32[]{:S(2)}, u32[]{:S(2)}) collective-permute-start(bf16[128,896]{1,0:T(8,128)(2,1)S(1)} %add_convert_fusion.4), channel_id=1, source_target_pairs={{0,4},{4,0},{8,12},{12,8},{16,20},{20,16},{24,28},{28,24},{1,5},{5... | collective-permute-start | bytes 688136 | tf_op jit(solution)/shard_map/ppermute | solution.py:20
  66.9 8.4 %collective-permute-start.29 = (bf16[64,896]{1,0:T(8,128)(2,1)S(1)}, bf16[64,896]{1,0:T(8,128)(2,1)S(1)}, u32[]{:S(2)}, u32[]{:S(2)}) collective-permute-start(bf16[64,896]{1,0:T(8,128)(2,1)S(1)} %add_convert_fusion.8), channel_id=1, source_target_pairs={{0,4},{4,0},{8,12},{12,8},{16,20},{20,16},{24,28},{28,24},{1,5},{5... | collective-permute-start | bytes 344072 | tf_op jit(solution)/shard_map/ppermute | solution.py:20
  75.4 8.1 %collective-permute-start.33 = (bf16[64,896]{1,0:T(8,128)(2,1)S(1)}, bf16[64,896]{1,0:T(8,128)(2,1)S(1)}, u32[]{:S(2)}, u32[]{:S(2)}) collective-permute-start(bf16[64,896]{1,0:T(8,128)(2,1)S(1)} %get-tuple-element.115), channel_id=1, source_target_pairs={{0,8},{4,12},{8,0},{12,4},{16,24},{20,28},{24,16},{28,20},{1,9},{5... | collective-permute-start | bytes 344072 | tf_op jit(solution)/shard_map/ppermute | solution.py:20
  75.6 11.8 %collective-permute-start.31 = (bf16[64,896]{1,0:T(8,128)(2,1)S(1)}, bf16[64,896]{1,0:T(8,128)(2,1)S(1)}, u32[]{:S(2)}, u32[]{:S(2)}) collective-permute-start(bf16[64,896]{1,0:T(8,128)(2,1)S(1)} %get-tuple-element.123), channel_id=1, source_target_pairs={{0,16},{4,20},{8,24},{12,28},{16,0},{20,4},{24,8},{28,12},{1,17},{... | collective-permute-start | bytes 344072 | tf_op jit(solution)/shard_map/ppermute | solution.py:20
  78.7 8.7 %collective-permute-start.32 = (bf16[64,896]{1,0:T(8,128)(2,1)S(1)}, bf16[64,896]{1,0:T(8,128)(2,1)S(1)}, u32[]{:S(2)}, u32[]{:S(2)}) collective-permute-start(bf16[64,896]{1,0:T(8,128)(2,1)S(1)} %get-tuple-element.122), channel_id=1, source_target_pairs={{0,24},{4,28},{8,16},{12,20},{16,8},{20,12},{24,0},{28,4},{1,25},{... | collective-permute-start | bytes 344072 | tf_op jit(solution)/shard_map/ppermute | solution.py:20
  80.0 7.4 %collective-permute-start.34 = (bf16[64,896]{1,0:T(8,128)(2,1)S(1)}, bf16[64,896]{1,0:T(8,128)(2,1)S(1)}, u32[]{:S(2)}, u32[]{:S(2)}) collective-permute-start(bf16[64,896]{1,0:T(8,128)(2,1)S(1)} %get-tuple-element.114), channel_id=1, source_target_pairs={{0,2},{1,3},{2,0},{3,1},{4,6},{5,7},{6,4},{7,5},{8,10},{9,11},{10,... | collective-permute-start | bytes 344072 | tf_op jit(solution)/shard_map/ppermute | solution.py:20
  (6 other events, 36.2 us)

commit v9 on v8

--- a/solution.py
+++ b/solution.py
@@ -408,21 +408,20 @@
     far_2, near_3, w_gate, w_up, page, both_1, *late_pieces = tie(
         (far_2, near_3, w_gate, w_up, page, both_1, *late_pieces)
     )
-    far_3 = flip(bare(near_3), "tp", 2)
-
     near_late = jnp.concatenate(late_pieces, axis=0)
-    far_late = flip(bare(near_late), "tp", 2)
+    far_3 = flip(jnp.concatenate([bare(near_3), bare(near_late)], axis=0), "tp", 2)
     near_odds = flip(near_late, "ep", 1)
     near_23 = flip(jnp.concatenate([near_2, near_3], axis=0), "tp", 1)
     early = [flip(array, "tp", 1) for array in (both_1, far_2)]
     queries, near_23, early = tie((queries, near_23, early))
     count = queries.shape[0]
-    attended = attend_part(ranks, lengths, queries, cache_pages, groups, 0, count // 2)
-    far_3, far_late, near_late, near_odds, attended = tie(
-        (far_3, far_late, near_late, near_odds, attended)
-    )
-    far_odds_y = flip(bare(cut(near_odds, 0, half)), "tp", 2)
-    far_odds_x = flip(cut(far_late, half, rest), "ep", 1)
+    some = count * 5 // 8
+    attended = attend_part(ranks, lengths, queries, cache_pages, groups, 0, some)
+    far_3, near_late, near_odds, attended, page = tie(
+        (far_3, near_late, near_odds, attended, page)
+    )
+    far_3, far_late = cut(far_3, 0, 1), cut(far_3, 1, len(late))
+    far_odds = flip(bare(near_odds), "tp", 2)
 
     def piece(start, part, array):
         return start * rows, (part,), part == 0, array
@@ -437,41 +436,38 @@
     )
     near_both = jnp.concatenate([near_late, near_odds], axis=0)
     early = [flip(array, "tp", 1) for array in (near_both, far_late)]
-    swapped = flip(page, "ep", 2)
-    first, far_odds_y, far_odds_x, early, swapped = tie(
-        (first, far_odds_y, far_odds_x, early, swapped)
-    )
-    page = page_take(page, swapped, 1)
+    swapped = flip(page, "ep", 1)
+    first, far_odds, early, swapped = tie((first, far_odds, early, swapped))
+    page = page_take(page, swapped, 0)
 
     def add_core(given, own):
         total = total_of(own, flip(given, "tp", 1))
         return jnp.split(total, 2, axis=0)
 
     sent, kept = add_core(*first)
-    last = [flip(array, "tp", 1) for array in (far_odds_y, far_odds_x)]
+    last = flip(far_odds, "tp", 1)
     over_23 = flip(cut(sent, 2, 2), "tp", 2)
     over_1 = flip(jnp.concatenate([cut(kept, 1, 1), cut(sent, 1, 1)], axis=1), "ep", 1)
-    swapped = flip(page, "ep", 1)
+    swapped = flip(page, "ep", 2)
     odds = len(late)
     pieces = [piece(0, 0, near_both), (0, (1,), False, early[0])]
     pieces += [piece(0, 2, far_late), piece(0, 3, early[1])]
-    pieces += [piece(odds, 2, far_odds_y), piece(odds, 3, last[0])]
-    pieces += [piece(odds + half, 2, far_odds_x), piece(odds + half, 3, last[1])]
+    pieces += [piece(odds, 2, far_odds), piece(odds, 3, last)]
     second = [
         *run_experts(
             ranks, pieces, w_gate, w_up, w_down, 2 * len(late) * rows, columns, top, False
         )
     ]
-    second, over_23, swapped = tie((second, over_23, swapped))
-    swapped, page = page_far(page_take(page, swapped, 0))
+    second, over_23, over_1, swapped = tie((second, over_23, over_1, swapped))
+    swapped, page = page_far(page_take(page, swapped, 1))
     late_sent, late_kept = add_core(*second)
     over_3 = flip(total_of(cut(kept, 3, 1), cut(over_23, 1, 1)), "ep", 1)
+    zero = flip(total_of(cut(sent, 0, 1), over_1[:, columns:]), "tp", 2)
     late_sent, late_kept = tie((late_sent, late_kept))
 
     over_y = flip(cut(late_sent, len(late), half), "tp", 2)
     over_x = flip(cut(late_sent, len(late) + half, rest), "ep", 1)
-    over_y, over_x, over_1, queries = tie((over_y, over_x, over_1, queries))
-    zero = flip(total_of(cut(sent, 0, 1), over_1[:, columns:]), "tp", 2)
+    over_y, over_x, over_3, zero, queries = tie((over_y, over_x, over_3, zero, queries))
     odd = total_of(
         cut(late_kept, len(late), len(late)), jnp.pad(over_y, ((0, rest * rows), (0, 0)))
     )
@@ -479,9 +475,9 @@
     even = total_of(cut(late_sent, 0, len(late)), jnp.pad(over_x, ((half * rows, 0), (0, 0))))
     even = flip(even, "tp", 2)
     attended = attend_part(
-        ranks, lengths, queries, cache_pages, groups, count // 2, count - count // 2, attended
-    )
-    odd, even, over_3, attended, swapped = tie((odd, even, over_3, attended, swapped))
+        ranks, lengths, queries, cache_pages, groups, some, count - some, attended
+    )
+    odd, even, attended, swapped = tie((odd, even, attended, swapped))
     if levels > 2:
         page = page_take(page, swapped, 2)
     even = total_of(cut(late_kept, 0, len(late)), even, odd)

time: 88.5 us -> 86 us (0.972)
  waiting for transfers between devices: 16.5 us -> 14.1 us
    ppermute x35 -> x32, waiting for transfers between devices: 16.5 us -> 14.1 us  [flip(): return lax.ppermute(block, axis, [(i, i ^ apart) for i in range(count)])]
    ppermute x35 -> x32, starting transfers between devices: 36.3 us -> 35.6 us  [flip(): return lax.ppermute(block, axis, [(i, i ^ apart) for i in range(count)])]
  transfers between devices with their start and end apart: 35 -> 32, of which waited for: 10 -> 8; matrix products, arithmetic and copies ran while one was open for 1% -> 1% of each run, Pallas kernels for 34% -> 35%
where the time goes in v9:
time: 86 us; the launch traced here: 85.6 us
  starting transfers between devices  35.6 us (41%)
  Pallas kernels  32.2 us (37%)
  waiting for transfers between devices  14.1 us (16%)
  other arithmetic  1.7 us (2%)
  between operations  1.61 us (2%)
    ppermute x32, starting transfers between devices, flip(): return lax.ppermute(block, axis, [(i, i ^ apart) for i in range(count)])  35.6 us
    ppermute x32, waiting for transfers between devices, flip(): return lax.ppermute(block, axis, [(i, i ^ apart) for i in range(count)])  14.1 us
    pallas_call x2, Pallas kernels, run_experts(): pl.pallas_call(kernel, out_shape=[pltpu.VMEM((2 * rows, columns), jnp.bfl...  11.8 us
    pallas_call x2, Pallas kernels, attend_part(): pl.pallas_call(kernel, out_shape=jax.ShapeDtypeStruct((count, heads, LAT)...  11.6 us
    pallas_call x1, Pallas kernels, load(): pl.pallas_call(load_kernel, out_shape=[pltpu.VMEM(w.shape, w.dtype) for w...  4.21 us
    pallas_call x1, Pallas kernels, attend_traded(): pl.pallas_call(functools.partial(attend_traded_kernel, groups), out_shape...  2.71 us
    pallas_call x1, Pallas kernels, pick(): pl.pallas_call(functools.partial(pick_kernel, groups), out_shape=(pltpu.V...  1.89 us
  transfers between devices with their start and end apart: 32, of which 8 were waited for; matrix products, arithmetic and copies ran while one was open for 1% of the time, Pallas kernels for 35%

profile of v9, /device:TPU:0, one launch (start us, length us, event | category | flops | bytes accessed | tf_op | source)
XLA Modules:
  0.0 85.6 jit_solution(7204496888499989511)
XLA Ops:
  0.7 1.9 %pick.1 = (bf16[64,1024]{1,0:T(8,128)(2,1)S(1)}, bf16[64,1920]{1,0:T(8,128)(2,1)S(1)}, bf16[576,256]{1,0:T(8,128)(2,1)S(1)}) custom-call(s32[2]{0:T(128)S(1)} %pad_add_fusion.ranks_ref, s32[32]{0:T(128)} %slots_ref.3, s32[8,64]{1,0:T(8,128)} %bitcast.15, f32[8,64]{1,0:T(8,128)} %bitcast.16, bf16[64,3584]{1,0:T(8,128)(2,1)} %refs_0_.2, ...), custom_call_target="tpu_custom_call" | custom-call | tf_op jit(solution)/shard_map/pick/pallas_call | solution.py:96
  2.6 3.1 %collective-permute-start = (bf16[64,1024]{1,0:T(8,128)(2,1)S(1)}, bf16[64,1024]{1,0:T(8,128)(2,1)S(1)}, u32[]{:S(2)}, u32[]{:S(2)}) collective-permute-start(bf16[64,1024]{1,0:T(8,128)(2,1)S(1)} %get-tuple-element.58.refs_1_), channel_id=1, source_target_pairs={{0,8},{4,12},{8,0},{12,4},{16,24},{20,28},{24,16},{28,20},{1,9},{5... | collective-permute-start | bytes 393224 | tf_op jit(solution)/shard_map/ppermute | solution.py:20
  5.7 1.5 %collective-permute-start.3 = (bf16[64,1920]{1,0:T(8,128)(2,1)S(1)}, bf16[64,1920]{1,0:T(8,128)(2,1)S(1)}, u32[]{:S(2)}, u32[]{:S(2)}) collective-permute-start(bf16[64,1920]{1,0:T(8,128)(2,1)S(1)} %get-tuple-element.65), channel_id=1, source_target_pairs={{0,4},{4,0},{8,12},{12,8},{16,20},{20,16},{24,28},{28,24},{1,5},{5... | collective-permute-start | bytes 737288 | tf_op jit(solution)/shard_map/ppermute | solution.py:20
  7.2 2.6 %collective-permute-start.4 = (bf16[64,1024]{1,0:T(8,128)(2,1)S(1)}, bf16[64,1024]{1,0:T(8,128)(2,1)S(1)}, u32[]{:S(2)}, u32[]{:S(2)}) collective-permute-start(bf16[64,1024]{1,0:T(8,128)(2,1)S(1)} %get-tuple-element.58.refs_1_), channel_id=1, source_target_pairs={{0,16},{4,20},{8,24},{12,28},{16,0},{20,4},{24,8},{28,12},{1,17},{... | collective-permute-start | bytes 393224 | tf_op jit(solution)/shard_map/ppermute | solution.py:20
  10.0 2.3 %collective-permute-start.2 = (bf16[64,1024]{1,0:T(8,128)(2,1)S(1)}, bf16[64,1024]{1,0:T(8,128)(2,1)S(1)}, u32[]{:S(2)}, u32[]{:S(2)}) collective-permute-start(bf16[64,1024]{1,0:T(8,128)(2,1)S(1)} %collective-permute-done.refs_4_), channel_id=1, source_target_pairs={{0,4},{4,0},{8,12},{12,8},{16,20},{20,16},{24,28},{28,24},{1,5},{5... | collective-permute-start | bytes 393224 | tf_op jit(solution)/shard_map/ppermute | solution.py:20
  12.3 1.5 %collective-permute-start.1 = (bf16[64,896]{1,0:T(8,128)(2,1)S(1)}, bf16[64,896]{1,0:T(8,128)(2,1)S(1)}, u32[]{:S(2)}, u32[]{:S(2)}) collective-permute-start(bf16[64,896]{1,0:T(8,128)(2,1)S(1)} %slice.79), channel_id=1, source_target_pairs={{0,2},{1,3},{2,0},{3,1},{4,6},{5,7},{6,4},{7,5},{8,10},{9,11},{10,... | collective-permute-start | bytes 344072 | tf_op jit(solution)/shard_map/ppermute | solution.py:20
  13.9 4.2 %load.1 = (bf16[3,3584,256]{2,1,0:T(8,128)(2,1)S(1)}, bf16[3,3584,256]{2,1,0:T(8,128)(2,1)S(1)}) custom-call(bf16[3,3584,256]{2,1,0:T(8,128)(2,1)} %refs_0_.1, bf16[3,3584,256]{2,1,0:T(8,128)(2,1)} %refs_1_), custom_call_target="tpu_custom_call" | custom-call | bytes 11010048 | tf_op jit(solution)/shard_map/load/pallas_call | solution.py:162
  18.1 1.4 %collective-permute-done.4 = bf16[64,1024]{1,0:T(8,128)(2,1)S(1)} collective-permute-done((bf16[64,1024]{1,0:T(8,128)(2,1)S(1)}, bf16[64,1024]{1,0:T(8,128)(2,1)S(1)}, u32[]{:S(2)}, u32[]{:S(2)}) %collective-permute-start.4) | collective-permute-done | bytes 131104 | tf_op jit(solution)/shard_map/ppermute | solution.py:20
  19.6 1.6 %collective-permute-start.6 = (bf16[192,896]{1,0:T(8,128)(2,1)S(1)}, bf16[192,896]{1,0:T(8,128)(2,1)S(1)}, u32[]{:S(2)}, u32[]{:S(2)}) collective-permute-start(bf16[192,896]{1,0:T(8,128)(2,1)S(1)} %pad_maximum_fusion), channel_id=1, source_target_pairs={{0,2},{1,3},{2,0},{3,1},{4,6},{5,7},{6,4},{7,5},{8,10},{9,11},{10,... | collective-permute-start | bytes 1032200 | tf_op jit(solution)/shard_map/ppermute | solution.py:20
  21.3 1.0 %collective-permute-start.7 = (bf16[128,1024]{1,0:T(8,128)(2,1)S(1)}, bf16[128,1024]{1,0:T(8,128)(2,1)S(1)}, u32[]{:S(2)}, u32[]{:S(2)}) collective-permute-start(bf16[128,1024]{1,0:T(8,128)(2,1)S(1)} %constant_dynamic-update-slice_fusion), channel_id=1, source_target_pairs={{0,4},{4,0},{8,12},{12,8},{16,20},{20,16},{24,28},{28,24},{1,5},{5... | collective-permute-start | bytes 786440 | tf_op jit(solution)/shard_map/ppermute | solution.py:20
  22.8 1.2 %collective-permute-done.10.refs_8_ = bf16[64,896]{1,0:T(8,128)(2,1)S(1)} collective-permute-done((bf16[64,896]{1,0:T(8,128)(2,1)S(1)}, bf16[64,896]{1,0:T(8,128)(2,1)S(1)}, u32[]{:S(2)}, u32[]{:S(2)}) %collective-permute-start.10) | collective-permute-done | bytes 114720 | tf_op jit(solution)/shard_map/ppermute | solution.py:20
  23.9 6.8 %attend_local.2.refs_0_ = bf16[16,128,512]{2,1,0:T(8,128)(2,1)} custom-call(s32[2]{0:T(128)S(1)} %pad_add_fusion.ranks_ref, s32[512]{0:T(512)S(1)} %copy-done.1, bf16[16,576,128]{2,1,0:T(8,128)(2,1)} %bitcast.12, bf16[16,576,256]{2,1,0:T(8,128)(2,1)} %bitcast.10), custom_call_target="tpu_custom_call" | custom-call | tf_op jit(solution)/shard_map/attend_local/pallas_call | solution.py:130
  31.0 1.1 %collective-permute-start.15 = (bf16[576,256]{1,0:T(8,128)(2,1)S(1)}, bf16[576,256]{1,0:T(8,128)(2,1)S(1)}, u32[]{:S(2)}, u32[]{:S(2)}) collective-permute-start(bf16[576,256]{1,0:T(8,128)(2,1)S(1)} %get-tuple-element.83), channel_id=1, source_target_pairs={{0,4},{4,0},{8,12},{12,8},{16,20},{20,16},{24,28},{28,24},{1,5},{5... | collective-permute-start | bytes 884744 | tf_op jit(solution)/shard_map/ppermute | solution.py:20
  33.4 1.1 %collective-permute-done.11.refs_10_ = bf16[64,896]{1,0:T(8,128)(2,1)S(1)} collective-permute-done((bf16[64,896]{1,0:T(8,128)(2,1)S(1)}, bf16[64,896]{1,0:T(8,128)(2,1)S(1)}, u32[]{:S(2)}, u32[]{:S(2)}) %collective-permute-start.11) | collective-permute-done | bytes 114720 | tf_op jit(solution)/shard_map/ppermute | solution.py:20
  34.5 6.2 %experts.2 = (bf16[512,896]{1,0:T(8,128)(2,1)S(1)}, bf16[512,896]{1,0:T(8,128)(2,1)S(1)}, bf16[3,256,3584]{2,1,0:T(8,128)(2,1)S(1)}) custom-call(s32[2]{0:T(128)S(1)} %pad_add_fusion.ranks_ref, bf16[64,3584]{1,0:T(8,128)(2,1)S(1)} %copy-done, bf16[64,1024]{1,0:T(8,128)(2,1)S(1)} %get-tuple-element.58.refs_1_, ...), custom_call_target="tpu_custom_call" | custom-call | tf_op jit(solution)/shard_map/experts/pallas_call | solution.py:307
  41.7 2.4 %collective-permute-start.20 = (bf16[576,256]{1,0:T(8,128)(2,1)S(1)}, bf16[576,256]{1,0:T(8,128)(2,1)S(1)}, u32[]{:S(2)}, u32[]{:S(2)}) collective-permute-start(bf16[576,256]{1,0:T(8,128)(2,1)S(1)} %broadcast_select_fusion.2), channel_id=1, source_target_pairs={{0,8},{4,12},{8,0},{12,4},{16,24},{20,28},{24,16},{28,20},{1,9},{5... | collective-permute-start | bytes 884744 | tf_op jit(solution)/shard_map/ppermute | solution.py:20
  45.1 1.5 %collective-permute-start.18 = (bf16[128,896]{1,0:T(8,128)(2,1)S(1)}, bf16[128,896]{1,0:T(8,128)(2,1)S(1)}, u32[]{:S(2)}, u32[]{:S(2)}) collective-permute-start(bf16[128,896]{1,0:T(8,128)(2,1)S(1)} %slice.104), channel_id=1, source_target_pairs={{0,2},{1,3},{2,0},{3,1},{4,6},{5,7},{6,4},{7,5},{8,10},{9,11},{10,... | collective-permute-start | bytes 688136 | tf_op jit(solution)/shard_map/ppermute | solution.py:20
  46.6 5.6 %experts.3 = (bf16[512,896]{1,0:T(8,128)(2,1)S(1)}, bf16[512,896]{1,0:T(8,128)(2,1)S(1)}) custom-call(s32[2]{0:T(128)S(1)} %pad_add_fusion.ranks_ref, bf16[256,1024]{1,0:T(8,128)(2,1)S(1)} %constant_dynamic-update-slice_fusion.2.refs_0_, bf16[256,1024]{1,0:T(8,128)(2,1)S(1)} %collective-permute-done.13.refs_1_, bf16[128,896]{1,0:T(8,128)(2,1)S(1)} %slice.84.refs_2_, ...), custom_call_target="tpu_custom_call" | custom-call | tf_op jit(solution)/shard_map/experts/pallas_call | solution.py:307
  52.9 1.5 %collective-permute-start.24 = (bf16[64,896]{1,0:T(8,128)(2,1)S(1)}, bf16[64,896]{1,0:T(8,128)(2,1)S(1)}, u32[]{:S(2)}, u32[]{:S(2)}) collective-permute-start(bf16[64,896]{1,0:T(8,128)(2,1)S(1)} %get-tuple-element.115), channel_id=1, source_target_pairs={{0,4},{4,0},{8,12},{12,8},{16,20},{20,16},{24,28},{28,24},{1,5},{5... | collective-permute-start | bytes 344072 | tf_op jit(solution)/shard_map/ppermute | solution.py:20
  54.4 1.5 %collective-permute-start.25 = (bf16[64,896]{1,0:T(8,128)(2,1)S(1)}, bf16[64,896]{1,0:T(8,128)(2,1)S(1)}, u32[]{:S(2)}, u32[]{:S(2)}) collective-permute-start(bf16[64,896]{1,0:T(8,128)(2,1)S(1)} %get-tuple-element.114), channel_id=1, source_target_pairs={{0,2},{1,3},{2,0},{3,1},{4,6},{5,7},{6,4},{7,5},{8,10},{9,11},{10,... | collective-permute-start | bytes 344072 | tf_op jit(solution)/shard_map/ppermute | solution.py:20
  56.2 0.9 %collective-permute-start.22 = (bf16[64,896]{1,0:T(8,128)(2,1)S(1)}, bf16[64,896]{1,0:T(8,128)(2,1)S(1)}, u32[]{:S(2)}, u32[]{:S(2)}) collective-permute-start(bf16[64,896]{1,0:T(8,128)(2,1)S(1)} %get-tuple-element.121), channel_id=1, source_target_pairs={{0,2},{1,3},{2,0},{3,1},{4,6},{5,7},{6,4},{7,5},{8,10},{9,11},{10,... | collective-permute-start | bytes 344072 | tf_op jit(solution)/shard_map/ppermute | solution.py:20
  57.2 1.5 %collective-permute-start.23 = (bf16[64,896]{1,0:T(8,128)(2,1)S(1)}, bf16[64,896]{1,0:T(8,128)(2,1)S(1)}, u32[]{:S(2)}, u32[]{:S(2)}) collective-permute-start(bf16[64,896]{1,0:T(8,128)(2,1)S(1)} %get-tuple-element.120), channel_id=1, source_target_pairs={{0,4},{4,0},{8,12},{12,8},{16,20},{20,16},{24,28},{28,24},{1,5},{5... | collective-permute-start | bytes 344072 | tf_op jit(solution)/shard_map/ppermute | solution.py:20
  58.7 2.3 %collective-permute-start.28 = (bf16[576,256]{1,0:T(8,128)(2,1)S(1)}, bf16[576,256]{1,0:T(8,128)(2,1)S(1)}, u32[]{:S(2)}, u32[]{:S(2)}) collective-permute-start(bf16[576,256]{1,0:T(8,128)(2,1)S(1)} %broadcast_select_fusion.1), channel_id=1, source_target_pairs={{0,16},{4,20},{8,24},{12,28},{16,0},{20,4},{24,8},{28,12},{1,17},{... | collective-permute-start | bytes 884744 | tf_op jit(solution)/shard_map/ppermute | solution.py:20
  61.0 1.1 %collective-permute-done.22 = bf16[64,896]{1,0:T(8,128)(2,1)S(1)} collective-permute-done((bf16[64,896]{1,0:T(8,128)(2,1)S(1)}, bf16[64,896]{1,0:T(8,128)(2,1)S(1)}, u32[]{:S(2)}, u32[]{:S(2)}) %collective-permute-start.22) | collective-permute-done | bytes 114720 | tf_op jit(solution)/shard_map/ppermute | solution.py:20
  62.2 1.6 %collective-permute-start.27 = (bf16[128,896]{1,0:T(8,128)(2,1)S(1)}, bf16[128,896]{1,0:T(8,128)(2,1)S(1)}, u32[]{:S(2)}, u32[]{:S(2)}) collective-permute-start(bf16[128,896]{1,0:T(8,128)(2,1)S(1)} %add_convert_fusion.3), channel_id=1, source_target_pairs={{0,2},{1,3},{2,0},{3,1},{4,6},{5,7},{6,4},{7,5},{8,10},{9,11},{10,... | collective-permute-start | bytes 688136 | tf_op jit(solution)/shard_map/ppermute | solution.py:20
  64.5 1.3 %collective-permute-start.31 = (bf16[64,896]{1,0:T(8,128)(2,1)S(1)}, bf16[64,896]{1,0:T(8,128)(2,1)S(1)}, u32[]{:S(2)}, u32[]{:S(2)}) collective-permute-start(bf16[64,896]{1,0:T(8,128)(2,1)S(1)} %add_convert_fusion.6), channel_id=1, source_target_pairs={{0,8},{4,12},{8,0},{12,4},{16,24},{20,28},{24,16},{28,20},{1,9},{5... | collective-permute-start | bytes 344072 | tf_op jit(solution)/shard_map/ppermute | solution.py:20
  65.7 4.9 %attend_local.3.old_ref = bf16[16,128,512]{2,1,0:T(8,128)(2,1)} custom-call(s32[2]{0:T(128)S(1)} %pad_add_fusion.ranks_ref, s32[512]{0:T(512)S(1)} %copy-done.1, bf16[16,576,128]{2,1,0:T(8,128)(2,1)} %bitcast.13, bf16[16,576,256]{2,1,0:T(8,128)(2,1)} %bitcast.11, bf16[16,128,512]{2,1,0:T(8,128)(2,1)} %attend_local.2.refs_0_), custom_call_target="tpu_custom_call", output_to_operand_aliasing={{}: (4, {})} | custom-call | tf_op jit(solution)/shard_map/attend_local/pallas_call | solution.py:130
  70.6 3.9 %collective-permute-done.28 = bf16[576,256]{1,0:T(8,128)(2,1)S(1)} collective-permute-done((bf16[576,256]{1,0:T(8,128)(2,1)S(1)}, bf16[576,256]{1,0:T(8,128)(2,1)S(1)}, u32[]{:S(2)}, u32[]{:S(2)}) %collective-permute-start.28) | collective-permute-done | bytes 294944 | tf_op jit(solution)/shard_map/ppermute | solution.py:20
  74.8 2.6 %collective-permute-start.30 = (bf16[64,896]{1,0:T(8,128)(2,1)S(1)}, bf16[64,896]{1,0:T(8,128)(2,1)S(1)}, u32[]{:S(2)}, u32[]{:S(2)}) collective-permute-start(bf16[64,896]{1,0:T(8,128)(2,1)S(1)} %get-tuple-element.122), channel_id=1, source_target_pairs={{0,24},{4,28},{8,16},{12,20},{16,8},{20,12},{24,0},{28,4},{1,25},{... | collective-permute-start | bytes 344072 | tf_op jit(solution)/shard_map/ppermute | solution.py:20
  77.4 2.7 %attend_traded.1 = bf16[16,128,512]{2,1,0:T(8,128)(2,1)} custom-call(s32[2]{0:T(128)S(1)} %pad_add_fusion.ranks_ref, s32[512]{0:T(512)S(1)} %copy-done.1, s32[32]{0:T(128)S(1)} %copy-done.2, s32[1]{0:T(128)S(6)} %copy.19.mask_ref, bf16[16,576,128]{2,1,0:T(8,128)(2,1)} %bitcast.14, ...), custom_call_target="tpu_custom_call", output_to_operand_aliasing={{}: (6, {})} | custom-call | flops 71303168 | bytes 573440 | tf_op jit(solution)/shard_map/attend_traded/pallas_call | solution.py:191
  80.1 4.7 %collective-permute-done.29 = bf16[64,896]{1,0:T(8,128)(2,1)S(1)} collective-permute-done((bf16[64,896]{1,0:T(8,128)(2,1)S(1)}, bf16[64,896]{1,0:T(8,128)(2,1)S(1)}, u32[]{:S(2)}, u32[]{:S(2)}) %collective-permute-start.29) | collective-permute-done | bytes 114720 | tf_op jit(solution)/shard_map/ppermute | solution.py:20
  84.9 0.7 add_convert_fusion.5
  (75 shorter events, 6.0 us)
Async XLA Ops:
  2.6 7.4 %collective-permute-start = (bf16[64,1024]{1,0:T(8,128)(2,1)S(1)}, bf16[64,1024]{1,0:T(8,128)(2,1)S(1)}, u32[]{:S(2)}, u32[]{:S(2)}) collective-permute-start(bf16[64,1024]{1,0:T(8,128)(2,1)S(1)} %get-tuple-element.58.refs_1_), channel_id=1, source_target_pairs={{0,8},{4,12},{8,0},{12,4},{16,24},{20,28},{24,16},{28,20},{1,9},{5... | collective-permute-start | bytes 393224 | tf_op jit(solution)/shard_map/ppermute | solution.py:20
  5.7 13.8 %collective-permute-start.3 = (bf16[64,1920]{1,0:T(8,128)(2,1)S(1)}, bf16[64,1920]{1,0:T(8,128)(2,1)S(1)}, u32[]{:S(2)}, u32[]{:S(2)}) collective-permute-start(bf16[64,1920]{1,0:T(8,128)(2,1)S(1)} %get-tuple-element.65), channel_id=1, source_target_pairs={{0,4},{4,0},{8,12},{12,8},{16,20},{20,16},{24,28},{28,24},{1,5},{5... | collective-permute-start | bytes 737288 | tf_op jit(solution)/shard_map/ppermute | solution.py:20
  7.2 12.3 %collective-permute-start.4 = (bf16[64,1024]{1,0:T(8,128)(2,1)S(1)}, bf16[64,1024]{1,0:T(8,128)(2,1)S(1)}, u32[]{:S(2)}, u32[]{:S(2)}) collective-permute-start(bf16[64,1024]{1,0:T(8,128)(2,1)S(1)} %get-tuple-element.58.refs_1_), channel_id=1, source_target_pairs={{0,16},{4,20},{8,24},{12,28},{16,0},{20,4},{24,8},{28,12},{1,17},{... | collective-permute-start | bytes 393224 | tf_op jit(solution)/shard_map/ppermute | solution.py:20
  9.8 9.7 %collective-permute-start.5 = (bf16[64,1024]{1,0:T(8,128)(2,1)S(1)}, bf16[64,1024]{1,0:T(8,128)(2,1)S(1)}, u32[]{:S(2)}, u32[]{:S(2)}) collective-permute-start(bf16[64,1024]{1,0:T(8,128)(2,1)S(1)} %get-tuple-element.58.refs_1_), channel_id=1, source_target_pairs={{0,24},{4,28},{8,16},{12,20},{16,8},{20,12},{24,0},{28,4},{1,25},{... | collective-permute-start | bytes 393224 | tf_op jit(solution)/shard_map/ppermute | solution.py:20
  10.0 9.5 %collective-permute-start.2 = (bf16[64,1024]{1,0:T(8,128)(2,1)S(1)}, bf16[64,1024]{1,0:T(8,128)(2,1)S(1)}, u32[]{:S(2)}, u32[]{:S(2)}) collective-permute-start(bf16[64,1024]{1,0:T(8,128)(2,1)S(1)} %collective-permute-done.refs_4_), channel_id=1, source_target_pairs={{0,4},{4,0},{8,12},{12,8},{16,20},{20,16},{24,28},{28,24},{1,5},{5... | collective-permute-start | bytes 393224 | tf_op jit(solution)/shard_map/ppermute | solution.py:20
  12.3 7.2 %collective-permute-start.1 = (bf16[64,896]{1,0:T(8,128)(2,1)S(1)}, bf16[64,896]{1,0:T(8,128)(2,1)S(1)}, u32[]{:S(2)}, u32[]{:S(2)}) collective-permute-start(bf16[64,896]{1,0:T(8,128)(2,1)S(1)} %slice.79), channel_id=1, source_target_pairs={{0,2},{1,3},{2,0},{3,1},{4,6},{5,7},{6,4},{7,5},{8,10},{9,11},{10,... | collective-permute-start | bytes 344072 | tf_op jit(solution)/shard_map/ppermute | solution.py:20
  19.6 11.1 %collective-permute-start.6 = (bf16[192,896]{1,0:T(8,128)(2,1)S(1)}, bf16[192,896]{1,0:T(8,128)(2,1)S(1)}, u32[]{:S(2)}, u32[]{:S(2)}) collective-permute-start(bf16[192,896]{1,0:T(8,128)(2,1)S(1)} %pad_maximum_fusion), channel_id=1, source_target_pairs={{0,2},{1,3},{2,0},{3,1},{4,6},{5,7},{6,4},{7,5},{8,10},{9,11},{10,... | collective-permute-start | bytes 1032200 | tf_op jit(solution)/shard_map/ppermute | solution.py:20
  21.2 2.7 %collective-permute-start.8 = (bf16[128,1024]{1,0:T(8,128)(2,1)S(1)}, bf16[128,1024]{1,0:T(8,128)(2,1)S(1)}, u32[]{:S(2)}, u32[]{:S(2)}) collective-permute-start(bf16[128,1024]{1,0:T(8,128)(2,1)S(1)} %pad_maximum_fusion.1), channel_id=1, source_target_pairs={{0,1},{1,0},{2,3},{3,2},{4,5},{5,4},{6,7},{7,6},{8,9},{9,8},{10,11... | collective-permute-start | bytes 786440 | tf_op jit(solution)/shard_map/ppermute | solution.py:20
  21.3 9.4 %collective-permute-start.7 = (bf16[128,1024]{1,0:T(8,128)(2,1)S(1)}, bf16[128,1024]{1,0:T(8,128)(2,1)S(1)}, u32[]{:S(2)}, u32[]{:S(2)}) collective-permute-start(bf16[128,1024]{1,0:T(8,128)(2,1)S(1)} %constant_dynamic-update-slice_fusion), channel_id=1, source_target_pairs={{0,4},{4,0},{8,12},{12,8},{16,20},{20,16},{24,28},{28,24},{1,5},{5... | collective-permute-start | bytes 786440 | tf_op jit(solution)/shard_map/ppermute | solution.py:20
  22.3 1.7 %collective-permute-start.9 = (bf16[64,1920]{1,0:T(8,128)(2,1)S(1)}, bf16[64,1920]{1,0:T(8,128)(2,1)S(1)}, u32[]{:S(2)}, u32[]{:S(2)}) collective-permute-start(bf16[64,1920]{1,0:T(8,128)(2,1)S(1)} %collective-permute-done.3.refs_2_), channel_id=1, source_target_pairs={{0,1},{1,0},{2,3},{3,2},{4,5},{5,4},{6,7},{7,6},{8,9},{9,8},{10,11... | collective-permute-start | bytes 737288 | tf_op jit(solution)/shard_map/ppermute | solution.py:20
  22.4 1.5 %collective-permute-start.10 = (bf16[64,896]{1,0:T(8,128)(2,1)S(1)}, bf16[64,896]{1,0:T(8,128)(2,1)S(1)}, u32[]{:S(2)}, u32[]{:S(2)}) collective-permute-start(bf16[64,896]{1,0:T(8,128)(2,1)S(1)} %collective-permute-done.1.refs_7_), channel_id=1, source_target_pairs={{0,1},{1,0},{2,3},{3,2},{4,5},{5,4},{6,7},{7,6},{8,9},{9,8},{10,11... | collective-permute-start | bytes 344072 | tf_op jit(solution)/shard_map/ppermute | solution.py:20
  30.8 9.9 %collective-permute-start.13 = (bf16[256,1024]{1,0:T(8,128)(2,1)S(1)}, bf16[256,1024]{1,0:T(8,128)(2,1)S(1)}, u32[]{:S(2)}, u32[]{:S(2)}) collective-permute-start(bf16[256,1024]{1,0:T(8,128)(2,1)S(1)} %constant_dynamic-update-slice_fusion.2.refs_0_), channel_id=1, source_target_pairs={{0,1},{1,0},{2,3},{3,2},{4,5},{5,4},{6,7},{7,6},{8,9},{9,8},{10,11... | collective-permute-start | bytes 1572872 | tf_op jit(solution)/shard_map/ppermute | solution.py:20
  31.0 9.7 %collective-permute-start.15 = (bf16[576,256]{1,0:T(8,128)(2,1)S(1)}, bf16[576,256]{1,0:T(8,128)(2,1)S(1)}, u32[]{:S(2)}, u32[]{:S(2)}) collective-permute-start(bf16[576,256]{1,0:T(8,128)(2,1)S(1)} %get-tuple-element.83), channel_id=1, source_target_pairs={{0,4},{4,0},{8,12},{12,8},{16,20},{20,16},{24,28},{28,24},{1,5},{5... | collective-permute-start | bytes 884744 | tf_op jit(solution)/shard_map/ppermute | solution.py:20
  32.1 8.6 %collective-permute-start.12 = (bf16[128,896]{1,0:T(8,128)(2,1)S(1)}, bf16[128,896]{1,0:T(8,128)(2,1)S(1)}, u32[]{:S(2)}, u32[]{:S(2)}) collective-permute-start(bf16[128,896]{1,0:T(8,128)(2,1)S(1)} %slice.83), channel_id=1, source_target_pairs={{0,2},{1,3},{2,0},{3,1},{4,6},{5,7},{6,4},{7,5},{8,10},{9,11},{10,... | collective-permute-start | bytes 688136 | tf_op jit(solution)/shard_map/ppermute | solution.py:20
  32.7 7.9 %collective-permute-start.14 = (bf16[128,896]{1,0:T(8,128)(2,1)S(1)}, bf16[128,896]{1,0:T(8,128)(2,1)S(1)}, u32[]{:S(2)}, u32[]{:S(2)}) collective-permute-start(bf16[128,896]{1,0:T(8,128)(2,1)S(1)} %slice.84.refs_2_), channel_id=1, source_target_pairs={{0,1},{1,0},{2,3},{3,2},{4,5},{5,4},{6,7},{7,6},{8,9},{9,8},{10,11... | collective-permute-start | bytes 688136 | tf_op jit(solution)/shard_map/ppermute | solution.py:20
  32.8 1.6 %collective-permute-start.11 = (bf16[64,896]{1,0:T(8,128)(2,1)S(1)}, bf16[64,896]{1,0:T(8,128)(2,1)S(1)}, u32[]{:S(2)}, u32[]{:S(2)}) collective-permute-start(bf16[64,896]{1,0:T(8,128)(2,1)S(1)} %slice.82.refs_9_), channel_id=1, source_target_pairs={{0,1},{1,0},{2,3},{3,2},{4,5},{5,4},{6,7},{7,6},{8,9},{9,8},{10,11... | collective-permute-start | bytes 344072 | tf_op jit(solution)/shard_map/ppermute | solution.py:20
  40.7 3.4 %collective-permute-start.17 = (bf16[512,896]{1,0:T(8,128)(2,1)S(1)}, bf16[512,896]{1,0:T(8,128)(2,1)S(1)}, u32[]{:S(2)}, u32[]{:S(2)}) collective-permute-start(bf16[512,896]{1,0:T(8,128)(2,1)S(1)} %get-tuple-element.91), channel_id=1, source_target_pairs={{0,1},{1,0},{2,3},{3,2},{4,5},{5,4},{6,7},{7,6},{8,9},{9,8},{10,11... | collective-permute-start | bytes 2752520 | tf_op jit(solution)/shard_map/ppermute | solution.py:20
  41.7 10.4 %collective-permute-start.20 = (bf16[576,256]{1,0:T(8,128)(2,1)S(1)}, bf16[576,256]{1,0:T(8,128)(2,1)S(1)}, u32[]{:S(2)}, u32[]{:S(2)}) collective-permute-start(bf16[576,256]{1,0:T(8,128)(2,1)S(1)} %broadcast_select_fusion.2), channel_id=1, source_target_pairs={{0,8},{4,12},{8,0},{12,4},{16,24},{20,28},{24,16},{28,20},{1,9},{5... | collective-permute-start | bytes 884744 | tf_op jit(solution)/shard_map/ppermute | solution.py:20
  44.1 2.5 %collective-permute-start.16 = (bf16[128,896]{1,0:T(8,128)(2,1)S(1)}, bf16[128,896]{1,0:T(8,128)(2,1)S(1)}, u32[]{:S(2)}, u32[]{:S(2)}) collective-permute-start(bf16[128,896]{1,0:T(8,128)(2,1)S(1)} %collective-permute-done.12.refs_4_), channel_id=1, source_target_pairs={{0,1},{1,0},{2,3},{3,2},{4,5},{5,4},{6,7},{7,6},{8,9},{9,8},{10,11... | collective-permute-start | bytes 688136 | tf_op jit(solution)/shard_map/ppermute | solution.py:20
  44.4 8.1 %collective-permute-start.19 = (bf16[64,1792]{1,0:T(8,128)(2,1)S(1)}, bf16[64,1792]{1,0:T(8,128)(2,1)S(1)}, u32[]{:S(2)}, u32[]{:S(2)}) collective-permute-start(bf16[64,1792]{1,0:T(8,128)(2,1)S(1)} %pad_maximum_fusion.2), channel_id=1, source_target_pairs={{0,4},{4,0},{8,12},{12,8},{16,20},{20,16},{24,28},{28,24},{1,5},{5... | collective-permute-start | bytes 688136 | tf_op jit(solution)/shard_map/ppermute | solution.py:20
  45.1 7.7 %collective-permute-start.18 = (bf16[128,896]{1,0:T(8,128)(2,1)S(1)}, bf16[128,896]{1,0:T(8,128)(2,1)S(1)}, u32[]{:S(2)}, u32[]{:S(2)}) collective-permute-start(bf16[128,896]{1,0:T(8,128)(2,1)S(1)} %slice.104), channel_id=1, source_target_pairs={{0,2},{1,3},{2,0},{3,1},{4,6},{5,7},{6,4},{7,5},{8,10},{9,11},{10,... | collective-permute-start | bytes 688136 | tf_op jit(solution)/shard_map/ppermute | solution.py:20
  52.8 3.1 %collective-permute-start.21 = (bf16[512,896]{1,0:T(8,128)(2,1)S(1)}, bf16[512,896]{1,0:T(8,128)(2,1)S(1)}, u32[]{:S(2)}, u32[]{:S(2)}) collective-permute-start(bf16[512,896]{1,0:T(8,128)(2,1)S(1)} %get-tuple-element.94), channel_id=1, source_target_pairs={{0,1},{1,0},{2,3},{3,2},{4,5},{5,4},{6,7},{7,6},{8,9},{9,8},{10,11... | collective-permute-start | bytes 2752520 | tf_op jit(solution)/shard_map/ppermute | solution.py:20
  52.9 8.1 %collective-permute-start.24 = (bf16[64,896]{1,0:T(8,128)(2,1)S(1)}, bf16[64,896]{1,0:T(8,128)(2,1)S(1)}, u32[]{:S(2)}, u32[]{:S(2)}) collective-permute-start(bf16[64,896]{1,0:T(8,128)(2,1)S(1)} %get-tuple-element.115), channel_id=1, source_target_pairs={{0,4},{4,0},{8,12},{12,8},{16,20},{20,16},{24,28},{28,24},{1,5},{5... | collective-permute-start | bytes 344072 | tf_op jit(solution)/shard_map/ppermute | solution.py:20
  54.4 6.6 %collective-permute-start.25 = (bf16[64,896]{1,0:T(8,128)(2,1)S(1)}, bf16[64,896]{1,0:T(8,128)(2,1)S(1)}, u32[]{:S(2)}, u32[]{:S(2)}) collective-permute-start(bf16[64,896]{1,0:T(8,128)(2,1)S(1)} %get-tuple-element.114), channel_id=1, source_target_pairs={{0,2},{1,3},{2,0},{3,1},{4,6},{5,7},{6,4},{7,5},{8,10},{9,11},{10,... | collective-permute-start | bytes 344072 | tf_op jit(solution)/shard_map/ppermute | solution.py:20
  56.2 5.9 %collective-permute-start.22 = (bf16[64,896]{1,0:T(8,128)(2,1)S(1)}, bf16[64,896]{1,0:T(8,128)(2,1)S(1)}, u32[]{:S(2)}, u32[]{:S(2)}) collective-permute-start(bf16[64,896]{1,0:T(8,128)(2,1)S(1)} %get-tuple-element.121), channel_id=1, source_target_pairs={{0,2},{1,3},{2,0},{3,1},{4,6},{5,7},{6,4},{7,5},{8,10},{9,11},{10,... | collective-permute-start | bytes 344072 | tf_op jit(solution)/shard_map/ppermute | solution.py:20
  57.2 4.9 %collective-permute-start.23 = (bf16[64,896]{1,0:T(8,128)(2,1)S(1)}, bf16[64,896]{1,0:T(8,128)(2,1)S(1)}, u32[]{:S(2)}, u32[]{:S(2)}) collective-permute-start(bf16[64,896]{1,0:T(8,128)(2,1)S(1)} %get-tuple-element.120), channel_id=1, source_target_pairs={{0,4},{4,0},{8,12},{12,8},{16,20},{20,16},{24,28},{28,24},{1,5},{5... | collective-permute-start | bytes 344072 | tf_op jit(solution)/shard_map/ppermute | solution.py:20
  58.7 15.9 %collective-permute-start.28 = (bf16[576,256]{1,0:T(8,128)(2,1)S(1)}, bf16[576,256]{1,0:T(8,128)(2,1)S(1)}, u32[]{:S(2)}, u32[]{:S(2)}) collective-permute-start(bf16[576,256]{1,0:T(8,128)(2,1)S(1)} %broadcast_select_fusion.1), channel_id=1, source_target_pairs={{0,16},{4,20},{8,24},{12,28},{16,0},{20,4},{24,8},{28,12},{1,17},{... | collective-permute-start | bytes 884744 | tf_op jit(solution)/shard_map/ppermute | solution.py:20
  62.2 12.4 %collective-permute-start.27 = (bf16[128,896]{1,0:T(8,128)(2,1)S(1)}, bf16[128,896]{1,0:T(8,128)(2,1)S(1)}, u32[]{:S(2)}, u32[]{:S(2)}) collective-permute-start(bf16[128,896]{1,0:T(8,128)(2,1)S(1)} %add_convert_fusion.3), channel_id=1, source_target_pairs={{0,2},{1,3},{2,0},{3,1},{4,6},{5,7},{6,4},{7,5},{8,10},{9,11},{10,... | collective-permute-start | bytes 688136 | tf_op jit(solution)/shard_map/ppermute | solution.py:20
  63.8 10.8 %collective-permute-start.26 = (bf16[128,896]{1,0:T(8,128)(2,1)S(1)}, bf16[128,896]{1,0:T(8,128)(2,1)S(1)}, u32[]{:S(2)}, u32[]{:S(2)}) collective-permute-start(bf16[128,896]{1,0:T(8,128)(2,1)S(1)} %add_convert_fusion.4), channel_id=1, source_target_pairs={{0,4},{4,0},{8,12},{12,8},{16,20},{20,16},{24,28},{28,24},{1,5},{5... | collective-permute-start | bytes 688136 | tf_op jit(solution)/shard_map/ppermute | solution.py:20
  64.5 15.6 %collective-permute-start.31 = (bf16[64,896]{1,0:T(8,128)(2,1)S(1)}, bf16[64,896]{1,0:T(8,128)(2,1)S(1)}, u32[]{:S(2)}, u32[]{:S(2)}) collective-permute-start(bf16[64,896]{1,0:T(8,128)(2,1)S(1)} %add_convert_fusion.6), channel_id=1, source_target_pairs={{0,8},{4,12},{8,0},{12,4},{16,24},{20,28},{24,16},{28,20},{1,9},{5... | collective-permute-start | bytes 344072 | tf_op jit(solution)/shard_map/ppermute | solution.py:20
  74.7 10.2 %collective-permute-start.29 = (bf16[64,896]{1,0:T(8,128)(2,1)S(1)}, bf16[64,896]{1,0:T(8,128)(2,1)S(1)}, u32[]{:S(2)}, u32[]{:S(2)}) collective-permute-start(bf16[64,896]{1,0:T(8,128)(2,1)S(1)} %get-tuple-element.123), channel_id=1, source_target_pairs={{0,16},{4,20},{8,24},{12,28},{16,0},{20,4},{24,8},{28,12},{1,17},{... | collective-permute-start | bytes 344072 | tf_op jit(solution)/shard_map/ppermute | solution.py:20
  74.8 10.1 %collective-permute-start.30 = (bf16[64,896]{1,0:T(8,128)(2,1)S(1)}, bf16[64,896]{1,0:T(8,128)(2,1)S(1)}, u32[]{:S(2)}, u32[]{:S(2)}) collective-permute-start(bf16[64,896]{1,0:T(8,128)(2,1)S(1)} %get-tuple-element.122), channel_id=1, source_target_pairs={{0,24},{4,28},{8,16},{12,20},{16,8},{20,12},{24,0},{28,4},{1,25},{... | collective-permute-start | bytes 344072 | tf_op jit(solution)/shard_map/ppermute | solution.py:20
  (3 other events, 16.4 us)

commit v10 on v9

--- a/solution.py
+++ b/solution.py
@@ -415,12 +415,18 @@
     early = [flip(array, "tp", 1) for array in (both_1, far_2)]
     queries, near_23, early = tie((queries, near_23, early))
     count = queries.shape[0]
-    some = count * 5 // 8
+    some = count // 2
     attended = attend_part(ranks, lengths, queries, cache_pages, groups, 0, some)
-    far_3, near_late, near_odds, attended, page = tie(
-        (far_3, near_late, near_odds, attended, page)
-    )
-    far_3, far_late = cut(far_3, 0, 1), cut(far_3, 1, len(late))
+    upper, lower = jnp.split(page, 2, axis=0)
+    swapped, upper = page_far(upper)
+    far_3, near_late, near_odds, attended, swapped = tie(
+        (far_3, near_late, near_odds, attended, swapped)
+    )
+    upper = page_take(upper, swapped, 2) if levels > 2 else upper
+    page = jnp.concatenate([upper, lower], axis=0)
+    core_3 = flip(far_3, "tp", 1)
+    far_late, core_late = cut(far_3, 1, len(late)), cut(core_3, 1, len(late))
+    far_3, core_3 = cut(far_3, 0, 1), cut(core_3, 0, 1)
     far_odds = flip(bare(near_odds), "tp", 2)
 
     def piece(start, part, array):
@@ -430,12 +436,12 @@
     pieces += [(rows, (0, 2), True, both_1), (rows, (1, 3), False, early[0])]
     pieces += [piece(2, 0, near_2), piece(3, 0, near_3), (2 * rows, (1,), False, near_23)]
     pieces += [piece(2, 2, far_2), piece(2, 3, early[1])]
-    pieces += [piece(3, 2, far_3), piece(3, 3, flip(far_3, "tp", 1))]
+    pieces += [piece(3, 2, far_3), piece(3, 3, core_3)]
     *first, w_down = run_experts(
         ranks, pieces, w_gate, w_up, w_down, 4 * rows, columns, top, True
     )
     near_both = jnp.concatenate([near_late, near_odds], axis=0)
-    early = [flip(array, "tp", 1) for array in (near_both, far_late)]
+    early = flip(near_both, "tp", 1)
     swapped = flip(page, "ep", 1)
     first, far_odds, early, swapped = tie((first, far_odds, early, swapped))
     page = page_take(page, swapped, 0)
@@ -450,8 +456,8 @@
     over_1 = flip(jnp.concatenate([cut(kept, 1, 1), cut(sent, 1, 1)], axis=1), "ep", 1)
     swapped = flip(page, "ep", 2)
     odds = len(late)
-    pieces = [piece(0, 0, near_both), (0, (1,), False, early[0])]
-    pieces += [piece(0, 2, far_late), piece(0, 3, early[1])]
+    pieces = [piece(0, 0, near_both), (0, (1,), False, early)]
+    pieces += [piece(0, 2, far_late), piece(0, 3, core_late)]
     pieces += [piece(odds, 2, far_odds), piece(odds, 3, last)]
     second = [
         *run_experts(
@@ -459,7 +465,9 @@
         )
     ]
     second, over_23, over_1, swapped = tie((second, over_23, over_1, swapped))
-    swapped, page = page_far(page_take(page, swapped, 1))
+    page = page_take(page, swapped, 1)
+    upper, lower = jnp.split(page, 2, axis=0)
+    swapped, lower = page_far(lower)
     late_sent, late_kept = add_core(*second)
     over_3 = flip(total_of(cut(kept, 3, 1), cut(over_23, 1, 1)), "ep", 1)
     zero = flip(total_of(cut(sent, 0, 1), over_1[:, columns:]), "tp", 2)
@@ -478,8 +486,8 @@
         ranks, lengths, queries, cache_pages, groups, some, count - some, attended
     )
     odd, even, attended, swapped = tie((odd, even, attended, swapped))
-    if levels > 2:
-        page = page_take(page, swapped, 2)
+    lower = page_take(lower, swapped, 2) if levels > 2 else lower
+    page = jnp.concatenate([upper, lower], axis=0)
     even = total_of(cut(late_kept, 0, len(late)), even, odd)
     back = [flip(cut(even, i, 1), "ep", 2 * m) for i, m in enumerate(late)]
     back.append(flip(total_of(cut(kept, 2, 1), cut(over_23, 0, 1), over_3), "ep", 2))

time: 86 us -> 83.5 us (0.971)
  starting transfers between devices: 35.6 us -> 33.3 us
    ppermute x32, starting transfers between devices: 35.6 us -> 33.3 us  [flip(): return lax.ppermute(block, axis, [(i, i ^ apart) for i in range(count)])]
  transfers between devices with their start and end apart: 32 -> 32, of which waited for: 8 -> 13; matrix products, arithmetic and copies ran while one was open for 1% -> 2% of each run, Pallas kernels for 35% -> 36%
where the time goes in v10:
time: 83.5 us; the launch traced here: 83.1 us
  starting transfers between devices  33.3 us (40%)
  Pallas kernels  31.7 us (38%)
  waiting for transfers between devices  14.3 us (17%)
  other arithmetic  1.81 us (2%)
  between operations  1.66 us (2%)
    ppermute x32, starting transfers between devices, flip(): return lax.ppermute(block, axis, [(i, i ^ apart) for i in range(count)])  33.3 us
    ppermute x32, waiting for transfers between devices, flip(): return lax.ppermute(block, axis, [(i, i ^ apart) for i in range(count)])  14.3 us
    pallas_call x2, Pallas kernels, run_experts(): pl.pallas_call(kernel, out_shape=[pltpu.VMEM((2 * rows, columns), jnp.bfl...  11.8 us
    pallas_call x2, Pallas kernels, attend_part(): pl.pallas_call(kernel, out_shape=jax.ShapeDtypeStruct((count, heads, LAT)...  11.1 us
    pallas_call x1, Pallas kernels, load(): pl.pallas_call(load_kernel, out_shape=[pltpu.VMEM(w.shape, w.dtype) for w...  4.21 us
    pallas_call x1, Pallas kernels, attend_traded(): pl.pallas_call(functools.partial(attend_traded_kernel, groups), out_shape...  2.71 us
    pallas_call x1, Pallas kernels, pick(): pl.pallas_call(functools.partial(pick_kernel, groups), out_shape=(pltpu.V...  1.89 us
  transfers between devices with their start and end apart: 32, of which 13 were waited for; matrix products, arithmetic and copies ran while one was open for 2% of the time, Pallas kernels for 36%

profile of v10, /device:TPU:0, one launch (start us, length us, event | category | flops | bytes accessed | tf_op | source)
XLA Modules:
  0.0 83.1 jit_solution(17570097536402633843)
XLA Ops:
  0.7 1.9 %pick.1 = (bf16[64,1024]{1,0:T(8,128)(2,1)S(1)}, bf16[64,1920]{1,0:T(8,128)(2,1)S(1)}, bf16[576,256]{1,0:T(8,128)(2,1)S(1)}) custom-call(s32[2]{0:T(128)S(1)} %pad_add_fusion.ranks_ref, s32[32]{0:T(128)} %slots_ref.3, s32[8,64]{1,0:T(8,128)} %bitcast.15, f32[8,64]{1,0:T(8,128)} %bitcast.16, bf16[64,3584]{1,0:T(8,128)(2,1)} %refs_0_.2, ...), custom_call_target="tpu_custom_call" | custom-call | tf_op jit(solution)/shard_map/pick/pallas_call | solution.py:96
  2.6 3.1 %collective-permute-start = (bf16[64,1024]{1,0:T(8,128)(2,1)S(1)}, bf16[64,1024]{1,0:T(8,128)(2,1)S(1)}, u32[]{:S(2)}, u32[]{:S(2)}) collective-permute-start(bf16[64,1024]{1,0:T(8,128)(2,1)S(1)} %get-tuple-element.57.refs_1_), channel_id=1, source_target_pairs={{0,8},{4,12},{8,0},{12,4},{16,24},{20,28},{24,16},{28,20},{1,9},{5... | collective-permute-start | bytes 393224 | tf_op jit(solution)/shard_map/ppermute | solution.py:20
  5.7 1.5 %collective-permute-start.3 = (bf16[64,1920]{1,0:T(8,128)(2,1)S(1)}, bf16[64,1920]{1,0:T(8,128)(2,1)S(1)}, u32[]{:S(2)}, u32[]{:S(2)}) collective-permute-start(bf16[64,1920]{1,0:T(8,128)(2,1)S(1)} %get-tuple-element.64), channel_id=1, source_target_pairs={{0,4},{4,0},{8,12},{12,8},{16,20},{20,16},{24,28},{28,24},{1,5},{5... | collective-permute-start | bytes 737288 | tf_op jit(solution)/shard_map/ppermute | solution.py:20
  7.2 2.6 %collective-permute-start.4 = (bf16[64,1024]{1,0:T(8,128)(2,1)S(1)}, bf16[64,1024]{1,0:T(8,128)(2,1)S(1)}, u32[]{:S(2)}, u32[]{:S(2)}) collective-permute-start(bf16[64,1024]{1,0:T(8,128)(2,1)S(1)} %get-tuple-element.57.refs_1_), channel_id=1, source_target_pairs={{0,16},{4,20},{8,24},{12,28},{16,0},{20,4},{24,8},{28,12},{1,17},{... | collective-permute-start | bytes 393224 | tf_op jit(solution)/shard_map/ppermute | solution.py:20
  10.0 2.3 %collective-permute-start.2 = (bf16[64,1024]{1,0:T(8,128)(2,1)S(1)}, bf16[64,1024]{1,0:T(8,128)(2,1)S(1)}, u32[]{:S(2)}, u32[]{:S(2)}) collective-permute-start(bf16[64,1024]{1,0:T(8,128)(2,1)S(1)} %collective-permute-done.refs_4_), channel_id=1, source_target_pairs={{0,4},{4,0},{8,12},{12,8},{16,20},{20,16},{24,28},{28,24},{1,5},{5... | collective-permute-start | bytes 393224 | tf_op jit(solution)/shard_map/ppermute | solution.py:20
  12.3 1.5 %collective-permute-start.1 = (bf16[64,896]{1,0:T(8,128)(2,1)S(1)}, bf16[64,896]{1,0:T(8,128)(2,1)S(1)}, u32[]{:S(2)}, u32[]{:S(2)}) collective-permute-start(bf16[64,896]{1,0:T(8,128)(2,1)S(1)} %slice.85), channel_id=1, source_target_pairs={{0,2},{1,3},{2,0},{3,1},{4,6},{5,7},{6,4},{7,5},{8,10},{9,11},{10,... | collective-permute-start | bytes 344072 | tf_op jit(solution)/shard_map/ppermute | solution.py:20
  13.9 4.2 %load.1 = (bf16[3,3584,256]{2,1,0:T(8,128)(2,1)S(1)}, bf16[3,3584,256]{2,1,0:T(8,128)(2,1)S(1)}) custom-call(bf16[3,3584,256]{2,1,0:T(8,128)(2,1)} %refs_0_.1, bf16[3,3584,256]{2,1,0:T(8,128)(2,1)} %refs_1_), custom_call_target="tpu_custom_call" | custom-call | bytes 11010048 | tf_op jit(solution)/shard_map/load/pallas_call | solution.py:162
  18.1 1.4 %collective-permute-done.4 = bf16[64,1024]{1,0:T(8,128)(2,1)S(1)} collective-permute-done((bf16[64,1024]{1,0:T(8,128)(2,1)S(1)}, bf16[64,1024]{1,0:T(8,128)(2,1)S(1)}, u32[]{:S(2)}, u32[]{:S(2)}) %collective-permute-start.4) | collective-permute-done | bytes 131104 | tf_op jit(solution)/shard_map/ppermute | solution.py:20
  19.7 1.5 %collective-permute-start.6 = (bf16[192,896]{1,0:T(8,128)(2,1)S(1)}, bf16[192,896]{1,0:T(8,128)(2,1)S(1)}, u32[]{:S(2)}, u32[]{:S(2)}) collective-permute-start(bf16[192,896]{1,0:T(8,128)(2,1)S(1)} %pad_maximum_fusion), channel_id=1, source_target_pairs={{0,2},{1,3},{2,0},{3,1},{4,6},{5,7},{6,4},{7,5},{8,10},{9,11},{10,... | collective-permute-start | bytes 1032200 | tf_op jit(solution)/shard_map/ppermute | solution.py:20
  21.8 0.9 %collective-permute-start.7 = (bf16[128,1024]{1,0:T(8,128)(2,1)S(1)}, bf16[128,1024]{1,0:T(8,128)(2,1)S(1)}, u32[]{:S(2)}, u32[]{:S(2)}) collective-permute-start(bf16[128,1024]{1,0:T(8,128)(2,1)S(1)} %constant_dynamic-update-slice_fusion), channel_id=1, source_target_pairs={{0,4},{4,0},{8,12},{12,8},{16,20},{20,16},{24,28},{28,24},{1,5},{5... | collective-permute-start | bytes 786440 | tf_op jit(solution)/shard_map/ppermute | solution.py:20
  23.0 3.4 %collective-permute-start.11 = (bf16[288,256]{1,0:T(8,128)(2,1)S(1)}, bf16[288,256]{1,0:T(8,128)(2,1)S(1)}, u32[]{:S(2)}, u32[]{:S(2)}) collective-permute-start(bf16[288,256]{1,0:T(8,128)(2,1)S(1)} %split.20), channel_id=1, source_target_pairs={{0,16},{4,20},{8,24},{12,28},{16,0},{20,4},{24,8},{28,12},{1,17},{... | collective-permute-start | bytes 442376 | tf_op jit(solution)/shard_map/ppermute | solution.py:20
  27.0 5.6 %attend_local.2.refs_0_ = bf16[16,128,512]{2,1,0:T(8,128)(2,1)} custom-call(s32[2]{0:T(128)S(1)} %pad_add_fusion.ranks_ref, s32[512]{0:T(512)S(1)} %copy-done.1, bf16[16,576,128]{2,1,0:T(8,128)(2,1)} %bitcast.12, bf16[16,576,256]{2,1,0:T(8,128)(2,1)} %bitcast.10), custom_call_target="tpu_custom_call" | custom-call | tf_op jit(solution)/shard_map/attend_local/pallas_call | solution.py:130
  32.6 1.0 %collective-permute-done.11 = bf16[288,256]{1,0:T(8,128)(2,1)S(1)} collective-permute-done((bf16[288,256]{1,0:T(8,128)(2,1)S(1)}, bf16[288,256]{1,0:T(8,128)(2,1)S(1)}, u32[]{:S(2)}, u32[]{:S(2)}) %collective-permute-start.11) | collective-permute-done | bytes 147488 | tf_op jit(solution)/shard_map/ppermute | solution.py:20
  34.3 1.4 %collective-permute-start.15 = (bf16[576,256]{1,0:T(8,128)(2,1)S(1)}, bf16[576,256]{1,0:T(8,128)(2,1)S(1)}, u32[]{:S(2)}, u32[]{:S(2)}) collective-permute-start(bf16[576,256]{1,0:T(8,128)(2,1)S(1)} %pad_maximum_fusion.1), channel_id=1, source_target_pairs={{0,4},{4,0},{8,12},{12,8},{16,20},{20,16},{24,28},{28,24},{1,5},{5... | collective-permute-start | bytes 884744 | tf_op jit(solution)/shard_map/ppermute | solution.py:20
  36.4 6.2 %experts.2 = (bf16[512,896]{1,0:T(8,128)(2,1)S(1)}, bf16[512,896]{1,0:T(8,128)(2,1)S(1)}, bf16[3,256,3584]{2,1,0:T(8,128)(2,1)S(1)}) custom-call(s32[2]{0:T(128)S(1)} %pad_add_fusion.ranks_ref, bf16[64,3584]{1,0:T(8,128)(2,1)S(1)} %copy-done, bf16[64,1024]{1,0:T(8,128)(2,1)S(1)} %get-tuple-element.57.refs_1_, ...), custom_call_target="tpu_custom_call" | custom-call | tf_op jit(solution)/shard_map/experts/pallas_call | solution.py:307
  44.0 1.7 %collective-permute-done.17 = bf16[512,896]{1,0:T(8,128)(2,1)S(1)} collective-permute-done((bf16[512,896]{1,0:T(8,128)(2,1)S(1)}, bf16[512,896]{1,0:T(8,128)(2,1)S(1)}, u32[]{:S(2)}, u32[]{:S(2)}) %collective-permute-start.17) | collective-permute-done | bytes 917536 | tf_op jit(solution)/shard_map/ppermute | solution.py:20
  46.1 1.4 %collective-permute-start.19 = (bf16[64,1792]{1,0:T(8,128)(2,1)S(1)}, bf16[64,1792]{1,0:T(8,128)(2,1)S(1)}, u32[]{:S(2)}, u32[]{:S(2)}) collective-permute-start(bf16[64,1792]{1,0:T(8,128)(2,1)S(1)} %pad_maximum_fusion.4), channel_id=1, source_target_pairs={{0,4},{4,0},{8,12},{12,8},{16,20},{20,16},{24,28},{28,24},{1,5},{5... | collective-permute-start | bytes 688136 | tf_op jit(solution)/shard_map/ppermute | solution.py:20
  48.1 5.6 %experts.3 = (bf16[512,896]{1,0:T(8,128)(2,1)S(1)}, bf16[512,896]{1,0:T(8,128)(2,1)S(1)}) custom-call(s32[2]{0:T(128)S(1)} %pad_add_fusion.ranks_ref, bf16[256,1024]{1,0:T(8,128)(2,1)S(1)} %constant_dynamic-update-slice_fusion.2.refs_0_, bf16[256,1024]{1,0:T(8,128)(2,1)S(1)} %collective-permute-done.14.refs_1_, bf16[128,896]{1,0:T(8,128)(2,1)S(1)} %slice.91.refs_2_, ...), custom_call_target="tpu_custom_call" | custom-call | tf_op jit(solution)/shard_map/experts/pallas_call | solution.py:307
  53.8 1.0 %collective-permute-done.18 = bf16[128,896]{1,0:T(8,128)(2,1)S(1)} collective-permute-done((bf16[128,896]{1,0:T(8,128)(2,1)S(1)}, bf16[128,896]{1,0:T(8,128)(2,1)S(1)}, u32[]{:S(2)}, u32[]{:S(2)}) %collective-permute-start.18) | collective-permute-done | bytes 229408 | tf_op jit(solution)/shard_map/ppermute | solution.py:20
  54.9 0.8 collective-permute-start.24
  55.7 0.9 %collective-permute-start.25 = (bf16[64,896]{1,0:T(8,128)(2,1)S(1)}, bf16[64,896]{1,0:T(8,128)(2,1)S(1)}, u32[]{:S(2)}, u32[]{:S(2)}) collective-permute-start(bf16[64,896]{1,0:T(8,128)(2,1)S(1)} %get-tuple-element.112), channel_id=1, source_target_pairs={{0,2},{1,3},{2,0},{3,1},{4,6},{5,7},{6,4},{7,5},{8,10},{9,11},{10,... | collective-permute-start | bytes 344072 | tf_op jit(solution)/shard_map/ppermute | solution.py:20
  56.6 0.8 collective-permute-done.21
  58.3 1.2 %collective-permute-start.23 = (bf16[64,896]{1,0:T(8,128)(2,1)S(1)}, bf16[64,896]{1,0:T(8,128)(2,1)S(1)}, u32[]{:S(2)}, u32[]{:S(2)}) collective-permute-start(bf16[64,896]{1,0:T(8,128)(2,1)S(1)} %get-tuple-element.118), channel_id=1, source_target_pairs={{0,4},{4,0},{8,12},{12,8},{16,20},{20,16},{24,28},{28,24},{1,5},{5... | collective-permute-start | bytes 344072 | tf_op jit(solution)/shard_map/ppermute | solution.py:20
  60.5 0.9 %collective-permute-done.25 = bf16[64,896]{1,0:T(8,128)(2,1)S(1)} collective-permute-done((bf16[64,896]{1,0:T(8,128)(2,1)S(1)}, bf16[64,896]{1,0:T(8,128)(2,1)S(1)}, u32[]{:S(2)}, u32[]{:S(2)}) %collective-permute-start.25) | collective-permute-done | bytes 114720 | tf_op jit(solution)/shard_map/ppermute | solution.py:20
  61.5 2.0 %collective-permute-done.22 = bf16[64,896]{1,0:T(8,128)(2,1)S(1)} collective-permute-done((bf16[64,896]{1,0:T(8,128)(2,1)S(1)}, bf16[64,896]{1,0:T(8,128)(2,1)S(1)}, u32[]{:S(2)}, u32[]{:S(2)}) %collective-permute-start.22) | collective-permute-done | bytes 114720 | tf_op jit(solution)/shard_map/ppermute | solution.py:20
  63.5 1.3 %collective-permute-start.27 = (bf16[128,896]{1,0:T(8,128)(2,1)S(1)}, bf16[128,896]{1,0:T(8,128)(2,1)S(1)}, u32[]{:S(2)}, u32[]{:S(2)}) collective-permute-start(bf16[128,896]{1,0:T(8,128)(2,1)S(1)} %add_convert_fusion.3), channel_id=1, source_target_pairs={{0,2},{1,3},{2,0},{3,1},{4,6},{5,7},{6,4},{7,5},{8,10},{9,11},{10,... | collective-permute-start | bytes 688136 | tf_op jit(solution)/shard_map/ppermute | solution.py:20
  64.8 0.8 collective-permute-start.26
  65.8 5.6 %attend_local.3.old_ref = bf16[16,128,512]{2,1,0:T(8,128)(2,1)} custom-call(s32[2]{0:T(128)S(1)} %pad_add_fusion.ranks_ref, s32[512]{0:T(512)S(1)} %copy-done.1, bf16[16,576,128]{2,1,0:T(8,128)(2,1)} %bitcast.13, bf16[16,576,256]{2,1,0:T(8,128)(2,1)} %bitcast.11, bf16[16,128,512]{2,1,0:T(8,128)(2,1)} %attend_local.2.refs_0_), custom_call_target="tpu_custom_call", output_to_operand_aliasing={{}: (4, {})} | custom-call | tf_op jit(solution)/shard_map/attend_local/pallas_call | solution.py:130
  71.5 2.5 %collective-permute-start.29 = (bf16[64,896]{1,0:T(8,128)(2,1)S(1)}, bf16[64,896]{1,0:T(8,128)(2,1)S(1)}, u32[]{:S(2)}, u32[]{:S(2)}) collective-permute-start(bf16[64,896]{1,0:T(8,128)(2,1)S(1)} %get-tuple-element.125), channel_id=1, source_target_pairs={{0,16},{4,20},{8,24},{12,28},{16,0},{20,4},{24,8},{28,12},{1,17},{... | collective-permute-start | bytes 344072 | tf_op jit(solution)/shard_map/ppermute | solution.py:20
  74.0 1.9 %collective-permute-start.30 = (bf16[64,896]{1,0:T(8,128)(2,1)S(1)}, bf16[64,896]{1,0:T(8,128)(2,1)S(1)}, u32[]{:S(2)}, u32[]{:S(2)}) collective-permute-start(bf16[64,896]{1,0:T(8,128)(2,1)S(1)} %get-tuple-element.124), channel_id=1, source_target_pairs={{0,24},{4,28},{8,16},{12,20},{16,8},{20,12},{24,0},{28,4},{1,25},{... | collective-permute-start | bytes 344072 | tf_op jit(solution)/shard_map/ppermute | solution.py:20
  75.9 2.7 %attend_traded.1 = bf16[16,128,512]{2,1,0:T(8,128)(2,1)} custom-call(s32[2]{0:T(128)S(1)} %pad_add_fusion.ranks_ref, s32[512]{0:T(512)S(1)} %copy-done.1, s32[32]{0:T(128)S(1)} %copy-done.2, s32[1]{0:T(128)S(6)} %copy.19.mask_ref, bf16[16,576,128]{2,1,0:T(8,128)(2,1)} %bitcast.14, ...), custom_call_target="tpu_custom_call", output_to_operand_aliasing={{}: (6, {})} | custom-call | flops 71303168 | bytes 573440 | tf_op jit(solution)/shard_map/attend_traded/pallas_call | solution.py:191
  78.7 3.7 %collective-permute-done.29 = bf16[64,896]{1,0:T(8,128)(2,1)S(1)} collective-permute-done((bf16[64,896]{1,0:T(8,128)(2,1)S(1)}, bf16[64,896]{1,0:T(8,128)(2,1)S(1)}, u32[]{:S(2)}, u32[]{:S(2)}) %collective-permute-start.29) | collective-permute-done | bytes 114720 | tf_op jit(solution)/shard_map/ppermute | solution.py:20
  (82 shorter events, 8.3 us)
Async XLA Ops:
  2.6 7.4 %collective-permute-start = (bf16[64,1024]{1,0:T(8,128)(2,1)S(1)}, bf16[64,1024]{1,0:T(8,128)(2,1)S(1)}, u32[]{:S(2)}, u32[]{:S(2)}) collective-permute-start(bf16[64,1024]{1,0:T(8,128)(2,1)S(1)} %get-tuple-element.57.refs_1_), channel_id=1, source_target_pairs={{0,8},{4,12},{8,0},{12,4},{16,24},{20,28},{24,16},{28,20},{1,9},{5... | collective-permute-start | bytes 393224 | tf_op jit(solution)/shard_map/ppermute | solution.py:20
  5.7 13.8 %collective-permute-start.3 = (bf16[64,1920]{1,0:T(8,128)(2,1)S(1)}, bf16[64,1920]{1,0:T(8,128)(2,1)S(1)}, u32[]{:S(2)}, u32[]{:S(2)}) collective-permute-start(bf16[64,1920]{1,0:T(8,128)(2,1)S(1)} %get-tuple-element.64), channel_id=1, source_target_pairs={{0,4},{4,0},{8,12},{12,8},{16,20},{20,16},{24,28},{28,24},{1,5},{5... | collective-permute-start | bytes 737288 | tf_op jit(solution)/shard_map/ppermute | solution.py:20
  7.2 12.3 %collective-permute-start.4 = (bf16[64,1024]{1,0:T(8,128)(2,1)S(1)}, bf16[64,1024]{1,0:T(8,128)(2,1)S(1)}, u32[]{:S(2)}, u32[]{:S(2)}) collective-permute-start(bf16[64,1024]{1,0:T(8,128)(2,1)S(1)} %get-tuple-element.57.refs_1_), channel_id=1, source_target_pairs={{0,16},{4,20},{8,24},{12,28},{16,0},{20,4},{24,8},{28,12},{1,17},{... | collective-permute-start | bytes 393224 | tf_op jit(solution)/shard_map/ppermute | solution.py:20
  9.8 9.7 %collective-permute-start.5 = (bf16[64,1024]{1,0:T(8,128)(2,1)S(1)}, bf16[64,1024]{1,0:T(8,128)(2,1)S(1)}, u32[]{:S(2)}, u32[]{:S(2)}) collective-permute-start(bf16[64,1024]{1,0:T(8,128)(2,1)S(1)} %get-tuple-element.57.refs_1_), channel_id=1, source_target_pairs={{0,24},{4,28},{8,16},{12,20},{16,8},{20,12},{24,0},{28,4},{1,25},{... | collective-permute-start | bytes 393224 | tf_op jit(solution)/shard_map/ppermute | solution.py:20
  10.0 9.5 %collective-permute-start.2 = (bf16[64,1024]{1,0:T(8,128)(2,1)S(1)}, bf16[64,1024]{1,0:T(8,128)(2,1)S(1)}, u32[]{:S(2)}, u32[]{:S(2)}) collective-permute-start(bf16[64,1024]{1,0:T(8,128)(2,1)S(1)} %collective-permute-done.refs_4_), channel_id=1, source_target_pairs={{0,4},{4,0},{8,12},{12,8},{16,20},{20,16},{24,28},{28,24},{1,5},{5... | collective-permute-start | bytes 393224 | tf_op jit(solution)/shard_map/ppermute | solution.py:20
  12.3 7.2 %collective-permute-start.1 = (bf16[64,896]{1,0:T(8,128)(2,1)S(1)}, bf16[64,896]{1,0:T(8,128)(2,1)S(1)}, u32[]{:S(2)}, u32[]{:S(2)}) collective-permute-start(bf16[64,896]{1,0:T(8,128)(2,1)S(1)} %slice.85), channel_id=1, source_target_pairs={{0,2},{1,3},{2,0},{3,1},{4,6},{5,7},{6,4},{7,5},{8,10},{9,11},{10,... | collective-permute-start | bytes 344072 | tf_op jit(solution)/shard_map/ppermute | solution.py:20
  19.7 14.0 %collective-permute-start.6 = (bf16[192,896]{1,0:T(8,128)(2,1)S(1)}, bf16[192,896]{1,0:T(8,128)(2,1)S(1)}, u32[]{:S(2)}, u32[]{:S(2)}) collective-permute-start(bf16[192,896]{1,0:T(8,128)(2,1)S(1)} %pad_maximum_fusion), channel_id=1, source_target_pairs={{0,2},{1,3},{2,0},{3,1},{4,6},{5,7},{6,4},{7,5},{8,10},{9,11},{10,... | collective-permute-start | bytes 1032200 | tf_op jit(solution)/shard_map/ppermute | solution.py:20
  21.2 5.8 %collective-permute-start.8 = (bf16[128,1024]{1,0:T(8,128)(2,1)S(1)}, bf16[128,1024]{1,0:T(8,128)(2,1)S(1)}, u32[]{:S(2)}, u32[]{:S(2)}) collective-permute-start(bf16[128,1024]{1,0:T(8,128)(2,1)S(1)} %pad_maximum_fusion.3), channel_id=1, source_target_pairs={{0,1},{1,0},{2,3},{3,2},{4,5},{5,4},{6,7},{7,6},{8,9},{9,8},{10,11... | collective-permute-start | bytes 786440 | tf_op jit(solution)/shard_map/ppermute | solution.py:20
  21.3 1.7 %collective-permute-start.10 = (bf16[64,896]{1,0:T(8,128)(2,1)S(1)}, bf16[64,896]{1,0:T(8,128)(2,1)S(1)}, u32[]{:S(2)}, u32[]{:S(2)}) collective-permute-start(bf16[64,896]{1,0:T(8,128)(2,1)S(1)} %collective-permute-done.1.refs_7_), channel_id=1, source_target_pairs={{0,1},{1,0},{2,3},{3,2},{4,5},{5,4},{6,7},{7,6},{8,9},{9,8},{10,11... | collective-permute-start | bytes 344072 | tf_op jit(solution)/shard_map/ppermute | solution.py:20
  21.8 11.9 %collective-permute-start.7 = (bf16[128,1024]{1,0:T(8,128)(2,1)S(1)}, bf16[128,1024]{1,0:T(8,128)(2,1)S(1)}, u32[]{:S(2)}, u32[]{:S(2)}) collective-permute-start(bf16[128,1024]{1,0:T(8,128)(2,1)S(1)} %constant_dynamic-update-slice_fusion), channel_id=1, source_target_pairs={{0,4},{4,0},{8,12},{12,8},{16,20},{20,16},{24,28},{28,24},{1,5},{5... | collective-permute-start | bytes 786440 | tf_op jit(solution)/shard_map/ppermute | solution.py:20
  22.7 4.3 %collective-permute-start.9 = (bf16[64,1920]{1,0:T(8,128)(2,1)S(1)}, bf16[64,1920]{1,0:T(8,128)(2,1)S(1)}, u32[]{:S(2)}, u32[]{:S(2)}) collective-permute-start(bf16[64,1920]{1,0:T(8,128)(2,1)S(1)} %collective-permute-done.3.refs_2_), channel_id=1, source_target_pairs={{0,1},{1,0},{2,3},{3,2},{4,5},{5,4},{6,7},{7,6},{8,9},{9,8},{10,11... | collective-permute-start | bytes 737288 | tf_op jit(solution)/shard_map/ppermute | solution.py:20
  23.0 10.7 %collective-permute-start.11 = (bf16[288,256]{1,0:T(8,128)(2,1)S(1)}, bf16[288,256]{1,0:T(8,128)(2,1)S(1)}, u32[]{:S(2)}, u32[]{:S(2)}) collective-permute-start(bf16[288,256]{1,0:T(8,128)(2,1)S(1)} %split.20), channel_id=1, source_target_pairs={{0,16},{4,20},{8,24},{12,28},{16,0},{20,4},{24,8},{28,12},{1,17},{... | collective-permute-start | bytes 442376 | tf_op jit(solution)/shard_map/ppermute | solution.py:20
  33.6 2.7 %collective-permute-start.12 = (bf16[192,896]{1,0:T(8,128)(2,1)S(1)}, bf16[192,896]{1,0:T(8,128)(2,1)S(1)}, u32[]{:S(2)}, u32[]{:S(2)}) collective-permute-start(bf16[192,896]{1,0:T(8,128)(2,1)S(1)} %collective-permute-done.6), channel_id=1, source_target_pairs={{0,1},{1,0},{2,3},{3,2},{4,5},{5,4},{6,7},{7,6},{8,9},{9,8},{10,11... | collective-permute-start | bytes 1032200 | tf_op jit(solution)/shard_map/ppermute | solution.py:20
  33.7 9.6 %collective-permute-start.14 = (bf16[256,1024]{1,0:T(8,128)(2,1)S(1)}, bf16[256,1024]{1,0:T(8,128)(2,1)S(1)}, u32[]{:S(2)}, u32[]{:S(2)}) collective-permute-start(bf16[256,1024]{1,0:T(8,128)(2,1)S(1)} %constant_dynamic-update-slice_fusion.2.refs_0_), channel_id=1, source_target_pairs={{0,1},{1,0},{2,3},{3,2},{4,5},{5,4},{6,7},{7,6},{8,9},{9,8},{10,11... | collective-permute-start | bytes 1572872 | tf_op jit(solution)/shard_map/ppermute | solution.py:20
  34.3 9.0 %collective-permute-start.15 = (bf16[576,256]{1,0:T(8,128)(2,1)S(1)}, bf16[576,256]{1,0:T(8,128)(2,1)S(1)}, u32[]{:S(2)}, u32[]{:S(2)}) collective-permute-start(bf16[576,256]{1,0:T(8,128)(2,1)S(1)} %pad_maximum_fusion.1), channel_id=1, source_target_pairs={{0,4},{4,0},{8,12},{12,8},{16,20},{20,16},{24,28},{28,24},{1,5},{5... | collective-permute-start | bytes 884744 | tf_op jit(solution)/shard_map/ppermute | solution.py:20
  35.7 7.3 %collective-permute-start.13 = (bf16[128,896]{1,0:T(8,128)(2,1)S(1)}, bf16[128,896]{1,0:T(8,128)(2,1)S(1)}, u32[]{:S(2)}, u32[]{:S(2)}) collective-permute-start(bf16[128,896]{1,0:T(8,128)(2,1)S(1)} %slice.90), channel_id=1, source_target_pairs={{0,2},{1,3},{2,0},{3,1},{4,6},{5,7},{6,4},{7,5},{8,10},{9,11},{10,... | collective-permute-start | bytes 688136 | tf_op jit(solution)/shard_map/ppermute | solution.py:20
  43.3 2.5 %collective-permute-start.17 = (bf16[512,896]{1,0:T(8,128)(2,1)S(1)}, bf16[512,896]{1,0:T(8,128)(2,1)S(1)}, u32[]{:S(2)}, u32[]{:S(2)}) collective-permute-start(bf16[512,896]{1,0:T(8,128)(2,1)S(1)} %get-tuple-element.89), channel_id=1, source_target_pairs={{0,1},{1,0},{2,3},{3,2},{4,5},{5,4},{6,7},{7,6},{8,9},{9,8},{10,11... | collective-permute-start | bytes 2752520 | tf_op jit(solution)/shard_map/ppermute | solution.py:20
  43.4 10.3 %collective-permute-start.20 = (bf16[576,256]{1,0:T(8,128)(2,1)S(1)}, bf16[576,256]{1,0:T(8,128)(2,1)S(1)}, u32[]{:S(2)}, u32[]{:S(2)}) collective-permute-start(bf16[576,256]{1,0:T(8,128)(2,1)S(1)} %broadcast_select_fusion.1), channel_id=1, source_target_pairs={{0,8},{4,12},{8,0},{12,4},{16,24},{20,28},{24,16},{28,20},{1,9},{5... | collective-permute-start | bytes 884744 | tf_op jit(solution)/shard_map/ppermute | solution.py:20
  43.5 4.6 %collective-permute-start.16 = (bf16[128,896]{1,0:T(8,128)(2,1)S(1)}, bf16[128,896]{1,0:T(8,128)(2,1)S(1)}, u32[]{:S(2)}, u32[]{:S(2)}) collective-permute-start(bf16[128,896]{1,0:T(8,128)(2,1)S(1)} %collective-permute-done.13.refs_4_), channel_id=1, source_target_pairs={{0,1},{1,0},{2,3},{3,2},{4,5},{5,4},{6,7},{7,6},{8,9},{9,8},{10,11... | collective-permute-start | bytes 688136 | tf_op jit(solution)/shard_map/ppermute | solution.py:20
  46.1 7.7 %collective-permute-start.19 = (bf16[64,1792]{1,0:T(8,128)(2,1)S(1)}, bf16[64,1792]{1,0:T(8,128)(2,1)S(1)}, u32[]{:S(2)}, u32[]{:S(2)}) collective-permute-start(bf16[64,1792]{1,0:T(8,128)(2,1)S(1)} %pad_maximum_fusion.4), channel_id=1, source_target_pairs={{0,4},{4,0},{8,12},{12,8},{16,20},{20,16},{24,28},{28,24},{1,5},{5... | collective-permute-start | bytes 688136 | tf_op jit(solution)/shard_map/ppermute | solution.py:20
  47.5 7.4 %collective-permute-start.18 = (bf16[128,896]{1,0:T(8,128)(2,1)S(1)}, bf16[128,896]{1,0:T(8,128)(2,1)S(1)}, u32[]{:S(2)}, u32[]{:S(2)}) collective-permute-start(bf16[128,896]{1,0:T(8,128)(2,1)S(1)} %slice.114), channel_id=1, source_target_pairs={{0,2},{1,3},{2,0},{3,1},{4,6},{5,7},{6,4},{7,5},{8,10},{9,11},{10,... | collective-permute-start | bytes 688136 | tf_op jit(solution)/shard_map/ppermute | solution.py:20
  54.8 2.5 %collective-permute-start.21 = (bf16[512,896]{1,0:T(8,128)(2,1)S(1)}, bf16[512,896]{1,0:T(8,128)(2,1)S(1)}, u32[]{:S(2)}, u32[]{:S(2)}) collective-permute-start(bf16[512,896]{1,0:T(8,128)(2,1)S(1)} %get-tuple-element.92), channel_id=1, source_target_pairs={{0,1},{1,0},{2,3},{3,2},{4,5},{5,4},{6,7},{7,6},{8,9},{9,8},{10,11... | collective-permute-start | bytes 2752520 | tf_op jit(solution)/shard_map/ppermute | solution.py:20
  54.9 5.6 %collective-permute-start.24 = (bf16[64,896]{1,0:T(8,128)(2,1)S(1)}, bf16[64,896]{1,0:T(8,128)(2,1)S(1)}, u32[]{:S(2)}, u32[]{:S(2)}) collective-permute-start(bf16[64,896]{1,0:T(8,128)(2,1)S(1)} %get-tuple-element.113), channel_id=1, source_target_pairs={{0,4},{4,0},{8,12},{12,8},{16,20},{20,16},{24,28},{28,24},{1,5},{5... | collective-permute-start | bytes 344072 | tf_op jit(solution)/shard_map/ppermute | solution.py:20
  55.7 5.8 %collective-permute-start.25 = (bf16[64,896]{1,0:T(8,128)(2,1)S(1)}, bf16[64,896]{1,0:T(8,128)(2,1)S(1)}, u32[]{:S(2)}, u32[]{:S(2)}) collective-permute-start(bf16[64,896]{1,0:T(8,128)(2,1)S(1)} %get-tuple-element.112), channel_id=1, source_target_pairs={{0,2},{1,3},{2,0},{3,1},{4,6},{5,7},{6,4},{7,5},{8,10},{9,11},{10,... | collective-permute-start | bytes 344072 | tf_op jit(solution)/shard_map/ppermute | solution.py:20
  57.7 5.8 %collective-permute-start.22 = (bf16[64,896]{1,0:T(8,128)(2,1)S(1)}, bf16[64,896]{1,0:T(8,128)(2,1)S(1)}, u32[]{:S(2)}, u32[]{:S(2)}) collective-permute-start(bf16[64,896]{1,0:T(8,128)(2,1)S(1)} %get-tuple-element.119), channel_id=1, source_target_pairs={{0,2},{1,3},{2,0},{3,1},{4,6},{5,7},{6,4},{7,5},{8,10},{9,11},{10,... | collective-permute-start | bytes 344072 | tf_op jit(solution)/shard_map/ppermute | solution.py:20
  58.3 5.2 %collective-permute-start.23 = (bf16[64,896]{1,0:T(8,128)(2,1)S(1)}, bf16[64,896]{1,0:T(8,128)(2,1)S(1)}, u32[]{:S(2)}, u32[]{:S(2)}) collective-permute-start(bf16[64,896]{1,0:T(8,128)(2,1)S(1)} %get-tuple-element.118), channel_id=1, source_target_pairs={{0,4},{4,0},{8,12},{12,8},{16,20},{20,16},{24,28},{28,24},{1,5},{5... | collective-permute-start | bytes 344072 | tf_op jit(solution)/shard_map/ppermute | solution.py:20
  59.5 11.9 %collective-permute-start.28 = (bf16[288,256]{1,0:T(8,128)(2,1)S(1)}, bf16[288,256]{1,0:T(8,128)(2,1)S(1)}, u32[]{:S(2)}, u32[]{:S(2)}) collective-permute-start(bf16[288,256]{1,0:T(8,128)(2,1)S(1)} %split.28), channel_id=1, source_target_pairs={{0,16},{4,20},{8,24},{12,28},{16,0},{20,4},{24,8},{28,12},{1,17},{... | collective-permute-start | bytes 442376 | tf_op jit(solution)/shard_map/ppermute | solution.py:20
  63.5 7.9 %collective-permute-start.27 = (bf16[128,896]{1,0:T(8,128)(2,1)S(1)}, bf16[128,896]{1,0:T(8,128)(2,1)S(1)}, u32[]{:S(2)}, u32[]{:S(2)}) collective-permute-start(bf16[128,896]{1,0:T(8,128)(2,1)S(1)} %add_convert_fusion.3), channel_id=1, source_target_pairs={{0,2},{1,3},{2,0},{3,1},{4,6},{5,7},{6,4},{7,5},{8,10},{9,11},{10,... | collective-permute-start | bytes 688136 | tf_op jit(solution)/shard_map/ppermute | solution.py:20
  64.8 6.6 %collective-permute-start.26 = (bf16[128,896]{1,0:T(8,128)(2,1)S(1)}, bf16[128,896]{1,0:T(8,128)(2,1)S(1)}, u32[]{:S(2)}, u32[]{:S(2)}) collective-permute-start(bf16[128,896]{1,0:T(8,128)(2,1)S(1)} %add_convert_fusion.4), channel_id=1, source_target_pairs={{0,4},{4,0},{8,12},{12,8},{16,20},{20,16},{24,28},{28,24},{1,5},{5... | collective-permute-start | bytes 688136 | tf_op jit(solution)/shard_map/ppermute | solution.py:20
  65.6 13.0 %collective-permute-start.31 = (bf16[64,896]{1,0:T(8,128)(2,1)S(1)}, bf16[64,896]{1,0:T(8,128)(2,1)S(1)}, u32[]{:S(2)}, u32[]{:S(2)}) collective-permute-start(bf16[64,896]{1,0:T(8,128)(2,1)S(1)} %add_convert_fusion.6), channel_id=1, source_target_pairs={{0,8},{4,12},{8,0},{12,4},{16,24},{20,28},{24,16},{28,20},{1,9},{5... | collective-permute-start | bytes 344072 | tf_op jit(solution)/shard_map/ppermute | solution.py:20
  71.5 10.9 %collective-permute-start.29 = (bf16[64,896]{1,0:T(8,128)(2,1)S(1)}, bf16[64,896]{1,0:T(8,128)(2,1)S(1)}, u32[]{:S(2)}, u32[]{:S(2)}) collective-permute-start(bf16[64,896]{1,0:T(8,128)(2,1)S(1)} %get-tuple-element.125), channel_id=1, source_target_pairs={{0,16},{4,20},{8,24},{12,28},{16,0},{20,4},{24,8},{28,12},{1,17},{... | collective-permute-start | bytes 344072 | tf_op jit(solution)/shard_map/ppermute | solution.py:20
  74.0 8.4 %collective-permute-start.30 = (bf16[64,896]{1,0:T(8,128)(2,1)S(1)}, bf16[64,896]{1,0:T(8,128)(2,1)S(1)}, u32[]{:S(2)}, u32[]{:S(2)}) collective-permute-start(bf16[64,896]{1,0:T(8,128)(2,1)S(1)} %get-tuple-element.124), channel_id=1, source_target_pairs={{0,24},{4,28},{8,16},{12,20},{16,8},{20,12},{24,0},{28,4},{1,25},{... | collective-permute-start | bytes 344072 | tf_op jit(solution)/shard_map/ppermute | solution.py:20
  (3 other events, 17.3 us)

commit v11 on v10

--- a/solution.py
+++ b/solution.py
@@ -142,7 +142,11 @@
         ),
         input_output_aliases={4: 0} if earlier else {},
         compiler_params=pltpu.CompilerParams(vmem_limit_bytes=8 * MIB),
-        cost_estimate=pl.CostEstimate(flops=0, bytes_accessed=0, transcendentals=0),
+        cost_estimate=pl.CostEstimate(
+            flops=2 * some * heads * slots * (width + LAT),
+            bytes_accessed=2 * some * (heads * (width + LAT) + slots * width),
+            transcendentals=some * heads * slots,
+        ),
         name="attend_local",
     )(ranks, lengths, in_hbm(queries), in_hbm(pages), *earlier)
 
@@ -220,7 +224,7 @@
     gate_ref,
     up_ref,
     source_ref,
-    given_ref,
+    given,
     kept_ref,
     *refs,
 ):
@@ -281,7 +285,13 @@
 
     if fetch:
         down_copy.wait()
-    for part, out_ref, half in ((3, given_ref, 0), (1, given_ref, 1), (2, kept_ref, 0), (0, kept_ref, 1)):
+    last = len(given) - 1
+    for part, out_ref, half in (
+        (3, given[0], 0),
+        (1, given[last], 1 - last),
+        (2, kept_ref, 0),
+        (0, kept_ref, 1),
+    ):
 
         @pl.loop(0, total_rows // stride)
         def _(step):
@@ -293,7 +303,7 @@
             ).astype(jnp.bfloat16)
 
 
-def run_experts(ranks, pieces, w_gate, w_up, w_down, rows, columns, top, fetch):
+def run_experts(ranks, pieces, w_gate, w_up, w_down, rows, columns, top, fetch, given):
     experts, width, units = w_gate.shape
     arrays = [piece for *_, piece in pieces]
     count = sum(1 if parts is None else len(parts) + has_meta for _, parts, has_meta, _ in pieces)
@@ -306,7 +316,11 @@
     down_shape = [pltpu.VMEM(w_down.shape, w_down.dtype)] if fetch else []
     return pl.pallas_call(
         kernel,
-        out_shape=[pltpu.VMEM((2 * rows, columns), jnp.bfloat16)] * 2 + down_shape,
+        out_shape=[
+            [pltpu.VMEM((2 * rows // given, columns), jnp.bfloat16)] * given,
+            pltpu.VMEM((2 * rows, columns), jnp.bfloat16),
+        ]
+        + down_shape,
         in_specs=[
             IN_SMEM,
             [ANYWHERE] * len(arrays),
@@ -314,7 +328,7 @@
             IN_VMEM,
             ANYWHERE if fetch else IN_VMEM,
         ],
-        out_specs=[IN_VMEM] * (2 + len(down_shape)),
+        out_specs=[[IN_VMEM] * given, IN_VMEM] + [IN_VMEM] * len(down_shape),
         scratch_shapes=[
             pltpu.VMEM((rows, width), jnp.bfloat16),
             pltpu.VMEM((rows, 128), jnp.bfloat16),
@@ -415,9 +429,10 @@
     early = [flip(array, "tp", 1) for array in (both_1, far_2)]
     queries, near_23, early = tie((queries, near_23, early))
     count = queries.shape[0]
-    some = count // 2
+    some = count // 4
     attended = attend_part(ranks, lengths, queries, cache_pages, groups, 0, some)
-    upper, lower = jnp.split(page, 2, axis=0)
+    least = page.shape[0] // 4
+    upper, lower = jnp.split(page, [least], axis=0)
     swapped, upper = page_far(upper)
     far_3, near_late, near_odds, attended, swapped = tie(
         (far_3, near_late, near_odds, attended, swapped)
@@ -438,7 +453,7 @@
     pieces += [piece(2, 2, far_2), piece(2, 3, early[1])]
     pieces += [piece(3, 2, far_3), piece(3, 3, core_3)]
     *first, w_down = run_experts(
-        ranks, pieces, w_gate, w_up, w_down, 4 * rows, columns, top, True
+        ranks, pieces, w_gate, w_up, w_down, 4 * rows, columns, top, True, 1
     )
     near_both = jnp.concatenate([near_late, near_odds], axis=0)
     early = flip(near_both, "tp", 1)
@@ -446,11 +461,8 @@
     first, far_odds, early, swapped = tie((first, far_odds, early, swapped))
     page = page_take(page, swapped, 0)
 
-    def add_core(given, own):
-        total = total_of(own, flip(given, "tp", 1))
-        return jnp.split(total, 2, axis=0)
-
-    sent, kept = add_core(*first)
+    (given,), own = first
+    sent, kept = jnp.split(total_of(own, flip(given, "tp", 1)), 2, axis=0)
     last = flip(far_odds, "tp", 1)
     over_23 = flip(cut(sent, 2, 2), "tp", 2)
     over_1 = flip(jnp.concatenate([cut(kept, 1, 1), cut(sent, 1, 1)], axis=1), "ep", 1)
@@ -461,21 +473,28 @@
     pieces += [piece(odds, 2, far_odds), piece(odds, 3, last)]
     second = [
         *run_experts(
-            ranks, pieces, w_gate, w_up, w_down, 2 * len(late) * rows, columns, top, False
+            ranks, pieces, w_gate, w_up, w_down, 2 * len(late) * rows, columns, top, False, 2
         )
     ]
     second, over_23, over_1, swapped = tie((second, over_23, over_1, swapped))
     page = page_take(page, swapped, 1)
-    upper, lower = jnp.split(page, 2, axis=0)
+    upper, lower = jnp.split(page, [least], axis=0)
     swapped, lower = page_far(lower)
-    late_sent, late_kept = add_core(*second)
+    (cross, side), own = second
+    late_sent, late_kept = jnp.split(own, 2, axis=0)
+    late_sent = total_of(late_sent, flip(cross, "tp", 1))
     over_3 = flip(total_of(cut(kept, 3, 1), cut(over_23, 1, 1)), "ep", 1)
     zero = flip(total_of(cut(sent, 0, 1), over_1[:, columns:]), "tp", 2)
-    late_sent, late_kept = tie((late_sent, late_kept))
+    late_sent, side, queries = tie((late_sent, side, queries))
+    side = flip(side, "tp", 1)
 
     over_y = flip(cut(late_sent, len(late), half), "tp", 2)
     over_x = flip(cut(late_sent, len(late) + half, rest), "ep", 1)
-    over_y, over_x, over_3, zero, queries = tie((over_y, over_x, over_3, zero, queries))
+    attended = attend_part(
+        ranks, lengths, queries, cache_pages, groups, some, some, attended
+    )
+    over_y, over_x, over_3, side, attended = tie((over_y, over_x, over_3, side, attended))
+    late_kept = total_of(late_kept, side)
     odd = total_of(
         cut(late_kept, len(late), len(late)), jnp.pad(over_y, ((0, rest * rows), (0, 0)))
     )
@@ -483,7 +502,7 @@
     even = total_of(cut(late_sent, 0, len(late)), jnp.pad(over_x, ((half * rows, 0), (0, 0))))
     even = flip(even, "tp", 2)
     attended = attend_part(
-        ranks, lengths, queries, cache_pages, groups, some, count - some, attended
+        ranks, lengths, queries, cache_pages, groups, 2 * some, count - 2 * some, attended
     )
     odd, even, attended, swapped = tie((odd, even, attended, swapped))
     lower = page_take(lower, swapped, 2) if levels > 2 else lower

time: 83.5 us -> 83.3 us (level)
  waiting for transfers between devices: 14.3 us -> 10.6 us
  starting transfers between devices: 33.3 us -> 35.1 us
  Pallas kernels: 31.7 us -> 33.5 us
    ppermute x32 -> x33, waiting for transfers between devices: 14.3 us -> 10.6 us  [flip(): return lax.ppermute(block, axis, [(i, i ^ apart) for i in range(count)])]
    ppermute x32 -> x33, starting transfers between devices: 33.3 us -> 35.1 us  [flip(): return lax.ppermute(block, axis, [(i, i ^ apart) for i in range(count)])]
    pallas_call x2 -> x3, Pallas kernels: 11.1 us -> 12.9 us  [attend_part(): pl.pallas_call(kernel, out_shape=jax.ShapeDtypeStruct((count, heads, LAT)...]
  transfers between devices with their start and end apart: 32 -> 33, of which waited for: 13 -> 8; matrix products, arithmetic and copies ran while one was open for 2% -> 1% of each run, Pallas kernels for 36% -> 38%
where the time goes in v11:
time: 83.3 us; the launch traced here: 83 us
  starting transfers between devices  35.1 us (42%)
  Pallas kernels  33.5 us (40%)
  waiting for transfers between devices  10.6 us (13%)
  other arithmetic  1.84 us (2%)
  between operations  1.69 us (2%)
    ppermute x33, starting transfers between devices, flip(): return lax.ppermute(block, axis, [(i, i ^ apart) for i in range(count)])  35.1 us
    pallas_call x3, Pallas kernels, attend_part(): pl.pallas_call(kernel, out_shape=jax.ShapeDtypeStruct((count, heads, LAT)...  12.9 us
    pallas_call x2, Pallas kernels, run_experts(): pl.pallas_call(kernel, out_shape=[[pltpu.VMEM((2 * rows // given, columns...  11.8 us
    ppermute x33, waiting for transfers between devices, flip(): return lax.ppermute(block, axis, [(i, i ^ apart) for i in range(count)])  10.6 us
    pallas_call x1, Pallas kernels, load(): pl.pallas_call(load_kernel, out_shape=[pltpu.VMEM(w.shape, w.dtype) for w...  4.21 us
    pallas_call x1, Pallas kernels, attend_traded(): pl.pallas_call(functools.partial(attend_traded_kernel, groups), out_shape...  2.71 us
    pallas_call x1, Pallas kernels, pick(): pl.pallas_call(functools.partial(pick_kernel, groups), out_shape=(pltpu.V...  1.89 us
  transfers between devices with their start and end apart: 33, of which 8 were waited for; matrix products, arithmetic and copies ran while one was open for 1% of the time, Pallas kernels for 38%

profile of v11, /device:TPU:0, one launch (start us, length us, event | category | flops | bytes accessed | tf_op | source)
XLA Modules:
  0.0 83.0 jit_solution(2775245447436867053)
XLA Ops:
  0.7 1.9 %pick.1 = (bf16[64,1024]{1,0:T(8,128)(2,1)S(1)}, bf16[64,1920]{1,0:T(8,128)(2,1)S(1)}, bf16[576,256]{1,0:T(8,128)(2,1)S(1)}) custom-call(s32[2]{0:T(128)S(1)} %pad_add_fusion.ranks_ref, s32[32]{0:T(128)} %slots_ref.3, s32[8,64]{1,0:T(8,128)} %bitcast.17, f32[8,64]{1,0:T(8,128)} %bitcast.18, bf16[64,3584]{1,0:T(8,128)(2,1)} %refs_0_.2, ...), custom_call_target="tpu_custom_call" | custom-call | tf_op jit(solution)/shard_map/pick/pallas_call | solution.py:96
  2.6 3.1 %collective-permute-start = (bf16[64,1024]{1,0:T(8,128)(2,1)S(1)}, bf16[64,1024]{1,0:T(8,128)(2,1)S(1)}, u32[]{:S(2)}, u32[]{:S(2)}) collective-permute-start(bf16[64,1024]{1,0:T(8,128)(2,1)S(1)} %get-tuple-element.60.refs_1_), channel_id=1, source_target_pairs={{0,8},{4,12},{8,0},{12,4},{16,24},{20,28},{24,16},{28,20},{1,9},{5... | collective-permute-start | bytes 393224 | tf_op jit(solution)/shard_map/ppermute | solution.py:20
  5.7 1.5 %collective-permute-start.3 = (bf16[64,1920]{1,0:T(8,128)(2,1)S(1)}, bf16[64,1920]{1,0:T(8,128)(2,1)S(1)}, u32[]{:S(2)}, u32[]{:S(2)}) collective-permute-start(bf16[64,1920]{1,0:T(8,128)(2,1)S(1)} %get-tuple-element.67), channel_id=1, source_target_pairs={{0,4},{4,0},{8,12},{12,8},{16,20},{20,16},{24,28},{28,24},{1,5},{5... | collective-permute-start | bytes 737288 | tf_op jit(solution)/shard_map/ppermute | solution.py:20
  7.2 2.6 %collective-permute-start.4 = (bf16[64,1024]{1,0:T(8,128)(2,1)S(1)}, bf16[64,1024]{1,0:T(8,128)(2,1)S(1)}, u32[]{:S(2)}, u32[]{:S(2)}) collective-permute-start(bf16[64,1024]{1,0:T(8,128)(2,1)S(1)} %get-tuple-element.60.refs_1_), channel_id=1, source_target_pairs={{0,16},{4,20},{8,24},{12,28},{16,0},{20,4},{24,8},{28,12},{1,17},{... | collective-permute-start | bytes 393224 | tf_op jit(solution)/shard_map/ppermute | solution.py:20
  10.0 2.3 %collective-permute-start.2 = (bf16[64,1024]{1,0:T(8,128)(2,1)S(1)}, bf16[64,1024]{1,0:T(8,128)(2,1)S(1)}, u32[]{:S(2)}, u32[]{:S(2)}) collective-permute-start(bf16[64,1024]{1,0:T(8,128)(2,1)S(1)} %collective-permute-done.refs_4_), channel_id=1, source_target_pairs={{0,4},{4,0},{8,12},{12,8},{16,20},{20,16},{24,28},{28,24},{1,5},{5... | collective-permute-start | bytes 393224 | tf_op jit(solution)/shard_map/ppermute | solution.py:20
  12.3 1.5 %collective-permute-start.1 = (bf16[64,896]{1,0:T(8,128)(2,1)S(1)}, bf16[64,896]{1,0:T(8,128)(2,1)S(1)}, u32[]{:S(2)}, u32[]{:S(2)}) collective-permute-start(bf16[64,896]{1,0:T(8,128)(2,1)S(1)} %slice.85), channel_id=1, source_target_pairs={{0,2},{1,3},{2,0},{3,1},{4,6},{5,7},{6,4},{7,5},{8,10},{9,11},{10,... | collective-permute-start | bytes 344072 | tf_op jit(solution)/shard_map/ppermute | solution.py:20
  13.9 4.2 %load.1 = (bf16[3,3584,256]{2,1,0:T(8,128)(2,1)S(1)}, bf16[3,3584,256]{2,1,0:T(8,128)(2,1)S(1)}) custom-call(bf16[3,3584,256]{2,1,0:T(8,128)(2,1)} %refs_0_.1, bf16[3,3584,256]{2,1,0:T(8,128)(2,1)} %refs_1_), custom_call_target="tpu_custom_call" | custom-call | bytes 11010048 | tf_op jit(solution)/shard_map/load/pallas_call | solution.py:166
  18.1 1.4 %collective-permute-done.4 = bf16[64,1024]{1,0:T(8,128)(2,1)S(1)} collective-permute-done((bf16[64,1024]{1,0:T(8,128)(2,1)S(1)}, bf16[64,1024]{1,0:T(8,128)(2,1)S(1)}, u32[]{:S(2)}, u32[]{:S(2)}) %collective-permute-start.4) | collective-permute-done | bytes 131104 | tf_op jit(solution)/shard_map/ppermute | solution.py:20
  19.7 1.5 %collective-permute-start.6 = (bf16[192,896]{1,0:T(8,128)(2,1)S(1)}, bf16[192,896]{1,0:T(8,128)(2,1)S(1)}, u32[]{:S(2)}, u32[]{:S(2)}) collective-permute-start(bf16[192,896]{1,0:T(8,128)(2,1)S(1)} %pad_maximum_fusion), channel_id=1, source_target_pairs={{0,2},{1,3},{2,0},{3,1},{4,6},{5,7},{6,4},{7,5},{8,10},{9,11},{10,... | collective-permute-start | bytes 1032200 | tf_op jit(solution)/shard_map/ppermute | solution.py:20
  21.8 0.9 %collective-permute-start.7 = (bf16[128,1024]{1,0:T(8,128)(2,1)S(1)}, bf16[128,1024]{1,0:T(8,128)(2,1)S(1)}, u32[]{:S(2)}, u32[]{:S(2)}) collective-permute-start(bf16[128,1024]{1,0:T(8,128)(2,1)S(1)} %constant_dynamic-update-slice_fusion), channel_id=1, source_target_pairs={{0,4},{4,0},{8,12},{12,8},{16,20},{20,16},{24,28},{28,24},{1,5},{5... | collective-permute-start | bytes 786440 | tf_op jit(solution)/shard_map/ppermute | solution.py:20
  22.7 1.3 %collective-permute-done.10.refs_8_ = bf16[64,896]{1,0:T(8,128)(2,1)S(1)} collective-permute-done((bf16[64,896]{1,0:T(8,128)(2,1)S(1)}, bf16[64,896]{1,0:T(8,128)(2,1)S(1)}, u32[]{:S(2)}, u32[]{:S(2)}) %collective-permute-start.10) | collective-permute-done | bytes 114720 | tf_op jit(solution)/shard_map/ppermute | solution.py:20
  24.0 3.0 %collective-permute-start.11 = (bf16[144,256]{1,0:T(8,128)(2,1)S(1)}, bf16[144,256]{1,0:T(8,128)(2,1)S(1)}, u32[]{:S(2)}, u32[]{:S(2)}) collective-permute-start(bf16[144,256]{1,0:T(8,128)(2,1)S(1)} %split.20), channel_id=1, source_target_pairs={{0,16},{4,20},{8,24},{12,28},{16,0},{20,4},{24,8},{28,12},{1,17},{... | collective-permute-start | bytes 221192 | tf_op jit(solution)/shard_map/ppermute | solution.py:20
  27.7 3.7 %attend_local.3.refs_0_ = bf16[16,128,512]{2,1,0:T(8,128)(2,1)} custom-call(s32[2]{0:T(128)S(1)} %pad_add_fusion.ranks_ref, s32[512]{0:T(512)S(1)} %copy-done.1, bf16[16,576,128]{2,1,0:T(8,128)(2,1)} %bitcast.13, bf16[16,576,256]{2,1,0:T(8,128)(2,1)} %bitcast.10), custom_call_target="tpu_custom_call" | custom-call | flops 285212672 | bytes 2293760 | tf_op jit(solution)/shard_map/attend_local/pallas_call | solution.py:130
  32.1 1.6 %collective-permute-start.15 = (bf16[576,256]{1,0:T(8,128)(2,1)S(1)}, bf16[576,256]{1,0:T(8,128)(2,1)S(1)}, u32[]{:S(2)}, u32[]{:S(2)}) collective-permute-start(bf16[576,256]{1,0:T(8,128)(2,1)S(1)} %pad_maximum_fusion.1), channel_id=1, source_target_pairs={{0,4},{4,0},{8,12},{12,8},{16,20},{20,16},{24,28},{28,24},{1,5},{5... | collective-permute-start | bytes 884744 | tf_op jit(solution)/shard_map/ppermute | solution.py:20
  34.3 6.2 %experts.2 = (bf16[512,896]{1,0:T(8,128)(2,1)S(1)}, bf16[512,896]{1,0:T(8,128)(2,1)S(1)}, bf16[3,256,3584]{2,1,0:T(8,128)(2,1)S(1)}) custom-call(s32[2]{0:T(128)S(1)} %pad_add_fusion.ranks_ref, bf16[64,3584]{1,0:T(8,128)(2,1)S(1)} %copy-done, bf16[64,1024]{1,0:T(8,128)(2,1)S(1)} %get-tuple-element.60.refs_1_, ...), custom_call_target="tpu_custom_call" | custom-call | tf_op jit(solution)/shard_map/experts/pallas_call | solution.py:317
  41.2 1.0 %collective-permute-start.20 = (bf16[576,256]{1,0:T(8,128)(2,1)S(1)}, bf16[576,256]{1,0:T(8,128)(2,1)S(1)}, u32[]{:S(2)}, u32[]{:S(2)}) collective-permute-start(bf16[576,256]{1,0:T(8,128)(2,1)S(1)} %broadcast_select_fusion.1), channel_id=1, source_target_pairs={{0,8},{4,12},{8,0},{12,4},{16,24},{20,28},{24,16},{28,20},{1,9},{5... | collective-permute-start | bytes 884744 | tf_op jit(solution)/shard_map/ppermute | solution.py:20
  42.4 1.2 %collective-permute-done.17 = bf16[512,896]{1,0:T(8,128)(2,1)S(1)} collective-permute-done((bf16[512,896]{1,0:T(8,128)(2,1)S(1)}, bf16[512,896]{1,0:T(8,128)(2,1)S(1)}, u32[]{:S(2)}, u32[]{:S(2)}) %collective-permute-start.17) | collective-permute-done | bytes 917536 | tf_op jit(solution)/shard_map/ppermute | solution.py:20
  43.9 1.6 %collective-permute-start.19 = (bf16[64,1792]{1,0:T(8,128)(2,1)S(1)}, bf16[64,1792]{1,0:T(8,128)(2,1)S(1)}, u32[]{:S(2)}, u32[]{:S(2)}) collective-permute-start(bf16[64,1792]{1,0:T(8,128)(2,1)S(1)} %pad_maximum_fusion.4), channel_id=1, source_target_pairs={{0,4},{4,0},{8,12},{12,8},{16,20},{20,16},{24,28},{28,24},{1,5},{5... | collective-permute-start | bytes 688136 | tf_op jit(solution)/shard_map/ppermute | solution.py:20
  46.1 5.6 %experts.3 = (bf16[256,896]{1,0:T(8,128)(2,1)S(1)}, bf16[256,896]{1,0:T(8,128)(2,1)S(1)}, bf16[512,896]{1,0:T(8,128)(2,1)S(1)}) custom-call(s32[2]{0:T(128)S(1)} %pad_add_fusion.ranks_ref, bf16[256,1024]{1,0:T(8,128)(2,1)S(1)} %constant_dynamic-update-slice_fusion.2.refs_0_, bf16[256,1024]{1,0:T(8,128)(2,1)S(1)} %collective-permute-done.14.refs_1_, ...), custom_call_target="tpu_custom_call" | custom-call | tf_op jit(solution)/shard_map/experts/pallas_call | solution.py:317
  51.7 1.2 %collective-permute-done.18 = bf16[128,896]{1,0:T(8,128)(2,1)S(1)} collective-permute-done((bf16[128,896]{1,0:T(8,128)(2,1)S(1)}, bf16[128,896]{1,0:T(8,128)(2,1)S(1)}, u32[]{:S(2)}, u32[]{:S(2)}) %collective-permute-start.18) | collective-permute-done | bytes 229408 | tf_op jit(solution)/shard_map/ppermute | solution.py:20
  53.5 1.2 %collective-permute-done.21 = bf16[256,896]{1,0:T(8,128)(2,1)S(1)} collective-permute-done((bf16[256,896]{1,0:T(8,128)(2,1)S(1)}, bf16[256,896]{1,0:T(8,128)(2,1)S(1)}, u32[]{:S(2)}, u32[]{:S(2)}) %collective-permute-start.21) | collective-permute-done | bytes 458784 | tf_op jit(solution)/shard_map/ppermute | solution.py:20
  55.6 1.0 %collective-permute-start.23 = (bf16[64,896]{1,0:T(8,128)(2,1)S(1)}, bf16[64,896]{1,0:T(8,128)(2,1)S(1)}, u32[]{:S(2)}, u32[]{:S(2)}) collective-permute-start(bf16[64,896]{1,0:T(8,128)(2,1)S(1)} %get-tuple-element.122), channel_id=1, source_target_pairs={{0,4},{4,0},{8,12},{12,8},{16,20},{20,16},{24,28},{28,24},{1,5},{5... | collective-permute-start | bytes 344072 | tf_op jit(solution)/shard_map/ppermute | solution.py:20
  56.7 1.6 %collective-permute-start.28 = (bf16[432,256]{1,0:T(8,128)(2,1)S(1)}, bf16[432,256]{1,0:T(8,128)(2,1)S(1)}, u32[]{:S(2)}, u32[]{:S(2)}) collective-permute-start(bf16[432,256]{1,0:T(8,128)(2,1)S(1)} %split.26), channel_id=1, source_target_pairs={{0,16},{4,20},{8,24},{12,28},{16,0},{20,4},{24,8},{28,12},{1,17},{... | collective-permute-start | bytes 663560 | tf_op jit(solution)/shard_map/ppermute | solution.py:20
  58.3 3.6 %attend_local.4.refs_0_ = bf16[16,128,512]{2,1,0:T(8,128)(2,1)} custom-call(s32[2]{0:T(128)S(1)} %pad_add_fusion.ranks_ref, s32[512]{0:T(512)S(1)} %copy-done.1, bf16[16,576,128]{2,1,0:T(8,128)(2,1)} %bitcast.14, bf16[16,576,256]{2,1,0:T(8,128)(2,1)} %bitcast.11, bf16[16,128,512]{2,1,0:T(8,128)(2,1)} %attend_local.3.refs_0_), custom_call_target="tpu_custom_call", output_to_operand_aliasing={{}: (4, {})} | custom-call | flops 285212672 | bytes 2293760 | tf_op jit(solution)/shard_map/attend_local/pallas_call | solution.py:130
  62.0 1.5 %collective-permute-start.27 = (bf16[128,896]{1,0:T(8,128)(2,1)S(1)}, bf16[128,896]{1,0:T(8,128)(2,1)S(1)}, u32[]{:S(2)}, u32[]{:S(2)}) collective-permute-start(bf16[128,896]{1,0:T(8,128)(2,1)S(1)} %add_convert_fusion.4), channel_id=1, source_target_pairs={{0,2},{1,3},{2,0},{3,1},{4,6},{5,7},{6,4},{7,5},{8,10},{9,11},{10,... | collective-permute-start | bytes 688136 | tf_op jit(solution)/shard_map/ppermute | solution.py:20
  64.4 0.9 %collective-permute-start.31 = (bf16[64,896]{1,0:T(8,128)(2,1)S(1)}, bf16[64,896]{1,0:T(8,128)(2,1)S(1)}, u32[]{:S(2)}, u32[]{:S(2)}) collective-permute-start(bf16[64,896]{1,0:T(8,128)(2,1)S(1)} %get-tuple-element.119), channel_id=1, source_target_pairs={{0,8},{4,12},{8,0},{12,4},{16,24},{20,28},{24,16},{28,20},{1,9},{5... | collective-permute-start | bytes 344072 | tf_op jit(solution)/shard_map/ppermute | solution.py:20
  66.0 5.6 %attend_local.5.old_ref = bf16[16,128,512]{2,1,0:T(8,128)(2,1)} custom-call(s32[2]{0:T(128)S(1)} %pad_add_fusion.ranks_ref, s32[512]{0:T(512)S(1)} %copy-done.1, bf16[16,576,128]{2,1,0:T(8,128)(2,1)} %bitcast.15, bf16[16,576,256]{2,1,0:T(8,128)(2,1)} %bitcast.12, bf16[16,128,512]{2,1,0:T(8,128)(2,1)} %attend_local.4.refs_0_), custom_call_target="tpu_custom_call", output_to_operand_aliasing={{}: (4, {})} | custom-call | flops 570425344 | bytes 4587520 | tf_op jit(solution)/shard_map/attend_local/pallas_call | solution.py:130
  71.7 1.5 %collective-permute-start.29 = (bf16[64,896]{1,0:T(8,128)(2,1)S(1)}, bf16[64,896]{1,0:T(8,128)(2,1)S(1)}, u32[]{:S(2)}, u32[]{:S(2)}) collective-permute-start(bf16[64,896]{1,0:T(8,128)(2,1)S(1)} %get-tuple-element.125), channel_id=1, source_target_pairs={{0,16},{4,20},{8,24},{12,28},{16,0},{20,4},{24,8},{28,12},{1,17},{... | collective-permute-start | bytes 344072 | tf_op jit(solution)/shard_map/ppermute | solution.py:20
  73.2 2.5 %collective-permute-start.30 = (bf16[64,896]{1,0:T(8,128)(2,1)S(1)}, bf16[64,896]{1,0:T(8,128)(2,1)S(1)}, u32[]{:S(2)}, u32[]{:S(2)}) collective-permute-start(bf16[64,896]{1,0:T(8,128)(2,1)S(1)} %get-tuple-element.124), channel_id=1, source_target_pairs={{0,24},{4,28},{8,16},{12,20},{16,8},{20,12},{24,0},{28,4},{1,25},{... | collective-permute-start | bytes 344072 | tf_op jit(solution)/shard_map/ppermute | solution.py:20
  75.8 2.7 %attend_traded.1 = bf16[16,128,512]{2,1,0:T(8,128)(2,1)} custom-call(s32[2]{0:T(128)S(1)} %pad_add_fusion.ranks_ref, s32[512]{0:T(512)S(1)} %copy-done.1, s32[32]{0:T(128)S(1)} %copy-done.2, s32[1]{0:T(128)S(6)} %copy.21.mask_ref, bf16[16,576,128]{2,1,0:T(8,128)(2,1)} %bitcast.16, ...), custom_call_target="tpu_custom_call", output_to_operand_aliasing={{}: (6, {})} | custom-call | flops 71303168 | bytes 573440 | tf_op jit(solution)/shard_map/attend_traded/pallas_call | solution.py:195
  78.5 3.8 %collective-permute-done.29 = bf16[64,896]{1,0:T(8,128)(2,1)S(1)} collective-permute-done((bf16[64,896]{1,0:T(8,128)(2,1)S(1)}, bf16[64,896]{1,0:T(8,128)(2,1)S(1)}, u32[]{:S(2)}, u32[]{:S(2)}) %collective-permute-start.29) | collective-permute-done | bytes 114720 | tf_op jit(solution)/shard_map/ppermute | solution.py:20
  82.2 0.7 add_convert_fusion.6
  (87 shorter events, 7.5 us)
Async XLA Ops:
  2.6 7.4 %collective-permute-start = (bf16[64,1024]{1,0:T(8,128)(2,1)S(1)}, bf16[64,1024]{1,0:T(8,128)(2,1)S(1)}, u32[]{:S(2)}, u32[]{:S(2)}) collective-permute-start(bf16[64,1024]{1,0:T(8,128)(2,1)S(1)} %get-tuple-element.60.refs_1_), channel_id=1, source_target_pairs={{0,8},{4,12},{8,0},{12,4},{16,24},{20,28},{24,16},{28,20},{1,9},{5... | collective-permute-start | bytes 393224 | tf_op jit(solution)/shard_map/ppermute | solution.py:20
  5.7 13.8 %collective-permute-start.3 = (bf16[64,1920]{1,0:T(8,128)(2,1)S(1)}, bf16[64,1920]{1,0:T(8,128)(2,1)S(1)}, u32[]{:S(2)}, u32[]{:S(2)}) collective-permute-start(bf16[64,1920]{1,0:T(8,128)(2,1)S(1)} %get-tuple-element.67), channel_id=1, source_target_pairs={{0,4},{4,0},{8,12},{12,8},{16,20},{20,16},{24,28},{28,24},{1,5},{5... | collective-permute-start | bytes 737288 | tf_op jit(solution)/shard_map/ppermute | solution.py:20
  7.2 12.3 %collective-permute-start.4 = (bf16[64,1024]{1,0:T(8,128)(2,1)S(1)}, bf16[64,1024]{1,0:T(8,128)(2,1)S(1)}, u32[]{:S(2)}, u32[]{:S(2)}) collective-permute-start(bf16[64,1024]{1,0:T(8,128)(2,1)S(1)} %get-tuple-element.60.refs_1_), channel_id=1, source_target_pairs={{0,16},{4,20},{8,24},{12,28},{16,0},{20,4},{24,8},{28,12},{1,17},{... | collective-permute-start | bytes 393224 | tf_op jit(solution)/shard_map/ppermute | solution.py:20
  9.8 9.7 %collective-permute-start.5 = (bf16[64,1024]{1,0:T(8,128)(2,1)S(1)}, bf16[64,1024]{1,0:T(8,128)(2,1)S(1)}, u32[]{:S(2)}, u32[]{:S(2)}) collective-permute-start(bf16[64,1024]{1,0:T(8,128)(2,1)S(1)} %get-tuple-element.60.refs_1_), channel_id=1, source_target_pairs={{0,24},{4,28},{8,16},{12,20},{16,8},{20,12},{24,0},{28,4},{1,25},{... | collective-permute-start | bytes 393224 | tf_op jit(solution)/shard_map/ppermute | solution.py:20
  10.0 9.5 %collective-permute-start.2 = (bf16[64,1024]{1,0:T(8,128)(2,1)S(1)}, bf16[64,1024]{1,0:T(8,128)(2,1)S(1)}, u32[]{:S(2)}, u32[]{:S(2)}) collective-permute-start(bf16[64,1024]{1,0:T(8,128)(2,1)S(1)} %collective-permute-done.refs_4_), channel_id=1, source_target_pairs={{0,4},{4,0},{8,12},{12,8},{16,20},{20,16},{24,28},{28,24},{1,5},{5... | collective-permute-start | bytes 393224 | tf_op jit(solution)/shard_map/ppermute | solution.py:20
  12.3 7.2 %collective-permute-start.1 = (bf16[64,896]{1,0:T(8,128)(2,1)S(1)}, bf16[64,896]{1,0:T(8,128)(2,1)S(1)}, u32[]{:S(2)}, u32[]{:S(2)}) collective-permute-start(bf16[64,896]{1,0:T(8,128)(2,1)S(1)} %slice.85), channel_id=1, source_target_pairs={{0,2},{1,3},{2,0},{3,1},{4,6},{5,7},{6,4},{7,5},{8,10},{9,11},{10,... | collective-permute-start | bytes 344072 | tf_op jit(solution)/shard_map/ppermute | solution.py:20
  19.7 11.7 %collective-permute-start.6 = (bf16[192,896]{1,0:T(8,128)(2,1)S(1)}, bf16[192,896]{1,0:T(8,128)(2,1)S(1)}, u32[]{:S(2)}, u32[]{:S(2)}) collective-permute-start(bf16[192,896]{1,0:T(8,128)(2,1)S(1)} %pad_maximum_fusion), channel_id=1, source_target_pairs={{0,2},{1,3},{2,0},{3,1},{4,6},{5,7},{6,4},{7,5},{8,10},{9,11},{10,... | collective-permute-start | bytes 1032200 | tf_op jit(solution)/shard_map/ppermute | solution.py:20
  21.2 6.5 %collective-permute-start.8 = (bf16[128,1024]{1,0:T(8,128)(2,1)S(1)}, bf16[128,1024]{1,0:T(8,128)(2,1)S(1)}, u32[]{:S(2)}, u32[]{:S(2)}) collective-permute-start(bf16[128,1024]{1,0:T(8,128)(2,1)S(1)} %pad_maximum_fusion.3), channel_id=1, source_target_pairs={{0,1},{1,0},{2,3},{3,2},{4,5},{5,4},{6,7},{7,6},{8,9},{9,8},{10,11... | collective-permute-start | bytes 786440 | tf_op jit(solution)/shard_map/ppermute | solution.py:20
  21.3 6.4 %collective-permute-start.9 = (bf16[64,1920]{1,0:T(8,128)(2,1)S(1)}, bf16[64,1920]{1,0:T(8,128)(2,1)S(1)}, u32[]{:S(2)}, u32[]{:S(2)}) collective-permute-start(bf16[64,1920]{1,0:T(8,128)(2,1)S(1)} %collective-permute-done.3.refs_2_), channel_id=1, source_target_pairs={{0,1},{1,0},{2,3},{3,2},{4,5},{5,4},{6,7},{7,6},{8,9},{9,8},{10,11... | collective-permute-start | bytes 737288 | tf_op jit(solution)/shard_map/ppermute | solution.py:20
  21.8 9.6 %collective-permute-start.7 = (bf16[128,1024]{1,0:T(8,128)(2,1)S(1)}, bf16[128,1024]{1,0:T(8,128)(2,1)S(1)}, u32[]{:S(2)}, u32[]{:S(2)}) collective-permute-start(bf16[128,1024]{1,0:T(8,128)(2,1)S(1)} %constant_dynamic-update-slice_fusion), channel_id=1, source_target_pairs={{0,4},{4,0},{8,12},{12,8},{16,20},{20,16},{24,28},{28,24},{1,5},{5... | collective-permute-start | bytes 786440 | tf_op jit(solution)/shard_map/ppermute | solution.py:20
  24.0 7.3 %collective-permute-start.11 = (bf16[144,256]{1,0:T(8,128)(2,1)S(1)}, bf16[144,256]{1,0:T(8,128)(2,1)S(1)}, u32[]{:S(2)}, u32[]{:S(2)}) collective-permute-start(bf16[144,256]{1,0:T(8,128)(2,1)S(1)} %split.20), channel_id=1, source_target_pairs={{0,16},{4,20},{8,24},{12,28},{16,0},{20,4},{24,8},{28,12},{1,17},{... | collective-permute-start | bytes 221192 | tf_op jit(solution)/shard_map/ppermute | solution.py:20
  31.4 2.9 %collective-permute-start.12 = (bf16[192,896]{1,0:T(8,128)(2,1)S(1)}, bf16[192,896]{1,0:T(8,128)(2,1)S(1)}, u32[]{:S(2)}, u32[]{:S(2)}) collective-permute-start(bf16[192,896]{1,0:T(8,128)(2,1)S(1)} %collective-permute-done.6), channel_id=1, source_target_pairs={{0,1},{1,0},{2,3},{3,2},{4,5},{5,4},{6,7},{7,6},{8,9},{9,8},{10,11... | collective-permute-start | bytes 1032200 | tf_op jit(solution)/shard_map/ppermute | solution.py:20
  31.5 9.6 %collective-permute-start.14 = (bf16[256,1024]{1,0:T(8,128)(2,1)S(1)}, bf16[256,1024]{1,0:T(8,128)(2,1)S(1)}, u32[]{:S(2)}, u32[]{:S(2)}) collective-permute-start(bf16[256,1024]{1,0:T(8,128)(2,1)S(1)} %constant_dynamic-update-slice_fusion.2.refs_0_), channel_id=1, source_target_pairs={{0,1},{1,0},{2,3},{3,2},{4,5},{5,4},{6,7},{7,6},{8,9},{9,8},{10,11... | collective-permute-start | bytes 1572872 | tf_op jit(solution)/shard_map/ppermute | solution.py:20
  32.1 9.0 %collective-permute-start.15 = (bf16[576,256]{1,0:T(8,128)(2,1)S(1)}, bf16[576,256]{1,0:T(8,128)(2,1)S(1)}, u32[]{:S(2)}, u32[]{:S(2)}) collective-permute-start(bf16[576,256]{1,0:T(8,128)(2,1)S(1)} %pad_maximum_fusion.1), channel_id=1, source_target_pairs={{0,4},{4,0},{8,12},{12,8},{16,20},{20,16},{24,28},{28,24},{1,5},{5... | collective-permute-start | bytes 884744 | tf_op jit(solution)/shard_map/ppermute | solution.py:20
  33.7 7.3 %collective-permute-start.13 = (bf16[128,896]{1,0:T(8,128)(2,1)S(1)}, bf16[128,896]{1,0:T(8,128)(2,1)S(1)}, u32[]{:S(2)}, u32[]{:S(2)}) collective-permute-start(bf16[128,896]{1,0:T(8,128)(2,1)S(1)} %slice.90), channel_id=1, source_target_pairs={{0,2},{1,3},{2,0},{3,1},{4,6},{5,7},{6,4},{7,5},{8,10},{9,11},{10,... | collective-permute-start | bytes 688136 | tf_op jit(solution)/shard_map/ppermute | solution.py:20
  41.1 2.5 %collective-permute-start.17 = (bf16[512,896]{1,0:T(8,128)(2,1)S(1)}, bf16[512,896]{1,0:T(8,128)(2,1)S(1)}, u32[]{:S(2)}, u32[]{:S(2)}) collective-permute-start(bf16[512,896]{1,0:T(8,128)(2,1)S(1)} %get-tuple-element.93), channel_id=1, source_target_pairs={{0,1},{1,0},{2,3},{3,2},{4,5},{5,4},{6,7},{7,6},{8,9},{9,8},{10,11... | collective-permute-start | bytes 2752520 | tf_op jit(solution)/shard_map/ppermute | solution.py:20
  41.2 10.4 %collective-permute-start.20 = (bf16[576,256]{1,0:T(8,128)(2,1)S(1)}, bf16[576,256]{1,0:T(8,128)(2,1)S(1)}, u32[]{:S(2)}, u32[]{:S(2)}) collective-permute-start(bf16[576,256]{1,0:T(8,128)(2,1)S(1)} %broadcast_select_fusion.1), channel_id=1, source_target_pairs={{0,8},{4,12},{8,0},{12,4},{16,24},{20,28},{24,16},{28,20},{1,9},{5... | collective-permute-start | bytes 884744 | tf_op jit(solution)/shard_map/ppermute | solution.py:20
  42.2 3.9 %collective-permute-start.16 = (bf16[128,896]{1,0:T(8,128)(2,1)S(1)}, bf16[128,896]{1,0:T(8,128)(2,1)S(1)}, u32[]{:S(2)}, u32[]{:S(2)}) collective-permute-start(bf16[128,896]{1,0:T(8,128)(2,1)S(1)} %collective-permute-done.13.refs_4_), channel_id=1, source_target_pairs={{0,1},{1,0},{2,3},{3,2},{4,5},{5,4},{6,7},{7,6},{8,9},{9,8},{10,11... | collective-permute-start | bytes 688136 | tf_op jit(solution)/shard_map/ppermute | solution.py:20
  43.9 7.8 %collective-permute-start.19 = (bf16[64,1792]{1,0:T(8,128)(2,1)S(1)}, bf16[64,1792]{1,0:T(8,128)(2,1)S(1)}, u32[]{:S(2)}, u32[]{:S(2)}) collective-permute-start(bf16[64,1792]{1,0:T(8,128)(2,1)S(1)} %pad_maximum_fusion.4), channel_id=1, source_target_pairs={{0,4},{4,0},{8,12},{12,8},{16,20},{20,16},{24,28},{28,24},{1,5},{5... | collective-permute-start | bytes 688136 | tf_op jit(solution)/shard_map/ppermute | solution.py:20
  45.4 7.4 %collective-permute-start.18 = (bf16[128,896]{1,0:T(8,128)(2,1)S(1)}, bf16[128,896]{1,0:T(8,128)(2,1)S(1)}, u32[]{:S(2)}, u32[]{:S(2)}) collective-permute-start(bf16[128,896]{1,0:T(8,128)(2,1)S(1)} %slice.114), channel_id=1, source_target_pairs={{0,2},{1,3},{2,0},{3,1},{4,6},{5,7},{6,4},{7,5},{8,10},{9,11},{10,... | collective-permute-start | bytes 688136 | tf_op jit(solution)/shard_map/ppermute | solution.py:20
  52.8 1.8 %collective-permute-start.21 = (bf16[256,896]{1,0:T(8,128)(2,1)S(1)}, bf16[256,896]{1,0:T(8,128)(2,1)S(1)}, u32[]{:S(2)}, u32[]{:S(2)}) collective-permute-start(bf16[256,896]{1,0:T(8,128)(2,1)S(1)} %get-tuple-element.96), channel_id=1, source_target_pairs={{0,1},{1,0},{2,3},{3,2},{4,5},{5,4},{6,7},{7,6},{8,9},{9,8},{10,11... | collective-permute-start | bytes 1376264 | tf_op jit(solution)/shard_map/ppermute | solution.py:20
  52.9 9.1 %collective-permute-start.24 = (bf16[64,896]{1,0:T(8,128)(2,1)S(1)}, bf16[64,896]{1,0:T(8,128)(2,1)S(1)}, u32[]{:S(2)}, u32[]{:S(2)}) collective-permute-start(bf16[64,896]{1,0:T(8,128)(2,1)S(1)} %add_convert_fusion.9), channel_id=1, source_target_pairs={{0,4},{4,0},{8,12},{12,8},{16,20},{20,16},{24,28},{28,24},{1,5},{5... | collective-permute-start | bytes 344072 | tf_op jit(solution)/shard_map/ppermute | solution.py:20
  54.8 7.2 %collective-permute-start.25 = (bf16[256,896]{1,0:T(8,128)(2,1)S(1)}, bf16[256,896]{1,0:T(8,128)(2,1)S(1)}, u32[]{:S(2)}, u32[]{:S(2)}) collective-permute-start(bf16[256,896]{1,0:T(8,128)(2,1)S(1)} %get-tuple-element.100), channel_id=1, source_target_pairs={{0,1},{1,0},{2,3},{3,2},{4,5},{5,4},{6,7},{7,6},{8,9},{9,8},{10,11... | collective-permute-start | bytes 1376264 | tf_op jit(solution)/shard_map/ppermute | solution.py:20
  55.0 6.9 %collective-permute-start.22 = (bf16[64,896]{1,0:T(8,128)(2,1)S(1)}, bf16[64,896]{1,0:T(8,128)(2,1)S(1)}, u32[]{:S(2)}, u32[]{:S(2)}) collective-permute-start(bf16[64,896]{1,0:T(8,128)(2,1)S(1)} %get-tuple-element.123), channel_id=1, source_target_pairs={{0,2},{1,3},{2,0},{3,1},{4,6},{5,7},{6,4},{7,5},{8,10},{9,11},{10,... | collective-permute-start | bytes 344072 | tf_op jit(solution)/shard_map/ppermute | solution.py:20
  55.6 6.3 %collective-permute-start.23 = (bf16[64,896]{1,0:T(8,128)(2,1)S(1)}, bf16[64,896]{1,0:T(8,128)(2,1)S(1)}, u32[]{:S(2)}, u32[]{:S(2)}) collective-permute-start(bf16[64,896]{1,0:T(8,128)(2,1)S(1)} %get-tuple-element.122), channel_id=1, source_target_pairs={{0,4},{4,0},{8,12},{12,8},{16,20},{20,16},{24,28},{28,24},{1,5},{5... | collective-permute-start | bytes 344072 | tf_op jit(solution)/shard_map/ppermute | solution.py:20
  56.7 14.8 %collective-permute-start.28 = (bf16[432,256]{1,0:T(8,128)(2,1)S(1)}, bf16[432,256]{1,0:T(8,128)(2,1)S(1)}, u32[]{:S(2)}, u32[]{:S(2)}) collective-permute-start(bf16[432,256]{1,0:T(8,128)(2,1)S(1)} %split.26), channel_id=1, source_target_pairs={{0,16},{4,20},{8,24},{12,28},{16,0},{20,4},{24,8},{28,12},{1,17},{... | collective-permute-start | bytes 663560 | tf_op jit(solution)/shard_map/ppermute | solution.py:20
  62.0 9.5 %collective-permute-start.27 = (bf16[128,896]{1,0:T(8,128)(2,1)S(1)}, bf16[128,896]{1,0:T(8,128)(2,1)S(1)}, u32[]{:S(2)}, u32[]{:S(2)}) collective-permute-start(bf16[128,896]{1,0:T(8,128)(2,1)S(1)} %add_convert_fusion.4), channel_id=1, source_target_pairs={{0,2},{1,3},{2,0},{3,1},{4,6},{5,7},{6,4},{7,5},{8,10},{9,11},{10,... | collective-permute-start | bytes 688136 | tf_op jit(solution)/shard_map/ppermute | solution.py:20
  63.7 7.8 %collective-permute-start.26 = (bf16[128,896]{1,0:T(8,128)(2,1)S(1)}, bf16[128,896]{1,0:T(8,128)(2,1)S(1)}, u32[]{:S(2)}, u32[]{:S(2)}) collective-permute-start(bf16[128,896]{1,0:T(8,128)(2,1)S(1)} %add_convert_fusion.5), channel_id=1, source_target_pairs={{0,4},{4,0},{8,12},{12,8},{16,20},{20,16},{24,28},{28,24},{1,5},{5... | collective-permute-start | bytes 688136 | tf_op jit(solution)/shard_map/ppermute | solution.py:20
  64.4 14.1 %collective-permute-start.31 = (bf16[64,896]{1,0:T(8,128)(2,1)S(1)}, bf16[64,896]{1,0:T(8,128)(2,1)S(1)}, u32[]{:S(2)}, u32[]{:S(2)}) collective-permute-start(bf16[64,896]{1,0:T(8,128)(2,1)S(1)} %get-tuple-element.119), channel_id=1, source_target_pairs={{0,8},{4,12},{8,0},{12,4},{16,24},{20,28},{24,16},{28,20},{1,9},{5... | collective-permute-start | bytes 344072 | tf_op jit(solution)/shard_map/ppermute | solution.py:20
  65.3 16.9 %collective-permute-start.32 = (bf16[64,896]{1,0:T(8,128)(2,1)S(1)}, bf16[64,896]{1,0:T(8,128)(2,1)S(1)}, u32[]{:S(2)}, u32[]{:S(2)}) collective-permute-start(bf16[64,896]{1,0:T(8,128)(2,1)S(1)} %get-tuple-element.118), channel_id=1, source_target_pairs={{0,2},{1,3},{2,0},{3,1},{4,6},{5,7},{6,4},{7,5},{8,10},{9,11},{10,... | collective-permute-start | bytes 344072 | tf_op jit(solution)/shard_map/ppermute | solution.py:20
  71.7 10.5 %collective-permute-start.29 = (bf16[64,896]{1,0:T(8,128)(2,1)S(1)}, bf16[64,896]{1,0:T(8,128)(2,1)S(1)}, u32[]{:S(2)}, u32[]{:S(2)}) collective-permute-start(bf16[64,896]{1,0:T(8,128)(2,1)S(1)} %get-tuple-element.125), channel_id=1, source_target_pairs={{0,16},{4,20},{8,24},{12,28},{16,0},{20,4},{24,8},{28,12},{1,17},{... | collective-permute-start | bytes 344072 | tf_op jit(solution)/shard_map/ppermute | solution.py:20
  73.2 9.0 %collective-permute-start.30 = (bf16[64,896]{1,0:T(8,128)(2,1)S(1)}, bf16[64,896]{1,0:T(8,128)(2,1)S(1)}, u32[]{:S(2)}, u32[]{:S(2)}) collective-permute-start(bf16[64,896]{1,0:T(8,128)(2,1)S(1)} %get-tuple-element.124), channel_id=1, source_target_pairs={{0,24},{4,28},{8,16},{12,20},{16,8},{20,12},{24,0},{28,4},{1,25},{... | collective-permute-start | bytes 344072 | tf_op jit(solution)/shard_map/ppermute | solution.py:20
  (4 other events, 18.1 us)

commit v12 on v11

--- a/solution.py
+++ b/solution.py
@@ -385,8 +385,6 @@
     rows = hidden.shape[0]
     pairs = ep_size // 2
     late = list(range(2, pairs))
-    half = len(late) // 2
-    rest = len(late) - half
     levels = ep_size.bit_length() - 1
     tie = lax.optimization_barrier
 
@@ -464,6 +462,7 @@
     (given,), own = first
     sent, kept = jnp.split(total_of(own, flip(given, "tp", 1)), 2, axis=0)
     last = flip(far_odds, "tp", 1)
+    sent, kept, last = tie((sent, kept, last))
     over_23 = flip(cut(sent, 2, 2), "tp", 2)
     over_1 = flip(jnp.concatenate([cut(kept, 1, 1), cut(sent, 1, 1)], axis=1), "ep", 1)
     swapped = flip(page, "ep", 2)
@@ -476,7 +475,7 @@
             ranks, pieces, w_gate, w_up, w_down, 2 * len(late) * rows, columns, top, False, 2
         )
     ]
-    second, over_23, over_1, swapped = tie((second, over_23, over_1, swapped))
+    second, over_23, swapped = tie((second, over_23, swapped))
     page = page_take(page, swapped, 1)
     upper, lower = jnp.split(page, [least], axis=0)
     swapped, lower = page_far(lower)
@@ -484,23 +483,18 @@
     late_sent, late_kept = jnp.split(own, 2, axis=0)
     late_sent = total_of(late_sent, flip(cross, "tp", 1))
     over_3 = flip(total_of(cut(kept, 3, 1), cut(over_23, 1, 1)), "ep", 1)
-    zero = flip(total_of(cut(sent, 0, 1), over_1[:, columns:]), "tp", 2)
     late_sent, side, queries = tie((late_sent, side, queries))
     side = flip(side, "tp", 1)
 
-    over_y = flip(cut(late_sent, len(late), half), "tp", 2)
-    over_x = flip(cut(late_sent, len(late) + half, rest), "ep", 1)
+    odd = flip(cut(late_sent, len(late), len(late)), "tp", 2)
+    even = flip(cut(late_sent, 0, len(late)), "tp", 2)
     attended = attend_part(
         ranks, lengths, queries, cache_pages, groups, some, some, attended
     )
-    over_y, over_x, over_3, side, attended = tie((over_y, over_x, over_3, side, attended))
+    odd, over_1, over_3, side, attended = tie((odd, over_1, over_3, side, attended))
+    zero = flip(total_of(cut(sent, 0, 1), over_1[:, columns:]), "tp", 2)
     late_kept = total_of(late_kept, side)
-    odd = total_of(
-        cut(late_kept, len(late), len(late)), jnp.pad(over_y, ((0, rest * rows), (0, 0)))
-    )
-    odd = flip(odd, "ep", 1)
-    even = total_of(cut(late_sent, 0, len(late)), jnp.pad(over_x, ((half * rows, 0), (0, 0))))
-    even = flip(even, "tp", 2)
+    odd = flip(total_of(cut(late_kept, len(late), len(late)), odd), "ep", 1)
     attended = attend_part(
         ranks, lengths, queries, cache_pages, groups, 2 * some, count - 2 * some, attended
     )

time: 83.3 us -> 82.9 us (level)
  waiting for transfers between devices: 10.6 us -> 9.49 us
    ppermute x33 -> x32, waiting for transfers between devices: 10.6 us -> 9.49 us  [flip(): return lax.ppermute(block, axis, [(i, i ^ apart) for i in range(count)])]
    ppermute x33 -> x32, starting transfers between devices: 35.1 us -> 35.8 us  [flip(): return lax.ppermute(block, axis, [(i, i ^ apart) for i in range(count)])]
  transfers between devices with their start and end apart: 33 -> 32, of which waited for: 8 -> 8; matrix products, arithmetic and copies ran while one was open for 1% -> 2% of each run, Pallas kernels for 38% -> 38%
where the time goes in v12:
time: 82.9 us; the launch traced here: 82.6 us
  starting transfers between devices  35.8 us (43%)
  Pallas kernels  33.5 us (40%)
  waiting for transfers between devices  9.49 us (11%)
  other arithmetic  1.78 us (2%)
  between operations  1.69 us (2%)
    ppermute x32, starting transfers between devices, flip(): return lax.ppermute(block, axis, [(i, i ^ apart) for i in range(count)])  35.8 us
    pallas_call x3, Pallas kernels, attend_part(): pl.pallas_call(kernel, out_shape=jax.ShapeDtypeStruct((count, heads, LAT)...  12.9 us
    pallas_call x2, Pallas kernels, run_experts(): pl.pallas_call(kernel, out_shape=[[pltpu.VMEM((2 * rows // given, columns...  11.8 us
    ppermute x32, waiting for transfers between devices, flip(): return lax.ppermute(block, axis, [(i, i ^ apart) for i in range(count)])  9.49 us
    pallas_call x1, Pallas kernels, load(): pl.pallas_call(load_kernel, out_shape=[pltpu.VMEM(w.shape, w.dtype) for w...  4.21 us
    pallas_call x1, Pallas kernels, attend_traded(): pl.pallas_call(functools.partial(attend_traded_kernel, groups), out_shape...  2.71 us
    pallas_call x1, Pallas kernels, pick(): pl.pallas_call(functools.partial(pick_kernel, groups), out_shape=(pltpu.V...  1.89 us
  transfers between devices with their start and end apart: 32, of which 8 were waited for; matrix products, arithmetic and copies ran while one was open for 2% of the time, Pallas kernels for 38%

profile of v12, /device:TPU:0, one launch (start us, length us, event | category | flops | bytes accessed | tf_op | source)
XLA Modules:
  0.0 82.6 jit_solution(15850742300397870585)
XLA Ops:
  0.7 1.9 %pick.1 = (bf16[64,1024]{1,0:T(8,128)(2,1)S(1)}, bf16[64,1920]{1,0:T(8,128)(2,1)S(1)}, bf16[576,256]{1,0:T(8,128)(2,1)S(1)}) custom-call(s32[2]{0:T(128)S(1)} %pad_add_fusion.ranks_ref, s32[32]{0:T(128)} %slots_ref.3, s32[8,64]{1,0:T(8,128)} %bitcast.17, f32[8,64]{1,0:T(8,128)} %bitcast.18, bf16[64,3584]{1,0:T(8,128)(2,1)} %refs_0_.2, ...), custom_call_target="tpu_custom_call" | custom-call | tf_op jit(solution)/shard_map/pick/pallas_call | solution.py:96
  2.6 3.1 %collective-permute-start = (bf16[64,1024]{1,0:T(8,128)(2,1)S(1)}, bf16[64,1024]{1,0:T(8,128)(2,1)S(1)}, u32[]{:S(2)}, u32[]{:S(2)}) collective-permute-start(bf16[64,1024]{1,0:T(8,128)(2,1)S(1)} %get-tuple-element.62.refs_1_), channel_id=1, source_target_pairs={{0,8},{4,12},{8,0},{12,4},{16,24},{20,28},{24,16},{28,20},{1,9},{5... | collective-permute-start | bytes 393224 | tf_op jit(solution)/shard_map/ppermute | solution.py:20
  5.7 1.5 %collective-permute-start.3 = (bf16[64,1920]{1,0:T(8,128)(2,1)S(1)}, bf16[64,1920]{1,0:T(8,128)(2,1)S(1)}, u32[]{:S(2)}, u32[]{:S(2)}) collective-permute-start(bf16[64,1920]{1,0:T(8,128)(2,1)S(1)} %get-tuple-element.69), channel_id=1, source_target_pairs={{0,4},{4,0},{8,12},{12,8},{16,20},{20,16},{24,28},{28,24},{1,5},{5... | collective-permute-start | bytes 737288 | tf_op jit(solution)/shard_map/ppermute | solution.py:20
  7.2 2.6 %collective-permute-start.4 = (bf16[64,1024]{1,0:T(8,128)(2,1)S(1)}, bf16[64,1024]{1,0:T(8,128)(2,1)S(1)}, u32[]{:S(2)}, u32[]{:S(2)}) collective-permute-start(bf16[64,1024]{1,0:T(8,128)(2,1)S(1)} %get-tuple-element.62.refs_1_), channel_id=1, source_target_pairs={{0,16},{4,20},{8,24},{12,28},{16,0},{20,4},{24,8},{28,12},{1,17},{... | collective-permute-start | bytes 393224 | tf_op jit(solution)/shard_map/ppermute | solution.py:20
  10.0 2.3 %collective-permute-start.2 = (bf16[64,1024]{1,0:T(8,128)(2,1)S(1)}, bf16[64,1024]{1,0:T(8,128)(2,1)S(1)}, u32[]{:S(2)}, u32[]{:S(2)}) collective-permute-start(bf16[64,1024]{1,0:T(8,128)(2,1)S(1)} %collective-permute-done.refs_4_), channel_id=1, source_target_pairs={{0,4},{4,0},{8,12},{12,8},{16,20},{20,16},{24,28},{28,24},{1,5},{5... | collective-permute-start | bytes 393224 | tf_op jit(solution)/shard_map/ppermute | solution.py:20
  12.3 1.5 %collective-permute-start.1 = (bf16[64,896]{1,0:T(8,128)(2,1)S(1)}, bf16[64,896]{1,0:T(8,128)(2,1)S(1)}, u32[]{:S(2)}, u32[]{:S(2)}) collective-permute-start(bf16[64,896]{1,0:T(8,128)(2,1)S(1)} %slice.75), channel_id=1, source_target_pairs={{0,2},{1,3},{2,0},{3,1},{4,6},{5,7},{6,4},{7,5},{8,10},{9,11},{10,... | collective-permute-start | bytes 344072 | tf_op jit(solution)/shard_map/ppermute | solution.py:20
  13.9 4.2 %load.1 = (bf16[3,3584,256]{2,1,0:T(8,128)(2,1)S(1)}, bf16[3,3584,256]{2,1,0:T(8,128)(2,1)S(1)}) custom-call(bf16[3,3584,256]{2,1,0:T(8,128)(2,1)} %refs_0_.1, bf16[3,3584,256]{2,1,0:T(8,128)(2,1)} %refs_1_), custom_call_target="tpu_custom_call" | custom-call | bytes 11010048 | tf_op jit(solution)/shard_map/load/pallas_call | solution.py:166
  18.1 1.4 %collective-permute-done.4 = bf16[64,1024]{1,0:T(8,128)(2,1)S(1)} collective-permute-done((bf16[64,1024]{1,0:T(8,128)(2,1)S(1)}, bf16[64,1024]{1,0:T(8,128)(2,1)S(1)}, u32[]{:S(2)}, u32[]{:S(2)}) %collective-permute-start.4) | collective-permute-done | bytes 131104 | tf_op jit(solution)/shard_map/ppermute | solution.py:20
  19.6 1.6 %collective-permute-start.6 = (bf16[192,896]{1,0:T(8,128)(2,1)S(1)}, bf16[192,896]{1,0:T(8,128)(2,1)S(1)}, u32[]{:S(2)}, u32[]{:S(2)}) collective-permute-start(bf16[192,896]{1,0:T(8,128)(2,1)S(1)} %pad_maximum_fusion), channel_id=1, source_target_pairs={{0,2},{1,3},{2,0},{3,1},{4,6},{5,7},{6,4},{7,5},{8,10},{9,11},{10,... | collective-permute-start | bytes 1032200 | tf_op jit(solution)/shard_map/ppermute | solution.py:20
  21.8 0.9 %collective-permute-start.7 = (bf16[128,1024]{1,0:T(8,128)(2,1)S(1)}, bf16[128,1024]{1,0:T(8,128)(2,1)S(1)}, u32[]{:S(2)}, u32[]{:S(2)}) collective-permute-start(bf16[128,1024]{1,0:T(8,128)(2,1)S(1)} %constant_dynamic-update-slice_fusion), channel_id=1, source_target_pairs={{0,4},{4,0},{8,12},{12,8},{16,20},{20,16},{24,28},{28,24},{1,5},{5... | collective-permute-start | bytes 786440 | tf_op jit(solution)/shard_map/ppermute | solution.py:20
  22.7 1.3 %collective-permute-done.10.refs_8_ = bf16[64,896]{1,0:T(8,128)(2,1)S(1)} collective-permute-done((bf16[64,896]{1,0:T(8,128)(2,1)S(1)}, bf16[64,896]{1,0:T(8,128)(2,1)S(1)}, u32[]{:S(2)}, u32[]{:S(2)}) %collective-permute-start.10) | collective-permute-done | bytes 114720 | tf_op jit(solution)/shard_map/ppermute | solution.py:20
  24.0 3.0 %collective-permute-start.11 = (bf16[144,256]{1,0:T(8,128)(2,1)S(1)}, bf16[144,256]{1,0:T(8,128)(2,1)S(1)}, u32[]{:S(2)}, u32[]{:S(2)}) collective-permute-start(bf16[144,256]{1,0:T(8,128)(2,1)S(1)} %split.24), channel_id=1, source_target_pairs={{0,16},{4,20},{8,24},{12,28},{16,0},{20,4},{24,8},{28,12},{1,17},{... | collective-permute-start | bytes 221192 | tf_op jit(solution)/shard_map/ppermute | solution.py:20
  27.7 3.7 %attend_local.3.refs_0_ = bf16[16,128,512]{2,1,0:T(8,128)(2,1)} custom-call(s32[2]{0:T(128)S(1)} %pad_add_fusion.ranks_ref, s32[512]{0:T(512)S(1)} %copy-done.1, bf16[16,576,128]{2,1,0:T(8,128)(2,1)} %bitcast.13, bf16[16,576,256]{2,1,0:T(8,128)(2,1)} %bitcast.10), custom_call_target="tpu_custom_call" | custom-call | flops 285212672 | bytes 2293760 | tf_op jit(solution)/shard_map/attend_local/pallas_call | solution.py:130
  32.1 1.6 %collective-permute-start.15 = (bf16[576,256]{1,0:T(8,128)(2,1)S(1)}, bf16[576,256]{1,0:T(8,128)(2,1)S(1)}, u32[]{:S(2)}, u32[]{:S(2)}) collective-permute-start(bf16[576,256]{1,0:T(8,128)(2,1)S(1)} %pad_maximum_fusion.1), channel_id=1, source_target_pairs={{0,4},{4,0},{8,12},{12,8},{16,20},{20,16},{24,28},{28,24},{1,5},{5... | collective-permute-start | bytes 884744 | tf_op jit(solution)/shard_map/ppermute | solution.py:20
  34.3 6.2 %experts.2 = (bf16[512,896]{1,0:T(8,128)(2,1)S(1)}, bf16[512,896]{1,0:T(8,128)(2,1)S(1)}, bf16[3,256,3584]{2,1,0:T(8,128)(2,1)S(1)}) custom-call(s32[2]{0:T(128)S(1)} %pad_add_fusion.ranks_ref, bf16[64,3584]{1,0:T(8,128)(2,1)S(1)} %copy-done, bf16[64,1024]{1,0:T(8,128)(2,1)S(1)} %get-tuple-element.62.refs_1_, ...), custom_call_target="tpu_custom_call" | custom-call | tf_op jit(solution)/shard_map/experts/pallas_call | solution.py:317
  41.7 1.1 %collective-permute-start.19 = (bf16[576,256]{1,0:T(8,128)(2,1)S(1)}, bf16[576,256]{1,0:T(8,128)(2,1)S(1)}, u32[]{:S(2)}, u32[]{:S(2)}) collective-permute-start(bf16[576,256]{1,0:T(8,128)(2,1)S(1)} %broadcast_select_fusion.1), channel_id=1, source_target_pairs={{0,8},{4,12},{8,0},{12,4},{16,24},{20,28},{24,16},{28,20},{1,9},{5... | collective-permute-start | bytes 884744 | tf_op jit(solution)/shard_map/ppermute | solution.py:20
  42.7 0.8 %collective-permute-done.16 = bf16[512,896]{1,0:T(8,128)(2,1)S(1)} collective-permute-done((bf16[512,896]{1,0:T(8,128)(2,1)S(1)}, bf16[512,896]{1,0:T(8,128)(2,1)S(1)}, u32[]{:S(2)}, u32[]{:S(2)}) %collective-permute-start.16) | collective-permute-done | bytes 917536 | tf_op jit(solution)/shard_map/ppermute | solution.py:20
  43.9 1.1 %collective-permute-start.18 = (bf16[128,896]{1,0:T(8,128)(2,1)S(1)}, bf16[128,896]{1,0:T(8,128)(2,1)S(1)}, u32[]{:S(2)}, u32[]{:S(2)}) collective-permute-start(bf16[128,896]{1,0:T(8,128)(2,1)S(1)} %slice.83), channel_id=1, source_target_pairs={{0,2},{1,3},{2,0},{3,1},{4,6},{5,7},{6,4},{7,5},{8,10},{9,11},{10,... | collective-permute-start | bytes 688136 | tf_op jit(solution)/shard_map/ppermute | solution.py:20
  45.1 5.6 %experts.3 = (bf16[256,896]{1,0:T(8,128)(2,1)S(1)}, bf16[256,896]{1,0:T(8,128)(2,1)S(1)}, bf16[512,896]{1,0:T(8,128)(2,1)S(1)}) custom-call(s32[2]{0:T(128)S(1)} %pad_add_fusion.ranks_ref, bf16[256,1024]{1,0:T(8,128)(2,1)S(1)} %constant_dynamic-update-slice_fusion.2.refs_0_, bf16[256,1024]{1,0:T(8,128)(2,1)S(1)} %collective-permute-done.14.refs_1_, ...), custom_call_target="tpu_custom_call" | custom-call | tf_op jit(solution)/shard_map/experts/pallas_call | solution.py:317
  50.7 0.9 %collective-permute-done.18 = bf16[128,896]{1,0:T(8,128)(2,1)S(1)} collective-permute-done((bf16[128,896]{1,0:T(8,128)(2,1)S(1)}, bf16[128,896]{1,0:T(8,128)(2,1)S(1)}, u32[]{:S(2)}, u32[]{:S(2)}) %collective-permute-start.18) | collective-permute-done | bytes 229408 | tf_op jit(solution)/shard_map/ppermute | solution.py:20
  51.7 1.6 %collective-permute-start.22 = (bf16[64,1792]{1,0:T(8,128)(2,1)S(1)}, bf16[64,1792]{1,0:T(8,128)(2,1)S(1)}, u32[]{:S(2)}, u32[]{:S(2)}) collective-permute-start(bf16[64,1792]{1,0:T(8,128)(2,1)S(1)} %pad_maximum_fusion.4), channel_id=1, source_target_pairs={{0,4},{4,0},{8,12},{12,8},{16,20},{20,16},{24,28},{28,24},{1,5},{5... | collective-permute-start | bytes 688136 | tf_op jit(solution)/shard_map/ppermute | solution.py:20
  54.1 1.1 %collective-permute-start.21 = (bf16[128,896]{1,0:T(8,128)(2,1)S(1)}, bf16[128,896]{1,0:T(8,128)(2,1)S(1)}, u32[]{:S(2)}, u32[]{:S(2)}) collective-permute-start(bf16[128,896]{1,0:T(8,128)(2,1)S(1)} %get-tuple-element.125), channel_id=1, source_target_pairs={{0,2},{1,3},{2,0},{3,1},{4,6},{5,7},{6,4},{7,5},{8,10},{9,11},{10,... | collective-permute-start | bytes 688136 | tf_op jit(solution)/shard_map/ppermute | solution.py:20
  55.3 1.6 %collective-permute-start.27 = (bf16[432,256]{1,0:T(8,128)(2,1)S(1)}, bf16[432,256]{1,0:T(8,128)(2,1)S(1)}, u32[]{:S(2)}, u32[]{:S(2)}) collective-permute-start(bf16[432,256]{1,0:T(8,128)(2,1)S(1)} %split.34), channel_id=1, source_target_pairs={{0,16},{4,20},{8,24},{12,28},{16,0},{20,4},{24,8},{28,12},{1,17},{... | collective-permute-start | bytes 663560 | tf_op jit(solution)/shard_map/ppermute | solution.py:20
  56.9 3.6 %attend_local.4.refs_0_ = bf16[16,128,512]{2,1,0:T(8,128)(2,1)} custom-call(s32[2]{0:T(128)S(1)} %pad_add_fusion.ranks_ref, s32[512]{0:T(512)S(1)} %copy-done.1, bf16[16,576,128]{2,1,0:T(8,128)(2,1)} %bitcast.14, bf16[16,576,256]{2,1,0:T(8,128)(2,1)} %bitcast.11, bf16[16,128,512]{2,1,0:T(8,128)(2,1)} %attend_local.3.refs_0_), custom_call_target="tpu_custom_call", output_to_operand_aliasing={{}: (4, {})} | custom-call | flops 285212672 | bytes 2293760 | tf_op jit(solution)/shard_map/attend_local/pallas_call | solution.py:130
  60.5 1.5 %collective-permute-start.26 = (bf16[128,896]{1,0:T(8,128)(2,1)S(1)}, bf16[128,896]{1,0:T(8,128)(2,1)S(1)}, u32[]{:S(2)}, u32[]{:S(2)}) collective-permute-start(bf16[128,896]{1,0:T(8,128)(2,1)S(1)} %get-tuple-element.124), channel_id=1, source_target_pairs={{0,2},{1,3},{2,0},{3,1},{4,6},{5,7},{6,4},{7,5},{8,10},{9,11},{10,... | collective-permute-start | bytes 688136 | tf_op jit(solution)/shard_map/ppermute | solution.py:20
  62.4 1.6 %collective-permute-start.25 = (bf16[128,896]{1,0:T(8,128)(2,1)S(1)}, bf16[128,896]{1,0:T(8,128)(2,1)S(1)}, u32[]{:S(2)}, u32[]{:S(2)}) collective-permute-start(bf16[128,896]{1,0:T(8,128)(2,1)S(1)} %add_convert_fusion.4), channel_id=1, source_target_pairs={{0,4},{4,0},{8,12},{12,8},{16,20},{20,16},{24,28},{28,24},{1,5},{5... | collective-permute-start | bytes 688136 | tf_op jit(solution)/shard_map/ppermute | solution.py:20
  64.2 1.1 %collective-permute-start.31 = (bf16[64,896]{1,0:T(8,128)(2,1)S(1)}, bf16[64,896]{1,0:T(8,128)(2,1)S(1)}, u32[]{:S(2)}, u32[]{:S(2)}) collective-permute-start(bf16[64,896]{1,0:T(8,128)(2,1)S(1)} %add_convert_fusion.6), channel_id=1, source_target_pairs={{0,2},{1,3},{2,0},{3,1},{4,6},{5,7},{6,4},{7,5},{8,10},{9,11},{10,... | collective-permute-start | bytes 344072 | tf_op jit(solution)/shard_map/ppermute | solution.py:20
  65.2 5.6 %attend_local.5.old_ref = bf16[16,128,512]{2,1,0:T(8,128)(2,1)} custom-call(s32[2]{0:T(128)S(1)} %pad_add_fusion.ranks_ref, s32[512]{0:T(512)S(1)} %copy-done.1, bf16[16,576,128]{2,1,0:T(8,128)(2,1)} %bitcast.15, bf16[16,576,256]{2,1,0:T(8,128)(2,1)} %bitcast.12, bf16[16,128,512]{2,1,0:T(8,128)(2,1)} %attend_local.4.refs_0_), custom_call_target="tpu_custom_call", output_to_operand_aliasing={{}: (4, {})} | custom-call | flops 570425344 | bytes 4587520 | tf_op jit(solution)/shard_map/attend_local/pallas_call | solution.py:130
  71.0 1.6 %collective-permute-start.28 = (bf16[64,896]{1,0:T(8,128)(2,1)S(1)}, bf16[64,896]{1,0:T(8,128)(2,1)S(1)}, u32[]{:S(2)}, u32[]{:S(2)}) collective-permute-start(bf16[64,896]{1,0:T(8,128)(2,1)S(1)} %get-tuple-element.127), channel_id=1, source_target_pairs={{0,16},{4,20},{8,24},{12,28},{16,0},{20,4},{24,8},{28,12},{1,17},{... | collective-permute-start | bytes 344072 | tf_op jit(solution)/shard_map/ppermute | solution.py:20
  72.5 2.3 %collective-permute-start.29 = (bf16[64,896]{1,0:T(8,128)(2,1)S(1)}, bf16[64,896]{1,0:T(8,128)(2,1)S(1)}, u32[]{:S(2)}, u32[]{:S(2)}) collective-permute-start(bf16[64,896]{1,0:T(8,128)(2,1)S(1)} %get-tuple-element.126), channel_id=1, source_target_pairs={{0,24},{4,28},{8,16},{12,20},{16,8},{20,12},{24,0},{28,4},{1,25},{... | collective-permute-start | bytes 344072 | tf_op jit(solution)/shard_map/ppermute | solution.py:20
  74.9 2.7 %attend_traded.1 = bf16[16,128,512]{2,1,0:T(8,128)(2,1)} custom-call(s32[2]{0:T(128)S(1)} %pad_add_fusion.ranks_ref, s32[512]{0:T(512)S(1)} %copy-done.1, s32[32]{0:T(128)S(1)} %copy-done.2, s32[1]{0:T(128)S(6)} %copy.21.mask_ref, bf16[16,576,128]{2,1,0:T(8,128)(2,1)} %bitcast.16, ...), custom_call_target="tpu_custom_call", output_to_operand_aliasing={{}: (6, {})} | custom-call | flops 71303168 | bytes 573440 | tf_op jit(solution)/shard_map/attend_traded/pallas_call | solution.py:195
  77.6 4.2 %collective-permute-done.28 = bf16[64,896]{1,0:T(8,128)(2,1)S(1)} collective-permute-done((bf16[64,896]{1,0:T(8,128)(2,1)S(1)}, bf16[64,896]{1,0:T(8,128)(2,1)S(1)}, u32[]{:S(2)}, u32[]{:S(2)}) %collective-permute-start.28) | collective-permute-done | bytes 114720 | tf_op jit(solution)/shard_map/ppermute | solution.py:20
  (87 shorter events, 6.3 us)
Async XLA Ops:
  2.6 7.4 %collective-permute-start = (bf16[64,1024]{1,0:T(8,128)(2,1)S(1)}, bf16[64,1024]{1,0:T(8,128)(2,1)S(1)}, u32[]{:S(2)}, u32[]{:S(2)}) collective-permute-start(bf16[64,1024]{1,0:T(8,128)(2,1)S(1)} %get-tuple-element.62.refs_1_), channel_id=1, source_target_pairs={{0,8},{4,12},{8,0},{12,4},{16,24},{20,28},{24,16},{28,20},{1,9},{5... | collective-permute-start | bytes 393224 | tf_op jit(solution)/shard_map/ppermute | solution.py:20
  5.7 13.8 %collective-permute-start.3 = (bf16[64,1920]{1,0:T(8,128)(2,1)S(1)}, bf16[64,1920]{1,0:T(8,128)(2,1)S(1)}, u32[]{:S(2)}, u32[]{:S(2)}) collective-permute-start(bf16[64,1920]{1,0:T(8,128)(2,1)S(1)} %get-tuple-element.69), channel_id=1, source_target_pairs={{0,4},{4,0},{8,12},{12,8},{16,20},{20,16},{24,28},{28,24},{1,5},{5... | collective-permute-start | bytes 737288 | tf_op jit(solution)/shard_map/ppermute | solution.py:20
  7.2 12.3 %collective-permute-start.4 = (bf16[64,1024]{1,0:T(8,128)(2,1)S(1)}, bf16[64,1024]{1,0:T(8,128)(2,1)S(1)}, u32[]{:S(2)}, u32[]{:S(2)}) collective-permute-start(bf16[64,1024]{1,0:T(8,128)(2,1)S(1)} %get-tuple-element.62.refs_1_), channel_id=1, source_target_pairs={{0,16},{4,20},{8,24},{12,28},{16,0},{20,4},{24,8},{28,12},{1,17},{... | collective-permute-start | bytes 393224 | tf_op jit(solution)/shard_map/ppermute | solution.py:20
  9.8 9.7 %collective-permute-start.5 = (bf16[64,1024]{1,0:T(8,128)(2,1)S(1)}, bf16[64,1024]{1,0:T(8,128)(2,1)S(1)}, u32[]{:S(2)}, u32[]{:S(2)}) collective-permute-start(bf16[64,1024]{1,0:T(8,128)(2,1)S(1)} %get-tuple-element.62.refs_1_), channel_id=1, source_target_pairs={{0,24},{4,28},{8,16},{12,20},{16,8},{20,12},{24,0},{28,4},{1,25},{... | collective-permute-start | bytes 393224 | tf_op jit(solution)/shard_map/ppermute | solution.py:20
  10.0 9.5 %collective-permute-start.2 = (bf16[64,1024]{1,0:T(8,128)(2,1)S(1)}, bf16[64,1024]{1,0:T(8,128)(2,1)S(1)}, u32[]{:S(2)}, u32[]{:S(2)}) collective-permute-start(bf16[64,1024]{1,0:T(8,128)(2,1)S(1)} %collective-permute-done.refs_4_), channel_id=1, source_target_pairs={{0,4},{4,0},{8,12},{12,8},{16,20},{20,16},{24,28},{28,24},{1,5},{5... | collective-permute-start | bytes 393224 | tf_op jit(solution)/shard_map/ppermute | solution.py:20
  12.3 7.1 %collective-permute-start.1 = (bf16[64,896]{1,0:T(8,128)(2,1)S(1)}, bf16[64,896]{1,0:T(8,128)(2,1)S(1)}, u32[]{:S(2)}, u32[]{:S(2)}) collective-permute-start(bf16[64,896]{1,0:T(8,128)(2,1)S(1)} %slice.75), channel_id=1, source_target_pairs={{0,2},{1,3},{2,0},{3,1},{4,6},{5,7},{6,4},{7,5},{8,10},{9,11},{10,... | collective-permute-start | bytes 344072 | tf_op jit(solution)/shard_map/ppermute | solution.py:20
  19.6 11.8 %collective-permute-start.6 = (bf16[192,896]{1,0:T(8,128)(2,1)S(1)}, bf16[192,896]{1,0:T(8,128)(2,1)S(1)}, u32[]{:S(2)}, u32[]{:S(2)}) collective-permute-start(bf16[192,896]{1,0:T(8,128)(2,1)S(1)} %pad_maximum_fusion), channel_id=1, source_target_pairs={{0,2},{1,3},{2,0},{3,1},{4,6},{5,7},{6,4},{7,5},{8,10},{9,11},{10,... | collective-permute-start | bytes 1032200 | tf_op jit(solution)/shard_map/ppermute | solution.py:20
  21.2 6.5 %collective-permute-start.8 = (bf16[128,1024]{1,0:T(8,128)(2,1)S(1)}, bf16[128,1024]{1,0:T(8,128)(2,1)S(1)}, u32[]{:S(2)}, u32[]{:S(2)}) collective-permute-start(bf16[128,1024]{1,0:T(8,128)(2,1)S(1)} %pad_maximum_fusion.3), channel_id=1, source_target_pairs={{0,1},{1,0},{2,3},{3,2},{4,5},{5,4},{6,7},{7,6},{8,9},{9,8},{10,11... | collective-permute-start | bytes 786440 | tf_op jit(solution)/shard_map/ppermute | solution.py:20
  21.3 6.4 %collective-permute-start.9 = (bf16[64,1920]{1,0:T(8,128)(2,1)S(1)}, bf16[64,1920]{1,0:T(8,128)(2,1)S(1)}, u32[]{:S(2)}, u32[]{:S(2)}) collective-permute-start(bf16[64,1920]{1,0:T(8,128)(2,1)S(1)} %collective-permute-done.3.refs_2_), channel_id=1, source_target_pairs={{0,1},{1,0},{2,3},{3,2},{4,5},{5,4},{6,7},{7,6},{8,9},{9,8},{10,11... | collective-permute-start | bytes 737288 | tf_op jit(solution)/shard_map/ppermute | solution.py:20
  21.8 9.6 %collective-permute-start.7 = (bf16[128,1024]{1,0:T(8,128)(2,1)S(1)}, bf16[128,1024]{1,0:T(8,128)(2,1)S(1)}, u32[]{:S(2)}, u32[]{:S(2)}) collective-permute-start(bf16[128,1024]{1,0:T(8,128)(2,1)S(1)} %constant_dynamic-update-slice_fusion), channel_id=1, source_target_pairs={{0,4},{4,0},{8,12},{12,8},{16,20},{20,16},{24,28},{28,24},{1,5},{5... | collective-permute-start | bytes 786440 | tf_op jit(solution)/shard_map/ppermute | solution.py:20
  22.7 1.3 %collective-permute-start.10 = (bf16[64,896]{1,0:T(8,128)(2,1)S(1)}, bf16[64,896]{1,0:T(8,128)(2,1)S(1)}, u32[]{:S(2)}, u32[]{:S(2)}) collective-permute-start(bf16[64,896]{1,0:T(8,128)(2,1)S(1)} %collective-permute-done.1.refs_7_), channel_id=1, source_target_pairs={{0,1},{1,0},{2,3},{3,2},{4,5},{5,4},{6,7},{7,6},{8,9},{9,8},{10,11... | collective-permute-start | bytes 344072 | tf_op jit(solution)/shard_map/ppermute | solution.py:20
  24.0 7.3 %collective-permute-start.11 = (bf16[144,256]{1,0:T(8,128)(2,1)S(1)}, bf16[144,256]{1,0:T(8,128)(2,1)S(1)}, u32[]{:S(2)}, u32[]{:S(2)}) collective-permute-start(bf16[144,256]{1,0:T(8,128)(2,1)S(1)} %split.24), channel_id=1, source_target_pairs={{0,16},{4,20},{8,24},{12,28},{16,0},{20,4},{24,8},{28,12},{1,17},{... | collective-permute-start | bytes 221192 | tf_op jit(solution)/shard_map/ppermute | solution.py:20
  31.4 2.9 %collective-permute-start.12 = (bf16[192,896]{1,0:T(8,128)(2,1)S(1)}, bf16[192,896]{1,0:T(8,128)(2,1)S(1)}, u32[]{:S(2)}, u32[]{:S(2)}) collective-permute-start(bf16[192,896]{1,0:T(8,128)(2,1)S(1)} %collective-permute-done.6), channel_id=1, source_target_pairs={{0,1},{1,0},{2,3},{3,2},{4,5},{5,4},{6,7},{7,6},{8,9},{9,8},{10,11... | collective-permute-start | bytes 1032200 | tf_op jit(solution)/shard_map/ppermute | solution.py:20
  31.5 9.6 %collective-permute-start.14 = (bf16[256,1024]{1,0:T(8,128)(2,1)S(1)}, bf16[256,1024]{1,0:T(8,128)(2,1)S(1)}, u32[]{:S(2)}, u32[]{:S(2)}) collective-permute-start(bf16[256,1024]{1,0:T(8,128)(2,1)S(1)} %constant_dynamic-update-slice_fusion.2.refs_0_), channel_id=1, source_target_pairs={{0,1},{1,0},{2,3},{3,2},{4,5},{5,4},{6,7},{7,6},{8,9},{9,8},{10,11... | collective-permute-start | bytes 1572872 | tf_op jit(solution)/shard_map/ppermute | solution.py:20
  32.1 9.0 %collective-permute-start.15 = (bf16[576,256]{1,0:T(8,128)(2,1)S(1)}, bf16[576,256]{1,0:T(8,128)(2,1)S(1)}, u32[]{:S(2)}, u32[]{:S(2)}) collective-permute-start(bf16[576,256]{1,0:T(8,128)(2,1)S(1)} %pad_maximum_fusion.1), channel_id=1, source_target_pairs={{0,4},{4,0},{8,12},{12,8},{16,20},{20,16},{24,28},{28,24},{1,5},{5... | collective-permute-start | bytes 884744 | tf_op jit(solution)/shard_map/ppermute | solution.py:20
  33.7 7.3 %collective-permute-start.13 = (bf16[128,896]{1,0:T(8,128)(2,1)S(1)}, bf16[128,896]{1,0:T(8,128)(2,1)S(1)}, u32[]{:S(2)}, u32[]{:S(2)}) collective-permute-start(bf16[128,896]{1,0:T(8,128)(2,1)S(1)} %slice.80), channel_id=1, source_target_pairs={{0,2},{1,3},{2,0},{3,1},{4,6},{5,7},{6,4},{7,5},{8,10},{9,11},{10,... | collective-permute-start | bytes 688136 | tf_op jit(solution)/shard_map/ppermute | solution.py:20
  41.1 2.5 %collective-permute-start.16 = (bf16[512,896]{1,0:T(8,128)(2,1)S(1)}, bf16[512,896]{1,0:T(8,128)(2,1)S(1)}, u32[]{:S(2)}, u32[]{:S(2)}) collective-permute-start(bf16[512,896]{1,0:T(8,128)(2,1)S(1)} %get-tuple-element.91), channel_id=1, source_target_pairs={{0,1},{1,0},{2,3},{3,2},{4,5},{5,4},{6,7},{7,6},{8,9},{9,8},{10,11... | collective-permute-start | bytes 2752520 | tf_op jit(solution)/shard_map/ppermute | solution.py:20
  41.1 2.8 %collective-permute-start.17 = (bf16[128,896]{1,0:T(8,128)(2,1)S(1)}, bf16[128,896]{1,0:T(8,128)(2,1)S(1)}, u32[]{:S(2)}, u32[]{:S(2)}) collective-permute-start(bf16[128,896]{1,0:T(8,128)(2,1)S(1)} %collective-permute-done.13.refs_4_), channel_id=1, source_target_pairs={{0,1},{1,0},{2,3},{3,2},{4,5},{5,4},{6,7},{7,6},{8,9},{9,8},{10,11... | collective-permute-start | bytes 688136 | tf_op jit(solution)/shard_map/ppermute | solution.py:20
  41.7 9.0 %collective-permute-start.19 = (bf16[576,256]{1,0:T(8,128)(2,1)S(1)}, bf16[576,256]{1,0:T(8,128)(2,1)S(1)}, u32[]{:S(2)}, u32[]{:S(2)}) collective-permute-start(bf16[576,256]{1,0:T(8,128)(2,1)S(1)} %broadcast_select_fusion.1), channel_id=1, source_target_pairs={{0,8},{4,12},{8,0},{12,4},{16,24},{20,28},{24,16},{28,20},{1,9},{5... | collective-permute-start | bytes 884744 | tf_op jit(solution)/shard_map/ppermute | solution.py:20
  43.9 7.7 %collective-permute-start.18 = (bf16[128,896]{1,0:T(8,128)(2,1)S(1)}, bf16[128,896]{1,0:T(8,128)(2,1)S(1)}, u32[]{:S(2)}, u32[]{:S(2)}) collective-permute-start(bf16[128,896]{1,0:T(8,128)(2,1)S(1)} %slice.83), channel_id=1, source_target_pairs={{0,2},{1,3},{2,0},{3,1},{4,6},{5,7},{6,4},{7,5},{8,10},{9,11},{10,... | collective-permute-start | bytes 688136 | tf_op jit(solution)/shard_map/ppermute | solution.py:20
  51.6 2.2 %collective-permute-start.20 = (bf16[256,896]{1,0:T(8,128)(2,1)S(1)}, bf16[256,896]{1,0:T(8,128)(2,1)S(1)}, u32[]{:S(2)}, u32[]{:S(2)}) collective-permute-start(bf16[256,896]{1,0:T(8,128)(2,1)S(1)} %get-tuple-element.100), channel_id=1, source_target_pairs={{0,1},{1,0},{2,3},{3,2},{4,5},{5,4},{6,7},{7,6},{8,9},{9,8},{10,11... | collective-permute-start | bytes 1376264 | tf_op jit(solution)/shard_map/ppermute | solution.py:20
  51.7 8.9 %collective-permute-start.22 = (bf16[64,1792]{1,0:T(8,128)(2,1)S(1)}, bf16[64,1792]{1,0:T(8,128)(2,1)S(1)}, u32[]{:S(2)}, u32[]{:S(2)}) collective-permute-start(bf16[64,1792]{1,0:T(8,128)(2,1)S(1)} %pad_maximum_fusion.4), channel_id=1, source_target_pairs={{0,4},{4,0},{8,12},{12,8},{16,20},{20,16},{24,28},{28,24},{1,5},{5... | collective-permute-start | bytes 688136 | tf_op jit(solution)/shard_map/ppermute | solution.py:20
  53.3 8.9 %collective-permute-start.23 = (bf16[64,896]{1,0:T(8,128)(2,1)S(1)}, bf16[64,896]{1,0:T(8,128)(2,1)S(1)}, u32[]{:S(2)}, u32[]{:S(2)}) collective-permute-start(bf16[64,896]{1,0:T(8,128)(2,1)S(1)} %add_convert_fusion.8), channel_id=1, source_target_pairs={{0,4},{4,0},{8,12},{12,8},{16,20},{20,16},{24,28},{28,24},{1,5},{5... | collective-permute-start | bytes 344072 | tf_op jit(solution)/shard_map/ppermute | solution.py:20
  54.0 8.2 %collective-permute-start.24 = (bf16[256,896]{1,0:T(8,128)(2,1)S(1)}, bf16[256,896]{1,0:T(8,128)(2,1)S(1)}, u32[]{:S(2)}, u32[]{:S(2)}) collective-permute-start(bf16[256,896]{1,0:T(8,128)(2,1)S(1)} %get-tuple-element.105), channel_id=1, source_target_pairs={{0,1},{1,0},{2,3},{3,2},{4,5},{5,4},{6,7},{7,6},{8,9},{9,8},{10,11... | collective-permute-start | bytes 1376264 | tf_op jit(solution)/shard_map/ppermute | solution.py:20
  54.1 8.1 %collective-permute-start.21 = (bf16[128,896]{1,0:T(8,128)(2,1)S(1)}, bf16[128,896]{1,0:T(8,128)(2,1)S(1)}, u32[]{:S(2)}, u32[]{:S(2)}) collective-permute-start(bf16[128,896]{1,0:T(8,128)(2,1)S(1)} %get-tuple-element.125), channel_id=1, source_target_pairs={{0,2},{1,3},{2,0},{3,1},{4,6},{5,7},{6,4},{7,5},{8,10},{9,11},{10,... | collective-permute-start | bytes 688136 | tf_op jit(solution)/shard_map/ppermute | solution.py:20
  55.3 15.5 %collective-permute-start.27 = (bf16[432,256]{1,0:T(8,128)(2,1)S(1)}, bf16[432,256]{1,0:T(8,128)(2,1)S(1)}, u32[]{:S(2)}, u32[]{:S(2)}) collective-permute-start(bf16[432,256]{1,0:T(8,128)(2,1)S(1)} %split.34), channel_id=1, source_target_pairs={{0,16},{4,20},{8,24},{12,28},{16,0},{20,4},{24,8},{28,12},{1,17},{... | collective-permute-start | bytes 663560 | tf_op jit(solution)/shard_map/ppermute | solution.py:20
  60.5 10.3 %collective-permute-start.26 = (bf16[128,896]{1,0:T(8,128)(2,1)S(1)}, bf16[128,896]{1,0:T(8,128)(2,1)S(1)}, u32[]{:S(2)}, u32[]{:S(2)}) collective-permute-start(bf16[128,896]{1,0:T(8,128)(2,1)S(1)} %get-tuple-element.124), channel_id=1, source_target_pairs={{0,2},{1,3},{2,0},{3,1},{4,6},{5,7},{6,4},{7,5},{8,10},{9,11},{10,... | collective-permute-start | bytes 688136 | tf_op jit(solution)/shard_map/ppermute | solution.py:20
  62.4 8.4 %collective-permute-start.25 = (bf16[128,896]{1,0:T(8,128)(2,1)S(1)}, bf16[128,896]{1,0:T(8,128)(2,1)S(1)}, u32[]{:S(2)}, u32[]{:S(2)}) collective-permute-start(bf16[128,896]{1,0:T(8,128)(2,1)S(1)} %add_convert_fusion.4), channel_id=1, source_target_pairs={{0,4},{4,0},{8,12},{12,8},{16,20},{20,16},{24,28},{28,24},{1,5},{5... | collective-permute-start | bytes 688136 | tf_op jit(solution)/shard_map/ppermute | solution.py:20
  64.0 13.6 %collective-permute-start.30 = (bf16[64,896]{1,0:T(8,128)(2,1)S(1)}, bf16[64,896]{1,0:T(8,128)(2,1)S(1)}, u32[]{:S(2)}, u32[]{:S(2)}) collective-permute-start(bf16[64,896]{1,0:T(8,128)(2,1)S(1)} %add_convert_fusion.7), channel_id=1, source_target_pairs={{0,8},{4,12},{8,0},{12,4},{16,24},{20,28},{24,16},{28,20},{1,9},{5... | collective-permute-start | bytes 344072 | tf_op jit(solution)/shard_map/ppermute | solution.py:20
  64.2 17.7 %collective-permute-start.31 = (bf16[64,896]{1,0:T(8,128)(2,1)S(1)}, bf16[64,896]{1,0:T(8,128)(2,1)S(1)}, u32[]{:S(2)}, u32[]{:S(2)}) collective-permute-start(bf16[64,896]{1,0:T(8,128)(2,1)S(1)} %add_convert_fusion.6), channel_id=1, source_target_pairs={{0,2},{1,3},{2,0},{3,1},{4,6},{5,7},{6,4},{7,5},{8,10},{9,11},{10,... | collective-permute-start | bytes 344072 | tf_op jit(solution)/shard_map/ppermute | solution.py:20
  71.0 10.9 %collective-permute-start.28 = (bf16[64,896]{1,0:T(8,128)(2,1)S(1)}, bf16[64,896]{1,0:T(8,128)(2,1)S(1)}, u32[]{:S(2)}, u32[]{:S(2)}) collective-permute-start(bf16[64,896]{1,0:T(8,128)(2,1)S(1)} %get-tuple-element.127), channel_id=1, source_target_pairs={{0,16},{4,20},{8,24},{12,28},{16,0},{20,4},{24,8},{28,12},{1,17},{... | collective-permute-start | bytes 344072 | tf_op jit(solution)/shard_map/ppermute | solution.py:20
  72.5 9.3 %collective-permute-start.29 = (bf16[64,896]{1,0:T(8,128)(2,1)S(1)}, bf16[64,896]{1,0:T(8,128)(2,1)S(1)}, u32[]{:S(2)}, u32[]{:S(2)}) collective-permute-start(bf16[64,896]{1,0:T(8,128)(2,1)S(1)} %get-tuple-element.126), channel_id=1, source_target_pairs={{0,24},{4,28},{8,16},{12,20},{16,8},{20,12},{24,0},{28,4},{1,25},{... | collective-permute-start | bytes 344072 | tf_op jit(solution)/shard_map/ppermute | solution.py:20
  (3 other events, 16.7 us)

commit v13 on v11

--- a/solution.py
+++ b/solution.py
@@ -142,11 +142,7 @@
         ),
         input_output_aliases={4: 0} if earlier else {},
         compiler_params=pltpu.CompilerParams(vmem_limit_bytes=8 * MIB),
-        cost_estimate=pl.CostEstimate(
-            flops=2 * some * heads * slots * (width + LAT),
-            bytes_accessed=2 * some * (heads * (width + LAT) + slots * width),
-            transcendentals=some * heads * slots,
-        ),
+        cost_estimate=pl.CostEstimate(flops=0, bytes_accessed=0, transcendentals=0),
         name="attend_local",
     )(ranks, lengths, in_hbm(queries), in_hbm(pages), *earlier)
 
@@ -177,43 +173,74 @@
     )(*[in_hbm(w) for w in arrays])
 
 
-def attend_traded_kernel(
-    groups, ranks_ref, lengths_ref, slots_ref, mask_ref, query_ref, page_ref, old_ref, out_ref
+def attend_rest(
+    ranks, lengths, swap_slot, swap_mask, queries, pages, page, attended, groups, first
 ):
-    partner = device_of(ranks_ref, groups, mask_ref[0])
-    length = lengths_ref[partner * old_ref.shape[0] + slots_ref[partner]]
-    out_ref[0] = attend_body(query_ref[0], page_ref[...], length)
-
-
-def attend_traded(ranks, lengths, swap_slot, swap_mask, queries, page, attended, groups):
-    _, width, heads = queries.shape
-    slots = page.shape[1]
-
-    def mine(i, ranks_ref, lengths_ref, slots_ref, mask_ref):
-        return slots_ref[device_of(ranks_ref, groups)], 0, 0
+    count, width, heads = queries.shape
+    slots = pages.shape[2]
+    some = count - first
+
+    def kernel(
+        ranks_ref,
+        lengths_ref,
+        slots_ref,
+        mask_ref,
+        query_ref,
+        pages_ref,
+        page_ref,
+        old_ref,
+        out_ref,
+    ):
+        step = pl.program_id(0)
+
+        @pl.when(step < some)
+        def _():
+            at = device_of(ranks_ref, groups) * count + first + step
+            out_ref[0] = attend_body(query_ref[0], pages_ref[0], lengths_ref[at])
+
+        @pl.when(step == some)
+        def _():
+            partner = device_of(ranks_ref, groups, mask_ref[0])
+            length = lengths_ref[partner * count + slots_ref[partner]]
+            out_ref[0] = attend_body(query_ref[0], page_ref[...], length)
+
+    def request(i, ranks_ref, lengths_ref, slots_ref, mask_ref):
+        return jnp.where(i < some, first + i, slots_ref[device_of(ranks_ref, groups)]), 0, 0
 
     return pl.pallas_call(
-        functools.partial(attend_traded_kernel, groups),
+        kernel,
         out_shape=jax.ShapeDtypeStruct(attended.shape, attended.dtype),
         grid_spec=pltpu.PrefetchScalarGridSpec(
             num_scalar_prefetch=4,
-            grid=(1,),
+            grid=(some + 1,),
             in_specs=[
-                pl.BlockSpec((1, width, heads), mine),
+                pl.BlockSpec((1, width, heads), request),
+                pl.BlockSpec(
+                    (1, width, slots), lambda i, *_: (jnp.minimum(first + i, count - 1), 0, 0)
+                ),
                 pl.BlockSpec((width, slots), lambda i, *_: (0, 0)),
                 ANYWHERE,
             ],
-            out_specs=pl.BlockSpec((1, heads, LAT), mine),
+            out_specs=pl.BlockSpec((1, heads, LAT), request),
         ),
-        input_output_aliases={6: 0},
-        compiler_params=pltpu.CompilerParams(vmem_limit_bytes=4 * MIB),
+        input_output_aliases={7: 0},
+        compiler_params=pltpu.CompilerParams(vmem_limit_bytes=6 * MIB),
         cost_estimate=pl.CostEstimate(
             flops=2 * heads * slots * (width + LAT),
             bytes_accessed=2 * (heads * (width + LAT) + slots * width),
             transcendentals=heads * slots,
         ),
-        name="attend_traded",
-    )(ranks, lengths, swap_slot, swap_mask, in_hbm(queries), page, attended)
+        name="attend_rest",
+    )(
+        ranks,
+        lengths,
+        swap_slot,
+        swap_mask,
+        in_hbm(queries),
+        in_hbm(pages),
+        page,
+        attended,
+    )
 
 
 def experts_kernel(
@@ -419,8 +446,8 @@
     far_2 = flip(bare(near_2), "tp", 2)
     near_3 = flip(near_2, "ep", 1)
     w_gate, w_up = load(w_gate, w_up)
-    far_2, near_3, w_gate, w_up, page, both_1, *late_pieces = tie(
-        (far_2, near_3, w_gate, w_up, page, both_1, *late_pieces)
+    far_2, near_3, w_gate, w_up, page, *late_pieces = tie(
+        (far_2, near_3, w_gate, w_up, page, *late_pieces)
     )
     near_late = jnp.concatenate(late_pieces, axis=0)
     far_3 = flip(jnp.concatenate([bare(near_3), bare(near_late)], axis=0), "tp", 2)
@@ -490,10 +517,7 @@
 
     over_y = flip(cut(late_sent, len(late), half), "tp", 2)
     over_x = flip(cut(late_sent, len(late) + half, rest), "ep", 1)
-    attended = attend_part(
-        ranks, lengths, queries, cache_pages, groups, some, some, attended
-    )
-    over_y, over_x, over_3, side, attended = tie((over_y, over_x, over_3, side, attended))
+    over_y, over_x, over_3, side, queries = tie((over_y, over_x, over_3, side, queries))
     late_kept = total_of(late_kept, side)
     odd = total_of(
         cut(late_kept, len(late), len(late)), jnp.pad(over_y, ((0, rest * rows), (0, 0)))
@@ -502,7 +526,7 @@
     even = total_of(cut(late_sent, 0, len(late)), jnp.pad(over_x, ((half * rows, 0), (0, 0))))
     even = flip(even, "tp", 2)
     attended = attend_part(
-        ranks, lengths, queries, cache_pages, groups, 2 * some, count - 2 * some, attended
+        ranks, lengths, queries, cache_pages, groups, some, 2 * some, attended
     )
     odd, even, attended, swapped = tie((odd, even, attended, swapped))
     lower = page_take(lower, swapped, 2) if levels > 2 else lower
@@ -510,8 +534,17 @@
     even = total_of(cut(late_kept, 0, len(late)), even, odd)
     back = [flip(cut(even, i, 1), "ep", 2 * m) for i, m in enumerate(late)]
     back.append(flip(total_of(cut(kept, 2, 1), cut(over_23, 0, 1), over_3), "ep", 2))
-    attended = attend_traded(
-        ranks, lengths, swap_slot, swap_mask, queries, page, attended, groups
+    attended = attend_rest(
+        ranks,
+        lengths,
+        swap_slot,
+        swap_mask,
+        queries,
+        cache_pages,
+        page,
+        attended,
+        groups,
+        3 * some,
     )
     *back, attended = tie((*back, attended))
     moe_out = total_of(cut(kept, 0, 1), over_1[:, :columns], zero, *back)

time: 83.3 us -> 82 us (0.984)
  starting transfers between devices: 35.1 us -> 33.6 us
    pallas_call x3 -> x2, Pallas kernels: 12.9 us -> 9.22 us  [attend_part(): pl.pallas_call(kernel, out_shape=jax.ShapeDtypeStruct((count, heads, LAT)...]
    pallas_call x1, Pallas kernels: 2.71 us -> 6.05 us  [attend_rest(): pl.pallas_call(kernel, out_shape=jax.ShapeDtypeStruct(attended.shape, att...]
    ppermute x33, starting transfers between devices: 35.1 us -> 33.6 us  [flip(): return lax.ppermute(block, axis, [(i, i ^ apart) for i in range(count)])]
  transfers between devices with their start and end apart: 33 -> 33, of which waited for: 8 -> 11; matrix products, arithmetic and copies ran while one was open for 1% -> 2% of each run, Pallas kernels for 38% -> 38%
where the time goes in v13:
time: 82 us; the launch traced here: 81.6 us
  starting transfers between devices  33.6 us (41%)
  Pallas kernels  33.2 us (40%)
  waiting for transfers between devices  10.9 us (13%)
  other arithmetic  1.84 us (2%)
  between operations  1.69 us (2%)
    ppermute x33, starting transfers between devices, flip(): return lax.ppermute(block, axis, [(i, i ^ apart) for i in range(count)])  33.6 us
    pallas_call x2, Pallas kernels, run_experts(): pl.pallas_call(kernel, out_shape=[[pltpu.VMEM((2 * rows // given, columns...  11.8 us
    ppermute x33, waiting for transfers between devices, flip(): return lax.ppermute(block, axis, [(i, i ^ apart) for i in range(count)])  10.9 us
    pallas_call x2, Pallas kernels, attend_part(): pl.pallas_call(kernel, out_shape=jax.ShapeDtypeStruct((count, heads, LAT)...  9.22 us
    pallas_call x1, Pallas kernels, attend_rest(): pl.pallas_call(kernel, out_shape=jax.ShapeDtypeStruct(attended.shape, att...  6.05 us
    pallas_call x1, Pallas kernels, load(): pl.pallas_call(load_kernel, out_shape=[pltpu.VMEM(w.shape, w.dtype) for w...  4.21 us
    pallas_call x1, Pallas kernels, pick(): pl.pallas_call(functools.partial(pick_kernel, groups), out_shape=(pltpu.V...  1.89 us
  transfers between devices with their start and end apart: 33, of which 11 were waited for; matrix products, arithmetic and copies ran while one was open for 2% of the time, Pallas kernels for 38%

profile of v13, /device:TPU:0, one launch (start us, length us, event | category | flops | bytes accessed | tf_op | source)
XLA Modules:
  0.0 81.6 jit_solution(17078655156937789214)
XLA Ops:
  0.7 1.9 %pick.1 = (bf16[64,1024]{1,0:T(8,128)(2,1)S(1)}, bf16[64,1920]{1,0:T(8,128)(2,1)S(1)}, bf16[576,256]{1,0:T(8,128)(2,1)S(1)}) custom-call(s32[2]{0:T(128)S(1)} %pad_add_fusion.ranks_ref, s32[32]{0:T(128)} %slots_ref.3, s32[8,64]{1,0:T(8,128)} %bitcast.16, f32[8,64]{1,0:T(8,128)} %bitcast.17, bf16[64,3584]{1,0:T(8,128)(2,1)} %refs_0_.2, ...), custom_call_target="tpu_custom_call" | custom-call | tf_op jit(solution)/shard_map/pick/pallas_call | solution.py:96
  2.6 3.1 %collective-permute-start = (bf16[64,1024]{1,0:T(8,128)(2,1)S(1)}, bf16[64,1024]{1,0:T(8,128)(2,1)S(1)}, u32[]{:S(2)}, u32[]{:S(2)}) collective-permute-start(bf16[64,1024]{1,0:T(8,128)(2,1)S(1)} %get-tuple-element.59.refs_1_), channel_id=1, source_target_pairs={{0,8},{4,12},{8,0},{12,4},{16,24},{20,28},{24,16},{28,20},{1,9},{5... | collective-permute-start | bytes 393224 | tf_op jit(solution)/shard_map/ppermute | solution.py:20
  5.7 2.6 %collective-permute-start.3 = (bf16[64,1024]{1,0:T(8,128)(2,1)S(1)}, bf16[64,1024]{1,0:T(8,128)(2,1)S(1)}, u32[]{:S(2)}, u32[]{:S(2)}) collective-permute-start(bf16[64,1024]{1,0:T(8,128)(2,1)S(1)} %get-tuple-element.59.refs_1_), channel_id=1, source_target_pairs={{0,16},{4,20},{8,24},{12,28},{16,0},{20,4},{24,8},{28,12},{1,17},{... | collective-permute-start | bytes 393224 | tf_op jit(solution)/shard_map/ppermute | solution.py:20
  8.3 2.5 %collective-permute-done.refs_4_ = bf16[64,1024]{1,0:T(8,128)(2,1)S(1)} collective-permute-done((bf16[64,1024]{1,0:T(8,128)(2,1)S(1)}, bf16[64,1024]{1,0:T(8,128)(2,1)S(1)}, u32[]{:S(2)}, u32[]{:S(2)}) %collective-permute-start) | collective-permute-done | bytes 131104 | tf_op jit(solution)/shard_map/ppermute | solution.py:20
  10.8 1.7 %collective-permute-start.2 = (bf16[64,1024]{1,0:T(8,128)(2,1)S(1)}, bf16[64,1024]{1,0:T(8,128)(2,1)S(1)}, u32[]{:S(2)}, u32[]{:S(2)}) collective-permute-start(bf16[64,1024]{1,0:T(8,128)(2,1)S(1)} %collective-permute-done.refs_4_), channel_id=1, source_target_pairs={{0,4},{4,0},{8,12},{12,8},{16,20},{20,16},{24,28},{28,24},{1,5},{5... | collective-permute-start | bytes 393224 | tf_op jit(solution)/shard_map/ppermute | solution.py:20
  12.5 1.5 %collective-permute-start.1 = (bf16[64,896]{1,0:T(8,128)(2,1)S(1)}, bf16[64,896]{1,0:T(8,128)(2,1)S(1)}, u32[]{:S(2)}, u32[]{:S(2)}) collective-permute-start(bf16[64,896]{1,0:T(8,128)(2,1)S(1)} %slice.85), channel_id=1, source_target_pairs={{0,2},{1,3},{2,0},{3,1},{4,6},{5,7},{6,4},{7,5},{8,10},{9,11},{10,... | collective-permute-start | bytes 344072 | tf_op jit(solution)/shard_map/ppermute | solution.py:20
  14.6 4.2 %load.1 = (bf16[3,3584,256]{2,1,0:T(8,128)(2,1)S(1)}, bf16[3,3584,256]{2,1,0:T(8,128)(2,1)S(1)}) custom-call(bf16[3,3584,256]{2,1,0:T(8,128)(2,1)} %refs_0_.1, bf16[3,3584,256]{2,1,0:T(8,128)(2,1)} %refs_1_), custom_call_target="tpu_custom_call" | custom-call | bytes 11010048 | tf_op jit(solution)/shard_map/load/pallas_call | solution.py:162
  19.0 1.4 %collective-permute-start.5 = (bf16[192,896]{1,0:T(8,128)(2,1)S(1)}, bf16[192,896]{1,0:T(8,128)(2,1)S(1)}, u32[]{:S(2)}, u32[]{:S(2)}) collective-permute-start(bf16[192,896]{1,0:T(8,128)(2,1)S(1)} %pad_maximum_fusion), channel_id=1, source_target_pairs={{0,2},{1,3},{2,0},{3,1},{4,6},{5,7},{6,4},{7,5},{8,10},{9,11},{10,... | collective-permute-start | bytes 1032200 | tf_op jit(solution)/shard_map/ppermute | solution.py:20
  20.4 1.6 %collective-permute-start.6 = (bf16[128,1024]{1,0:T(8,128)(2,1)S(1)}, bf16[128,1024]{1,0:T(8,128)(2,1)S(1)}, u32[]{:S(2)}, u32[]{:S(2)}) collective-permute-start(bf16[128,1024]{1,0:T(8,128)(2,1)S(1)} %constant_dynamic-update-slice_fusion), channel_id=1, source_target_pairs={{0,4},{4,0},{8,12},{12,8},{16,20},{20,16},{24,28},{28,24},{1,5},{5... | collective-permute-start | bytes 786440 | tf_op jit(solution)/shard_map/ppermute | solution.py:20
  22.5 1.2 %collective-permute-done.10.refs_8_ = bf16[64,896]{1,0:T(8,128)(2,1)S(1)} collective-permute-done((bf16[64,896]{1,0:T(8,128)(2,1)S(1)}, bf16[64,896]{1,0:T(8,128)(2,1)S(1)}, u32[]{:S(2)}, u32[]{:S(2)}) %collective-permute-start.10) | collective-permute-done | bytes 114720 | tf_op jit(solution)/shard_map/ppermute | solution.py:20
  23.7 3.0 %collective-permute-start.11 = (bf16[144,256]{1,0:T(8,128)(2,1)S(1)}, bf16[144,256]{1,0:T(8,128)(2,1)S(1)}, u32[]{:S(2)}, u32[]{:S(2)}) collective-permute-start(bf16[144,256]{1,0:T(8,128)(2,1)S(1)} %split.20), channel_id=1, source_target_pairs={{0,16},{4,20},{8,24},{12,28},{16,0},{20,4},{24,8},{28,12},{1,17},{... | collective-permute-start | bytes 221192 | tf_op jit(solution)/shard_map/ppermute | solution.py:20
  27.4 3.7 %attend_local.2.refs_0_ = bf16[16,128,512]{2,1,0:T(8,128)(2,1)} custom-call(s32[2]{0:T(128)S(1)} %pad_add_fusion.ranks_ref, s32[512]{0:T(512)S(1)} %copy-done.1, bf16[16,576,128]{2,1,0:T(8,128)(2,1)} %bitcast.13, bf16[16,576,256]{2,1,0:T(8,128)(2,1)} %bitcast.10), custom_call_target="tpu_custom_call" | custom-call | tf_op jit(solution)/shard_map/attend_local/pallas_call | solution.py:130
  33.1 6.2 %experts.2 = (bf16[512,896]{1,0:T(8,128)(2,1)S(1)}, bf16[512,896]{1,0:T(8,128)(2,1)S(1)}, bf16[3,256,3584]{2,1,0:T(8,128)(2,1)S(1)}) custom-call(s32[2]{0:T(128)S(1)} %pad_add_fusion.ranks_ref, bf16[64,3584]{1,0:T(8,128)(2,1)S(1)} %copy-done, bf16[64,1024]{1,0:T(8,128)(2,1)S(1)} %get-tuple-element.59.refs_1_, ...), custom_call_target="tpu_custom_call" | custom-call | tf_op jit(solution)/shard_map/experts/pallas_call | solution.py:344
  39.7 1.1 %collective-permute-done.15 = bf16[576,256]{1,0:T(8,128)(2,1)S(1)} collective-permute-done((bf16[576,256]{1,0:T(8,128)(2,1)S(1)}, bf16[576,256]{1,0:T(8,128)(2,1)S(1)}, u32[]{:S(2)}, u32[]{:S(2)}) %collective-permute-start.15) | collective-permute-done | bytes 294944 | tf_op jit(solution)/shard_map/ppermute | solution.py:20
  41.5 1.7 %collective-permute-done.17 = bf16[512,896]{1,0:T(8,128)(2,1)S(1)} collective-permute-done((bf16[512,896]{1,0:T(8,128)(2,1)S(1)}, bf16[512,896]{1,0:T(8,128)(2,1)S(1)}, u32[]{:S(2)}, u32[]{:S(2)}) %collective-permute-start.17) | collective-permute-done | bytes 917536 | tf_op jit(solution)/shard_map/ppermute | solution.py:20
  44.2 1.0 %collective-permute-start.18 = (bf16[128,896]{1,0:T(8,128)(2,1)S(1)}, bf16[128,896]{1,0:T(8,128)(2,1)S(1)}, u32[]{:S(2)}, u32[]{:S(2)}) collective-permute-start(bf16[128,896]{1,0:T(8,128)(2,1)S(1)} %slice.114), channel_id=1, source_target_pairs={{0,2},{1,3},{2,0},{3,1},{4,6},{5,7},{6,4},{7,5},{8,10},{9,11},{10,... | collective-permute-start | bytes 688136 | tf_op jit(solution)/shard_map/ppermute | solution.py:20
  45.3 5.6 %experts.3 = (bf16[256,896]{1,0:T(8,128)(2,1)S(1)}, bf16[256,896]{1,0:T(8,128)(2,1)S(1)}, bf16[512,896]{1,0:T(8,128)(2,1)S(1)}) custom-call(s32[2]{0:T(128)S(1)} %pad_add_fusion.ranks_ref, bf16[256,1024]{1,0:T(8,128)(2,1)S(1)} %constant_dynamic-update-slice_fusion.2.refs_0_, bf16[256,1024]{1,0:T(8,128)(2,1)S(1)} %collective-permute-done.14.refs_1_, ...), custom_call_target="tpu_custom_call" | custom-call | tf_op jit(solution)/shard_map/experts/pallas_call | solution.py:344
  51.6 1.6 %collective-permute-start.24 = (bf16[64,896]{1,0:T(8,128)(2,1)S(1)}, bf16[64,896]{1,0:T(8,128)(2,1)S(1)}, u32[]{:S(2)}, u32[]{:S(2)}) collective-permute-start(bf16[64,896]{1,0:T(8,128)(2,1)S(1)} %add_convert_fusion.9), channel_id=1, source_target_pairs={{0,4},{4,0},{8,12},{12,8},{16,20},{20,16},{24,28},{28,24},{1,5},{5... | collective-permute-start | bytes 344072 | tf_op jit(solution)/shard_map/ppermute | solution.py:20
  53.7 1.1 %collective-permute-start.22 = (bf16[64,896]{1,0:T(8,128)(2,1)S(1)}, bf16[64,896]{1,0:T(8,128)(2,1)S(1)}, u32[]{:S(2)}, u32[]{:S(2)}) collective-permute-start(bf16[64,896]{1,0:T(8,128)(2,1)S(1)} %get-tuple-element.121), channel_id=1, source_target_pairs={{0,2},{1,3},{2,0},{3,1},{4,6},{5,7},{6,4},{7,5},{8,10},{9,11},{10,... | collective-permute-start | bytes 344072 | tf_op jit(solution)/shard_map/ppermute | solution.py:20
  54.8 1.0 %collective-permute-start.23 = (bf16[64,896]{1,0:T(8,128)(2,1)S(1)}, bf16[64,896]{1,0:T(8,128)(2,1)S(1)}, u32[]{:S(2)}, u32[]{:S(2)}) collective-permute-start(bf16[64,896]{1,0:T(8,128)(2,1)S(1)} %get-tuple-element.120), channel_id=1, source_target_pairs={{0,4},{4,0},{8,12},{12,8},{16,20},{20,16},{24,28},{28,24},{1,5},{5... | collective-permute-start | bytes 344072 | tf_op jit(solution)/shard_map/ppermute | solution.py:20
  55.9 1.8 %collective-permute-start.28 = (bf16[432,256]{1,0:T(8,128)(2,1)S(1)}, bf16[432,256]{1,0:T(8,128)(2,1)S(1)}, u32[]{:S(2)}, u32[]{:S(2)}) collective-permute-start(bf16[432,256]{1,0:T(8,128)(2,1)S(1)} %split.26), channel_id=1, source_target_pairs={{0,16},{4,20},{8,24},{12,28},{16,0},{20,4},{24,8},{28,12},{1,17},{... | collective-permute-start | bytes 663560 | tf_op jit(solution)/shard_map/ppermute | solution.py:20
  57.7 1.5 %collective-permute-done.22 = bf16[64,896]{1,0:T(8,128)(2,1)S(1)} collective-permute-done((bf16[64,896]{1,0:T(8,128)(2,1)S(1)}, bf16[64,896]{1,0:T(8,128)(2,1)S(1)}, u32[]{:S(2)}, u32[]{:S(2)}) %collective-permute-start.22) | collective-permute-done | bytes 114720 | tf_op jit(solution)/shard_map/ppermute | solution.py:20
  59.2 0.8 collective-permute-done.23
  60.0 1.0 %collective-permute-start.27 = (bf16[128,896]{1,0:T(8,128)(2,1)S(1)}, bf16[128,896]{1,0:T(8,128)(2,1)S(1)}, u32[]{:S(2)}, u32[]{:S(2)}) collective-permute-start(bf16[128,896]{1,0:T(8,128)(2,1)S(1)} %add_convert_fusion.4), channel_id=1, source_target_pairs={{0,2},{1,3},{2,0},{3,1},{4,6},{5,7},{6,4},{7,5},{8,10},{9,11},{10,... | collective-permute-start | bytes 688136 | tf_op jit(solution)/shard_map/ppermute | solution.py:20
  61.2 1.6 %collective-permute-start.26 = (bf16[128,896]{1,0:T(8,128)(2,1)S(1)}, bf16[128,896]{1,0:T(8,128)(2,1)S(1)}, u32[]{:S(2)}, u32[]{:S(2)}) collective-permute-start(bf16[128,896]{1,0:T(8,128)(2,1)S(1)} %add_convert_fusion.5), channel_id=1, source_target_pairs={{0,4},{4,0},{8,12},{12,8},{16,20},{20,16},{24,28},{28,24},{1,5},{5... | collective-permute-start | bytes 688136 | tf_op jit(solution)/shard_map/ppermute | solution.py:20
  63.5 1.3 %collective-permute-start.32 = (bf16[64,896]{1,0:T(8,128)(2,1)S(1)}, bf16[64,896]{1,0:T(8,128)(2,1)S(1)}, u32[]{:S(2)}, u32[]{:S(2)}) collective-permute-start(bf16[64,896]{1,0:T(8,128)(2,1)S(1)} %get-tuple-element.116), channel_id=1, source_target_pairs={{0,2},{1,3},{2,0},{3,1},{4,6},{5,7},{6,4},{7,5},{8,10},{9,11},{10,... | collective-permute-start | bytes 344072 | tf_op jit(solution)/shard_map/ppermute | solution.py:20
  64.8 5.6 %attend_local.3.old_ref = bf16[16,128,512]{2,1,0:T(8,128)(2,1)} custom-call(s32[2]{0:T(128)S(1)} %pad_add_fusion.ranks_ref, s32[512]{0:T(512)S(1)} %copy-done.1, bf16[16,576,128]{2,1,0:T(8,128)(2,1)} %bitcast.14, bf16[16,576,256]{2,1,0:T(8,128)(2,1)} %bitcast.11, bf16[16,128,512]{2,1,0:T(8,128)(2,1)} %attend_local.2.refs_0_), custom_call_target="tpu_custom_call", output_to_operand_aliasing={{}: (4, {})} | custom-call | tf_op jit(solution)/shard_map/attend_local/pallas_call | solution.py:130
  70.6 2.4 %collective-permute-start.29 = (bf16[64,896]{1,0:T(8,128)(2,1)S(1)}, bf16[64,896]{1,0:T(8,128)(2,1)S(1)}, u32[]{:S(2)}, u32[]{:S(2)}) collective-permute-start(bf16[64,896]{1,0:T(8,128)(2,1)S(1)} %get-tuple-element.123), channel_id=1, source_target_pairs={{0,16},{4,20},{8,24},{12,28},{16,0},{20,4},{24,8},{28,12},{1,17},{... | collective-permute-start | bytes 344072 | tf_op jit(solution)/shard_map/ppermute | solution.py:20
  73.0 0.9 %collective-permute-start.30 = (bf16[64,896]{1,0:T(8,128)(2,1)S(1)}, bf16[64,896]{1,0:T(8,128)(2,1)S(1)}, u32[]{:S(2)}, u32[]{:S(2)}) collective-permute-start(bf16[64,896]{1,0:T(8,128)(2,1)S(1)} %get-tuple-element.122), channel_id=1, source_target_pairs={{0,24},{4,28},{8,16},{12,20},{16,8},{20,12},{24,0},{28,4},{1,25},{... | collective-permute-start | bytes 344072 | tf_op jit(solution)/shard_map/ppermute | solution.py:20
  73.9 6.1 %attend_rest.1 = bf16[16,128,512]{2,1,0:T(8,128)(2,1)} custom-call(s32[2]{0:T(128)S(1)} %pad_add_fusion.ranks_ref, s32[512]{0:T(512)S(1)} %copy-done.1, s32[32]{0:T(128)S(1)} %copy-done.2, s32[1]{0:T(128)S(6)} %copy.19.mask_ref, bf16[16,576,128]{2,1,0:T(8,128)(2,1)} %bitcast.15, bf16[16,576,256]{2,1,0:T(8,128)(2,1)} %bitcast.12, ...), custom_call_target="tpu_custom_call", output_to_operand_aliasing={{}: (7, {})} | custom-call | flops 71303168 | bytes 573440 | tf_op jit(solution)/shard_map/attend_rest/pallas_call | solution.py:210
  80.0 0.9 %collective-permute-done.29 = bf16[64,896]{1,0:T(8,128)(2,1)S(1)} collective-permute-done((bf16[64,896]{1,0:T(8,128)(2,1)S(1)}, bf16[64,896]{1,0:T(8,128)(2,1)S(1)}, u32[]{:S(2)}, u32[]{:S(2)}) %collective-permute-start.29) | collective-permute-done | bytes 114720 | tf_op jit(solution)/shard_map/ppermute | solution.py:20
  80.8 0.7 add_convert_fusion.6
  (86 shorter events, 7.9 us)
Async XLA Ops:
  2.6 8.2 %collective-permute-start = (bf16[64,1024]{1,0:T(8,128)(2,1)S(1)}, bf16[64,1024]{1,0:T(8,128)(2,1)S(1)}, u32[]{:S(2)}, u32[]{:S(2)}) collective-permute-start(bf16[64,1024]{1,0:T(8,128)(2,1)S(1)} %get-tuple-element.59.refs_1_), channel_id=1, source_target_pairs={{0,8},{4,12},{8,0},{12,4},{16,24},{20,28},{24,16},{28,20},{1,9},{5... | collective-permute-start | bytes 393224 | tf_op jit(solution)/shard_map/ppermute | solution.py:20
  5.7 13.1 %collective-permute-start.3 = (bf16[64,1024]{1,0:T(8,128)(2,1)S(1)}, bf16[64,1024]{1,0:T(8,128)(2,1)S(1)}, u32[]{:S(2)}, u32[]{:S(2)}) collective-permute-start(bf16[64,1024]{1,0:T(8,128)(2,1)S(1)} %get-tuple-element.59.refs_1_), channel_id=1, source_target_pairs={{0,16},{4,20},{8,24},{12,28},{16,0},{20,4},{24,8},{28,12},{1,17},{... | collective-permute-start | bytes 393224 | tf_op jit(solution)/shard_map/ppermute | solution.py:20
  8.3 10.5 %collective-permute-start.4 = (bf16[64,1024]{1,0:T(8,128)(2,1)S(1)}, bf16[64,1024]{1,0:T(8,128)(2,1)S(1)}, u32[]{:S(2)}, u32[]{:S(2)}) collective-permute-start(bf16[64,1024]{1,0:T(8,128)(2,1)S(1)} %get-tuple-element.59.refs_1_), channel_id=1, source_target_pairs={{0,24},{4,28},{8,16},{12,20},{16,8},{20,12},{24,0},{28,4},{1,25},{... | collective-permute-start | bytes 393224 | tf_op jit(solution)/shard_map/ppermute | solution.py:20
  10.8 8.0 %collective-permute-start.2 = (bf16[64,1024]{1,0:T(8,128)(2,1)S(1)}, bf16[64,1024]{1,0:T(8,128)(2,1)S(1)}, u32[]{:S(2)}, u32[]{:S(2)}) collective-permute-start(bf16[64,1024]{1,0:T(8,128)(2,1)S(1)} %collective-permute-done.refs_4_), channel_id=1, source_target_pairs={{0,4},{4,0},{8,12},{12,8},{16,20},{20,16},{24,28},{28,24},{1,5},{5... | collective-permute-start | bytes 393224 | tf_op jit(solution)/shard_map/ppermute | solution.py:20
  12.5 6.3 %collective-permute-start.1 = (bf16[64,896]{1,0:T(8,128)(2,1)S(1)}, bf16[64,896]{1,0:T(8,128)(2,1)S(1)}, u32[]{:S(2)}, u32[]{:S(2)}) collective-permute-start(bf16[64,896]{1,0:T(8,128)(2,1)S(1)} %slice.85), channel_id=1, source_target_pairs={{0,2},{1,3},{2,0},{3,1},{4,6},{5,7},{6,4},{7,5},{8,10},{9,11},{10,... | collective-permute-start | bytes 344072 | tf_op jit(solution)/shard_map/ppermute | solution.py:20
  14.0 8.0 %collective-permute-start.8 = (bf16[64,1920]{1,0:T(8,128)(2,1)S(1)}, bf16[64,1920]{1,0:T(8,128)(2,1)S(1)}, u32[]{:S(2)}, u32[]{:S(2)}) collective-permute-start(bf16[64,1920]{1,0:T(8,128)(2,1)S(1)} %get-tuple-element.69), channel_id=1, source_target_pairs={{0,4},{4,0},{8,12},{12,8},{16,20},{20,16},{24,28},{28,24},{1,5},{5... | collective-permute-start | bytes 737288 | tf_op jit(solution)/shard_map/ppermute | solution.py:20
  19.0 12.1 %collective-permute-start.5 = (bf16[192,896]{1,0:T(8,128)(2,1)S(1)}, bf16[192,896]{1,0:T(8,128)(2,1)S(1)}, u32[]{:S(2)}, u32[]{:S(2)}) collective-permute-start(bf16[192,896]{1,0:T(8,128)(2,1)S(1)} %pad_maximum_fusion), channel_id=1, source_target_pairs={{0,2},{1,3},{2,0},{3,1},{4,6},{5,7},{6,4},{7,5},{8,10},{9,11},{10,... | collective-permute-start | bytes 1032200 | tf_op jit(solution)/shard_map/ppermute | solution.py:20
  20.4 7.0 %collective-permute-start.7 = (bf16[128,1024]{1,0:T(8,128)(2,1)S(1)}, bf16[128,1024]{1,0:T(8,128)(2,1)S(1)}, u32[]{:S(2)}, u32[]{:S(2)}) collective-permute-start(bf16[128,1024]{1,0:T(8,128)(2,1)S(1)} %pad_maximum_fusion.3), channel_id=1, source_target_pairs={{0,1},{1,0},{2,3},{3,2},{4,5},{5,4},{6,7},{7,6},{8,9},{9,8},{10,11... | collective-permute-start | bytes 786440 | tf_op jit(solution)/shard_map/ppermute | solution.py:20
  20.4 10.6 %collective-permute-start.6 = (bf16[128,1024]{1,0:T(8,128)(2,1)S(1)}, bf16[128,1024]{1,0:T(8,128)(2,1)S(1)}, u32[]{:S(2)}, u32[]{:S(2)}) collective-permute-start(bf16[128,1024]{1,0:T(8,128)(2,1)S(1)} %constant_dynamic-update-slice_fusion), channel_id=1, source_target_pairs={{0,4},{4,0},{8,12},{12,8},{16,20},{20,16},{24,28},{28,24},{1,5},{5... | collective-permute-start | bytes 786440 | tf_op jit(solution)/shard_map/ppermute | solution.py:20
  22.0 5.3 %collective-permute-start.9 = (bf16[64,1920]{1,0:T(8,128)(2,1)S(1)}, bf16[64,1920]{1,0:T(8,128)(2,1)S(1)}, u32[]{:S(2)}, u32[]{:S(2)}) collective-permute-start(bf16[64,1920]{1,0:T(8,128)(2,1)S(1)} %collective-permute-done.8.refs_2_), channel_id=1, source_target_pairs={{0,1},{1,0},{2,3},{3,2},{4,5},{5,4},{6,7},{7,6},{8,9},{9,8},{10,11... | collective-permute-start | bytes 737288 | tf_op jit(solution)/shard_map/ppermute | solution.py:20
  23.7 7.3 %collective-permute-start.11 = (bf16[144,256]{1,0:T(8,128)(2,1)S(1)}, bf16[144,256]{1,0:T(8,128)(2,1)S(1)}, u32[]{:S(2)}, u32[]{:S(2)}) collective-permute-start(bf16[144,256]{1,0:T(8,128)(2,1)S(1)} %split.20), channel_id=1, source_target_pairs={{0,16},{4,20},{8,24},{12,28},{16,0},{20,4},{24,8},{28,12},{1,17},{... | collective-permute-start | bytes 221192 | tf_op jit(solution)/shard_map/ppermute | solution.py:20
  31.0 2.0 %collective-permute-start.12 = (bf16[192,896]{1,0:T(8,128)(2,1)S(1)}, bf16[192,896]{1,0:T(8,128)(2,1)S(1)}, u32[]{:S(2)}, u32[]{:S(2)}) collective-permute-start(bf16[192,896]{1,0:T(8,128)(2,1)S(1)} %collective-permute-done.5), channel_id=1, source_target_pairs={{0,1},{1,0},{2,3},{3,2},{4,5},{5,4},{6,7},{7,6},{8,9},{9,8},{10,11... | collective-permute-start | bytes 1032200 | tf_op jit(solution)/shard_map/ppermute | solution.py:20
  31.2 9.6 %collective-permute-start.14 = (bf16[256,1024]{1,0:T(8,128)(2,1)S(1)}, bf16[256,1024]{1,0:T(8,128)(2,1)S(1)}, u32[]{:S(2)}, u32[]{:S(2)}) collective-permute-start(bf16[256,1024]{1,0:T(8,128)(2,1)S(1)} %constant_dynamic-update-slice_fusion.2.refs_0_), channel_id=1, source_target_pairs={{0,1},{1,0},{2,3},{3,2},{4,5},{5,4},{6,7},{7,6},{8,9},{9,8},{10,11... | collective-permute-start | bytes 1572872 | tf_op jit(solution)/shard_map/ppermute | solution.py:20
  31.8 9.0 %collective-permute-start.15 = (bf16[576,256]{1,0:T(8,128)(2,1)S(1)}, bf16[576,256]{1,0:T(8,128)(2,1)S(1)}, u32[]{:S(2)}, u32[]{:S(2)}) collective-permute-start(bf16[576,256]{1,0:T(8,128)(2,1)S(1)} %pad_maximum_fusion.1), channel_id=1, source_target_pairs={{0,4},{4,0},{8,12},{12,8},{16,20},{20,16},{24,28},{28,24},{1,5},{5... | collective-permute-start | bytes 884744 | tf_op jit(solution)/shard_map/ppermute | solution.py:20
  32.4 7.3 %collective-permute-start.13 = (bf16[128,896]{1,0:T(8,128)(2,1)S(1)}, bf16[128,896]{1,0:T(8,128)(2,1)S(1)}, u32[]{:S(2)}, u32[]{:S(2)}) collective-permute-start(bf16[128,896]{1,0:T(8,128)(2,1)S(1)} %slice.90), channel_id=1, source_target_pairs={{0,2},{1,3},{2,0},{3,1},{4,6},{5,7},{6,4},{7,5},{8,10},{9,11},{10,... | collective-permute-start | bytes 688136 | tf_op jit(solution)/shard_map/ppermute | solution.py:20
  40.8 2.5 %collective-permute-start.17 = (bf16[512,896]{1,0:T(8,128)(2,1)S(1)}, bf16[512,896]{1,0:T(8,128)(2,1)S(1)}, u32[]{:S(2)}, u32[]{:S(2)}) collective-permute-start(bf16[512,896]{1,0:T(8,128)(2,1)S(1)} %get-tuple-element.91), channel_id=1, source_target_pairs={{0,1},{1,0},{2,3},{3,2},{4,5},{5,4},{6,7},{7,6},{8,9},{9,8},{10,11... | collective-permute-start | bytes 2752520 | tf_op jit(solution)/shard_map/ppermute | solution.py:20
  40.9 10.0 %collective-permute-start.20 = (bf16[576,256]{1,0:T(8,128)(2,1)S(1)}, bf16[576,256]{1,0:T(8,128)(2,1)S(1)}, u32[]{:S(2)}, u32[]{:S(2)}) collective-permute-start(bf16[576,256]{1,0:T(8,128)(2,1)S(1)} %broadcast_select_fusion.1), channel_id=1, source_target_pairs={{0,8},{4,12},{8,0},{12,4},{16,24},{20,28},{24,16},{28,20},{1,9},{5... | collective-permute-start | bytes 884744 | tf_op jit(solution)/shard_map/ppermute | solution.py:20
  41.3 3.9 %collective-permute-start.16 = (bf16[128,896]{1,0:T(8,128)(2,1)S(1)}, bf16[128,896]{1,0:T(8,128)(2,1)S(1)}, u32[]{:S(2)}, u32[]{:S(2)}) collective-permute-start(bf16[128,896]{1,0:T(8,128)(2,1)S(1)} %collective-permute-done.13.refs_4_), channel_id=1, source_target_pairs={{0,1},{1,0},{2,3},{3,2},{4,5},{5,4},{6,7},{7,6},{8,9},{9,8},{10,11... | collective-permute-start | bytes 688136 | tf_op jit(solution)/shard_map/ppermute | solution.py:20
  43.6 7.7 %collective-permute-start.19 = (bf16[64,1792]{1,0:T(8,128)(2,1)S(1)}, bf16[64,1792]{1,0:T(8,128)(2,1)S(1)}, u32[]{:S(2)}, u32[]{:S(2)}) collective-permute-start(bf16[64,1792]{1,0:T(8,128)(2,1)S(1)} %pad_maximum_fusion.4), channel_id=1, source_target_pairs={{0,4},{4,0},{8,12},{12,8},{16,20},{20,16},{24,28},{28,24},{1,5},{5... | collective-permute-start | bytes 688136 | tf_op jit(solution)/shard_map/ppermute | solution.py:20
  44.2 7.4 %collective-permute-start.18 = (bf16[128,896]{1,0:T(8,128)(2,1)S(1)}, bf16[128,896]{1,0:T(8,128)(2,1)S(1)}, u32[]{:S(2)}, u32[]{:S(2)}) collective-permute-start(bf16[128,896]{1,0:T(8,128)(2,1)S(1)} %slice.114), channel_id=1, source_target_pairs={{0,2},{1,3},{2,0},{3,1},{4,6},{5,7},{6,4},{7,5},{8,10},{9,11},{10,... | collective-permute-start | bytes 688136 | tf_op jit(solution)/shard_map/ppermute | solution.py:20
  51.5 1.8 %collective-permute-start.21 = (bf16[256,896]{1,0:T(8,128)(2,1)S(1)}, bf16[256,896]{1,0:T(8,128)(2,1)S(1)}, u32[]{:S(2)}, u32[]{:S(2)}) collective-permute-start(bf16[256,896]{1,0:T(8,128)(2,1)S(1)} %get-tuple-element.94), channel_id=1, source_target_pairs={{0,1},{1,0},{2,3},{3,2},{4,5},{5,4},{6,7},{7,6},{8,9},{9,8},{10,11... | collective-permute-start | bytes 1376264 | tf_op jit(solution)/shard_map/ppermute | solution.py:20
  51.6 6.1 %collective-permute-start.24 = (bf16[64,896]{1,0:T(8,128)(2,1)S(1)}, bf16[64,896]{1,0:T(8,128)(2,1)S(1)}, u32[]{:S(2)}, u32[]{:S(2)}) collective-permute-start(bf16[64,896]{1,0:T(8,128)(2,1)S(1)} %add_convert_fusion.9), channel_id=1, source_target_pairs={{0,4},{4,0},{8,12},{12,8},{16,20},{20,16},{24,28},{28,24},{1,5},{5... | collective-permute-start | bytes 344072 | tf_op jit(solution)/shard_map/ppermute | solution.py:20
  53.5 6.5 %collective-permute-start.25 = (bf16[256,896]{1,0:T(8,128)(2,1)S(1)}, bf16[256,896]{1,0:T(8,128)(2,1)S(1)}, u32[]{:S(2)}, u32[]{:S(2)}) collective-permute-start(bf16[256,896]{1,0:T(8,128)(2,1)S(1)} %get-tuple-element.98), channel_id=1, source_target_pairs={{0,1},{1,0},{2,3},{3,2},{4,5},{5,4},{6,7},{7,6},{8,9},{9,8},{10,11... | collective-permute-start | bytes 1376264 | tf_op jit(solution)/shard_map/ppermute | solution.py:20
  53.7 5.5 %collective-permute-start.22 = (bf16[64,896]{1,0:T(8,128)(2,1)S(1)}, bf16[64,896]{1,0:T(8,128)(2,1)S(1)}, u32[]{:S(2)}, u32[]{:S(2)}) collective-permute-start(bf16[64,896]{1,0:T(8,128)(2,1)S(1)} %get-tuple-element.121), channel_id=1, source_target_pairs={{0,2},{1,3},{2,0},{3,1},{4,6},{5,7},{6,4},{7,5},{8,10},{9,11},{10,... | collective-permute-start | bytes 344072 | tf_op jit(solution)/shard_map/ppermute | solution.py:20
  54.8 5.1 %collective-permute-start.23 = (bf16[64,896]{1,0:T(8,128)(2,1)S(1)}, bf16[64,896]{1,0:T(8,128)(2,1)S(1)}, u32[]{:S(2)}, u32[]{:S(2)}) collective-permute-start(bf16[64,896]{1,0:T(8,128)(2,1)S(1)} %get-tuple-element.120), channel_id=1, source_target_pairs={{0,4},{4,0},{8,12},{12,8},{16,20},{20,16},{24,28},{28,24},{1,5},{5... | collective-permute-start | bytes 344072 | tf_op jit(solution)/shard_map/ppermute | solution.py:20
  55.9 14.5 %collective-permute-start.28 = (bf16[432,256]{1,0:T(8,128)(2,1)S(1)}, bf16[432,256]{1,0:T(8,128)(2,1)S(1)}, u32[]{:S(2)}, u32[]{:S(2)}) collective-permute-start(bf16[432,256]{1,0:T(8,128)(2,1)S(1)} %split.26), channel_id=1, source_target_pairs={{0,16},{4,20},{8,24},{12,28},{16,0},{20,4},{24,8},{28,12},{1,17},{... | collective-permute-start | bytes 663560 | tf_op jit(solution)/shard_map/ppermute | solution.py:20
  60.0 10.4 %collective-permute-start.27 = (bf16[128,896]{1,0:T(8,128)(2,1)S(1)}, bf16[128,896]{1,0:T(8,128)(2,1)S(1)}, u32[]{:S(2)}, u32[]{:S(2)}) collective-permute-start(bf16[128,896]{1,0:T(8,128)(2,1)S(1)} %add_convert_fusion.4), channel_id=1, source_target_pairs={{0,2},{1,3},{2,0},{3,1},{4,6},{5,7},{6,4},{7,5},{8,10},{9,11},{10,... | collective-permute-start | bytes 688136 | tf_op jit(solution)/shard_map/ppermute | solution.py:20
  61.2 9.2 %collective-permute-start.26 = (bf16[128,896]{1,0:T(8,128)(2,1)S(1)}, bf16[128,896]{1,0:T(8,128)(2,1)S(1)}, u32[]{:S(2)}, u32[]{:S(2)}) collective-permute-start(bf16[128,896]{1,0:T(8,128)(2,1)S(1)} %add_convert_fusion.5), channel_id=1, source_target_pairs={{0,4},{4,0},{8,12},{12,8},{16,20},{20,16},{24,28},{28,24},{1,5},{5... | collective-permute-start | bytes 688136 | tf_op jit(solution)/shard_map/ppermute | solution.py:20
  62.9 17.1 %collective-permute-start.31 = (bf16[64,896]{1,0:T(8,128)(2,1)S(1)}, bf16[64,896]{1,0:T(8,128)(2,1)S(1)}, u32[]{:S(2)}, u32[]{:S(2)}) collective-permute-start(bf16[64,896]{1,0:T(8,128)(2,1)S(1)} %get-tuple-element.117), channel_id=1, source_target_pairs={{0,8},{4,12},{8,0},{12,4},{16,24},{20,28},{24,16},{28,20},{1,9},{5... | collective-permute-start | bytes 344072 | tf_op jit(solution)/shard_map/ppermute | solution.py:20
  63.5 17.3 %collective-permute-start.32 = (bf16[64,896]{1,0:T(8,128)(2,1)S(1)}, bf16[64,896]{1,0:T(8,128)(2,1)S(1)}, u32[]{:S(2)}, u32[]{:S(2)}) collective-permute-start(bf16[64,896]{1,0:T(8,128)(2,1)S(1)} %get-tuple-element.116), channel_id=1, source_target_pairs={{0,2},{1,3},{2,0},{3,1},{4,6},{5,7},{6,4},{7,5},{8,10},{9,11},{10,... | collective-permute-start | bytes 344072 | tf_op jit(solution)/shard_map/ppermute | solution.py:20
  70.6 10.3 %collective-permute-start.29 = (bf16[64,896]{1,0:T(8,128)(2,1)S(1)}, bf16[64,896]{1,0:T(8,128)(2,1)S(1)}, u32[]{:S(2)}, u32[]{:S(2)}) collective-permute-start(bf16[64,896]{1,0:T(8,128)(2,1)S(1)} %get-tuple-element.123), channel_id=1, source_target_pairs={{0,16},{4,20},{8,24},{12,28},{16,0},{20,4},{24,8},{28,12},{1,17},{... | collective-permute-start | bytes 344072 | tf_op jit(solution)/shard_map/ppermute | solution.py:20
  73.0 7.8 %collective-permute-start.30 = (bf16[64,896]{1,0:T(8,128)(2,1)S(1)}, bf16[64,896]{1,0:T(8,128)(2,1)S(1)}, u32[]{:S(2)}, u32[]{:S(2)}) collective-permute-start(bf16[64,896]{1,0:T(8,128)(2,1)S(1)} %get-tuple-element.122), channel_id=1, source_target_pairs={{0,24},{4,28},{8,16},{12,20},{16,8},{20,12},{24,0},{28,4},{1,25},{... | collective-permute-start | bytes 344072 | tf_op jit(solution)/shard_map/ppermute | solution.py:20
  (4 other events, 30.9 us)

commit v14 on v13

--- a/solution.py
+++ b/solution.py
@@ -178,7 +178,9 @@
 ):
     count, width, heads = queries.shape
     slots = pages.shape[2]
-    some = count - first
+    each = 2
+    steps = (count - first) // each
+    skip = first // each
 
     def kernel(
         ranks_ref,
@@ -192,39 +194,45 @@
         out_ref,
     ):
         step = pl.program_id(0)
-
-        @pl.when(step < some)
-        def _():
-            at = device_of(ranks_ref, groups) * count + first + step
-            out_ref[0] = attend_body(query_ref[0], pages_ref[0], lengths_ref[at])
-
-        @pl.when(step == some)
-        def _():
-            partner = device_of(ranks_ref, groups, mask_ref[0])
-            length = lengths_ref[partner * count + slots_ref[partner]]
-            out_ref[0] = attend_body(query_ref[0], page_ref[...], length)
+        device = device_of(ranks_ref, groups)
+        partner = device_of(ranks_ref, groups, mask_ref[0])
+        mine = slots_ref[device]
+        far_length = lengths_ref[partner * count + slots_ref[partner]]
+        block = jnp.where(step < steps, skip + step, mine // each)
+        for i in range(each):
+            at = block * each + i
+            traded = (step == steps) & (at == mine)
+
+            @pl.when(jnp.logical_not(traded))
+            def _():
+                out_ref[i] = attend_body(
+                    query_ref[i], pages_ref[i], lengths_ref[device * count + at]
+                )
+
+            @pl.when(traded)
+            def _():
+                out_ref[i] = attend_body(query_ref[i], page_ref[...], far_length)
 
     def request(i, ranks_ref, lengths_ref, slots_ref, mask_ref):
-        return jnp.where(i < some, first + i, slots_ref[device_of(ranks_ref, groups)]), 0, 0
+        mine = slots_ref[device_of(ranks_ref, groups)]
+        return jnp.where(i < steps, skip + i, mine // each), 0, 0
 
     return pl.pallas_call(
         kernel,
         out_shape=jax.ShapeDtypeStruct(attended.shape, attended.dtype),
         grid_spec=pltpu.PrefetchScalarGridSpec(
             num_scalar_prefetch=4,
-            grid=(some + 1,),
+            grid=(steps + 1,),
             in_specs=[
-                pl.BlockSpec((1, width, heads), request),
-                pl.BlockSpec(
-                    (1, width, slots), lambda i, *_: (jnp.minimum(first + i, count - 1), 0, 0)
-                ),
+                pl.BlockSpec((each, width, heads), request),
+                pl.BlockSpec((each, width, slots), request),
                 pl.BlockSpec((width, slots), lambda i, *_: (0, 0)),
                 ANYWHERE,
             ],
-            out_specs=pl.BlockSpec((1, heads, LAT), request),
+            out_specs=pl.BlockSpec((each, heads, LAT), request),
         ),
         input_output_aliases={7: 0},
-        compiler_params=pltpu.CompilerParams(vmem_limit_bytes=6 * MIB),
+        compiler_params=pltpu.CompilerParams(vmem_limit_bytes=8 * MIB),
         cost_estimate=pl.CostEstimate(
             flops=2 * heads * slots * (width + LAT),
             bytes_accessed=2 * (heads * (width + LAT) + slots * width),
@@ -452,11 +460,12 @@
     near_late = jnp.concatenate(late_pieces, axis=0)
     far_3 = flip(jnp.concatenate([bare(near_3), bare(near_late)], axis=0), "tp", 2)
     near_odds = flip(near_late, "ep", 1)
-    near_23 = flip(jnp.concatenate([near_2, near_3], axis=0), "tp", 1)
-    early = [flip(array, "tp", 1) for array in (both_1, far_2)]
-    queries, near_23, early = tie((queries, near_23, early))
+    wide = jnp.pad(far_2, ((0, 0), (0, near_2.shape[1] - columns)))
+    core_23 = flip(jnp.concatenate([near_2, near_3, wide], axis=0), "tp", 1)
+    core_1 = flip(both_1, "tp", 1)
+    queries, core_1, core_23 = tie((queries, core_1, core_23))
     count = queries.shape[0]
-    some = count // 4
+    some, middle = count // 4, count * 5 // 8
     attended = attend_part(ranks, lengths, queries, cache_pages, groups, 0, some)
     least = page.shape[0] // 4
     upper, lower = jnp.split(page, [least], axis=0)
@@ -475,9 +484,9 @@
         return start * rows, (part,), part == 0, array
 
     pieces = [(0, None, False, hidden), (0, (), True, own)]
-    pieces += [(rows, (0, 2), True, both_1), (rows, (1, 3), False, early[0])]
-    pieces += [piece(2, 0, near_2), piece(3, 0, near_3), (2 * rows, (1,), False, near_23)]
-    pieces += [piece(2, 2, far_2), piece(2, 3, early[1])]
+    pieces += [(rows, (0, 2), True, both_1), (rows, (1, 3), False, core_1)]
+    pieces += [piece(2, 0, near_2), piece(3, 0, near_3), piece(2, 1, cut(core_23, 0, 2))]
+    pieces += [piece(2, 2, far_2), piece(2, 3, bare(cut(core_23, 2, 1)))]
     pieces += [piece(3, 2, far_3), piece(3, 3, core_3)]
     *first, w_down = run_experts(
         ranks, pieces, w_gate, w_up, w_down, 4 * rows, columns, top, True, 1
@@ -526,7 +535,7 @@
     even = total_of(cut(late_sent, 0, len(late)), jnp.pad(over_x, ((half * rows, 0), (0, 0))))
     even = flip(even, "tp", 2)
     attended = attend_part(
-        ranks, lengths, queries, cache_pages, groups, some, 2 * some, attended
+        ranks, lengths, queries, cache_pages, groups, some, middle - some, attended
     )
     odd, even, attended, swapped = tie((odd, even, attended, swapped))
     lower = page_take(lower, swapped, 2) if levels > 2 else lower
@@ -544,7 +553,7 @@
         page,
         attended,
         groups,
-        3 * some,
+        middle,
     )
     *back, attended = tie((*back, attended))
     moe_out = total_of(cut(kept, 0, 1), over_1[:, :columns], zero, *back)

time: 82 us -> 81.1 us (0.989)
  waiting for transfers between devices: 10.9 us -> 5.91 us
  starting transfers between devices: 33.6 us -> 37.3 us
    ppermute x33 -> x32, waiting for transfers between devices: 10.9 us -> 5.91 us  [flip(): return lax.ppermute(block, axis, [(i, i ^ apart) for i in range(count)])]
    ppermute x33 -> x32, starting transfers between devices: 33.6 us -> 37.3 us  [flip(): return lax.ppermute(block, axis, [(i, i ^ apart) for i in range(count)])]
    pallas_call x1, Pallas kernels: 6.05 us -> 7.24 us  [attend_rest(): pl.pallas_call(kernel, out_shape=jax.ShapeDtypeStruct(attended.shape, att...]
  transfers between devices with their start and end apart: 33 -> 32, of which waited for: 11 -> 9; matrix products, arithmetic and copies ran while one was open for 2% -> 2% of each run, Pallas kernels for 38% -> 39%
where the time goes in v14:
time: 81.1 us; the launch traced here: 80.8 us
  starting transfers between devices  37.3 us (46%)
  Pallas kernels  33.7 us (42%)
  waiting for transfers between devices  5.91 us (7%)
  other arithmetic  1.82 us (2%)
  between operations  1.73 us (2%)
    ppermute x32, starting transfers between devices, flip(): return lax.ppermute(block, axis, [(i, i ^ apart) for i in range(count)])  37.3 us
    pallas_call x2, Pallas kernels, run_experts(): pl.pallas_call(kernel, out_shape=[[pltpu.VMEM((2 * rows // given, columns...  11.8 us
    pallas_call x2, Pallas kernels, attend_part(): pl.pallas_call(kernel, out_shape=jax.ShapeDtypeStruct((count, heads, LAT)...  8.53 us
    pallas_call x1, Pallas kernels, attend_rest(): pl.pallas_call(kernel, out_shape=jax.ShapeDtypeStruct(attended.shape, att...  7.24 us
    ppermute x32, waiting for transfers between devices, flip(): return lax.ppermute(block, axis, [(i, i ^ apart) for i in range(count)])  5.91 us
    pallas_call x1, Pallas kernels, load(): pl.pallas_call(load_kernel, out_shape=[pltpu.VMEM(w.shape, w.dtype) for w...  4.21 us
    pallas_call x1, Pallas kernels, pick(): pl.pallas_call(functools.partial(pick_kernel, groups), out_shape=(pltpu.V...  1.89 us
  transfers between devices with their start and end apart: 32, of which 9 were waited for; matrix products, arithmetic and copies ran while one was open for 2% of the time, Pallas kernels for 39%

profile of v14, /device:TPU:0, one launch (start us, length us, event | category | flops | bytes accessed | tf_op | source)
XLA Modules:
  0.0 80.8 jit_solution(1498989156826427425)
XLA Ops:
  0.7 1.9 %pick.1 = (bf16[64,1024]{1,0:T(8,128)(2,1)S(1)}, bf16[64,1920]{1,0:T(8,128)(2,1)S(1)}, bf16[576,256]{1,0:T(8,128)(2,1)S(1)}) custom-call(s32[2]{0:T(128)S(1)} %pad_add_fusion.ranks_ref, s32[32]{0:T(128)} %slots_ref.3, s32[8,64]{1,0:T(8,128)} %bitcast.16, f32[8,64]{1,0:T(8,128)} %bitcast.17, bf16[64,3584]{1,0:T(8,128)(2,1)} %refs_0_.2, ...), custom_call_target="tpu_custom_call" | custom-call | tf_op jit(solution)/shard_map/pick/pallas_call | solution.py:96
  2.6 3.1 %collective-permute-start = (bf16[64,1024]{1,0:T(8,128)(2,1)S(1)}, bf16[64,1024]{1,0:T(8,128)(2,1)S(1)}, u32[]{:S(2)}, u32[]{:S(2)}) collective-permute-start(bf16[64,1024]{1,0:T(8,128)(2,1)S(1)} %get-tuple-element.58.refs_1_), channel_id=1, source_target_pairs={{0,8},{4,12},{8,0},{12,4},{16,24},{20,28},{24,16},{28,20},{1,9},{5... | collective-permute-start | bytes 393224 | tf_op jit(solution)/shard_map/ppermute | solution.py:20
  5.7 2.6 %collective-permute-start.3 = (bf16[64,1024]{1,0:T(8,128)(2,1)S(1)}, bf16[64,1024]{1,0:T(8,128)(2,1)S(1)}, u32[]{:S(2)}, u32[]{:S(2)}) collective-permute-start(bf16[64,1024]{1,0:T(8,128)(2,1)S(1)} %get-tuple-element.58.refs_1_), channel_id=1, source_target_pairs={{0,16},{4,20},{8,24},{12,28},{16,0},{20,4},{24,8},{28,12},{1,17},{... | collective-permute-start | bytes 393224 | tf_op jit(solution)/shard_map/ppermute | solution.py:20
  8.3 2.5 %collective-permute-done.refs_4_ = bf16[64,1024]{1,0:T(8,128)(2,1)S(1)} collective-permute-done((bf16[64,1024]{1,0:T(8,128)(2,1)S(1)}, bf16[64,1024]{1,0:T(8,128)(2,1)S(1)}, u32[]{:S(2)}, u32[]{:S(2)}) %collective-permute-start) | collective-permute-done | bytes 131104 | tf_op jit(solution)/shard_map/ppermute | solution.py:20
  10.8 1.7 %collective-permute-start.2 = (bf16[64,1024]{1,0:T(8,128)(2,1)S(1)}, bf16[64,1024]{1,0:T(8,128)(2,1)S(1)}, u32[]{:S(2)}, u32[]{:S(2)}) collective-permute-start(bf16[64,1024]{1,0:T(8,128)(2,1)S(1)} %collective-permute-done.refs_4_), channel_id=1, source_target_pairs={{0,4},{4,0},{8,12},{12,8},{16,20},{20,16},{24,28},{28,24},{1,5},{5... | collective-permute-start | bytes 393224 | tf_op jit(solution)/shard_map/ppermute | solution.py:20
  12.5 1.5 %collective-permute-start.1 = (bf16[64,896]{1,0:T(8,128)(2,1)S(1)}, bf16[64,896]{1,0:T(8,128)(2,1)S(1)}, u32[]{:S(2)}, u32[]{:S(2)}) collective-permute-start(bf16[64,896]{1,0:T(8,128)(2,1)S(1)} %slice.93), channel_id=1, source_target_pairs={{0,2},{1,3},{2,0},{3,1},{4,6},{5,7},{6,4},{7,5},{8,10},{9,11},{10,... | collective-permute-start | bytes 344072 | tf_op jit(solution)/shard_map/ppermute | solution.py:20
  14.6 4.2 %load.1 = (bf16[3,3584,256]{2,1,0:T(8,128)(2,1)S(1)}, bf16[3,3584,256]{2,1,0:T(8,128)(2,1)S(1)}) custom-call(bf16[3,3584,256]{2,1,0:T(8,128)(2,1)} %refs_0_.1, bf16[3,3584,256]{2,1,0:T(8,128)(2,1)} %refs_1_), custom_call_target="tpu_custom_call" | custom-call | bytes 11010048 | tf_op jit(solution)/shard_map/load/pallas_call | solution.py:162
  19.1 1.4 %collective-permute-start.5 = (bf16[192,896]{1,0:T(8,128)(2,1)S(1)}, bf16[192,896]{1,0:T(8,128)(2,1)S(1)}, u32[]{:S(2)}, u32[]{:S(2)}) collective-permute-start(bf16[192,896]{1,0:T(8,128)(2,1)S(1)} %pad_maximum_fusion), channel_id=1, source_target_pairs={{0,2},{1,3},{2,0},{3,1},{4,6},{5,7},{6,4},{7,5},{8,10},{9,11},{10,... | collective-permute-start | bytes 1032200 | tf_op jit(solution)/shard_map/ppermute | solution.py:20
  20.5 1.5 %collective-permute-start.6 = (bf16[128,1024]{1,0:T(8,128)(2,1)S(1)}, bf16[128,1024]{1,0:T(8,128)(2,1)S(1)}, u32[]{:S(2)}, u32[]{:S(2)}) collective-permute-start(bf16[128,1024]{1,0:T(8,128)(2,1)S(1)} %constant_dynamic-update-slice_fusion), channel_id=1, source_target_pairs={{0,4},{4,0},{8,12},{12,8},{16,20},{20,16},{24,28},{28,24},{1,5},{5... | collective-permute-start | bytes 786440 | tf_op jit(solution)/shard_map/ppermute | solution.py:20
  22.0 3.0 %collective-permute-start.10 = (bf16[144,256]{1,0:T(8,128)(2,1)S(1)}, bf16[144,256]{1,0:T(8,128)(2,1)S(1)}, u32[]{:S(2)}, u32[]{:S(2)}) collective-permute-start(bf16[144,256]{1,0:T(8,128)(2,1)S(1)} %split.20), channel_id=1, source_target_pairs={{0,16},{4,20},{8,24},{12,28},{16,0},{20,4},{24,8},{28,12},{1,17},{... | collective-permute-start | bytes 221192 | tf_op jit(solution)/shard_map/ppermute | solution.py:20
  25.7 3.6 %attend_local.2.refs_0_ = bf16[16,128,512]{2,1,0:T(8,128)(2,1)} custom-call(s32[2]{0:T(128)S(1)} %pad_add_fusion.ranks_ref, s32[512]{0:T(512)S(1)} %copy-done.1, bf16[16,576,128]{2,1,0:T(8,128)(2,1)} %bitcast.13, bf16[16,576,256]{2,1,0:T(8,128)(2,1)} %bitcast.10), custom_call_target="tpu_custom_call" | custom-call | tf_op jit(solution)/shard_map/attend_local/pallas_call | solution.py:130
  30.2 1.6 %collective-permute-start.14 = (bf16[576,256]{1,0:T(8,128)(2,1)S(1)}, bf16[576,256]{1,0:T(8,128)(2,1)S(1)}, u32[]{:S(2)}, u32[]{:S(2)}) collective-permute-start(bf16[576,256]{1,0:T(8,128)(2,1)S(1)} %pad_maximum_fusion.1), channel_id=1, source_target_pairs={{0,4},{4,0},{8,12},{12,8},{16,20},{20,16},{24,28},{28,24},{1,5},{5... | collective-permute-start | bytes 884744 | tf_op jit(solution)/shard_map/ppermute | solution.py:20
  31.8 1.4 %collective-permute-start.12 = (bf16[128,896]{1,0:T(8,128)(2,1)S(1)}, bf16[128,896]{1,0:T(8,128)(2,1)S(1)}, u32[]{:S(2)}, u32[]{:S(2)}) collective-permute-start(bf16[128,896]{1,0:T(8,128)(2,1)S(1)} %slice.100), channel_id=1, source_target_pairs={{0,2},{1,3},{2,0},{3,1},{4,6},{5,7},{6,4},{7,5},{8,10},{9,11},{10,... | collective-permute-start | bytes 688136 | tf_op jit(solution)/shard_map/ppermute | solution.py:20
  33.3 6.2 %experts.2 = (bf16[512,896]{1,0:T(8,128)(2,1)S(1)}, bf16[512,896]{1,0:T(8,128)(2,1)S(1)}, bf16[3,256,3584]{2,1,0:T(8,128)(2,1)S(1)}) custom-call(s32[2]{0:T(128)S(1)} %pad_add_fusion.ranks_ref, bf16[64,3584]{1,0:T(8,128)(2,1)S(1)} %copy-done, bf16[64,1024]{1,0:T(8,128)(2,1)S(1)} %get-tuple-element.58.refs_1_, ...), custom_call_target="tpu_custom_call" | custom-call | tf_op jit(solution)/shard_map/experts/pallas_call | solution.py:352
  39.7 2.0 %collective-permute-start.19 = (bf16[576,256]{1,0:T(8,128)(2,1)S(1)}, bf16[576,256]{1,0:T(8,128)(2,1)S(1)}, u32[]{:S(2)}, u32[]{:S(2)}) collective-permute-start(bf16[576,256]{1,0:T(8,128)(2,1)S(1)} %broadcast_select_fusion.1), channel_id=1, source_target_pairs={{0,8},{4,12},{8,0},{12,4},{16,24},{20,28},{24,16},{28,20},{1,9},{5... | collective-permute-start | bytes 884744 | tf_op jit(solution)/shard_map/ppermute | solution.py:20
  42.4 1.2 %collective-permute-start.18 = (bf16[64,1792]{1,0:T(8,128)(2,1)S(1)}, bf16[64,1792]{1,0:T(8,128)(2,1)S(1)}, u32[]{:S(2)}, u32[]{:S(2)}) collective-permute-start(bf16[64,1792]{1,0:T(8,128)(2,1)S(1)} %pad_maximum_fusion.3), channel_id=1, source_target_pairs={{0,4},{4,0},{8,12},{12,8},{16,20},{20,16},{24,28},{28,24},{1,5},{5... | collective-permute-start | bytes 688136 | tf_op jit(solution)/shard_map/ppermute | solution.py:20
  43.6 1.3 %collective-permute-start.17 = (bf16[128,896]{1,0:T(8,128)(2,1)S(1)}, bf16[128,896]{1,0:T(8,128)(2,1)S(1)}, u32[]{:S(2)}, u32[]{:S(2)}) collective-permute-start(bf16[128,896]{1,0:T(8,128)(2,1)S(1)} %slice.124), channel_id=1, source_target_pairs={{0,2},{1,3},{2,0},{3,1},{4,6},{5,7},{6,4},{7,5},{8,10},{9,11},{10,... | collective-permute-start | bytes 688136 | tf_op jit(solution)/shard_map/ppermute | solution.py:20
  45.0 5.6 %experts.3 = (bf16[256,896]{1,0:T(8,128)(2,1)S(1)}, bf16[256,896]{1,0:T(8,128)(2,1)S(1)}, bf16[512,896]{1,0:T(8,128)(2,1)S(1)}) custom-call(s32[2]{0:T(128)S(1)} %pad_add_fusion.ranks_ref, bf16[256,1024]{1,0:T(8,128)(2,1)S(1)} %constant_dynamic-update-slice_fusion.2.refs_0_, bf16[256,1024]{1,0:T(8,128)(2,1)S(1)} %collective-permute-done.13.refs_1_, ...), custom_call_target="tpu_custom_call" | custom-call | tf_op jit(solution)/shard_map/experts/pallas_call | solution.py:352
  51.0 1.0 %collective-permute-start.23 = (bf16[64,896]{1,0:T(8,128)(2,1)S(1)}, bf16[64,896]{1,0:T(8,128)(2,1)S(1)}, u32[]{:S(2)}, u32[]{:S(2)}) collective-permute-start(bf16[64,896]{1,0:T(8,128)(2,1)S(1)} %add_convert_fusion.9), channel_id=1, source_target_pairs={{0,4},{4,0},{8,12},{12,8},{16,20},{20,16},{24,28},{28,24},{1,5},{5... | collective-permute-start | bytes 344072 | tf_op jit(solution)/shard_map/ppermute | solution.py:20
  52.0 0.8 collective-permute-done.20
  53.1 1.4 %collective-permute-start.21 = (bf16[64,896]{1,0:T(8,128)(2,1)S(1)}, bf16[64,896]{1,0:T(8,128)(2,1)S(1)}, u32[]{:S(2)}, u32[]{:S(2)}) collective-permute-start(bf16[64,896]{1,0:T(8,128)(2,1)S(1)} %get-tuple-element.119), channel_id=1, source_target_pairs={{0,2},{1,3},{2,0},{3,1},{4,6},{5,7},{6,4},{7,5},{8,10},{9,11},{10,... | collective-permute-start | bytes 344072 | tf_op jit(solution)/shard_map/ppermute | solution.py:20
  55.2 3.0 %collective-permute-start.27 = (bf16[432,256]{1,0:T(8,128)(2,1)S(1)}, bf16[432,256]{1,0:T(8,128)(2,1)S(1)}, u32[]{:S(2)}, u32[]{:S(2)}) collective-permute-start(bf16[432,256]{1,0:T(8,128)(2,1)S(1)} %split.26), channel_id=1, source_target_pairs={{0,16},{4,20},{8,24},{12,28},{16,0},{20,4},{24,8},{28,12},{1,17},{... | collective-permute-start | bytes 663560 | tf_op jit(solution)/shard_map/ppermute | solution.py:20
  58.6 1.1 %collective-permute-done.22 = bf16[64,896]{1,0:T(8,128)(2,1)S(1)} collective-permute-done((bf16[64,896]{1,0:T(8,128)(2,1)S(1)}, bf16[64,896]{1,0:T(8,128)(2,1)S(1)}, u32[]{:S(2)}, u32[]{:S(2)}) %collective-permute-start.22) | collective-permute-done | bytes 114720 | tf_op jit(solution)/shard_map/ppermute | solution.py:20
  59.7 0.8 collective-permute-start.26
  60.7 1.0 %collective-permute-start.25 = (bf16[128,896]{1,0:T(8,128)(2,1)S(1)}, bf16[128,896]{1,0:T(8,128)(2,1)S(1)}, u32[]{:S(2)}, u32[]{:S(2)}) collective-permute-start(bf16[128,896]{1,0:T(8,128)(2,1)S(1)} %add_convert_fusion.5), channel_id=1, source_target_pairs={{0,4},{4,0},{8,12},{12,8},{16,20},{20,16},{24,28},{28,24},{1,5},{5... | collective-permute-start | bytes 688136 | tf_op jit(solution)/shard_map/ppermute | solution.py:20
  61.7 2.0 %collective-permute-start.30 = (bf16[64,896]{1,0:T(8,128)(2,1)S(1)}, bf16[64,896]{1,0:T(8,128)(2,1)S(1)}, u32[]{:S(2)}, u32[]{:S(2)}) collective-permute-start(bf16[64,896]{1,0:T(8,128)(2,1)S(1)} %get-tuple-element.115), channel_id=1, source_target_pairs={{0,8},{4,12},{8,0},{12,4},{16,24},{20,28},{24,16},{28,20},{1,9},{5... | collective-permute-start | bytes 344072 | tf_op jit(solution)/shard_map/ppermute | solution.py:20
  63.7 0.9 %collective-permute-start.31 = (bf16[64,896]{1,0:T(8,128)(2,1)S(1)}, bf16[64,896]{1,0:T(8,128)(2,1)S(1)}, u32[]{:S(2)}, u32[]{:S(2)}) collective-permute-start(bf16[64,896]{1,0:T(8,128)(2,1)S(1)} %get-tuple-element.114), channel_id=1, source_target_pairs={{0,2},{1,3},{2,0},{3,1},{4,6},{5,7},{6,4},{7,5},{8,10},{9,11},{10,... | collective-permute-start | bytes 344072 | tf_op jit(solution)/shard_map/ppermute | solution.py:20
  64.7 4.9 %attend_local.3.old_ref = bf16[16,128,512]{2,1,0:T(8,128)(2,1)} custom-call(s32[2]{0:T(128)S(1)} %pad_add_fusion.ranks_ref, s32[512]{0:T(512)S(1)} %copy-done.1, bf16[16,576,128]{2,1,0:T(8,128)(2,1)} %bitcast.14, bf16[16,576,256]{2,1,0:T(8,128)(2,1)} %bitcast.11, bf16[16,128,512]{2,1,0:T(8,128)(2,1)} %attend_local.2.refs_0_), custom_call_target="tpu_custom_call", output_to_operand_aliasing={{}: (4, {})} | custom-call | tf_op jit(solution)/shard_map/attend_local/pallas_call | solution.py:130
  69.7 2.0 %collective-permute-start.28 = (bf16[64,896]{1,0:T(8,128)(2,1)S(1)}, bf16[64,896]{1,0:T(8,128)(2,1)S(1)}, u32[]{:S(2)}, u32[]{:S(2)}) collective-permute-start(bf16[64,896]{1,0:T(8,128)(2,1)S(1)} %get-tuple-element.121), channel_id=1, source_target_pairs={{0,16},{4,20},{8,24},{12,28},{16,0},{20,4},{24,8},{28,12},{1,17},{... | collective-permute-start | bytes 344072 | tf_op jit(solution)/shard_map/ppermute | solution.py:20
  71.7 0.6 collective-permute-start.29
  72.4 7.2 %attend_rest.1 = bf16[16,128,512]{2,1,0:T(8,128)(2,1)} custom-call(s32[2]{0:T(128)S(1)} %pad_add_fusion.ranks_ref, s32[512]{0:T(512)S(1)} %copy-done.1, s32[32]{0:T(128)S(1)} %copy-done.2, s32[1]{0:T(128)S(6)} %copy.19.mask_ref, bf16[16,576,128]{2,1,0:T(8,128)(2,1)} %bitcast.15, bf16[16,576,256]{2,1,0:T(8,128)(2,1)} %bitcast.12, ...), custom_call_target="tpu_custom_call", output_to_operand_aliasing={{}: (7, {})} | custom-call | flops 71303168 | bytes 573440 | tf_op jit(solution)/shard_map/attend_rest/pallas_call | solution.py:220
  80.0 0.7 add_convert_fusion.6
  (86 shorter events, 5.2 us)
Async XLA Ops:
  2.6 8.2 %collective-permute-start = (bf16[64,1024]{1,0:T(8,128)(2,1)S(1)}, bf16[64,1024]{1,0:T(8,128)(2,1)S(1)}, u32[]{:S(2)}, u32[]{:S(2)}) collective-permute-start(bf16[64,1024]{1,0:T(8,128)(2,1)S(1)} %get-tuple-element.58.refs_1_), channel_id=1, source_target_pairs={{0,8},{4,12},{8,0},{12,4},{16,24},{20,28},{24,16},{28,20},{1,9},{5... | collective-permute-start | bytes 393224 | tf_op jit(solution)/shard_map/ppermute | solution.py:20
  5.7 13.1 %collective-permute-start.3 = (bf16[64,1024]{1,0:T(8,128)(2,1)S(1)}, bf16[64,1024]{1,0:T(8,128)(2,1)S(1)}, u32[]{:S(2)}, u32[]{:S(2)}) collective-permute-start(bf16[64,1024]{1,0:T(8,128)(2,1)S(1)} %get-tuple-element.58.refs_1_), channel_id=1, source_target_pairs={{0,16},{4,20},{8,24},{12,28},{16,0},{20,4},{24,8},{28,12},{1,17},{... | collective-permute-start | bytes 393224 | tf_op jit(solution)/shard_map/ppermute | solution.py:20
  8.3 10.5 %collective-permute-start.4 = (bf16[64,1024]{1,0:T(8,128)(2,1)S(1)}, bf16[64,1024]{1,0:T(8,128)(2,1)S(1)}, u32[]{:S(2)}, u32[]{:S(2)}) collective-permute-start(bf16[64,1024]{1,0:T(8,128)(2,1)S(1)} %get-tuple-element.58.refs_1_), channel_id=1, source_target_pairs={{0,24},{4,28},{8,16},{12,20},{16,8},{20,12},{24,0},{28,4},{1,25},{... | collective-permute-start | bytes 393224 | tf_op jit(solution)/shard_map/ppermute | solution.py:20
  10.8 8.0 %collective-permute-start.2 = (bf16[64,1024]{1,0:T(8,128)(2,1)S(1)}, bf16[64,1024]{1,0:T(8,128)(2,1)S(1)}, u32[]{:S(2)}, u32[]{:S(2)}) collective-permute-start(bf16[64,1024]{1,0:T(8,128)(2,1)S(1)} %collective-permute-done.refs_4_), channel_id=1, source_target_pairs={{0,4},{4,0},{8,12},{12,8},{16,20},{20,16},{24,28},{28,24},{1,5},{5... | collective-permute-start | bytes 393224 | tf_op jit(solution)/shard_map/ppermute | solution.py:20
  12.5 6.3 %collective-permute-start.1 = (bf16[64,896]{1,0:T(8,128)(2,1)S(1)}, bf16[64,896]{1,0:T(8,128)(2,1)S(1)}, u32[]{:S(2)}, u32[]{:S(2)}) collective-permute-start(bf16[64,896]{1,0:T(8,128)(2,1)S(1)} %slice.93), channel_id=1, source_target_pairs={{0,2},{1,3},{2,0},{3,1},{4,6},{5,7},{6,4},{7,5},{8,10},{9,11},{10,... | collective-permute-start | bytes 344072 | tf_op jit(solution)/shard_map/ppermute | solution.py:20
  14.0 7.9 %collective-permute-start.7 = (bf16[64,1920]{1,0:T(8,128)(2,1)S(1)}, bf16[64,1920]{1,0:T(8,128)(2,1)S(1)}, u32[]{:S(2)}, u32[]{:S(2)}) collective-permute-start(bf16[64,1920]{1,0:T(8,128)(2,1)S(1)} %get-tuple-element.68), channel_id=1, source_target_pairs={{0,4},{4,0},{8,12},{12,8},{16,20},{20,16},{24,28},{28,24},{1,5},{5... | collective-permute-start | bytes 737288 | tf_op jit(solution)/shard_map/ppermute | solution.py:20
  18.9 6.8 %collective-permute-start.9 = (bf16[192,1024]{1,0:T(8,128)(2,1)S(1)}, bf16[192,1024]{1,0:T(8,128)(2,1)S(1)}, u32[]{:S(2)}, u32[]{:S(2)}) collective-permute-start(bf16[192,1024]{1,0:T(8,128)(2,1)S(1)} %fusion.1), channel_id=1, source_target_pairs={{0,1},{1,0},{2,3},{3,2},{4,5},{5,4},{6,7},{7,6},{8,9},{9,8},{10,11... | collective-permute-start | bytes 1179656 | tf_op jit(solution)/shard_map/ppermute | solution.py:20
  19.1 10.5 %collective-permute-start.5 = (bf16[192,896]{1,0:T(8,128)(2,1)S(1)}, bf16[192,896]{1,0:T(8,128)(2,1)S(1)}, u32[]{:S(2)}, u32[]{:S(2)}) collective-permute-start(bf16[192,896]{1,0:T(8,128)(2,1)S(1)} %pad_maximum_fusion), channel_id=1, source_target_pairs={{0,2},{1,3},{2,0},{3,1},{4,6},{5,7},{6,4},{7,5},{8,10},{9,11},{10,... | collective-permute-start | bytes 1032200 | tf_op jit(solution)/shard_map/ppermute | solution.py:20
  20.5 9.0 %collective-permute-start.6 = (bf16[128,1024]{1,0:T(8,128)(2,1)S(1)}, bf16[128,1024]{1,0:T(8,128)(2,1)S(1)}, u32[]{:S(2)}, u32[]{:S(2)}) collective-permute-start(bf16[128,1024]{1,0:T(8,128)(2,1)S(1)} %constant_dynamic-update-slice_fusion), channel_id=1, source_target_pairs={{0,4},{4,0},{8,12},{12,8},{16,20},{20,16},{24,28},{28,24},{1,5},{5... | collective-permute-start | bytes 786440 | tf_op jit(solution)/shard_map/ppermute | solution.py:20
  22.0 3.7 %collective-permute-start.8 = (bf16[64,1920]{1,0:T(8,128)(2,1)S(1)}, bf16[64,1920]{1,0:T(8,128)(2,1)S(1)}, u32[]{:S(2)}, u32[]{:S(2)}) collective-permute-start(bf16[64,1920]{1,0:T(8,128)(2,1)S(1)} %collective-permute-done.7.refs_2_), channel_id=1, source_target_pairs={{0,1},{1,0},{2,3},{3,2},{4,5},{5,4},{6,7},{7,6},{8,9},{9,8},{10,11... | collective-permute-start | bytes 737288 | tf_op jit(solution)/shard_map/ppermute | solution.py:20
  22.0 7.5 %collective-permute-start.10 = (bf16[144,256]{1,0:T(8,128)(2,1)S(1)}, bf16[144,256]{1,0:T(8,128)(2,1)S(1)}, u32[]{:S(2)}, u32[]{:S(2)}) collective-permute-start(bf16[144,256]{1,0:T(8,128)(2,1)S(1)} %split.20), channel_id=1, source_target_pairs={{0,16},{4,20},{8,24},{12,28},{16,0},{20,4},{24,8},{28,12},{1,17},{... | collective-permute-start | bytes 221192 | tf_op jit(solution)/shard_map/ppermute | solution.py:20
  29.6 3.7 %collective-permute-start.11 = (bf16[192,896]{1,0:T(8,128)(2,1)S(1)}, bf16[192,896]{1,0:T(8,128)(2,1)S(1)}, u32[]{:S(2)}, u32[]{:S(2)}) collective-permute-start(bf16[192,896]{1,0:T(8,128)(2,1)S(1)} %collective-permute-done.5), channel_id=1, source_target_pairs={{0,1},{1,0},{2,3},{3,2},{4,5},{5,4},{6,7},{7,6},{8,9},{9,8},{10,11... | collective-permute-start | bytes 1032200 | tf_op jit(solution)/shard_map/ppermute | solution.py:20
  29.7 9.9 %collective-permute-start.13 = (bf16[256,1024]{1,0:T(8,128)(2,1)S(1)}, bf16[256,1024]{1,0:T(8,128)(2,1)S(1)}, u32[]{:S(2)}, u32[]{:S(2)}) collective-permute-start(bf16[256,1024]{1,0:T(8,128)(2,1)S(1)} %constant_dynamic-update-slice_fusion.2.refs_0_), channel_id=1, source_target_pairs={{0,1},{1,0},{2,3},{3,2},{4,5},{5,4},{6,7},{7,6},{8,9},{9,8},{10,11... | collective-permute-start | bytes 1572872 | tf_op jit(solution)/shard_map/ppermute | solution.py:20
  30.2 9.3 %collective-permute-start.14 = (bf16[576,256]{1,0:T(8,128)(2,1)S(1)}, bf16[576,256]{1,0:T(8,128)(2,1)S(1)}, u32[]{:S(2)}, u32[]{:S(2)}) collective-permute-start(bf16[576,256]{1,0:T(8,128)(2,1)S(1)} %pad_maximum_fusion.1), channel_id=1, source_target_pairs={{0,4},{4,0},{8,12},{12,8},{16,20},{20,16},{24,28},{28,24},{1,5},{5... | collective-permute-start | bytes 884744 | tf_op jit(solution)/shard_map/ppermute | solution.py:20
  31.8 7.7 %collective-permute-start.12 = (bf16[128,896]{1,0:T(8,128)(2,1)S(1)}, bf16[128,896]{1,0:T(8,128)(2,1)S(1)}, u32[]{:S(2)}, u32[]{:S(2)}) collective-permute-start(bf16[128,896]{1,0:T(8,128)(2,1)S(1)} %slice.100), channel_id=1, source_target_pairs={{0,2},{1,3},{2,0},{3,1},{4,6},{5,7},{6,4},{7,5},{8,10},{9,11},{10,... | collective-permute-start | bytes 688136 | tf_op jit(solution)/shard_map/ppermute | solution.py:20
  39.6 2.5 %collective-permute-start.16 = (bf16[512,896]{1,0:T(8,128)(2,1)S(1)}, bf16[512,896]{1,0:T(8,128)(2,1)S(1)}, u32[]{:S(2)}, u32[]{:S(2)}) collective-permute-start(bf16[512,896]{1,0:T(8,128)(2,1)S(1)} %get-tuple-element.89), channel_id=1, source_target_pairs={{0,1},{1,0},{2,3},{3,2},{4,5},{5,4},{6,7},{7,6},{8,9},{9,8},{10,11... | collective-permute-start | bytes 2752520 | tf_op jit(solution)/shard_map/ppermute | solution.py:20
  39.7 10.8 %collective-permute-start.19 = (bf16[576,256]{1,0:T(8,128)(2,1)S(1)}, bf16[576,256]{1,0:T(8,128)(2,1)S(1)}, u32[]{:S(2)}, u32[]{:S(2)}) collective-permute-start(bf16[576,256]{1,0:T(8,128)(2,1)S(1)} %broadcast_select_fusion.1), channel_id=1, source_target_pairs={{0,8},{4,12},{8,0},{12,4},{16,24},{20,28},{24,16},{28,20},{1,9},{5... | collective-permute-start | bytes 884744 | tf_op jit(solution)/shard_map/ppermute | solution.py:20
  41.8 3.2 %collective-permute-start.15 = (bf16[128,896]{1,0:T(8,128)(2,1)S(1)}, bf16[128,896]{1,0:T(8,128)(2,1)S(1)}, u32[]{:S(2)}, u32[]{:S(2)}) collective-permute-start(bf16[128,896]{1,0:T(8,128)(2,1)S(1)} %collective-permute-done.12.refs_4_), channel_id=1, source_target_pairs={{0,1},{1,0},{2,3},{3,2},{4,5},{5,4},{6,7},{7,6},{8,9},{9,8},{10,11... | collective-permute-start | bytes 688136 | tf_op jit(solution)/shard_map/ppermute | solution.py:20
  42.4 8.1 %collective-permute-start.18 = (bf16[64,1792]{1,0:T(8,128)(2,1)S(1)}, bf16[64,1792]{1,0:T(8,128)(2,1)S(1)}, u32[]{:S(2)}, u32[]{:S(2)}) collective-permute-start(bf16[64,1792]{1,0:T(8,128)(2,1)S(1)} %pad_maximum_fusion.3), channel_id=1, source_target_pairs={{0,4},{4,0},{8,12},{12,8},{16,20},{20,16},{24,28},{28,24},{1,5},{5... | collective-permute-start | bytes 688136 | tf_op jit(solution)/shard_map/ppermute | solution.py:20
  43.6 7.4 %collective-permute-start.17 = (bf16[128,896]{1,0:T(8,128)(2,1)S(1)}, bf16[128,896]{1,0:T(8,128)(2,1)S(1)}, u32[]{:S(2)}, u32[]{:S(2)}) collective-permute-start(bf16[128,896]{1,0:T(8,128)(2,1)S(1)} %slice.124), channel_id=1, source_target_pairs={{0,2},{1,3},{2,0},{3,1},{4,6},{5,7},{6,4},{7,5},{8,10},{9,11},{10,... | collective-permute-start | bytes 688136 | tf_op jit(solution)/shard_map/ppermute | solution.py:20
  51.0 1.8 %collective-permute-start.20 = (bf16[256,896]{1,0:T(8,128)(2,1)S(1)}, bf16[256,896]{1,0:T(8,128)(2,1)S(1)}, u32[]{:S(2)}, u32[]{:S(2)}) collective-permute-start(bf16[256,896]{1,0:T(8,128)(2,1)S(1)} %get-tuple-element.92), channel_id=1, source_target_pairs={{0,1},{1,0},{2,3},{3,2},{4,5},{5,4},{6,7},{7,6},{8,9},{9,8},{10,11... | collective-permute-start | bytes 1376264 | tf_op jit(solution)/shard_map/ppermute | solution.py:20
  51.0 7.2 %collective-permute-start.23 = (bf16[64,896]{1,0:T(8,128)(2,1)S(1)}, bf16[64,896]{1,0:T(8,128)(2,1)S(1)}, u32[]{:S(2)}, u32[]{:S(2)}) collective-permute-start(bf16[64,896]{1,0:T(8,128)(2,1)S(1)} %add_convert_fusion.9), channel_id=1, source_target_pairs={{0,4},{4,0},{8,12},{12,8},{16,20},{20,16},{24,28},{28,24},{1,5},{5... | collective-permute-start | bytes 344072 | tf_op jit(solution)/shard_map/ppermute | solution.py:20
  52.9 6.8 %collective-permute-start.24 = (bf16[256,896]{1,0:T(8,128)(2,1)S(1)}, bf16[256,896]{1,0:T(8,128)(2,1)S(1)}, u32[]{:S(2)}, u32[]{:S(2)}) collective-permute-start(bf16[256,896]{1,0:T(8,128)(2,1)S(1)} %get-tuple-element.96), channel_id=1, source_target_pairs={{0,1},{1,0},{2,3},{3,2},{4,5},{5,4},{6,7},{7,6},{8,9},{9,8},{10,11... | collective-permute-start | bytes 1376264 | tf_op jit(solution)/shard_map/ppermute | solution.py:20
  53.1 5.5 %collective-permute-start.21 = (bf16[64,896]{1,0:T(8,128)(2,1)S(1)}, bf16[64,896]{1,0:T(8,128)(2,1)S(1)}, u32[]{:S(2)}, u32[]{:S(2)}) collective-permute-start(bf16[64,896]{1,0:T(8,128)(2,1)S(1)} %get-tuple-element.119), channel_id=1, source_target_pairs={{0,2},{1,3},{2,0},{3,1},{4,6},{5,7},{6,4},{7,5},{8,10},{9,11},{10,... | collective-permute-start | bytes 344072 | tf_op jit(solution)/shard_map/ppermute | solution.py:20
  54.5 5.1 %collective-permute-start.22 = (bf16[64,896]{1,0:T(8,128)(2,1)S(1)}, bf16[64,896]{1,0:T(8,128)(2,1)S(1)}, u32[]{:S(2)}, u32[]{:S(2)}) collective-permute-start(bf16[64,896]{1,0:T(8,128)(2,1)S(1)} %get-tuple-element.118), channel_id=1, source_target_pairs={{0,4},{4,0},{8,12},{12,8},{16,20},{20,16},{24,28},{28,24},{1,5},{5... | collective-permute-start | bytes 344072 | tf_op jit(solution)/shard_map/ppermute | solution.py:20
  55.2 14.4 %collective-permute-start.27 = (bf16[432,256]{1,0:T(8,128)(2,1)S(1)}, bf16[432,256]{1,0:T(8,128)(2,1)S(1)}, u32[]{:S(2)}, u32[]{:S(2)}) collective-permute-start(bf16[432,256]{1,0:T(8,128)(2,1)S(1)} %split.26), channel_id=1, source_target_pairs={{0,16},{4,20},{8,24},{12,28},{16,0},{20,4},{24,8},{28,12},{1,17},{... | collective-permute-start | bytes 663560 | tf_op jit(solution)/shard_map/ppermute | solution.py:20
  59.7 9.8 %collective-permute-start.26 = (bf16[128,896]{1,0:T(8,128)(2,1)S(1)}, bf16[128,896]{1,0:T(8,128)(2,1)S(1)}, u32[]{:S(2)}, u32[]{:S(2)}) collective-permute-start(bf16[128,896]{1,0:T(8,128)(2,1)S(1)} %add_convert_fusion.4), channel_id=1, source_target_pairs={{0,2},{1,3},{2,0},{3,1},{4,6},{5,7},{6,4},{7,5},{8,10},{9,11},{10,... | collective-permute-start | bytes 688136 | tf_op jit(solution)/shard_map/ppermute | solution.py:20
  60.7 8.9 %collective-permute-start.25 = (bf16[128,896]{1,0:T(8,128)(2,1)S(1)}, bf16[128,896]{1,0:T(8,128)(2,1)S(1)}, u32[]{:S(2)}, u32[]{:S(2)}) collective-permute-start(bf16[128,896]{1,0:T(8,128)(2,1)S(1)} %add_convert_fusion.5), channel_id=1, source_target_pairs={{0,4},{4,0},{8,12},{12,8},{16,20},{20,16},{24,28},{28,24},{1,5},{5... | collective-permute-start | bytes 688136 | tf_op jit(solution)/shard_map/ppermute | solution.py:20
  61.7 17.9 %collective-permute-start.30 = (bf16[64,896]{1,0:T(8,128)(2,1)S(1)}, bf16[64,896]{1,0:T(8,128)(2,1)S(1)}, u32[]{:S(2)}, u32[]{:S(2)}) collective-permute-start(bf16[64,896]{1,0:T(8,128)(2,1)S(1)} %get-tuple-element.115), channel_id=1, source_target_pairs={{0,8},{4,12},{8,0},{12,4},{16,24},{20,28},{24,16},{28,20},{1,9},{5... | collective-permute-start | bytes 344072 | tf_op jit(solution)/shard_map/ppermute | solution.py:20
  63.7 16.3 %collective-permute-start.31 = (bf16[64,896]{1,0:T(8,128)(2,1)S(1)}, bf16[64,896]{1,0:T(8,128)(2,1)S(1)}, u32[]{:S(2)}, u32[]{:S(2)}) collective-permute-start(bf16[64,896]{1,0:T(8,128)(2,1)S(1)} %get-tuple-element.114), channel_id=1, source_target_pairs={{0,2},{1,3},{2,0},{3,1},{4,6},{5,7},{6,4},{7,5},{8,10},{9,11},{10,... | collective-permute-start | bytes 344072 | tf_op jit(solution)/shard_map/ppermute | solution.py:20
  69.7 10.3 %collective-permute-start.28 = (bf16[64,896]{1,0:T(8,128)(2,1)S(1)}, bf16[64,896]{1,0:T(8,128)(2,1)S(1)}, u32[]{:S(2)}, u32[]{:S(2)}) collective-permute-start(bf16[64,896]{1,0:T(8,128)(2,1)S(1)} %get-tuple-element.121), channel_id=1, source_target_pairs={{0,16},{4,20},{8,24},{12,28},{16,0},{20,4},{24,8},{28,12},{1,17},{... | collective-permute-start | bytes 344072 | tf_op jit(solution)/shard_map/ppermute | solution.py:20
  71.7 8.3 %collective-permute-start.29 = (bf16[64,896]{1,0:T(8,128)(2,1)S(1)}, bf16[64,896]{1,0:T(8,128)(2,1)S(1)}, u32[]{:S(2)}, u32[]{:S(2)}) collective-permute-start(bf16[64,896]{1,0:T(8,128)(2,1)S(1)} %get-tuple-element.120), channel_id=1, source_target_pairs={{0,24},{4,28},{8,16},{12,20},{16,8},{20,12},{24,0},{28,4},{1,25},{... | collective-permute-start | bytes 344072 | tf_op jit(solution)/shard_map/ppermute | solution.py:20
  (3 other events, 27.9 us)

commit v15 on v14

--- a/solution.py
+++ b/solution.py
@@ -198,20 +198,21 @@
         partner = device_of(ranks_ref, groups, mask_ref[0])
         mine = slots_ref[device]
         far_length = lengths_ref[partner * count + slots_ref[partner]]
-        block = jnp.where(step < steps, skip + step, mine // each)
-        for i in range(each):
-            at = block * each + i
-            traded = (step == steps) & (at == mine)
-
-            @pl.when(jnp.logical_not(traded))
-            def _():
-                out_ref[i] = attend_body(
-                    query_ref[i], pages_ref[i], lengths_ref[device * count + at]
-                )
-
-            @pl.when(traded)
-            def _():
-                out_ref[i] = attend_body(query_ref[i], page_ref[...], far_length)
+
+        @pl.when(step < steps)
+        def _():
+            for i in range(each):
+                at = device * count + first + step * each + i
+                out_ref[i] = attend_body(query_ref[i], pages_ref[i], lengths_ref[at])
+
+        @pl.when(step == steps)
+        def _():
+            for i in range(each):
+                at = mine // each * each + i
+                traded = at == mine
+                page = jnp.where(traded, page_ref[...], pages_ref[i])
+                length = jnp.where(traded, far_length, lengths_ref[device * count + at])
+                out_ref[i] = attend_body(query_ref[i], page, length)
 
     def request(i, ranks_ref, lengths_ref, slots_ref, mask_ref):
         mine = slots_ref[device_of(ranks_ref, groups)]
@@ -450,10 +451,11 @@
     near_2 = flip(own, "ep", 2)
     both_1 = flip(both, "ep", 1)
 
+    (w_gate,) = load(w_gate)
     near_2, w_gate, w_up = tie((near_2, w_gate, w_up))
     far_2 = flip(bare(near_2), "tp", 2)
     near_3 = flip(near_2, "ep", 1)
-    w_gate, w_up = load(w_gate, w_up)
+    (w_up,) = load(w_up)
     far_2, near_3, w_gate, w_up, page, *late_pieces = tie(
         (far_2, near_3, w_gate, w_up, page, *late_pieces)
     )

time: 81.1 us -> 80.9 us (level)
    pallas_call x1, Pallas kernels: 7.24 us -> 5.75 us  [attend_rest(): pl.pallas_call(kernel, out_shape=jax.ShapeDtypeStruct(attended.shape, att...]
    pallas_call x1 -> x2, Pallas kernels: 4.21 us -> 5.14 us  [load(): pl.pallas_call(load_kernel, out_shape=[pltpu.VMEM(w.shape, w.dtype) for w...]
  transfers between devices with their start and end apart: 32 -> 32, of which waited for: 9 -> 8; matrix products, arithmetic and copies ran while one was open for 2% -> 2% of each run, Pallas kernels for 39% -> 39%
where the time goes in v15:
time: 80.9 us; the launch traced here: 80.5 us
  starting transfers between devices  38 us (47%)
  Pallas kernels  33.1 us (41%)
  waiting for transfers between devices  5.46 us (7%)
  other arithmetic  1.82 us (2%)
  between operations  1.72 us (2%)
    ppermute x32, starting transfers between devices, flip(): return lax.ppermute(block, axis, [(i, i ^ apart) for i in range(count)])  38 us
    pallas_call x2, Pallas kernels, run_experts(): pl.pallas_call(kernel, out_shape=[[pltpu.VMEM((2 * rows // given, columns...  11.8 us
    pallas_call x2, Pallas kernels, attend_part(): pl.pallas_call(kernel, out_shape=jax.ShapeDtypeStruct((count, heads, LAT)...  8.53 us
    pallas_call x1, Pallas kernels, attend_rest(): pl.pallas_call(kernel, out_shape=jax.ShapeDtypeStruct(attended.shape, att...  5.75 us
    ppermute x32, waiting for transfers between devices, flip(): return lax.ppermute(block, axis, [(i, i ^ apart) for i in range(count)])  5.46 us
    pallas_call x2, Pallas kernels, load(): pl.pallas_call(load_kernel, out_shape=[pltpu.VMEM(w.shape, w.dtype) for w...  5.14 us
    pallas_call x1, Pallas kernels, pick(): pl.pallas_call(functools.partial(pick_kernel, groups), out_shape=(pltpu.V...  1.89 us
  transfers between devices with their start and end apart: 32, of which 8 were waited for; matrix products, arithmetic and copies ran while one was open for 2% of the time, Pallas kernels for 39%

profile of v15, /device:TPU:0, one launch (start us, length us, event | category | flops | bytes accessed | tf_op | source)
XLA Modules:
  0.0 80.5 jit_solution(2997367653611986083)
XLA Ops:
  0.7 1.9 %pick.1 = (bf16[64,1024]{1,0:T(8,128)(2,1)S(1)}, bf16[64,1920]{1,0:T(8,128)(2,1)S(1)}, bf16[576,256]{1,0:T(8,128)(2,1)S(1)}) custom-call(s32[2]{0:T(128)S(1)} %pad_add_fusion.ranks_ref, s32[32]{0:T(128)} %slots_ref.3, s32[8,64]{1,0:T(8,128)} %bitcast.16, f32[8,64]{1,0:T(8,128)} %bitcast.17, bf16[64,3584]{1,0:T(8,128)(2,1)} %refs_0_.4, ...), custom_call_target="tpu_custom_call" | custom-call | tf_op jit(solution)/shard_map/pick/pallas_call | solution.py:96
  2.6 3.1 %collective-permute-start = (bf16[64,1024]{1,0:T(8,128)(2,1)S(1)}, bf16[64,1024]{1,0:T(8,128)(2,1)S(1)}, u32[]{:S(2)}, u32[]{:S(2)}) collective-permute-start(bf16[64,1024]{1,0:T(8,128)(2,1)S(1)} %get-tuple-element.56.refs_1_), channel_id=1, source_target_pairs={{0,8},{4,12},{8,0},{12,4},{16,24},{20,28},{24,16},{28,20},{1,9},{5... | collective-permute-start | bytes 393224 | tf_op jit(solution)/shard_map/ppermute | solution.py:20
  5.7 2.6 %collective-permute-start.3 = (bf16[64,1024]{1,0:T(8,128)(2,1)S(1)}, bf16[64,1024]{1,0:T(8,128)(2,1)S(1)}, u32[]{:S(2)}, u32[]{:S(2)}) collective-permute-start(bf16[64,1024]{1,0:T(8,128)(2,1)S(1)} %get-tuple-element.56.refs_1_), channel_id=1, source_target_pairs={{0,16},{4,20},{8,24},{12,28},{16,0},{20,4},{24,8},{28,12},{1,17},{... | collective-permute-start | bytes 393224 | tf_op jit(solution)/shard_map/ppermute | solution.py:20
  8.3 2.6 %load.2.others_0_ = bf16[3,3584,256]{2,1,0:T(8,128)(2,1)S(1)} custom-call(bf16[3,3584,256]{2,1,0:T(8,128)(2,1)} %refs_0_.2), custom_call_target="tpu_custom_call" | custom-call | bytes 5505024 | tf_op jit(solution)/shard_map/load/pallas_call | solution.py:162
  10.9 1.8 %collective-permute-start.2 = (bf16[64,1024]{1,0:T(8,128)(2,1)S(1)}, bf16[64,1024]{1,0:T(8,128)(2,1)S(1)}, u32[]{:S(2)}, u32[]{:S(2)}) collective-permute-start(bf16[64,1024]{1,0:T(8,128)(2,1)S(1)} %collective-permute-done.refs_4_), channel_id=1, source_target_pairs={{0,4},{4,0},{8,12},{12,8},{16,20},{20,16},{24,28},{28,24},{1,5},{5... | collective-permute-start | bytes 393224 | tf_op jit(solution)/shard_map/ppermute | solution.py:20
  12.7 1.6 %collective-permute-start.1 = (bf16[64,896]{1,0:T(8,128)(2,1)S(1)}, bf16[64,896]{1,0:T(8,128)(2,1)S(1)}, u32[]{:S(2)}, u32[]{:S(2)}) collective-permute-start(bf16[64,896]{1,0:T(8,128)(2,1)S(1)} %slice.93), channel_id=1, source_target_pairs={{0,2},{1,3},{2,0},{3,1},{4,6},{5,7},{6,4},{7,5},{8,10},{9,11},{10,... | collective-permute-start | bytes 344072 | tf_op jit(solution)/shard_map/ppermute | solution.py:20
  14.8 2.6 %load.3.others_1_ = bf16[3,3584,256]{2,1,0:T(8,128)(2,1)S(1)} custom-call(bf16[3,3584,256]{2,1,0:T(8,128)(2,1)} %refs_0_.3), custom_call_target="tpu_custom_call" | custom-call | bytes 5505024 | tf_op jit(solution)/shard_map/load/pallas_call | solution.py:162
  17.4 1.3 %collective-permute-done.3 = bf16[64,1024]{1,0:T(8,128)(2,1)S(1)} collective-permute-done((bf16[64,1024]{1,0:T(8,128)(2,1)S(1)}, bf16[64,1024]{1,0:T(8,128)(2,1)S(1)}, u32[]{:S(2)}, u32[]{:S(2)}) %collective-permute-start.3) | collective-permute-done | bytes 131104 | tf_op jit(solution)/shard_map/ppermute | solution.py:20
  18.9 1.6 %collective-permute-start.5 = (bf16[192,896]{1,0:T(8,128)(2,1)S(1)}, bf16[192,896]{1,0:T(8,128)(2,1)S(1)}, u32[]{:S(2)}, u32[]{:S(2)}) collective-permute-start(bf16[192,896]{1,0:T(8,128)(2,1)S(1)} %pad_maximum_fusion), channel_id=1, source_target_pairs={{0,2},{1,3},{2,0},{3,1},{4,6},{5,7},{6,4},{7,5},{8,10},{9,11},{10,... | collective-permute-start | bytes 1032200 | tf_op jit(solution)/shard_map/ppermute | solution.py:20
  20.5 1.5 %collective-permute-start.6 = (bf16[128,1024]{1,0:T(8,128)(2,1)S(1)}, bf16[128,1024]{1,0:T(8,128)(2,1)S(1)}, u32[]{:S(2)}, u32[]{:S(2)}) collective-permute-start(bf16[128,1024]{1,0:T(8,128)(2,1)S(1)} %constant_dynamic-update-slice_fusion), channel_id=1, source_target_pairs={{0,4},{4,0},{8,12},{12,8},{16,20},{20,16},{24,28},{28,24},{1,5},{5... | collective-permute-start | bytes 786440 | tf_op jit(solution)/shard_map/ppermute | solution.py:20
  22.0 3.0 %collective-permute-start.10 = (bf16[144,256]{1,0:T(8,128)(2,1)S(1)}, bf16[144,256]{1,0:T(8,128)(2,1)S(1)}, u32[]{:S(2)}, u32[]{:S(2)}) collective-permute-start(bf16[144,256]{1,0:T(8,128)(2,1)S(1)} %split.20), channel_id=1, source_target_pairs={{0,16},{4,20},{8,24},{12,28},{16,0},{20,4},{24,8},{28,12},{1,17},{... | collective-permute-start | bytes 221192 | tf_op jit(solution)/shard_map/ppermute | solution.py:20
  25.7 3.6 %attend_local.2.refs_0_ = bf16[16,128,512]{2,1,0:T(8,128)(2,1)} custom-call(s32[2]{0:T(128)S(1)} %pad_add_fusion.ranks_ref, s32[512]{0:T(512)S(1)} %copy-done.1, bf16[16,576,128]{2,1,0:T(8,128)(2,1)} %bitcast.13, bf16[16,576,256]{2,1,0:T(8,128)(2,1)} %bitcast.10), custom_call_target="tpu_custom_call" | custom-call | tf_op jit(solution)/shard_map/attend_local/pallas_call | solution.py:130
  30.1 1.5 %collective-permute-start.14 = (bf16[576,256]{1,0:T(8,128)(2,1)S(1)}, bf16[576,256]{1,0:T(8,128)(2,1)S(1)}, u32[]{:S(2)}, u32[]{:S(2)}) collective-permute-start(bf16[576,256]{1,0:T(8,128)(2,1)S(1)} %pad_maximum_fusion.1), channel_id=1, source_target_pairs={{0,4},{4,0},{8,12},{12,8},{16,20},{20,16},{24,28},{28,24},{1,5},{5... | collective-permute-start | bytes 884744 | tf_op jit(solution)/shard_map/ppermute | solution.py:20
  31.7 1.6 %collective-permute-start.12 = (bf16[128,896]{1,0:T(8,128)(2,1)S(1)}, bf16[128,896]{1,0:T(8,128)(2,1)S(1)}, u32[]{:S(2)}, u32[]{:S(2)}) collective-permute-start(bf16[128,896]{1,0:T(8,128)(2,1)S(1)} %slice.100), channel_id=1, source_target_pairs={{0,2},{1,3},{2,0},{3,1},{4,6},{5,7},{6,4},{7,5},{8,10},{9,11},{10,... | collective-permute-start | bytes 688136 | tf_op jit(solution)/shard_map/ppermute | solution.py:20
  33.3 6.2 %experts.2 = (bf16[512,896]{1,0:T(8,128)(2,1)S(1)}, bf16[512,896]{1,0:T(8,128)(2,1)S(1)}, bf16[3,256,3584]{2,1,0:T(8,128)(2,1)S(1)}) custom-call(s32[2]{0:T(128)S(1)} %pad_add_fusion.ranks_ref, bf16[64,3584]{1,0:T(8,128)(2,1)S(1)} %copy-done, bf16[64,1024]{1,0:T(8,128)(2,1)S(1)} %get-tuple-element.56.refs_1_, ...), custom_call_target="tpu_custom_call" | custom-call | tf_op jit(solution)/shard_map/experts/pallas_call | solution.py:353
  39.7 2.0 %collective-permute-start.19 = (bf16[576,256]{1,0:T(8,128)(2,1)S(1)}, bf16[576,256]{1,0:T(8,128)(2,1)S(1)}, u32[]{:S(2)}, u32[]{:S(2)}) collective-permute-start(bf16[576,256]{1,0:T(8,128)(2,1)S(1)} %broadcast_select_fusion.1), channel_id=1, source_target_pairs={{0,8},{4,12},{8,0},{12,4},{16,24},{20,28},{24,16},{28,20},{1,9},{5... | collective-permute-start | bytes 884744 | tf_op jit(solution)/shard_map/ppermute | solution.py:20
  42.4 1.0 %collective-permute-start.18 = (bf16[64,1792]{1,0:T(8,128)(2,1)S(1)}, bf16[64,1792]{1,0:T(8,128)(2,1)S(1)}, u32[]{:S(2)}, u32[]{:S(2)}) collective-permute-start(bf16[64,1792]{1,0:T(8,128)(2,1)S(1)} %pad_maximum_fusion.3), channel_id=1, source_target_pairs={{0,4},{4,0},{8,12},{12,8},{16,20},{20,16},{24,28},{28,24},{1,5},{5... | collective-permute-start | bytes 688136 | tf_op jit(solution)/shard_map/ppermute | solution.py:20
  43.4 1.5 %collective-permute-start.17 = (bf16[128,896]{1,0:T(8,128)(2,1)S(1)}, bf16[128,896]{1,0:T(8,128)(2,1)S(1)}, u32[]{:S(2)}, u32[]{:S(2)}) collective-permute-start(bf16[128,896]{1,0:T(8,128)(2,1)S(1)} %slice.124), channel_id=1, source_target_pairs={{0,2},{1,3},{2,0},{3,1},{4,6},{5,7},{6,4},{7,5},{8,10},{9,11},{10,... | collective-permute-start | bytes 688136 | tf_op jit(solution)/shard_map/ppermute | solution.py:20
  45.0 5.6 %experts.3 = (bf16[256,896]{1,0:T(8,128)(2,1)S(1)}, bf16[256,896]{1,0:T(8,128)(2,1)S(1)}, bf16[512,896]{1,0:T(8,128)(2,1)S(1)}) custom-call(s32[2]{0:T(128)S(1)} %pad_add_fusion.ranks_ref, bf16[256,1024]{1,0:T(8,128)(2,1)S(1)} %constant_dynamic-update-slice_fusion.2.refs_0_, bf16[256,1024]{1,0:T(8,128)(2,1)S(1)} %collective-permute-done.13.refs_1_, ...), custom_call_target="tpu_custom_call" | custom-call | tf_op jit(solution)/shard_map/experts/pallas_call | solution.py:353
  50.9 1.2 %collective-permute-start.23 = (bf16[64,896]{1,0:T(8,128)(2,1)S(1)}, bf16[64,896]{1,0:T(8,128)(2,1)S(1)}, u32[]{:S(2)}, u32[]{:S(2)}) collective-permute-start(bf16[64,896]{1,0:T(8,128)(2,1)S(1)} %add_convert_fusion.9), channel_id=1, source_target_pairs={{0,4},{4,0},{8,12},{12,8},{16,20},{20,16},{24,28},{28,24},{1,5},{5... | collective-permute-start | bytes 344072 | tf_op jit(solution)/shard_map/ppermute | solution.py:20
  53.0 1.6 %collective-permute-start.21 = (bf16[64,896]{1,0:T(8,128)(2,1)S(1)}, bf16[64,896]{1,0:T(8,128)(2,1)S(1)}, u32[]{:S(2)}, u32[]{:S(2)}) collective-permute-start(bf16[64,896]{1,0:T(8,128)(2,1)S(1)} %get-tuple-element.115), channel_id=1, source_target_pairs={{0,2},{1,3},{2,0},{3,1},{4,6},{5,7},{6,4},{7,5},{8,10},{9,11},{10,... | collective-permute-start | bytes 344072 | tf_op jit(solution)/shard_map/ppermute | solution.py:20
  55.2 3.0 %collective-permute-start.27 = (bf16[432,256]{1,0:T(8,128)(2,1)S(1)}, bf16[432,256]{1,0:T(8,128)(2,1)S(1)}, u32[]{:S(2)}, u32[]{:S(2)}) collective-permute-start(bf16[432,256]{1,0:T(8,128)(2,1)S(1)} %split.26), channel_id=1, source_target_pairs={{0,16},{4,20},{8,24},{12,28},{16,0},{20,4},{24,8},{28,12},{1,17},{... | collective-permute-start | bytes 663560 | tf_op jit(solution)/shard_map/ppermute | solution.py:20
  58.5 1.2 %collective-permute-done.22 = bf16[64,896]{1,0:T(8,128)(2,1)S(1)} collective-permute-done((bf16[64,896]{1,0:T(8,128)(2,1)S(1)}, bf16[64,896]{1,0:T(8,128)(2,1)S(1)}, u32[]{:S(2)}, u32[]{:S(2)}) %collective-permute-start.22) | collective-permute-done | bytes 114720 | tf_op jit(solution)/shard_map/ppermute | solution.py:20
  59.7 0.8 %collective-permute-start.26 = (bf16[128,896]{1,0:T(8,128)(2,1)S(1)}, bf16[128,896]{1,0:T(8,128)(2,1)S(1)}, u32[]{:S(2)}, u32[]{:S(2)}) collective-permute-start(bf16[128,896]{1,0:T(8,128)(2,1)S(1)} %add_convert_fusion.4), channel_id=1, source_target_pairs={{0,2},{1,3},{2,0},{3,1},{4,6},{5,7},{6,4},{7,5},{8,10},{9,11},{10,... | collective-permute-start | bytes 688136 | tf_op jit(solution)/shard_map/ppermute | solution.py:20
  60.7 1.0 %collective-permute-start.25 = (bf16[128,896]{1,0:T(8,128)(2,1)S(1)}, bf16[128,896]{1,0:T(8,128)(2,1)S(1)}, u32[]{:S(2)}, u32[]{:S(2)}) collective-permute-start(bf16[128,896]{1,0:T(8,128)(2,1)S(1)} %add_convert_fusion.5), channel_id=1, source_target_pairs={{0,4},{4,0},{8,12},{12,8},{16,20},{20,16},{24,28},{28,24},{1,5},{5... | collective-permute-start | bytes 688136 | tf_op jit(solution)/shard_map/ppermute | solution.py:20
  61.7 2.0 %collective-permute-start.30 = (bf16[64,896]{1,0:T(8,128)(2,1)S(1)}, bf16[64,896]{1,0:T(8,128)(2,1)S(1)}, u32[]{:S(2)}, u32[]{:S(2)}) collective-permute-start(bf16[64,896]{1,0:T(8,128)(2,1)S(1)} %get-tuple-element.111), channel_id=1, source_target_pairs={{0,8},{4,12},{8,0},{12,4},{16,24},{20,28},{24,16},{28,20},{1,9},{5... | collective-permute-start | bytes 344072 | tf_op jit(solution)/shard_map/ppermute | solution.py:20
  63.7 0.9 %collective-permute-start.31 = (bf16[64,896]{1,0:T(8,128)(2,1)S(1)}, bf16[64,896]{1,0:T(8,128)(2,1)S(1)}, u32[]{:S(2)}, u32[]{:S(2)}) collective-permute-start(bf16[64,896]{1,0:T(8,128)(2,1)S(1)} %get-tuple-element.110), channel_id=1, source_target_pairs={{0,2},{1,3},{2,0},{3,1},{4,6},{5,7},{6,4},{7,5},{8,10},{9,11},{10,... | collective-permute-start | bytes 344072 | tf_op jit(solution)/shard_map/ppermute | solution.py:20
  64.7 4.9 %attend_local.3.old_ref = bf16[16,128,512]{2,1,0:T(8,128)(2,1)} custom-call(s32[2]{0:T(128)S(1)} %pad_add_fusion.ranks_ref, s32[512]{0:T(512)S(1)} %copy-done.1, bf16[16,576,128]{2,1,0:T(8,128)(2,1)} %bitcast.14, bf16[16,576,256]{2,1,0:T(8,128)(2,1)} %bitcast.11, bf16[16,128,512]{2,1,0:T(8,128)(2,1)} %attend_local.2.refs_0_), custom_call_target="tpu_custom_call", output_to_operand_aliasing={{}: (4, {})} | custom-call | tf_op jit(solution)/shard_map/attend_local/pallas_call | solution.py:130
  69.7 1.2 %collective-permute-start.28 = (bf16[64,896]{1,0:T(8,128)(2,1)S(1)}, bf16[64,896]{1,0:T(8,128)(2,1)S(1)}, u32[]{:S(2)}, u32[]{:S(2)}) collective-permute-start(bf16[64,896]{1,0:T(8,128)(2,1)S(1)} %get-tuple-element.117), channel_id=1, source_target_pairs={{0,16},{4,20},{8,24},{12,28},{16,0},{20,4},{24,8},{28,12},{1,17},{... | collective-permute-start | bytes 344072 | tf_op jit(solution)/shard_map/ppermute | solution.py:20
  70.9 1.4 %collective-permute-start.29 = (bf16[64,896]{1,0:T(8,128)(2,1)S(1)}, bf16[64,896]{1,0:T(8,128)(2,1)S(1)}, u32[]{:S(2)}, u32[]{:S(2)}) collective-permute-start(bf16[64,896]{1,0:T(8,128)(2,1)S(1)} %get-tuple-element.116), channel_id=1, source_target_pairs={{0,24},{4,28},{8,16},{12,20},{16,8},{20,12},{24,0},{28,4},{1,25},{... | collective-permute-start | bytes 344072 | tf_op jit(solution)/shard_map/ppermute | solution.py:20
  72.4 5.8 %attend_rest.1 = bf16[16,128,512]{2,1,0:T(8,128)(2,1)} custom-call(s32[2]{0:T(128)S(1)} %pad_add_fusion.ranks_ref, s32[512]{0:T(512)S(1)} %copy-done.1, s32[32]{0:T(128)S(1)} %copy-done.2, s32[1]{0:T(128)S(6)} %copy.19.mask_ref, bf16[16,576,128]{2,1,0:T(8,128)(2,1)} %bitcast.15, bf16[16,576,256]{2,1,0:T(8,128)(2,1)} %bitcast.12, ...), custom_call_target="tpu_custom_call", output_to_operand_aliasing={{}: (7, {})} | custom-call | flops 71303168 | bytes 573440 | tf_op jit(solution)/shard_map/attend_rest/pallas_call | solution.py:221
  78.1 1.6 %collective-permute-done.28 = bf16[64,896]{1,0:T(8,128)(2,1)S(1)} collective-permute-done((bf16[64,896]{1,0:T(8,128)(2,1)S(1)}, bf16[64,896]{1,0:T(8,128)(2,1)S(1)}, u32[]{:S(2)}, u32[]{:S(2)}) %collective-permute-start.28) | collective-permute-done | bytes 114720 | tf_op jit(solution)/shard_map/ppermute | solution.py:20
  (87 shorter events, 5.8 us)
Async XLA Ops:
  2.6 8.3 %collective-permute-start = (bf16[64,1024]{1,0:T(8,128)(2,1)S(1)}, bf16[64,1024]{1,0:T(8,128)(2,1)S(1)}, u32[]{:S(2)}, u32[]{:S(2)}) collective-permute-start(bf16[64,1024]{1,0:T(8,128)(2,1)S(1)} %get-tuple-element.56.refs_1_), channel_id=1, source_target_pairs={{0,8},{4,12},{8,0},{12,4},{16,24},{20,28},{24,16},{28,20},{1,9},{5... | collective-permute-start | bytes 393224 | tf_op jit(solution)/shard_map/ppermute | solution.py:20
  5.7 12.9 %collective-permute-start.3 = (bf16[64,1024]{1,0:T(8,128)(2,1)S(1)}, bf16[64,1024]{1,0:T(8,128)(2,1)S(1)}, u32[]{:S(2)}, u32[]{:S(2)}) collective-permute-start(bf16[64,1024]{1,0:T(8,128)(2,1)S(1)} %get-tuple-element.56.refs_1_), channel_id=1, source_target_pairs={{0,16},{4,20},{8,24},{12,28},{16,0},{20,4},{24,8},{28,12},{1,17},{... | collective-permute-start | bytes 393224 | tf_op jit(solution)/shard_map/ppermute | solution.py:20
  8.3 10.3 %collective-permute-start.4 = (bf16[64,1024]{1,0:T(8,128)(2,1)S(1)}, bf16[64,1024]{1,0:T(8,128)(2,1)S(1)}, u32[]{:S(2)}, u32[]{:S(2)}) collective-permute-start(bf16[64,1024]{1,0:T(8,128)(2,1)S(1)} %get-tuple-element.56.refs_1_), channel_id=1, source_target_pairs={{0,24},{4,28},{8,16},{12,20},{16,8},{20,12},{24,0},{28,4},{1,25},{... | collective-permute-start | bytes 393224 | tf_op jit(solution)/shard_map/ppermute | solution.py:20
  10.9 7.8 %collective-permute-start.2 = (bf16[64,1024]{1,0:T(8,128)(2,1)S(1)}, bf16[64,1024]{1,0:T(8,128)(2,1)S(1)}, u32[]{:S(2)}, u32[]{:S(2)}) collective-permute-start(bf16[64,1024]{1,0:T(8,128)(2,1)S(1)} %collective-permute-done.refs_4_), channel_id=1, source_target_pairs={{0,4},{4,0},{8,12},{12,8},{16,20},{20,16},{24,28},{28,24},{1,5},{5... | collective-permute-start | bytes 393224 | tf_op jit(solution)/shard_map/ppermute | solution.py:20
  12.7 6.0 %collective-permute-start.1 = (bf16[64,896]{1,0:T(8,128)(2,1)S(1)}, bf16[64,896]{1,0:T(8,128)(2,1)S(1)}, u32[]{:S(2)}, u32[]{:S(2)}) collective-permute-start(bf16[64,896]{1,0:T(8,128)(2,1)S(1)} %slice.93), channel_id=1, source_target_pairs={{0,2},{1,3},{2,0},{3,1},{4,6},{5,7},{6,4},{7,5},{8,10},{9,11},{10,... | collective-permute-start | bytes 344072 | tf_op jit(solution)/shard_map/ppermute | solution.py:20
  14.3 7.7 %collective-permute-start.7 = (bf16[64,1920]{1,0:T(8,128)(2,1)S(1)}, bf16[64,1920]{1,0:T(8,128)(2,1)S(1)}, u32[]{:S(2)}, u32[]{:S(2)}) collective-permute-start(bf16[64,1920]{1,0:T(8,128)(2,1)S(1)} %get-tuple-element.64), channel_id=1, source_target_pairs={{0,4},{4,0},{8,12},{12,8},{16,20},{20,16},{24,28},{28,24},{1,5},{5... | collective-permute-start | bytes 737288 | tf_op jit(solution)/shard_map/ppermute | solution.py:20
  18.7 7.0 %collective-permute-start.9 = (bf16[192,1024]{1,0:T(8,128)(2,1)S(1)}, bf16[192,1024]{1,0:T(8,128)(2,1)S(1)}, u32[]{:S(2)}, u32[]{:S(2)}) collective-permute-start(bf16[192,1024]{1,0:T(8,128)(2,1)S(1)} %fusion.1), channel_id=1, source_target_pairs={{0,1},{1,0},{2,3},{3,2},{4,5},{5,4},{6,7},{7,6},{8,9},{9,8},{10,11... | collective-permute-start | bytes 1179656 | tf_op jit(solution)/shard_map/ppermute | solution.py:20
  18.9 10.6 %collective-permute-start.5 = (bf16[192,896]{1,0:T(8,128)(2,1)S(1)}, bf16[192,896]{1,0:T(8,128)(2,1)S(1)}, u32[]{:S(2)}, u32[]{:S(2)}) collective-permute-start(bf16[192,896]{1,0:T(8,128)(2,1)S(1)} %pad_maximum_fusion), channel_id=1, source_target_pairs={{0,2},{1,3},{2,0},{3,1},{4,6},{5,7},{6,4},{7,5},{8,10},{9,11},{10,... | collective-permute-start | bytes 1032200 | tf_op jit(solution)/shard_map/ppermute | solution.py:20
  20.5 9.0 %collective-permute-start.6 = (bf16[128,1024]{1,0:T(8,128)(2,1)S(1)}, bf16[128,1024]{1,0:T(8,128)(2,1)S(1)}, u32[]{:S(2)}, u32[]{:S(2)}) collective-permute-start(bf16[128,1024]{1,0:T(8,128)(2,1)S(1)} %constant_dynamic-update-slice_fusion), channel_id=1, source_target_pairs={{0,4},{4,0},{8,12},{12,8},{16,20},{20,16},{24,28},{28,24},{1,5},{5... | collective-permute-start | bytes 786440 | tf_op jit(solution)/shard_map/ppermute | solution.py:20
  22.0 3.7 %collective-permute-start.8 = (bf16[64,1920]{1,0:T(8,128)(2,1)S(1)}, bf16[64,1920]{1,0:T(8,128)(2,1)S(1)}, u32[]{:S(2)}, u32[]{:S(2)}) collective-permute-start(bf16[64,1920]{1,0:T(8,128)(2,1)S(1)} %collective-permute-done.7.refs_2_), channel_id=1, source_target_pairs={{0,1},{1,0},{2,3},{3,2},{4,5},{5,4},{6,7},{7,6},{8,9},{9,8},{10,11... | collective-permute-start | bytes 737288 | tf_op jit(solution)/shard_map/ppermute | solution.py:20
  22.0 7.5 %collective-permute-start.10 = (bf16[144,256]{1,0:T(8,128)(2,1)S(1)}, bf16[144,256]{1,0:T(8,128)(2,1)S(1)}, u32[]{:S(2)}, u32[]{:S(2)}) collective-permute-start(bf16[144,256]{1,0:T(8,128)(2,1)S(1)} %split.20), channel_id=1, source_target_pairs={{0,16},{4,20},{8,24},{12,28},{16,0},{20,4},{24,8},{28,12},{1,17},{... | collective-permute-start | bytes 221192 | tf_op jit(solution)/shard_map/ppermute | solution.py:20
  29.5 3.8 %collective-permute-start.11 = (bf16[192,896]{1,0:T(8,128)(2,1)S(1)}, bf16[192,896]{1,0:T(8,128)(2,1)S(1)}, u32[]{:S(2)}, u32[]{:S(2)}) collective-permute-start(bf16[192,896]{1,0:T(8,128)(2,1)S(1)} %collective-permute-done.5), channel_id=1, source_target_pairs={{0,1},{1,0},{2,3},{3,2},{4,5},{5,4},{6,7},{7,6},{8,9},{9,8},{10,11... | collective-permute-start | bytes 1032200 | tf_op jit(solution)/shard_map/ppermute | solution.py:20
  29.7 9.9 %collective-permute-start.13 = (bf16[256,1024]{1,0:T(8,128)(2,1)S(1)}, bf16[256,1024]{1,0:T(8,128)(2,1)S(1)}, u32[]{:S(2)}, u32[]{:S(2)}) collective-permute-start(bf16[256,1024]{1,0:T(8,128)(2,1)S(1)} %constant_dynamic-update-slice_fusion.2.refs_0_), channel_id=1, source_target_pairs={{0,1},{1,0},{2,3},{3,2},{4,5},{5,4},{6,7},{7,6},{8,9},{9,8},{10,11... | collective-permute-start | bytes 1572872 | tf_op jit(solution)/shard_map/ppermute | solution.py:20
  30.1 9.4 %collective-permute-start.14 = (bf16[576,256]{1,0:T(8,128)(2,1)S(1)}, bf16[576,256]{1,0:T(8,128)(2,1)S(1)}, u32[]{:S(2)}, u32[]{:S(2)}) collective-permute-start(bf16[576,256]{1,0:T(8,128)(2,1)S(1)} %pad_maximum_fusion.1), channel_id=1, source_target_pairs={{0,4},{4,0},{8,12},{12,8},{16,20},{20,16},{24,28},{28,24},{1,5},{5... | collective-permute-start | bytes 884744 | tf_op jit(solution)/shard_map/ppermute | solution.py:20
  31.7 7.9 %collective-permute-start.12 = (bf16[128,896]{1,0:T(8,128)(2,1)S(1)}, bf16[128,896]{1,0:T(8,128)(2,1)S(1)}, u32[]{:S(2)}, u32[]{:S(2)}) collective-permute-start(bf16[128,896]{1,0:T(8,128)(2,1)S(1)} %slice.100), channel_id=1, source_target_pairs={{0,2},{1,3},{2,0},{3,1},{4,6},{5,7},{6,4},{7,5},{8,10},{9,11},{10,... | collective-permute-start | bytes 688136 | tf_op jit(solution)/shard_map/ppermute | solution.py:20
  39.6 2.5 %collective-permute-start.16 = (bf16[512,896]{1,0:T(8,128)(2,1)S(1)}, bf16[512,896]{1,0:T(8,128)(2,1)S(1)}, u32[]{:S(2)}, u32[]{:S(2)}) collective-permute-start(bf16[512,896]{1,0:T(8,128)(2,1)S(1)} %get-tuple-element.85), channel_id=1, source_target_pairs={{0,1},{1,0},{2,3},{3,2},{4,5},{5,4},{6,7},{7,6},{8,9},{9,8},{10,11... | collective-permute-start | bytes 2752520 | tf_op jit(solution)/shard_map/ppermute | solution.py:20
  39.7 10.8 %collective-permute-start.19 = (bf16[576,256]{1,0:T(8,128)(2,1)S(1)}, bf16[576,256]{1,0:T(8,128)(2,1)S(1)}, u32[]{:S(2)}, u32[]{:S(2)}) collective-permute-start(bf16[576,256]{1,0:T(8,128)(2,1)S(1)} %broadcast_select_fusion.1), channel_id=1, source_target_pairs={{0,8},{4,12},{8,0},{12,4},{16,24},{20,28},{24,16},{28,20},{1,9},{5... | collective-permute-start | bytes 884744 | tf_op jit(solution)/shard_map/ppermute | solution.py:20
  41.8 3.2 %collective-permute-start.15 = (bf16[128,896]{1,0:T(8,128)(2,1)S(1)}, bf16[128,896]{1,0:T(8,128)(2,1)S(1)}, u32[]{:S(2)}, u32[]{:S(2)}) collective-permute-start(bf16[128,896]{1,0:T(8,128)(2,1)S(1)} %collective-permute-done.12.refs_4_), channel_id=1, source_target_pairs={{0,1},{1,0},{2,3},{3,2},{4,5},{5,4},{6,7},{7,6},{8,9},{9,8},{10,11... | collective-permute-start | bytes 688136 | tf_op jit(solution)/shard_map/ppermute | solution.py:20
  42.4 8.1 %collective-permute-start.18 = (bf16[64,1792]{1,0:T(8,128)(2,1)S(1)}, bf16[64,1792]{1,0:T(8,128)(2,1)S(1)}, u32[]{:S(2)}, u32[]{:S(2)}) collective-permute-start(bf16[64,1792]{1,0:T(8,128)(2,1)S(1)} %pad_maximum_fusion.3), channel_id=1, source_target_pairs={{0,4},{4,0},{8,12},{12,8},{16,20},{20,16},{24,28},{28,24},{1,5},{5... | collective-permute-start | bytes 688136 | tf_op jit(solution)/shard_map/ppermute | solution.py:20
  43.4 7.4 %collective-permute-start.17 = (bf16[128,896]{1,0:T(8,128)(2,1)S(1)}, bf16[128,896]{1,0:T(8,128)(2,1)S(1)}, u32[]{:S(2)}, u32[]{:S(2)}) collective-permute-start(bf16[128,896]{1,0:T(8,128)(2,1)S(1)} %slice.124), channel_id=1, source_target_pairs={{0,2},{1,3},{2,0},{3,1},{4,6},{5,7},{6,4},{7,5},{8,10},{9,11},{10,... | collective-permute-start | bytes 688136 | tf_op jit(solution)/shard_map/ppermute | solution.py:20
  50.8 1.8 %collective-permute-start.20 = (bf16[256,896]{1,0:T(8,128)(2,1)S(1)}, bf16[256,896]{1,0:T(8,128)(2,1)S(1)}, u32[]{:S(2)}, u32[]{:S(2)}) collective-permute-start(bf16[256,896]{1,0:T(8,128)(2,1)S(1)} %get-tuple-element.88), channel_id=1, source_target_pairs={{0,1},{1,0},{2,3},{3,2},{4,5},{5,4},{6,7},{7,6},{8,9},{9,8},{10,11... | collective-permute-start | bytes 1376264 | tf_op jit(solution)/shard_map/ppermute | solution.py:20
  50.9 7.3 %collective-permute-start.23 = (bf16[64,896]{1,0:T(8,128)(2,1)S(1)}, bf16[64,896]{1,0:T(8,128)(2,1)S(1)}, u32[]{:S(2)}, u32[]{:S(2)}) collective-permute-start(bf16[64,896]{1,0:T(8,128)(2,1)S(1)} %add_convert_fusion.9), channel_id=1, source_target_pairs={{0,4},{4,0},{8,12},{12,8},{16,20},{20,16},{24,28},{28,24},{1,5},{5... | collective-permute-start | bytes 344072 | tf_op jit(solution)/shard_map/ppermute | solution.py:20
  52.8 6.9 %collective-permute-start.24 = (bf16[256,896]{1,0:T(8,128)(2,1)S(1)}, bf16[256,896]{1,0:T(8,128)(2,1)S(1)}, u32[]{:S(2)}, u32[]{:S(2)}) collective-permute-start(bf16[256,896]{1,0:T(8,128)(2,1)S(1)} %get-tuple-element.92), channel_id=1, source_target_pairs={{0,1},{1,0},{2,3},{3,2},{4,5},{5,4},{6,7},{7,6},{8,9},{9,8},{10,11... | collective-permute-start | bytes 1376264 | tf_op jit(solution)/shard_map/ppermute | solution.py:20
  53.0 5.5 %collective-permute-start.21 = (bf16[64,896]{1,0:T(8,128)(2,1)S(1)}, bf16[64,896]{1,0:T(8,128)(2,1)S(1)}, u32[]{:S(2)}, u32[]{:S(2)}) collective-permute-start(bf16[64,896]{1,0:T(8,128)(2,1)S(1)} %get-tuple-element.115), channel_id=1, source_target_pairs={{0,2},{1,3},{2,0},{3,1},{4,6},{5,7},{6,4},{7,5},{8,10},{9,11},{10,... | collective-permute-start | bytes 344072 | tf_op jit(solution)/shard_map/ppermute | solution.py:20
  54.5 5.1 %collective-permute-start.22 = (bf16[64,896]{1,0:T(8,128)(2,1)S(1)}, bf16[64,896]{1,0:T(8,128)(2,1)S(1)}, u32[]{:S(2)}, u32[]{:S(2)}) collective-permute-start(bf16[64,896]{1,0:T(8,128)(2,1)S(1)} %get-tuple-element.114), channel_id=1, source_target_pairs={{0,4},{4,0},{8,12},{12,8},{16,20},{20,16},{24,28},{28,24},{1,5},{5... | collective-permute-start | bytes 344072 | tf_op jit(solution)/shard_map/ppermute | solution.py:20
  55.2 14.4 %collective-permute-start.27 = (bf16[432,256]{1,0:T(8,128)(2,1)S(1)}, bf16[432,256]{1,0:T(8,128)(2,1)S(1)}, u32[]{:S(2)}, u32[]{:S(2)}) collective-permute-start(bf16[432,256]{1,0:T(8,128)(2,1)S(1)} %split.26), channel_id=1, source_target_pairs={{0,16},{4,20},{8,24},{12,28},{16,0},{20,4},{24,8},{28,12},{1,17},{... | collective-permute-start | bytes 663560 | tf_op jit(solution)/shard_map/ppermute | solution.py:20
  59.7 9.8 %collective-permute-start.26 = (bf16[128,896]{1,0:T(8,128)(2,1)S(1)}, bf16[128,896]{1,0:T(8,128)(2,1)S(1)}, u32[]{:S(2)}, u32[]{:S(2)}) collective-permute-start(bf16[128,896]{1,0:T(8,128)(2,1)S(1)} %add_convert_fusion.4), channel_id=1, source_target_pairs={{0,2},{1,3},{2,0},{3,1},{4,6},{5,7},{6,4},{7,5},{8,10},{9,11},{10,... | collective-permute-start | bytes 688136 | tf_op jit(solution)/shard_map/ppermute | solution.py:20
  60.7 8.9 %collective-permute-start.25 = (bf16[128,896]{1,0:T(8,128)(2,1)S(1)}, bf16[128,896]{1,0:T(8,128)(2,1)S(1)}, u32[]{:S(2)}, u32[]{:S(2)}) collective-permute-start(bf16[128,896]{1,0:T(8,128)(2,1)S(1)} %add_convert_fusion.5), channel_id=1, source_target_pairs={{0,4},{4,0},{8,12},{12,8},{16,20},{20,16},{24,28},{28,24},{1,5},{5... | collective-permute-start | bytes 688136 | tf_op jit(solution)/shard_map/ppermute | solution.py:20
  61.7 16.4 %collective-permute-start.30 = (bf16[64,896]{1,0:T(8,128)(2,1)S(1)}, bf16[64,896]{1,0:T(8,128)(2,1)S(1)}, u32[]{:S(2)}, u32[]{:S(2)}) collective-permute-start(bf16[64,896]{1,0:T(8,128)(2,1)S(1)} %get-tuple-element.111), channel_id=1, source_target_pairs={{0,8},{4,12},{8,0},{12,4},{16,24},{20,28},{24,16},{28,20},{1,9},{5... | collective-permute-start | bytes 344072 | tf_op jit(solution)/shard_map/ppermute | solution.py:20
  63.7 16.0 %collective-permute-start.31 = (bf16[64,896]{1,0:T(8,128)(2,1)S(1)}, bf16[64,896]{1,0:T(8,128)(2,1)S(1)}, u32[]{:S(2)}, u32[]{:S(2)}) collective-permute-start(bf16[64,896]{1,0:T(8,128)(2,1)S(1)} %get-tuple-element.110), channel_id=1, source_target_pairs={{0,2},{1,3},{2,0},{3,1},{4,6},{5,7},{6,4},{7,5},{8,10},{9,11},{10,... | collective-permute-start | bytes 344072 | tf_op jit(solution)/shard_map/ppermute | solution.py:20
  69.7 10.0 %collective-permute-start.28 = (bf16[64,896]{1,0:T(8,128)(2,1)S(1)}, bf16[64,896]{1,0:T(8,128)(2,1)S(1)}, u32[]{:S(2)}, u32[]{:S(2)}) collective-permute-start(bf16[64,896]{1,0:T(8,128)(2,1)S(1)} %get-tuple-element.117), channel_id=1, source_target_pairs={{0,16},{4,20},{8,24},{12,28},{16,0},{20,4},{24,8},{28,12},{1,17},{... | collective-permute-start | bytes 344072 | tf_op jit(solution)/shard_map/ppermute | solution.py:20
  70.9 8.8 %collective-permute-start.29 = (bf16[64,896]{1,0:T(8,128)(2,1)S(1)}, bf16[64,896]{1,0:T(8,128)(2,1)S(1)}, u32[]{:S(2)}, u32[]{:S(2)}) collective-permute-start(bf16[64,896]{1,0:T(8,128)(2,1)S(1)} %get-tuple-element.116), channel_id=1, source_target_pairs={{0,24},{4,28},{8,16},{12,20},{16,8},{20,12},{24,0},{28,4},{1,25},{... | collective-permute-start | bytes 344072 | tf_op jit(solution)/shard_map/ppermute | solution.py:20
  (3 other events, 27.7 us)

commit v16 on v15

--- a/solution.py
+++ b/solution.py
@@ -467,7 +467,7 @@
     core_1 = flip(both_1, "tp", 1)
     queries, core_1, core_23 = tie((queries, core_1, core_23))
     count = queries.shape[0]
-    some, middle = count // 4, count * 5 // 8
+    some, middle = count // 4, count // 2
     attended = attend_part(ranks, lengths, queries, cache_pages, groups, 0, some)
     least = page.shape[0] // 4
     upper, lower = jnp.split(page, [least], axis=0)

time: 80.9 us -> 80.4 us (level)
  starting transfers between devices: 38 us -> 39.1 us
  waiting for transfers between devices: 5.46 us -> 4.44 us
    pallas_call x2, Pallas kernels: 8.53 us -> 7.3 us  [attend_part(): pl.pallas_call(kernel, out_shape=jax.ShapeDtypeStruct((count, heads, LAT)...]
    ppermute x32, starting transfers between devices: 38 us -> 39.1 us  [flip(): return lax.ppermute(block, axis, [(i, i ^ apart) for i in range(count)])]
    ppermute x32, waiting for transfers between devices: 5.46 us -> 4.44 us  [flip(): return lax.ppermute(block, axis, [(i, i ^ apart) for i in range(count)])]
  transfers between devices with their start and end apart: 32 -> 32, of which waited for: 8 -> 9; matrix products, arithmetic and copies ran while one was open for 2% -> 2% of each run, Pallas kernels for 39% -> 38%
where the time goes in v16:
time: 80.4 us; the launch traced here: 79.9 us
  starting transfers between devices  39.1 us (49%)
  Pallas kernels  32.6 us (41%)
  waiting for transfers between devices  4.44 us (6%)
  other arithmetic  1.82 us (2%)
  between operations  1.71 us (2%)
    ppermute x32, starting transfers between devices, flip(): return lax.ppermute(block, axis, [(i, i ^ apart) for i in range(count)])  39.1 us
    pallas_call x2, Pallas kernels, run_experts(): pl.pallas_call(kernel, out_shape=[[pltpu.VMEM((2 * rows // given, columns...  11.8 us
    pallas_call x2, Pallas kernels, attend_part(): pl.pallas_call(kernel, out_shape=jax.ShapeDtypeStruct((count, heads, LAT)...  7.3 us
    pallas_call x1, Pallas kernels, attend_rest(): pl.pallas_call(kernel, out_shape=jax.ShapeDtypeStruct(attended.shape, att...  6.45 us
    pallas_call x2, Pallas kernels, load(): pl.pallas_call(load_kernel, out_shape=[pltpu.VMEM(w.shape, w.dtype) for w...  5.14 us
    ppermute x32, waiting for transfers between devices, flip(): return lax.ppermute(block, axis, [(i, i ^ apart) for i in range(count)])  4.44 us
    pallas_call x1, Pallas kernels, pick(): pl.pallas_call(functools.partial(pick_kernel, groups), out_shape=(pltpu.V...  1.89 us
  transfers between devices with their start and end apart: 32, of which 9 were waited for; matrix products, arithmetic and copies ran while one was open for 2% of the time, Pallas kernels for 38%

profile of v16, /device:TPU:0, one launch (start us, length us, event | category | flops | bytes accessed | tf_op | source)
XLA Modules:
  0.0 79.9 jit_solution(8474772738669418164)
XLA Ops:
  0.7 1.9 %pick.1 = (bf16[64,1024]{1,0:T(8,128)(2,1)S(1)}, bf16[64,1920]{1,0:T(8,128)(2,1)S(1)}, bf16[576,256]{1,0:T(8,128)(2,1)S(1)}) custom-call(s32[2]{0:T(128)S(1)} %pad_add_fusion.ranks_ref, s32[32]{0:T(128)} %slots_ref.3, s32[8,64]{1,0:T(8,128)} %bitcast.16, f32[8,64]{1,0:T(8,128)} %bitcast.17, bf16[64,3584]{1,0:T(8,128)(2,1)} %refs_0_.4, ...), custom_call_target="tpu_custom_call" | custom-call | tf_op jit(solution)/shard_map/pick/pallas_call | solution.py:96
  2.6 3.1 %collective-permute-start = (bf16[64,1024]{1,0:T(8,128)(2,1)S(1)}, bf16[64,1024]{1,0:T(8,128)(2,1)S(1)}, u32[]{:S(2)}, u32[]{:S(2)}) collective-permute-start(bf16[64,1024]{1,0:T(8,128)(2,1)S(1)} %get-tuple-element.56.refs_1_), channel_id=1, source_target_pairs={{0,8},{4,12},{8,0},{12,4},{16,24},{20,28},{24,16},{28,20},{1,9},{5... | collective-permute-start | bytes 393224 | tf_op jit(solution)/shard_map/ppermute | solution.py:20
  5.7 2.6 %collective-permute-start.3 = (bf16[64,1024]{1,0:T(8,128)(2,1)S(1)}, bf16[64,1024]{1,0:T(8,128)(2,1)S(1)}, u32[]{:S(2)}, u32[]{:S(2)}) collective-permute-start(bf16[64,1024]{1,0:T(8,128)(2,1)S(1)} %get-tuple-element.56.refs_1_), channel_id=1, source_target_pairs={{0,16},{4,20},{8,24},{12,28},{16,0},{20,4},{24,8},{28,12},{1,17},{... | collective-permute-start | bytes 393224 | tf_op jit(solution)/shard_map/ppermute | solution.py:20
  8.3 2.6 %load.2.others_0_ = bf16[3,3584,256]{2,1,0:T(8,128)(2,1)S(1)} custom-call(bf16[3,3584,256]{2,1,0:T(8,128)(2,1)} %refs_0_.2), custom_call_target="tpu_custom_call" | custom-call | bytes 5505024 | tf_op jit(solution)/shard_map/load/pallas_call | solution.py:162
  10.9 1.8 %collective-permute-start.2 = (bf16[64,1024]{1,0:T(8,128)(2,1)S(1)}, bf16[64,1024]{1,0:T(8,128)(2,1)S(1)}, u32[]{:S(2)}, u32[]{:S(2)}) collective-permute-start(bf16[64,1024]{1,0:T(8,128)(2,1)S(1)} %collective-permute-done.refs_4_), channel_id=1, source_target_pairs={{0,4},{4,0},{8,12},{12,8},{16,20},{20,16},{24,28},{28,24},{1,5},{5... | collective-permute-start | bytes 393224 | tf_op jit(solution)/shard_map/ppermute | solution.py:20
  12.7 1.6 %collective-permute-start.1 = (bf16[64,896]{1,0:T(8,128)(2,1)S(1)}, bf16[64,896]{1,0:T(8,128)(2,1)S(1)}, u32[]{:S(2)}, u32[]{:S(2)}) collective-permute-start(bf16[64,896]{1,0:T(8,128)(2,1)S(1)} %slice.93), channel_id=1, source_target_pairs={{0,2},{1,3},{2,0},{3,1},{4,6},{5,7},{6,4},{7,5},{8,10},{9,11},{10,... | collective-permute-start | bytes 344072 | tf_op jit(solution)/shard_map/ppermute | solution.py:20
  14.8 2.6 %load.3.others_1_ = bf16[3,3584,256]{2,1,0:T(8,128)(2,1)S(1)} custom-call(bf16[3,3584,256]{2,1,0:T(8,128)(2,1)} %refs_0_.3), custom_call_target="tpu_custom_call" | custom-call | bytes 5505024 | tf_op jit(solution)/shard_map/load/pallas_call | solution.py:162
  17.4 1.2 %collective-permute-done.3 = bf16[64,1024]{1,0:T(8,128)(2,1)S(1)} collective-permute-done((bf16[64,1024]{1,0:T(8,128)(2,1)S(1)}, bf16[64,1024]{1,0:T(8,128)(2,1)S(1)}, u32[]{:S(2)}, u32[]{:S(2)}) %collective-permute-start.3) | collective-permute-done | bytes 131104 | tf_op jit(solution)/shard_map/ppermute | solution.py:20
  18.9 1.6 %collective-permute-start.5 = (bf16[192,896]{1,0:T(8,128)(2,1)S(1)}, bf16[192,896]{1,0:T(8,128)(2,1)S(1)}, u32[]{:S(2)}, u32[]{:S(2)}) collective-permute-start(bf16[192,896]{1,0:T(8,128)(2,1)S(1)} %pad_maximum_fusion), channel_id=1, source_target_pairs={{0,2},{1,3},{2,0},{3,1},{4,6},{5,7},{6,4},{7,5},{8,10},{9,11},{10,... | collective-permute-start | bytes 1032200 | tf_op jit(solution)/shard_map/ppermute | solution.py:20
  20.5 1.5 %collective-permute-start.6 = (bf16[128,1024]{1,0:T(8,128)(2,1)S(1)}, bf16[128,1024]{1,0:T(8,128)(2,1)S(1)}, u32[]{:S(2)}, u32[]{:S(2)}) collective-permute-start(bf16[128,1024]{1,0:T(8,128)(2,1)S(1)} %constant_dynamic-update-slice_fusion), channel_id=1, source_target_pairs={{0,4},{4,0},{8,12},{12,8},{16,20},{20,16},{24,28},{28,24},{1,5},{5... | collective-permute-start | bytes 786440 | tf_op jit(solution)/shard_map/ppermute | solution.py:20
  22.0 3.0 %collective-permute-start.10 = (bf16[144,256]{1,0:T(8,128)(2,1)S(1)}, bf16[144,256]{1,0:T(8,128)(2,1)S(1)}, u32[]{:S(2)}, u32[]{:S(2)}) collective-permute-start(bf16[144,256]{1,0:T(8,128)(2,1)S(1)} %split.20), channel_id=1, source_target_pairs={{0,16},{4,20},{8,24},{12,28},{16,0},{20,4},{24,8},{28,12},{1,17},{... | collective-permute-start | bytes 221192 | tf_op jit(solution)/shard_map/ppermute | solution.py:20
  25.7 3.6 %attend_local.2.refs_0_ = bf16[16,128,512]{2,1,0:T(8,128)(2,1)} custom-call(s32[2]{0:T(128)S(1)} %pad_add_fusion.ranks_ref, s32[512]{0:T(512)S(1)} %copy-done.1, bf16[16,576,128]{2,1,0:T(8,128)(2,1)} %bitcast.13, bf16[16,576,256]{2,1,0:T(8,128)(2,1)} %bitcast.10), custom_call_target="tpu_custom_call" | custom-call | tf_op jit(solution)/shard_map/attend_local/pallas_call | solution.py:130
  30.1 1.5 %collective-permute-start.14 = (bf16[576,256]{1,0:T(8,128)(2,1)S(1)}, bf16[576,256]{1,0:T(8,128)(2,1)S(1)}, u32[]{:S(2)}, u32[]{:S(2)}) collective-permute-start(bf16[576,256]{1,0:T(8,128)(2,1)S(1)} %pad_maximum_fusion.1), channel_id=1, source_target_pairs={{0,4},{4,0},{8,12},{12,8},{16,20},{20,16},{24,28},{28,24},{1,5},{5... | collective-permute-start | bytes 884744 | tf_op jit(solution)/shard_map/ppermute | solution.py:20
  31.6 1.6 %collective-permute-start.12 = (bf16[128,896]{1,0:T(8,128)(2,1)S(1)}, bf16[128,896]{1,0:T(8,128)(2,1)S(1)}, u32[]{:S(2)}, u32[]{:S(2)}) collective-permute-start(bf16[128,896]{1,0:T(8,128)(2,1)S(1)} %slice.100), channel_id=1, source_target_pairs={{0,2},{1,3},{2,0},{3,1},{4,6},{5,7},{6,4},{7,5},{8,10},{9,11},{10,... | collective-permute-start | bytes 688136 | tf_op jit(solution)/shard_map/ppermute | solution.py:20
  33.3 6.2 %experts.2 = (bf16[512,896]{1,0:T(8,128)(2,1)S(1)}, bf16[512,896]{1,0:T(8,128)(2,1)S(1)}, bf16[3,256,3584]{2,1,0:T(8,128)(2,1)S(1)}) custom-call(s32[2]{0:T(128)S(1)} %pad_add_fusion.ranks_ref, bf16[64,3584]{1,0:T(8,128)(2,1)S(1)} %copy-done, bf16[64,1024]{1,0:T(8,128)(2,1)S(1)} %get-tuple-element.56.refs_1_, ...), custom_call_target="tpu_custom_call" | custom-call | tf_op jit(solution)/shard_map/experts/pallas_call | solution.py:353
  39.7 2.0 %collective-permute-start.19 = (bf16[576,256]{1,0:T(8,128)(2,1)S(1)}, bf16[576,256]{1,0:T(8,128)(2,1)S(1)}, u32[]{:S(2)}, u32[]{:S(2)}) collective-permute-start(bf16[576,256]{1,0:T(8,128)(2,1)S(1)} %broadcast_select_fusion.1), channel_id=1, source_target_pairs={{0,8},{4,12},{8,0},{12,4},{16,24},{20,28},{24,16},{28,20},{1,9},{5... | collective-permute-start | bytes 884744 | tf_op jit(solution)/shard_map/ppermute | solution.py:20
  42.4 1.0 %collective-permute-start.18 = (bf16[64,1792]{1,0:T(8,128)(2,1)S(1)}, bf16[64,1792]{1,0:T(8,128)(2,1)S(1)}, u32[]{:S(2)}, u32[]{:S(2)}) collective-permute-start(bf16[64,1792]{1,0:T(8,128)(2,1)S(1)} %pad_maximum_fusion.3), channel_id=1, source_target_pairs={{0,4},{4,0},{8,12},{12,8},{16,20},{20,16},{24,28},{28,24},{1,5},{5... | collective-permute-start | bytes 688136 | tf_op jit(solution)/shard_map/ppermute | solution.py:20
  43.4 1.5 %collective-permute-start.17 = (bf16[128,896]{1,0:T(8,128)(2,1)S(1)}, bf16[128,896]{1,0:T(8,128)(2,1)S(1)}, u32[]{:S(2)}, u32[]{:S(2)}) collective-permute-start(bf16[128,896]{1,0:T(8,128)(2,1)S(1)} %slice.124), channel_id=1, source_target_pairs={{0,2},{1,3},{2,0},{3,1},{4,6},{5,7},{6,4},{7,5},{8,10},{9,11},{10,... | collective-permute-start | bytes 688136 | tf_op jit(solution)/shard_map/ppermute | solution.py:20
  45.0 5.6 %experts.3 = (bf16[256,896]{1,0:T(8,128)(2,1)S(1)}, bf16[256,896]{1,0:T(8,128)(2,1)S(1)}, bf16[512,896]{1,0:T(8,128)(2,1)S(1)}) custom-call(s32[2]{0:T(128)S(1)} %pad_add_fusion.ranks_ref, bf16[256,1024]{1,0:T(8,128)(2,1)S(1)} %constant_dynamic-update-slice_fusion.2.refs_0_, bf16[256,1024]{1,0:T(8,128)(2,1)S(1)} %collective-permute-done.13.refs_1_, ...), custom_call_target="tpu_custom_call" | custom-call | tf_op jit(solution)/shard_map/experts/pallas_call | solution.py:353
  50.9 1.1 %collective-permute-start.23 = (bf16[64,896]{1,0:T(8,128)(2,1)S(1)}, bf16[64,896]{1,0:T(8,128)(2,1)S(1)}, u32[]{:S(2)}, u32[]{:S(2)}) collective-permute-start(bf16[64,896]{1,0:T(8,128)(2,1)S(1)} %add_convert_fusion.9), channel_id=1, source_target_pairs={{0,4},{4,0},{8,12},{12,8},{16,20},{20,16},{24,28},{28,24},{1,5},{5... | collective-permute-start | bytes 344072 | tf_op jit(solution)/shard_map/ppermute | solution.py:20
  53.0 1.5 %collective-permute-start.21 = (bf16[64,896]{1,0:T(8,128)(2,1)S(1)}, bf16[64,896]{1,0:T(8,128)(2,1)S(1)}, u32[]{:S(2)}, u32[]{:S(2)}) collective-permute-start(bf16[64,896]{1,0:T(8,128)(2,1)S(1)} %get-tuple-element.115), channel_id=1, source_target_pairs={{0,2},{1,3},{2,0},{3,1},{4,6},{5,7},{6,4},{7,5},{8,10},{9,11},{10,... | collective-permute-start | bytes 344072 | tf_op jit(solution)/shard_map/ppermute | solution.py:20
  55.2 3.0 %collective-permute-start.27 = (bf16[432,256]{1,0:T(8,128)(2,1)S(1)}, bf16[432,256]{1,0:T(8,128)(2,1)S(1)}, u32[]{:S(2)}, u32[]{:S(2)}) collective-permute-start(bf16[432,256]{1,0:T(8,128)(2,1)S(1)} %split.26), channel_id=1, source_target_pairs={{0,16},{4,20},{8,24},{12,28},{16,0},{20,4},{24,8},{28,12},{1,17},{... | collective-permute-start | bytes 663560 | tf_op jit(solution)/shard_map/ppermute | solution.py:20
  58.5 1.2 %collective-permute-done.22 = bf16[64,896]{1,0:T(8,128)(2,1)S(1)} collective-permute-done((bf16[64,896]{1,0:T(8,128)(2,1)S(1)}, bf16[64,896]{1,0:T(8,128)(2,1)S(1)}, u32[]{:S(2)}, u32[]{:S(2)}) %collective-permute-start.22) | collective-permute-done | bytes 114720 | tf_op jit(solution)/shard_map/ppermute | solution.py:20
  59.7 0.8 %collective-permute-start.26 = (bf16[128,896]{1,0:T(8,128)(2,1)S(1)}, bf16[128,896]{1,0:T(8,128)(2,1)S(1)}, u32[]{:S(2)}, u32[]{:S(2)}) collective-permute-start(bf16[128,896]{1,0:T(8,128)(2,1)S(1)} %add_convert_fusion.4), channel_id=1, source_target_pairs={{0,2},{1,3},{2,0},{3,1},{4,6},{5,7},{6,4},{7,5},{8,10},{9,11},{10,... | collective-permute-start | bytes 688136 | tf_op jit(solution)/shard_map/ppermute | solution.py:20
  60.7 1.0 %collective-permute-start.25 = (bf16[128,896]{1,0:T(8,128)(2,1)S(1)}, bf16[128,896]{1,0:T(8,128)(2,1)S(1)}, u32[]{:S(2)}, u32[]{:S(2)}) collective-permute-start(bf16[128,896]{1,0:T(8,128)(2,1)S(1)} %add_convert_fusion.5), channel_id=1, source_target_pairs={{0,4},{4,0},{8,12},{12,8},{16,20},{20,16},{24,28},{28,24},{1,5},{5... | collective-permute-start | bytes 688136 | tf_op jit(solution)/shard_map/ppermute | solution.py:20
  61.7 2.0 %collective-permute-start.30 = (bf16[64,896]{1,0:T(8,128)(2,1)S(1)}, bf16[64,896]{1,0:T(8,128)(2,1)S(1)}, u32[]{:S(2)}, u32[]{:S(2)}) collective-permute-start(bf16[64,896]{1,0:T(8,128)(2,1)S(1)} %get-tuple-element.111), channel_id=1, source_target_pairs={{0,8},{4,12},{8,0},{12,4},{16,24},{20,28},{24,16},{28,20},{1,9},{5... | collective-permute-start | bytes 344072 | tf_op jit(solution)/shard_map/ppermute | solution.py:20
  63.7 0.9 %collective-permute-start.31 = (bf16[64,896]{1,0:T(8,128)(2,1)S(1)}, bf16[64,896]{1,0:T(8,128)(2,1)S(1)}, u32[]{:S(2)}, u32[]{:S(2)}) collective-permute-start(bf16[64,896]{1,0:T(8,128)(2,1)S(1)} %get-tuple-element.110), channel_id=1, source_target_pairs={{0,2},{1,3},{2,0},{3,1},{4,6},{5,7},{6,4},{7,5},{8,10},{9,11},{10,... | collective-permute-start | bytes 344072 | tf_op jit(solution)/shard_map/ppermute | solution.py:20
  64.7 3.6 %attend_local.3.old_ref = bf16[16,128,512]{2,1,0:T(8,128)(2,1)} custom-call(s32[2]{0:T(128)S(1)} %pad_add_fusion.ranks_ref, s32[512]{0:T(512)S(1)} %copy-done.1, bf16[16,576,128]{2,1,0:T(8,128)(2,1)} %bitcast.14, bf16[16,576,256]{2,1,0:T(8,128)(2,1)} %bitcast.11, bf16[16,128,512]{2,1,0:T(8,128)(2,1)} %attend_local.2.refs_0_), custom_call_target="tpu_custom_call", output_to_operand_aliasing={{}: (4, {})} | custom-call | tf_op jit(solution)/shard_map/attend_local/pallas_call | solution.py:130
  68.6 2.4 %collective-permute-start.28 = (bf16[64,896]{1,0:T(8,128)(2,1)S(1)}, bf16[64,896]{1,0:T(8,128)(2,1)S(1)}, u32[]{:S(2)}, u32[]{:S(2)}) collective-permute-start(bf16[64,896]{1,0:T(8,128)(2,1)S(1)} %get-tuple-element.117), channel_id=1, source_target_pairs={{0,16},{4,20},{8,24},{12,28},{16,0},{20,4},{24,8},{28,12},{1,17},{... | collective-permute-start | bytes 344072 | tf_op jit(solution)/shard_map/ppermute | solution.py:20
  70.9 1.4 %collective-permute-start.29 = (bf16[64,896]{1,0:T(8,128)(2,1)S(1)}, bf16[64,896]{1,0:T(8,128)(2,1)S(1)}, u32[]{:S(2)}, u32[]{:S(2)}) collective-permute-start(bf16[64,896]{1,0:T(8,128)(2,1)S(1)} %get-tuple-element.116), channel_id=1, source_target_pairs={{0,24},{4,28},{8,16},{12,20},{16,8},{20,12},{24,0},{28,4},{1,25},{... | collective-permute-start | bytes 344072 | tf_op jit(solution)/shard_map/ppermute | solution.py:20
  72.3 6.5 %attend_rest.1 = bf16[16,128,512]{2,1,0:T(8,128)(2,1)} custom-call(s32[2]{0:T(128)S(1)} %pad_add_fusion.ranks_ref, s32[512]{0:T(512)S(1)} %copy-done.1, s32[32]{0:T(128)S(1)} %copy-done.2, s32[1]{0:T(128)S(6)} %copy.19.mask_ref, bf16[16,576,128]{2,1,0:T(8,128)(2,1)} %bitcast.15, bf16[16,576,256]{2,1,0:T(8,128)(2,1)} %bitcast.12, ...), custom_call_target="tpu_custom_call", output_to_operand_aliasing={{}: (7, {})} | custom-call | flops 71303168 | bytes 573440 | tf_op jit(solution)/shard_map/attend_rest/pallas_call | solution.py:221
  79.2 0.7 add_convert_fusion.6
  (87 shorter events, 5.7 us)
Async XLA Ops:
  2.6 8.3 %collective-permute-start = (bf16[64,1024]{1,0:T(8,128)(2,1)S(1)}, bf16[64,1024]{1,0:T(8,128)(2,1)S(1)}, u32[]{:S(2)}, u32[]{:S(2)}) collective-permute-start(bf16[64,1024]{1,0:T(8,128)(2,1)S(1)} %get-tuple-element.56.refs_1_), channel_id=1, source_target_pairs={{0,8},{4,12},{8,0},{12,4},{16,24},{20,28},{24,16},{28,20},{1,9},{5... | collective-permute-start | bytes 393224 | tf_op jit(solution)/shard_map/ppermute | solution.py:20
  5.7 12.9 %collective-permute-start.3 = (bf16[64,1024]{1,0:T(8,128)(2,1)S(1)}, bf16[64,1024]{1,0:T(8,128)(2,1)S(1)}, u32[]{:S(2)}, u32[]{:S(2)}) collective-permute-start(bf16[64,1024]{1,0:T(8,128)(2,1)S(1)} %get-tuple-element.56.refs_1_), channel_id=1, source_target_pairs={{0,16},{4,20},{8,24},{12,28},{16,0},{20,4},{24,8},{28,12},{1,17},{... | collective-permute-start | bytes 393224 | tf_op jit(solution)/shard_map/ppermute | solution.py:20
  8.3 10.4 %collective-permute-start.4 = (bf16[64,1024]{1,0:T(8,128)(2,1)S(1)}, bf16[64,1024]{1,0:T(8,128)(2,1)S(1)}, u32[]{:S(2)}, u32[]{:S(2)}) collective-permute-start(bf16[64,1024]{1,0:T(8,128)(2,1)S(1)} %get-tuple-element.56.refs_1_), channel_id=1, source_target_pairs={{0,24},{4,28},{8,16},{12,20},{16,8},{20,12},{24,0},{28,4},{1,25},{... | collective-permute-start | bytes 393224 | tf_op jit(solution)/shard_map/ppermute | solution.py:20
  10.9 7.8 %collective-permute-start.2 = (bf16[64,1024]{1,0:T(8,128)(2,1)S(1)}, bf16[64,1024]{1,0:T(8,128)(2,1)S(1)}, u32[]{:S(2)}, u32[]{:S(2)}) collective-permute-start(bf16[64,1024]{1,0:T(8,128)(2,1)S(1)} %collective-permute-done.refs_4_), channel_id=1, source_target_pairs={{0,4},{4,0},{8,12},{12,8},{16,20},{20,16},{24,28},{28,24},{1,5},{5... | collective-permute-start | bytes 393224 | tf_op jit(solution)/shard_map/ppermute | solution.py:20
  12.7 6.0 %collective-permute-start.1 = (bf16[64,896]{1,0:T(8,128)(2,1)S(1)}, bf16[64,896]{1,0:T(8,128)(2,1)S(1)}, u32[]{:S(2)}, u32[]{:S(2)}) collective-permute-start(bf16[64,896]{1,0:T(8,128)(2,1)S(1)} %slice.93), channel_id=1, source_target_pairs={{0,2},{1,3},{2,0},{3,1},{4,6},{5,7},{6,4},{7,5},{8,10},{9,11},{10,... | collective-permute-start | bytes 344072 | tf_op jit(solution)/shard_map/ppermute | solution.py:20
  14.3 7.7 %collective-permute-start.7 = (bf16[64,1920]{1,0:T(8,128)(2,1)S(1)}, bf16[64,1920]{1,0:T(8,128)(2,1)S(1)}, u32[]{:S(2)}, u32[]{:S(2)}) collective-permute-start(bf16[64,1920]{1,0:T(8,128)(2,1)S(1)} %get-tuple-element.64), channel_id=1, source_target_pairs={{0,4},{4,0},{8,12},{12,8},{16,20},{20,16},{24,28},{28,24},{1,5},{5... | collective-permute-start | bytes 737288 | tf_op jit(solution)/shard_map/ppermute | solution.py:20
  18.7 7.0 %collective-permute-start.9 = (bf16[192,1024]{1,0:T(8,128)(2,1)S(1)}, bf16[192,1024]{1,0:T(8,128)(2,1)S(1)}, u32[]{:S(2)}, u32[]{:S(2)}) collective-permute-start(bf16[192,1024]{1,0:T(8,128)(2,1)S(1)} %fusion.1), channel_id=1, source_target_pairs={{0,1},{1,0},{2,3},{3,2},{4,5},{5,4},{6,7},{7,6},{8,9},{9,8},{10,11... | collective-permute-start | bytes 1179656 | tf_op jit(solution)/shard_map/ppermute | solution.py:20
  18.9 10.6 %collective-permute-start.5 = (bf16[192,896]{1,0:T(8,128)(2,1)S(1)}, bf16[192,896]{1,0:T(8,128)(2,1)S(1)}, u32[]{:S(2)}, u32[]{:S(2)}) collective-permute-start(bf16[192,896]{1,0:T(8,128)(2,1)S(1)} %pad_maximum_fusion), channel_id=1, source_target_pairs={{0,2},{1,3},{2,0},{3,1},{4,6},{5,7},{6,4},{7,5},{8,10},{9,11},{10,... | collective-permute-start | bytes 1032200 | tf_op jit(solution)/shard_map/ppermute | solution.py:20
  20.5 9.0 %collective-permute-start.6 = (bf16[128,1024]{1,0:T(8,128)(2,1)S(1)}, bf16[128,1024]{1,0:T(8,128)(2,1)S(1)}, u32[]{:S(2)}, u32[]{:S(2)}) collective-permute-start(bf16[128,1024]{1,0:T(8,128)(2,1)S(1)} %constant_dynamic-update-slice_fusion), channel_id=1, source_target_pairs={{0,4},{4,0},{8,12},{12,8},{16,20},{20,16},{24,28},{28,24},{1,5},{5... | collective-permute-start | bytes 786440 | tf_op jit(solution)/shard_map/ppermute | solution.py:20
  22.0 3.7 %collective-permute-start.8 = (bf16[64,1920]{1,0:T(8,128)(2,1)S(1)}, bf16[64,1920]{1,0:T(8,128)(2,1)S(1)}, u32[]{:S(2)}, u32[]{:S(2)}) collective-permute-start(bf16[64,1920]{1,0:T(8,128)(2,1)S(1)} %collective-permute-done.7.refs_2_), channel_id=1, source_target_pairs={{0,1},{1,0},{2,3},{3,2},{4,5},{5,4},{6,7},{7,6},{8,9},{9,8},{10,11... | collective-permute-start | bytes 737288 | tf_op jit(solution)/shard_map/ppermute | solution.py:20
  22.0 7.5 %collective-permute-start.10 = (bf16[144,256]{1,0:T(8,128)(2,1)S(1)}, bf16[144,256]{1,0:T(8,128)(2,1)S(1)}, u32[]{:S(2)}, u32[]{:S(2)}) collective-permute-start(bf16[144,256]{1,0:T(8,128)(2,1)S(1)} %split.20), channel_id=1, source_target_pairs={{0,16},{4,20},{8,24},{12,28},{16,0},{20,4},{24,8},{28,12},{1,17},{... | collective-permute-start | bytes 221192 | tf_op jit(solution)/shard_map/ppermute | solution.py:20
  29.5 3.8 %collective-permute-start.11 = (bf16[192,896]{1,0:T(8,128)(2,1)S(1)}, bf16[192,896]{1,0:T(8,128)(2,1)S(1)}, u32[]{:S(2)}, u32[]{:S(2)}) collective-permute-start(bf16[192,896]{1,0:T(8,128)(2,1)S(1)} %collective-permute-done.5), channel_id=1, source_target_pairs={{0,1},{1,0},{2,3},{3,2},{4,5},{5,4},{6,7},{7,6},{8,9},{9,8},{10,11... | collective-permute-start | bytes 1032200 | tf_op jit(solution)/shard_map/ppermute | solution.py:20
  29.7 9.9 %collective-permute-start.13 = (bf16[256,1024]{1,0:T(8,128)(2,1)S(1)}, bf16[256,1024]{1,0:T(8,128)(2,1)S(1)}, u32[]{:S(2)}, u32[]{:S(2)}) collective-permute-start(bf16[256,1024]{1,0:T(8,128)(2,1)S(1)} %constant_dynamic-update-slice_fusion.2.refs_0_), channel_id=1, source_target_pairs={{0,1},{1,0},{2,3},{3,2},{4,5},{5,4},{6,7},{7,6},{8,9},{9,8},{10,11... | collective-permute-start | bytes 1572872 | tf_op jit(solution)/shard_map/ppermute | solution.py:20
  30.1 9.4 %collective-permute-start.14 = (bf16[576,256]{1,0:T(8,128)(2,1)S(1)}, bf16[576,256]{1,0:T(8,128)(2,1)S(1)}, u32[]{:S(2)}, u32[]{:S(2)}) collective-permute-start(bf16[576,256]{1,0:T(8,128)(2,1)S(1)} %pad_maximum_fusion.1), channel_id=1, source_target_pairs={{0,4},{4,0},{8,12},{12,8},{16,20},{20,16},{24,28},{28,24},{1,5},{5... | collective-permute-start | bytes 884744 | tf_op jit(solution)/shard_map/ppermute | solution.py:20
  31.6 7.9 %collective-permute-start.12 = (bf16[128,896]{1,0:T(8,128)(2,1)S(1)}, bf16[128,896]{1,0:T(8,128)(2,1)S(1)}, u32[]{:S(2)}, u32[]{:S(2)}) collective-permute-start(bf16[128,896]{1,0:T(8,128)(2,1)S(1)} %slice.100), channel_id=1, source_target_pairs={{0,2},{1,3},{2,0},{3,1},{4,6},{5,7},{6,4},{7,5},{8,10},{9,11},{10,... | collective-permute-start | bytes 688136 | tf_op jit(solution)/shard_map/ppermute | solution.py:20
  39.6 2.5 %collective-permute-start.16 = (bf16[512,896]{1,0:T(8,128)(2,1)S(1)}, bf16[512,896]{1,0:T(8,128)(2,1)S(1)}, u32[]{:S(2)}, u32[]{:S(2)}) collective-permute-start(bf16[512,896]{1,0:T(8,128)(2,1)S(1)} %get-tuple-element.85), channel_id=1, source_target_pairs={{0,1},{1,0},{2,3},{3,2},{4,5},{5,4},{6,7},{7,6},{8,9},{9,8},{10,11... | collective-permute-start | bytes 2752520 | tf_op jit(solution)/shard_map/ppermute | solution.py:20
  39.7 10.8 %collective-permute-start.19 = (bf16[576,256]{1,0:T(8,128)(2,1)S(1)}, bf16[576,256]{1,0:T(8,128)(2,1)S(1)}, u32[]{:S(2)}, u32[]{:S(2)}) collective-permute-start(bf16[576,256]{1,0:T(8,128)(2,1)S(1)} %broadcast_select_fusion.1), channel_id=1, source_target_pairs={{0,8},{4,12},{8,0},{12,4},{16,24},{20,28},{24,16},{28,20},{1,9},{5... | collective-permute-start | bytes 884744 | tf_op jit(solution)/shard_map/ppermute | solution.py:20
  41.8 3.2 %collective-permute-start.15 = (bf16[128,896]{1,0:T(8,128)(2,1)S(1)}, bf16[128,896]{1,0:T(8,128)(2,1)S(1)}, u32[]{:S(2)}, u32[]{:S(2)}) collective-permute-start(bf16[128,896]{1,0:T(8,128)(2,1)S(1)} %collective-permute-done.12.refs_4_), channel_id=1, source_target_pairs={{0,1},{1,0},{2,3},{3,2},{4,5},{5,4},{6,7},{7,6},{8,9},{9,8},{10,11... | collective-permute-start | bytes 688136 | tf_op jit(solution)/shard_map/ppermute | solution.py:20
  42.4 8.1 %collective-permute-start.18 = (bf16[64,1792]{1,0:T(8,128)(2,1)S(1)}, bf16[64,1792]{1,0:T(8,128)(2,1)S(1)}, u32[]{:S(2)}, u32[]{:S(2)}) collective-permute-start(bf16[64,1792]{1,0:T(8,128)(2,1)S(1)} %pad_maximum_fusion.3), channel_id=1, source_target_pairs={{0,4},{4,0},{8,12},{12,8},{16,20},{20,16},{24,28},{28,24},{1,5},{5... | collective-permute-start | bytes 688136 | tf_op jit(solution)/shard_map/ppermute | solution.py:20
  43.4 7.4 %collective-permute-start.17 = (bf16[128,896]{1,0:T(8,128)(2,1)S(1)}, bf16[128,896]{1,0:T(8,128)(2,1)S(1)}, u32[]{:S(2)}, u32[]{:S(2)}) collective-permute-start(bf16[128,896]{1,0:T(8,128)(2,1)S(1)} %slice.124), channel_id=1, source_target_pairs={{0,2},{1,3},{2,0},{3,1},{4,6},{5,7},{6,4},{7,5},{8,10},{9,11},{10,... | collective-permute-start | bytes 688136 | tf_op jit(solution)/shard_map/ppermute | solution.py:20
  50.9 1.8 %collective-permute-start.20 = (bf16[256,896]{1,0:T(8,128)(2,1)S(1)}, bf16[256,896]{1,0:T(8,128)(2,1)S(1)}, u32[]{:S(2)}, u32[]{:S(2)}) collective-permute-start(bf16[256,896]{1,0:T(8,128)(2,1)S(1)} %get-tuple-element.88), channel_id=1, source_target_pairs={{0,1},{1,0},{2,3},{3,2},{4,5},{5,4},{6,7},{7,6},{8,9},{9,8},{10,11... | collective-permute-start | bytes 1376264 | tf_op jit(solution)/shard_map/ppermute | solution.py:20
  50.9 7.3 %collective-permute-start.23 = (bf16[64,896]{1,0:T(8,128)(2,1)S(1)}, bf16[64,896]{1,0:T(8,128)(2,1)S(1)}, u32[]{:S(2)}, u32[]{:S(2)}) collective-permute-start(bf16[64,896]{1,0:T(8,128)(2,1)S(1)} %add_convert_fusion.9), channel_id=1, source_target_pairs={{0,4},{4,0},{8,12},{12,8},{16,20},{20,16},{24,28},{28,24},{1,5},{5... | collective-permute-start | bytes 344072 | tf_op jit(solution)/shard_map/ppermute | solution.py:20
  52.8 6.9 %collective-permute-start.24 = (bf16[256,896]{1,0:T(8,128)(2,1)S(1)}, bf16[256,896]{1,0:T(8,128)(2,1)S(1)}, u32[]{:S(2)}, u32[]{:S(2)}) collective-permute-start(bf16[256,896]{1,0:T(8,128)(2,1)S(1)} %get-tuple-element.92), channel_id=1, source_target_pairs={{0,1},{1,0},{2,3},{3,2},{4,5},{5,4},{6,7},{7,6},{8,9},{9,8},{10,11... | collective-permute-start | bytes 1376264 | tf_op jit(solution)/shard_map/ppermute | solution.py:20
  53.0 5.5 %collective-permute-start.21 = (bf16[64,896]{1,0:T(8,128)(2,1)S(1)}, bf16[64,896]{1,0:T(8,128)(2,1)S(1)}, u32[]{:S(2)}, u32[]{:S(2)}) collective-permute-start(bf16[64,896]{1,0:T(8,128)(2,1)S(1)} %get-tuple-element.115), channel_id=1, source_target_pairs={{0,2},{1,3},{2,0},{3,1},{4,6},{5,7},{6,4},{7,5},{8,10},{9,11},{10,... | collective-permute-start | bytes 344072 | tf_op jit(solution)/shard_map/ppermute | solution.py:20
  54.5 5.1 %collective-permute-start.22 = (bf16[64,896]{1,0:T(8,128)(2,1)S(1)}, bf16[64,896]{1,0:T(8,128)(2,1)S(1)}, u32[]{:S(2)}, u32[]{:S(2)}) collective-permute-start(bf16[64,896]{1,0:T(8,128)(2,1)S(1)} %get-tuple-element.114), channel_id=1, source_target_pairs={{0,4},{4,0},{8,12},{12,8},{16,20},{20,16},{24,28},{28,24},{1,5},{5... | collective-permute-start | bytes 344072 | tf_op jit(solution)/shard_map/ppermute | solution.py:20
  55.2 13.3 %collective-permute-start.27 = (bf16[432,256]{1,0:T(8,128)(2,1)S(1)}, bf16[432,256]{1,0:T(8,128)(2,1)S(1)}, u32[]{:S(2)}, u32[]{:S(2)}) collective-permute-start(bf16[432,256]{1,0:T(8,128)(2,1)S(1)} %split.26), channel_id=1, source_target_pairs={{0,16},{4,20},{8,24},{12,28},{16,0},{20,4},{24,8},{28,12},{1,17},{... | collective-permute-start | bytes 663560 | tf_op jit(solution)/shard_map/ppermute | solution.py:20
  59.7 8.7 %collective-permute-start.26 = (bf16[128,896]{1,0:T(8,128)(2,1)S(1)}, bf16[128,896]{1,0:T(8,128)(2,1)S(1)}, u32[]{:S(2)}, u32[]{:S(2)}) collective-permute-start(bf16[128,896]{1,0:T(8,128)(2,1)S(1)} %add_convert_fusion.4), channel_id=1, source_target_pairs={{0,2},{1,3},{2,0},{3,1},{4,6},{5,7},{6,4},{7,5},{8,10},{9,11},{10,... | collective-permute-start | bytes 688136 | tf_op jit(solution)/shard_map/ppermute | solution.py:20
  60.7 7.8 %collective-permute-start.25 = (bf16[128,896]{1,0:T(8,128)(2,1)S(1)}, bf16[128,896]{1,0:T(8,128)(2,1)S(1)}, u32[]{:S(2)}, u32[]{:S(2)}) collective-permute-start(bf16[128,896]{1,0:T(8,128)(2,1)S(1)} %add_convert_fusion.5), channel_id=1, source_target_pairs={{0,4},{4,0},{8,12},{12,8},{16,20},{20,16},{24,28},{28,24},{1,5},{5... | collective-permute-start | bytes 688136 | tf_op jit(solution)/shard_map/ppermute | solution.py:20
  61.7 17.1 %collective-permute-start.30 = (bf16[64,896]{1,0:T(8,128)(2,1)S(1)}, bf16[64,896]{1,0:T(8,128)(2,1)S(1)}, u32[]{:S(2)}, u32[]{:S(2)}) collective-permute-start(bf16[64,896]{1,0:T(8,128)(2,1)S(1)} %get-tuple-element.111), channel_id=1, source_target_pairs={{0,8},{4,12},{8,0},{12,4},{16,24},{20,28},{24,16},{28,20},{1,9},{5... | collective-permute-start | bytes 344072 | tf_op jit(solution)/shard_map/ppermute | solution.py:20
  63.7 15.5 %collective-permute-start.31 = (bf16[64,896]{1,0:T(8,128)(2,1)S(1)}, bf16[64,896]{1,0:T(8,128)(2,1)S(1)}, u32[]{:S(2)}, u32[]{:S(2)}) collective-permute-start(bf16[64,896]{1,0:T(8,128)(2,1)S(1)} %get-tuple-element.110), channel_id=1, source_target_pairs={{0,2},{1,3},{2,0},{3,1},{4,6},{5,7},{6,4},{7,5},{8,10},{9,11},{10,... | collective-permute-start | bytes 344072 | tf_op jit(solution)/shard_map/ppermute | solution.py:20
  68.6 10.6 %collective-permute-start.28 = (bf16[64,896]{1,0:T(8,128)(2,1)S(1)}, bf16[64,896]{1,0:T(8,128)(2,1)S(1)}, u32[]{:S(2)}, u32[]{:S(2)}) collective-permute-start(bf16[64,896]{1,0:T(8,128)(2,1)S(1)} %get-tuple-element.117), channel_id=1, source_target_pairs={{0,16},{4,20},{8,24},{12,28},{16,0},{20,4},{24,8},{28,12},{1,17},{... | collective-permute-start | bytes 344072 | tf_op jit(solution)/shard_map/ppermute | solution.py:20
  70.9 8.2 %collective-permute-start.29 = (bf16[64,896]{1,0:T(8,128)(2,1)S(1)}, bf16[64,896]{1,0:T(8,128)(2,1)S(1)}, u32[]{:S(2)}, u32[]{:S(2)}) collective-permute-start(bf16[64,896]{1,0:T(8,128)(2,1)S(1)} %get-tuple-element.116), channel_id=1, source_target_pairs={{0,24},{4,28},{8,16},{12,20},{16,8},{20,12},{24,0},{28,4},{1,25},{... | collective-permute-start | bytes 344072 | tf_op jit(solution)/shard_map/ppermute | solution.py:20
  (3 other events, 27.6 us)
